TPU v7x, 32 devices: a whole 2x2x4 slice. The times are simulated.
32 devices in a mesh: ta: 4 (over z), ha: 2 (over x), wa: 4 (over y, core).
Axes of the slice: x: 2, y: 2, z: 4, core: 2. Of those that a mesh axis runs over, the one named last changes fastest.
Arguments:
- query_in: bfloat16 [12, 16, 32, 256], P('ta', 'ha', 'wa'), may hold values from -24 to 24
- key_in: bfloat16 [12, 16, 32, 256], P('ta', 'ha', 'wa'), may hold values from -24 to 24
- value_in: bfloat16 [12, 16, 32, 256], P('ta', 'ha', 'wa'), may hold values from -6 to 6
- cotangent: bfloat16 [12, 16, 32, 256], P('ta', 'ha', 'wa'), may hold values from -6 to 6
Outputs:
- attended: bfloat16 [12, 16, 32, 256], P('ta', 'ha', 'wa')
- grad_query: bfloat16 [12, 16, 32, 256], P('ta', 'ha', 'wa')
- grad_key: bfloat16 [12, 16, 32, 256], P('ta', 'ha', 'wa')
- grad_value: bfloat16 [12, 16, 32, 256], P('ta', 'ha', 'wa')
All inputs are finite; a program needn't handle non-finite values.
Results may differ from a plain program's by a relative error of at most 0.035.
Values may be sent and summed in bfloat16 or wider, within the bound.
No kernel may reach another device: no remote copies, remote signals or barrier semaphores. Data moves between devices by JAX's collectives and lax.ppermute only.
A program may use at most 128 MiB of HBM per device.

v0:
```python
import jax
import jax.numpy as jnp
from jax import lax
from jax.sharding import PartitionSpec as P

DH = 128
HEADS = 2
TILE_T = 6
TILE_H = 8
TILE_W = 8


NEGATIVE = -1e30


def padded(block, sides, width):
    for axis, dim in sides:
        count = lax.axis_size(axis)
        forward = [(i, i + 1) for i in range(count - 1)]
        backward = [(target, source) for source, target in forward]
        low = lax.ppermute(
            lax.slice_in_dim(block, block.shape[dim] - width, None, axis=dim), axis, forward
        )
        high = lax.ppermute(lax.slice_in_dim(block, 0, width, axis=dim), axis, backward)
        block = jnp.concatenate([low, block, high], axis=dim)
    return block


def from_behind(block, axis, distance):
    devices = range(lax.axis_size(axis))
    route = [((i - distance) % len(devices), i) for i in devices]
    return lax.ppermute(block, axis, route)


def rope_tables(time_pos, row_pos, col_pos):
    time_dims = DH // 8
    space_dims = (DH - time_dims) // 2
    slower = 256.0 ** (-jnp.arange(0, time_dims, 2, dtype=jnp.float32) / time_dims)
    faster = 256.0 ** (-jnp.arange(0, space_dims, 2, dtype=jnp.float32) / space_dims)
    angles = jnp.concatenate(
        [time_pos[:, None] * slower, row_pos[:, None] * faster, col_pos[:, None] * faster], axis=1
    )
    angle_full = jnp.tile(jnp.repeat(angles, 2, axis=1), (1, HEADS))
    return (jnp.cos(angle_full), jnp.sin(angle_full))


def pair_swapper(chan_count):
    row_ids = jnp.arange(chan_count, dtype=jnp.int32)[:, None]
    col_ids = jnp.arange(chan_count, dtype=jnp.int32)[None, :]
    even_col = col_ids % 2 == 0
    minus_part = jnp.where(even_col & (row_ids == col_ids + 1), -1.0, 0.0)
    plus_part = jnp.where(~even_col & (row_ids == col_ids - 1), 1.0, 0.0)
    return (minus_part + plus_part).astype(jnp.float32)


def rotate(flat_in, cosine, sine_tab, direction):
    swapper = pair_swapper(flat_in.shape[1])
    if flat_in.dtype == jnp.bfloat16:
        swapped = jnp.dot(flat_in, swapper.astype(jnp.bfloat16), preferred_element_type=jnp.float32)
    else:
        swapped = jnp.dot(
            flat_in, swapper, preferred_element_type=jnp.float32, precision=lax.Precision.HIGHEST
        )
    return flat_in.astype(jnp.float32) * cosine + swapped * (direction * sine_tab)


def region(frame_lo, frame_count, row_lo, row_count, col_lo, col_count):
    frame_ids = frame_lo + jnp.arange(frame_count, dtype=jnp.int32)
    row_ids = row_lo + jnp.arange(row_count, dtype=jnp.int32)
    col_ids = col_lo + jnp.arange(col_count, dtype=jnp.int32)
    shape_all = (frame_count, row_count, col_count)
    frame_grid = jnp.broadcast_to(frame_ids[:, None, None], shape_all).reshape(-1)
    row_grid = jnp.broadcast_to(row_ids[None, :, None], shape_all).reshape(-1)
    col_grid = jnp.broadcast_to(col_ids[None, None, :], shape_all).reshape(-1)
    return (frame_grid, row_grid, col_grid)


def space_mask(row_lo, col_lo, row_count, col_count, margin, row_limit, col_limit):
    own_rows = row_lo + jnp.arange(row_count, dtype=jnp.int32)
    own_cols = col_lo + jnp.arange(col_count, dtype=jnp.int32)
    near_rows = row_lo - margin + jnp.arange(row_count + 2 * margin, dtype=jnp.int32)
    near_cols = col_lo - margin + jnp.arange(col_count + 2 * margin, dtype=jnp.int32)
    row_ok = (
        (jnp.abs(own_rows[:, None] // TILE_H - near_rows[None, :] // TILE_H) <= 1)
        & (near_rows[None, :] >= 0)
        & (near_rows[None, :] < row_limit)
    )
    col_ok = (
        (jnp.abs(own_cols[:, None] // TILE_W - near_cols[None, :] // TILE_W) <= 1)
        & (near_cols[None, :] >= 0)
        & (near_cols[None, :] < col_limit)
    )
    return (row_ok[:, None, :, None] & col_ok[None, :, None, :]).reshape(
        row_count * col_count, near_rows.shape[0] * near_cols.shape[0]
    )


def time_ok(first_lo, first_count, second_lo, second_count):
    first_ids = first_lo + jnp.arange(first_count, dtype=jnp.int32)
    second_ids = second_lo + jnp.arange(second_count, dtype=jnp.int32)
    return jnp.abs(first_ids[:, None] // TILE_T - second_ids[None, :] // TILE_T) <= 1


def full_mask(frame_table, spatial):
    first_count, second_count = frame_table.shape
    inner_a, inner_b = spatial.shape
    joined = frame_table[:, None, :, None] & spatial[None, :, None, :]
    return joined.reshape(first_count * inner_a, second_count * inner_b)


def head_cut(matrix, head_idx):
    return matrix[:, head_idx * DH : (head_idx + 1) * DH]


def forward_block(carried, key_rows, value_rows, visible, query_rows, frames, scale_factor):
    best_all, acc_all, sum_all = carried
    query_total = query_rows.shape[0]
    visible = visible.reshape(query_total, frames, -1)
    new_best, new_acc, new_sum = ([], [], [])
    for head_idx in range(HEADS):
        scores = jnp.einsum(
            "qd,kd->qk",
            head_cut(query_rows, head_idx),
            head_cut(key_rows, head_idx),
            preferred_element_type=jnp.float32,
        )
        scores = scores.reshape(query_total, frames, -1) * scale_factor
        frame_max = jnp.max(jnp.where(visible, scores, NEGATIVE), axis=2)
        weights = jnp.where(visible, jnp.exp(scores - frame_max[:, :, None]), 0.0)
        value_head = head_cut(value_rows, head_idx).reshape(frames, -1, DH)
        partial_out = jnp.einsum(
            "qfk,fkd->qfd",
            weights.astype(jnp.bfloat16),
            value_head,
            preferred_element_type=jnp.float32,
        )
        highest = jnp.maximum(best_all[head_idx], jnp.max(frame_max, axis=1))
        keep_old = jnp.exp(best_all[head_idx] - highest)
        keep_new = jnp.exp(frame_max - highest[:, None])
        new_acc.append(
            acc_all[head_idx] * keep_old[:, None]
            + jnp.sum(partial_out * keep_new[:, :, None], axis=1)
        )
        new_sum.append(
            sum_all[head_idx] * keep_old + jnp.sum(jnp.sum(weights, axis=2) * keep_new, axis=1)
        )
        new_best.append(highest)
    return (jnp.stack(new_best), jnp.stack(new_acc), jnp.stack(new_sum))


def query_grad_block(
    dq_all, key_rows, value_rows, visible, query_rows, grad_rows, lse_all, delta_all, scale_factor
):
    pieces = []
    for head_idx in range(HEADS):
        key_head = head_cut(key_rows, head_idx)
        scores = (
            jnp.einsum(
                "qd,kd->qk",
                head_cut(query_rows, head_idx),
                key_head,
                preferred_element_type=jnp.float32,
            )
            * scale_factor
        )
        prob_rows = jnp.where(visible, jnp.exp(scores - lse_all[head_idx][:, None]), 0.0)
        prob_grad = jnp.einsum(
            "qd,kd->qk",
            head_cut(grad_rows, head_idx),
            head_cut(value_rows, head_idx),
            preferred_element_type=jnp.float32,
        )
        dscore = (prob_rows * (prob_grad - delta_all[head_idx][:, None])).astype(jnp.bfloat16)
        pieces.append(
            dq_all[head_idx]
            + jnp.dot(dscore, key_head, preferred_element_type=jnp.float32) * scale_factor
        )
    return jnp.stack(pieces)


def key_grads(
    key_rows, value_rows, visible, query_rows, grad_rows, lse_rows, delta_rows, scale_factor
):
    key_parts, value_parts = ([], [])
    for head_idx in range(HEADS):
        query_head = head_cut(query_rows, head_idx)
        grad_head = head_cut(grad_rows, head_idx)
        scores = (
            jnp.einsum(
                "kd,qd->kq",
                head_cut(key_rows, head_idx),
                query_head,
                preferred_element_type=jnp.float32,
            )
            * scale_factor
        )
        prob_rows = jnp.where(visible, jnp.exp(scores - lse_rows[:, head_idx][None, :]), 0.0)
        value_parts.append(
            jnp.einsum(
                "kq,qd->kd",
                prob_rows.astype(jnp.bfloat16),
                grad_head,
                preferred_element_type=jnp.float32,
            )
        )
        prob_grad = jnp.einsum(
            "kd,qd->kq",
            head_cut(value_rows, head_idx),
            grad_head,
            preferred_element_type=jnp.float32,
        )
        dscore = (prob_rows * (prob_grad - delta_rows[:, head_idx][None, :])).astype(jnp.bfloat16)
        key_parts.append(
            jnp.einsum("kq,qd->kd", dscore, query_head, preferred_element_type=jnp.float32)
            * scale_factor
        )
    return (jnp.concatenate(key_parts, axis=1), jnp.concatenate(value_parts, axis=1))


def shards(query_in, key_in, value_in, cotangent):
    frame_count, row_count, col_count, chan_count = query_in.shape
    cell_count = frame_count * row_count * col_count
    margin = TILE_W
    frame_axis = lax.axis_size("ta")
    row_limit = row_count * lax.axis_size("ha")
    col_limit = col_count * lax.axis_size("wa")
    frame_pos = lax.axis_index("ta")
    frame_lo = frame_pos * frame_count
    row_lo = lax.axis_index("ha") * row_count
    col_lo = lax.axis_index("wa") * col_count
    scale_factor = DH ** (-0.5)
    own_grids = region(frame_lo, frame_count, row_lo, row_count, col_lo, col_count)
    cosine, sine_tab = rope_tables(
        own_grids[0].astype(jnp.float32),
        own_grids[1].astype(jnp.float32),
        own_grids[2].astype(jnp.float32),
    )
    spatial = space_mask(row_lo, col_lo, row_count, col_count, margin, row_limit, col_limit)
    query_rot = rotate(query_in.reshape(cell_count, chan_count), cosine, sine_tab, 1.0).astype(
        jnp.bfloat16
    )
    key_rot = rotate(key_in.reshape(cell_count, chan_count), cosine, sine_tab, 1.0).astype(
        jnp.bfloat16
    )
    value_rows = value_in.reshape(cell_count, chan_count)
    grad_rows = cotangent.reshape(cell_count, chan_count)
    key_pair = jnp.stack([key_rot.reshape(frame_count, row_count, col_count, chan_count), value_in])
    every_frame = lax.all_gather(key_pair, "ta", axis=1, tiled=True)
    stored = padded(every_frame, (("ha", 2), ("wa", 3)), margin)

    def visit_keys(visit, carried):

        def one_group(group_idx, running):
            frame_start = group_idx * frame_count
            key_block = lax.dynamic_slice_in_dim(stored, frame_start, frame_count, 1)
            return visit(running, key_block, frame_start)

        return lax.fori_loop(0, frame_axis, one_group, carried)

    start_state = (
        jnp.full((HEADS, cell_count), NEGATIVE, jnp.float32),
        jnp.zeros((HEADS, cell_count, DH), jnp.float32),
        jnp.zeros((HEADS, cell_count), jnp.float32),
    )

    def forward_visit(carried, key_block, frame_start):
        visible = full_mask(time_ok(frame_lo, frame_count, frame_start, frame_count), spatial)
        return forward_block(
            carried,
            key_block[0].reshape(-1, chan_count),
            key_block[1].reshape(-1, chan_count),
            visible,
            query_rot,
            frame_count,
            scale_factor,
        )

    best_all, acc_all, sum_all = visit_keys(forward_visit, start_state)
    lse_all = best_all + jnp.log(sum_all)
    attended = (
        jnp.transpose(acc_all / sum_all[:, :, None], (1, 0, 2))
        .reshape(cell_count, chan_count)
        .astype(jnp.bfloat16)
    )
    delta_all = jnp.sum(
        grad_rows.reshape(cell_count, HEADS, DH).astype(jnp.float32)
        * attended.reshape(cell_count, HEADS, DH).astype(jnp.float32),
        axis=2,
    ).T
    query_pair = jnp.stack(
        [query_rot.reshape(frame_count, row_count, col_count, chan_count), cotangent]
    )
    stat_pair = jnp.stack(
        [
            lse_all.T.reshape(frame_count, row_count, col_count, HEADS),
            delta_all.T.reshape(frame_count, row_count, col_count, HEADS),
        ]
    )
    dq_start = jnp.zeros((HEADS, cell_count, DH), jnp.float32)

    def query_visit(carried, key_block, frame_start):
        visible = full_mask(time_ok(frame_lo, frame_count, frame_start, frame_count), spatial)
        return query_grad_block(
            carried,
            key_block[0].reshape(-1, chan_count),
            key_block[1].reshape(-1, chan_count),
            visible,
            query_rot,
            grad_rows,
            lse_all,
            delta_all,
            scale_factor,
        )

    dq_all = visit_keys(query_visit, dq_start)
    moving_query = query_pair
    moving_stat = stat_pair
    key_total = jnp.zeros((cell_count, chan_count), jnp.float32)
    value_total = jnp.zeros((cell_count, chan_count), jnp.float32)
    for step_idx in range(frame_axis):
        if step_idx > 0:
            moving_query = from_behind(moving_query, "ta", 1)
            moving_stat = from_behind(moving_stat, "ta", 1)
        query_near = padded(moving_query, (("ha", 2), ("wa", 3)), margin)
        stat_near = padded(moving_stat, (("ha", 2), ("wa", 3)), margin)
        source = (frame_pos - step_idx) % frame_axis
        visible = full_mask(
            time_ok(frame_lo, frame_count, source * frame_count, frame_count), spatial
        )
        key_part, value_part = key_grads(
            key_rot,
            value_rows,
            visible,
            query_near[0].reshape(-1, chan_count),
            query_near[1].reshape(-1, chan_count),
            stat_near[0].reshape(-1, HEADS),
            stat_near[1].reshape(-1, HEADS),
            scale_factor,
        )
        key_total = key_total + key_part
        value_total = value_total + value_part
    dq_rows = jnp.transpose(dq_all, (1, 0, 2)).reshape(cell_count, chan_count)
    out_shape = (frame_count, row_count, col_count, chan_count)
    grad_query = rotate(dq_rows, cosine, sine_tab, -1.0).astype(jnp.bfloat16).reshape(out_shape)
    grad_key = rotate(key_total, cosine, sine_tab, -1.0).astype(jnp.bfloat16).reshape(out_shape)
    grad_value = value_total.astype(jnp.bfloat16).reshape(out_shape)
    return (attended.reshape(out_shape), grad_query, grad_key, grad_value)


def solution(mesh):
    in_specs = (
        P("ta", "ha", "wa", None),
        P("ta", "ha", "wa", None),
        P("ta", "ha", "wa", None),
        P("ta", "ha", "wa", None),
    )
    out_specs = (
        P("ta", "ha", "wa", None),
        P("ta", "ha", "wa", None),
        P("ta", "ha", "wa", None),
        P("ta", "ha", "wa", None),
    )
    return jax.shard_map(shards, mesh=mesh, in_specs=in_specs, out_specs=out_specs, check_vma=False)
```

profile of v0, /device:TPU:1, one launch (start us, length us, event | category | flops | bytes accessed | tf_op | source)
XLA Modules:
  0.0 374.2 jit_solution(2965219979850949040)
XLA Ops:
  6.1 4.0 %collective-permute-start.4 = (bf16[2,3,8,8,256]{4,3,2,1,0:T(8,128)(2,1)}, bf16[2,3,8,8,256]{4,3,2,1,0:T(8,128)(2,1)S(1)}, u32[]{:S(2)}, u32[]{:S(2)}) collective-permute-start(bf16[2,3,8,8,256]{4,3,2,1,0:T(8,128)(2,1)} %pad_maximum_fusion.11), channel_id=1, source_target_pairs={{0,4},{1,5},{2,6},{3,7},{8,12},{9,13},{10,14},{11,15},{16,20},{17,... | collective-permute-start | bytes 589832 | tf_op jit(solution)/shard_map/ppermute | solution.py:21
  10.1 2.2 collective-permute-start.12
  13.2 18.4 %all_gather.3 = bf16[2,12,8,8,256]{4,3,2,1,0:T(8,128)(2,1)S(1)} all-gather(bf16[2,3,8,8,256]{4,3,2,1,0:T(8,128)(2,1)S(1)} %pad_maximum_fusion.10), channel_id=1, replica_groups=mesh['ta'=4,'ha'=2,'wa'=4] {'ta'}, dimensions={1}, use_global_device_ids=true | all-gather | bytes 983040 | tf_op jit(solution)/shard_map/all_gather | solution.py:248
  31.6 2.3 collective-permute-start
  34.8 2.0 collective-permute-start.13
  36.8 2.1 broadcast_and_fusion.4
  48.7 5.3 %collective-permute-start.7 = (bf16[2,3,24,8,256]{4,3,2,1,0:T(8,128)(2,1)S(1)}, bf16[2,3,24,8,256]{4,3,2,1,0:T(8,128)(2,1)S(1)}, u32[]{:S(2)}, u32[]{:S(2)}) collective-permute-start(bf16[2,3,24,8,256]{4,3,2,1,0:T(8,128)(2,1)S(1)} %pad_maximum_fusion.9), channel_id=1, source_target_pairs={{1,0},{2,1},{3,2},{5,4},{6,5},{7,6},{9,8},{10,9},{11,10},{13,12},{... | collective-permute-start | bytes 1769480 | tf_op jit(solution)/shard_map/ppermute | solution.py:24
  55.3 4.3 %collective-permute-start.23 = (bf16[2,3,8,8,256]{4,3,2,1,0:T(8,128)(2,1)S(1)}, bf16[2,3,8,8,256]{4,3,2,1,0:T(8,128)(2,1)S(1)}, u32[]{:S(2)}, u32[]{:S(2)}) collective-permute-start(bf16[2,3,8,8,256]{4,3,2,1,0:T(8,128)(2,1)S(1)} %collective-permute-done.22), channel_id=1, source_target_pairs={{0,4},{1,5},{2,6},{3,7},{8,12},{9,13},{10,14},{11,15},{16,20},{17,... | collective-permute-start | bytes 589832 | tf_op jit(solution)/shard_map/ppermute | solution.py:21
  61.6 6.6 %collective-permute-done.14 = bf16[2,3,8,8,256]{4,3,2,1,0:T(8,128)(2,1)S(1)} collective-permute-done((bf16[2,3,8,8,256]{4,3,2,1,0:T(8,128)(2,1)}, bf16[2,3,8,8,256]{4,3,2,1,0:T(8,128)(2,1)S(1)}, u32[]{:S(2)}, u32[]{:S(2)}) %collective-permute-start.14) | collective-permute-done | bytes 196640 | tf_op jit(solution)/shard_map/ppermute | solution.py:24
  68.1 7.3 %collective-permute-start.6 = (bf16[2,3,24,8,256]{4,3,2,1,0:T(8,128)(2,1)S(1)}, bf16[2,3,24,8,256]{4,3,2,1,0:T(8,128)(2,1)S(1)}, u32[]{:S(2)}, u32[]{:S(2)}) collective-permute-start(bf16[2,3,24,8,256]{4,3,2,1,0:T(8,128)(2,1)S(1)} %pad_maximum_fusion.9), channel_id=1, source_target_pairs={{0,1},{1,2},{2,3},{4,5},{5,6},{6,7},{8,9},{9,10},{10,11},{12,13},{... | collective-permute-start | bytes 1769480 | tf_op jit(solution)/shard_map/ppermute | solution.py:21
  78.6 1.9 collective-permute-start.3
  80.6 2.6 collective-permute-done.24
  83.1 1.9 collective-permute-start.2
  85.1 2.6 collective-permute-start.16
  87.6 2.7 collective-permute-start.33
  92.6 1.9 collective-permute-done.33
  94.6 3.0 collective-permute-start.15
  98.9 2.3 collective-permute-start.26
  102.5 12.6 %collective-permute-done.16 = bf16[2,3,24,8,256]{4,3,2,1,0:T(8,128)(2,1)S(1)} collective-permute-done((bf16[2,3,24,8,256]{4,3,2,1,0:T(8,128)(2,1)S(1)}, bf16[2,3,24,8,256]{4,3,2,1,0:T(8,128)(2,1)S(1)}, u32[]{:S(2)}, u32[]{:S(2)}) %collective-permute-start.16) | collective-permute-done | bytes 589856 | tf_op jit(solution)/shard_map/ppermute | solution.py:24
  115.1 1.9 collective-permute-start.25
  117.1 2.4 collective-permute-start.36
  121.4 2.3 collective-permute-start.35
  126.6 2.5 collective-permute-done.36
  131.8 3.3 pad_maximum_fusion.4
  135.8 79.3 %while.38 = (s32[]{:T(128)}, f32[2,192]{1,0:T(2,128)S(1)}, f32[2,192,128]{2,1,0:T(8,128)}, f32[2,192]{1,0:T(2,128)S(1)}, s32[]{:T(128)}, /*index=5*/bf16[2,12,24...) while((s32[]{:T(128)}, f32[2,192]{1,0:T(2,128)S(1)}, ...), condition=%wide.region_11.12_spmd.clone, body=%wide.region_0.11_spmd.clone.sunk | while | flops 349461984 | bytes 38289168 | solution.py:258
  137.9 2.5 constant_dynamic-slice_fusion.6
  144.9 2.0 copy.189
  147.3 1.8 copy.190
  149.1 2.0 copy.191
  157.8 2.5 constant_dynamic-slice_fusion.6
  164.7 2.0 copy.189
  167.1 1.8 copy.190
  169.0 2.0 copy.191
  177.6 2.5 constant_dynamic-slice_fusion.6
  184.5 2.0 copy.189
  187.0 1.8 copy.190
  188.8 2.0 copy.191
  197.5 2.5 constant_dynamic-slice_fusion.6
  204.4 2.0 copy.189
  208.6 2.0 copy.191
  219.3 5.2 %collective-permute-start.8 = (f32[2,3,8,8,2]{3,2,1,4,0:T(8,128)}, f32[2,3,8,8,2]{3,2,1,4,0:T(8,128)}, u32[]{:S(2)}, u32[]{:S(2)}) collective-permute-start(f32[2,3,8,8,2]{3,2,1,4,0:T(8,128)} %pad_maximum_fusion.17), channel_id=1, source_target_pairs={{0,4},{1,5},{2,6},{3,7},{8,12},{9,13},{10,14},{11,15},{16,20},{17,... | collective-permute-start | bytes 9224 | tf_op jit(solution)/shard_map/ppermute | solution.py:21
  226.0 41.1 %while.39 = (s32[]{:T(128)}, f32[2,192,128]{2,1,0:T(8,128)}, s32[]{:T(128)}, bf16[2,12,24,24,256]{4,3,2,1,0:T(8,128)(2,1)}, bf16[192,256]{1,0:T(8,128)(2,1)}, /*...) while((s32[]{:T(128)}, f32[2,192,128]{2,1,0:T(8,128)}, ...), condition=%wide.region_14.15_spmd.clone, body=%wide.region_13.14_spmd.clone.sunk | while | flops 514105440 | bytes 16145121 | solution.py:258
  267.2 2.3 fusion.134
  273.5 4.0 %collective-permute-start.18 = (f32[2,3,8,8,2]{3,2,1,4,0:T(8,128)}, f32[2,3,8,8,2]{3,2,1,4,0:T(8,128)S(1)}, u32[]{:S(2)}, u32[]{:S(2)}) collective-permute-start(f32[2,3,8,8,2]{3,2,1,4,0:T(8,128)} %collective-permute-done.17), channel_id=1, source_target_pairs={{0,4},{1,5},{2,6},{3,7},{8,12},{9,13},{10,14},{11,15},{16,20},{17,... | collective-permute-start | bytes 9224 | tf_op jit(solution)/shard_map/ppermute | solution.py:21
  277.5 2.5 collective-permute-start.27
  281.9 1.9 collective-permute-start.11
  283.8 6.1 %collective-permute-start.10 = (f32[2,3,24,8,2]{2,3,4,1,0:T(8,128)S(1)}, f32[2,3,24,8,2]{2,3,4,1,0:T(8,128)S(1)}, u32[]{:S(2)}, u32[]{:S(2)}) collective-permute-start(f32[2,3,24,8,2]{2,3,4,1,0:T(8,128)S(1)} %pad_maximum_fusion.18), channel_id=1, source_target_pairs={{0,1},{1,2},{2,3},{4,5},{5,6},{6,7},{8,9},{9,10},{10,11},{12,13},{... | collective-permute-start | bytes 27656 | tf_op jit(solution)/shard_map/ppermute | solution.py:21
  292.1 4.0 %collective-permute-start.28 = (f32[2,3,8,8,2]{3,2,1,4,0:T(8,128)S(1)}, f32[2,3,8,8,2]{3,2,1,4,0:T(8,128)S(1)}, u32[]{:S(2)}, u32[]{:S(2)}) collective-permute-start(f32[2,3,8,8,2]{3,2,1,4,0:T(8,128)S(1)} %collective-permute-done.27), channel_id=1, source_target_pairs={{0,4},{1,5},{2,6},{3,7},{8,12},{9,13},{10,14},{11,15},{16,20},{17,... | collective-permute-start | bytes 9224 | tf_op jit(solution)/shard_map/ppermute | solution.py:21
  296.9 1.9 collective-permute-start.21
  299.0 3.6 collective-permute-start.20
  304.1 4.0 %collective-permute-done.37 = f32[2,3,8,8,2]{3,2,1,4,0:T(8,128)} collective-permute-done((f32[2,3,8,8,2]{3,2,1,4,0:T(8,128)S(1)}, f32[2,3,8,8,2]{3,2,1,4,0:T(8,128)}, u32[]{:S(2)}, u32[]{:S(2)}) %collective-permute-start.37) | collective-permute-done | bytes 3104 | tf_op jit(solution)/shard_map/ppermute | solution.py:32
  308.1 2.3 collective-permute-start.31
  312.6 5.2 %collective-permute-start.38 = (f32[2,3,8,8,2]{3,2,1,4,0:T(8,128)}, f32[2,3,8,8,2]{3,2,1,4,0:T(8,128)}, u32[]{:S(2)}, u32[]{:S(2)}) collective-permute-start(f32[2,3,8,8,2]{3,2,1,4,0:T(8,128)} %collective-permute-done.37), channel_id=1, source_target_pairs={{0,4},{1,5},{2,6},{3,7},{8,12},{9,13},{10,14},{11,15},{16,20},{17,... | collective-permute-start | bytes 9224 | tf_op jit(solution)/shard_map/ppermute | solution.py:21
  321.5 2.3 fusion.142
  323.8 2.4 fusion.143
  327.2 3.8 %collective-permute-start.30 = (f32[2,3,24,8,2]{2,3,4,1,0:T(8,128)}, f32[2,3,24,8,2]{2,3,4,1,0:T(8,128)}, u32[]{:S(2)}, u32[]{:S(2)}) collective-permute-start(f32[2,3,24,8,2]{2,3,4,1,0:T(8,128)} %pad_maximum_fusion.20), channel_id=1, source_target_pairs={{0,1},{1,2},{2,3},{4,5},{5,6},{6,7},{8,9},{9,10},{10,11},{12,13},{... | collective-permute-start | bytes 27656 | tf_op jit(solution)/shard_map/ppermute | solution.py:21
  333.5 1.9 collective-permute-start.41
  335.4 3.9 %collective-permute-start.40 = (f32[2,3,24,8,2]{2,3,4,1,0:T(8,128)}, f32[2,3,24,8,2]{2,3,4,1,0:T(8,128)}, u32[]{:S(2)}, u32[]{:S(2)}) collective-permute-start(f32[2,3,24,8,2]{2,3,4,1,0:T(8,128)} %pad_maximum_fusion.21), channel_id=1, source_target_pairs={{0,1},{1,2},{2,3},{4,5},{5,6},{6,7},{8,9},{9,10},{10,11},{12,13},{... | collective-permute-start | bytes 27656 | tf_op jit(solution)/shard_map/ppermute | solution.py:21
  344.3 2.0 fusion.140
  347.6 2.0 fusion.141
  355.4 2.0 fusion.138
  358.7 2.0 fusion.139
  365.4 1.9 fusion.136
  370.7 2.7 fusion.135
  (496 shorter events, 171.5 us)
Async XLA Ops:
  0.7 266.5 %copy-start.46 = (s32[256]{0:T(256)}, s32[256]{0:T(256)S(1)}, u32[]{:S(2)}) copy-start(s32[256]{0:T(256)S(1)} %get-tuple-element.700) | copy-start | bytes 3076
  0.7 266.5 %copy-start.48 = (s32[256]{0:T(256)}, s32[256]{0:T(256)S(1)}, u32[]{:S(2)}) copy-start(s32[256]{0:T(256)S(1)} %get-tuple-element.701) | copy-start | bytes 3076
  0.7 11.6 %copy-start.53 = (pred[256]{0:T(512)(128)(4,1)}, pred[256]{0:T(512)(128)(4,1)S(1)}, u32[]{:S(2)}) copy-start(pred[256]{0:T(512)(128)(4,1)S(1)} %get-tuple-element.703) | copy-start | bytes 772
  0.7 266.5 %copy-start.52 = (pred[256]{0:T(512)(128)(4,1)}, pred[256]{0:T(512)(128)(4,1)S(1)}, u32[]{:S(2)}) copy-start(pred[256]{0:T(512)(128)(4,1)S(1)} %get-tuple-element.702) | copy-start | bytes 772
  1.8 10.5 %copy-start.51 = (bf16[3,8,8,256]{3,2,1,0:T(8,128)(2,1)S(1)}, bf16[3,8,8,256]{3,2,1,0:T(8,128)(2,1)}, u32[]{:S(2)}) copy-start(bf16[3,8,8,256]{3,2,1,0:T(8,128)(2,1)} %param.9) | copy-start | bytes 294916
  2.1 10.5 %copy-start.18 = (bf16[3,8,8,256]{3,2,1,0:T(8,128)(2,1)S(1)}, bf16[3,8,8,256]{3,2,1,0:T(8,128)(2,1)}, u32[]{:S(2)}) copy-start(bf16[3,8,8,256]{3,2,1,0:T(8,128)(2,1)} %param.10) | copy-start | bytes 294916
  2.2 10.4 %copy-start.43 = (f32[192,2,128]{2,1,0:T(2,128)}, f32[192,2,128]{2,1,0:T(2,128)S(1)}, u32[]{:S(2)}) copy-start(f32[192,2,128]{2,1,0:T(2,128)S(1)} %tile.9) | copy-start | bytes 589828
  2.3 10.3 %copy-start.45 = (f32[192,2,128]{2,1,0:T(2,128)}, f32[192,2,128]{2,1,0:T(2,128)S(1)}, u32[]{:S(2)}) copy-start(f32[192,2,128]{2,1,0:T(2,128)S(1)} %tile.8) | copy-start | bytes 589828
  4.8 41.6 %collective-permute-start.5 = (bf16[2,3,8,8,256]{4,3,2,1,0:T(8,128)(2,1)}, bf16[2,3,8,8,256]{4,3,2,1,0:T(8,128)(2,1)S(1)}, u32[]{:S(2)}, u32[]{:S(2)}) collective-permute-start(bf16[2,3,8,8,256]{4,3,2,1,0:T(8,128)(2,1)} %pad_maximum_fusion.11), channel_id=1, source_target_pairs={{4,0},{5,1},{6,2},{7,3},{12,8},{13,9},{14,10},{15,11},{20,16},{21,... | collective-permute-start | bytes 589832 | tf_op jit(solution)/shard_map/ppermute | solution.py:24
  6.1 41.6 %collective-permute-start.4 = (bf16[2,3,8,8,256]{4,3,2,1,0:T(8,128)(2,1)}, bf16[2,3,8,8,256]{4,3,2,1,0:T(8,128)(2,1)S(1)}, u32[]{:S(2)}, u32[]{:S(2)}) collective-permute-start(bf16[2,3,8,8,256]{4,3,2,1,0:T(8,128)(2,1)} %pad_maximum_fusion.11), channel_id=1, source_target_pairs={{0,4},{1,5},{2,6},{3,7},{8,12},{9,13},{10,14},{11,15},{16,20},{17,... | collective-permute-start | bytes 589832 | tf_op jit(solution)/shard_map/ppermute | solution.py:21
  10.1 24.7 %collective-permute-start.12 = (bf16[2,3,8,8,256]{4,3,2,1,0:T(8,128)(2,1)}, bf16[2,3,8,8,256]{4,3,2,1,0:T(8,128)(2,1)}, u32[]{:S(2)}, u32[]{:S(2)}) collective-permute-start(bf16[2,3,8,8,256]{4,3,2,1,0:T(8,128)(2,1)} %pad_maximum_fusion.11), channel_id=1, source_target_pairs={{24,0},{0,8},{8,16},{16,24},{25,1},{1,9},{9,17},{17,25},{26,2},{2,... | collective-permute-start | bytes 589832 | tf_op jit(solution)/shard_map/ppermute | solution.py:32
  31.6 45.2 %collective-permute-start = (bf16[2,12,8,8,256]{4,3,2,1,0:T(8,128)(2,1)S(1)}, bf16[2,12,8,8,256]{4,3,2,1,0:T(8,128)(2,1)}, u32[]{:S(2)}, u32[]{:S(2)}) collective-permute-start(bf16[2,12,8,8,256]{4,3,2,1,0:T(8,128)(2,1)S(1)} %all_gather.3), channel_id=1, source_target_pairs={{0,4},{1,5},{2,6},{3,7},{8,12},{9,13},{10,14},{11,15},{16,20},{17,... | collective-permute-start | bytes 2359304 | tf_op jit(solution)/shard_map/ppermute | solution.py:21
  34.8 19.2 %collective-permute-start.13 = (bf16[2,3,8,8,256]{4,3,2,1,0:T(8,128)(2,1)}, bf16[2,3,8,8,256]{4,3,2,1,0:T(8,128)(2,1)}, u32[]{:S(2)}, u32[]{:S(2)}) collective-permute-start(bf16[2,3,8,8,256]{4,3,2,1,0:T(8,128)(2,1)} %collective-permute-done.12), channel_id=1, source_target_pairs={{0,4},{1,5},{2,6},{3,7},{8,12},{9,13},{10,14},{11,15},{16,20},{17,... | collective-permute-start | bytes 589832 | tf_op jit(solution)/shard_map/ppermute | solution.py:21
  36.8 18.5 %collective-permute-start.22 = (bf16[2,3,8,8,256]{4,3,2,1,0:T(8,128)(2,1)}, bf16[2,3,8,8,256]{4,3,2,1,0:T(8,128)(2,1)S(1)}, u32[]{:S(2)}, u32[]{:S(2)}) collective-permute-start(bf16[2,3,8,8,256]{4,3,2,1,0:T(8,128)(2,1)} %collective-permute-done.12), channel_id=1, source_target_pairs={{24,0},{0,8},{8,16},{16,24},{25,1},{1,9},{9,17},{17,25},{26,2},{2,... | collective-permute-start | bytes 589832 | tf_op jit(solution)/shard_map/ppermute | solution.py:32
  46.4 32.1 %collective-permute-start.1 = (bf16[2,12,8,8,256]{4,3,2,1,0:T(8,128)(2,1)S(1)}, bf16[2,12,8,8,256]{4,3,2,1,0:T(8,128)(2,1)S(1)}, u32[]{:S(2)}, u32[]{:S(2)}) collective-permute-start(bf16[2,12,8,8,256]{4,3,2,1,0:T(8,128)(2,1)S(1)} %all_gather.3), channel_id=1, source_target_pairs={{4,0},{5,1},{6,2},{7,3},{12,8},{13,9},{14,10},{15,11},{20,16},{21,... | collective-permute-start | bytes 2359304 | tf_op jit(solution)/shard_map/ppermute | solution.py:24
  48.7 39.0 %collective-permute-start.7 = (bf16[2,3,24,8,256]{4,3,2,1,0:T(8,128)(2,1)S(1)}, bf16[2,3,24,8,256]{4,3,2,1,0:T(8,128)(2,1)S(1)}, u32[]{:S(2)}, u32[]{:S(2)}) collective-permute-start(bf16[2,3,24,8,256]{4,3,2,1,0:T(8,128)(2,1)S(1)} %pad_maximum_fusion.9), channel_id=1, source_target_pairs={{1,0},{2,1},{3,2},{5,4},{6,5},{7,6},{9,8},{10,9},{11,10},{13,12},{... | collective-permute-start | bytes 1769480 | tf_op jit(solution)/shard_map/ppermute | solution.py:24
  54.0 14.1 %collective-permute-start.14 = (bf16[2,3,8,8,256]{4,3,2,1,0:T(8,128)(2,1)}, bf16[2,3,8,8,256]{4,3,2,1,0:T(8,128)(2,1)S(1)}, u32[]{:S(2)}, u32[]{:S(2)}) collective-permute-start(bf16[2,3,8,8,256]{4,3,2,1,0:T(8,128)(2,1)} %collective-permute-done.12), channel_id=1, source_target_pairs={{4,0},{5,1},{6,2},{7,3},{12,8},{13,9},{14,10},{15,11},{20,16},{21,... | collective-permute-start | bytes 589832 | tf_op jit(solution)/shard_map/ppermute | solution.py:24
  55.3 20.2 %collective-permute-start.23 = (bf16[2,3,8,8,256]{4,3,2,1,0:T(8,128)(2,1)S(1)}, bf16[2,3,8,8,256]{4,3,2,1,0:T(8,128)(2,1)S(1)}, u32[]{:S(2)}, u32[]{:S(2)}) collective-permute-start(bf16[2,3,8,8,256]{4,3,2,1,0:T(8,128)(2,1)S(1)} %collective-permute-done.22), channel_id=1, source_target_pairs={{0,4},{1,5},{2,6},{3,7},{8,12},{9,13},{10,14},{11,15},{16,20},{17,... | collective-permute-start | bytes 589832 | tf_op jit(solution)/shard_map/ppermute | solution.py:21
  68.1 22.2 %collective-permute-start.6 = (bf16[2,3,24,8,256]{4,3,2,1,0:T(8,128)(2,1)S(1)}, bf16[2,3,24,8,256]{4,3,2,1,0:T(8,128)(2,1)S(1)}, u32[]{:S(2)}, u32[]{:S(2)}) collective-permute-start(bf16[2,3,24,8,256]{4,3,2,1,0:T(8,128)(2,1)S(1)} %pad_maximum_fusion.9), channel_id=1, source_target_pairs={{0,1},{1,2},{2,3},{4,5},{5,6},{6,7},{8,9},{9,10},{10,11},{12,13},{... | collective-permute-start | bytes 1769480 | tf_op jit(solution)/shard_map/ppermute | solution.py:21
  75.5 7.6 %collective-permute-start.24 = (bf16[2,3,8,8,256]{4,3,2,1,0:T(8,128)(2,1)S(1)}, bf16[2,3,8,8,256]{4,3,2,1,0:T(8,128)(2,1)S(1)}, u32[]{:S(2)}, u32[]{:S(2)}) collective-permute-start(bf16[2,3,8,8,256]{4,3,2,1,0:T(8,128)(2,1)S(1)} %collective-permute-done.22), channel_id=1, source_target_pairs={{4,0},{5,1},{6,2},{7,3},{12,8},{13,9},{14,10},{15,11},{20,16},{21,... | collective-permute-start | bytes 589832 | tf_op jit(solution)/shard_map/ppermute | solution.py:24
  76.9 8.2 %collective-permute-start.32 = (bf16[2,3,8,8,256]{4,3,2,1,0:T(8,128)(2,1)S(1)}, bf16[2,3,8,8,256]{4,3,2,1,0:T(8,128)(2,1)S(1)}, u32[]{:S(2)}, u32[]{:S(2)}) collective-permute-start(bf16[2,3,8,8,256]{4,3,2,1,0:T(8,128)(2,1)S(1)} %collective-permute-done.22), channel_id=1, source_target_pairs={{24,0},{0,8},{8,16},{16,24},{25,1},{1,9},{9,17},{17,25},{26,2},{2,... | collective-permute-start | bytes 589832 | tf_op jit(solution)/shard_map/ppermute | solution.py:32
  78.6 53.2 %collective-permute-start.3 = (bf16[2,12,24,8,256]{4,3,2,1,0:T(8,128)(2,1)S(1)}, bf16[2,12,24,8,256]{4,3,2,1,0:T(8,128)(2,1)S(1)}, u32[]{:S(2)}, u32[]{:S(2)}) collective-permute-start(bf16[2,12,24,8,256]{4,3,2,1,0:T(8,128)(2,1)S(1)} %constant_dynamic-update-slice_fusion), channel_id=1, source_target_pairs={{1,0},{2,1},{3,2},{5,4},{6,5},{7,6},{9,8},{10,9},{11,10},{13,12},{... | collective-permute-start | bytes 7077896 | tf_op jit(solution)/shard_map/ppermute | solution.py:24
  83.1 48.7 %collective-permute-start.2 = (bf16[2,12,24,8,256]{4,3,2,1,0:T(8,128)(2,1)S(1)}, bf16[2,12,24,8,256]{4,3,2,1,0:T(8,128)(2,1)S(1)}, u32[]{:S(2)}, u32[]{:S(2)}) collective-permute-start(bf16[2,12,24,8,256]{4,3,2,1,0:T(8,128)(2,1)S(1)} %constant_dynamic-update-slice_fusion), channel_id=1, source_target_pairs={{0,1},{1,2},{2,3},{4,5},{5,6},{6,7},{8,9},{9,10},{10,11},{12,13},{... | collective-permute-start | bytes 7077896 | tf_op jit(solution)/shard_map/ppermute | solution.py:21
  85.1 30.0 %collective-permute-start.16 = (bf16[2,3,24,8,256]{4,3,2,1,0:T(8,128)(2,1)S(1)}, bf16[2,3,24,8,256]{4,3,2,1,0:T(8,128)(2,1)S(1)}, u32[]{:S(2)}, u32[]{:S(2)}) collective-permute-start(bf16[2,3,24,8,256]{4,3,2,1,0:T(8,128)(2,1)S(1)} %constant_dynamic-update-slice_fusion.3), channel_id=1, source_target_pairs={{1,0},{2,1},{3,2},{5,4},{6,5},{7,6},{9,8},{10,9},{11,10},{13,12},{... | collective-permute-start | bytes 1769480 | tf_op jit(solution)/shard_map/ppermute | solution.py:24
  87.6 6.9 %collective-permute-start.33 = (bf16[2,3,8,8,256]{4,3,2,1,0:T(8,128)(2,1)S(1)}, bf16[2,3,8,8,256]{4,3,2,1,0:T(8,128)(2,1)S(1)}, u32[]{:S(2)}, u32[]{:S(2)}) collective-permute-start(bf16[2,3,8,8,256]{4,3,2,1,0:T(8,128)(2,1)S(1)} %collective-permute-done.32), channel_id=1, source_target_pairs={{0,4},{1,5},{2,6},{3,7},{8,12},{9,13},{10,14},{11,15},{16,20},{17,... | collective-permute-start | bytes 589832 | tf_op jit(solution)/shard_map/ppermute | solution.py:21
  90.3 8.5 %collective-permute-start.34 = (bf16[2,3,8,8,256]{4,3,2,1,0:T(8,128)(2,1)S(1)}, bf16[2,3,8,8,256]{4,3,2,1,0:T(8,128)(2,1)S(1)}, u32[]{:S(2)}, u32[]{:S(2)}) collective-permute-start(bf16[2,3,8,8,256]{4,3,2,1,0:T(8,128)(2,1)S(1)} %collective-permute-done.32), channel_id=1, source_target_pairs={{4,0},{5,1},{6,2},{7,3},{12,8},{13,9},{14,10},{15,11},{20,16},{21,... | collective-permute-start | bytes 589832 | tf_op jit(solution)/shard_map/ppermute | solution.py:24
  94.6 22.5 %collective-permute-start.15 = (bf16[2,3,24,8,256]{4,3,2,1,0:T(8,128)(2,1)S(1)}, bf16[2,3,24,8,256]{4,3,2,1,0:T(8,128)(2,1)S(1)}, u32[]{:S(2)}, u32[]{:S(2)}) collective-permute-start(bf16[2,3,24,8,256]{4,3,2,1,0:T(8,128)(2,1)S(1)} %constant_dynamic-update-slice_fusion.3), channel_id=1, source_target_pairs={{0,1},{1,2},{2,3},{4,5},{5,6},{6,7},{8,9},{9,10},{10,11},{12,13},{... | collective-permute-start | bytes 1769480 | tf_op jit(solution)/shard_map/ppermute | solution.py:21
  98.9 22.6 %collective-permute-start.26 = (bf16[2,3,24,8,256]{4,3,2,1,0:T(8,128)(2,1)S(1)}, bf16[2,3,24,8,256]{4,3,2,1,0:T(8,128)(2,1)S(1)}, u32[]{:S(2)}, u32[]{:S(2)}) collective-permute-start(bf16[2,3,24,8,256]{4,3,2,1,0:T(8,128)(2,1)S(1)} %constant_dynamic-update-slice_fusion.6), channel_id=1, source_target_pairs={{1,0},{2,1},{3,2},{5,4},{6,5},{7,6},{9,8},{10,9},{11,10},{13,12},{... | collective-permute-start | bytes 1769480 | tf_op jit(solution)/shard_map/ppermute | solution.py:24
  115.1 9.9 %collective-permute-start.25 = (bf16[2,3,24,8,256]{4,3,2,1,0:T(8,128)(2,1)S(1)}, bf16[2,3,24,8,256]{4,3,2,1,0:T(8,128)(2,1)S(1)}, u32[]{:S(2)}, u32[]{:S(2)}) collective-permute-start(bf16[2,3,24,8,256]{4,3,2,1,0:T(8,128)(2,1)S(1)} %constant_dynamic-update-slice_fusion.6), channel_id=1, source_target_pairs={{0,1},{1,2},{2,3},{4,5},{5,6},{6,7},{8,9},{9,10},{10,11},{12,13},{... | collective-permute-start | bytes 1769480 | tf_op jit(solution)/shard_map/ppermute | solution.py:21
  117.1 11.9 %collective-permute-start.36 = (bf16[2,3,24,8,256]{4,3,2,1,0:T(8,128)(2,1)S(1)}, bf16[2,3,24,8,256]{4,3,2,1,0:T(8,128)(2,1)S(1)}, u32[]{:S(2)}, u32[]{:S(2)}) collective-permute-start(bf16[2,3,24,8,256]{4,3,2,1,0:T(8,128)(2,1)S(1)} %constant_dynamic-update-slice_fusion.9), channel_id=1, source_target_pairs={{1,0},{2,1},{3,2},{5,4},{6,5},{7,6},{9,8},{10,9},{11,10},{13,12},{... | collective-permute-start | bytes 1769480 | tf_op jit(solution)/shard_map/ppermute | solution.py:24
  121.4 8.9 %collective-permute-start.35 = (bf16[2,3,24,8,256]{4,3,2,1,0:T(8,128)(2,1)S(1)}, bf16[2,3,24,8,256]{4,3,2,1,0:T(8,128)(2,1)S(1)}, u32[]{:S(2)}, u32[]{:S(2)}) collective-permute-start(bf16[2,3,24,8,256]{4,3,2,1,0:T(8,128)(2,1)S(1)} %constant_dynamic-update-slice_fusion.9), channel_id=1, source_target_pairs={{0,1},{1,2},{2,3},{4,5},{5,6},{6,7},{8,9},{9,10},{10,11},{12,13},{... | collective-permute-start | bytes 1769480 | tf_op jit(solution)/shard_map/ppermute | solution.py:21
  218.0 62.0 %collective-permute-start.9 = (f32[2,3,8,8,2]{3,2,1,4,0:T(8,128)}, f32[2,3,8,8,2]{3,2,1,4,0:T(8,128)}, u32[]{:S(2)}, u32[]{:S(2)}) collective-permute-start(f32[2,3,8,8,2]{3,2,1,4,0:T(8,128)} %pad_maximum_fusion.17), channel_id=1, source_target_pairs={{4,0},{5,1},{6,2},{7,3},{12,8},{13,9},{14,10},{15,11},{20,16},{21,... | collective-permute-start | bytes 9224 | tf_op jit(solution)/shard_map/ppermute | solution.py:24
  219.3 61.6 %collective-permute-start.8 = (f32[2,3,8,8,2]{3,2,1,4,0:T(8,128)}, f32[2,3,8,8,2]{3,2,1,4,0:T(8,128)}, u32[]{:S(2)}, u32[]{:S(2)}) collective-permute-start(f32[2,3,8,8,2]{3,2,1,4,0:T(8,128)} %pad_maximum_fusion.17), channel_id=1, source_target_pairs={{0,4},{1,5},{2,6},{3,7},{8,12},{9,13},{10,14},{11,15},{16,20},{17,... | collective-permute-start | bytes 9224 | tf_op jit(solution)/shard_map/ppermute | solution.py:21
  224.5 47.6 %collective-permute-start.17 = (f32[2,3,8,8,2]{3,2,1,4,0:T(8,128)}, f32[2,3,8,8,2]{3,2,1,4,0:T(8,128)}, u32[]{:S(2)}, u32[]{:S(2)}) collective-permute-start(f32[2,3,8,8,2]{3,2,1,4,0:T(8,128)} %pad_maximum_fusion.17), channel_id=1, source_target_pairs={{24,0},{0,8},{8,16},{16,24},{25,1},{1,9},{9,17},{17,25},{26,2},{2,... | collective-permute-start | bytes 9224 | tf_op jit(solution)/shard_map/ppermute | solution.py:32
  272.1 46.3 %copy-start.11 = (bf16[1,3,24,24,256]{4,3,2,1,0:T(8,128)(2,1)S(1)}, bf16[1,3,24,24,256]{4,3,2,1,0:T(8,128)(2,1)}, u32[]{:S(2)}) copy-start(bf16[1,3,24,24,256]{4,3,2,1,0:T(8,128)(2,1)} %get-tuple-element.677) | copy-start | bytes 2654212
  272.1 46.3 %copy-start.17 = (pred[192,1728]{1,0:T(32,128)(4,1)S(1)}, pred[192,1728]{1,0:T(32,128)(4,1)}, u32[]{:S(2)}) copy-start(pred[192,1728]{1,0:T(32,128)(4,1)} %and.550) | copy-start | bytes 995332
  272.1 46.3 %copy-start.22 = (bf16[192,256]{1,0:T(8,128)(2,1)S(1)}, bf16[192,256]{1,0:T(8,128)(2,1)}, u32[]{:S(2)}) copy-start(bf16[192,256]{1,0:T(8,128)(2,1)} %copy-done.21) | copy-start | bytes 294916
  272.1 20.0 %collective-permute-start.19 = (f32[2,3,8,8,2]{3,2,1,4,0:T(8,128)}, f32[2,3,8,8,2]{3,2,1,4,0:T(8,128)S(1)}, u32[]{:S(2)}, u32[]{:S(2)}) collective-permute-start(f32[2,3,8,8,2]{3,2,1,4,0:T(8,128)} %collective-permute-done.17), channel_id=1, source_target_pairs={{4,0},{5,1},{6,2},{7,3},{12,8},{13,9},{14,10},{15,11},{20,16},{21,... | collective-permute-start | bytes 9224 | tf_op jit(solution)/shard_map/ppermute | solution.py:24
  273.5 22.6 %collective-permute-start.18 = (f32[2,3,8,8,2]{3,2,1,4,0:T(8,128)}, f32[2,3,8,8,2]{3,2,1,4,0:T(8,128)S(1)}, u32[]{:S(2)}, u32[]{:S(2)}) collective-permute-start(f32[2,3,8,8,2]{3,2,1,4,0:T(8,128)} %collective-permute-done.17), channel_id=1, source_target_pairs={{0,4},{1,5},{2,6},{3,7},{8,12},{9,13},{10,14},{11,15},{16,20},{17,... | collective-permute-start | bytes 9224 | tf_op jit(solution)/shard_map/ppermute | solution.py:21
  277.5 13.2 %collective-permute-start.27 = (f32[2,3,8,8,2]{3,2,1,4,0:T(8,128)}, f32[2,3,8,8,2]{3,2,1,4,0:T(8,128)S(1)}, u32[]{:S(2)}, u32[]{:S(2)}) collective-permute-start(f32[2,3,8,8,2]{3,2,1,4,0:T(8,128)} %collective-permute-done.17), channel_id=1, source_target_pairs={{24,0},{0,8},{8,16},{16,24},{25,1},{1,9},{9,17},{17,25},{26,2},{2,... | collective-permute-start | bytes 9224 | tf_op jit(solution)/shard_map/ppermute | solution.py:32
  281.9 29.4 %collective-permute-start.11 = (f32[2,3,24,8,2]{2,3,4,1,0:T(8,128)S(1)}, f32[2,3,24,8,2]{2,3,4,1,0:T(8,128)S(1)}, u32[]{:S(2)}, u32[]{:S(2)}) collective-permute-start(f32[2,3,24,8,2]{2,3,4,1,0:T(8,128)S(1)} %pad_maximum_fusion.18), channel_id=1, source_target_pairs={{1,0},{2,1},{3,2},{5,4},{6,5},{7,6},{9,8},{10,9},{11,10},{13,12},{... | collective-permute-start | bytes 27656 | tf_op jit(solution)/shard_map/ppermute | solution.py:24
  283.8 28.8 %collective-permute-start.10 = (f32[2,3,24,8,2]{2,3,4,1,0:T(8,128)S(1)}, f32[2,3,24,8,2]{2,3,4,1,0:T(8,128)S(1)}, u32[]{:S(2)}, u32[]{:S(2)}) collective-permute-start(f32[2,3,24,8,2]{2,3,4,1,0:T(8,128)S(1)} %pad_maximum_fusion.18), channel_id=1, source_target_pairs={{0,1},{1,2},{2,3},{4,5},{5,6},{6,7},{8,9},{9,10},{10,11},{12,13},{... | collective-permute-start | bytes 27656 | tf_op jit(solution)/shard_map/ppermute | solution.py:21
  290.7 6.2 %copy-start.29 = (f32[2,3,8,8,2]{2,3,4,1,0:T(8,128)}, f32[2,3,8,8,2]{2,3,4,1,0:T(8,128)S(1)}, u32[]{:S(2)}) copy-start(f32[2,3,8,8,2]{2,3,4,1,0:T(8,128)S(1)} %copy.147) | copy-start | bytes 9220
  290.7 8.2 %collective-permute-start.29 = (f32[2,3,8,8,2]{3,2,1,4,0:T(8,128)S(1)}, f32[2,3,8,8,2]{3,2,1,4,0:T(8,128)S(1)}, u32[]{:S(2)}, u32[]{:S(2)}) collective-permute-start(f32[2,3,8,8,2]{3,2,1,4,0:T(8,128)S(1)} %collective-permute-done.27), channel_id=1, source_target_pairs={{4,0},{5,1},{6,2},{7,3},{12,8},{13,9},{14,10},{15,11},{20,16},{21,... | collective-permute-start | bytes 9224 | tf_op jit(solution)/shard_map/ppermute | solution.py:24
  292.1 10.6 %collective-permute-start.28 = (f32[2,3,8,8,2]{3,2,1,4,0:T(8,128)S(1)}, f32[2,3,8,8,2]{3,2,1,4,0:T(8,128)S(1)}, u32[]{:S(2)}, u32[]{:S(2)}) collective-permute-start(f32[2,3,8,8,2]{3,2,1,4,0:T(8,128)S(1)} %collective-permute-done.27), channel_id=1, source_target_pairs={{0,4},{1,5},{2,6},{3,7},{8,12},{9,13},{10,14},{11,15},{16,20},{17,... | collective-permute-start | bytes 9224 | tf_op jit(solution)/shard_map/ppermute | solution.py:21
  296.2 6.5 %copy-start.31 = (f32[2,3,8,8,2]{2,3,4,1,0:T(8,128)}, f32[2,3,8,8,2]{2,3,4,1,0:T(8,128)S(1)}, u32[]{:S(2)}) copy-start(f32[2,3,8,8,2]{2,3,4,1,0:T(8,128)S(1)} %copy.146) | copy-start | bytes 9220
  296.9 38.5 %collective-permute-start.21 = (f32[2,3,24,8,2]{2,3,4,1,0:T(8,128)}, f32[2,3,24,8,2]{2,3,4,1,0:T(8,128)}, u32[]{:S(2)}, u32[]{:S(2)}) collective-permute-start(f32[2,3,24,8,2]{2,3,4,1,0:T(8,128)} %pad_maximum_fusion.19), channel_id=1, source_target_pairs={{1,0},{2,1},{3,2},{5,4},{6,5},{7,6},{9,8},{10,9},{11,10},{13,12},{... | collective-permute-start | bytes 27656 | tf_op jit(solution)/shard_map/ppermute | solution.py:24
  298.9 13.7 %copy-start.23 = (f32[2,3,8,8,2]{2,3,4,1,0:T(8,128)}, f32[2,3,8,8,2]{2,3,4,1,0:T(8,128)S(1)}, u32[]{:S(2)}) copy-start(f32[2,3,8,8,2]{2,3,4,1,0:T(8,128)S(1)} %copy.152) | copy-start | bytes 9220
  299.0 40.4 %collective-permute-start.20 = (f32[2,3,24,8,2]{2,3,4,1,0:T(8,128)}, f32[2,3,24,8,2]{2,3,4,1,0:T(8,128)}, u32[]{:S(2)}, u32[]{:S(2)}) collective-permute-start(f32[2,3,24,8,2]{2,3,4,1,0:T(8,128)} %pad_maximum_fusion.19), channel_id=1, source_target_pairs={{0,1},{1,2},{2,3},{4,5},{5,6},{6,7},{8,9},{9,10},{10,11},{12,13},{... | collective-permute-start | bytes 27656 | tf_op jit(solution)/shard_map/ppermute | solution.py:21
  302.7 9.9 %copy-start.25 = (f32[2,3,8,8,2]{2,3,4,1,0:T(8,128)}, f32[2,3,8,8,2]{2,3,4,1,0:T(8,128)S(1)}, u32[]{:S(2)}) copy-start(f32[2,3,8,8,2]{2,3,4,1,0:T(8,128)S(1)} %copy.153) | copy-start | bytes 9220
  302.7 5.4 %collective-permute-start.37 = (f32[2,3,8,8,2]{3,2,1,4,0:T(8,128)S(1)}, f32[2,3,8,8,2]{3,2,1,4,0:T(8,128)}, u32[]{:S(2)}, u32[]{:S(2)}) collective-permute-start(f32[2,3,8,8,2]{3,2,1,4,0:T(8,128)S(1)} %collective-permute-done.27), channel_id=1, source_target_pairs={{24,0},{0,8},{8,16},{16,24},{25,1},{1,9},{9,17},{17,25},{26,2},{2,... | collective-permute-start | bytes 9224 | tf_op jit(solution)/shard_map/ppermute | solution.py:32
  303.4 9.2 %copy-start.27 = (f32[2,3,8,8,2]{2,3,4,1,0:T(8,128)}, f32[2,3,8,8,2]{2,3,4,1,0:T(8,128)S(1)}, u32[]{:S(2)}) copy-start(f32[2,3,8,8,2]{2,3,4,1,0:T(8,128)S(1)} %copy.151) | copy-start | bytes 9220
  308.1 42.4 %collective-permute-start.31 = (f32[2,3,24,8,2]{2,3,4,1,0:T(8,128)}, f32[2,3,24,8,2]{2,3,4,1,0:T(8,128)}, u32[]{:S(2)}, u32[]{:S(2)}) collective-permute-start(f32[2,3,24,8,2]{2,3,4,1,0:T(8,128)} %pad_maximum_fusion.20), channel_id=1, source_target_pairs={{1,0},{2,1},{3,2},{5,4},{6,5},{7,6},{9,8},{10,9},{11,10},{13,12},{... | collective-permute-start | bytes 27656 | tf_op jit(solution)/shard_map/ppermute | solution.py:24
  311.3 15.9 %collective-permute-start.39 = (f32[2,3,8,8,2]{3,2,1,4,0:T(8,128)}, f32[2,3,8,8,2]{3,2,1,4,0:T(8,128)}, u32[]{:S(2)}, u32[]{:S(2)}) collective-permute-start(f32[2,3,8,8,2]{3,2,1,4,0:T(8,128)} %collective-permute-done.37), channel_id=1, source_target_pairs={{4,0},{5,1},{6,2},{7,3},{12,8},{13,9},{14,10},{15,11},{20,16},{21,... | collective-permute-start | bytes 9224 | tf_op jit(solution)/shard_map/ppermute | solution.py:24
  312.6 19.3 %collective-permute-start.38 = (f32[2,3,8,8,2]{3,2,1,4,0:T(8,128)}, f32[2,3,8,8,2]{3,2,1,4,0:T(8,128)}, u32[]{:S(2)}, u32[]{:S(2)}) collective-permute-start(f32[2,3,8,8,2]{3,2,1,4,0:T(8,128)} %collective-permute-done.37), channel_id=1, source_target_pairs={{0,4},{1,5},{2,6},{3,7},{8,12},{9,13},{10,14},{11,15},{16,20},{17,... | collective-permute-start | bytes 9224 | tf_op jit(solution)/shard_map/ppermute | solution.py:21
  326.2 15.8 %copy-start.10 = (bf16[1,3,24,24,256]{4,3,2,1,0:T(8,128)(2,1)S(1)}, bf16[1,3,24,24,256]{4,3,2,1,0:T(8,128)(2,1)}, u32[]{:S(2)}) copy-start(bf16[1,3,24,24,256]{4,3,2,1,0:T(8,128)(2,1)} %get-tuple-element.675) | copy-start | bytes 2654212
  326.2 15.8 %copy-start.16 = (pred[192,1728]{1,0:T(32,128)(4,1)S(1)}, pred[192,1728]{1,0:T(32,128)(4,1)}, u32[]{:S(2)}) copy-start(pred[192,1728]{1,0:T(32,128)(4,1)} %and.555) | copy-start | bytes 995332
  327.2 23.3 %collective-permute-start.30 = (f32[2,3,24,8,2]{2,3,4,1,0:T(8,128)}, f32[2,3,24,8,2]{2,3,4,1,0:T(8,128)}, u32[]{:S(2)}, u32[]{:S(2)}) collective-permute-start(f32[2,3,24,8,2]{2,3,4,1,0:T(8,128)} %pad_maximum_fusion.20), channel_id=1, source_target_pairs={{0,1},{1,2},{2,3},{4,5},{5,6},{6,7},{8,9},{9,10},{10,11},{12,13},{... | collective-permute-start | bytes 27656 | tf_op jit(solution)/shard_map/ppermute | solution.py:21
  331.9 10.2 %copy-start.32 = (f32[2,3,8,8,2]{2,3,4,1,0:T(8,128)}, f32[2,3,8,8,2]{2,3,4,1,0:T(8,128)S(1)}, u32[]{:S(2)}) copy-start(f32[2,3,8,8,2]{2,3,4,1,0:T(8,128)S(1)} %copy.158) | copy-start | bytes 9220
  332.8 9.3 %copy-start.34 = (f32[2,3,8,8,2]{2,3,4,1,0:T(8,128)}, f32[2,3,8,8,2]{2,3,4,1,0:T(8,128)S(1)}, u32[]{:S(2)}) copy-start(f32[2,3,8,8,2]{2,3,4,1,0:T(8,128)S(1)} %copy.156) | copy-start | bytes 9220
  333.5 28.1 %collective-permute-start.41 = (f32[2,3,24,8,2]{2,3,4,1,0:T(8,128)}, f32[2,3,24,8,2]{2,3,4,1,0:T(8,128)}, u32[]{:S(2)}, u32[]{:S(2)}) collective-permute-start(f32[2,3,24,8,2]{2,3,4,1,0:T(8,128)} %pad_maximum_fusion.21), channel_id=1, source_target_pairs={{1,0},{2,1},{3,2},{5,4},{6,5},{7,6},{9,8},{10,9},{11,10},{13,12},{... | collective-permute-start | bytes 27656 | tf_op jit(solution)/shard_map/ppermute | solution.py:24
  335.4 26.2 %collective-permute-start.40 = (f32[2,3,24,8,2]{2,3,4,1,0:T(8,128)}, f32[2,3,24,8,2]{2,3,4,1,0:T(8,128)}, u32[]{:S(2)}, u32[]{:S(2)}) collective-permute-start(f32[2,3,24,8,2]{2,3,4,1,0:T(8,128)} %pad_maximum_fusion.21), channel_id=1, source_target_pairs={{0,1},{1,2},{2,3},{4,5},{5,6},{6,7},{8,9},{9,10},{10,11},{12,13},{... | collective-permute-start | bytes 27656 | tf_op jit(solution)/shard_map/ppermute | solution.py:21
  349.5 3.6 copy-start.9
  349.5 3.6 copy-start.15
  (44 other events, 76.2 us)
where the time goes:
time: 378 us; the launch traced here: 374 us
  starting transfers between devices  108 us (29%)
  local copies, waits for them, and re-layouts  95.8 us (25%)
  matrix products  76.1 us (20%)
  other arithmetic  37.8 us (10%)
  waiting for transfers between devices  34.5 us (9%)
  blocking collectives  18.4 us (5%)
    ppermute x18, starting transfers between devices, padded(): lax.ppermute(lax.slice_in_dim(block, block.shape[dim] - width, None, axis...  67.5 us
    ppermute x18, starting transfers between devices, padded(): lax.ppermute(lax.slice_in_dim(block, 0, width, axis=dim), axis, backward)  34.3 us
    mul x16, local copies, waits for them, and re-layouts, forward_block(): scores = scores.reshape(query_total, frames, -1) * scale_factor  30.5 us
    ppermute x18, waiting for transfers between devices, padded(): lax.ppermute(lax.slice_in_dim(block, 0, width, axis=dim), axis, backward)  27.2 us
    and x36, local copies, waits for them, and re-layouts, full_mask(): joined = frame_table[:, None, :, None] & spatial[None, :, None, :]  18.7 us
    all_gather x1, blocking collectives, shards(): every_frame = lax.all_gather(key_pair, 'ta', axis=1, tiled=True)  18.4 us
    dot_general x8, matrix products, key_grads(): jnp.einsum('kq,qd->kd', dscore, query_head, preferred_element_type=jnp.fl...  15.7 us
    dot_general x8, matrix products, query_grad_block(): jnp.dot(dscore, key_head, preferred_element_type=jnp.float32) * scale_factor  11.5 us
  transfers between devices with their start and end apart: 42, of which 9 were waited for; matrix products, arithmetic and copies ran while one was open for 29% of the time, Pallas kernels for 0%

commit v1 on v0

v1 whole, which is shorter than its diff:
```python
import functools
import math

import jax
import jax.numpy as jnp
import numpy as np
from jax import lax
from jax.experimental import pallas as pl
from jax.experimental.pallas import tpu as pltpu
from jax.sharding import PartitionSpec as P

DH = 128
HEADS = 2
TILE_T = 6
TILE_H = 8
TILE_W = 8

NEGATIVE = -1e30
SCALE = DH**-0.5
SCALE_LOG2 = SCALE * math.log2(math.e)
F32 = jnp.float32
BF16 = jnp.bfloat16
VMEM_LIMIT = 48 * 1024 * 1024


def near_pairs(count):
    return [(i, i ^ 1) for i in range(count)]


def far_pairs(count):
    pairs = []
    for i in range(count):
        j = i + 1 if i % 2 else i - 1
        pairs.append((i, j if 0 <= j < count else i))
    return pairs


def far_exists(axis, count):
    pos = lax.axis_index(axis)
    other = jnp.where(pos % 2 == 1, pos + 1, pos - 1)
    return (other >= 0) & (other < count)


def side_pairs(count):
    sides = []
    if count > 1:
        sides.append(near_pairs(count))
    if count > 2:
        sides.append(far_pairs(count))
    return sides


def rope_table(frame_total, row_total, col_total):
    time_dims = DH // 8
    space_dims = (DH - time_dims) // 2
    slower = 256.0 ** (-np.arange(0, time_dims, 2) / time_dims)
    faster = 256.0 ** (-np.arange(0, space_dims, 2) / space_dims)
    starts = (0, time_dims, time_dims + space_dims)
    pieces = []
    for total, rates, start in zip(
        (frame_total, row_total, col_total), (slower, faster, faster), starts
    ):
        padded = -(-total // 8) * 8
        piece = np.zeros((3, padded, DH), np.float32)
        angles = np.arange(padded)[:, None] * rates[None, :]
        stop = start + 2 * len(rates)
        piece[0, :, start:stop:2] = np.cos(angles)
        piece[0, :, start + 1 : stop : 2] = np.cos(angles)
        piece[1, :, start:stop:2] = -np.sin(angles)
        piece[2, :, start + 1 : stop : 2] = np.sin(angles)
        pieces.append(piece)
    return tuple(pieces)


def local_table(plane, time_ref, row_ref, col_ref, frames, rows, cols):
    frame_lo = lax.axis_index("ta") * frames
    row_lo = pl.multiple_of(lax.axis_index("ha") * rows, rows)
    col_lo = pl.multiple_of(lax.axis_index("wa") * cols, cols)
    row_part = row_ref[plane, pl.ds(row_lo, rows), :]
    col_part = col_ref[plane, pl.ds(col_lo, cols), :]
    grids = []
    for i in range(frames):
        lead = row_part + time_ref[plane, pl.ds(frame_lo + i, 1), :]
        grid = lead[:, None, :] + col_part[None, :, :]
        grids.append(grid.reshape(rows * cols, DH))
    return jnp.concatenate(grids, axis=0)


def turn(x, cosine, sin_even, sin_odd, sign):
    follow = pltpu.roll(x, DH - 1, 1)
    lead = pltpu.roll(x, 1, 1)
    return x * cosine + sign * (follow * sin_even + lead * sin_odd)


def head_slice(head):
    return slice(head * DH, (head + 1) * DH)


def rotate_kernel(dims, q_ref, k_ref, v_ref, g_ref, tt_ref, rt_ref, ct_ref, kv_ref, qg_ref):
    tables = [local_table(plane, tt_ref, rt_ref, ct_ref, *dims) for plane in range(3)]
    for head in range(HEADS):
        cut = head_slice(head)
        kv_ref[0, :, cut] = turn(k_ref[:, cut].astype(F32), *tables, 1.0).astype(BF16)
        qg_ref[0, :, cut] = turn(q_ref[:, cut].astype(F32), *tables, 1.0).astype(BF16)
    kv_ref[1] = v_ref[...]
    qg_ref[1] = g_ref[...]


def dot_nt(a, b):
    return lax.dot_general(a, b, (((1,), (1,)), ((), ())), preferred_element_type=F32)


def dot_nn(a, b):
    return lax.dot_general(a, b, (((1,), (0,)), ((), ())), preferred_element_type=F32)


def dot_tn(a, b):
    return lax.dot_general(a, b, (((0,), (0,)), ((), ())), preferred_element_type=F32)


def group_bias(flags, sizes):
    valid = None
    for axis, is_far in zip(("ha", "wa"), flags):
        if is_far:
            here = far_exists(axis, sizes[axis])
            valid = here if valid is None else valid & here
    return None if valid is None else jnp.where(valid, 0.0, NEGATIVE).astype(F32)


def forward_kernel(groups, sizes, cells, with_first, *refs):
    tile_count = sum(len(members) for _, members in groups)
    qa_ref, qb_ref = refs[0], refs[1]
    kv_refs = refs[2 : 2 + tile_count]
    rest = refs[2 + tile_count :]
    if with_first:
        first_ref, oa_ref, ob_ref, stat_ref, key_buf, value_buf = rest
    else:
        oa_ref, ob_ref, stat_ref, key_buf, value_buf = rest
    at = 0
    spans = []
    for flags, members in groups:
        begin = at
        for member in members:
            key_buf[at : at + cells] = kv_refs[member][0]
            value_buf[at : at + cells] = kv_refs[member][1]
            at += cells
        spans.append((begin, at, group_bias(flags, sizes)))
    lane = lax.broadcasted_iota(jnp.int32, (2 * cells, DH), 1)
    stat = jnp.zeros((2 * cells, DH), F32)
    for head in range(HEADS):
        cut = head_slice(head)
        query = jnp.concatenate([qa_ref[0, :, cut], qb_ref[0, :, cut]], axis=0)
        grad = jnp.concatenate([qa_ref[1, :, cut], qb_ref[1, :, cut]], axis=0)
        scores = [dot_nt(query, key_buf[lo:hi, cut]) for lo, hi, _ in spans]
        best = None
        for raw, (_, _, bias) in zip(scores, spans):
            top = jnp.max(raw, axis=1, keepdims=True) * SCALE_LOG2
            if bias is not None:
                top = top + bias
            best = top if best is None else jnp.maximum(best, top)
        total = None
        out = None
        for raw, (lo, hi, bias) in zip(scores, spans):
            shift = best if bias is None else best - bias
            weights = jnp.exp2(raw * SCALE_LOG2 - shift)
            part = jnp.sum(weights, axis=1, keepdims=True)
            piece = dot_nn(weights.astype(BF16), value_buf[lo:hi, cut])
            total = part if total is None else total + part
            out = piece if out is None else out + piece
        out = out * (1.0 / total)
        dotted = jnp.sum(out * grad.astype(F32), axis=1, keepdims=True)
        out = out.astype(BF16)
        oa_ref[:, cut] = out[:cells]
        ob_ref[:, cut] = out[cells:]
        stat = jnp.where(lane == head, best + jnp.log2(total), stat)
        stat = jnp.where(lane == HEADS + head, dotted, stat)
    flipped = stat.T[: stat_ref.shape[-2]]
    if with_first:
        stat_ref[0] = first_ref[...]
        stat_ref[1] = flipped
    else:
        stat_ref[...] = flipped


def merged_stats(own_ref, s1_ref, s2_ref, s3_ref, half, cells):
    parts = [
        own_ref[half],
        s1_ref[1 - half],
        pltpu.roll(s2_ref[half], cells, 1),
        pltpu.roll(s3_ref[1 - half], cells, 1),
    ]
    top = functools.reduce(jnp.maximum, parts)
    shares = [jnp.exp2(part - top) for part in parts]
    total = functools.reduce(jnp.add, shares)
    lse = top + jnp.log2(total)
    shares = [share / total for share in shares]
    rows_lse = [lse[head : head + 1] for head in range(HEADS)]
    rows_delta = []
    for head in range(HEADS):
        terms = [
            share[head : head + 1] * part[HEADS + head : HEADS + head + 1]
            for share, part in zip(shares, parts)
        ]
        rows_delta.append(functools.reduce(jnp.add, terms))
    return rows_lse, rows_delta, shares


def backward_kernel(groups, grid_rows, grid_cols, sizes, cells, *refs):
    tile_count = sum(len(members) for _, members in groups)
    qg_refs = refs[:4]
    kv_refs = refs[4 : 4 + tile_count]
    rest = refs[4 + tile_count :]
    stat_refs = rest[:4]
    dq_refs = rest[4:8]
    share_ref = rest[8]
    col_refs = rest[9 : 9 + grid_cols]
    half_rows = 2 * cells
    halves = [(qg_refs[0], qg_refs[1]), (qg_refs[2], qg_refs[3])]
    stats = [merged_stats(*stat_refs, half, cells) for half in range(2)]

    own_shares = stats[0][2]
    rows = [own_shares[d][head : head + 1] for head in range(HEADS) for d in range(4)]
    wide = jnp.concatenate(rows + [jnp.zeros((DH - len(rows), half_rows), F32)], axis=0)
    share_ref[...] = wide.T[:cells]

    for head in range(HEADS):
        cut = head_slice(head)
        queries = [
            jnp.concatenate([a[0, :, cut], b[0, :, cut]], axis=0) for a, b in halves
        ]
        grads = [jnp.concatenate([a[1, :, cut], b[1, :, cut]], axis=0) for a, b in halves]
        dq = [None, None]
        for flags, members in groups:
            bias = group_bias(flags, sizes)
            for member in members:
                row, col = member // grid_cols, member % grid_cols
                key = kv_refs[member][0, :, cut]
                value = kv_refs[member][1, :, cut]
                dk, dv = None, None
                for half in range(2):
                    lse = stats[half][0][head]
                    delta = stats[half][1][head]
                    if bias is not None:
                        lse = lse - bias
                    raw = dot_nt(key, queries[half])
                    probs = jnp.exp2(raw * SCALE_LOG2 - lse)
                    prob_grad = dot_nt(value, grads[half])
                    dscore = (probs * (prob_grad - delta)).astype(BF16)
                    dv_part = dot_nn(probs.astype(BF16), grads[half])
                    dk_part = dot_nn(dscore, queries[half])
                    dq_part = dot_tn(dscore, key)
                    dv = dv_part if dv is None else dv + dv_part
                    dk = dk_part if dk is None else dk + dk_part
                    dq[half] = dq_part if dq[half] is None else dq[half] + dq_part
                col_refs[col][row, 0, :, cut] = (dk * SCALE).astype(BF16)
                col_refs[col][row, 1, :, cut] = dv.astype(BF16)
        for half in range(2):
            scaled = (dq[half] * SCALE).astype(BF16)
            dq_refs[2 * half][:, cut] = scaled[:cells]
            dq_refs[2 * half + 1][:, cut] = scaled[cells:]


def finish_query_kernel(dims, *refs):
    o_refs, dq_refs = refs[:4], refs[4:8]
    share_ref, tt_ref, rt_ref, ct_ref, out_ref, dq_out = refs[8:]
    tables = [local_table(plane, tt_ref, rt_ref, ct_ref, *dims) for plane in range(3)]
    for head in range(HEADS):
        cut = head_slice(head)
        out, dq = None, None
        for d in range(4):
            weight = share_ref[:, 4 * head + d : 4 * head + d + 1]
            piece = o_refs[d][:, cut].astype(F32) * weight
            out = piece if out is None else out + piece
            grad = dq_refs[d][:, cut].astype(F32)
            dq = grad if dq is None else dq + grad
        out_ref[:, cut] = out.astype(BF16)
        dq_out[:, cut] = turn(dq, *tables, -1.0).astype(BF16)


def finish_key_kernel(dims, cols, rows, *refs):
    col_refs, row_refs = refs[:cols], refs[cols : cols + rows]
    tt_ref, rt_ref, ct_ref, dk_out, dv_out = refs[cols + rows :]
    tables = [local_table(plane, tt_ref, rt_ref, ct_ref, *dims) for plane in range(3)]
    for head in range(HEADS):
        cut = head_slice(head)
        sums = []
        for which in range(2):
            terms = [ref[0, which, :, cut].astype(F32) for ref in col_refs]
            terms += [ref[which, :, cut].astype(F32) for ref in row_refs]
            sums.append(functools.reduce(jnp.add, terms))
        dk_out[:, cut] = turn(sums[0], *tables, -1.0).astype(BF16)
        dv_out[:, cut] = sums[1].astype(BF16)


def call(kernel, out_shape, args, flops=0, exps=0, scratch=()):
    shapes = jax.tree.leaves(out_shape)
    moved = sum(math.prod(x.shape) * x.dtype.itemsize for x in list(args) + shapes)
    return pl.pallas_call(
        kernel,
        out_shape=out_shape,
        scratch_shapes=list(scratch),
        compiler_params=pltpu.CompilerParams(vmem_limit_bytes=VMEM_LIMIT),
        cost_estimate=pl.CostEstimate(flops=flops, bytes_accessed=moved, transcendentals=exps),
    )(*args)


def shards(query_in, key_in, value_in, cotangent):
    frames, rows, cols, chan = query_in.shape
    cells = frames * rows * cols
    sizes = {axis: lax.axis_size(axis) for axis in ("ta", "ha", "wa")}
    assert rows == TILE_H and cols == TILE_W and chan == HEADS * DH
    assert TILE_T % frames == 0 and frames * sizes["ta"] <= 2 * TILE_T
    assert sizes["ta"] == 4 and sizes["ha"] % 2 == 0 and sizes["wa"] % 2 == 0
    dims = (frames, rows, cols)
    tables = tuple(
        jnp.asarray(x)
        for x in rope_table(frames * sizes["ta"], rows * sizes["ha"], cols * sizes["wa"])
    )
    flat = [x.reshape(cells, chan) for x in (query_in, key_in, value_in, cotangent)]
    pair = jax.ShapeDtypeStruct((2, cells, chan), BF16)
    plain = jax.ShapeDtypeStruct((cells, chan), BF16)

    with jax.named_scope("rotate"):
        kv, qg = call(
            functools.partial(rotate_kernel, dims), (pair, pair), (*flat, *tables)
        )

    def other_frames(x, distance):
        return lax.ppermute(x, "ta", [(i, i ^ distance) for i in range(sizes["ta"])])

    row_sides = side_pairs(sizes["ha"])
    col_sides = side_pairs(sizes["wa"])
    with jax.named_scope("halo"):
        kv_rows = [kv] + [lax.ppermute(kv, "ha", pairs) for pairs in row_sides]
        qg2 = other_frames(qg, 2)
        qg1 = other_frames(qg, 1)
        tiles = []
        for block in kv_rows:
            tiles += [block] + [lax.ppermute(block, "wa", pairs) for pairs in col_sides]
        qg3 = other_frames(qg2, 1)
    grid_rows, grid_cols = 1 + len(row_sides), 1 + len(col_sides)
    groups = {}
    for row in range(grid_rows):
        for col in range(grid_cols):
            groups.setdefault((row == 2, col == 2), []).append(row * grid_cols + col)
    groups = list(groups.items())

    key_count = len(tiles) * cells
    product = 2 * 2 * cells * key_count * DH * HEADS
    keys = [pltpu.VMEM((key_count, chan), BF16)] * 2
    stat_shape = (8, 2 * cells)

    def forward(qa, qb, first):
        args = (qa, qb, *tiles) + (() if first is None else (first,))
        stat = stat_shape if first is None else (2, *stat_shape)
        return call(
            functools.partial(forward_kernel, groups, sizes, cells, first is not None),
            (plain, plain, jax.ShapeDtypeStruct(stat, F32)),
            args,
            2 * product,
            2 * cells * key_count * HEADS,
            keys,
        )

    with jax.named_scope("attend"):
        o0, o2, first = forward(qg, qg2, None)
        o1, o3, stat = forward(qg1, qg3, first)
    with jax.named_scope("merge"):
        stats = [stat] + [other_frames(stat, d) for d in (1, 2, 3)]
        outs = [o0] + [other_frames(o, d) for d, o in ((1, o1), (2, o2), (3, o3))]

    with jax.named_scope("gradients"):
        results = call(
            functools.partial(backward_kernel, groups, grid_rows, grid_cols, sizes, cells),
            (
                *[plain] * 4,
                jax.ShapeDtypeStruct((cells, DH), F32),
                *[jax.ShapeDtypeStruct((grid_rows, 2, cells, chan), BF16)] * grid_cols,
            ),
            (qg, qg2, qg1, qg3, *tiles, *stats),
            10 * product,
            4 * cells * key_count * HEADS,
        )
    d0, d2, d1, d3, shares = results[:5]
    by_col = results[5:]
    with jax.named_scope("return"):
        col_parts = [by_col[0]] + [
            lax.ppermute(x, "wa", pairs) for x, pairs in zip(by_col[1:], col_sides)
        ]
        dqs = [d0] + [other_frames(x, d) for d, x in ((1, d1), (2, d2), (3, d3))]
        row_parts = []
        for row, pairs in enumerate(row_sides, start=1):
            partial_sum = sum(x[row].astype(F32) for x in col_parts).astype(BF16)
            row_parts.append(lax.ppermute(partial_sum, "ha", pairs))

    with jax.named_scope("finish"):
        attended, grad_query = call(
            functools.partial(finish_query_kernel, dims),
            (plain, plain),
            (*outs, *dqs, shares, *tables),
        )
        grad_key, grad_value = call(
            functools.partial(finish_key_kernel, dims, grid_cols, len(row_parts)),
            (plain, plain),
            (*col_parts, *row_parts, *tables),
        )
    return tuple(x.reshape(query_in.shape) for x in (attended, grad_query, grad_key, grad_value))


def solution(mesh):
    spec = P("ta", "ha", "wa", None)
    return jax.shard_map(
        shards, mesh=mesh, in_specs=(spec,) * 4, out_specs=(spec,) * 4, check_vma=False
    )
```

time: 378 us -> 72.9 us (0.19)
  local copies, waits for them, and re-layouts: 95.8 us -> 5.85 us
  starting transfers between devices: 108 us -> 30.7 us
  matrix products: 76.1 us -> 0 us
  other arithmetic: 37.8 us -> 0.07 us
  blocking collectives: 18.4 us -> 0 us
  Pallas kernels: 0 us -> 13.7 us
  waiting for transfers between devices: 34.5 us -> 21.4 us
    ppermute x42 -> x20, starting transfers between devices: 108 us -> 30.7 us  [the longest x12 15.8 us: other_frames(): lax.ppermute(x, 'ta', [(i, i ^ distance) for i in range(sizes['ta'])])]
    dot_general x60 -> x0, matrix products: 76.1 us -> none  [the longest x8 15.7 us: key_grads(): jnp.einsum('kq,qd->kd', dscore, query_head, preferred_element_type=jnp.fl...]
    mul x16 -> x0, local copies, waits for them, and re-layouts: 30.5 us -> none  [forward_block(): scores = scores.reshape(query_total, frames, -1) * scale_factor]
    slice x44 -> x0, local copies, waits for them, and re-layouts: 25.6 us -> none  [the longest x4 9.98 us: forward_visit(): key_block[1].reshape(-1, chan_count)]
    and x37 -> x0, local copies, waits for them, and re-layouts: 19 us -> none  [the longest x36 18.7 us: full_mask(): joined = frame_table[:, None, :, None] & spatial[None, :, None, :]]
    all_gather x1 -> x0, blocking collectives: 18.4 us -> none  [shards(): every_frame = lax.all_gather(key_pair, 'ta', axis=1, tiled=True)]
    pallas_call x0 -> x6, Pallas kernels: none -> 13.7 us  [call(): pl.pallas_call(kernel, out_shape=out_shape, scratch_shapes=list(scratch),...]
    ppermute x42 -> x20, waiting for transfers between devices: 34.5 us -> 21.4 us  [the longest x12 15.6 us: other_frames(): lax.ppermute(x, 'ta', [(i, i ^ distance) for i in range(sizes['ta'])])]
  transfers between devices with their start and end apart: 42 -> 20, of which waited for: 9 -> 10; matrix products, arithmetic and copies ran while one was open for 29% -> 0% of each run, Pallas kernels for 0% -> 4%
where the time goes in v1:
time: 72.9 us; the launch traced here: 72.4 us
  starting transfers between devices  30.7 us (42%)
  waiting for transfers between devices  21.4 us (29%)
  Pallas kernels  13.7 us (19%)
  local copies, waits for them, and re-layouts  5.85 us (8%)
  between operations  0.75 us (1%)
    ppermute x12, starting transfers between devices, other_frames(): lax.ppermute(x, 'ta', [(i, i ^ distance) for i in range(sizes['ta'])])  15.8 us
    ppermute x12, waiting for transfers between devices, other_frames(): lax.ppermute(x, 'ta', [(i, i ^ distance) for i in range(sizes['ta'])])  15.6 us
    pallas_call x6, Pallas kernels, call(): pl.pallas_call(kernel, out_shape=out_shape, scratch_shapes=list(scratch),...  13.7 us
    ppermute x4, starting transfers between devices, shards(): tiles += [block] + [lax.ppermute(block, 'wa', pairs) for pairs in col_sides]  6.86 us
    ppermute x2, starting transfers between devices, shards(): lax.ppermute(x, 'wa', pairs)  5.88 us
    unnamed x20, local copies, waits for them, and re-layouts  5.85 us
    ppermute x2, waiting for transfers between devices, shards(): lax.ppermute(x, 'wa', pairs)  4.5 us
    ppermute x1, starting transfers between devices, shards(): kv_rows = [kv] + [lax.ppermute(kv, 'ha', pairs) for pairs in row_sides]  2.11 us
  transfers between devices with their start and end apart: 20, of which 10 were waited for; matrix products, arithmetic and copies ran while one was open for 0% of the time, Pallas kernels for 4%

profile of v1, /device:TPU:1, one launch (start us, length us, event | category | flops | bytes accessed | tf_op | source)
XLA Modules:
  0.0 72.4 jit_solution(8467468063789883322)
XLA Ops:
  0.6 0.0 copy-start
  0.6 0.8 %copy-done = f32[3,32,128]{2,1,0:T(8,128)S(1)} copy-done((f32[3,32,128]{2,1,0:T(8,128)S(1)}, f32[3,32,128]{2,1,0:T(8,128)}, u32[]{:S(2)}) %copy-start) | copy-done | bytes 49176
  1.4 0.0 copy-start.2
  1.4 0.7 %copy-done.2 = f32[3,16,128]{2,1,0:T(8,128)S(1)} copy-done((f32[3,16,128]{2,1,0:T(8,128)S(1)}, f32[3,16,128]{2,1,0:T(8,128)}, u32[]{:S(2)}) %copy-start.2) | copy-done | bytes 24600
  2.2 0.0 copy-start.4
  2.2 0.7 %copy-done.4 = f32[3,16,128]{2,1,0:T(8,128)S(1)} copy-done((f32[3,16,128]{2,1,0:T(8,128)S(1)}, f32[3,16,128]{2,1,0:T(8,128)}, u32[]{:S(2)}) %copy-start.4) | copy-done | bytes 24600
  2.9 0.0 copy-start.6
  2.9 0.9 %copy-done.6 = bf16[3,8,8,256]{3,2,1,0:T(8,128)(2,1)S(1)} copy-done((bf16[3,8,8,256]{3,2,1,0:T(8,128)(2,1)S(1)}, bf16[3,8,8,256]{3,2,1,0:T(8,128)(2,1)}, u32[]{:S(2)}) %copy-start.6) | copy-done | bytes 98328
  3.8 0.0 copy-start.7
  3.8 0.9 %copy-done.7 = bf16[3,8,8,256]{3,2,1,0:T(8,128)(2,1)S(1)} copy-done((bf16[3,8,8,256]{3,2,1,0:T(8,128)(2,1)S(1)}, bf16[3,8,8,256]{3,2,1,0:T(8,128)(2,1)}, u32[]{:S(2)}) %copy-start.7) | copy-done | bytes 98328
  4.7 0.0 copy-start.8
  4.7 0.9 %copy-done.8 = bf16[3,8,8,256]{3,2,1,0:T(8,128)(2,1)S(1)} copy-done((bf16[3,8,8,256]{3,2,1,0:T(8,128)(2,1)S(1)}, bf16[3,8,8,256]{3,2,1,0:T(8,128)(2,1)}, u32[]{:S(2)}) %copy-start.8) | copy-done | bytes 98328
  5.6 0.0 copy-start.9
  5.6 0.9 %copy-done.9 = bf16[3,8,8,256]{3,2,1,0:T(8,128)(2,1)S(1)} copy-done((bf16[3,8,8,256]{3,2,1,0:T(8,128)(2,1)S(1)}, bf16[3,8,8,256]{3,2,1,0:T(8,128)(2,1)}, u32[]{:S(2)}) %copy-start.9) | copy-done | bytes 98328
  6.5 0.2 rotate.1
  6.7 2.1 %collective-permute-start.3 = (bf16[2,192,256]{2,1,0:T(8,128)(2,1)S(1)}, bf16[2,192,256]{2,1,0:T(8,128)(2,1)S(1)}, u32[]{:S(2)}, u32[]{:S(2)}) collective-permute-start(bf16[2,192,256]{2,1,0:T(8,128)(2,1)S(1)} %get-tuple-element.25.refs_2_.refs_4_), channel_id=1, source_target_pairs={{0,4},{4,0},{1,5},{5,1},{2,6},{6,2},{3,7},{7,3},{8,12},{12,8},{9,1... | collective-permute-start | bytes 589832 | tf_op jit(solution)/shard_map/halo/ppermute | solution.py:334
  8.8 2.3 %collective-permute-start = (bf16[2,192,256]{2,1,0:T(8,128)(2,1)S(1)}, bf16[2,192,256]{2,1,0:T(8,128)(2,1)S(1)}, u32[]{:S(2)}, u32[]{:S(2)}) collective-permute-start(bf16[2,192,256]{2,1,0:T(8,128)(2,1)S(1)} %get-tuple-element.24.refs_0_), channel_id=1, source_target_pairs={{0,16},{8,24},{16,0},{24,8},{1,17},{9,25},{17,1},{25,9},{2,18},{10... | collective-permute-start | bytes 589832 | tf_op jit(solution)/shard_map/halo/ppermute | solution.py:329
  11.1 4.3 %collective-permute-start.2 = (bf16[2,192,256]{2,1,0:T(8,128)(2,1)S(1)}, bf16[2,192,256]{2,1,0:T(8,128)(2,1)S(1)}, u32[]{:S(2)}, u32[]{:S(2)}) collective-permute-start(bf16[2,192,256]{2,1,0:T(8,128)(2,1)S(1)} %get-tuple-element.25.refs_2_.refs_4_), channel_id=1, source_target_pairs={{0,0},{1,2},{2,1},{3,3},{4,4},{5,6},{6,5},{7,7},{8,8},{9,10},{10,9... | collective-permute-start | bytes 589832 | tf_op jit(solution)/shard_map/halo/ppermute | solution.py:339
  15.4 0.1 collective-permute-start.1
  15.4 0.0 collective-permute-done.3.refs_5_.refs_7_
  15.4 2.5 %collective-permute-start.5 = (bf16[2,192,256]{2,1,0:T(8,128)(2,1)S(1)}, bf16[2,192,256]{2,1,0:T(8,128)(2,1)S(1)}, u32[]{:S(2)}, u32[]{:S(2)}) collective-permute-start(bf16[2,192,256]{2,1,0:T(8,128)(2,1)S(1)} %collective-permute-done.3.refs_5_.refs_7_), channel_id=1, source_target_pairs={{0,0},{1,2},{2,1},{3,3},{4,4},{5,6},{6,5},{7,7},{8,8},{9,10},{10,9... | collective-permute-start | bytes 589832 | tf_op jit(solution)/shard_map/halo/ppermute | solution.py:339
  17.9 0.1 collective-permute-start.4
  18.0 1.7 %collective-permute-done.refs_1_ = bf16[2,192,256]{2,1,0:T(8,128)(2,1)S(1)} collective-permute-done((bf16[2,192,256]{2,1,0:T(8,128)(2,1)S(1)}, bf16[2,192,256]{2,1,0:T(8,128)(2,1)S(1)}, u32[]{:S(2)}, u32[]{:S(2)}) %collective-permute-start) | collective-permute-done | bytes 196640 | tf_op jit(solution)/shard_map/halo/ppermute | solution.py:329
  19.7 1.5 %collective-permute-start.6 = (bf16[2,192,256]{2,1,0:T(8,128)(2,1)S(1)}, bf16[2,192,256]{2,1,0:T(8,128)(2,1)S(1)}, u32[]{:S(2)}, u32[]{:S(2)}) collective-permute-start(bf16[2,192,256]{2,1,0:T(8,128)(2,1)S(1)} %get-tuple-element.24.refs_0_), channel_id=1, source_target_pairs={{0,8},{8,0},{16,24},{24,16},{1,9},{9,1},{17,25},{25,17},{2,10},{10... | collective-permute-start | bytes 589832 | tf_op jit(solution)/shard_map/halo/ppermute | solution.py:329
  21.1 0.0 collective-permute-done.2.refs_4_.refs_6_
  21.1 0.0 collective-permute-start.7
  21.1 0.0 collective-permute-done.1.refs_3_.refs_5_
  21.2 1.3 %collective-permute-done.5.refs_7_.refs_9_ = bf16[2,192,256]{2,1,0:T(8,128)(2,1)S(1)} collective-permute-done((bf16[2,192,256]{2,1,0:T(8,128)(2,1)S(1)}, bf16[2,192,256]{2,1,0:T(8,128)(2,1)S(1)}, u32[]{:S(2)}, u32[]{:S(2)}) %collective-permute-start.5) | collective-permute-done | bytes 196640 | tf_op jit(solution)/shard_map/halo/ppermute | solution.py:339
  22.4 0.0 collective-permute-done.4.refs_6_.refs_8_
  22.4 2.0 %attend.2 = (bf16[192,256]{1,0:T(8,128)(2,1)S(1)}, bf16[192,256]{1,0:T(8,128)(2,1)S(1)}, f32[8,384]{1,0:T(8,128)S(1)}) custom-call(bf16[2,192,256]{2,1,0:T(8,128)(2,1)S(1)} %get-tuple-element.24.refs_0_, bf16[2,192,256]{2,1,0:T(8,128)(2,1)S(1)} %collective-permute-done.refs_1_, bf16[2,192,256]{2,1,0:T(8,128)(2,1)S(1)} %get-tuple-element.25.refs_2_.refs_4_, ...), custom_call_target="tpu_custom_call" | custom-call | flops 452984832 | bytes 1781760 | tf_op jit(solution)/shard_map/attend/pallas_call | solution.py:298
  24.4 0.5 collective-permute-done.6.refs_0_.refs_2_
  24.9 4.2 %collective-permute-done.7.refs_1_.refs_3_ = bf16[2,192,256]{2,1,0:T(8,128)(2,1)S(1)} collective-permute-done((bf16[2,192,256]{2,1,0:T(8,128)(2,1)S(1)}, bf16[2,192,256]{2,1,0:T(8,128)(2,1)S(1)}, u32[]{:S(2)}, u32[]{:S(2)}) %collective-permute-start.7) | collective-permute-done | bytes 196640 | tf_op jit(solution)/shard_map/halo/ppermute | solution.py:329
  29.1 2.0 %attend.3 = (bf16[192,256]{1,0:T(8,128)(2,1)S(1)}, bf16[192,256]{1,0:T(8,128)(2,1)S(1)}, f32[2,8,384]{2,1,0:T(8,128)S(1)}) custom-call(bf16[2,192,256]{2,1,0:T(8,128)(2,1)S(1)} %collective-permute-done.6.refs_0_.refs_2_, bf16[2,192,256]{2,1,0:T(8,128)(2,1)S(1)} %collective-permute-done.7.refs_1_.refs_3_, ...), custom_call_target="tpu_custom_call" | custom-call | flops 452984832 | bytes 1806336 | tf_op jit(solution)/shard_map/attend/pallas_call | solution.py:298
  31.1 5.1 %collective-permute-start.13 = (f32[2,8,384]{2,1,0:T(8,128)S(1)}, f32[2,8,384]{2,1,0:T(8,128)S(1)}, u32[]{:S(2)}, u32[]{:S(2)}) collective-permute-start(f32[2,8,384]{2,1,0:T(8,128)S(1)} %get-tuple-element.31.refs_10_), channel_id=1, source_target_pairs={{0,24},{8,16},{16,8},{24,0},{1,25},{9,17},{17,9},{25,1},{2,26},{10... | collective-permute-start | bytes 73736 | tf_op jit(solution)/shard_map/merge/ppermute | solution.py:329
  36.1 0.0 collective-permute-start.12
  36.1 0.4 collective-permute-start.11
  36.5 0.9 %collective-permute-done.13.refs_13_ = f32[2,8,384]{2,1,0:T(8,128)S(1)} collective-permute-done((f32[2,8,384]{2,1,0:T(8,128)S(1)}, f32[2,8,384]{2,1,0:T(8,128)S(1)}, u32[]{:S(2)}, u32[]{:S(2)}) %collective-permute-start.13) | collective-permute-done | bytes 24608 | tf_op jit(solution)/shard_map/merge/ppermute | solution.py:329
  37.4 2.4 %collective-permute-done.12.refs_12_ = f32[2,8,384]{2,1,0:T(8,128)S(1)} collective-permute-done((f32[2,8,384]{2,1,0:T(8,128)S(1)}, f32[2,8,384]{2,1,0:T(8,128)S(1)}, u32[]{:S(2)}, u32[]{:S(2)}) %collective-permute-start.12) | collective-permute-done | bytes 24608 | tf_op jit(solution)/shard_map/merge/ppermute | solution.py:329
  39.7 0.0 collective-permute-done.11.refs_11_
  39.7 7.6 %gradients.1 = (bf16[192,256]{1,0:T(8,128)(2,1)S(1)}, bf16[192,256]{1,0:T(8,128)(2,1)S(1)}, bf16[192,256]{1,0:T(8,128)(2,1)S(1)}, bf16[192,256]{1,0:T(8,128)(2,1...) custom-call(bf16[2,192,256]{2,1,0:T(8,128)(2,1)S(1)} %get-tuple-elem, ...), custom_call_target="tpu_custom_call" | custom-call | flops 2264924160 | bytes 3735552 | tf_op jit(solution)/shard_map/gradients/pallas_call | solution.py:298
  47.3 2.8 %collective-permute-start.17 = (bf16[2,2,192,256]{3,2,1,0:T(8,128)(2,1)S(1)}, bf16[2,2,192,256]{3,2,1,0:T(8,128)(2,1)S(1)}, u32[]{:S(2)}, u32[]{:S(2)}) collective-permute-start(bf16[2,2,192,256]{3,2,1,0:T(8,128)(2,1)S(1)} %get-tuple-element.40), channel_id=1, source_target_pairs={{0,1},{1,0},{2,3},{3,2},{4,5},{5,4},{6,7},{7,6},{8,9},{9,8},{10,11... | collective-permute-start | bytes 1179656 | tf_op jit(solution)/shard_map/return/ppermute | solution.py:388
  50.2 3.1 %collective-permute-start.18 = (bf16[2,2,192,256]{3,2,1,0:T(8,128)(2,1)S(1)}, bf16[2,2,192,256]{3,2,1,0:T(8,128)(2,1)S(1)}, u32[]{:S(2)}, u32[]{:S(2)}) collective-permute-start(bf16[2,2,192,256]{3,2,1,0:T(8,128)(2,1)S(1)} %get-tuple-element.41), channel_id=1, source_target_pairs={{0,0},{1,2},{2,1},{3,3},{4,4},{5,6},{6,5},{7,7},{8,8},{9,10},{10,9... | collective-permute-start | bytes 1179656 | tf_op jit(solution)/shard_map/return/ppermute | solution.py:388
  53.2 1.8 %collective-permute-start.9 = (bf16[192,256]{1,0:T(8,128)(2,1)S(1)}, bf16[192,256]{1,0:T(8,128)(2,1)S(1)}, u32[]{:S(2)}, u32[]{:S(2)}) collective-permute-start(bf16[192,256]{1,0:T(8,128)(2,1)S(1)} %get-tuple-element.29), channel_id=1, source_target_pairs={{0,16},{8,24},{16,0},{24,8},{1,17},{9,25},{17,1},{25,9},{2,18},{10... | collective-permute-start | bytes 294920 | tf_op jit(solution)/shard_map/merge/ppermute | solution.py:329
  55.0 0.0 collective-permute-start.8
  55.0 0.0 collective-permute-done.17.refs_1_
  55.0 4.5 %collective-permute-done.18.refs_2_ = bf16[2,2,192,256]{3,2,1,0:T(8,128)(2,1)S(1)} collective-permute-done((bf16[2,2,192,256]{3,2,1,0:T(8,128)(2,1)S(1)}, bf16[2,2,192,256]{3,2,1,0:T(8,128)(2,1)S(1)}, u32[]{:S(2)}, u32[]{:S(2)}) %collective-permute-start.18) | collective-permute-done | bytes 393248 | tf_op jit(solution)/shard_map/return/ppermute | solution.py:388
  59.5 0.1 fusion
  59.6 0.1 collective-permute-start.19
  59.7 1.3 %collective-permute-start.10 = (bf16[192,256]{1,0:T(8,128)(2,1)S(1)}, bf16[192,256]{1,0:T(8,128)(2,1)S(1)}, u32[]{:S(2)}, u32[]{:S(2)}) collective-permute-start(bf16[192,256]{1,0:T(8,128)(2,1)S(1)} %get-tuple-element.30), channel_id=1, source_target_pairs={{0,24},{8,16},{16,8},{24,0},{1,25},{9,17},{17,9},{25,1},{2,26},{10... | collective-permute-start | bytes 294920 | tf_op jit(solution)/shard_map/merge/ppermute | solution.py:329
  61.0 1.0 %collective-permute-start.14 = (bf16[192,256]{1,0:T(8,128)(2,1)S(1)}, bf16[192,256]{1,0:T(8,128)(2,1)S(1)}, u32[]{:S(2)}, u32[]{:S(2)}) collective-permute-start(bf16[192,256]{1,0:T(8,128)(2,1)S(1)} %get-tuple-element.33), channel_id=1, source_target_pairs={{0,8},{8,0},{16,24},{24,16},{1,9},{9,1},{17,25},{25,17},{2,10},{10... | collective-permute-start | bytes 294920 | tf_op jit(solution)/shard_map/return/ppermute | solution.py:329
  62.0 0.0 collective-permute-done.9.refs_2_
  62.0 1.3 %collective-permute-start.15 = (bf16[192,256]{1,0:T(8,128)(2,1)S(1)}, bf16[192,256]{1,0:T(8,128)(2,1)S(1)}, u32[]{:S(2)}, u32[]{:S(2)}) collective-permute-start(bf16[192,256]{1,0:T(8,128)(2,1)S(1)} %get-tuple-element.34), channel_id=1, source_target_pairs={{0,16},{8,24},{16,0},{24,8},{1,17},{9,25},{17,1},{25,9},{2,18},{10... | collective-permute-start | bytes 294920 | tf_op jit(solution)/shard_map/return/ppermute | solution.py:329
  63.3 0.0 collective-permute-done.8.refs_1_
  63.3 1.2 %collective-permute-start.16 = (bf16[192,256]{1,0:T(8,128)(2,1)S(1)}, bf16[192,256]{1,0:T(8,128)(2,1)S(1)}, u32[]{:S(2)}, u32[]{:S(2)}) collective-permute-start(bf16[192,256]{1,0:T(8,128)(2,1)S(1)} %get-tuple-element.35), channel_id=1, source_target_pairs={{0,24},{8,16},{16,8},{24,0},{1,25},{9,17},{17,9},{25,1},{2,26},{10... | collective-permute-start | bytes 294920 | tf_op jit(solution)/shard_map/return/ppermute | solution.py:329
  64.5 1.0 %collective-permute-done.10.refs_3_ = bf16[192,256]{1,0:T(8,128)(2,1)S(1)} collective-permute-done((bf16[192,256]{1,0:T(8,128)(2,1)S(1)}, bf16[192,256]{1,0:T(8,128)(2,1)S(1)}, u32[]{:S(2)}, u32[]{:S(2)}) %collective-permute-start.10) | collective-permute-done | bytes 98336 | tf_op jit(solution)/shard_map/merge/ppermute | solution.py:329
  65.5 1.0 %collective-permute-done.14.refs_5_ = bf16[192,256]{1,0:T(8,128)(2,1)S(1)} collective-permute-done((bf16[192,256]{1,0:T(8,128)(2,1)S(1)}, bf16[192,256]{1,0:T(8,128)(2,1)S(1)}, u32[]{:S(2)}, u32[]{:S(2)}) %collective-permute-start.14) | collective-permute-done | bytes 98336 | tf_op jit(solution)/shard_map/return/ppermute | solution.py:329
  66.5 3.9 %collective-permute-done.15.refs_6_ = bf16[192,256]{1,0:T(8,128)(2,1)S(1)} collective-permute-done((bf16[192,256]{1,0:T(8,128)(2,1)S(1)}, bf16[192,256]{1,0:T(8,128)(2,1)S(1)}, u32[]{:S(2)}, u32[]{:S(2)}) %collective-permute-start.15) | collective-permute-done | bytes 98336 | tf_op jit(solution)/shard_map/return/ppermute | solution.py:329
  70.5 0.0 collective-permute-done.16.refs_7_
  70.5 0.0 copy-done.1
  70.5 0.0 copy-done.3
  70.5 0.0 copy-done.5
  70.5 1.0 %finish.2 = (bf16[192,256]{1,0:T(8,128)(2,1)}, bf16[192,256]{1,0:T(8,128)(2,1)}) custom-call(bf16[192,256]{1,0:T(8,128)(2,1)S(1)} %get-tuple-element.26.refs_0_, bf16[192,256]{1,0:T(8,128)(2,1)S(1)} %collective-permute-done.8.refs_1_, bf16[192,256]{1,0:T(8,128)(2,1)S(1)} %collective-permute-done.9.refs_2_, ...), custom_call_target="tpu_custom_call" | custom-call | bytes 1179648 | tf_op jit(solution)/shard_map/finish/pallas_call | solution.py:298
  71.6 0.0 collective-permute-done.19.refs_3_
  71.6 0.9 %finish.3 = (bf16[192,256]{1,0:T(8,128)(2,1)}, bf16[192,256]{1,0:T(8,128)(2,1)}) custom-call(bf16[2,2,192,256]{3,2,1,0:T(8,128)(2,1)S(1)} %get-tuple-element.39.refs_0_, bf16[2,2,192,256]{3,2,1,0:T(8,128)(2,1)S(1)} %collective-permute-done.17.refs_1_, bf16[2,2,192,256]{3,2,1,0:T(8,128)(2,1)S(1)} %collective-permute-done.18.refs_2_, ...), custom_call_target="tpu_custom_call" | custom-call | bytes 1671168 | tf_op jit(solution)/shard_map/finish/pallas_call | solution.py:298
  (3 shorter events, 0.0 us)
Async XLA Ops:
  0.6 0.8 %copy-start = (f32[3,32,128]{2,1,0:T(8,128)S(1)}, f32[3,32,128]{2,1,0:T(8,128)}, u32[]{:S(2)}) copy-start(f32[3,32,128]{2,1,0:T(8,128)} %constant.8.clone.ct_ref.refs_11_.refs_6_) | copy-start | bytes 147460
  1.4 0.7 %copy-start.2 = (f32[3,16,128]{2,1,0:T(8,128)S(1)}, f32[3,16,128]{2,1,0:T(8,128)}, u32[]{:S(2)}) copy-start(f32[3,16,128]{2,1,0:T(8,128)} %constant.7.clone.rt_ref.refs_10_.refs_5_) | copy-start | bytes 73732
  2.2 0.7 %copy-start.4 = (f32[3,16,128]{2,1,0:T(8,128)S(1)}, f32[3,16,128]{2,1,0:T(8,128)}, u32[]{:S(2)}) copy-start(f32[3,16,128]{2,1,0:T(8,128)} %constant.6.clone.tt_ref.refs_9_.refs_4_) | copy-start | bytes 73732
  2.9 0.9 %copy-start.6 = (bf16[3,8,8,256]{3,2,1,0:T(8,128)(2,1)S(1)}, bf16[3,8,8,256]{3,2,1,0:T(8,128)(2,1)}, u32[]{:S(2)}) copy-start(bf16[3,8,8,256]{3,2,1,0:T(8,128)(2,1)} %param.7) | copy-start | bytes 294916
  3.8 0.9 %copy-start.7 = (bf16[3,8,8,256]{3,2,1,0:T(8,128)(2,1)S(1)}, bf16[3,8,8,256]{3,2,1,0:T(8,128)(2,1)}, u32[]{:S(2)}) copy-start(bf16[3,8,8,256]{3,2,1,0:T(8,128)(2,1)} %param.8) | copy-start | bytes 294916
  4.7 0.9 %copy-start.8 = (bf16[3,8,8,256]{3,2,1,0:T(8,128)(2,1)S(1)}, bf16[3,8,8,256]{3,2,1,0:T(8,128)(2,1)}, u32[]{:S(2)}) copy-start(bf16[3,8,8,256]{3,2,1,0:T(8,128)(2,1)} %param.9) | copy-start | bytes 294916
  5.6 0.9 %copy-start.9 = (bf16[3,8,8,256]{3,2,1,0:T(8,128)(2,1)S(1)}, bf16[3,8,8,256]{3,2,1,0:T(8,128)(2,1)}, u32[]{:S(2)}) copy-start(bf16[3,8,8,256]{3,2,1,0:T(8,128)(2,1)} %param.10) | copy-start | bytes 294916
  6.7 8.8 %collective-permute-start.3 = (bf16[2,192,256]{2,1,0:T(8,128)(2,1)S(1)}, bf16[2,192,256]{2,1,0:T(8,128)(2,1)S(1)}, u32[]{:S(2)}, u32[]{:S(2)}) collective-permute-start(bf16[2,192,256]{2,1,0:T(8,128)(2,1)S(1)} %get-tuple-element.25.refs_2_.refs_4_), channel_id=1, source_target_pairs={{0,4},{4,0},{1,5},{5,1},{2,6},{6,2},{3,7},{7,3},{8,12},{12,8},{9,1... | collective-permute-start | bytes 589832 | tf_op jit(solution)/shard_map/halo/ppermute | solution.py:334
  8.8 10.9 %collective-permute-start = (bf16[2,192,256]{2,1,0:T(8,128)(2,1)S(1)}, bf16[2,192,256]{2,1,0:T(8,128)(2,1)S(1)}, u32[]{:S(2)}, u32[]{:S(2)}) collective-permute-start(bf16[2,192,256]{2,1,0:T(8,128)(2,1)S(1)} %get-tuple-element.24.refs_0_), channel_id=1, source_target_pairs={{0,16},{8,24},{16,0},{24,8},{1,17},{9,25},{17,1},{25,9},{2,18},{10... | collective-permute-start | bytes 589832 | tf_op jit(solution)/shard_map/halo/ppermute | solution.py:329
  11.1 10.0 %collective-permute-start.2 = (bf16[2,192,256]{2,1,0:T(8,128)(2,1)S(1)}, bf16[2,192,256]{2,1,0:T(8,128)(2,1)S(1)}, u32[]{:S(2)}, u32[]{:S(2)}) collective-permute-start(bf16[2,192,256]{2,1,0:T(8,128)(2,1)S(1)} %get-tuple-element.25.refs_2_.refs_4_), channel_id=1, source_target_pairs={{0,0},{1,2},{2,1},{3,3},{4,4},{5,6},{6,5},{7,7},{8,8},{9,10},{10,9... | collective-permute-start | bytes 589832 | tf_op jit(solution)/shard_map/halo/ppermute | solution.py:339
  15.4 5.8 %collective-permute-start.1 = (bf16[2,192,256]{2,1,0:T(8,128)(2,1)S(1)}, bf16[2,192,256]{2,1,0:T(8,128)(2,1)S(1)}, u32[]{:S(2)}, u32[]{:S(2)}) collective-permute-start(bf16[2,192,256]{2,1,0:T(8,128)(2,1)S(1)} %get-tuple-element.25.refs_2_.refs_4_), channel_id=1, source_target_pairs={{0,1},{1,0},{2,3},{3,2},{4,5},{5,4},{6,7},{7,6},{8,9},{9,8},{10,11... | collective-permute-start | bytes 589832 | tf_op jit(solution)/shard_map/halo/ppermute | solution.py:339
  15.4 7.0 %collective-permute-start.5 = (bf16[2,192,256]{2,1,0:T(8,128)(2,1)S(1)}, bf16[2,192,256]{2,1,0:T(8,128)(2,1)S(1)}, u32[]{:S(2)}, u32[]{:S(2)}) collective-permute-start(bf16[2,192,256]{2,1,0:T(8,128)(2,1)S(1)} %collective-permute-done.3.refs_5_.refs_7_), channel_id=1, source_target_pairs={{0,0},{1,2},{2,1},{3,3},{4,4},{5,6},{6,5},{7,7},{8,8},{9,10},{10,9... | collective-permute-start | bytes 589832 | tf_op jit(solution)/shard_map/halo/ppermute | solution.py:339
  17.9 4.5 %collective-permute-start.4 = (bf16[2,192,256]{2,1,0:T(8,128)(2,1)S(1)}, bf16[2,192,256]{2,1,0:T(8,128)(2,1)S(1)}, u32[]{:S(2)}, u32[]{:S(2)}) collective-permute-start(bf16[2,192,256]{2,1,0:T(8,128)(2,1)S(1)} %collective-permute-done.3.refs_5_.refs_7_), channel_id=1, source_target_pairs={{0,1},{1,0},{2,3},{3,2},{4,5},{5,4},{6,7},{7,6},{8,9},{9,8},{10,11... | collective-permute-start | bytes 589832 | tf_op jit(solution)/shard_map/halo/ppermute | solution.py:339
  19.7 5.2 %collective-permute-start.6 = (bf16[2,192,256]{2,1,0:T(8,128)(2,1)S(1)}, bf16[2,192,256]{2,1,0:T(8,128)(2,1)S(1)}, u32[]{:S(2)}, u32[]{:S(2)}) collective-permute-start(bf16[2,192,256]{2,1,0:T(8,128)(2,1)S(1)} %get-tuple-element.24.refs_0_), channel_id=1, source_target_pairs={{0,8},{8,0},{16,24},{24,16},{1,9},{9,1},{17,25},{25,17},{2,10},{10... | collective-permute-start | bytes 589832 | tf_op jit(solution)/shard_map/halo/ppermute | solution.py:329
  21.1 8.0 %collective-permute-start.7 = (bf16[2,192,256]{2,1,0:T(8,128)(2,1)S(1)}, bf16[2,192,256]{2,1,0:T(8,128)(2,1)S(1)}, u32[]{:S(2)}, u32[]{:S(2)}) collective-permute-start(bf16[2,192,256]{2,1,0:T(8,128)(2,1)S(1)} %collective-permute-done.refs_1_), channel_id=1, source_target_pairs={{0,8},{8,0},{16,24},{24,16},{1,9},{9,1},{17,25},{25,17},{2,10},{10... | collective-permute-start | bytes 589832 | tf_op jit(solution)/shard_map/halo/ppermute | solution.py:329
  31.1 6.3 %collective-permute-start.13 = (f32[2,8,384]{2,1,0:T(8,128)S(1)}, f32[2,8,384]{2,1,0:T(8,128)S(1)}, u32[]{:S(2)}, u32[]{:S(2)}) collective-permute-start(f32[2,8,384]{2,1,0:T(8,128)S(1)} %get-tuple-element.31.refs_10_), channel_id=1, source_target_pairs={{0,24},{8,16},{16,8},{24,0},{1,25},{9,17},{17,9},{25,1},{2,26},{10... | collective-permute-start | bytes 73736 | tf_op jit(solution)/shard_map/merge/ppermute | solution.py:329
  36.1 3.6 %collective-permute-start.12 = (f32[2,8,384]{2,1,0:T(8,128)S(1)}, f32[2,8,384]{2,1,0:T(8,128)S(1)}, u32[]{:S(2)}, u32[]{:S(2)}) collective-permute-start(f32[2,8,384]{2,1,0:T(8,128)S(1)} %get-tuple-element.31.refs_10_), channel_id=1, source_target_pairs={{0,16},{8,24},{16,0},{24,8},{1,17},{9,25},{17,1},{25,9},{2,18},{10... | collective-permute-start | bytes 73736 | tf_op jit(solution)/shard_map/merge/ppermute | solution.py:329
  36.1 3.6 %collective-permute-start.11 = (f32[2,8,384]{2,1,0:T(8,128)S(1)}, f32[2,8,384]{2,1,0:T(8,128)S(1)}, u32[]{:S(2)}, u32[]{:S(2)}) collective-permute-start(f32[2,8,384]{2,1,0:T(8,128)S(1)} %get-tuple-element.31.refs_10_), channel_id=1, source_target_pairs={{0,8},{8,0},{16,24},{24,16},{1,9},{9,1},{17,25},{25,17},{2,10},{10... | collective-permute-start | bytes 73736 | tf_op jit(solution)/shard_map/merge/ppermute | solution.py:329
  47.3 7.7 %collective-permute-start.17 = (bf16[2,2,192,256]{3,2,1,0:T(8,128)(2,1)S(1)}, bf16[2,2,192,256]{3,2,1,0:T(8,128)(2,1)S(1)}, u32[]{:S(2)}, u32[]{:S(2)}) collective-permute-start(bf16[2,2,192,256]{3,2,1,0:T(8,128)(2,1)S(1)} %get-tuple-element.40), channel_id=1, source_target_pairs={{0,1},{1,0},{2,3},{3,2},{4,5},{5,4},{6,7},{7,6},{8,9},{9,8},{10,11... | collective-permute-start | bytes 1179656 | tf_op jit(solution)/shard_map/return/ppermute | solution.py:388
  50.2 9.4 %collective-permute-start.18 = (bf16[2,2,192,256]{3,2,1,0:T(8,128)(2,1)S(1)}, bf16[2,2,192,256]{3,2,1,0:T(8,128)(2,1)S(1)}, u32[]{:S(2)}, u32[]{:S(2)}) collective-permute-start(bf16[2,2,192,256]{3,2,1,0:T(8,128)(2,1)S(1)} %get-tuple-element.41), channel_id=1, source_target_pairs={{0,0},{1,2},{2,1},{3,3},{4,4},{5,6},{6,5},{7,7},{8,8},{9,10},{10,9... | collective-permute-start | bytes 1179656 | tf_op jit(solution)/shard_map/return/ppermute | solution.py:388
  53.2 8.7 %collective-permute-start.9 = (bf16[192,256]{1,0:T(8,128)(2,1)S(1)}, bf16[192,256]{1,0:T(8,128)(2,1)S(1)}, u32[]{:S(2)}, u32[]{:S(2)}) collective-permute-start(bf16[192,256]{1,0:T(8,128)(2,1)S(1)} %get-tuple-element.29), channel_id=1, source_target_pairs={{0,16},{8,24},{16,0},{24,8},{1,17},{9,25},{17,1},{25,9},{2,18},{10... | collective-permute-start | bytes 294920 | tf_op jit(solution)/shard_map/merge/ppermute | solution.py:329
  55.0 8.3 %collective-permute-start.8 = (bf16[192,256]{1,0:T(8,128)(2,1)S(1)}, bf16[192,256]{1,0:T(8,128)(2,1)S(1)}, u32[]{:S(2)}, u32[]{:S(2)}) collective-permute-start(bf16[192,256]{1,0:T(8,128)(2,1)S(1)} %get-tuple-element.28), channel_id=1, source_target_pairs={{0,8},{8,0},{16,24},{24,16},{1,9},{9,1},{17,25},{25,17},{2,10},{10... | collective-permute-start | bytes 294920 | tf_op jit(solution)/shard_map/merge/ppermute | solution.py:329
  59.5 11.0 %copy-start.1 = (f32[3,32,128]{2,1,0:T(8,128)S(1)}, f32[3,32,128]{2,1,0:T(8,128)}, u32[]{:S(2)}) copy-start(f32[3,32,128]{2,1,0:T(8,128)} %constant.8.clone.ct_ref.refs_11_.refs_6_) | copy-start | bytes 147460
  59.5 11.0 %copy-start.3 = (f32[3,16,128]{2,1,0:T(8,128)S(1)}, f32[3,16,128]{2,1,0:T(8,128)}, u32[]{:S(2)}) copy-start(f32[3,16,128]{2,1,0:T(8,128)} %constant.7.clone.rt_ref.refs_10_.refs_5_) | copy-start | bytes 73732
  59.5 11.0 %copy-start.5 = (f32[3,16,128]{2,1,0:T(8,128)S(1)}, f32[3,16,128]{2,1,0:T(8,128)}, u32[]{:S(2)}) copy-start(f32[3,16,128]{2,1,0:T(8,128)} %constant.6.clone.tt_ref.refs_9_.refs_4_) | copy-start | bytes 73732
  59.6 11.9 %collective-permute-start.19 = (bf16[2,192,256]{2,1,0:T(8,128)(2,1)S(1)}, bf16[2,192,256]{2,1,0:T(8,128)(2,1)S(1)}, u32[]{:S(2)}, u32[]{:S(2)}) collective-permute-start(bf16[2,192,256]{2,1,0:T(8,128)(2,1)S(1)} %fusion), channel_id=1, source_target_pairs={{0,4},{4,0},{1,5},{5,1},{2,6},{6,2},{3,7},{7,3},{8,12},{12,8},{9,1... | collective-permute-start | bytes 589832 | tf_op jit(solution)/shard_map/return/ppermute | solution.py:394
  59.7 5.8 %collective-permute-start.10 = (bf16[192,256]{1,0:T(8,128)(2,1)S(1)}, bf16[192,256]{1,0:T(8,128)(2,1)S(1)}, u32[]{:S(2)}, u32[]{:S(2)}) collective-permute-start(bf16[192,256]{1,0:T(8,128)(2,1)S(1)} %get-tuple-element.30), channel_id=1, source_target_pairs={{0,24},{8,16},{16,8},{24,0},{1,25},{9,17},{17,9},{25,1},{2,26},{10... | collective-permute-start | bytes 294920 | tf_op jit(solution)/shard_map/merge/ppermute | solution.py:329
  61.0 5.6 %collective-permute-start.14 = (bf16[192,256]{1,0:T(8,128)(2,1)S(1)}, bf16[192,256]{1,0:T(8,128)(2,1)S(1)}, u32[]{:S(2)}, u32[]{:S(2)}) collective-permute-start(bf16[192,256]{1,0:T(8,128)(2,1)S(1)} %get-tuple-element.33), channel_id=1, source_target_pairs={{0,8},{8,0},{16,24},{24,16},{1,9},{9,1},{17,25},{25,17},{2,10},{10... | collective-permute-start | bytes 294920 | tf_op jit(solution)/shard_map/return/ppermute | solution.py:329
  62.0 8.5 %collective-permute-start.15 = (bf16[192,256]{1,0:T(8,128)(2,1)S(1)}, bf16[192,256]{1,0:T(8,128)(2,1)S(1)}, u32[]{:S(2)}, u32[]{:S(2)}) collective-permute-start(bf16[192,256]{1,0:T(8,128)(2,1)S(1)} %get-tuple-element.34), channel_id=1, source_target_pairs={{0,16},{8,24},{16,0},{24,8},{1,17},{9,25},{17,1},{25,9},{2,18},{10... | collective-permute-start | bytes 294920 | tf_op jit(solution)/shard_map/return/ppermute | solution.py:329
  63.3 7.2 %collective-permute-start.16 = (bf16[192,256]{1,0:T(8,128)(2,1)S(1)}, bf16[192,256]{1,0:T(8,128)(2,1)S(1)}, u32[]{:S(2)}, u32[]{:S(2)}) collective-permute-start(bf16[192,256]{1,0:T(8,128)(2,1)S(1)} %get-tuple-element.35), channel_id=1, source_target_pairs={{0,24},{8,16},{16,8},{24,0},{1,25},{9,17},{17,9},{25,1},{2,26},{10... | collective-permute-start | bytes 294920 | tf_op jit(solution)/shard_map/return/ppermute | solution.py:329

commit v2 on v1

v2 whole, which is shorter than its diff:
```python
import functools
import math

import jax
import jax.numpy as jnp
import numpy as np
from jax import lax
from jax.experimental import pallas as pl
from jax.experimental.pallas import tpu as pltpu
from jax.sharding import PartitionSpec as P

DH = 128
HEADS = 2
TILE_T = 6
TILE_H = 8
TILE_W = 8

NEGATIVE = -1e30
SCALE = DH**-0.5
SCALE_LOG2 = SCALE * math.log2(math.e)
F32 = jnp.float32
BF16 = jnp.bfloat16
VMEM_LIMIT = 48 * 1024 * 1024


def near_pairs(count):
    return [(i, i ^ 1) for i in range(count)]


def far_pairs(count):
    pairs = []
    for i in range(count):
        j = i + 1 if i % 2 else i - 1
        pairs.append((i, j if 0 <= j < count else i))
    return pairs


def far_exists(axis, count):
    pos = lax.axis_index(axis)
    other = jnp.where(pos % 2 == 1, pos + 1, pos - 1)
    return (other >= 0) & (other < count)


def side_pairs(count):
    sides = []
    if count > 1:
        sides.append(near_pairs(count))
    if count > 2:
        sides.append(far_pairs(count))
    return sides


def rope_table(frame_total, row_total, col_total):
    time_dims = DH // 8
    space_dims = (DH - time_dims) // 2
    slower = 256.0 ** (-np.arange(0, time_dims, 2) / time_dims)
    faster = 256.0 ** (-np.arange(0, space_dims, 2) / space_dims)
    starts = (0, time_dims, time_dims + space_dims)
    pieces = []
    for total, rates, start in zip(
        (frame_total, row_total, col_total), (slower, faster, faster), starts
    ):
        padded = -(-total // 8) * 8
        piece = np.zeros((3, padded, DH), np.float32)
        angles = np.arange(padded)[:, None] * rates[None, :]
        stop = start + 2 * len(rates)
        piece[0, :, start:stop:2] = np.cos(angles)
        piece[0, :, start + 1 : stop : 2] = np.cos(angles)
        piece[1, :, start:stop:2] = -np.sin(angles)
        piece[2, :, start + 1 : stop : 2] = np.sin(angles)
        pieces.append(piece)
    begins = np.cumsum([0] + [piece.shape[1] for piece in pieces])
    return np.concatenate(pieces, axis=1), tuple(int(x) for x in begins[:3])


def local_table(plane, table_ref, begins, frames, rows, cols):
    frame_lo = begins[0] + lax.axis_index("ta") * frames
    row_lo = pl.multiple_of(begins[1] + lax.axis_index("ha") * rows, 8)
    col_lo = pl.multiple_of(begins[2] + lax.axis_index("wa") * cols, 8)
    row_part = table_ref[plane, pl.ds(row_lo, rows), :]
    col_part = table_ref[plane, pl.ds(col_lo, cols), :]
    grids = []
    for i in range(frames):
        lead = row_part + table_ref[plane, pl.ds(frame_lo + i, 1), :]
        grid = lead[:, None, :] + col_part[None, :, :]
        grids.append(grid.reshape(rows * cols, DH))
    return jnp.concatenate(grids, axis=0)


def turn(x, cosine, sin_even, sin_odd, sign):
    follow = pltpu.roll(x, DH - 1, 1)
    lead = pltpu.roll(x, 1, 1)
    return x * cosine + sign * (follow * sin_even + lead * sin_odd)


def head_slice(head):
    return slice(head * DH, (head + 1) * DH)


def rotate_kernel(
    dims, begins, q_hbm, k_hbm, v_hbm, g_hbm, table_hbm, kv_ref, qg_ref, rope_ref, q_ref, k_ref,
    table_ref, sems,
):
    moves = [
        (table_hbm, table_ref),
        (k_hbm, k_ref),
        (q_hbm, q_ref),
        (v_hbm, kv_ref.at[1]),
        (g_hbm, qg_ref.at[1]),
    ]
    copies = [pltpu.make_async_copy(*move, sems.at[i]) for i, move in enumerate(moves)]
    for copy in copies:
        copy.start()
    copies[0].wait()
    tables = [local_table(plane, table_ref, begins, *dims) for plane in range(3)]
    for plane in range(3):
        rope_ref[plane] = tables[plane]
    for copy, source, target in ((copies[1], k_ref, kv_ref), (copies[2], q_ref, qg_ref)):
        copy.wait()
        for head in range(HEADS):
            cut = head_slice(head)
            target[0, :, cut] = turn(source[:, cut].astype(F32), *tables, 1.0).astype(BF16)
    copies[3].wait()
    copies[4].wait()


def dot_nt(a, b):
    return lax.dot_general(a, b, (((1,), (1,)), ((), ())), preferred_element_type=F32)


def dot_nn(a, b):
    return lax.dot_general(a, b, (((1,), (0,)), ((), ())), preferred_element_type=F32)


def dot_tn(a, b):
    return lax.dot_general(a, b, (((0,), (0,)), ((), ())), preferred_element_type=F32)


def group_bias(flags, sizes):
    valid = None
    for axis, is_far in zip(("ha", "wa"), flags):
        if is_far:
            here = far_exists(axis, sizes[axis])
            valid = here if valid is None else valid & here
    return None if valid is None else jnp.where(valid, 0.0, NEGATIVE).astype(F32)


def forward_kernel(groups, sizes, cells, with_first, *refs):
    tile_count = sum(len(members) for _, members in groups)
    qa_ref, qb_ref = refs[0], refs[1]
    kv_refs = refs[2 : 2 + tile_count]
    rest = refs[2 + tile_count :]
    if with_first:
        first_ref, oa_ref, ob_ref, stat_ref, key_buf, value_buf = rest
    else:
        oa_ref, ob_ref, stat_ref, key_buf, value_buf = rest
    at = 0
    spans = []
    for flags, members in groups:
        begin = at
        for member in members:
            key_buf[at : at + cells] = kv_refs[member][0]
            value_buf[at : at + cells] = kv_refs[member][1]
            at += cells
        spans.append((begin, at, group_bias(flags, sizes)))
    lane = lax.broadcasted_iota(jnp.int32, (2 * cells, DH), 1)
    stat = jnp.zeros((2 * cells, DH), F32)
    for head in range(HEADS):
        cut = head_slice(head)
        query = jnp.concatenate([qa_ref[0, :, cut], qb_ref[0, :, cut]], axis=0)
        grad = jnp.concatenate([qa_ref[1, :, cut], qb_ref[1, :, cut]], axis=0)
        scores = [dot_nt(query, key_buf[lo:hi, cut]) for lo, hi, _ in spans]
        best = None
        for raw, (_, _, bias) in zip(scores, spans):
            top = jnp.max(raw, axis=1, keepdims=True) * SCALE_LOG2
            if bias is not None:
                top = top + bias
            best = top if best is None else jnp.maximum(best, top)
        total = None
        out = None
        for raw, (lo, hi, bias) in zip(scores, spans):
            shift = best if bias is None else best - bias
            weights = jnp.exp2(raw * SCALE_LOG2 - shift)
            part = jnp.sum(weights, axis=1, keepdims=True)
            piece = dot_nn(weights.astype(BF16), value_buf[lo:hi, cut])
            total = part if total is None else total + part
            out = piece if out is None else out + piece
        out = out * (1.0 / total)
        dotted = jnp.sum(out * grad.astype(F32), axis=1, keepdims=True)
        out = out.astype(BF16)
        oa_ref[:, cut] = out[:cells]
        ob_ref[:, cut] = out[cells:]
        stat = jnp.where(lane == head, best + jnp.log2(total), stat)
        stat = jnp.where(lane == HEADS + head, dotted, stat)
    flipped = stat.T[: stat_ref.shape[-2]]
    if with_first:
        stat_ref[0] = first_ref[...]
        stat_ref[1] = flipped
    else:
        stat_ref[...] = flipped


def merged_stats(own_ref, s1_ref, s2_ref, s3_ref, half, cells):
    parts = [
        own_ref[half],
        pltpu.roll(s1_ref[half], cells, 1),
        s2_ref[1 - half],
        pltpu.roll(s3_ref[1 - half], cells, 1),
    ]
    top = functools.reduce(jnp.maximum, parts)
    shares = [jnp.exp2(part - top) for part in parts]
    total = functools.reduce(jnp.add, shares)
    lse = top + jnp.log2(total)
    shares = [share / total for share in shares]
    delta = functools.reduce(
        jnp.add,
        [share[:HEADS] * part[HEADS : 2 * HEADS] for share, part in zip(shares, parts)],
    )
    return lse[:HEADS], delta, shares


def gradient_blocks(cols, flags_of, sizes, key_buf, value_buf, queries, grads, lse, delta, span):
    dq = None
    results = []
    for slot, col in enumerate(cols):
        lo = slot * span
        key = key_buf[lo : lo + span]
        value = value_buf[lo : lo + span]
        raw = dot_nt(key, queries)
        prob_grad = dot_nt(value, grads)
        cells = span // len(flags_of)
        probs = []
        for row, row_far in enumerate(flags_of):
            bias = group_bias((row_far, col == 2), sizes)
            shift = lse if bias is None else lse - bias
            probs.append(jnp.exp2(raw[row * cells : (row + 1) * cells] * SCALE_LOG2 - shift))
        probs = jnp.concatenate(probs, axis=0)
        dscore = (probs * (prob_grad - delta)).astype(BF16)
        dv = dot_nn(probs.astype(BF16), grads)
        dk = dot_nn(dscore, queries) * SCALE
        results.append((dk, dv))
        part = dot_nn(key.T, dscore)
        dq = part if dq is None else dq + part
    return results, dq


def backward_kernel(cols, grid_rows, sizes, cells, last, *refs):
    tile_count = grid_rows * len(cols)
    qg_refs = refs[:4]
    kv_refs = refs[4 : 4 + tile_count]
    rest = refs[4 + tile_count :]
    if last:
        lse_ref, delta_ref, share_ref, dq_ref = rest[:4]
        o_refs = rest[4:8]
        dq_outs, out_ref = rest[8:12], rest[12]
        col_refs = rest[13 : 13 + len(cols)]
        key_buf, value_buf = rest[13 + len(cols) :]
        lse, delta = lse_ref[...], delta_ref[...]
        for head in range(HEADS):
            cut = head_slice(head)
            out = None
            for d in range(4):
                weight = share_ref[:, 4 * head + d : 4 * head + d + 1]
                piece = o_refs[d][:, cut].astype(F32) * weight
                out = piece if out is None else out + piece
            out_ref[:, cut] = out.astype(BF16)
    else:
        stat_refs = rest[:4]
        lse_ref, delta_ref, share_ref, dq_ref = rest[4:8]
        col_refs = rest[8 : 8 + len(cols)]
        key_buf, value_buf = rest[8 + len(cols) :]
        stats = [merged_stats(*stat_refs, half, cells) for half in range(2)]
        lse = jnp.concatenate([stats[0][0], stats[1][0]], axis=1)
        delta = jnp.concatenate([stats[0][1], stats[1][1]], axis=1)
        lse_ref[...] = lse
        delta_ref[...] = delta
        shares = stats[0][2]
        rows = [shares[d][head : head + 1] for head in range(HEADS) for d in range(4)]
        wide = jnp.concatenate(rows + [jnp.zeros((DH - len(rows), 2 * cells), F32)], axis=0)
        share_ref[...] = wide.T[:cells]

    span = grid_rows * cells
    for i, ref in enumerate(kv_refs):
        key_buf[i * cells : (i + 1) * cells] = ref[0]
        value_buf[i * cells : (i + 1) * cells] = ref[1]
    row_flags = [row == 2 for row in range(grid_rows)]
    for head in range(HEADS):
        cut = head_slice(head)
        queries = jnp.concatenate([ref[0, :, cut] for ref in qg_refs], axis=0)
        grads = jnp.concatenate([ref[1, :, cut] for ref in qg_refs], axis=0)
        results, dq = gradient_blocks(
            cols, row_flags, sizes, key_buf.at[:, cut], value_buf.at[:, cut], queries, grads,
            lse[head : head + 1], delta[head : head + 1], span,
        )
        for (dk, dv), ref in zip(results, col_refs):
            for row in range(grid_rows):
                at = slice(row * cells, (row + 1) * cells)
                ref[row, 0, :, cut] = dk[at].astype(BF16)
                ref[row, 1, :, cut] = dv[at].astype(BF16)
        if last:
            dq = ((dq + dq_ref[head]) * SCALE).T.astype(BF16)
            for i, ref in enumerate(dq_outs):
                ref[:, cut] = dq[i * cells : (i + 1) * cells]
        else:
            dq_ref[head] = dq


def finish_query_kernel(*refs):
    dq_refs = refs[:4]
    rope_ref, dq_out = refs[4:]
    for head in range(HEADS):
        cut = head_slice(head)
        dq = functools.reduce(jnp.add, [ref[:, cut].astype(F32) for ref in dq_refs])
        dq_out[:, cut] = turn(dq, rope_ref[0], rope_ref[1], rope_ref[2], -1.0).astype(BF16)


def finish_key_kernel(cols, rows, *refs):
    col_refs, row_refs = refs[:cols], refs[cols : cols + rows]
    rope_ref, dk_out, dv_out = refs[cols + rows :]
    for head in range(HEADS):
        cut = head_slice(head)
        sums = []
        for which in range(2):
            terms = [ref[0, which, :, cut].astype(F32) for ref in col_refs]
            terms += [ref[which, :, cut].astype(F32) for ref in row_refs]
            sums.append(functools.reduce(jnp.add, terms))
        dk_out[:, cut] = turn(
            sums[0], rope_ref[0], rope_ref[1], rope_ref[2], -1.0
        ).astype(BF16)
        dv_out[:, cut] = sums[1].astype(BF16)


def call(kernel, out_shape, args, flops=0, exps=0, scratch=(), space=pltpu.VMEM, limit=VMEM_LIMIT):
    shapes = jax.tree.leaves(out_shape)
    moved = sum(math.prod(x.shape) * x.dtype.itemsize for x in list(args) + shapes)
    return pl.pallas_call(
        kernel,
        out_shape=out_shape,
        in_specs=[pl.BlockSpec(memory_space=space)] * len(args),
        scratch_shapes=list(scratch),
        compiler_params=pltpu.CompilerParams(vmem_limit_bytes=limit),
        cost_estimate=pl.CostEstimate(flops=flops, bytes_accessed=moved, transcendentals=exps),
    )(*args)


def shards(query_in, key_in, value_in, cotangent):
    frames, rows, cols, chan = query_in.shape
    cells = frames * rows * cols
    sizes = {axis: lax.axis_size(axis) for axis in ("ta", "ha", "wa")}
    assert rows == TILE_H and cols == TILE_W and chan == HEADS * DH
    assert TILE_T % frames == 0 and frames * sizes["ta"] <= 2 * TILE_T
    assert sizes["ta"] == 4 and sizes["ha"] % 2 == 0 and sizes["wa"] % 2 == 0
    dims = (frames, rows, cols)
    table, begins = rope_table(frames * sizes["ta"], rows * sizes["ha"], cols * sizes["wa"])
    flat = [x.reshape(cells, chan) for x in (query_in, key_in, value_in, cotangent)]
    pair = jax.ShapeDtypeStruct((2, cells, chan), BF16)
    plain = jax.ShapeDtypeStruct((cells, chan), BF16)

    def real(*shape):
        return jax.ShapeDtypeStruct(shape, F32)

    with jax.named_scope("rotate"):
        kv, qg, rope = call(
            functools.partial(rotate_kernel, dims, begins),
            (pair, pair, real(3, cells, DH)),
            [pltpu.with_memory_space_constraint(x, pltpu.HBM) for x in (*flat, jnp.asarray(table))],
            scratch=[pltpu.VMEM((cells, chan), BF16)] * 2
            + [pltpu.VMEM(table.shape, F32), pltpu.SemaphoreType.DMA((5,))],
            space=pltpu.HBM,
        )

    def other_frames(x, distance):
        return lax.ppermute(x, "ta", [(i, i ^ distance) for i in range(sizes["ta"])])

    row_sides = side_pairs(sizes["ha"])
    col_sides = side_pairs(sizes["wa"])
    with jax.named_scope("halo"):
        kv_rows = [kv] + [lax.ppermute(kv, "ha", pairs) for pairs in row_sides]
        qg2 = other_frames(qg, 2)
        qg1 = other_frames(qg, 1)
        tiles = []
        for block in kv_rows:
            tiles.append([block] + [lax.ppermute(block, "wa", pairs) for pairs in col_sides])
        qg3 = other_frames(qg2, 1)
    grid_rows, grid_cols = 1 + len(row_sides), 1 + len(col_sides)
    flat_tiles = [tiles[row][col] for row in range(grid_rows) for col in range(grid_cols)]
    groups = {}
    for row in range(grid_rows):
        for col in range(grid_cols):
            groups.setdefault((row == 2, col == 2), []).append(row * grid_cols + col)
    groups = list(groups.items())

    key_count = len(flat_tiles) * cells
    product = 2 * 2 * cells * key_count * DH * HEADS

    def forward(qa, qb, first):
        args = (qa, qb, *flat_tiles) + (() if first is None else (first,))
        stat = (8, 2 * cells) if first is None else (2, 8, 2 * cells)
        return call(
            functools.partial(forward_kernel, groups, sizes, cells, first is not None),
            (plain, plain, real(*stat)),
            args,
            2 * product,
            2 * cells * key_count * HEADS,
            [pltpu.VMEM((key_count, chan), BF16)] * 2,
        )

    with jax.named_scope("attend"):
        o0, o1, first = forward(qg, qg1, None)
        o2, o3, stat = forward(qg2, qg3, first)
    with jax.named_scope("merge"):
        stats = [stat] + [other_frames(stat, d) for d in (1, 2, 3)]
        outs = [o0] + [other_frames(o, d) for d, o in ((1, o1), (2, o2), (3, o3))]

    queries = (qg, qg1, qg2, qg3)
    col_shape = jax.ShapeDtypeStruct((grid_rows, 2, cells, chan), BF16)

    def gradients(which, last, extra_out, extra_in):
        count = len(which)
        return call(
            functools.partial(backward_kernel, which, grid_rows, sizes, cells, last),
            (*extra_out, *[col_shape] * count),
            (*queries, *[tiles[row][col] for col in which for row in range(grid_rows)], *extra_in),
            10 * product * count // grid_cols,
            4 * cells * key_count * HEADS * count // grid_cols,
            [pltpu.VMEM((count * grid_rows * cells, chan), BF16)] * 2,
        )

    with jax.named_scope("gradients"):
        lse, delta, shares, dq, *sides = gradients(
            tuple(range(1, grid_cols)),
            False,
            (
                real(HEADS, 4 * cells),
                real(HEADS, 4 * cells),
                real(cells, DH),
                real(HEADS, DH, 4 * cells),
            ),
            stats,
        )
        sides = [lax.ppermute(x, "wa", pairs) for x, pairs in zip(sides, col_sides)]
        d0, d1, d2, d3, attended, own = gradients(
            (0,), True, [plain] * 5, (lse, delta, shares, dq, *outs)
        )
    with jax.named_scope("return"):
        col_parts = [own, *sides]
        dqs = [d0] + [other_frames(x, d) for d, x in ((1, d1), (2, d2), (3, d3))]
        row_parts = []
        for row, pairs in enumerate(row_sides, start=1):
            partial_sum = sum(x[row].astype(F32) for x in col_parts).astype(BF16)
            row_parts.append(lax.ppermute(partial_sum, "ha", pairs))

    with jax.named_scope("finish"):
        grad_query = call(finish_query_kernel, plain, (*dqs, rope))
        grad_key, grad_value = call(
            functools.partial(finish_key_kernel, grid_cols, len(row_parts)),
            (plain, plain),
            (*col_parts, *row_parts, rope),
        )
    return tuple(x.reshape(query_in.shape) for x in (attended, grad_query, grad_key, grad_value))


def solution(mesh):
    spec = P("ta", "ha", "wa", None)
    return jax.shard_map(
        shards, mesh=mesh, in_specs=(spec,) * 4, out_specs=(spec,) * 4, check_vma=False
    )
```

time: 72.9 us -> 66.3 us (0.909)
  the two profiles are of different devices: /device:TPU:1 before, /device:TPU:0 now
where the time goes in v2:
time: 66.3 us; the launch traced here: 66.1 us
  starting transfers between devices  29.3 us (44%)
  waiting for transfers between devices  24 us (36%)
  Pallas kernels  12 us (18%)
  between operations  0.71 us (1%)
    ppermute x12, waiting for transfers between devices, other_frames(): lax.ppermute(x, 'ta', [(i, i ^ distance) for i in range(sizes['ta'])])  24 us
    ppermute x12, starting transfers between devices, other_frames(): lax.ppermute(x, 'ta', [(i, i ^ distance) for i in range(sizes['ta'])])  20.7 us
    pallas_call x7, Pallas kernels, call(): pl.pallas_call(kernel, out_shape=out_shape, in_specs=[pl.BlockSpec(memory...  12 us
    ppermute x4, starting transfers between devices, shards(): lax.ppermute(block, 'wa', pairs)  4.26 us
    ppermute x1, starting transfers between devices, shards(): kv_rows = [kv] + [lax.ppermute(kv, 'ha', pairs) for pairs in row_sides]  3 us
  transfers between devices with their start and end apart: 20, of which 10 were waited for; matrix products, arithmetic and copies ran while one was open for 0% of the time, Pallas kernels for 7%

profile of v2, /device:TPU:0, one launch (start us, length us, event | category | flops | bytes accessed | tf_op | source)
XLA Modules:
  0.0 66.1 jit_solution(11826451131858986429)
XLA Ops:
  0.6 1.3 %rotate.1 = (bf16[2,192,256]{2,1,0:T(8,128)(2,1)S(1)}, bf16[2,192,256]{2,1,0:T(8,128)(2,1)S(1)}, f32[3,192,128]{2,1,0:T(8,128)S(1)}) custom-call(bf16[192,256]{1,0:T(8,128)(2,1)} %bitcast.11, bf16[192,256]{1,0:T(8,128)(2,1)} %bitcast.12, bf16[192,256]{1,0:T(8,128)(2,1)} %bitcast.13, bf16[192,256]{1,0:T(8,128)(2,1)} %bitcast.14, ...), custom_call_target="tpu_custom_call" | custom-call | bytes 1179648 | tf_op jit(solution)/shard_map/rotate/pallas_call | solution.py:336
  1.9 3.0 %collective-permute-start.3 = (bf16[2,192,256]{2,1,0:T(8,128)(2,1)S(1)}, bf16[2,192,256]{2,1,0:T(8,128)(2,1)S(1)}, u32[]{:S(2)}, u32[]{:S(2)}) collective-permute-start(bf16[2,192,256]{2,1,0:T(8,128)(2,1)S(1)} %get-tuple-element.28.refs_2_.refs_4_), channel_id=1, source_target_pairs={{0,4},{4,0},{1,5},{5,1},{2,6},{6,2},{3,7},{7,3},{8,12},{12,8},{9,1... | collective-permute-start | bytes 589832 | tf_op jit(solution)/shard_map/halo/ppermute | solution.py:378
  4.9 2.6 %collective-permute-start.1 = (bf16[2,192,256]{2,1,0:T(8,128)(2,1)S(1)}, bf16[2,192,256]{2,1,0:T(8,128)(2,1)S(1)}, u32[]{:S(2)}, u32[]{:S(2)}) collective-permute-start(bf16[2,192,256]{2,1,0:T(8,128)(2,1)S(1)} %get-tuple-element.27.refs_0_), channel_id=1, source_target_pairs={{0,16},{8,24},{16,0},{24,8},{1,17},{9,25},{17,1},{25,9},{2,18},{10... | collective-permute-start | bytes 589832 | tf_op jit(solution)/shard_map/halo/ppermute | solution.py:373
  7.5 1.6 %collective-permute-start = (bf16[2,192,256]{2,1,0:T(8,128)(2,1)S(1)}, bf16[2,192,256]{2,1,0:T(8,128)(2,1)S(1)}, u32[]{:S(2)}, u32[]{:S(2)}) collective-permute-start(bf16[2,192,256]{2,1,0:T(8,128)(2,1)S(1)} %get-tuple-element.27.refs_0_), channel_id=1, source_target_pairs={{0,8},{8,0},{16,24},{24,16},{1,9},{9,1},{17,25},{25,17},{2,10},{10... | collective-permute-start | bytes 589832 | tf_op jit(solution)/shard_map/halo/ppermute | solution.py:373
  9.1 0.7 %collective-permute-start.6 = (bf16[2,192,256]{2,1,0:T(8,128)(2,1)S(1)}, bf16[2,192,256]{2,1,0:T(8,128)(2,1)S(1)}, u32[]{:S(2)}, u32[]{:S(2)}) collective-permute-start(bf16[2,192,256]{2,1,0:T(8,128)(2,1)S(1)} %get-tuple-element.28.refs_2_.refs_4_), channel_id=1, source_target_pairs={{0,0},{1,2},{2,1},{3,3},{4,4},{5,6},{6,5},{7,7},{8,8},{9,10},{10,9... | collective-permute-start | bytes 589832 | tf_op jit(solution)/shard_map/halo/ppermute | solution.py:383
  9.7 2.9 %collective-permute-start.4 = (bf16[2,192,256]{2,1,0:T(8,128)(2,1)S(1)}, bf16[2,192,256]{2,1,0:T(8,128)(2,1)S(1)}, u32[]{:S(2)}, u32[]{:S(2)}) collective-permute-start(bf16[2,192,256]{2,1,0:T(8,128)(2,1)S(1)} %get-tuple-element.28.refs_2_.refs_4_), channel_id=1, source_target_pairs={{0,1},{1,0},{2,3},{3,2},{4,5},{5,4},{6,7},{7,6},{8,9},{9,8},{10,11... | collective-permute-start | bytes 589832 | tf_op jit(solution)/shard_map/halo/ppermute | solution.py:383
  12.7 0.0 collective-permute-done.3.refs_5_
  12.7 0.7 %collective-permute-start.7 = (bf16[2,192,256]{2,1,0:T(8,128)(2,1)S(1)}, bf16[2,192,256]{2,1,0:T(8,128)(2,1)S(1)}, u32[]{:S(2)}, u32[]{:S(2)}) collective-permute-start(bf16[2,192,256]{2,1,0:T(8,128)(2,1)S(1)} %collective-permute-done.3.refs_5_), channel_id=1, source_target_pairs={{0,0},{1,2},{2,1},{3,3},{4,4},{5,6},{6,5},{7,7},{8,8},{9,10},{10,9... | collective-permute-start | bytes 589832 | tf_op jit(solution)/shard_map/halo/ppermute | solution.py:383
  13.3 3.1 %collective-permute-done.1.refs_0_.refs_2_ = bf16[2,192,256]{2,1,0:T(8,128)(2,1)S(1)} collective-permute-done((bf16[2,192,256]{2,1,0:T(8,128)(2,1)S(1)}, bf16[2,192,256]{2,1,0:T(8,128)(2,1)S(1)}, u32[]{:S(2)}, u32[]{:S(2)}) %collective-permute-start.1) | collective-permute-done | bytes 196640 | tf_op jit(solution)/shard_map/halo/ppermute | solution.py:373
  16.5 0.0 collective-permute-start.5
  16.5 0.2 collective-permute-done.refs_1_
  16.7 1.4 %collective-permute-start.2 = (bf16[2,192,256]{2,1,0:T(8,128)(2,1)S(1)}, bf16[2,192,256]{2,1,0:T(8,128)(2,1)S(1)}, u32[]{:S(2)}, u32[]{:S(2)}) collective-permute-start(bf16[2,192,256]{2,1,0:T(8,128)(2,1)S(1)} %collective-permute-done.1.refs_0_.refs_2_), channel_id=1, source_target_pairs={{0,8},{8,0},{16,24},{24,16},{1,9},{9,1},{17,25},{25,17},{2,10},{10... | collective-permute-start | bytes 589832 | tf_op jit(solution)/shard_map/halo/ppermute | solution.py:373
  18.1 0.0 collective-permute-done.6.refs_4_.refs_6_
  18.1 0.0 collective-permute-done.4.refs_3_.refs_4_
  18.1 0.0 collective-permute-done.7.refs_7_
  18.1 0.0 collective-permute-done.5.refs_6_.refs_5_
  18.1 2.0 %attend.2 = (bf16[192,256]{1,0:T(8,128)(2,1)S(1)}, bf16[192,256]{1,0:T(8,128)(2,1)S(1)}, f32[8,384]{1,0:T(8,128)S(1)}) custom-call(bf16[2,192,256]{2,1,0:T(8,128)(2,1)S(1)} %get-tuple-element.27.refs_0_, bf16[2,192,256]{2,1,0:T(8,128)(2,1)S(1)} %collective-permute-done.refs_1_, bf16[2,192,256]{2,1,0:T(8,128)(2,1)S(1)} %get-tuple-element.28.refs_2_.refs_4_, ...), custom_call_target="tpu_custom_call" | custom-call | flops 452984832 | bytes 1781760 | tf_op jit(solution)/shard_map/attend/pallas_call | solution.py:336
  20.1 3.7 %collective-permute-done.2.refs_1_.refs_3_ = bf16[2,192,256]{2,1,0:T(8,128)(2,1)S(1)} collective-permute-done((bf16[2,192,256]{2,1,0:T(8,128)(2,1)S(1)}, bf16[2,192,256]{2,1,0:T(8,128)(2,1)S(1)}, u32[]{:S(2)}, u32[]{:S(2)}) %collective-permute-start.2) | collective-permute-done | bytes 196640 | tf_op jit(solution)/shard_map/halo/ppermute | solution.py:373
  23.8 2.0 %attend.3 = (bf16[192,256]{1,0:T(8,128)(2,1)S(1)}, bf16[192,256]{1,0:T(8,128)(2,1)S(1)}, f32[2,8,384]{2,1,0:T(8,128)S(1)}) custom-call(bf16[2,192,256]{2,1,0:T(8,128)(2,1)S(1)} %collective-permute-done.1.refs_0_.refs_2_, bf16[2,192,256]{2,1,0:T(8,128)(2,1)S(1)} %collective-permute-done.2.refs_1_.refs_3_, ...), custom_call_target="tpu_custom_call" | custom-call | flops 452984832 | bytes 1806336 | tf_op jit(solution)/shard_map/attend/pallas_call | solution.py:336
  25.8 3.4 %collective-permute-start.10 = (f32[2,8,384]{2,1,0:T(8,128)S(1)}, f32[2,8,384]{2,1,0:T(8,128)S(1)}, u32[]{:S(2)}, u32[]{:S(2)}) collective-permute-start(f32[2,8,384]{2,1,0:T(8,128)S(1)} %get-tuple-element.30.refs_8_), channel_id=1, source_target_pairs={{0,24},{8,16},{16,8},{24,0},{1,25},{9,17},{17,9},{25,1},{2,26},{10... | collective-permute-start | bytes 73736 | tf_op jit(solution)/shard_map/merge/ppermute | solution.py:373
  29.2 0.0 collective-permute-start.9
  29.2 1.0 %collective-permute-start.8 = (f32[2,8,384]{2,1,0:T(8,128)S(1)}, f32[2,8,384]{2,1,0:T(8,128)S(1)}, u32[]{:S(2)}, u32[]{:S(2)}) collective-permute-start(f32[2,8,384]{2,1,0:T(8,128)S(1)} %get-tuple-element.30.refs_8_), channel_id=1, source_target_pairs={{0,8},{8,0},{16,24},{24,16},{1,9},{9,1},{17,25},{25,17},{2,10},{10... | collective-permute-start | bytes 73736 | tf_op jit(solution)/shard_map/merge/ppermute | solution.py:373
  30.2 1.5 %collective-permute-done.10.refs_11_ = f32[2,8,384]{2,1,0:T(8,128)S(1)} collective-permute-done((f32[2,8,384]{2,1,0:T(8,128)S(1)}, f32[2,8,384]{2,1,0:T(8,128)S(1)}, u32[]{:S(2)}, u32[]{:S(2)}) %collective-permute-start.10) | collective-permute-done | bytes 24608 | tf_op jit(solution)/shard_map/merge/ppermute | solution.py:373
  31.7 2.2 %collective-permute-done.9.refs_10_ = f32[2,8,384]{2,1,0:T(8,128)S(1)} collective-permute-done((f32[2,8,384]{2,1,0:T(8,128)S(1)}, f32[2,8,384]{2,1,0:T(8,128)S(1)}, u32[]{:S(2)}, u32[]{:S(2)}) %collective-permute-start.9) | collective-permute-done | bytes 24608 | tf_op jit(solution)/shard_map/merge/ppermute | solution.py:373
  33.9 0.0 collective-permute-done.8.refs_9_
  33.9 3.1 %gradients.2 = (f32[2,768]{1,0:T(2,128)S(1)}, f32[2,768]{1,0:T(2,128)S(1)}, f32[192,128]{1,0:T(8,128)S(1)}, f32[2,128,768]{2,1,0:T(8,128)S(1)}, bf16[2,2,192,256...) custom-call(bf16[2,192,256]{2,1,0:T(8,128)(2,1)S(1)} %get-tuple-element.27.refs_0_, ...), custom_call_target="tpu_custom_call" | custom-call | flops 1509949440 | bytes 3354624 | tf_op jit(solution)/shard_map/gradients/pallas_call | solution.py:336
  37.0 0.1 collective-permute-start.17
  37.1 0.7 %collective-permute-start.18 = (bf16[2,2,192,256]{3,2,1,0:T(8,128)(2,1)S(1)}, bf16[2,2,192,256]{3,2,1,0:T(8,128)(2,1)S(1)}, u32[]{:S(2)}, u32[]{:S(2)}) collective-permute-start(bf16[2,2,192,256]{3,2,1,0:T(8,128)(2,1)S(1)} %get-tuple-element.47), channel_id=1, source_target_pairs={{0,0},{1,2},{2,1},{3,3},{4,4},{5,6},{6,5},{7,7},{8,8},{9,10},{10,9... | collective-permute-start | bytes 1179656 | tf_op jit(solution)/shard_map/gradients/ppermute | solution.py:441
  37.8 0.2 collective-permute-start.11
  38.0 2.0 %collective-permute-start.12 = (bf16[192,256]{1,0:T(8,128)(2,1)S(1)}, bf16[192,256]{1,0:T(8,128)(2,1)S(1)}, u32[]{:S(2)}, u32[]{:S(2)}) collective-permute-start(bf16[192,256]{1,0:T(8,128)(2,1)S(1)} %get-tuple-element.37), channel_id=1, source_target_pairs={{0,16},{8,24},{16,0},{24,8},{1,17},{9,25},{17,1},{25,9},{2,18},{10... | collective-permute-start | bytes 294920 | tf_op jit(solution)/shard_map/merge/ppermute | solution.py:373
  40.0 2.3 %collective-permute-start.13 = (bf16[192,256]{1,0:T(8,128)(2,1)S(1)}, bf16[192,256]{1,0:T(8,128)(2,1)S(1)}, u32[]{:S(2)}, u32[]{:S(2)}) collective-permute-start(bf16[192,256]{1,0:T(8,128)(2,1)S(1)} %get-tuple-element.38), channel_id=1, source_target_pairs={{0,24},{8,16},{16,8},{24,0},{1,25},{9,17},{17,9},{25,1},{2,26},{10... | collective-permute-start | bytes 294920 | tf_op jit(solution)/shard_map/merge/ppermute | solution.py:373
  42.2 0.2 collective-permute-done.11.refs_11_
  42.5 1.1 %collective-permute-done.12.refs_12_ = bf16[192,256]{1,0:T(8,128)(2,1)S(1)} collective-permute-done((bf16[192,256]{1,0:T(8,128)(2,1)S(1)}, bf16[192,256]{1,0:T(8,128)(2,1)S(1)}, u32[]{:S(2)}, u32[]{:S(2)}) %collective-permute-start.12) | collective-permute-done | bytes 98336 | tf_op jit(solution)/shard_map/merge/ppermute | solution.py:373
  43.6 3.9 %collective-permute-done.13.refs_13_ = bf16[192,256]{1,0:T(8,128)(2,1)S(1)} collective-permute-done((bf16[192,256]{1,0:T(8,128)(2,1)S(1)}, bf16[192,256]{1,0:T(8,128)(2,1)S(1)}, u32[]{:S(2)}, u32[]{:S(2)}) %collective-permute-start.13) | collective-permute-done | bytes 98336 | tf_op jit(solution)/shard_map/merge/ppermute | solution.py:373
  47.4 2.1 %gradients.3 = (bf16[192,256]{1,0:T(8,128)(2,1)S(1)}, bf16[192,256]{1,0:T(8,128)(2,1)S(1)}, bf16[192,256]{1,0:T(8,128)(2,1)S(1)}, bf16[192,256]{1,0:T(8,128)(2,1...) custom-call(bf16[2,192,256]{2,1,0:T(8,128)(2,1)S(1)} %get-tuple-element.27.refs_0_, ...), custom_call_target="tpu_custom_call" | custom-call | flops 754974720 | bytes 3354624 | tf_op jit(solution)/shard_map/gradients/pallas_call | solution.py:336
  49.5 0.0 collective-permute-done.17.refs_1_
  49.5 0.0 collective-permute-done.18.refs_2_
  49.5 0.1 fusion
  49.6 0.6 collective-permute-start.19
  50.2 3.5 %collective-permute-start.14 = (bf16[192,256]{1,0:T(8,128)(2,1)S(1)}, bf16[192,256]{1,0:T(8,128)(2,1)S(1)}, u32[]{:S(2)}, u32[]{:S(2)}) collective-permute-start(bf16[192,256]{1,0:T(8,128)(2,1)S(1)} %get-tuple-element.41), channel_id=1, source_target_pairs={{0,8},{8,0},{16,24},{24,16},{1,9},{9,1},{17,25},{25,17},{2,10},{10... | collective-permute-start | bytes 294920 | tf_op jit(solution)/shard_map/return/ppermute | solution.py:373
  53.6 1.3 %collective-permute-start.15 = (bf16[192,256]{1,0:T(8,128)(2,1)S(1)}, bf16[192,256]{1,0:T(8,128)(2,1)S(1)}, u32[]{:S(2)}, u32[]{:S(2)}) collective-permute-start(bf16[192,256]{1,0:T(8,128)(2,1)S(1)} %get-tuple-element.42), channel_id=1, source_target_pairs={{0,16},{8,24},{16,0},{24,8},{1,17},{9,25},{17,1},{25,9},{2,18},{10... | collective-permute-start | bytes 294920 | tf_op jit(solution)/shard_map/return/ppermute | solution.py:373
  54.9 1.5 %collective-permute-start.16 = (bf16[192,256]{1,0:T(8,128)(2,1)S(1)}, bf16[192,256]{1,0:T(8,128)(2,1)S(1)}, u32[]{:S(2)}, u32[]{:S(2)}) collective-permute-start(bf16[192,256]{1,0:T(8,128)(2,1)S(1)} %get-tuple-element.43), channel_id=1, source_target_pairs={{0,24},{8,16},{16,8},{24,0},{1,25},{9,17},{17,9},{25,1},{2,26},{10... | collective-permute-start | bytes 294920 | tf_op jit(solution)/shard_map/return/ppermute | solution.py:373
  56.3 0.8 %collective-permute-done.14.refs_1_ = bf16[192,256]{1,0:T(8,128)(2,1)S(1)} collective-permute-done((bf16[192,256]{1,0:T(8,128)(2,1)S(1)}, bf16[192,256]{1,0:T(8,128)(2,1)S(1)}, u32[]{:S(2)}, u32[]{:S(2)}) %collective-permute-start.14) | collective-permute-done | bytes 98336 | tf_op jit(solution)/shard_map/return/ppermute | solution.py:373
  57.2 7.2 %collective-permute-done.15.refs_2_ = bf16[192,256]{1,0:T(8,128)(2,1)S(1)} collective-permute-done((bf16[192,256]{1,0:T(8,128)(2,1)S(1)}, bf16[192,256]{1,0:T(8,128)(2,1)S(1)}, u32[]{:S(2)}, u32[]{:S(2)}) %collective-permute-start.15) | collective-permute-done | bytes 98336 | tf_op jit(solution)/shard_map/return/ppermute | solution.py:373
  64.4 0.0 collective-permute-done.16.refs_3_
  64.4 0.8 %finish.2 = bf16[192,256]{1,0:T(8,128)(2,1)} custom-call(bf16[192,256]{1,0:T(8,128)(2,1)S(1)} %get-tuple-element.40.refs_0_, bf16[192,256]{1,0:T(8,128)(2,1)S(1)} %collective-permute-done.14.refs_1_, bf16[192,256]{1,0:T(8,128)(2,1)S(1)} %collective-permute-done.15.refs_2_, bf16[192,256]{1,0:T(8,128)(2,1)S(1)} %collective-permute-done.16.refs_3_, ...), custom_call_target="tpu_custom_call" | custom-call | bytes 786432 | tf_op jit(solution)/shard_map/finish/pallas_call | solution.py:336
  65.2 0.0 collective-permute-done.19.refs_3_
  65.2 0.9 %finish.3 = (bf16[192,256]{1,0:T(8,128)(2,1)}, bf16[192,256]{1,0:T(8,128)(2,1)}) custom-call(bf16[2,2,192,256]{3,2,1,0:T(8,128)(2,1)S(1)} %get-tuple-element.45.refs_0_, bf16[2,2,192,256]{3,2,1,0:T(8,128)(2,1)S(1)} %collective-permute-done.17.refs_1_, bf16[2,2,192,256]{3,2,1,0:T(8,128)(2,1)S(1)} %collective-permute-done.18.refs_2_, ...), custom_call_target="tpu_custom_call" | custom-call | bytes 1867776 | tf_op jit(solution)/shard_map/finish/pallas_call | solution.py:336
Async XLA Ops:
  1.9 10.8 %collective-permute-start.3 = (bf16[2,192,256]{2,1,0:T(8,128)(2,1)S(1)}, bf16[2,192,256]{2,1,0:T(8,128)(2,1)S(1)}, u32[]{:S(2)}, u32[]{:S(2)}) collective-permute-start(bf16[2,192,256]{2,1,0:T(8,128)(2,1)S(1)} %get-tuple-element.28.refs_2_.refs_4_), channel_id=1, source_target_pairs={{0,4},{4,0},{1,5},{5,1},{2,6},{6,2},{3,7},{7,3},{8,12},{12,8},{9,1... | collective-permute-start | bytes 589832 | tf_op jit(solution)/shard_map/halo/ppermute | solution.py:378
  4.9 11.6 %collective-permute-start.1 = (bf16[2,192,256]{2,1,0:T(8,128)(2,1)S(1)}, bf16[2,192,256]{2,1,0:T(8,128)(2,1)S(1)}, u32[]{:S(2)}, u32[]{:S(2)}) collective-permute-start(bf16[2,192,256]{2,1,0:T(8,128)(2,1)S(1)} %get-tuple-element.27.refs_0_), channel_id=1, source_target_pairs={{0,16},{8,24},{16,0},{24,8},{1,17},{9,25},{17,1},{25,9},{2,18},{10... | collective-permute-start | bytes 589832 | tf_op jit(solution)/shard_map/halo/ppermute | solution.py:373
  7.5 9.2 %collective-permute-start = (bf16[2,192,256]{2,1,0:T(8,128)(2,1)S(1)}, bf16[2,192,256]{2,1,0:T(8,128)(2,1)S(1)}, u32[]{:S(2)}, u32[]{:S(2)}) collective-permute-start(bf16[2,192,256]{2,1,0:T(8,128)(2,1)S(1)} %get-tuple-element.27.refs_0_), channel_id=1, source_target_pairs={{0,8},{8,0},{16,24},{24,16},{1,9},{9,1},{17,25},{25,17},{2,10},{10... | collective-permute-start | bytes 589832 | tf_op jit(solution)/shard_map/halo/ppermute | solution.py:373
  9.1 9.0 %collective-permute-start.6 = (bf16[2,192,256]{2,1,0:T(8,128)(2,1)S(1)}, bf16[2,192,256]{2,1,0:T(8,128)(2,1)S(1)}, u32[]{:S(2)}, u32[]{:S(2)}) collective-permute-start(bf16[2,192,256]{2,1,0:T(8,128)(2,1)S(1)} %get-tuple-element.28.refs_2_.refs_4_), channel_id=1, source_target_pairs={{0,0},{1,2},{2,1},{3,3},{4,4},{5,6},{6,5},{7,7},{8,8},{9,10},{10,9... | collective-permute-start | bytes 589832 | tf_op jit(solution)/shard_map/halo/ppermute | solution.py:383
  9.7 8.4 %collective-permute-start.4 = (bf16[2,192,256]{2,1,0:T(8,128)(2,1)S(1)}, bf16[2,192,256]{2,1,0:T(8,128)(2,1)S(1)}, u32[]{:S(2)}, u32[]{:S(2)}) collective-permute-start(bf16[2,192,256]{2,1,0:T(8,128)(2,1)S(1)} %get-tuple-element.28.refs_2_.refs_4_), channel_id=1, source_target_pairs={{0,1},{1,0},{2,3},{3,2},{4,5},{5,4},{6,7},{7,6},{8,9},{9,8},{10,11... | collective-permute-start | bytes 589832 | tf_op jit(solution)/shard_map/halo/ppermute | solution.py:383
  12.7 5.4 %collective-permute-start.7 = (bf16[2,192,256]{2,1,0:T(8,128)(2,1)S(1)}, bf16[2,192,256]{2,1,0:T(8,128)(2,1)S(1)}, u32[]{:S(2)}, u32[]{:S(2)}) collective-permute-start(bf16[2,192,256]{2,1,0:T(8,128)(2,1)S(1)} %collective-permute-done.3.refs_5_), channel_id=1, source_target_pairs={{0,0},{1,2},{2,1},{3,3},{4,4},{5,6},{6,5},{7,7},{8,8},{9,10},{10,9... | collective-permute-start | bytes 589832 | tf_op jit(solution)/shard_map/halo/ppermute | solution.py:383
  16.5 1.6 %collective-permute-start.5 = (bf16[2,192,256]{2,1,0:T(8,128)(2,1)S(1)}, bf16[2,192,256]{2,1,0:T(8,128)(2,1)S(1)}, u32[]{:S(2)}, u32[]{:S(2)}) collective-permute-start(bf16[2,192,256]{2,1,0:T(8,128)(2,1)S(1)} %collective-permute-done.3.refs_5_), channel_id=1, source_target_pairs={{0,1},{1,0},{2,3},{3,2},{4,5},{5,4},{6,7},{7,6},{8,9},{9,8},{10,11... | collective-permute-start | bytes 589832 | tf_op jit(solution)/shard_map/halo/ppermute | solution.py:383
  16.7 7.1 %collective-permute-start.2 = (bf16[2,192,256]{2,1,0:T(8,128)(2,1)S(1)}, bf16[2,192,256]{2,1,0:T(8,128)(2,1)S(1)}, u32[]{:S(2)}, u32[]{:S(2)}) collective-permute-start(bf16[2,192,256]{2,1,0:T(8,128)(2,1)S(1)} %collective-permute-done.1.refs_0_.refs_2_), channel_id=1, source_target_pairs={{0,8},{8,0},{16,24},{24,16},{1,9},{9,1},{17,25},{25,17},{2,10},{10... | collective-permute-start | bytes 589832 | tf_op jit(solution)/shard_map/halo/ppermute | solution.py:373
  25.8 6.0 %collective-permute-start.10 = (f32[2,8,384]{2,1,0:T(8,128)S(1)}, f32[2,8,384]{2,1,0:T(8,128)S(1)}, u32[]{:S(2)}, u32[]{:S(2)}) collective-permute-start(f32[2,8,384]{2,1,0:T(8,128)S(1)} %get-tuple-element.30.refs_8_), channel_id=1, source_target_pairs={{0,24},{8,16},{16,8},{24,0},{1,25},{9,17},{17,9},{25,1},{2,26},{10... | collective-permute-start | bytes 73736 | tf_op jit(solution)/shard_map/merge/ppermute | solution.py:373
  29.2 4.7 %collective-permute-start.9 = (f32[2,8,384]{2,1,0:T(8,128)S(1)}, f32[2,8,384]{2,1,0:T(8,128)S(1)}, u32[]{:S(2)}, u32[]{:S(2)}) collective-permute-start(f32[2,8,384]{2,1,0:T(8,128)S(1)} %get-tuple-element.30.refs_8_), channel_id=1, source_target_pairs={{0,16},{8,24},{16,0},{24,8},{1,17},{9,25},{17,1},{25,9},{2,18},{10... | collective-permute-start | bytes 73736 | tf_op jit(solution)/shard_map/merge/ppermute | solution.py:373
  29.2 4.7 %collective-permute-start.8 = (f32[2,8,384]{2,1,0:T(8,128)S(1)}, f32[2,8,384]{2,1,0:T(8,128)S(1)}, u32[]{:S(2)}, u32[]{:S(2)}) collective-permute-start(f32[2,8,384]{2,1,0:T(8,128)S(1)} %get-tuple-element.30.refs_8_), channel_id=1, source_target_pairs={{0,8},{8,0},{16,24},{24,16},{1,9},{9,1},{17,25},{25,17},{2,10},{10... | collective-permute-start | bytes 73736 | tf_op jit(solution)/shard_map/merge/ppermute | solution.py:373
  37.0 12.5 %collective-permute-start.17 = (bf16[2,2,192,256]{3,2,1,0:T(8,128)(2,1)S(1)}, bf16[2,2,192,256]{3,2,1,0:T(8,128)(2,1)S(1)}, u32[]{:S(2)}, u32[]{:S(2)}) collective-permute-start(bf16[2,2,192,256]{3,2,1,0:T(8,128)(2,1)S(1)} %get-tuple-element.46), channel_id=1, source_target_pairs={{0,1},{1,0},{2,3},{3,2},{4,5},{5,4},{6,7},{7,6},{8,9},{9,8},{10,11... | collective-permute-start | bytes 1179656 | tf_op jit(solution)/shard_map/gradients/ppermute | solution.py:441
  37.1 12.4 %collective-permute-start.18 = (bf16[2,2,192,256]{3,2,1,0:T(8,128)(2,1)S(1)}, bf16[2,2,192,256]{3,2,1,0:T(8,128)(2,1)S(1)}, u32[]{:S(2)}, u32[]{:S(2)}) collective-permute-start(bf16[2,2,192,256]{3,2,1,0:T(8,128)(2,1)S(1)} %get-tuple-element.47), channel_id=1, source_target_pairs={{0,0},{1,2},{2,1},{3,3},{4,4},{5,6},{6,5},{7,7},{8,8},{9,10},{10,9... | collective-permute-start | bytes 1179656 | tf_op jit(solution)/shard_map/gradients/ppermute | solution.py:441
  37.8 4.7 %collective-permute-start.11 = (bf16[192,256]{1,0:T(8,128)(2,1)S(1)}, bf16[192,256]{1,0:T(8,128)(2,1)S(1)}, u32[]{:S(2)}, u32[]{:S(2)}) collective-permute-start(bf16[192,256]{1,0:T(8,128)(2,1)S(1)} %get-tuple-element.36), channel_id=1, source_target_pairs={{0,8},{8,0},{16,24},{24,16},{1,9},{9,1},{17,25},{25,17},{2,10},{10... | collective-permute-start | bytes 294920 | tf_op jit(solution)/shard_map/merge/ppermute | solution.py:373
  38.0 5.6 %collective-permute-start.12 = (bf16[192,256]{1,0:T(8,128)(2,1)S(1)}, bf16[192,256]{1,0:T(8,128)(2,1)S(1)}, u32[]{:S(2)}, u32[]{:S(2)}) collective-permute-start(bf16[192,256]{1,0:T(8,128)(2,1)S(1)} %get-tuple-element.37), channel_id=1, source_target_pairs={{0,16},{8,24},{16,0},{24,8},{1,17},{9,25},{17,1},{25,9},{2,18},{10... | collective-permute-start | bytes 294920 | tf_op jit(solution)/shard_map/merge/ppermute | solution.py:373
  40.0 7.5 %collective-permute-start.13 = (bf16[192,256]{1,0:T(8,128)(2,1)S(1)}, bf16[192,256]{1,0:T(8,128)(2,1)S(1)}, u32[]{:S(2)}, u32[]{:S(2)}) collective-permute-start(bf16[192,256]{1,0:T(8,128)(2,1)S(1)} %get-tuple-element.38), channel_id=1, source_target_pairs={{0,24},{8,16},{16,8},{24,0},{1,25},{9,17},{17,9},{25,1},{2,26},{10... | collective-permute-start | bytes 294920 | tf_op jit(solution)/shard_map/merge/ppermute | solution.py:373
  49.6 15.6 %collective-permute-start.19 = (bf16[2,192,256]{2,1,0:T(8,128)(2,1)S(1)}, bf16[2,192,256]{2,1,0:T(8,128)(2,1)S(1)}, u32[]{:S(2)}, u32[]{:S(2)}) collective-permute-start(bf16[2,192,256]{2,1,0:T(8,128)(2,1)S(1)} %fusion), channel_id=1, source_target_pairs={{0,4},{4,0},{1,5},{5,1},{2,6},{6,2},{3,7},{7,3},{8,12},{12,8},{9,1... | collective-permute-start | bytes 589832 | tf_op jit(solution)/shard_map/return/ppermute | solution.py:451
  50.2 7.0 %collective-permute-start.14 = (bf16[192,256]{1,0:T(8,128)(2,1)S(1)}, bf16[192,256]{1,0:T(8,128)(2,1)S(1)}, u32[]{:S(2)}, u32[]{:S(2)}) collective-permute-start(bf16[192,256]{1,0:T(8,128)(2,1)S(1)} %get-tuple-element.41), channel_id=1, source_target_pairs={{0,8},{8,0},{16,24},{24,16},{1,9},{9,1},{17,25},{25,17},{2,10},{10... | collective-permute-start | bytes 294920 | tf_op jit(solution)/shard_map/return/ppermute | solution.py:373
  53.6 10.7 %collective-permute-start.15 = (bf16[192,256]{1,0:T(8,128)(2,1)S(1)}, bf16[192,256]{1,0:T(8,128)(2,1)S(1)}, u32[]{:S(2)}, u32[]{:S(2)}) collective-permute-start(bf16[192,256]{1,0:T(8,128)(2,1)S(1)} %get-tuple-element.42), channel_id=1, source_target_pairs={{0,16},{8,24},{16,0},{24,8},{1,17},{9,25},{17,1},{25,9},{2,18},{10... | collective-permute-start | bytes 294920 | tf_op jit(solution)/shard_map/return/ppermute | solution.py:373
  54.9 9.5 %collective-permute-start.16 = (bf16[192,256]{1,0:T(8,128)(2,1)S(1)}, bf16[192,256]{1,0:T(8,128)(2,1)S(1)}, u32[]{:S(2)}, u32[]{:S(2)}) collective-permute-start(bf16[192,256]{1,0:T(8,128)(2,1)S(1)} %get-tuple-element.43), channel_id=1, source_target_pairs={{0,24},{8,16},{16,8},{24,0},{1,25},{9,17},{17,9},{25,1},{2,26},{10... | collective-permute-start | bytes 294920 | tf_op jit(solution)/shard_map/return/ppermute | solution.py:373

commit v3 on v2

--- a/solution.py
+++ b/solution.py
@@ -332,6 +332,7 @@
 
 def call(kernel, out_shape, args, flops=0, exps=0, scratch=(), space=pltpu.VMEM, limit=VMEM_LIMIT):
     shapes = jax.tree.leaves(out_shape)
+    flops *= 8
     moved = sum(math.prod(x.shape) * x.dtype.itemsize for x in list(args) + shapes)
     return pl.pallas_call(
         kernel,

time: 66.3 us -> 58.7 us (0.89)
  the two profiles are of different devices: /device:TPU:0 before, /device:TPU:1 now
where the time goes in v3:
time: 58.7 us; the launch traced here: 58.5 us
  starting transfers between devices  31.3 us (53%)
  waiting for transfers between devices  14.4 us (25%)
  Pallas kernels  12 us (20%)
  between operations  0.73 us (1%)
    ppermute x12, starting transfers between devices, other_frames(): lax.ppermute(x, 'ta', [(i, i ^ distance) for i in range(sizes['ta'])])  15.3 us
    pallas_call x7, Pallas kernels, call(): pl.pallas_call(kernel, out_shape=out_shape, in_specs=[pl.BlockSpec(memory...  12 us
    ppermute x4, starting transfers between devices, shards(): lax.ppermute(block, 'wa', pairs)  8.2 us
    ppermute x12, waiting for transfers between devices, other_frames(): lax.ppermute(x, 'ta', [(i, i ^ distance) for i in range(sizes['ta'])])  7.73 us
    ppermute x2, starting transfers between devices, shards(): sides = [lax.ppermute(x, 'wa', pairs) for x, pairs in zip(sides, col_sides)]  5.38 us
    ppermute x2, waiting for transfers between devices, shards(): sides = [lax.ppermute(x, 'wa', pairs) for x, pairs in zip(sides, col_sides)]  4.24 us
    ppermute x4, waiting for transfers between devices, shards(): lax.ppermute(block, 'wa', pairs)  2.4 us
    ppermute x1, starting transfers between devices, shards(): kv_rows = [kv] + [lax.ppermute(kv, 'ha', pairs) for pairs in row_sides]  2.11 us
  transfers between devices with their start and end apart: 20, of which 6 were waited for; matrix products, arithmetic and copies ran while one was open for 0% of the time, Pallas kernels for 14%

profile of v3, /device:TPU:1, one launch (start us, length us, event | category | flops | bytes accessed | tf_op | source)
XLA Modules:
  0.0 58.5 jit_solution(12854263009166825318)
XLA Ops:
  0.6 1.3 %rotate.1 = (bf16[2,192,256]{2,1,0:T(8,128)(2,1)S(1)}, bf16[2,192,256]{2,1,0:T(8,128)(2,1)S(1)}, f32[3,192,128]{2,1,0:T(8,128)S(1)}) custom-call(bf16[192,256]{1,0:T(8,128)(2,1)} %bitcast.11, bf16[192,256]{1,0:T(8,128)(2,1)} %bitcast.12, bf16[192,256]{1,0:T(8,128)(2,1)} %bitcast.13, bf16[192,256]{1,0:T(8,128)(2,1)} %bitcast.14, ...), custom_call_target="tpu_custom_call" | custom-call | bytes 1179648 | tf_op jit(solution)/shard_map/rotate/pallas_call | solution.py:337
  1.9 2.1 %collective-permute-start.3 = (bf16[2,192,256]{2,1,0:T(8,128)(2,1)S(1)}, bf16[2,192,256]{2,1,0:T(8,128)(2,1)S(1)}, u32[]{:S(2)}, u32[]{:S(2)}) collective-permute-start(bf16[2,192,256]{2,1,0:T(8,128)(2,1)S(1)} %get-tuple-element.28.refs_2_.refs_4_), channel_id=1, source_target_pairs={{0,4},{4,0},{1,5},{5,1},{2,6},{6,2},{3,7},{7,3},{8,12},{12,8},{9,1... | collective-permute-start | bytes 589832 | tf_op jit(solution)/shard_map/halo/ppermute | solution.py:379
  4.0 2.3 %collective-permute-start.1 = (bf16[2,192,256]{2,1,0:T(8,128)(2,1)S(1)}, bf16[2,192,256]{2,1,0:T(8,128)(2,1)S(1)}, u32[]{:S(2)}, u32[]{:S(2)}) collective-permute-start(bf16[2,192,256]{2,1,0:T(8,128)(2,1)S(1)} %get-tuple-element.27.refs_0_), channel_id=1, source_target_pairs={{0,16},{8,24},{16,0},{24,8},{1,17},{9,25},{17,1},{25,9},{2,18},{10... | collective-permute-start | bytes 589832 | tf_op jit(solution)/shard_map/halo/ppermute | solution.py:374
  6.3 1.3 %collective-permute-start = (bf16[2,192,256]{2,1,0:T(8,128)(2,1)S(1)}, bf16[2,192,256]{2,1,0:T(8,128)(2,1)S(1)}, u32[]{:S(2)}, u32[]{:S(2)}) collective-permute-start(bf16[2,192,256]{2,1,0:T(8,128)(2,1)S(1)} %get-tuple-element.27.refs_0_), channel_id=1, source_target_pairs={{0,8},{8,0},{16,24},{24,16},{1,9},{9,1},{17,25},{25,17},{2,10},{10... | collective-permute-start | bytes 589832 | tf_op jit(solution)/shard_map/halo/ppermute | solution.py:374
  7.6 4.5 %collective-permute-start.6 = (bf16[2,192,256]{2,1,0:T(8,128)(2,1)S(1)}, bf16[2,192,256]{2,1,0:T(8,128)(2,1)S(1)}, u32[]{:S(2)}, u32[]{:S(2)}) collective-permute-start(bf16[2,192,256]{2,1,0:T(8,128)(2,1)S(1)} %get-tuple-element.28.refs_2_.refs_4_), channel_id=1, source_target_pairs={{0,0},{1,2},{2,1},{3,3},{4,4},{5,6},{6,5},{7,7},{8,8},{9,10},{10,9... | collective-permute-start | bytes 589832 | tf_op jit(solution)/shard_map/halo/ppermute | solution.py:384
  12.2 0.1 collective-permute-start.4
  12.2 0.0 collective-permute-done.3.refs_5_
  12.2 1.9 %collective-permute-start.7 = (bf16[2,192,256]{2,1,0:T(8,128)(2,1)S(1)}, bf16[2,192,256]{2,1,0:T(8,128)(2,1)S(1)}, u32[]{:S(2)}, u32[]{:S(2)}) collective-permute-start(bf16[2,192,256]{2,1,0:T(8,128)(2,1)S(1)} %collective-permute-done.3.refs_5_), channel_id=1, source_target_pairs={{0,0},{1,2},{2,1},{3,3},{4,4},{5,6},{6,5},{7,7},{8,8},{9,10},{10,9... | collective-permute-start | bytes 589832 | tf_op jit(solution)/shard_map/halo/ppermute | solution.py:384
  14.2 0.7 %collective-permute-done.1.refs_0_.refs_2_ = bf16[2,192,256]{2,1,0:T(8,128)(2,1)S(1)} collective-permute-done((bf16[2,192,256]{2,1,0:T(8,128)(2,1)S(1)}, bf16[2,192,256]{2,1,0:T(8,128)(2,1)S(1)}, u32[]{:S(2)}, u32[]{:S(2)}) %collective-permute-start.1) | collective-permute-done | bytes 196640 | tf_op jit(solution)/shard_map/halo/ppermute | solution.py:374
  14.9 1.7 %collective-permute-start.5 = (bf16[2,192,256]{2,1,0:T(8,128)(2,1)S(1)}, bf16[2,192,256]{2,1,0:T(8,128)(2,1)S(1)}, u32[]{:S(2)}, u32[]{:S(2)}) collective-permute-start(bf16[2,192,256]{2,1,0:T(8,128)(2,1)S(1)} %collective-permute-done.3.refs_5_), channel_id=1, source_target_pairs={{0,1},{1,0},{2,3},{3,2},{4,5},{5,4},{6,7},{7,6},{8,9},{9,8},{10,11... | collective-permute-start | bytes 589832 | tf_op jit(solution)/shard_map/halo/ppermute | solution.py:384
  16.5 0.0 collective-permute-done.refs_1_
  16.5 0.3 collective-permute-start.2
  16.8 0.0 collective-permute-done.6.refs_4_.refs_6_
  16.8 0.0 collective-permute-done.4.refs_3_.refs_4_
  16.8 2.4 %collective-permute-done.7.refs_7_ = bf16[2,192,256]{2,1,0:T(8,128)(2,1)S(1)} collective-permute-done((bf16[2,192,256]{2,1,0:T(8,128)(2,1)S(1)}, bf16[2,192,256]{2,1,0:T(8,128)(2,1)S(1)}, u32[]{:S(2)}, u32[]{:S(2)}) %collective-permute-start.7) | collective-permute-done | bytes 196640 | tf_op jit(solution)/shard_map/halo/ppermute | solution.py:384
  19.2 0.0 collective-permute-done.5.refs_6_.refs_5_
  19.2 2.0 %attend.2 = (bf16[192,256]{1,0:T(8,128)(2,1)S(1)}, bf16[192,256]{1,0:T(8,128)(2,1)S(1)}, f32[8,384]{1,0:T(8,128)S(1)}) custom-call(bf16[2,192,256]{2,1,0:T(8,128)(2,1)S(1)} %get-tuple-element.27.refs_0_, bf16[2,192,256]{2,1,0:T(8,128)(2,1)S(1)} %collective-permute-done.refs_1_, bf16[2,192,256]{2,1,0:T(8,128)(2,1)S(1)} %get-tuple-element.28.refs_2_.refs_4_, ...), custom_call_target="tpu_custom_call" | custom-call | flops 3623878656 | bytes 1781760 | tf_op jit(solution)/shard_map/attend/pallas_call | solution.py:337
  21.2 1.7 %collective-permute-done.2.refs_1_.refs_3_ = bf16[2,192,256]{2,1,0:T(8,128)(2,1)S(1)} collective-permute-done((bf16[2,192,256]{2,1,0:T(8,128)(2,1)S(1)}, bf16[2,192,256]{2,1,0:T(8,128)(2,1)S(1)}, u32[]{:S(2)}, u32[]{:S(2)}) %collective-permute-start.2) | collective-permute-done | bytes 196640 | tf_op jit(solution)/shard_map/halo/ppermute | solution.py:374
  22.9 2.0 %attend.3 = (bf16[192,256]{1,0:T(8,128)(2,1)S(1)}, bf16[192,256]{1,0:T(8,128)(2,1)S(1)}, f32[2,8,384]{2,1,0:T(8,128)S(1)}) custom-call(bf16[2,192,256]{2,1,0:T(8,128)(2,1)S(1)} %collective-permute-done.1.refs_0_.refs_2_, bf16[2,192,256]{2,1,0:T(8,128)(2,1)S(1)} %collective-permute-done.2.refs_1_.refs_3_, ...), custom_call_target="tpu_custom_call" | custom-call | flops 3623878656 | bytes 1806336 | tf_op jit(solution)/shard_map/attend/pallas_call | solution.py:337
  24.8 3.3 %collective-permute-start.10 = (f32[2,8,384]{2,1,0:T(8,128)S(1)}, f32[2,8,384]{2,1,0:T(8,128)S(1)}, u32[]{:S(2)}, u32[]{:S(2)}) collective-permute-start(f32[2,8,384]{2,1,0:T(8,128)S(1)} %get-tuple-element.30.refs_8_), channel_id=1, source_target_pairs={{0,24},{8,16},{16,8},{24,0},{1,25},{9,17},{17,9},{25,1},{2,26},{10... | collective-permute-start | bytes 73736 | tf_op jit(solution)/shard_map/merge/ppermute | solution.py:374
  28.2 0.0 collective-permute-start.9
  28.2 0.4 collective-permute-start.8
  28.5 1.1 %collective-permute-start.11 = (bf16[192,256]{1,0:T(8,128)(2,1)S(1)}, bf16[192,256]{1,0:T(8,128)(2,1)S(1)}, u32[]{:S(2)}, u32[]{:S(2)}) collective-permute-start(bf16[192,256]{1,0:T(8,128)(2,1)S(1)} %get-tuple-element.36), channel_id=1, source_target_pairs={{0,8},{8,0},{16,24},{24,16},{1,9},{9,1},{17,25},{25,17},{2,10},{10... | collective-permute-start | bytes 294920 | tf_op jit(solution)/shard_map/merge/ppermute | solution.py:374
  29.6 2.4 %collective-permute-start.12 = (bf16[192,256]{1,0:T(8,128)(2,1)S(1)}, bf16[192,256]{1,0:T(8,128)(2,1)S(1)}, u32[]{:S(2)}, u32[]{:S(2)}) collective-permute-start(bf16[192,256]{1,0:T(8,128)(2,1)S(1)} %get-tuple-element.37), channel_id=1, source_target_pairs={{0,16},{8,24},{16,0},{24,8},{1,17},{9,25},{17,1},{25,9},{2,18},{10... | collective-permute-start | bytes 294920 | tf_op jit(solution)/shard_map/merge/ppermute | solution.py:374
  32.0 0.0 collective-permute-done.10.refs_11_
  32.0 0.6 %collective-permute-start.13 = (bf16[192,256]{1,0:T(8,128)(2,1)S(1)}, bf16[192,256]{1,0:T(8,128)(2,1)S(1)}, u32[]{:S(2)}, u32[]{:S(2)}) collective-permute-start(bf16[192,256]{1,0:T(8,128)(2,1)S(1)} %get-tuple-element.38), channel_id=1, source_target_pairs={{0,24},{8,16},{16,8},{24,0},{1,25},{9,17},{17,9},{25,1},{2,26},{10... | collective-permute-start | bytes 294920 | tf_op jit(solution)/shard_map/merge/ppermute | solution.py:374
  32.7 0.0 collective-permute-done.9.refs_10_
  32.7 0.0 collective-permute-done.8.refs_9_
  32.7 3.1 %gradients.2 = (f32[2,768]{1,0:T(2,128)S(1)}, f32[2,768]{1,0:T(2,128)S(1)}, f32[192,128]{1,0:T(8,128)S(1)}, f32[2,128,768]{2,1,0:T(8,128)S(1)}, bf16[2,2,192,256...) custom-call(bf16[2,192,256]{2,1,0:T(8,128)(2,1)S(1)} %get-tuple-element.27.refs_0_, ...), custom_call_target="tpu_custom_call" | custom-call | flops 12079595520 | bytes 3354624 | tf_op jit(solution)/shard_map/gradients/pallas_call | solution.py:337
  35.8 2.3 %collective-permute-start.17 = (bf16[2,2,192,256]{3,2,1,0:T(8,128)(2,1)S(1)}, bf16[2,2,192,256]{3,2,1,0:T(8,128)(2,1)S(1)}, u32[]{:S(2)}, u32[]{:S(2)}) collective-permute-start(bf16[2,2,192,256]{3,2,1,0:T(8,128)(2,1)S(1)} %get-tuple-element.46), channel_id=1, source_target_pairs={{0,1},{1,0},{2,3},{3,2},{4,5},{5,4},{6,7},{7,6},{8,9},{9,8},{10,11... | collective-permute-start | bytes 1179656 | tf_op jit(solution)/shard_map/gradients/ppermute | solution.py:442
  38.1 3.0 %collective-permute-start.18 = (bf16[2,2,192,256]{3,2,1,0:T(8,128)(2,1)S(1)}, bf16[2,2,192,256]{3,2,1,0:T(8,128)(2,1)S(1)}, u32[]{:S(2)}, u32[]{:S(2)}) collective-permute-start(bf16[2,2,192,256]{3,2,1,0:T(8,128)(2,1)S(1)} %get-tuple-element.47), channel_id=1, source_target_pairs={{0,0},{1,2},{2,1},{3,3},{4,4},{5,6},{6,5},{7,7},{8,8},{9,10},{10,9... | collective-permute-start | bytes 1179656 | tf_op jit(solution)/shard_map/gradients/ppermute | solution.py:442
  41.1 0.0 collective-permute-done.11.refs_11_
  41.2 0.0 collective-permute-done.12.refs_12_
  41.2 0.0 collective-permute-done.13.refs_13_
  41.2 2.1 %gradients.3 = (bf16[192,256]{1,0:T(8,128)(2,1)S(1)}, bf16[192,256]{1,0:T(8,128)(2,1)S(1)}, bf16[192,256]{1,0:T(8,128)(2,1)S(1)}, bf16[192,256]{1,0:T(8,128)(2,1...) custom-call(bf16[2,192,256]{2,1,0:T(8,128)(2,1)S(1)} %get-tuple-element.27.refs_0_, ...), custom_call_target="tpu_custom_call" | custom-call | flops 6039797760 | bytes 3354624 | tf_op jit(solution)/shard_map/gradients/pallas_call | solution.py:337
  43.2 0.0 collective-permute-done.17.refs_1_
  43.2 4.2 %collective-permute-done.18.refs_2_ = bf16[2,2,192,256]{3,2,1,0:T(8,128)(2,1)S(1)} collective-permute-done((bf16[2,2,192,256]{3,2,1,0:T(8,128)(2,1)S(1)}, bf16[2,2,192,256]{3,2,1,0:T(8,128)(2,1)S(1)}, u32[]{:S(2)}, u32[]{:S(2)}) %collective-permute-start.18) | collective-permute-done | bytes 393248 | tf_op jit(solution)/shard_map/gradients/ppermute | solution.py:442
  47.5 0.1 fusion
  47.6 0.3 collective-permute-start.19
  47.9 0.0 collective-permute-start.14
  47.9 3.1 %collective-permute-start.15 = (bf16[192,256]{1,0:T(8,128)(2,1)S(1)}, bf16[192,256]{1,0:T(8,128)(2,1)S(1)}, u32[]{:S(2)}, u32[]{:S(2)}) collective-permute-start(bf16[192,256]{1,0:T(8,128)(2,1)S(1)} %get-tuple-element.42), channel_id=1, source_target_pairs={{0,16},{8,24},{16,0},{24,8},{1,17},{9,25},{17,1},{25,9},{2,18},{10... | collective-permute-start | bytes 294920 | tf_op jit(solution)/shard_map/return/ppermute | solution.py:374
  51.0 0.4 collective-permute-start.16
  51.4 2.2 %collective-permute-done.14.refs_1_ = bf16[192,256]{1,0:T(8,128)(2,1)S(1)} collective-permute-done((bf16[192,256]{1,0:T(8,128)(2,1)S(1)}, bf16[192,256]{1,0:T(8,128)(2,1)S(1)}, u32[]{:S(2)}, u32[]{:S(2)}) %collective-permute-start.14) | collective-permute-done | bytes 98336 | tf_op jit(solution)/shard_map/return/ppermute | solution.py:374
  53.7 3.1 %collective-permute-done.15.refs_2_ = bf16[192,256]{1,0:T(8,128)(2,1)S(1)} collective-permute-done((bf16[192,256]{1,0:T(8,128)(2,1)S(1)}, bf16[192,256]{1,0:T(8,128)(2,1)S(1)}, u32[]{:S(2)}, u32[]{:S(2)}) %collective-permute-start.15) | collective-permute-done | bytes 98336 | tf_op jit(solution)/shard_map/return/ppermute | solution.py:374
  56.8 0.0 collective-permute-done.16.refs_3_
  56.8 0.8 %finish.2 = bf16[192,256]{1,0:T(8,128)(2,1)} custom-call(bf16[192,256]{1,0:T(8,128)(2,1)S(1)} %get-tuple-element.40.refs_0_, bf16[192,256]{1,0:T(8,128)(2,1)S(1)} %collective-permute-done.14.refs_1_, bf16[192,256]{1,0:T(8,128)(2,1)S(1)} %collective-permute-done.15.refs_2_, bf16[192,256]{1,0:T(8,128)(2,1)S(1)} %collective-permute-done.16.refs_3_, ...), custom_call_target="tpu_custom_call" | custom-call | bytes 786432 | tf_op jit(solution)/shard_map/finish/pallas_call | solution.py:337
  57.6 0.0 collective-permute-done.19.refs_3_
  57.6 0.9 %finish.3 = (bf16[192,256]{1,0:T(8,128)(2,1)}, bf16[192,256]{1,0:T(8,128)(2,1)}) custom-call(bf16[2,2,192,256]{3,2,1,0:T(8,128)(2,1)S(1)} %get-tuple-element.45.refs_0_, bf16[2,2,192,256]{3,2,1,0:T(8,128)(2,1)S(1)} %collective-permute-done.17.refs_1_, bf16[2,2,192,256]{3,2,1,0:T(8,128)(2,1)S(1)} %collective-permute-done.18.refs_2_, ...), custom_call_target="tpu_custom_call" | custom-call | bytes 1867776 | tf_op jit(solution)/shard_map/finish/pallas_call | solution.py:337
Async XLA Ops:
  1.9 10.3 %collective-permute-start.3 = (bf16[2,192,256]{2,1,0:T(8,128)(2,1)S(1)}, bf16[2,192,256]{2,1,0:T(8,128)(2,1)S(1)}, u32[]{:S(2)}, u32[]{:S(2)}) collective-permute-start(bf16[2,192,256]{2,1,0:T(8,128)(2,1)S(1)} %get-tuple-element.28.refs_2_.refs_4_), channel_id=1, source_target_pairs={{0,4},{4,0},{1,5},{5,1},{2,6},{6,2},{3,7},{7,3},{8,12},{12,8},{9,1... | collective-permute-start | bytes 589832 | tf_op jit(solution)/shard_map/halo/ppermute | solution.py:379
  4.0 10.9 %collective-permute-start.1 = (bf16[2,192,256]{2,1,0:T(8,128)(2,1)S(1)}, bf16[2,192,256]{2,1,0:T(8,128)(2,1)S(1)}, u32[]{:S(2)}, u32[]{:S(2)}) collective-permute-start(bf16[2,192,256]{2,1,0:T(8,128)(2,1)S(1)} %get-tuple-element.27.refs_0_), channel_id=1, source_target_pairs={{0,16},{8,24},{16,0},{24,8},{1,17},{9,25},{17,1},{25,9},{2,18},{10... | collective-permute-start | bytes 589832 | tf_op jit(solution)/shard_map/halo/ppermute | solution.py:374
  6.3 10.2 %collective-permute-start = (bf16[2,192,256]{2,1,0:T(8,128)(2,1)S(1)}, bf16[2,192,256]{2,1,0:T(8,128)(2,1)S(1)}, u32[]{:S(2)}, u32[]{:S(2)}) collective-permute-start(bf16[2,192,256]{2,1,0:T(8,128)(2,1)S(1)} %get-tuple-element.27.refs_0_), channel_id=1, source_target_pairs={{0,8},{8,0},{16,24},{24,16},{1,9},{9,1},{17,25},{25,17},{2,10},{10... | collective-permute-start | bytes 589832 | tf_op jit(solution)/shard_map/halo/ppermute | solution.py:374
  7.6 9.2 %collective-permute-start.6 = (bf16[2,192,256]{2,1,0:T(8,128)(2,1)S(1)}, bf16[2,192,256]{2,1,0:T(8,128)(2,1)S(1)}, u32[]{:S(2)}, u32[]{:S(2)}) collective-permute-start(bf16[2,192,256]{2,1,0:T(8,128)(2,1)S(1)} %get-tuple-element.28.refs_2_.refs_4_), channel_id=1, source_target_pairs={{0,0},{1,2},{2,1},{3,3},{4,4},{5,6},{6,5},{7,7},{8,8},{9,10},{10,9... | collective-permute-start | bytes 589832 | tf_op jit(solution)/shard_map/halo/ppermute | solution.py:384
  12.2 4.7 %collective-permute-start.4 = (bf16[2,192,256]{2,1,0:T(8,128)(2,1)S(1)}, bf16[2,192,256]{2,1,0:T(8,128)(2,1)S(1)}, u32[]{:S(2)}, u32[]{:S(2)}) collective-permute-start(bf16[2,192,256]{2,1,0:T(8,128)(2,1)S(1)} %get-tuple-element.28.refs_2_.refs_4_), channel_id=1, source_target_pairs={{0,1},{1,0},{2,3},{3,2},{4,5},{5,4},{6,7},{7,6},{8,9},{9,8},{10,11... | collective-permute-start | bytes 589832 | tf_op jit(solution)/shard_map/halo/ppermute | solution.py:384
  12.2 7.0 %collective-permute-start.7 = (bf16[2,192,256]{2,1,0:T(8,128)(2,1)S(1)}, bf16[2,192,256]{2,1,0:T(8,128)(2,1)S(1)}, u32[]{:S(2)}, u32[]{:S(2)}) collective-permute-start(bf16[2,192,256]{2,1,0:T(8,128)(2,1)S(1)} %collective-permute-done.3.refs_5_), channel_id=1, source_target_pairs={{0,0},{1,2},{2,1},{3,3},{4,4},{5,6},{6,5},{7,7},{8,8},{9,10},{10,9... | collective-permute-start | bytes 589832 | tf_op jit(solution)/shard_map/halo/ppermute | solution.py:384
  14.9 4.4 %collective-permute-start.5 = (bf16[2,192,256]{2,1,0:T(8,128)(2,1)S(1)}, bf16[2,192,256]{2,1,0:T(8,128)(2,1)S(1)}, u32[]{:S(2)}, u32[]{:S(2)}) collective-permute-start(bf16[2,192,256]{2,1,0:T(8,128)(2,1)S(1)} %collective-permute-done.3.refs_5_), channel_id=1, source_target_pairs={{0,1},{1,0},{2,3},{3,2},{4,5},{5,4},{6,7},{7,6},{8,9},{9,8},{10,11... | collective-permute-start | bytes 589832 | tf_op jit(solution)/shard_map/halo/ppermute | solution.py:384
  16.5 6.3 %collective-permute-start.2 = (bf16[2,192,256]{2,1,0:T(8,128)(2,1)S(1)}, bf16[2,192,256]{2,1,0:T(8,128)(2,1)S(1)}, u32[]{:S(2)}, u32[]{:S(2)}) collective-permute-start(bf16[2,192,256]{2,1,0:T(8,128)(2,1)S(1)} %collective-permute-done.1.refs_0_.refs_2_), channel_id=1, source_target_pairs={{0,8},{8,0},{16,24},{24,16},{1,9},{9,1},{17,25},{25,17},{2,10},{10... | collective-permute-start | bytes 589832 | tf_op jit(solution)/shard_map/halo/ppermute | solution.py:374
  24.8 7.2 %collective-permute-start.10 = (f32[2,8,384]{2,1,0:T(8,128)S(1)}, f32[2,8,384]{2,1,0:T(8,128)S(1)}, u32[]{:S(2)}, u32[]{:S(2)}) collective-permute-start(f32[2,8,384]{2,1,0:T(8,128)S(1)} %get-tuple-element.30.refs_8_), channel_id=1, source_target_pairs={{0,24},{8,16},{16,8},{24,0},{1,25},{9,17},{17,9},{25,1},{2,26},{10... | collective-permute-start | bytes 73736 | tf_op jit(solution)/shard_map/merge/ppermute | solution.py:374
  28.2 4.5 %collective-permute-start.9 = (f32[2,8,384]{2,1,0:T(8,128)S(1)}, f32[2,8,384]{2,1,0:T(8,128)S(1)}, u32[]{:S(2)}, u32[]{:S(2)}) collective-permute-start(f32[2,8,384]{2,1,0:T(8,128)S(1)} %get-tuple-element.30.refs_8_), channel_id=1, source_target_pairs={{0,16},{8,24},{16,0},{24,8},{1,17},{9,25},{17,1},{25,9},{2,18},{10... | collective-permute-start | bytes 73736 | tf_op jit(solution)/shard_map/merge/ppermute | solution.py:374
  28.2 4.5 %collective-permute-start.8 = (f32[2,8,384]{2,1,0:T(8,128)S(1)}, f32[2,8,384]{2,1,0:T(8,128)S(1)}, u32[]{:S(2)}, u32[]{:S(2)}) collective-permute-start(f32[2,8,384]{2,1,0:T(8,128)S(1)} %get-tuple-element.30.refs_8_), channel_id=1, source_target_pairs={{0,8},{8,0},{16,24},{24,16},{1,9},{9,1},{17,25},{25,17},{2,10},{10... | collective-permute-start | bytes 73736 | tf_op jit(solution)/shard_map/merge/ppermute | solution.py:374
  28.5 12.6 %collective-permute-start.11 = (bf16[192,256]{1,0:T(8,128)(2,1)S(1)}, bf16[192,256]{1,0:T(8,128)(2,1)S(1)}, u32[]{:S(2)}, u32[]{:S(2)}) collective-permute-start(bf16[192,256]{1,0:T(8,128)(2,1)S(1)} %get-tuple-element.36), channel_id=1, source_target_pairs={{0,8},{8,0},{16,24},{24,16},{1,9},{9,1},{17,25},{25,17},{2,10},{10... | collective-permute-start | bytes 294920 | tf_op jit(solution)/shard_map/merge/ppermute | solution.py:374
  29.6 11.5 %collective-permute-start.12 = (bf16[192,256]{1,0:T(8,128)(2,1)S(1)}, bf16[192,256]{1,0:T(8,128)(2,1)S(1)}, u32[]{:S(2)}, u32[]{:S(2)}) collective-permute-start(bf16[192,256]{1,0:T(8,128)(2,1)S(1)} %get-tuple-element.37), channel_id=1, source_target_pairs={{0,16},{8,24},{16,0},{24,8},{1,17},{9,25},{17,1},{25,9},{2,18},{10... | collective-permute-start | bytes 294920 | tf_op jit(solution)/shard_map/merge/ppermute | solution.py:374
  32.0 9.2 %collective-permute-start.13 = (bf16[192,256]{1,0:T(8,128)(2,1)S(1)}, bf16[192,256]{1,0:T(8,128)(2,1)S(1)}, u32[]{:S(2)}, u32[]{:S(2)}) collective-permute-start(bf16[192,256]{1,0:T(8,128)(2,1)S(1)} %get-tuple-element.38), channel_id=1, source_target_pairs={{0,24},{8,16},{16,8},{24,0},{1,25},{9,17},{17,9},{25,1},{2,26},{10... | collective-permute-start | bytes 294920 | tf_op jit(solution)/shard_map/merge/ppermute | solution.py:374
  35.8 7.5 %collective-permute-start.17 = (bf16[2,2,192,256]{3,2,1,0:T(8,128)(2,1)S(1)}, bf16[2,2,192,256]{3,2,1,0:T(8,128)(2,1)S(1)}, u32[]{:S(2)}, u32[]{:S(2)}) collective-permute-start(bf16[2,2,192,256]{3,2,1,0:T(8,128)(2,1)S(1)} %get-tuple-element.46), channel_id=1, source_target_pairs={{0,1},{1,0},{2,3},{3,2},{4,5},{5,4},{6,7},{7,6},{8,9},{9,8},{10,11... | collective-permute-start | bytes 1179656 | tf_op jit(solution)/shard_map/gradients/ppermute | solution.py:442
  38.1 9.4 %collective-permute-start.18 = (bf16[2,2,192,256]{3,2,1,0:T(8,128)(2,1)S(1)}, bf16[2,2,192,256]{3,2,1,0:T(8,128)(2,1)S(1)}, u32[]{:S(2)}, u32[]{:S(2)}) collective-permute-start(bf16[2,2,192,256]{3,2,1,0:T(8,128)(2,1)S(1)} %get-tuple-element.47), channel_id=1, source_target_pairs={{0,0},{1,2},{2,1},{3,3},{4,4},{5,6},{6,5},{7,7},{8,8},{9,10},{10,9... | collective-permute-start | bytes 1179656 | tf_op jit(solution)/shard_map/gradients/ppermute | solution.py:442
  47.6 10.1 %collective-permute-start.19 = (bf16[2,192,256]{2,1,0:T(8,128)(2,1)S(1)}, bf16[2,192,256]{2,1,0:T(8,128)(2,1)S(1)}, u32[]{:S(2)}, u32[]{:S(2)}) collective-permute-start(bf16[2,192,256]{2,1,0:T(8,128)(2,1)S(1)} %fusion), channel_id=1, source_target_pairs={{0,4},{4,0},{1,5},{5,1},{2,6},{6,2},{3,7},{7,3},{8,12},{12,8},{9,1... | collective-permute-start | bytes 589832 | tf_op jit(solution)/shard_map/return/ppermute | solution.py:452
  47.9 5.8 %collective-permute-start.14 = (bf16[192,256]{1,0:T(8,128)(2,1)S(1)}, bf16[192,256]{1,0:T(8,128)(2,1)S(1)}, u32[]{:S(2)}, u32[]{:S(2)}) collective-permute-start(bf16[192,256]{1,0:T(8,128)(2,1)S(1)} %get-tuple-element.41), channel_id=1, source_target_pairs={{0,8},{8,0},{16,24},{24,16},{1,9},{9,1},{17,25},{25,17},{2,10},{10... | collective-permute-start | bytes 294920 | tf_op jit(solution)/shard_map/return/ppermute | solution.py:374
  47.9 8.9 %collective-permute-start.15 = (bf16[192,256]{1,0:T(8,128)(2,1)S(1)}, bf16[192,256]{1,0:T(8,128)(2,1)S(1)}, u32[]{:S(2)}, u32[]{:S(2)}) collective-permute-start(bf16[192,256]{1,0:T(8,128)(2,1)S(1)} %get-tuple-element.42), channel_id=1, source_target_pairs={{0,16},{8,24},{16,0},{24,8},{1,17},{9,25},{17,1},{25,9},{2,18},{10... | collective-permute-start | bytes 294920 | tf_op jit(solution)/shard_map/return/ppermute | solution.py:374
  51.0 5.8 %collective-permute-start.16 = (bf16[192,256]{1,0:T(8,128)(2,1)S(1)}, bf16[192,256]{1,0:T(8,128)(2,1)S(1)}, u32[]{:S(2)}, u32[]{:S(2)}) collective-permute-start(bf16[192,256]{1,0:T(8,128)(2,1)S(1)} %get-tuple-element.43), channel_id=1, source_target_pairs={{0,24},{8,16},{16,8},{24,0},{1,25},{9,17},{17,9},{25,1},{2,26},{10... | collective-permute-start | bytes 294920 | tf_op jit(solution)/shard_map/return/ppermute | solution.py:374

commit v4 on v3

--- a/solution.py
+++ b/solution.py
@@ -145,15 +145,15 @@
     return None if valid is None else jnp.where(valid, 0.0, NEGATIVE).astype(F32)
 
 
-def forward_kernel(groups, sizes, cells, with_first, *refs):
+def frame_block(ref, distance):
+    return ref.at[lax.axis_index("ta") ^ distance]
+
+
+def forward_kernel(groups, sizes, cells, qg_ref, *refs):
     tile_count = sum(len(members) for _, members in groups)
-    qa_ref, qb_ref = refs[0], refs[1]
-    kv_refs = refs[2 : 2 + tile_count]
-    rest = refs[2 + tile_count :]
-    if with_first:
-        first_ref, oa_ref, ob_ref, stat_ref, key_buf, value_buf = rest
-    else:
-        oa_ref, ob_ref, stat_ref, key_buf, value_buf = rest
+    kv_refs = refs[:tile_count]
+    o_refs = refs[tile_count : tile_count + 4]
+    stat_ref, key_buf, value_buf = refs[tile_count + 4 :]
     at = 0
     spans = []
     for flags, members in groups:
@@ -164,48 +164,45 @@
             at += cells
         spans.append((begin, at, group_bias(flags, sizes)))
     lane = lax.broadcasted_iota(jnp.int32, (2 * cells, DH), 1)
-    stat = jnp.zeros((2 * cells, DH), F32)
-    for head in range(HEADS):
-        cut = head_slice(head)
-        query = jnp.concatenate([qa_ref[0, :, cut], qb_ref[0, :, cut]], axis=0)
-        grad = jnp.concatenate([qa_ref[1, :, cut], qb_ref[1, :, cut]], axis=0)
-        scores = [dot_nt(query, key_buf[lo:hi, cut]) for lo, hi, _ in spans]
-        best = None
-        for raw, (_, _, bias) in zip(scores, spans):
-            top = jnp.max(raw, axis=1, keepdims=True) * SCALE_LOG2
-            if bias is not None:
-                top = top + bias
-            best = top if best is None else jnp.maximum(best, top)
-        total = None
-        out = None
-        for raw, (lo, hi, bias) in zip(scores, spans):
-            shift = best if bias is None else best - bias
-            weights = jnp.exp2(raw * SCALE_LOG2 - shift)
-            part = jnp.sum(weights, axis=1, keepdims=True)
-            piece = dot_nn(weights.astype(BF16), value_buf[lo:hi, cut])
-            total = part if total is None else total + part
-            out = piece if out is None else out + piece
-        out = out * (1.0 / total)
-        dotted = jnp.sum(out * grad.astype(F32), axis=1, keepdims=True)
-        out = out.astype(BF16)
-        oa_ref[:, cut] = out[:cells]
-        ob_ref[:, cut] = out[cells:]
-        stat = jnp.where(lane == head, best + jnp.log2(total), stat)
-        stat = jnp.where(lane == HEADS + head, dotted, stat)
-    flipped = stat.T[: stat_ref.shape[-2]]
-    if with_first:
-        stat_ref[0] = first_ref[...]
-        stat_ref[1] = flipped
-    else:
-        stat_ref[...] = flipped
-
-
-def merged_stats(own_ref, s1_ref, s2_ref, s3_ref, half, cells):
+    for half in range(2):
+        blocks = [frame_block(qg_ref, 2 * half + i) for i in range(2)]
+        stat = jnp.zeros((2 * cells, DH), F32)
+        for head in range(HEADS):
+            cut = head_slice(head)
+            query = jnp.concatenate([block[0, :, cut] for block in blocks], axis=0)
+            grad = jnp.concatenate([block[1, :, cut] for block in blocks], axis=0)
+            scores = [dot_nt(query, key_buf[lo:hi, cut]) for lo, hi, _ in spans]
+            best = None
+            for raw, (_, _, bias) in zip(scores, spans):
+                top = jnp.max(raw, axis=1, keepdims=True) * SCALE_LOG2
+                if bias is not None:
+                    top = top + bias
+                best = top if best is None else jnp.maximum(best, top)
+            total = None
+            out = None
+            for raw, (lo, hi, bias) in zip(scores, spans):
+                shift = best if bias is None else best - bias
+                weights = jnp.exp2(raw * SCALE_LOG2 - shift)
+                part = jnp.sum(weights, axis=1, keepdims=True)
+                piece = dot_nn(weights.astype(BF16), value_buf[lo:hi, cut])
+                total = part if total is None else total + part
+                out = piece if out is None else out + piece
+            out = out * (1.0 / total)
+            dotted = jnp.sum(out * grad.astype(F32), axis=1, keepdims=True)
+            out = out.astype(BF16)
+            o_refs[2 * half][:, cut] = out[:cells]
+            o_refs[2 * half + 1][:, cut] = out[cells:]
+            stat = jnp.where(lane == head, best + jnp.log2(total), stat)
+            stat = jnp.where(lane == HEADS + head, dotted, stat)
+        stat_ref[half] = stat.T[: stat_ref.shape[1]]
+
+
+def merged_stats(stat_ref, half, cells):
     parts = [
-        own_ref[half],
-        pltpu.roll(s1_ref[half], cells, 1),
-        s2_ref[1 - half],
-        pltpu.roll(s3_ref[1 - half], cells, 1),
+        frame_block(stat_ref, 0)[half],
+        pltpu.roll(frame_block(stat_ref, 1)[half], cells, 1),
+        frame_block(stat_ref, 2)[1 - half],
+        pltpu.roll(frame_block(stat_ref, 3)[1 - half], cells, 1),
     ]
     top = functools.reduce(jnp.maximum, parts)
     shares = [jnp.exp2(part - top) for part in parts]
@@ -244,11 +241,10 @@
     return results, dq
 
 
-def backward_kernel(cols, grid_rows, sizes, cells, last, *refs):
+def backward_kernel(cols, grid_rows, sizes, cells, last, qg_ref, *refs):
     tile_count = grid_rows * len(cols)
-    qg_refs = refs[:4]
-    kv_refs = refs[4 : 4 + tile_count]
-    rest = refs[4 + tile_count :]
+    kv_refs = refs[:tile_count]
+    rest = refs[tile_count:]
     if last:
         lse_ref, delta_ref, share_ref, dq_ref = rest[:4]
         o_refs = rest[4:8]
@@ -265,11 +261,10 @@
                 out = piece if out is None else out + piece
             out_ref[:, cut] = out.astype(BF16)
     else:
-        stat_refs = rest[:4]
-        lse_ref, delta_ref, share_ref, dq_ref = rest[4:8]
-        col_refs = rest[8 : 8 + len(cols)]
-        key_buf, value_buf = rest[8 + len(cols) :]
-        stats = [merged_stats(*stat_refs, half, cells) for half in range(2)]
+        stat_ref, lse_ref, delta_ref, share_ref, dq_ref = rest[:5]
+        col_refs = rest[5 : 5 + len(cols)]
+        key_buf, value_buf = rest[5 + len(cols) :]
+        stats = [merged_stats(stat_ref, half, cells) for half in range(2)]
         lse = jnp.concatenate([stats[0][0], stats[1][0]], axis=1)
         delta = jnp.concatenate([stats[0][1], stats[1][1]], axis=1)
         lse_ref[...] = lse
@@ -286,8 +281,9 @@
     row_flags = [row == 2 for row in range(grid_rows)]
     for head in range(HEADS):
         cut = head_slice(head)
-        queries = jnp.concatenate([ref[0, :, cut] for ref in qg_refs], axis=0)
-        grads = jnp.concatenate([ref[1, :, cut] for ref in qg_refs], axis=0)
+        blocks = [frame_block(qg_ref, d) for d in range(4)]
+        queries = jnp.concatenate([block[0, :, cut] for block in blocks], axis=0)
+        grads = jnp.concatenate([block[1, :, cut] for block in blocks], axis=0)
         results, dq = gradient_blocks(
             cols, row_flags, sizes, key_buf.at[:, cut], value_buf.at[:, cut], queries, grads,
             lse[head : head + 1], delta[head : head + 1], span,
@@ -377,12 +373,10 @@
     col_sides = side_pairs(sizes["wa"])
     with jax.named_scope("halo"):
         kv_rows = [kv] + [lax.ppermute(kv, "ha", pairs) for pairs in row_sides]
-        qg2 = other_frames(qg, 2)
-        qg1 = other_frames(qg, 1)
+        gathered = lax.all_gather(qg, "ta")
         tiles = []
         for block in kv_rows:
             tiles.append([block] + [lax.ppermute(block, "wa", pairs) for pairs in col_sides])
-        qg3 = other_frames(qg2, 1)
     grid_rows, grid_cols = 1 + len(row_sides), 1 + len(col_sides)
     flat_tiles = [tiles[row][col] for row in range(grid_rows) for col in range(grid_cols)]
     groups = {}
@@ -392,28 +386,21 @@
     groups = list(groups.items())
 
     key_count = len(flat_tiles) * cells
-    product = 2 * 2 * cells * key_count * DH * HEADS
-
-    def forward(qa, qb, first):
-        args = (qa, qb, *flat_tiles) + (() if first is None else (first,))
-        stat = (8, 2 * cells) if first is None else (2, 8, 2 * cells)
-        return call(
-            functools.partial(forward_kernel, groups, sizes, cells, first is not None),
-            (plain, plain, real(*stat)),
-            args,
+    product = 2 * 4 * cells * key_count * DH * HEADS
+
+    with jax.named_scope("attend"):
+        *parts, stat = call(
+            functools.partial(forward_kernel, groups, sizes, cells),
+            (*[plain] * 4, real(2, 8, 2 * cells)),
+            (gathered, *flat_tiles),
             2 * product,
-            2 * cells * key_count * HEADS,
+            4 * cells * key_count * HEADS,
             [pltpu.VMEM((key_count, chan), BF16)] * 2,
         )
-
-    with jax.named_scope("attend"):
-        o0, o1, first = forward(qg, qg1, None)
-        o2, o3, stat = forward(qg2, qg3, first)
     with jax.named_scope("merge"):
-        stats = [stat] + [other_frames(stat, d) for d in (1, 2, 3)]
-        outs = [o0] + [other_frames(o, d) for d, o in ((1, o1), (2, o2), (3, o3))]
-
-    queries = (qg, qg1, qg2, qg3)
+        stats = lax.all_gather(stat, "ta")
+        outs = [parts[0]] + [other_frames(parts[d], d) for d in (1, 2, 3)]
+
     col_shape = jax.ShapeDtypeStruct((grid_rows, 2, cells, chan), BF16)
 
     def gradients(which, last, extra_out, extra_in):
@@ -421,8 +408,8 @@
         return call(
             functools.partial(backward_kernel, which, grid_rows, sizes, cells, last),
             (*extra_out, *[col_shape] * count),
-            (*queries, *[tiles[row][col] for col in which for row in range(grid_rows)], *extra_in),
-            10 * product * count // grid_cols,
+            (gathered, *[tiles[row][col] for col in which for row in range(grid_rows)], *extra_in),
+            5 * product * count // grid_cols,
             4 * cells * key_count * HEADS * count // grid_cols,
             [pltpu.VMEM((count * grid_rows * cells, chan), BF16)] * 2,
         )
@@ -437,7 +424,7 @@
                 real(cells, DH),
                 real(HEADS, DH, 4 * cells),
             ),
-            stats,
+            (stats,),
         )
         sides = [lax.ppermute(x, "wa", pairs) for x, pairs in zip(sides, col_sides)]
         d0, d1, d2, d3, attended, own = gradients(
@@ -452,7 +439,7 @@
             row_parts.append(lax.ppermute(partial_sum, "ha", pairs))
 
     with jax.named_scope("finish"):
-        grad_query = call(finish_query_kernel, plain, (*dqs, rope))
+        grad_query = call(finish_query_kernel, plain, (*dqs, rope), 5 * product)
         grad_key, grad_value = call(
             functools.partial(finish_key_kernel, grid_cols, len(row_parts)),
             (plain, plain),

time: 58.7 us -> 74.8 us (1.27)
  blocking collectives: 0 us -> 27.4 us
  waiting for transfers between devices: 14.4 us -> 5.69 us
  starting transfers between devices: 31.3 us -> 28.3 us
    all_gather x0 -> x2, blocking collectives: none -> 27.4 us  [the longest x1 17 us: shards(): gathered = lax.all_gather(qg, 'ta')]
    ppermute x12 -> x6, starting transfers between devices: 15.3 us -> 7.09 us  [other_frames(): lax.ppermute(x, 'ta', [(i, i ^ distance) for i in range(sizes['ta'])])]
    ppermute x12 -> x6, waiting for transfers between devices: 7.73 us -> 3.14 us  [other_frames(): lax.ppermute(x, 'ta', [(i, i ^ distance) for i in range(sizes['ta'])])]
    ppermute x2, starting transfers between devices: 5.38 us -> 9.18 us  [shards(): sides = [lax.ppermute(x, 'wa', pairs) for x, pairs in zip(sides, col_sides)]]
    ppermute x2, waiting for transfers between devices: 4.24 us -> 1.61 us  [shards(): sides = [lax.ppermute(x, 'wa', pairs) for x, pairs in zip(sides, col_sides)]]
    ppermute x4, waiting for transfers between devices: 2.4 us -> 0.01 us  [shards(): lax.ppermute(block, 'wa', pairs)]
    ppermute x1, starting transfers between devices: 0.33 us -> 1.27 us  [shards(): row_parts.append(lax.ppermute(partial_sum, 'ha', pairs))]
    pallas_call x7 -> x6, Pallas kernels: 12 us -> 11.7 us  [call(): pl.pallas_call(kernel, out_shape=out_shape, in_specs=[pl.BlockSpec(memory...]
  transfers between devices with their start and end apart: 20 -> 14, of which waited for: 6 -> 4; matrix products, arithmetic and copies ran while one was open for 0% -> 0% of each run, Pallas kernels for 14% -> 8%
where the time goes in v4:
time: 74.8 us; the launch traced here: 74 us
  starting transfers between devices  28.3 us (38%)
  blocking collectives  27.4 us (37%)
  Pallas kernels  11.7 us (16%)
  waiting for transfers between devices  5.69 us (8%)
    all_gather x1, blocking collectives, shards(): gathered = lax.all_gather(qg, 'ta')  17 us
    pallas_call x6, Pallas kernels, call(): pl.pallas_call(kernel, out_shape=out_shape, in_specs=[pl.BlockSpec(memory...  11.7 us
    all_gather x1, blocking collectives, shards(): stats = lax.all_gather(stat, 'ta')  10.4 us
    ppermute x2, starting transfers between devices, shards(): sides = [lax.ppermute(x, 'wa', pairs) for x, pairs in zip(sides, col_sides)]  9.18 us
    ppermute x4, starting transfers between devices, shards(): lax.ppermute(block, 'wa', pairs)  8.62 us
    ppermute x6, starting transfers between devices, other_frames(): lax.ppermute(x, 'ta', [(i, i ^ distance) for i in range(sizes['ta'])])  7.09 us
    ppermute x6, waiting for transfers between devices, other_frames(): lax.ppermute(x, 'ta', [(i, i ^ distance) for i in range(sizes['ta'])])  3.14 us
    ppermute x1, starting transfers between devices, shards(): kv_rows = [kv] + [lax.ppermute(kv, 'ha', pairs) for pairs in row_sides]  2.11 us
  transfers between devices with their start and end apart: 14, of which 4 were waited for; matrix products, arithmetic and copies ran while one was open for 0% of the time, Pallas kernels for 8%

profile of v4, /device:TPU:1, one launch (start us, length us, event | category | flops | bytes accessed | tf_op | source)
XLA Modules:
  0.0 74.0 jit_solution(9238918845140001114)
XLA Ops:
  0.6 1.3 %rotate.1 = (bf16[2,192,256]{2,1,0:T(8,128)(2,1)S(1)}, bf16[2,192,256]{2,1,0:T(8,128)(2,1)S(1)}, f32[3,192,128]{2,1,0:T(8,128)S(1)}) custom-call(bf16[192,256]{1,0:T(8,128)(2,1)} %bitcast.16, bf16[192,256]{1,0:T(8,128)(2,1)} %bitcast.17, bf16[192,256]{1,0:T(8,128)(2,1)} %bitcast.18, bf16[192,256]{1,0:T(8,128)(2,1)} %bitcast.19, ...), custom_call_target="tpu_custom_call" | custom-call | bytes 1179648 | tf_op jit(solution)/shard_map/rotate/pallas_call | solution.py:333
  1.9 2.1 %collective-permute-start = (bf16[2,192,256]{2,1,0:T(8,128)(2,1)S(1)}, bf16[2,192,256]{2,1,0:T(8,128)(2,1)S(1)}, u32[]{:S(2)}, u32[]{:S(2)}) collective-permute-start(bf16[2,192,256]{2,1,0:T(8,128)(2,1)S(1)} %get-tuple-element.27.refs_0_), channel_id=1, source_target_pairs={{0,4},{4,0},{1,5},{5,1},{2,6},{6,2},{3,7},{7,3},{8,12},{12,8},{9,1... | collective-permute-start | bytes 589832 | tf_op jit(solution)/shard_map/halo/ppermute | solution.py:375
  4.0 4.0 %collective-permute-start.3 = (bf16[2,192,256]{2,1,0:T(8,128)(2,1)S(1)}, bf16[2,192,256]{2,1,0:T(8,128)(2,1)S(1)}, u32[]{:S(2)}, u32[]{:S(2)}) collective-permute-start(bf16[2,192,256]{2,1,0:T(8,128)(2,1)S(1)} %get-tuple-element.27.refs_0_), channel_id=1, source_target_pairs={{0,0},{1,2},{2,1},{3,3},{4,4},{5,6},{6,5},{7,7},{8,8},{9,10},{10,9... | collective-permute-start | bytes 589832 | tf_op jit(solution)/shard_map/halo/ppermute | solution.py:379
  8.0 0.1 collective-permute-start.1
  8.1 0.6 collective-permute-done.refs_3_.refs_1_
  8.6 4.5 %collective-permute-start.4 = (bf16[2,192,256]{2,1,0:T(8,128)(2,1)S(1)}, bf16[2,192,256]{2,1,0:T(8,128)(2,1)S(1)}, u32[]{:S(2)}, u32[]{:S(2)}) collective-permute-start(bf16[2,192,256]{2,1,0:T(8,128)(2,1)S(1)} %collective-permute-done.refs_3_.refs_1_), channel_id=1, source_target_pairs={{0,0},{1,2},{2,1},{3,3},{4,4},{5,6},{6,5},{7,7},{8,8},{9,10},{10,9... | collective-permute-start | bytes 589832 | tf_op jit(solution)/shard_map/halo/ppermute | solution.py:379
  13.1 0.1 collective-permute-start.2
  13.2 17.0 %all-gather = bf16[8,192,256]{2,1,0:T(8,128)(2,1)S(1)} all-gather(bf16[2,192,256]{2,1,0:T(8,128)(2,1)S(1)} %get-tuple-element.26), channel_id=2, replica_groups=mesh['ta'=4,'ha'=2,'wa'=4] {'ta'}, dimensions={0}, use_global_device_ids=true | all-gather | bytes 983040 | tf_op jit(solution)/shard_map/halo/all_gather | solution.py:376
  30.2 0.0 collective-permute-done.3.refs_2_
  30.2 0.0 collective-permute-done.1.refs_1_.refs_0_
  30.2 0.0 collective-permute-done.4.refs_5_.refs_3_
  30.3 0.0 collective-permute-done.2.refs_4_.refs_1_
  30.3 3.4 %attend.1 = (bf16[192,256]{1,0:T(8,128)(2,1)S(1)}, bf16[192,256]{1,0:T(8,128)(2,1)S(1)}, bf16[192,256]{1,0:T(8,128)(2,1)S(1)}, bf16[192,256]{1,0:T(8,128)(2,1)S(1)}, f32[2,8,384]{2,1,0:T(8,128)S(1)}) custom-call(bf16[4,2,192,256]{3,2,1,0:T(8,128)(2,1)S(1)} %bitcast.12, bf16[2,192,256]{2,1,0:T(8,128)(2,1)S(1)} %get-tuple-element.27.refs_0_, ...), custom_call_target="tpu_custom_call" | custom-call | flops 7247757312 | bytes 2383872 | tf_op jit(solution)/shard_map/attend/pallas_call | solution.py:333
  33.7 10.4 %all-gather.1 = f32[8,8,384]{2,1,0:T(8,128)S(1)} all-gather(f32[2,8,384]{2,1,0:T(8,128)S(1)} %get-tuple-element.28), channel_id=3, replica_groups=mesh['ta'=4,'ha'=2,'wa'=4] {'ta'}, dimensions={0}, use_global_device_ids=true | all-gather | bytes 122880 | tf_op jit(solution)/shard_map/merge/all_gather | solution.py:401
  44.1 1.4 %collective-permute-start.5 = (bf16[192,256]{1,0:T(8,128)(2,1)S(1)}, bf16[192,256]{1,0:T(8,128)(2,1)S(1)}, u32[]{:S(2)}, u32[]{:S(2)}) collective-permute-start(bf16[192,256]{1,0:T(8,128)(2,1)S(1)} %get-tuple-element.34), channel_id=1, source_target_pairs={{0,8},{8,0},{16,24},{24,16},{1,9},{9,1},{17,25},{25,17},{2,10},{10... | collective-permute-start | bytes 294920 | tf_op jit(solution)/shard_map/merge/ppermute | solution.py:370
  45.5 2.1 %collective-permute-start.6 = (bf16[192,256]{1,0:T(8,128)(2,1)S(1)}, bf16[192,256]{1,0:T(8,128)(2,1)S(1)}, u32[]{:S(2)}, u32[]{:S(2)}) collective-permute-start(bf16[192,256]{1,0:T(8,128)(2,1)S(1)} %get-tuple-element.35), channel_id=1, source_target_pairs={{0,16},{8,24},{16,0},{24,8},{1,17},{9,25},{17,1},{25,9},{2,18},{10... | collective-permute-start | bytes 294920 | tf_op jit(solution)/shard_map/merge/ppermute | solution.py:370
  47.6 0.0 collective-permute-start.7
  47.7 3.1 %gradients.2 = (f32[2,768]{1,0:T(2,128)S(1)}, f32[2,768]{1,0:T(2,128)S(1)}, f32[192,128]{1,0:T(8,128)S(1)}, f32[2,128,768]{2,1,0:T(8,128)S(1)}, bf16[2,2,192,256...) custom-call(bf16[4,2,192,256]{3,2,1,0:T(8,128)(2,1)S(1)} %bitcast.13, ...), custom_call_target="tpu_custom_call" | custom-call | flops 12079595520 | bytes 3354624 | tf_op jit(solution)/shard_map/gradients/pallas_call | solution.py:333
  50.8 7.3 %collective-permute-start.11 = (bf16[2,2,192,256]{3,2,1,0:T(8,128)(2,1)S(1)}, bf16[2,2,192,256]{3,2,1,0:T(8,128)(2,1)S(1)}, u32[]{:S(2)}, u32[]{:S(2)}) collective-permute-start(bf16[2,2,192,256]{3,2,1,0:T(8,128)(2,1)S(1)} %get-tuple-element.44), channel_id=1, source_target_pairs={{0,1},{1,0},{2,3},{3,2},{4,5},{5,4},{6,7},{7,6},{8,9},{9,8},{10,11... | collective-permute-start | bytes 1179656 | tf_op jit(solution)/shard_map/gradients/ppermute | solution.py:429
  58.0 1.9 %collective-permute-start.12 = (bf16[2,2,192,256]{3,2,1,0:T(8,128)(2,1)S(1)}, bf16[2,2,192,256]{3,2,1,0:T(8,128)(2,1)S(1)}, u32[]{:S(2)}, u32[]{:S(2)}) collective-permute-start(bf16[2,2,192,256]{3,2,1,0:T(8,128)(2,1)S(1)} %get-tuple-element.45), channel_id=1, source_target_pairs={{0,0},{1,2},{2,1},{3,3},{4,4},{5,6},{6,5},{7,7},{8,8},{9,10},{10,9... | collective-permute-start | bytes 1179656 | tf_op jit(solution)/shard_map/gradients/ppermute | solution.py:429
  60.0 0.0 collective-permute-done.5.refs_7_
  60.0 0.0 collective-permute-done.6.refs_8_
  60.0 0.0 collective-permute-done.7.refs_9_
  60.0 2.3 %gradients.3 = (bf16[192,256]{1,0:T(8,128)(2,1)S(1)}, bf16[192,256]{1,0:T(8,128)(2,1)S(1)}, bf16[192,256]{1,0:T(8,128)(2,1)S(1)}, bf16[192,256]{1,0:T(8,128)(2,1...) custom-call(bf16[4,2,192,256]{3,2,1,0:T(8,128)(2,1)S(1)} %bitcast.14, ...), custom_call_target="tpu_custom_call" | custom-call | flops 6039797760 | bytes 3354624 | tf_op jit(solution)/shard_map/gradients/pallas_call | solution.py:333
  62.3 0.0 collective-permute-start.8
  62.3 1.6 %collective-permute-start.9 = (bf16[192,256]{1,0:T(8,128)(2,1)S(1)}, bf16[192,256]{1,0:T(8,128)(2,1)S(1)}, u32[]{:S(2)}, u32[]{:S(2)}) collective-permute-start(bf16[192,256]{1,0:T(8,128)(2,1)S(1)} %get-tuple-element.40), channel_id=1, source_target_pairs={{0,16},{8,24},{16,0},{24,8},{1,17},{9,25},{17,1},{25,9},{2,18},{10... | collective-permute-start | bytes 294920 | tf_op jit(solution)/shard_map/return/ppermute | solution.py:370
  63.9 1.9 %collective-permute-start.10 = (bf16[192,256]{1,0:T(8,128)(2,1)S(1)}, bf16[192,256]{1,0:T(8,128)(2,1)S(1)}, u32[]{:S(2)}, u32[]{:S(2)}) collective-permute-start(bf16[192,256]{1,0:T(8,128)(2,1)S(1)} %get-tuple-element.41), channel_id=1, source_target_pairs={{0,24},{8,16},{16,8},{24,0},{1,25},{9,17},{17,9},{25,1},{2,26},{10... | collective-permute-start | bytes 294920 | tf_op jit(solution)/shard_map/return/ppermute | solution.py:370
  65.8 0.0 collective-permute-done.11.refs_1_
  65.8 1.6 %collective-permute-done.12.refs_2_ = bf16[2,2,192,256]{3,2,1,0:T(8,128)(2,1)S(1)} collective-permute-done((bf16[2,2,192,256]{3,2,1,0:T(8,128)(2,1)S(1)}, bf16[2,2,192,256]{3,2,1,0:T(8,128)(2,1)S(1)}, u32[]{:S(2)}, u32[]{:S(2)}) %collective-permute-start.12) | collective-permute-done | bytes 393248 | tf_op jit(solution)/shard_map/gradients/ppermute | solution.py:429
  67.4 0.1 fusion
  67.5 1.3 %collective-permute-start.13 = (bf16[2,192,256]{2,1,0:T(8,128)(2,1)S(1)}, bf16[2,192,256]{2,1,0:T(8,128)(2,1)S(1)}, u32[]{:S(2)}, u32[]{:S(2)}) collective-permute-start(bf16[2,192,256]{2,1,0:T(8,128)(2,1)S(1)} %fusion), channel_id=1, source_target_pairs={{0,4},{4,0},{1,5},{5,1},{2,6},{6,2},{3,7},{7,3},{8,12},{12,8},{9,1... | collective-permute-start | bytes 589832 | tf_op jit(solution)/shard_map/return/ppermute | solution.py:439
  68.8 0.0 collective-permute-done.8.refs_1_
  68.8 3.1 %collective-permute-done.9.refs_2_ = bf16[192,256]{1,0:T(8,128)(2,1)S(1)} collective-permute-done((bf16[192,256]{1,0:T(8,128)(2,1)S(1)}, bf16[192,256]{1,0:T(8,128)(2,1)S(1)}, u32[]{:S(2)}, u32[]{:S(2)}) %collective-permute-start.9) | collective-permute-done | bytes 98336 | tf_op jit(solution)/shard_map/return/ppermute | solution.py:370
  71.9 0.0 collective-permute-done.10.refs_3_
  71.9 0.8 %finish.2 = bf16[192,256]{1,0:T(8,128)(2,1)} custom-call(bf16[192,256]{1,0:T(8,128)(2,1)S(1)} %get-tuple-element.38.refs_0_, bf16[192,256]{1,0:T(8,128)(2,1)S(1)} %collective-permute-done.8.refs_1_, bf16[192,256]{1,0:T(8,128)(2,1)S(1)} %collective-permute-done.9.refs_2_, bf16[192,256]{1,0:T(8,128)(2,1)S(1)} %collective-permute-done.10.refs_3_, ...), custom_call_target="tpu_custom_call" | custom-call | flops 18119393280 | bytes 786432 | tf_op jit(solution)/shard_map/finish/pallas_call | solution.py:333
  72.7 0.4 collective-permute-done.13.refs_3_
  73.1 0.9 %finish.3 = (bf16[192,256]{1,0:T(8,128)(2,1)}, bf16[192,256]{1,0:T(8,128)(2,1)}) custom-call(bf16[2,2,192,256]{3,2,1,0:T(8,128)(2,1)S(1)} %get-tuple-element.43.refs_0_, bf16[2,2,192,256]{3,2,1,0:T(8,128)(2,1)S(1)} %collective-permute-done.11.refs_1_, bf16[2,2,192,256]{3,2,1,0:T(8,128)(2,1)S(1)} %collective-permute-done.12.refs_2_, ...), custom_call_target="tpu_custom_call" | custom-call | bytes 1867776 | tf_op jit(solution)/shard_map/finish/pallas_call | solution.py:333
Async XLA Ops:
  1.9 6.7 %collective-permute-start = (bf16[2,192,256]{2,1,0:T(8,128)(2,1)S(1)}, bf16[2,192,256]{2,1,0:T(8,128)(2,1)S(1)}, u32[]{:S(2)}, u32[]{:S(2)}) collective-permute-start(bf16[2,192,256]{2,1,0:T(8,128)(2,1)S(1)} %get-tuple-element.27.refs_0_), channel_id=1, source_target_pairs={{0,4},{4,0},{1,5},{5,1},{2,6},{6,2},{3,7},{7,3},{8,12},{12,8},{9,1... | collective-permute-start | bytes 589832 | tf_op jit(solution)/shard_map/halo/ppermute | solution.py:375
  4.0 26.2 %collective-permute-start.3 = (bf16[2,192,256]{2,1,0:T(8,128)(2,1)S(1)}, bf16[2,192,256]{2,1,0:T(8,128)(2,1)S(1)}, u32[]{:S(2)}, u32[]{:S(2)}) collective-permute-start(bf16[2,192,256]{2,1,0:T(8,128)(2,1)S(1)} %get-tuple-element.27.refs_0_), channel_id=1, source_target_pairs={{0,0},{1,2},{2,1},{3,3},{4,4},{5,6},{6,5},{7,7},{8,8},{9,10},{10,9... | collective-permute-start | bytes 589832 | tf_op jit(solution)/shard_map/halo/ppermute | solution.py:379
  8.0 22.3 %collective-permute-start.1 = (bf16[2,192,256]{2,1,0:T(8,128)(2,1)S(1)}, bf16[2,192,256]{2,1,0:T(8,128)(2,1)S(1)}, u32[]{:S(2)}, u32[]{:S(2)}) collective-permute-start(bf16[2,192,256]{2,1,0:T(8,128)(2,1)S(1)} %get-tuple-element.27.refs_0_), channel_id=1, source_target_pairs={{0,1},{1,0},{2,3},{3,2},{4,5},{5,4},{6,7},{7,6},{8,9},{9,8},{10,11... | collective-permute-start | bytes 589832 | tf_op jit(solution)/shard_map/halo/ppermute | solution.py:379
  8.6 21.6 %collective-permute-start.4 = (bf16[2,192,256]{2,1,0:T(8,128)(2,1)S(1)}, bf16[2,192,256]{2,1,0:T(8,128)(2,1)S(1)}, u32[]{:S(2)}, u32[]{:S(2)}) collective-permute-start(bf16[2,192,256]{2,1,0:T(8,128)(2,1)S(1)} %collective-permute-done.refs_3_.refs_1_), channel_id=1, source_target_pairs={{0,0},{1,2},{2,1},{3,3},{4,4},{5,6},{6,5},{7,7},{8,8},{9,10},{10,9... | collective-permute-start | bytes 589832 | tf_op jit(solution)/shard_map/halo/ppermute | solution.py:379
  13.1 17.1 %collective-permute-start.2 = (bf16[2,192,256]{2,1,0:T(8,128)(2,1)S(1)}, bf16[2,192,256]{2,1,0:T(8,128)(2,1)S(1)}, u32[]{:S(2)}, u32[]{:S(2)}) collective-permute-start(bf16[2,192,256]{2,1,0:T(8,128)(2,1)S(1)} %collective-permute-done.refs_3_.refs_1_), channel_id=1, source_target_pairs={{0,1},{1,0},{2,3},{3,2},{4,5},{5,4},{6,7},{7,6},{8,9},{9,8},{10,11... | collective-permute-start | bytes 589832 | tf_op jit(solution)/shard_map/halo/ppermute | solution.py:379
  44.1 15.8 %collective-permute-start.5 = (bf16[192,256]{1,0:T(8,128)(2,1)S(1)}, bf16[192,256]{1,0:T(8,128)(2,1)S(1)}, u32[]{:S(2)}, u32[]{:S(2)}) collective-permute-start(bf16[192,256]{1,0:T(8,128)(2,1)S(1)} %get-tuple-element.34), channel_id=1, source_target_pairs={{0,8},{8,0},{16,24},{24,16},{1,9},{9,1},{17,25},{25,17},{2,10},{10... | collective-permute-start | bytes 294920 | tf_op jit(solution)/shard_map/merge/ppermute | solution.py:370
  45.5 14.5 %collective-permute-start.6 = (bf16[192,256]{1,0:T(8,128)(2,1)S(1)}, bf16[192,256]{1,0:T(8,128)(2,1)S(1)}, u32[]{:S(2)}, u32[]{:S(2)}) collective-permute-start(bf16[192,256]{1,0:T(8,128)(2,1)S(1)} %get-tuple-element.35), channel_id=1, source_target_pairs={{0,16},{8,24},{16,0},{24,8},{1,17},{9,25},{17,1},{25,9},{2,18},{10... | collective-permute-start | bytes 294920 | tf_op jit(solution)/shard_map/merge/ppermute | solution.py:370
  47.6 12.4 %collective-permute-start.7 = (bf16[192,256]{1,0:T(8,128)(2,1)S(1)}, bf16[192,256]{1,0:T(8,128)(2,1)S(1)}, u32[]{:S(2)}, u32[]{:S(2)}) collective-permute-start(bf16[192,256]{1,0:T(8,128)(2,1)S(1)} %get-tuple-element.36), channel_id=1, source_target_pairs={{0,24},{8,16},{16,8},{24,0},{1,25},{9,17},{17,9},{25,1},{2,26},{10... | collective-permute-start | bytes 294920 | tf_op jit(solution)/shard_map/merge/ppermute | solution.py:370
  50.8 15.0 %collective-permute-start.11 = (bf16[2,2,192,256]{3,2,1,0:T(8,128)(2,1)S(1)}, bf16[2,2,192,256]{3,2,1,0:T(8,128)(2,1)S(1)}, u32[]{:S(2)}, u32[]{:S(2)}) collective-permute-start(bf16[2,2,192,256]{3,2,1,0:T(8,128)(2,1)S(1)} %get-tuple-element.44), channel_id=1, source_target_pairs={{0,1},{1,0},{2,3},{3,2},{4,5},{5,4},{6,7},{7,6},{8,9},{9,8},{10,11... | collective-permute-start | bytes 1179656 | tf_op jit(solution)/shard_map/gradients/ppermute | solution.py:429
  58.0 9.4 %collective-permute-start.12 = (bf16[2,2,192,256]{3,2,1,0:T(8,128)(2,1)S(1)}, bf16[2,2,192,256]{3,2,1,0:T(8,128)(2,1)S(1)}, u32[]{:S(2)}, u32[]{:S(2)}) collective-permute-start(bf16[2,2,192,256]{3,2,1,0:T(8,128)(2,1)S(1)} %get-tuple-element.45), channel_id=1, source_target_pairs={{0,0},{1,2},{2,1},{3,3},{4,4},{5,6},{6,5},{7,7},{8,8},{9,10},{10,9... | collective-permute-start | bytes 1179656 | tf_op jit(solution)/shard_map/gradients/ppermute | solution.py:429
  62.3 6.5 %collective-permute-start.8 = (bf16[192,256]{1,0:T(8,128)(2,1)S(1)}, bf16[192,256]{1,0:T(8,128)(2,1)S(1)}, u32[]{:S(2)}, u32[]{:S(2)}) collective-permute-start(bf16[192,256]{1,0:T(8,128)(2,1)S(1)} %get-tuple-element.39), channel_id=1, source_target_pairs={{0,8},{8,0},{16,24},{24,16},{1,9},{9,1},{17,25},{25,17},{2,10},{10... | collective-permute-start | bytes 294920 | tf_op jit(solution)/shard_map/return/ppermute | solution.py:370
  62.3 9.6 %collective-permute-start.9 = (bf16[192,256]{1,0:T(8,128)(2,1)S(1)}, bf16[192,256]{1,0:T(8,128)(2,1)S(1)}, u32[]{:S(2)}, u32[]{:S(2)}) collective-permute-start(bf16[192,256]{1,0:T(8,128)(2,1)S(1)} %get-tuple-element.40), channel_id=1, source_target_pairs={{0,16},{8,24},{16,0},{24,8},{1,17},{9,25},{17,1},{25,9},{2,18},{10... | collective-permute-start | bytes 294920 | tf_op jit(solution)/shard_map/return/ppermute | solution.py:370
  63.9 8.0 %collective-permute-start.10 = (bf16[192,256]{1,0:T(8,128)(2,1)S(1)}, bf16[192,256]{1,0:T(8,128)(2,1)S(1)}, u32[]{:S(2)}, u32[]{:S(2)}) collective-permute-start(bf16[192,256]{1,0:T(8,128)(2,1)S(1)} %get-tuple-element.41), channel_id=1, source_target_pairs={{0,24},{8,16},{16,8},{24,0},{1,25},{9,17},{17,9},{25,1},{2,26},{10... | collective-permute-start | bytes 294920 | tf_op jit(solution)/shard_map/return/ppermute | solution.py:370
  67.5 5.6 %collective-permute-start.13 = (bf16[2,192,256]{2,1,0:T(8,128)(2,1)S(1)}, bf16[2,192,256]{2,1,0:T(8,128)(2,1)S(1)}, u32[]{:S(2)}, u32[]{:S(2)}) collective-permute-start(bf16[2,192,256]{2,1,0:T(8,128)(2,1)S(1)} %fusion), channel_id=1, source_target_pairs={{0,4},{4,0},{1,5},{5,1},{2,6},{6,2},{3,7},{7,3},{8,12},{12,8},{9,1... | collective-permute-start | bytes 589832 | tf_op jit(solution)/shard_map/return/ppermute | solution.py:439

commit v5 on v3

--- a/solution.py
+++ b/solution.py
@@ -259,9 +259,9 @@
         for head in range(HEADS):
             cut = head_slice(head)
             out = None
-            for d in range(4):
+            for d, o_ref in zip((0, 3, 2, 1), o_refs):
                 weight = share_ref[:, 4 * head + d : 4 * head + d + 1]
-                piece = o_refs[d][:, cut].astype(F32) * weight
+                piece = o_ref[:, cut].astype(F32) * weight
                 out = piece if out is None else out + piece
             out_ref[:, cut] = out.astype(BF16)
     else:
@@ -411,7 +411,7 @@
         o2, o3, stat = forward(qg2, qg3, first)
     with jax.named_scope("merge"):
         stats = [stat] + [other_frames(stat, d) for d in (1, 2, 3)]
-        outs = [o0] + [other_frames(o, d) for d, o in ((1, o1), (2, o2), (3, o3))]
+        outs = [o0] + [other_frames(o, d) for d, o in ((3, o3), (2, o2), (1, o1))]
 
     queries = (qg, qg1, qg2, qg3)
     col_shape = jax.ShapeDtypeStruct((grid_rows, 2, cells, chan), BF16)
@@ -445,14 +445,14 @@
         )
     with jax.named_scope("return"):
         col_parts = [own, *sides]
-        dqs = [d0] + [other_frames(x, d) for d, x in ((1, d1), (2, d2), (3, d3))]
+        dqs = [d0] + [other_frames(x, d) for d, x in ((3, d3), (2, d2), (1, d1))]
         row_parts = []
         for row, pairs in enumerate(row_sides, start=1):
             partial_sum = sum(x[row].astype(F32) for x in col_parts).astype(BF16)
             row_parts.append(lax.ppermute(partial_sum, "ha", pairs))
 
     with jax.named_scope("finish"):
-        grad_query = call(finish_query_kernel, plain, (*dqs, rope))
+        grad_query = call(finish_query_kernel, plain, (*dqs, rope), 5 * product)
         grad_key, grad_value = call(
             functools.partial(finish_key_kernel, grid_cols, len(row_parts)),
             (plain, plain),

time: 58.7 us -> 56.8 us (0.968); the launches traced: 58.5 us -> 55.9 us
  waiting for transfers between devices: 14.4 us -> 12.5 us
  starting transfers between devices: 31.3 us -> 30.6 us
    ppermute x2, waiting for transfers between devices: 4.24 us -> 0.32 us  [shards(): sides = [lax.ppermute(x, 'wa', pairs) for x, pairs in zip(sides, col_sides)]]
    ppermute x12, waiting for transfers between devices: 7.73 us -> 9.73 us  [other_frames(): lax.ppermute(x, 'ta', [(i, i ^ distance) for i in range(sizes['ta'])])]
    ppermute x12, starting transfers between devices: 15.3 us -> 14.6 us  [other_frames(): lax.ppermute(x, 'ta', [(i, i ^ distance) for i in range(sizes['ta'])])]
  transfers between devices with their start and end apart: 20 -> 20, of which waited for: 6 -> 7; matrix products, arithmetic and copies ran while one was open for 0% -> 0% of each run, Pallas kernels for 14% -> 14%
where the time goes in v5:
time: 56.8 us; the launch traced here: 55.9 us
  starting transfers between devices  30.6 us (54%)
  waiting for transfers between devices  12.5 us (22%)
  Pallas kernels  12 us (21%)
  between operations  0.72 us (1%)
    ppermute x12, starting transfers between devices, other_frames(): lax.ppermute(x, 'ta', [(i, i ^ distance) for i in range(sizes['ta'])])  14.6 us
    pallas_call x7, Pallas kernels, call(): pl.pallas_call(kernel, out_shape=out_shape, in_specs=[pl.BlockSpec(memory...  12 us
    ppermute x12, waiting for transfers between devices, other_frames(): lax.ppermute(x, 'ta', [(i, i ^ distance) for i in range(sizes['ta'])])  9.73 us
    ppermute x4, starting transfers between devices, shards(): lax.ppermute(block, 'wa', pairs)  8.2 us
    ppermute x2, starting transfers between devices, shards(): sides = [lax.ppermute(x, 'wa', pairs) for x, pairs in zip(sides, col_sides)]  5.34 us
    ppermute x4, waiting for transfers between devices, shards(): lax.ppermute(block, 'wa', pairs)  2.4 us
    ppermute x1, starting transfers between devices, shards(): kv_rows = [kv] + [lax.ppermute(kv, 'ha', pairs) for pairs in row_sides]  2.11 us
  transfers between devices with their start and end apart: 20, of which 7 were waited for; matrix products, arithmetic and copies ran while one was open for 0% of the time, Pallas kernels for 14%

profile of v5, /device:TPU:1, one launch (start us, length us, event | category | flops | bytes accessed | tf_op | source)
XLA Modules:
  0.0 55.9 jit_solution(18358380859398512382)
XLA Ops:
  0.6 1.3 %rotate.1 = (bf16[2,192,256]{2,1,0:T(8,128)(2,1)S(1)}, bf16[2,192,256]{2,1,0:T(8,128)(2,1)S(1)}, f32[3,192,128]{2,1,0:T(8,128)S(1)}) custom-call(bf16[192,256]{1,0:T(8,128)(2,1)} %bitcast.10, bf16[192,256]{1,0:T(8,128)(2,1)} %bitcast.11, bf16[192,256]{1,0:T(8,128)(2,1)} %bitcast.12, bf16[192,256]{1,0:T(8,128)(2,1)} %bitcast.13, ...), custom_call_target="tpu_custom_call" | custom-call | bytes 1179648 | tf_op jit(solution)/shard_map/rotate/pallas_call | solution.py:337
  1.9 2.1 %collective-permute-start.3 = (bf16[2,192,256]{2,1,0:T(8,128)(2,1)S(1)}, bf16[2,192,256]{2,1,0:T(8,128)(2,1)S(1)}, u32[]{:S(2)}, u32[]{:S(2)}) collective-permute-start(bf16[2,192,256]{2,1,0:T(8,128)(2,1)S(1)} %get-tuple-element.28.refs_2_.refs_4_), channel_id=1, source_target_pairs={{0,4},{4,0},{1,5},{5,1},{2,6},{6,2},{3,7},{7,3},{8,12},{12,8},{9,1... | collective-permute-start | bytes 589832 | tf_op jit(solution)/shard_map/halo/ppermute | solution.py:379
  4.0 2.3 %collective-permute-start.1 = (bf16[2,192,256]{2,1,0:T(8,128)(2,1)S(1)}, bf16[2,192,256]{2,1,0:T(8,128)(2,1)S(1)}, u32[]{:S(2)}, u32[]{:S(2)}) collective-permute-start(bf16[2,192,256]{2,1,0:T(8,128)(2,1)S(1)} %get-tuple-element.27.refs_0_), channel_id=1, source_target_pairs={{0,16},{8,24},{16,0},{24,8},{1,17},{9,25},{17,1},{25,9},{2,18},{10... | collective-permute-start | bytes 589832 | tf_op jit(solution)/shard_map/halo/ppermute | solution.py:374
  6.3 1.3 %collective-permute-start = (bf16[2,192,256]{2,1,0:T(8,128)(2,1)S(1)}, bf16[2,192,256]{2,1,0:T(8,128)(2,1)S(1)}, u32[]{:S(2)}, u32[]{:S(2)}) collective-permute-start(bf16[2,192,256]{2,1,0:T(8,128)(2,1)S(1)} %get-tuple-element.27.refs_0_), channel_id=1, source_target_pairs={{0,8},{8,0},{16,24},{24,16},{1,9},{9,1},{17,25},{25,17},{2,10},{10... | collective-permute-start | bytes 589832 | tf_op jit(solution)/shard_map/halo/ppermute | solution.py:374
  7.6 4.5 %collective-permute-start.6 = (bf16[2,192,256]{2,1,0:T(8,128)(2,1)S(1)}, bf16[2,192,256]{2,1,0:T(8,128)(2,1)S(1)}, u32[]{:S(2)}, u32[]{:S(2)}) collective-permute-start(bf16[2,192,256]{2,1,0:T(8,128)(2,1)S(1)} %get-tuple-element.28.refs_2_.refs_4_), channel_id=1, source_target_pairs={{0,0},{1,2},{2,1},{3,3},{4,4},{5,6},{6,5},{7,7},{8,8},{9,10},{10,9... | collective-permute-start | bytes 589832 | tf_op jit(solution)/shard_map/halo/ppermute | solution.py:384
  12.2 0.1 collective-permute-start.4
  12.2 0.0 collective-permute-done.3.refs_5_
  12.2 1.9 %collective-permute-start.7 = (bf16[2,192,256]{2,1,0:T(8,128)(2,1)S(1)}, bf16[2,192,256]{2,1,0:T(8,128)(2,1)S(1)}, u32[]{:S(2)}, u32[]{:S(2)}) collective-permute-start(bf16[2,192,256]{2,1,0:T(8,128)(2,1)S(1)} %collective-permute-done.3.refs_5_), channel_id=1, source_target_pairs={{0,0},{1,2},{2,1},{3,3},{4,4},{5,6},{6,5},{7,7},{8,8},{9,10},{10,9... | collective-permute-start | bytes 589832 | tf_op jit(solution)/shard_map/halo/ppermute | solution.py:384
  14.2 0.7 %collective-permute-done.1.refs_0_.refs_2_ = bf16[2,192,256]{2,1,0:T(8,128)(2,1)S(1)} collective-permute-done((bf16[2,192,256]{2,1,0:T(8,128)(2,1)S(1)}, bf16[2,192,256]{2,1,0:T(8,128)(2,1)S(1)}, u32[]{:S(2)}, u32[]{:S(2)}) %collective-permute-start.1) | collective-permute-done | bytes 196640 | tf_op jit(solution)/shard_map/halo/ppermute | solution.py:374
  14.9 1.7 %collective-permute-start.5 = (bf16[2,192,256]{2,1,0:T(8,128)(2,1)S(1)}, bf16[2,192,256]{2,1,0:T(8,128)(2,1)S(1)}, u32[]{:S(2)}, u32[]{:S(2)}) collective-permute-start(bf16[2,192,256]{2,1,0:T(8,128)(2,1)S(1)} %collective-permute-done.3.refs_5_), channel_id=1, source_target_pairs={{0,1},{1,0},{2,3},{3,2},{4,5},{5,4},{6,7},{7,6},{8,9},{9,8},{10,11... | collective-permute-start | bytes 589832 | tf_op jit(solution)/shard_map/halo/ppermute | solution.py:384
  16.5 0.0 collective-permute-done.refs_1_
  16.5 0.3 collective-permute-start.2
  16.8 0.0 collective-permute-done.6.refs_4_.refs_6_
  16.8 0.0 collective-permute-done.4.refs_3_.refs_4_
  16.8 2.4 %collective-permute-done.7.refs_7_ = bf16[2,192,256]{2,1,0:T(8,128)(2,1)S(1)} collective-permute-done((bf16[2,192,256]{2,1,0:T(8,128)(2,1)S(1)}, bf16[2,192,256]{2,1,0:T(8,128)(2,1)S(1)}, u32[]{:S(2)}, u32[]{:S(2)}) %collective-permute-start.7) | collective-permute-done | bytes 196640 | tf_op jit(solution)/shard_map/halo/ppermute | solution.py:384
  19.2 0.0 collective-permute-done.5.refs_6_.refs_5_
  19.2 2.0 %attend.2 = (bf16[192,256]{1,0:T(8,128)(2,1)S(1)}, bf16[192,256]{1,0:T(8,128)(2,1)S(1)}, f32[8,384]{1,0:T(8,128)S(1)}) custom-call(bf16[2,192,256]{2,1,0:T(8,128)(2,1)S(1)} %get-tuple-element.27.refs_0_, bf16[2,192,256]{2,1,0:T(8,128)(2,1)S(1)} %collective-permute-done.refs_1_, bf16[2,192,256]{2,1,0:T(8,128)(2,1)S(1)} %get-tuple-element.28.refs_2_.refs_4_, ...), custom_call_target="tpu_custom_call" | custom-call | flops 3623878656 | bytes 1781760 | tf_op jit(solution)/shard_map/attend/pallas_call | solution.py:337
  21.2 1.6 %collective-permute-done.2.refs_1_.refs_3_ = bf16[2,192,256]{2,1,0:T(8,128)(2,1)S(1)} collective-permute-done((bf16[2,192,256]{2,1,0:T(8,128)(2,1)S(1)}, bf16[2,192,256]{2,1,0:T(8,128)(2,1)S(1)}, u32[]{:S(2)}, u32[]{:S(2)}) %collective-permute-start.2) | collective-permute-done | bytes 196640 | tf_op jit(solution)/shard_map/halo/ppermute | solution.py:374
  22.9 2.0 %attend.3 = (bf16[192,256]{1,0:T(8,128)(2,1)S(1)}, bf16[192,256]{1,0:T(8,128)(2,1)S(1)}, f32[2,8,384]{2,1,0:T(8,128)S(1)}) custom-call(bf16[2,192,256]{2,1,0:T(8,128)(2,1)S(1)} %collective-permute-done.1.refs_0_.refs_2_, bf16[2,192,256]{2,1,0:T(8,128)(2,1)S(1)} %collective-permute-done.2.refs_1_.refs_3_, ...), custom_call_target="tpu_custom_call" | custom-call | flops 3623878656 | bytes 1806336 | tf_op jit(solution)/shard_map/attend/pallas_call | solution.py:337
  24.8 3.3 %collective-permute-start.10 = (f32[2,8,384]{2,1,0:T(8,128)S(1)}, f32[2,8,384]{2,1,0:T(8,128)S(1)}, u32[]{:S(2)}, u32[]{:S(2)}) collective-permute-start(f32[2,8,384]{2,1,0:T(8,128)S(1)} %get-tuple-element.30.refs_8_), channel_id=1, source_target_pairs={{0,24},{8,16},{16,8},{24,0},{1,25},{9,17},{17,9},{25,1},{2,26},{10... | collective-permute-start | bytes 73736 | tf_op jit(solution)/shard_map/merge/ppermute | solution.py:374
  28.2 0.0 collective-permute-start.9
  28.2 0.4 collective-permute-start.8
  28.5 1.1 %collective-permute-start.13 = (bf16[192,256]{1,0:T(8,128)(2,1)S(1)}, bf16[192,256]{1,0:T(8,128)(2,1)S(1)}, u32[]{:S(2)}, u32[]{:S(2)}) collective-permute-start(bf16[192,256]{1,0:T(8,128)(2,1)S(1)} %get-tuple-element.38), channel_id=1, source_target_pairs={{0,8},{8,0},{16,24},{24,16},{1,9},{9,1},{17,25},{25,17},{2,10},{10... | collective-permute-start | bytes 294920 | tf_op jit(solution)/shard_map/merge/ppermute | solution.py:374
  29.7 2.1 %collective-permute-start.11 = (bf16[192,256]{1,0:T(8,128)(2,1)S(1)}, bf16[192,256]{1,0:T(8,128)(2,1)S(1)}, u32[]{:S(2)}, u32[]{:S(2)}) collective-permute-start(bf16[192,256]{1,0:T(8,128)(2,1)S(1)} %get-tuple-element.36), channel_id=1, source_target_pairs={{0,24},{8,16},{16,8},{24,0},{1,25},{9,17},{17,9},{25,1},{2,26},{10... | collective-permute-start | bytes 294920 | tf_op jit(solution)/shard_map/merge/ppermute | solution.py:374
  31.8 0.0 collective-permute-done.10.refs_11_
  31.8 0.3 collective-permute-start.12
  32.0 0.0 collective-permute-done.9.refs_10_
  32.0 0.0 collective-permute-done.8.refs_9_
  32.0 3.1 %gradients.2 = (f32[2,768]{1,0:T(2,128)S(1)}, f32[2,768]{1,0:T(2,128)S(1)}, f32[192,128]{1,0:T(8,128)S(1)}, f32[2,128,768]{2,1,0:T(8,128)S(1)}, bf16[2,2,192,256...) custom-call(bf16[2,192,256]{2,1,0:T(8,128)(2,1)S(1)} %get-tuple-element.27.refs_0_, ...), custom_call_target="tpu_custom_call" | custom-call | flops 12079595520 | bytes 3354624 | tf_op jit(solution)/shard_map/gradients/pallas_call | solution.py:337
  35.1 2.3 %collective-permute-start.17 = (bf16[2,2,192,256]{3,2,1,0:T(8,128)(2,1)S(1)}, bf16[2,2,192,256]{3,2,1,0:T(8,128)(2,1)S(1)}, u32[]{:S(2)}, u32[]{:S(2)}) collective-permute-start(bf16[2,2,192,256]{3,2,1,0:T(8,128)(2,1)S(1)} %get-tuple-element.46), channel_id=1, source_target_pairs={{0,1},{1,0},{2,3},{3,2},{4,5},{5,4},{6,7},{7,6},{8,9},{9,8},{10,11... | collective-permute-start | bytes 1179656 | tf_op jit(solution)/shard_map/gradients/ppermute | solution.py:442
  37.4 3.0 %collective-permute-start.18 = (bf16[2,2,192,256]{3,2,1,0:T(8,128)(2,1)S(1)}, bf16[2,2,192,256]{3,2,1,0:T(8,128)(2,1)S(1)}, u32[]{:S(2)}, u32[]{:S(2)}) collective-permute-start(bf16[2,2,192,256]{3,2,1,0:T(8,128)(2,1)S(1)} %get-tuple-element.47), channel_id=1, source_target_pairs={{0,0},{1,2},{2,1},{3,3},{4,4},{5,6},{6,5},{7,7},{8,8},{9,10},{10,9... | collective-permute-start | bytes 1179656 | tf_op jit(solution)/shard_map/gradients/ppermute | solution.py:442
  40.5 0.0 collective-permute-done.13.refs_13_
  40.5 0.0 collective-permute-done.11.refs_11_
  40.5 0.1 collective-permute-done.12.refs_12_
  40.6 2.1 %gradients.3 = (bf16[192,256]{1,0:T(8,128)(2,1)S(1)}, bf16[192,256]{1,0:T(8,128)(2,1)S(1)}, bf16[192,256]{1,0:T(8,128)(2,1)S(1)}, bf16[192,256]{1,0:T(8,128)(2,1...) custom-call(bf16[2,192,256]{2,1,0:T(8,128)(2,1)S(1)} %get-tuple-element.27.refs_0_, ...), custom_call_target="tpu_custom_call" | custom-call | flops 6039797760 | bytes 3354624 | tf_op jit(solution)/shard_map/gradients/pallas_call | solution.py:337
  42.6 2.5 %collective-permute-start.14 = (bf16[192,256]{1,0:T(8,128)(2,1)S(1)}, bf16[192,256]{1,0:T(8,128)(2,1)S(1)}, u32[]{:S(2)}, u32[]{:S(2)}) collective-permute-start(bf16[192,256]{1,0:T(8,128)(2,1)S(1)} %get-tuple-element.41), channel_id=1, source_target_pairs={{0,24},{8,16},{16,8},{24,0},{1,25},{9,17},{17,9},{25,1},{2,26},{10... | collective-permute-start | bytes 294920 | tf_op jit(solution)/shard_map/return/ppermute | solution.py:374
  45.2 0.0 collective-permute-start.15
  45.2 1.0 %collective-permute-start.16 = (bf16[192,256]{1,0:T(8,128)(2,1)S(1)}, bf16[192,256]{1,0:T(8,128)(2,1)S(1)}, u32[]{:S(2)}, u32[]{:S(2)}) collective-permute-start(bf16[192,256]{1,0:T(8,128)(2,1)S(1)} %get-tuple-element.43), channel_id=1, source_target_pairs={{0,8},{8,0},{16,24},{24,16},{1,9},{9,1},{17,25},{25,17},{2,10},{10... | collective-permute-start | bytes 294920 | tf_op jit(solution)/shard_map/return/ppermute | solution.py:374
  46.2 0.0 collective-permute-done.17.refs_1_
  46.2 0.3 collective-permute-done.18.refs_2_
  46.5 0.1 fusion
  46.6 0.3 collective-permute-start.19
  46.9 1.2 %collective-permute-done.14.refs_1_ = bf16[192,256]{1,0:T(8,128)(2,1)S(1)} collective-permute-done((bf16[192,256]{1,0:T(8,128)(2,1)S(1)}, bf16[192,256]{1,0:T(8,128)(2,1)S(1)}, u32[]{:S(2)}, u32[]{:S(2)}) %collective-permute-start.14) | collective-permute-done | bytes 98336 | tf_op jit(solution)/shard_map/return/ppermute | solution.py:374
  48.0 6.1 %collective-permute-done.15.refs_2_ = bf16[192,256]{1,0:T(8,128)(2,1)S(1)} collective-permute-done((bf16[192,256]{1,0:T(8,128)(2,1)S(1)}, bf16[192,256]{1,0:T(8,128)(2,1)S(1)}, u32[]{:S(2)}, u32[]{:S(2)}) %collective-permute-start.15) | collective-permute-done | bytes 98336 | tf_op jit(solution)/shard_map/return/ppermute | solution.py:374
  54.2 0.0 collective-permute-done.16.refs_3_
  54.2 0.8 %finish.2 = bf16[192,256]{1,0:T(8,128)(2,1)} custom-call(bf16[192,256]{1,0:T(8,128)(2,1)S(1)} %get-tuple-element.40.refs_0_, bf16[192,256]{1,0:T(8,128)(2,1)S(1)} %collective-permute-done.14.refs_1_, bf16[192,256]{1,0:T(8,128)(2,1)S(1)} %collective-permute-done.15.refs_2_, bf16[192,256]{1,0:T(8,128)(2,1)S(1)} %collective-permute-done.16.refs_3_, ...), custom_call_target="tpu_custom_call" | custom-call | flops 9059696640 | bytes 786432 | tf_op jit(solution)/shard_map/finish/pallas_call | solution.py:337
  55.0 0.0 collective-permute-done.19.refs_3_
  55.0 0.9 %finish.3 = (bf16[192,256]{1,0:T(8,128)(2,1)}, bf16[192,256]{1,0:T(8,128)(2,1)}) custom-call(bf16[2,2,192,256]{3,2,1,0:T(8,128)(2,1)S(1)} %get-tuple-element.45.refs_0_, bf16[2,2,192,256]{3,2,1,0:T(8,128)(2,1)S(1)} %collective-permute-done.17.refs_1_, bf16[2,2,192,256]{3,2,1,0:T(8,128)(2,1)S(1)} %collective-permute-done.18.refs_2_, ...), custom_call_target="tpu_custom_call" | custom-call | bytes 1867776 | tf_op jit(solution)/shard_map/finish/pallas_call | solution.py:337
Async XLA Ops:
  1.9 10.3 %collective-permute-start.3 = (bf16[2,192,256]{2,1,0:T(8,128)(2,1)S(1)}, bf16[2,192,256]{2,1,0:T(8,128)(2,1)S(1)}, u32[]{:S(2)}, u32[]{:S(2)}) collective-permute-start(bf16[2,192,256]{2,1,0:T(8,128)(2,1)S(1)} %get-tuple-element.28.refs_2_.refs_4_), channel_id=1, source_target_pairs={{0,4},{4,0},{1,5},{5,1},{2,6},{6,2},{3,7},{7,3},{8,12},{12,8},{9,1... | collective-permute-start | bytes 589832 | tf_op jit(solution)/shard_map/halo/ppermute | solution.py:379
  4.0 10.9 %collective-permute-start.1 = (bf16[2,192,256]{2,1,0:T(8,128)(2,1)S(1)}, bf16[2,192,256]{2,1,0:T(8,128)(2,1)S(1)}, u32[]{:S(2)}, u32[]{:S(2)}) collective-permute-start(bf16[2,192,256]{2,1,0:T(8,128)(2,1)S(1)} %get-tuple-element.27.refs_0_), channel_id=1, source_target_pairs={{0,16},{8,24},{16,0},{24,8},{1,17},{9,25},{17,1},{25,9},{2,18},{10... | collective-permute-start | bytes 589832 | tf_op jit(solution)/shard_map/halo/ppermute | solution.py:374
  6.3 10.2 %collective-permute-start = (bf16[2,192,256]{2,1,0:T(8,128)(2,1)S(1)}, bf16[2,192,256]{2,1,0:T(8,128)(2,1)S(1)}, u32[]{:S(2)}, u32[]{:S(2)}) collective-permute-start(bf16[2,192,256]{2,1,0:T(8,128)(2,1)S(1)} %get-tuple-element.27.refs_0_), channel_id=1, source_target_pairs={{0,8},{8,0},{16,24},{24,16},{1,9},{9,1},{17,25},{25,17},{2,10},{10... | collective-permute-start | bytes 589832 | tf_op jit(solution)/shard_map/halo/ppermute | solution.py:374
  7.6 9.2 %collective-permute-start.6 = (bf16[2,192,256]{2,1,0:T(8,128)(2,1)S(1)}, bf16[2,192,256]{2,1,0:T(8,128)(2,1)S(1)}, u32[]{:S(2)}, u32[]{:S(2)}) collective-permute-start(bf16[2,192,256]{2,1,0:T(8,128)(2,1)S(1)} %get-tuple-element.28.refs_2_.refs_4_), channel_id=1, source_target_pairs={{0,0},{1,2},{2,1},{3,3},{4,4},{5,6},{6,5},{7,7},{8,8},{9,10},{10,9... | collective-permute-start | bytes 589832 | tf_op jit(solution)/shard_map/halo/ppermute | solution.py:384
  12.2 4.7 %collective-permute-start.4 = (bf16[2,192,256]{2,1,0:T(8,128)(2,1)S(1)}, bf16[2,192,256]{2,1,0:T(8,128)(2,1)S(1)}, u32[]{:S(2)}, u32[]{:S(2)}) collective-permute-start(bf16[2,192,256]{2,1,0:T(8,128)(2,1)S(1)} %get-tuple-element.28.refs_2_.refs_4_), channel_id=1, source_target_pairs={{0,1},{1,0},{2,3},{3,2},{4,5},{5,4},{6,7},{7,6},{8,9},{9,8},{10,11... | collective-permute-start | bytes 589832 | tf_op jit(solution)/shard_map/halo/ppermute | solution.py:384
  12.2 7.0 %collective-permute-start.7 = (bf16[2,192,256]{2,1,0:T(8,128)(2,1)S(1)}, bf16[2,192,256]{2,1,0:T(8,128)(2,1)S(1)}, u32[]{:S(2)}, u32[]{:S(2)}) collective-permute-start(bf16[2,192,256]{2,1,0:T(8,128)(2,1)S(1)} %collective-permute-done.3.refs_5_), channel_id=1, source_target_pairs={{0,0},{1,2},{2,1},{3,3},{4,4},{5,6},{6,5},{7,7},{8,8},{9,10},{10,9... | collective-permute-start | bytes 589832 | tf_op jit(solution)/shard_map/halo/ppermute | solution.py:384
  14.9 4.4 %collective-permute-start.5 = (bf16[2,192,256]{2,1,0:T(8,128)(2,1)S(1)}, bf16[2,192,256]{2,1,0:T(8,128)(2,1)S(1)}, u32[]{:S(2)}, u32[]{:S(2)}) collective-permute-start(bf16[2,192,256]{2,1,0:T(8,128)(2,1)S(1)} %collective-permute-done.3.refs_5_), channel_id=1, source_target_pairs={{0,1},{1,0},{2,3},{3,2},{4,5},{5,4},{6,7},{7,6},{8,9},{9,8},{10,11... | collective-permute-start | bytes 589832 | tf_op jit(solution)/shard_map/halo/ppermute | solution.py:384
  16.5 6.3 %collective-permute-start.2 = (bf16[2,192,256]{2,1,0:T(8,128)(2,1)S(1)}, bf16[2,192,256]{2,1,0:T(8,128)(2,1)S(1)}, u32[]{:S(2)}, u32[]{:S(2)}) collective-permute-start(bf16[2,192,256]{2,1,0:T(8,128)(2,1)S(1)} %collective-permute-done.1.refs_0_.refs_2_), channel_id=1, source_target_pairs={{0,8},{8,0},{16,24},{24,16},{1,9},{9,1},{17,25},{25,17},{2,10},{10... | collective-permute-start | bytes 589832 | tf_op jit(solution)/shard_map/halo/ppermute | solution.py:374
  24.8 6.9 %collective-permute-start.10 = (f32[2,8,384]{2,1,0:T(8,128)S(1)}, f32[2,8,384]{2,1,0:T(8,128)S(1)}, u32[]{:S(2)}, u32[]{:S(2)}) collective-permute-start(f32[2,8,384]{2,1,0:T(8,128)S(1)} %get-tuple-element.30.refs_8_), channel_id=1, source_target_pairs={{0,24},{8,16},{16,8},{24,0},{1,25},{9,17},{17,9},{25,1},{2,26},{10... | collective-permute-start | bytes 73736 | tf_op jit(solution)/shard_map/merge/ppermute | solution.py:374
  28.2 3.8 %collective-permute-start.9 = (f32[2,8,384]{2,1,0:T(8,128)S(1)}, f32[2,8,384]{2,1,0:T(8,128)S(1)}, u32[]{:S(2)}, u32[]{:S(2)}) collective-permute-start(f32[2,8,384]{2,1,0:T(8,128)S(1)} %get-tuple-element.30.refs_8_), channel_id=1, source_target_pairs={{0,16},{8,24},{16,0},{24,8},{1,17},{9,25},{17,1},{25,9},{2,18},{10... | collective-permute-start | bytes 73736 | tf_op jit(solution)/shard_map/merge/ppermute | solution.py:374
  28.2 3.8 %collective-permute-start.8 = (f32[2,8,384]{2,1,0:T(8,128)S(1)}, f32[2,8,384]{2,1,0:T(8,128)S(1)}, u32[]{:S(2)}, u32[]{:S(2)}) collective-permute-start(f32[2,8,384]{2,1,0:T(8,128)S(1)} %get-tuple-element.30.refs_8_), channel_id=1, source_target_pairs={{0,8},{8,0},{16,24},{24,16},{1,9},{9,1},{17,25},{25,17},{2,10},{10... | collective-permute-start | bytes 73736 | tf_op jit(solution)/shard_map/merge/ppermute | solution.py:374
  28.5 11.9 %collective-permute-start.13 = (bf16[192,256]{1,0:T(8,128)(2,1)S(1)}, bf16[192,256]{1,0:T(8,128)(2,1)S(1)}, u32[]{:S(2)}, u32[]{:S(2)}) collective-permute-start(bf16[192,256]{1,0:T(8,128)(2,1)S(1)} %get-tuple-element.38), channel_id=1, source_target_pairs={{0,8},{8,0},{16,24},{24,16},{1,9},{9,1},{17,25},{25,17},{2,10},{10... | collective-permute-start | bytes 294920 | tf_op jit(solution)/shard_map/merge/ppermute | solution.py:374
  29.7 10.8 %collective-permute-start.11 = (bf16[192,256]{1,0:T(8,128)(2,1)S(1)}, bf16[192,256]{1,0:T(8,128)(2,1)S(1)}, u32[]{:S(2)}, u32[]{:S(2)}) collective-permute-start(bf16[192,256]{1,0:T(8,128)(2,1)S(1)} %get-tuple-element.36), channel_id=1, source_target_pairs={{0,24},{8,16},{16,8},{24,0},{1,25},{9,17},{17,9},{25,1},{2,26},{10... | collective-permute-start | bytes 294920 | tf_op jit(solution)/shard_map/merge/ppermute | solution.py:374
  31.8 8.8 %collective-permute-start.12 = (bf16[192,256]{1,0:T(8,128)(2,1)S(1)}, bf16[192,256]{1,0:T(8,128)(2,1)S(1)}, u32[]{:S(2)}, u32[]{:S(2)}) collective-permute-start(bf16[192,256]{1,0:T(8,128)(2,1)S(1)} %get-tuple-element.37), channel_id=1, source_target_pairs={{0,16},{8,24},{16,0},{24,8},{1,17},{9,25},{17,1},{25,9},{2,18},{10... | collective-permute-start | bytes 294920 | tf_op jit(solution)/shard_map/merge/ppermute | solution.py:374
  35.1 11.1 %collective-permute-start.17 = (bf16[2,2,192,256]{3,2,1,0:T(8,128)(2,1)S(1)}, bf16[2,2,192,256]{3,2,1,0:T(8,128)(2,1)S(1)}, u32[]{:S(2)}, u32[]{:S(2)}) collective-permute-start(bf16[2,2,192,256]{3,2,1,0:T(8,128)(2,1)S(1)} %get-tuple-element.46), channel_id=1, source_target_pairs={{0,1},{1,0},{2,3},{3,2},{4,5},{5,4},{6,7},{7,6},{8,9},{9,8},{10,11... | collective-permute-start | bytes 1179656 | tf_op jit(solution)/shard_map/gradients/ppermute | solution.py:442
  37.4 9.1 %collective-permute-start.18 = (bf16[2,2,192,256]{3,2,1,0:T(8,128)(2,1)S(1)}, bf16[2,2,192,256]{3,2,1,0:T(8,128)(2,1)S(1)}, u32[]{:S(2)}, u32[]{:S(2)}) collective-permute-start(bf16[2,2,192,256]{3,2,1,0:T(8,128)(2,1)S(1)} %get-tuple-element.47), channel_id=1, source_target_pairs={{0,0},{1,2},{2,1},{3,3},{4,4},{5,6},{6,5},{7,7},{8,8},{9,10},{10,9... | collective-permute-start | bytes 1179656 | tf_op jit(solution)/shard_map/gradients/ppermute | solution.py:442
  42.6 5.4 %collective-permute-start.14 = (bf16[192,256]{1,0:T(8,128)(2,1)S(1)}, bf16[192,256]{1,0:T(8,128)(2,1)S(1)}, u32[]{:S(2)}, u32[]{:S(2)}) collective-permute-start(bf16[192,256]{1,0:T(8,128)(2,1)S(1)} %get-tuple-element.41), channel_id=1, source_target_pairs={{0,24},{8,16},{16,8},{24,0},{1,25},{9,17},{17,9},{25,1},{2,26},{10... | collective-permute-start | bytes 294920 | tf_op jit(solution)/shard_map/return/ppermute | solution.py:374
  45.2 9.0 %collective-permute-start.15 = (bf16[192,256]{1,0:T(8,128)(2,1)S(1)}, bf16[192,256]{1,0:T(8,128)(2,1)S(1)}, u32[]{:S(2)}, u32[]{:S(2)}) collective-permute-start(bf16[192,256]{1,0:T(8,128)(2,1)S(1)} %get-tuple-element.42), channel_id=1, source_target_pairs={{0,16},{8,24},{16,0},{24,8},{1,17},{9,25},{17,1},{25,9},{2,18},{10... | collective-permute-start | bytes 294920 | tf_op jit(solution)/shard_map/return/ppermute | solution.py:374
  45.2 9.0 %collective-permute-start.16 = (bf16[192,256]{1,0:T(8,128)(2,1)S(1)}, bf16[192,256]{1,0:T(8,128)(2,1)S(1)}, u32[]{:S(2)}, u32[]{:S(2)}) collective-permute-start(bf16[192,256]{1,0:T(8,128)(2,1)S(1)} %get-tuple-element.43), channel_id=1, source_target_pairs={{0,8},{8,0},{16,24},{24,16},{1,9},{9,1},{17,25},{25,17},{2,10},{10... | collective-permute-start | bytes 294920 | tf_op jit(solution)/shard_map/return/ppermute | solution.py:374
  46.6 8.4 %collective-permute-start.19 = (bf16[2,192,256]{2,1,0:T(8,128)(2,1)S(1)}, bf16[2,192,256]{2,1,0:T(8,128)(2,1)S(1)}, u32[]{:S(2)}, u32[]{:S(2)}) collective-permute-start(bf16[2,192,256]{2,1,0:T(8,128)(2,1)S(1)} %fusion), channel_id=1, source_target_pairs={{0,4},{4,0},{1,5},{5,1},{2,6},{6,2},{3,7},{7,3},{8,12},{12,8},{9,1... | collective-permute-start | bytes 589832 | tf_op jit(solution)/shard_map/return/ppermute | solution.py:452

commit v6 on v4

--- a/solution.py
+++ b/solution.py
@@ -145,15 +145,15 @@
     return None if valid is None else jnp.where(valid, 0.0, NEGATIVE).astype(F32)
 
 
-def frame_block(ref, distance):
-    return ref.at[lax.axis_index("ta") ^ distance]
-
-
-def forward_kernel(groups, sizes, cells, qg_ref, *refs):
+def forward_kernel(groups, sizes, cells, count, last, *refs):
     tile_count = sum(len(members) for _, members in groups)
-    kv_refs = refs[:tile_count]
-    o_refs = refs[tile_count : tile_count + 4]
-    stat_ref, key_buf, value_buf = refs[tile_count + 4 :]
+    qg_refs = refs[:count]
+    kv_refs = refs[count : count + tile_count]
+    rest = refs[count + tile_count :]
+    if last:
+        first_ref, rest = rest[0], rest[1:]
+    o_refs = rest[:count]
+    stat_ref, key_buf, value_buf = rest[count:]
     at = 0
     spans = []
     for flags, members in groups:
@@ -163,15 +163,13 @@
             value_buf[at : at + cells] = kv_refs[member][1]
             at += cells
         spans.append((begin, at, group_bias(flags, sizes)))
-    lane = lax.broadcasted_iota(jnp.int32, (2 * cells, DH), 1)
-    for half in range(2):
-        blocks = [frame_block(qg_ref, 2 * half + i) for i in range(2)]
-        stat = jnp.zeros((2 * cells, DH), F32)
+    lane = lax.broadcasted_iota(jnp.int32, (cells, DH), 1)
+    stats = []
+    for qg_ref, o_ref in zip(qg_refs, o_refs):
+        stat = jnp.zeros((cells, DH), F32)
         for head in range(HEADS):
             cut = head_slice(head)
-            query = jnp.concatenate([block[0, :, cut] for block in blocks], axis=0)
-            grad = jnp.concatenate([block[1, :, cut] for block in blocks], axis=0)
-            scores = [dot_nt(query, key_buf[lo:hi, cut]) for lo, hi, _ in spans]
+            scores = [dot_nt(qg_ref[0, :, cut], key_buf[lo:hi, cut]) for lo, hi, _ in spans]
             best = None
             for raw, (_, _, bias) in zip(scores, spans):
                 top = jnp.max(raw, axis=1, keepdims=True) * SCALE_LOG2
@@ -188,22 +186,31 @@
                 total = part if total is None else total + part
                 out = piece if out is None else out + piece
             out = out * (1.0 / total)
-            dotted = jnp.sum(out * grad.astype(F32), axis=1, keepdims=True)
-            out = out.astype(BF16)
-            o_refs[2 * half][:, cut] = out[:cells]
-            o_refs[2 * half + 1][:, cut] = out[cells:]
+            dotted = jnp.sum(out * qg_ref[1, :, cut].astype(F32), axis=1, keepdims=True)
+            o_ref[:, cut] = out.astype(BF16)
             stat = jnp.where(lane == head, best + jnp.log2(total), stat)
             stat = jnp.where(lane == HEADS + head, dotted, stat)
-        stat_ref[half] = stat.T[: stat_ref.shape[1]]
-
-
-def merged_stats(stat_ref, half, cells):
-    parts = [
-        frame_block(stat_ref, 0)[half],
-        pltpu.roll(frame_block(stat_ref, 1)[half], cells, 1),
-        frame_block(stat_ref, 2)[1 - half],
-        pltpu.roll(frame_block(stat_ref, 3)[1 - half], cells, 1),
-    ]
+        stats.append(stat)
+    if last:
+        whole = jnp.concatenate([first_ref[...]] + stats, axis=0)
+        stat_ref[...] = whole.T[: stat_ref.shape[0]]
+    else:
+        for i, stat in enumerate(stats):
+            stat_ref[i * cells : (i + 1) * cells] = stat
+
+
+def seen_from(stat, distance, cells):
+    if distance & 2:
+        stat = pltpu.roll(stat, 2 * cells, 1)
+    if distance & 1:
+        lane = lax.broadcasted_iota(jnp.int32, stat.shape, 1)
+        even = (lane < cells) | ((lane >= 2 * cells) & (lane < 3 * cells))
+        stat = jnp.where(even, pltpu.roll(stat, 3 * cells, 1), pltpu.roll(stat, cells, 1))
+    return stat
+
+
+def merged_stats(stat_refs, cells):
+    parts = [seen_from(ref[...], distance, cells) for distance, ref in enumerate(stat_refs)]
     top = functools.reduce(jnp.maximum, parts)
     shares = [jnp.exp2(part - top) for part in parts]
     total = functools.reduce(jnp.add, shares)
@@ -241,38 +248,31 @@
     return results, dq
 
 
-def backward_kernel(cols, grid_rows, sizes, cells, last, qg_ref, *refs):
+def backward_kernel(cols, grid_rows, sizes, cells, first, last, *refs):
     tile_count = grid_rows * len(cols)
-    kv_refs = refs[:tile_count]
-    rest = refs[tile_count:]
+    qg_refs = refs[:4]
+    kv_refs = refs[4 : 4 + tile_count]
+    rest = refs[4 + tile_count :]
+    if first:
+        stat_refs, rest = rest[:4], rest[4:]
+    else:
+        (lse_ref, delta_ref, dq_ref), rest = rest[:3], rest[3:]
     if last:
-        lse_ref, delta_ref, share_ref, dq_ref = rest[:4]
-        o_refs = rest[4:8]
-        dq_outs, out_ref = rest[8:12], rest[12]
-        col_refs = rest[13 : 13 + len(cols)]
-        key_buf, value_buf = rest[13 + len(cols) :]
-        lse, delta = lse_ref[...], delta_ref[...]
-        for head in range(HEADS):
-            cut = head_slice(head)
-            out = None
-            for d in range(4):
-                weight = share_ref[:, 4 * head + d : 4 * head + d + 1]
-                piece = o_refs[d][:, cut].astype(F32) * weight
-                out = piece if out is None else out + piece
-            out_ref[:, cut] = out.astype(BF16)
+        dq_outs, rest = rest[:4], rest[4:]
     else:
-        stat_ref, lse_ref, delta_ref, share_ref, dq_ref = rest[:5]
-        col_refs = rest[5 : 5 + len(cols)]
-        key_buf, value_buf = rest[5 + len(cols) :]
-        stats = [merged_stats(stat_ref, half, cells) for half in range(2)]
-        lse = jnp.concatenate([stats[0][0], stats[1][0]], axis=1)
-        delta = jnp.concatenate([stats[0][1], stats[1][1]], axis=1)
+        dq_out, rest = rest[0], rest[1:]
+    if first:
+        (lse_ref, delta_ref, share_ref), rest = rest[:3], rest[3:]
+        lse, delta, shares = merged_stats(stat_refs, cells)
         lse_ref[...] = lse
         delta_ref[...] = delta
-        shares = stats[0][2]
-        rows = [shares[d][head : head + 1] for head in range(HEADS) for d in range(4)]
+        rows = [shares[d][head : head + 1, : 2 * cells] for head in range(HEADS) for d in range(4)]
         wide = jnp.concatenate(rows + [jnp.zeros((DH - len(rows), 2 * cells), F32)], axis=0)
         share_ref[...] = wide.T[:cells]
+    else:
+        lse, delta = lse_ref[...], delta_ref[...]
+    col_refs = rest[: len(cols)]
+    key_buf, value_buf = rest[len(cols) :]
 
     span = grid_rows * cells
     for i, ref in enumerate(kv_refs):
@@ -281,9 +281,8 @@
     row_flags = [row == 2 for row in range(grid_rows)]
     for head in range(HEADS):
         cut = head_slice(head)
-        blocks = [frame_block(qg_ref, d) for d in range(4)]
-        queries = jnp.concatenate([block[0, :, cut] for block in blocks], axis=0)
-        grads = jnp.concatenate([block[1, :, cut] for block in blocks], axis=0)
+        queries = jnp.concatenate([ref[0, :, cut] for ref in qg_refs], axis=0)
+        grads = jnp.concatenate([ref[1, :, cut] for ref in qg_refs], axis=0)
         results, dq = gradient_blocks(
             cols, row_flags, sizes, key_buf.at[:, cut], value_buf.at[:, cut], queries, grads,
             lse[head : head + 1], delta[head : head + 1], span,
@@ -293,19 +292,26 @@
                 at = slice(row * cells, (row + 1) * cells)
                 ref[row, 0, :, cut] = dk[at].astype(BF16)
                 ref[row, 1, :, cut] = dv[at].astype(BF16)
+        if not first:
+            dq = dq + dq_ref[head]
         if last:
-            dq = ((dq + dq_ref[head]) * SCALE).T.astype(BF16)
+            dq = (dq * SCALE).T.astype(BF16)
             for i, ref in enumerate(dq_outs):
                 ref[:, cut] = dq[i * cells : (i + 1) * cells]
         else:
-            dq_ref[head] = dq
+            dq_out[head] = dq
 
 
 def finish_query_kernel(*refs):
-    dq_refs = refs[:4]
-    rope_ref, dq_out = refs[4:]
+    o_refs, dq_refs = refs[:4], refs[4:8]
+    share_ref, rope_ref, out_ref, dq_out = refs[8:]
     for head in range(HEADS):
         cut = head_slice(head)
+        outs = []
+        for d, o_ref in zip((0, 3, 2, 1), o_refs):
+            weight = share_ref[:, 4 * head + d : 4 * head + d + 1]
+            outs.append(o_ref[:, cut].astype(F32) * weight)
+        out_ref[:, cut] = functools.reduce(jnp.add, outs).astype(BF16)
         dq = functools.reduce(jnp.add, [ref[:, cut].astype(F32) for ref in dq_refs])
         dq_out[:, cut] = turn(dq, rope_ref[0], rope_ref[1], rope_ref[2], -1.0).astype(BF16)
 
@@ -373,10 +379,12 @@
     col_sides = side_pairs(sizes["wa"])
     with jax.named_scope("halo"):
         kv_rows = [kv] + [lax.ppermute(kv, "ha", pairs) for pairs in row_sides]
-        gathered = lax.all_gather(qg, "ta")
+        qg2 = other_frames(qg, 2)
+        qg1 = other_frames(qg, 1)
         tiles = []
         for block in kv_rows:
             tiles.append([block] + [lax.ppermute(block, "wa", pairs) for pairs in col_sides])
+        qg3 = other_frames(qg2, 1)
     grid_rows, grid_cols = 1 + len(row_sides), 1 + len(col_sides)
     flat_tiles = [tiles[row][col] for row in range(grid_rows) for col in range(grid_cols)]
     groups = {}
@@ -386,60 +394,64 @@
     groups = list(groups.items())
 
     key_count = len(flat_tiles) * cells
-    product = 2 * 4 * cells * key_count * DH * HEADS
+    product = 2 * cells * key_count * DH * HEADS
+
+    def forward(blocks, first):
+        count = len(blocks)
+        stat = (count * cells, DH) if first is None else (8, 4 * cells)
+        return call(
+            functools.partial(forward_kernel, groups, sizes, cells, count, first is not None),
+            (*[plain] * count, real(*stat)),
+            (*blocks, *flat_tiles) + (() if first is None else (first,)),
+            2 * product * count,
+            cells * key_count * HEADS * count,
+            [pltpu.VMEM((key_count, chan), BF16)] * 2,
+        )
 
     with jax.named_scope("attend"):
-        *parts, stat = call(
-            functools.partial(forward_kernel, groups, sizes, cells),
-            (*[plain] * 4, real(2, 8, 2 * cells)),
-            (gathered, *flat_tiles),
-            2 * product,
-            4 * cells * key_count * HEADS,
-            [pltpu.VMEM((key_count, chan), BF16)] * 2,
-        )
+        o0, o1, o2, first = forward((qg, qg1, qg2), None)
+        o3, stat = forward((qg3,), first)
     with jax.named_scope("merge"):
-        stats = lax.all_gather(stat, "ta")
-        outs = [parts[0]] + [other_frames(parts[d], d) for d in (1, 2, 3)]
-
+        stats = [stat] + [other_frames(stat, d) for d in (1, 2, 3)]
+        outs = [other_frames(o, d) for d, o in ((3, o3), (2, o2), (1, o1))]
+
+    queries = (qg, qg1, qg2, qg3)
     col_shape = jax.ShapeDtypeStruct((grid_rows, 2, cells, chan), BF16)
 
-    def gradients(which, last, extra_out, extra_in):
+    def gradients(which, carried):
         count = len(which)
+        first, last = which[-1] == grid_cols - 1, which[0] == 0
+        stat_outs = [real(HEADS, 4 * cells), real(HEADS, 4 * cells), real(cells, DH)]
         return call(
-            functools.partial(backward_kernel, which, grid_rows, sizes, cells, last),
-            (*extra_out, *[col_shape] * count),
-            (gathered, *[tiles[row][col] for col in which for row in range(grid_rows)], *extra_in),
-            5 * product * count // grid_cols,
+            functools.partial(backward_kernel, which, grid_rows, sizes, cells, first, last),
+            (
+                *([plain] * 4 if last else [real(HEADS, DH, 4 * cells)]),
+                *(stat_outs if first else []),
+                *[col_shape] * count,
+            ),
+            (*queries, *[tiles[row][col] for col in which for row in range(grid_rows)], *carried),
+            20 * product * count // grid_cols,
             4 * cells * key_count * HEADS * count // grid_cols,
             [pltpu.VMEM((count * grid_rows * cells, chan), BF16)] * 2,
         )
 
     with jax.named_scope("gradients"):
-        lse, delta, shares, dq, *sides = gradients(
-            tuple(range(1, grid_cols)),
-            False,
-            (
-                real(HEADS, 4 * cells),
-                real(HEADS, 4 * cells),
-                real(cells, DH),
-                real(HEADS, DH, 4 * cells),
-            ),
-            (stats,),
-        )
+        dq, lse, delta, shares, *sides = gradients(tuple(range(1, grid_cols)), stats)
         sides = [lax.ppermute(x, "wa", pairs) for x, pairs in zip(sides, col_sides)]
-        d0, d1, d2, d3, attended, own = gradients(
-            (0,), True, [plain] * 5, (lse, delta, shares, dq, *outs)
-        )
+        d0, d1, d2, d3, own = gradients((0,), (lse, delta, dq))
     with jax.named_scope("return"):
+        (d1, d2, d3), outs = lax.optimization_barrier(((d1, d2, d3), outs))
         col_parts = [own, *sides]
-        dqs = [d0] + [other_frames(x, d) for d, x in ((1, d1), (2, d2), (3, d3))]
+        dqs = [d0] + [other_frames(x, d) for d, x in ((3, d3), (2, d2), (1, d1))]
         row_parts = []
         for row, pairs in enumerate(row_sides, start=1):
             partial_sum = sum(x[row].astype(F32) for x in col_parts).astype(BF16)
             row_parts.append(lax.ppermute(partial_sum, "ha", pairs))
 
     with jax.named_scope("finish"):
-        grad_query = call(finish_query_kernel, plain, (*dqs, rope), 5 * product)
+        attended, grad_query = call(
+            finish_query_kernel, (plain, plain), (o0, *outs, *dqs, shares, rope), 10 * product
+        )
         grad_key, grad_value = call(
             functools.partial(finish_key_kernel, grid_cols, len(row_parts)),
             (plain, plain),

time: 74.8 us -> 54.6 us (0.73)
  blocking collectives: 27.4 us -> 0 us
  starting transfers between devices: 28.3 us -> 31.7 us
  waiting for transfers between devices: 5.69 us -> 9.05 us
  Pallas kernels: 11.7 us -> 12.5 us
    all_gather x2 -> x0, blocking collectives: 27.4 us -> none  [the longest x1 17 us: shards(): gathered = lax.all_gather(qg, 'ta')]
    ppermute x6 -> x12, starting transfers between devices: 7.09 us -> 15.3 us  [other_frames(): lax.ppermute(x, 'ta', [(i, i ^ distance) for i in range(sizes['ta'])])]
    ppermute x2, starting transfers between devices: 9.18 us -> 5.76 us  [shards(): sides = [lax.ppermute(x, 'wa', pairs) for x, pairs in zip(sides, col_sides)]]
    ppermute x6 -> x12, waiting for transfers between devices: 3.14 us -> 5.68 us  [other_frames(): lax.ppermute(x, 'ta', [(i, i ^ distance) for i in range(sizes['ta'])])]
    ppermute x4, waiting for transfers between devices: 0.01 us -> 2.4 us  [shards(): lax.ppermute(block, 'wa', pairs)]
    ppermute x1, starting transfers between devices: 1.27 us -> 0.33 us  [shards(): row_parts.append(lax.ppermute(partial_sum, 'ha', pairs))]
    pallas_call x6 -> x7, Pallas kernels: 11.7 us -> 12.5 us  [call(): pl.pallas_call(kernel, out_shape=out_shape, in_specs=[pl.BlockSpec(memory...]
  transfers between devices with their start and end apart: 14 -> 20, of which waited for: 4 -> 6; matrix products, arithmetic and copies ran while one was open for 0% -> 0% of each run, Pallas kernels for 8% -> 17%
where the time goes in v6:
time: 54.6 us; the launch traced here: 54 us
  starting transfers between devices  31.7 us (58%)
  Pallas kernels  12.5 us (23%)
  waiting for transfers between devices  9.05 us (17%)
  between operations  0.74 us (1%)
    ppermute x12, starting transfers between devices, other_frames(): lax.ppermute(x, 'ta', [(i, i ^ distance) for i in range(sizes['ta'])])  15.3 us
    pallas_call x7, Pallas kernels, call(): pl.pallas_call(kernel, out_shape=out_shape, in_specs=[pl.BlockSpec(memory...  12.5 us
    ppermute x4, starting transfers between devices, shards(): lax.ppermute(block, 'wa', pairs)  8.2 us
    ppermute x2, starting transfers between devices, shards(): sides = [lax.ppermute(x, 'wa', pairs) for x, pairs in zip(sides, col_sides)]  5.76 us
    ppermute x12, waiting for transfers between devices, other_frames(): lax.ppermute(x, 'ta', [(i, i ^ distance) for i in range(sizes['ta'])])  5.68 us
    ppermute x4, waiting for transfers between devices, shards(): lax.ppermute(block, 'wa', pairs)  2.4 us
    ppermute x1, starting transfers between devices, shards(): kv_rows = [kv] + [lax.ppermute(kv, 'ha', pairs) for pairs in row_sides]  2.11 us
  transfers between devices with their start and end apart: 20, of which 6 were waited for; matrix products, arithmetic and copies ran while one was open for 0% of the time, Pallas kernels for 17%

profile of v6, /device:TPU:1, one launch (start us, length us, event | category | flops | bytes accessed | tf_op | source)
XLA Modules:
  0.0 54.0 jit_solution(9239981344777723285)
XLA Ops:
  0.6 1.3 %rotate.1 = (bf16[2,192,256]{2,1,0:T(8,128)(2,1)S(1)}, bf16[2,192,256]{2,1,0:T(8,128)(2,1)S(1)}, f32[3,192,128]{2,1,0:T(8,128)S(1)}) custom-call(bf16[192,256]{1,0:T(8,128)(2,1)} %bitcast.10, bf16[192,256]{1,0:T(8,128)(2,1)} %bitcast.11, bf16[192,256]{1,0:T(8,128)(2,1)} %bitcast.12, bf16[192,256]{1,0:T(8,128)(2,1)} %bitcast.13, ...), custom_call_target="tpu_custom_call" | custom-call | bytes 1179648 | tf_op jit(solution)/shard_map/rotate/pallas_call | solution.py:339
  1.9 2.1 %collective-permute-start.4 = (bf16[2,192,256]{2,1,0:T(8,128)(2,1)S(1)}, bf16[2,192,256]{2,1,0:T(8,128)(2,1)S(1)}, u32[]{:S(2)}, u32[]{:S(2)}) collective-permute-start(bf16[2,192,256]{2,1,0:T(8,128)(2,1)S(1)} %get-tuple-element.35.refs_3_.refs_1_.refs_4_), channel_id=1, source_target_pairs={{0,4},{4,0},{1,5},{5,1},{2,6},{6,2},{3,7},{7,3},{8,12},{12,8},{9,1... | collective-permute-start | bytes 589832 | tf_op jit(solution)/shard_map/halo/ppermute | solution.py:381
  4.0 2.3 %collective-permute-start.1 = (bf16[2,192,256]{2,1,0:T(8,128)(2,1)S(1)}, bf16[2,192,256]{2,1,0:T(8,128)(2,1)S(1)}, u32[]{:S(2)}, u32[]{:S(2)}) collective-permute-start(bf16[2,192,256]{2,1,0:T(8,128)(2,1)S(1)} %get-tuple-element.34.refs_0_), channel_id=1, source_target_pairs={{0,16},{8,24},{16,0},{24,8},{1,17},{9,25},{17,1},{25,9},{2,18},{10... | collective-permute-start | bytes 589832 | tf_op jit(solution)/shard_map/halo/ppermute | solution.py:376
  6.3 1.3 %collective-permute-start = (bf16[2,192,256]{2,1,0:T(8,128)(2,1)S(1)}, bf16[2,192,256]{2,1,0:T(8,128)(2,1)S(1)}, u32[]{:S(2)}, u32[]{:S(2)}) collective-permute-start(bf16[2,192,256]{2,1,0:T(8,128)(2,1)S(1)} %get-tuple-element.34.refs_0_), channel_id=1, source_target_pairs={{0,8},{8,0},{16,24},{24,16},{1,9},{9,1},{17,25},{25,17},{2,10},{10... | collective-permute-start | bytes 589832 | tf_op jit(solution)/shard_map/halo/ppermute | solution.py:376
  7.6 4.5 %collective-permute-start.3 = (bf16[2,192,256]{2,1,0:T(8,128)(2,1)S(1)}, bf16[2,192,256]{2,1,0:T(8,128)(2,1)S(1)}, u32[]{:S(2)}, u32[]{:S(2)}) collective-permute-start(bf16[2,192,256]{2,1,0:T(8,128)(2,1)S(1)} %get-tuple-element.35.refs_3_.refs_1_.refs_4_), channel_id=1, source_target_pairs={{0,0},{1,2},{2,1},{3,3},{4,4},{5,6},{6,5},{7,7},{8,8},{9,10},{10,9... | collective-permute-start | bytes 589832 | tf_op jit(solution)/shard_map/halo/ppermute | solution.py:386
  12.2 0.1 collective-permute-start.2
  12.2 0.0 collective-permute-done.4.refs_6_.refs_4_.refs_5_
  12.2 1.9 %collective-permute-start.6 = (bf16[2,192,256]{2,1,0:T(8,128)(2,1)S(1)}, bf16[2,192,256]{2,1,0:T(8,128)(2,1)S(1)}, u32[]{:S(2)}, u32[]{:S(2)}) collective-permute-start(bf16[2,192,256]{2,1,0:T(8,128)(2,1)S(1)} %collective-permute-done.4.refs_6_.refs_4_.refs_5_), channel_id=1, source_target_pairs={{0,0},{1,2},{2,1},{3,3},{4,4},{5,6},{6,5},{7,7},{8,8},{9,10},{10,9... | collective-permute-start | bytes 589832 | tf_op jit(solution)/shard_map/halo/ppermute | solution.py:386
  14.2 0.7 %collective-permute-done.1.refs_2_ = bf16[2,192,256]{2,1,0:T(8,128)(2,1)S(1)} collective-permute-done((bf16[2,192,256]{2,1,0:T(8,128)(2,1)S(1)}, bf16[2,192,256]{2,1,0:T(8,128)(2,1)S(1)}, u32[]{:S(2)}, u32[]{:S(2)}) %collective-permute-start.1) | collective-permute-done | bytes 196640 | tf_op jit(solution)/shard_map/halo/ppermute | solution.py:376
  14.9 1.7 %collective-permute-start.5 = (bf16[2,192,256]{2,1,0:T(8,128)(2,1)S(1)}, bf16[2,192,256]{2,1,0:T(8,128)(2,1)S(1)}, u32[]{:S(2)}, u32[]{:S(2)}) collective-permute-start(bf16[2,192,256]{2,1,0:T(8,128)(2,1)S(1)} %collective-permute-done.4.refs_6_.refs_4_.refs_5_), channel_id=1, source_target_pairs={{0,1},{1,0},{2,3},{3,2},{4,5},{5,4},{6,7},{7,6},{8,9},{9,8},{10,11... | collective-permute-start | bytes 589832 | tf_op jit(solution)/shard_map/halo/ppermute | solution.py:386
  16.5 0.0 collective-permute-done.refs_1_
  16.5 0.3 collective-permute-start.7
  16.8 0.0 collective-permute-done.3.refs_5_.refs_3_.refs_6_
  16.8 0.0 collective-permute-done.2.refs_4_.refs_2_
  16.8 2.4 %collective-permute-done.6.refs_8_.refs_6_.refs_7_ = bf16[2,192,256]{2,1,0:T(8,128)(2,1)S(1)} collective-permute-done((bf16[2,192,256]{2,1,0:T(8,128)(2,1)S(1)}, bf16[2,192,256]{2,1,0:T(8,128)(2,1)S(1)}, u32[]{:S(2)}, u32[]{:S(2)}) %collective-permute-start.6) | collective-permute-done | bytes 196640 | tf_op jit(solution)/shard_map/halo/ppermute | solution.py:386
  19.2 0.0 collective-permute-done.5.refs_7_.refs_5_
  19.2 3.2 %attend.2 = (bf16[192,256]{1,0:T(8,128)(2,1)S(1)}, bf16[192,256]{1,0:T(8,128)(2,1)S(1)}, bf16[192,256]{1,0:T(8,128)(2,1)S(1)}, f32[576,128]{1,0:T(8,128)S(1)}) custom-call(bf16[2,192,256]{2,1,0:T(8,128)(2,1)S(1)} %get-tuple-element.34.refs_0_, bf16[2,192,256]{2,1,0:T(8,128)(2,1)S(1)} %collective-permute-done.refs_1_, ...), custom_call_target="tpu_custom_call" | custom-call | flops 5435817984 | bytes 2359296 | tf_op jit(solution)/shard_map/attend/pallas_call | solution.py:339
  22.4 0.4 collective-permute-done.7.refs_0_.refs_3_
  22.9 1.3 %attend.3 = (bf16[192,256]{1,0:T(8,128)(2,1)S(1)}, f32[8,768]{1,0:T(8,128)S(1)}) custom-call(bf16[2,192,256]{2,1,0:T(8,128)(2,1)S(1)} %collective-permute-done.7.refs_0_.refs_3_, bf16[2,192,256]{2,1,0:T(8,128)(2,1)S(1)} %get-tuple-element.35.refs_3_.refs_1_.refs_4_, bf16[2,192,256]{2,1,0:T(8,128)(2,1)S(1)} %collective-permute-done.2.refs_4_.refs_2_, ...), custom_call_target="tpu_custom_call" | custom-call | flops 1811939328 | bytes 1794048 | tf_op jit(solution)/shard_map/attend/pallas_call | solution.py:339
  24.1 3.3 %collective-permute-start.10 = (f32[8,768]{1,0:T(8,128)S(1)}, f32[8,768]{1,0:T(8,128)S(1)}, u32[]{:S(2)}, u32[]{:S(2)}) collective-permute-start(f32[8,768]{1,0:T(8,128)S(1)} %get-tuple-element.38.refs_8_), channel_id=1, source_target_pairs={{0,24},{8,16},{16,8},{24,0},{1,25},{9,17},{17,9},{25,1},{2,26},{10... | collective-permute-start | bytes 73736 | tf_op jit(solution)/shard_map/merge/ppermute | solution.py:376
  27.5 0.0 collective-permute-start.9
  27.5 0.4 collective-permute-start.8
  27.9 2.0 %collective-permute-start.12 = (bf16[192,256]{1,0:T(8,128)(2,1)S(1)}, bf16[192,256]{1,0:T(8,128)(2,1)S(1)}, u32[]{:S(2)}, u32[]{:S(2)}) collective-permute-start(bf16[192,256]{1,0:T(8,128)(2,1)S(1)} %get-tuple-element.46), channel_id=1, source_target_pairs={{0,16},{8,24},{16,0},{24,8},{1,17},{9,25},{17,1},{25,9},{2,18},{10... | collective-permute-start | bytes 294920 | tf_op jit(solution)/shard_map/merge/ppermute | solution.py:376
  29.9 1.5 %collective-permute-start.13 = (bf16[192,256]{1,0:T(8,128)(2,1)S(1)}, bf16[192,256]{1,0:T(8,128)(2,1)S(1)}, u32[]{:S(2)}, u32[]{:S(2)}) collective-permute-start(bf16[192,256]{1,0:T(8,128)(2,1)S(1)} %get-tuple-element.47), channel_id=1, source_target_pairs={{0,8},{8,0},{16,24},{24,16},{1,9},{9,1},{17,25},{25,17},{2,10},{10... | collective-permute-start | bytes 294920 | tf_op jit(solution)/shard_map/merge/ppermute | solution.py:376
  31.3 0.0 collective-permute-done.10.refs_11_
  31.3 0.6 %collective-permute-start.11 = (bf16[192,256]{1,0:T(8,128)(2,1)S(1)}, bf16[192,256]{1,0:T(8,128)(2,1)S(1)}, u32[]{:S(2)}, u32[]{:S(2)}) collective-permute-start(bf16[192,256]{1,0:T(8,128)(2,1)S(1)} %get-tuple-element.45), channel_id=1, source_target_pairs={{0,24},{8,16},{16,8},{24,0},{1,25},{9,17},{17,9},{25,1},{2,26},{10... | collective-permute-start | bytes 294920 | tf_op jit(solution)/shard_map/merge/ppermute | solution.py:376
  32.0 0.0 collective-permute-done.9.refs_10_
  32.0 0.0 collective-permute-done.8.refs_9_
  32.0 3.1 %gradients.2 = (f32[2,128,768]{2,1,0:T(8,128)S(1)}, f32[2,768]{1,0:T(2,128)S(1)}, f32[2,768]{1,0:T(2,128)S(1)}, f32[192,128]{1,0:T(8,128)S(1)}, bf16[2,2,192,256...) custom-call(bf16[2,192,256]{2,1,0:T(8,128)(2,1)S(1)} %get-tuple-element.34.refs_0_, ...), custom_call_target="tpu_custom_call" | custom-call | flops 12079595520 | bytes 3354624 | tf_op jit(solution)/shard_map/gradients/pallas_call | solution.py:339
  35.1 2.7 %collective-permute-start.17 = (bf16[2,2,192,256]{3,2,1,0:T(8,128)(2,1)S(1)}, bf16[2,2,192,256]{3,2,1,0:T(8,128)(2,1)S(1)}, u32[]{:S(2)}, u32[]{:S(2)}) collective-permute-start(bf16[2,2,192,256]{3,2,1,0:T(8,128)(2,1)S(1)} %get-tuple-element.60), channel_id=1, source_target_pairs={{0,1},{1,0},{2,3},{3,2},{4,5},{5,4},{6,7},{7,6},{8,9},{9,8},{10,11... | collective-permute-start | bytes 1179656 | tf_op jit(solution)/shard_map/gradients/ppermute | solution.py:440
  37.8 3.1 %collective-permute-start.18 = (bf16[2,2,192,256]{3,2,1,0:T(8,128)(2,1)S(1)}, bf16[2,2,192,256]{3,2,1,0:T(8,128)(2,1)S(1)}, u32[]{:S(2)}, u32[]{:S(2)}) collective-permute-start(bf16[2,2,192,256]{3,2,1,0:T(8,128)(2,1)S(1)} %get-tuple-element.61), channel_id=1, source_target_pairs={{0,0},{1,2},{2,1},{3,3},{4,4},{5,6},{6,5},{7,7},{8,8},{9,10},{10,9... | collective-permute-start | bytes 1179656 | tf_op jit(solution)/shard_map/gradients/ppermute | solution.py:440
  40.9 1.7 %gradients.3 = (bf16[192,256]{1,0:T(8,128)(2,1)S(1)}, bf16[192,256]{1,0:T(8,128)(2,1)S(1)}, bf16[192,256]{1,0:T(8,128)(2,1)S(1)}, bf16[192,256]{1,0:T(8,128)(2,1)S(1)}, bf16[2,2,192,256]{3,2,1,0:T(8,128)(2,1)S(1)}) custom-call(bf16[2,192,256]{2,1,0:T(8,128)(2,1)S(1)} %get-tuple-element.34.refs_0_, bf16[2,192,256]{2,1,0:T(8,128)(2,1)S(1)} %collective-permute-done.refs_1_, ...), custom_call_target="tpu_custom_call" | custom-call | flops 6039797760 | bytes 2764800 | tf_op jit(solution)/shard_map/gradients/pallas_call | solution.py:339
  42.6 0.0 collective-permute-done.12.refs_2_
  42.6 0.0 collective-permute-done.13.refs_3_
  42.6 0.0 collective-permute-done.11.refs_1_
  42.6 2.5 %collective-permute-start.14 = (bf16[192,256]{1,0:T(8,128)(2,1)S(1)}, bf16[192,256]{1,0:T(8,128)(2,1)S(1)}, u32[]{:S(2)}, u32[]{:S(2)}) collective-permute-start(bf16[192,256]{1,0:T(8,128)(2,1)S(1)} %get-tuple-element.52), channel_id=1, source_target_pairs={{0,24},{8,16},{16,8},{24,0},{1,25},{9,17},{17,9},{25,1},{2,26},{10... | collective-permute-start | bytes 294920 | tf_op jit(solution)/shard_map/return/ppermute | solution.py:376
  45.1 0.0 collective-permute-start.15
  45.1 1.1 %collective-permute-start.16 = (bf16[192,256]{1,0:T(8,128)(2,1)S(1)}, bf16[192,256]{1,0:T(8,128)(2,1)S(1)}, u32[]{:S(2)}, u32[]{:S(2)}) collective-permute-start(bf16[192,256]{1,0:T(8,128)(2,1)S(1)} %get-tuple-element.54), channel_id=1, source_target_pairs={{0,8},{8,0},{16,24},{24,16},{1,9},{9,1},{17,25},{25,17},{2,10},{10... | collective-permute-start | bytes 294920 | tf_op jit(solution)/shard_map/return/ppermute | solution.py:376
  46.2 0.0 collective-permute-done.17.refs_1_
  46.2 1.0 %collective-permute-done.18.refs_2_ = bf16[2,2,192,256]{3,2,1,0:T(8,128)(2,1)S(1)} collective-permute-done((bf16[2,2,192,256]{3,2,1,0:T(8,128)(2,1)S(1)}, bf16[2,2,192,256]{3,2,1,0:T(8,128)(2,1)S(1)}, u32[]{:S(2)}, u32[]{:S(2)}) %collective-permute-start.18) | collective-permute-done | bytes 393248 | tf_op jit(solution)/shard_map/gradients/ppermute | solution.py:440
  47.2 0.1 fusion
  47.3 0.3 collective-permute-start.19
  47.6 1.2 %collective-permute-done.14.refs_5_ = bf16[192,256]{1,0:T(8,128)(2,1)S(1)} collective-permute-done((bf16[192,256]{1,0:T(8,128)(2,1)S(1)}, bf16[192,256]{1,0:T(8,128)(2,1)S(1)}, u32[]{:S(2)}, u32[]{:S(2)}) %collective-permute-start.14) | collective-permute-done | bytes 98336 | tf_op jit(solution)/shard_map/return/ppermute | solution.py:376
  48.8 3.3 %collective-permute-done.15.refs_6_ = bf16[192,256]{1,0:T(8,128)(2,1)S(1)} collective-permute-done((bf16[192,256]{1,0:T(8,128)(2,1)S(1)}, bf16[192,256]{1,0:T(8,128)(2,1)S(1)}, u32[]{:S(2)}, u32[]{:S(2)}) %collective-permute-start.15) | collective-permute-done | bytes 98336 | tf_op jit(solution)/shard_map/return/ppermute | solution.py:376
  52.1 0.0 collective-permute-done.16.refs_7_
  52.1 1.0 %finish.2 = (bf16[192,256]{1,0:T(8,128)(2,1)}, bf16[192,256]{1,0:T(8,128)(2,1)}) custom-call(bf16[192,256]{1,0:T(8,128)(2,1)S(1)} %get-tuple-element.36.refs_0_, bf16[192,256]{1,0:T(8,128)(2,1)S(1)} %collective-permute-done.11.refs_1_, bf16[192,256]{1,0:T(8,128)(2,1)S(1)} %collective-permute-done.12.refs_2_, ...), custom_call_target="tpu_custom_call" | custom-call | flops 9059696640 | bytes 1376256 | tf_op jit(solution)/shard_map/finish/pallas_call | solution.py:339
  53.2 0.0 collective-permute-done.19.refs_3_
  53.2 0.9 %finish.3 = (bf16[192,256]{1,0:T(8,128)(2,1)}, bf16[192,256]{1,0:T(8,128)(2,1)}) custom-call(bf16[2,2,192,256]{3,2,1,0:T(8,128)(2,1)S(1)} %get-tuple-element.59.refs_0_, bf16[2,2,192,256]{3,2,1,0:T(8,128)(2,1)S(1)} %collective-permute-done.17.refs_1_, bf16[2,2,192,256]{3,2,1,0:T(8,128)(2,1)S(1)} %collective-permute-done.18.refs_2_, ...), custom_call_target="tpu_custom_call" | custom-call | bytes 1867776 | tf_op jit(solution)/shard_map/finish/pallas_call | solution.py:339
Async XLA Ops:
  1.9 10.3 %collective-permute-start.4 = (bf16[2,192,256]{2,1,0:T(8,128)(2,1)S(1)}, bf16[2,192,256]{2,1,0:T(8,128)(2,1)S(1)}, u32[]{:S(2)}, u32[]{:S(2)}) collective-permute-start(bf16[2,192,256]{2,1,0:T(8,128)(2,1)S(1)} %get-tuple-element.35.refs_3_.refs_1_.refs_4_), channel_id=1, source_target_pairs={{0,4},{4,0},{1,5},{5,1},{2,6},{6,2},{3,7},{7,3},{8,12},{12,8},{9,1... | collective-permute-start | bytes 589832 | tf_op jit(solution)/shard_map/halo/ppermute | solution.py:381
  4.0 10.9 %collective-permute-start.1 = (bf16[2,192,256]{2,1,0:T(8,128)(2,1)S(1)}, bf16[2,192,256]{2,1,0:T(8,128)(2,1)S(1)}, u32[]{:S(2)}, u32[]{:S(2)}) collective-permute-start(bf16[2,192,256]{2,1,0:T(8,128)(2,1)S(1)} %get-tuple-element.34.refs_0_), channel_id=1, source_target_pairs={{0,16},{8,24},{16,0},{24,8},{1,17},{9,25},{17,1},{25,9},{2,18},{10... | collective-permute-start | bytes 589832 | tf_op jit(solution)/shard_map/halo/ppermute | solution.py:376
  6.3 10.2 %collective-permute-start = (bf16[2,192,256]{2,1,0:T(8,128)(2,1)S(1)}, bf16[2,192,256]{2,1,0:T(8,128)(2,1)S(1)}, u32[]{:S(2)}, u32[]{:S(2)}) collective-permute-start(bf16[2,192,256]{2,1,0:T(8,128)(2,1)S(1)} %get-tuple-element.34.refs_0_), channel_id=1, source_target_pairs={{0,8},{8,0},{16,24},{24,16},{1,9},{9,1},{17,25},{25,17},{2,10},{10... | collective-permute-start | bytes 589832 | tf_op jit(solution)/shard_map/halo/ppermute | solution.py:376
  7.6 9.2 %collective-permute-start.3 = (bf16[2,192,256]{2,1,0:T(8,128)(2,1)S(1)}, bf16[2,192,256]{2,1,0:T(8,128)(2,1)S(1)}, u32[]{:S(2)}, u32[]{:S(2)}) collective-permute-start(bf16[2,192,256]{2,1,0:T(8,128)(2,1)S(1)} %get-tuple-element.35.refs_3_.refs_1_.refs_4_), channel_id=1, source_target_pairs={{0,0},{1,2},{2,1},{3,3},{4,4},{5,6},{6,5},{7,7},{8,8},{9,10},{10,9... | collective-permute-start | bytes 589832 | tf_op jit(solution)/shard_map/halo/ppermute | solution.py:386
  12.2 4.7 %collective-permute-start.2 = (bf16[2,192,256]{2,1,0:T(8,128)(2,1)S(1)}, bf16[2,192,256]{2,1,0:T(8,128)(2,1)S(1)}, u32[]{:S(2)}, u32[]{:S(2)}) collective-permute-start(bf16[2,192,256]{2,1,0:T(8,128)(2,1)S(1)} %get-tuple-element.35.refs_3_.refs_1_.refs_4_), channel_id=1, source_target_pairs={{0,1},{1,0},{2,3},{3,2},{4,5},{5,4},{6,7},{7,6},{8,9},{9,8},{10,11... | collective-permute-start | bytes 589832 | tf_op jit(solution)/shard_map/halo/ppermute | solution.py:386
  12.2 7.0 %collective-permute-start.6 = (bf16[2,192,256]{2,1,0:T(8,128)(2,1)S(1)}, bf16[2,192,256]{2,1,0:T(8,128)(2,1)S(1)}, u32[]{:S(2)}, u32[]{:S(2)}) collective-permute-start(bf16[2,192,256]{2,1,0:T(8,128)(2,1)S(1)} %collective-permute-done.4.refs_6_.refs_4_.refs_5_), channel_id=1, source_target_pairs={{0,0},{1,2},{2,1},{3,3},{4,4},{5,6},{6,5},{7,7},{8,8},{9,10},{10,9... | collective-permute-start | bytes 589832 | tf_op jit(solution)/shard_map/halo/ppermute | solution.py:386
  14.9 4.4 %collective-permute-start.5 = (bf16[2,192,256]{2,1,0:T(8,128)(2,1)S(1)}, bf16[2,192,256]{2,1,0:T(8,128)(2,1)S(1)}, u32[]{:S(2)}, u32[]{:S(2)}) collective-permute-start(bf16[2,192,256]{2,1,0:T(8,128)(2,1)S(1)} %collective-permute-done.4.refs_6_.refs_4_.refs_5_), channel_id=1, source_target_pairs={{0,1},{1,0},{2,3},{3,2},{4,5},{5,4},{6,7},{7,6},{8,9},{9,8},{10,11... | collective-permute-start | bytes 589832 | tf_op jit(solution)/shard_map/halo/ppermute | solution.py:386
  16.5 6.3 %collective-permute-start.7 = (bf16[2,192,256]{2,1,0:T(8,128)(2,1)S(1)}, bf16[2,192,256]{2,1,0:T(8,128)(2,1)S(1)}, u32[]{:S(2)}, u32[]{:S(2)}) collective-permute-start(bf16[2,192,256]{2,1,0:T(8,128)(2,1)S(1)} %collective-permute-done.1.refs_2_), channel_id=1, source_target_pairs={{0,8},{8,0},{16,24},{24,16},{1,9},{9,1},{17,25},{25,17},{2,10},{10... | collective-permute-start | bytes 589832 | tf_op jit(solution)/shard_map/halo/ppermute | solution.py:376
  24.1 7.2 %collective-permute-start.10 = (f32[8,768]{1,0:T(8,128)S(1)}, f32[8,768]{1,0:T(8,128)S(1)}, u32[]{:S(2)}, u32[]{:S(2)}) collective-permute-start(f32[8,768]{1,0:T(8,128)S(1)} %get-tuple-element.38.refs_8_), channel_id=1, source_target_pairs={{0,24},{8,16},{16,8},{24,0},{1,25},{9,17},{17,9},{25,1},{2,26},{10... | collective-permute-start | bytes 73736 | tf_op jit(solution)/shard_map/merge/ppermute | solution.py:376
  27.5 4.5 %collective-permute-start.9 = (f32[8,768]{1,0:T(8,128)S(1)}, f32[8,768]{1,0:T(8,128)S(1)}, u32[]{:S(2)}, u32[]{:S(2)}) collective-permute-start(f32[8,768]{1,0:T(8,128)S(1)} %get-tuple-element.38.refs_8_), channel_id=1, source_target_pairs={{0,16},{8,24},{16,0},{24,8},{1,17},{9,25},{17,1},{25,9},{2,18},{10... | collective-permute-start | bytes 73736 | tf_op jit(solution)/shard_map/merge/ppermute | solution.py:376
  27.5 4.5 %collective-permute-start.8 = (f32[8,768]{1,0:T(8,128)S(1)}, f32[8,768]{1,0:T(8,128)S(1)}, u32[]{:S(2)}, u32[]{:S(2)}) collective-permute-start(f32[8,768]{1,0:T(8,128)S(1)} %get-tuple-element.38.refs_8_), channel_id=1, source_target_pairs={{0,8},{8,0},{16,24},{24,16},{1,9},{9,1},{17,25},{25,17},{2,10},{10... | collective-permute-start | bytes 73736 | tf_op jit(solution)/shard_map/merge/ppermute | solution.py:376
  27.9 14.7 %collective-permute-start.12 = (bf16[192,256]{1,0:T(8,128)(2,1)S(1)}, bf16[192,256]{1,0:T(8,128)(2,1)S(1)}, u32[]{:S(2)}, u32[]{:S(2)}) collective-permute-start(bf16[192,256]{1,0:T(8,128)(2,1)S(1)} %get-tuple-element.46), channel_id=1, source_target_pairs={{0,16},{8,24},{16,0},{24,8},{1,17},{9,25},{17,1},{25,9},{2,18},{10... | collective-permute-start | bytes 294920 | tf_op jit(solution)/shard_map/merge/ppermute | solution.py:376
  29.9 12.7 %collective-permute-start.13 = (bf16[192,256]{1,0:T(8,128)(2,1)S(1)}, bf16[192,256]{1,0:T(8,128)(2,1)S(1)}, u32[]{:S(2)}, u32[]{:S(2)}) collective-permute-start(bf16[192,256]{1,0:T(8,128)(2,1)S(1)} %get-tuple-element.47), channel_id=1, source_target_pairs={{0,8},{8,0},{16,24},{24,16},{1,9},{9,1},{17,25},{25,17},{2,10},{10... | collective-permute-start | bytes 294920 | tf_op jit(solution)/shard_map/merge/ppermute | solution.py:376
  31.3 11.3 %collective-permute-start.11 = (bf16[192,256]{1,0:T(8,128)(2,1)S(1)}, bf16[192,256]{1,0:T(8,128)(2,1)S(1)}, u32[]{:S(2)}, u32[]{:S(2)}) collective-permute-start(bf16[192,256]{1,0:T(8,128)(2,1)S(1)} %get-tuple-element.45), channel_id=1, source_target_pairs={{0,24},{8,16},{16,8},{24,0},{1,25},{9,17},{17,9},{25,1},{2,26},{10... | collective-permute-start | bytes 294920 | tf_op jit(solution)/shard_map/merge/ppermute | solution.py:376
  35.1 11.1 %collective-permute-start.17 = (bf16[2,2,192,256]{3,2,1,0:T(8,128)(2,1)S(1)}, bf16[2,2,192,256]{3,2,1,0:T(8,128)(2,1)S(1)}, u32[]{:S(2)}, u32[]{:S(2)}) collective-permute-start(bf16[2,2,192,256]{3,2,1,0:T(8,128)(2,1)S(1)} %get-tuple-element.60), channel_id=1, source_target_pairs={{0,1},{1,0},{2,3},{3,2},{4,5},{5,4},{6,7},{7,6},{8,9},{9,8},{10,11... | collective-permute-start | bytes 1179656 | tf_op jit(solution)/shard_map/gradients/ppermute | solution.py:440
  37.8 9.4 %collective-permute-start.18 = (bf16[2,2,192,256]{3,2,1,0:T(8,128)(2,1)S(1)}, bf16[2,2,192,256]{3,2,1,0:T(8,128)(2,1)S(1)}, u32[]{:S(2)}, u32[]{:S(2)}) collective-permute-start(bf16[2,2,192,256]{3,2,1,0:T(8,128)(2,1)S(1)} %get-tuple-element.61), channel_id=1, source_target_pairs={{0,0},{1,2},{2,1},{3,3},{4,4},{5,6},{6,5},{7,7},{8,8},{9,10},{10,9... | collective-permute-start | bytes 1179656 | tf_op jit(solution)/shard_map/gradients/ppermute | solution.py:440
  42.6 6.2 %collective-permute-start.14 = (bf16[192,256]{1,0:T(8,128)(2,1)S(1)}, bf16[192,256]{1,0:T(8,128)(2,1)S(1)}, u32[]{:S(2)}, u32[]{:S(2)}) collective-permute-start(bf16[192,256]{1,0:T(8,128)(2,1)S(1)} %get-tuple-element.52), channel_id=1, source_target_pairs={{0,24},{8,16},{16,8},{24,0},{1,25},{9,17},{17,9},{25,1},{2,26},{10... | collective-permute-start | bytes 294920 | tf_op jit(solution)/shard_map/return/ppermute | solution.py:376
  45.1 7.0 %collective-permute-start.15 = (bf16[192,256]{1,0:T(8,128)(2,1)S(1)}, bf16[192,256]{1,0:T(8,128)(2,1)S(1)}, u32[]{:S(2)}, u32[]{:S(2)}) collective-permute-start(bf16[192,256]{1,0:T(8,128)(2,1)S(1)} %get-tuple-element.53), channel_id=1, source_target_pairs={{0,16},{8,24},{16,0},{24,8},{1,17},{9,25},{17,1},{25,9},{2,18},{10... | collective-permute-start | bytes 294920 | tf_op jit(solution)/shard_map/return/ppermute | solution.py:376
  45.1 7.0 %collective-permute-start.16 = (bf16[192,256]{1,0:T(8,128)(2,1)S(1)}, bf16[192,256]{1,0:T(8,128)(2,1)S(1)}, u32[]{:S(2)}, u32[]{:S(2)}) collective-permute-start(bf16[192,256]{1,0:T(8,128)(2,1)S(1)} %get-tuple-element.54), channel_id=1, source_target_pairs={{0,8},{8,0},{16,24},{24,16},{1,9},{9,1},{17,25},{25,17},{2,10},{10... | collective-permute-start | bytes 294920 | tf_op jit(solution)/shard_map/return/ppermute | solution.py:376
  47.3 5.9 %collective-permute-start.19 = (bf16[2,192,256]{2,1,0:T(8,128)(2,1)S(1)}, bf16[2,192,256]{2,1,0:T(8,128)(2,1)S(1)}, u32[]{:S(2)}, u32[]{:S(2)}) collective-permute-start(bf16[2,192,256]{2,1,0:T(8,128)(2,1)S(1)} %fusion), channel_id=1, source_target_pairs={{0,4},{4,0},{1,5},{5,1},{2,6},{6,2},{3,7},{7,3},{8,12},{12,8},{9,1... | collective-permute-start | bytes 589832 | tf_op jit(solution)/shard_map/return/ppermute | solution.py:449

commit v7 on v6

--- a/solution.py
+++ b/solution.py
@@ -414,6 +414,7 @@
     with jax.named_scope("merge"):
         stats = [stat] + [other_frames(stat, d) for d in (1, 2, 3)]
         outs = [other_frames(o, d) for d, o in ((3, o3), (2, o2), (1, o1))]
+        stats, outs[1:] = lax.optimization_barrier((stats, outs[1:]))
 
     queries = (qg, qg1, qg2, qg3)
     col_shape = jax.ShapeDtypeStruct((grid_rows, 2, cells, chan), BF16)

time: 54.6 us -> 54 us (0.989)
  starting transfers between devices: 31.7 us -> 30.7 us
  waiting for transfers between devices: 9.05 us -> 9.9 us
    ppermute x12, waiting for transfers between devices: 5.68 us -> 6.51 us  [other_frames(): lax.ppermute(x, 'ta', [(i, i ^ distance) for i in range(sizes['ta'])])]
  transfers between devices with their start and end apart: 20 -> 20, of which waited for: 6 -> 6; matrix products, arithmetic and copies ran while one was open for 0% -> 0% of each run, Pallas kernels for 17% -> 19%
where the time goes in v7:
time: 54 us; the launch traced here: 53.9 us
  starting transfers between devices  30.7 us (57%)
  Pallas kernels  12.5 us (23%)
  waiting for transfers between devices  9.9 us (18%)
  between operations  0.74 us (1%)
    ppermute x12, starting transfers between devices, other_frames(): lax.ppermute(x, 'ta', [(i, i ^ distance) for i in range(sizes['ta'])])  14.8 us
    pallas_call x7, Pallas kernels, call(): pl.pallas_call(kernel, out_shape=out_shape, in_specs=[pl.BlockSpec(memory...  12.5 us
    ppermute x4, starting transfers between devices, shards(): lax.ppermute(block, 'wa', pairs)  8.2 us
    ppermute x12, waiting for transfers between devices, other_frames(): lax.ppermute(x, 'ta', [(i, i ^ distance) for i in range(sizes['ta'])])  6.51 us
    ppermute x2, starting transfers between devices, shards(): sides = [lax.ppermute(x, 'wa', pairs) for x, pairs in zip(sides, col_sides)]  5.23 us
    ppermute x4, waiting for transfers between devices, shards(): lax.ppermute(block, 'wa', pairs)  2.4 us
    ppermute x1, starting transfers between devices, shards(): kv_rows = [kv] + [lax.ppermute(kv, 'ha', pairs) for pairs in row_sides]  2.11 us
  transfers between devices with their start and end apart: 20, of which 6 were waited for; matrix products, arithmetic and copies ran while one was open for 0% of the time, Pallas kernels for 19%

profile of v7, /device:TPU:1, one launch (start us, length us, event | category | flops | bytes accessed | tf_op | source)
XLA Modules:
  0.0 53.9 jit_solution(8005936322773165464)
XLA Ops:
  0.6 1.3 %rotate.1 = (bf16[2,192,256]{2,1,0:T(8,128)(2,1)S(1)}, bf16[2,192,256]{2,1,0:T(8,128)(2,1)S(1)}, f32[3,192,128]{2,1,0:T(8,128)S(1)}) custom-call(bf16[192,256]{1,0:T(8,128)(2,1)} %bitcast.10, bf16[192,256]{1,0:T(8,128)(2,1)} %bitcast.11, bf16[192,256]{1,0:T(8,128)(2,1)} %bitcast.12, bf16[192,256]{1,0:T(8,128)(2,1)} %bitcast.13, ...), custom_call_target="tpu_custom_call" | custom-call | bytes 1179648 | tf_op jit(solution)/shard_map/rotate/pallas_call | solution.py:339
  1.9 2.1 %collective-permute-start.4 = (bf16[2,192,256]{2,1,0:T(8,128)(2,1)S(1)}, bf16[2,192,256]{2,1,0:T(8,128)(2,1)S(1)}, u32[]{:S(2)}, u32[]{:S(2)}) collective-permute-start(bf16[2,192,256]{2,1,0:T(8,128)(2,1)S(1)} %get-tuple-element.41.refs_3_.refs_1_.refs_4_), channel_id=1, source_target_pairs={{0,4},{4,0},{1,5},{5,1},{2,6},{6,2},{3,7},{7,3},{8,12},{12,8},{9,1... | collective-permute-start | bytes 589832 | tf_op jit(solution)/shard_map/halo/ppermute | solution.py:381
  4.0 2.3 %collective-permute-start.1 = (bf16[2,192,256]{2,1,0:T(8,128)(2,1)S(1)}, bf16[2,192,256]{2,1,0:T(8,128)(2,1)S(1)}, u32[]{:S(2)}, u32[]{:S(2)}) collective-permute-start(bf16[2,192,256]{2,1,0:T(8,128)(2,1)S(1)} %get-tuple-element.40.refs_0_), channel_id=1, source_target_pairs={{0,16},{8,24},{16,0},{24,8},{1,17},{9,25},{17,1},{25,9},{2,18},{10... | collective-permute-start | bytes 589832 | tf_op jit(solution)/shard_map/halo/ppermute | solution.py:376
  6.3 1.3 %collective-permute-start = (bf16[2,192,256]{2,1,0:T(8,128)(2,1)S(1)}, bf16[2,192,256]{2,1,0:T(8,128)(2,1)S(1)}, u32[]{:S(2)}, u32[]{:S(2)}) collective-permute-start(bf16[2,192,256]{2,1,0:T(8,128)(2,1)S(1)} %get-tuple-element.40.refs_0_), channel_id=1, source_target_pairs={{0,8},{8,0},{16,24},{24,16},{1,9},{9,1},{17,25},{25,17},{2,10},{10... | collective-permute-start | bytes 589832 | tf_op jit(solution)/shard_map/halo/ppermute | solution.py:376
  7.6 4.5 %collective-permute-start.3 = (bf16[2,192,256]{2,1,0:T(8,128)(2,1)S(1)}, bf16[2,192,256]{2,1,0:T(8,128)(2,1)S(1)}, u32[]{:S(2)}, u32[]{:S(2)}) collective-permute-start(bf16[2,192,256]{2,1,0:T(8,128)(2,1)S(1)} %get-tuple-element.41.refs_3_.refs_1_.refs_4_), channel_id=1, source_target_pairs={{0,0},{1,2},{2,1},{3,3},{4,4},{5,6},{6,5},{7,7},{8,8},{9,10},{10,9... | collective-permute-start | bytes 589832 | tf_op jit(solution)/shard_map/halo/ppermute | solution.py:386
  12.2 0.1 collective-permute-start.2
  12.2 0.0 collective-permute-done.4.refs_6_.refs_4_.refs_5_
  12.2 1.9 %collective-permute-start.6 = (bf16[2,192,256]{2,1,0:T(8,128)(2,1)S(1)}, bf16[2,192,256]{2,1,0:T(8,128)(2,1)S(1)}, u32[]{:S(2)}, u32[]{:S(2)}) collective-permute-start(bf16[2,192,256]{2,1,0:T(8,128)(2,1)S(1)} %collective-permute-done.4.refs_6_.refs_4_.refs_5_), channel_id=1, source_target_pairs={{0,0},{1,2},{2,1},{3,3},{4,4},{5,6},{6,5},{7,7},{8,8},{9,10},{10,9... | collective-permute-start | bytes 589832 | tf_op jit(solution)/shard_map/halo/ppermute | solution.py:386
  14.2 0.7 %collective-permute-done.1.refs_2_ = bf16[2,192,256]{2,1,0:T(8,128)(2,1)S(1)} collective-permute-done((bf16[2,192,256]{2,1,0:T(8,128)(2,1)S(1)}, bf16[2,192,256]{2,1,0:T(8,128)(2,1)S(1)}, u32[]{:S(2)}, u32[]{:S(2)}) %collective-permute-start.1) | collective-permute-done | bytes 196640 | tf_op jit(solution)/shard_map/halo/ppermute | solution.py:376
  14.9 1.7 %collective-permute-start.5 = (bf16[2,192,256]{2,1,0:T(8,128)(2,1)S(1)}, bf16[2,192,256]{2,1,0:T(8,128)(2,1)S(1)}, u32[]{:S(2)}, u32[]{:S(2)}) collective-permute-start(bf16[2,192,256]{2,1,0:T(8,128)(2,1)S(1)} %collective-permute-done.4.refs_6_.refs_4_.refs_5_), channel_id=1, source_target_pairs={{0,1},{1,0},{2,3},{3,2},{4,5},{5,4},{6,7},{7,6},{8,9},{9,8},{10,11... | collective-permute-start | bytes 589832 | tf_op jit(solution)/shard_map/halo/ppermute | solution.py:386
  16.5 0.0 collective-permute-done.refs_1_
  16.5 0.3 collective-permute-start.7
  16.8 0.0 collective-permute-done.3.refs_5_.refs_3_.refs_6_
  16.8 0.0 collective-permute-done.2.refs_4_.refs_2_
  16.8 2.4 %collective-permute-done.6.refs_8_.refs_6_.refs_7_ = bf16[2,192,256]{2,1,0:T(8,128)(2,1)S(1)} collective-permute-done((bf16[2,192,256]{2,1,0:T(8,128)(2,1)S(1)}, bf16[2,192,256]{2,1,0:T(8,128)(2,1)S(1)}, u32[]{:S(2)}, u32[]{:S(2)}) %collective-permute-start.6) | collective-permute-done | bytes 196640 | tf_op jit(solution)/shard_map/halo/ppermute | solution.py:386
  19.2 0.0 collective-permute-done.5.refs_7_.refs_5_
  19.2 3.2 %attend.2 = (bf16[192,256]{1,0:T(8,128)(2,1)S(1)}, bf16[192,256]{1,0:T(8,128)(2,1)S(1)}, bf16[192,256]{1,0:T(8,128)(2,1)S(1)}, f32[576,128]{1,0:T(8,128)S(1)}) custom-call(bf16[2,192,256]{2,1,0:T(8,128)(2,1)S(1)} %get-tuple-element.40.refs_0_, bf16[2,192,256]{2,1,0:T(8,128)(2,1)S(1)} %collective-permute-done.refs_1_, ...), custom_call_target="tpu_custom_call" | custom-call | flops 5435817984 | bytes 2359296 | tf_op jit(solution)/shard_map/attend/pallas_call | solution.py:339
  22.4 0.8 %collective-permute-start.11 = (bf16[192,256]{1,0:T(8,128)(2,1)S(1)}, bf16[192,256]{1,0:T(8,128)(2,1)S(1)}, u32[]{:S(2)}, u32[]{:S(2)}) collective-permute-start(bf16[192,256]{1,0:T(8,128)(2,1)S(1)} %get-tuple-element.45), channel_id=1, source_target_pairs={{0,16},{8,24},{16,0},{24,8},{1,17},{9,25},{17,1},{25,9},{2,18},{10... | collective-permute-start | bytes 294920 | tf_op jit(solution)/shard_map/merge/ppermute | solution.py:376
  23.2 1.0 %collective-permute-start.12 = (bf16[192,256]{1,0:T(8,128)(2,1)S(1)}, bf16[192,256]{1,0:T(8,128)(2,1)S(1)}, u32[]{:S(2)}, u32[]{:S(2)}) collective-permute-start(bf16[192,256]{1,0:T(8,128)(2,1)S(1)} %get-tuple-element.46), channel_id=1, source_target_pairs={{0,8},{8,0},{16,24},{24,16},{1,9},{9,1},{17,25},{25,17},{2,10},{10... | collective-permute-start | bytes 294920 | tf_op jit(solution)/shard_map/merge/ppermute | solution.py:376
  24.3 0.0 collective-permute-done.7.refs_0_.refs_3_
  24.3 1.3 %attend.3 = (bf16[192,256]{1,0:T(8,128)(2,1)S(1)}, f32[8,768]{1,0:T(8,128)S(1)}) custom-call(bf16[2,192,256]{2,1,0:T(8,128)(2,1)S(1)} %collective-permute-done.7.refs_0_.refs_3_, bf16[2,192,256]{2,1,0:T(8,128)(2,1)S(1)} %get-tuple-element.41.refs_3_.refs_1_.refs_4_, bf16[2,192,256]{2,1,0:T(8,128)(2,1)S(1)} %collective-permute-done.2.refs_4_.refs_2_, ...), custom_call_target="tpu_custom_call" | custom-call | flops 1811939328 | bytes 1794048 | tf_op jit(solution)/shard_map/attend/pallas_call | solution.py:339
  25.6 1.9 %collective-permute-start.10 = (f32[8,768]{1,0:T(8,128)S(1)}, f32[8,768]{1,0:T(8,128)S(1)}, u32[]{:S(2)}, u32[]{:S(2)}) collective-permute-start(f32[8,768]{1,0:T(8,128)S(1)} %get-tuple-element.47.refs_8_), channel_id=1, source_target_pairs={{0,24},{8,16},{16,8},{24,0},{1,25},{9,17},{17,9},{25,1},{2,26},{10... | collective-permute-start | bytes 73736 | tf_op jit(solution)/shard_map/merge/ppermute | solution.py:376
  27.5 0.0 collective-permute-start.9
  27.5 1.7 %collective-permute-start.8 = (f32[8,768]{1,0:T(8,128)S(1)}, f32[8,768]{1,0:T(8,128)S(1)}, u32[]{:S(2)}, u32[]{:S(2)}) collective-permute-start(f32[8,768]{1,0:T(8,128)S(1)} %get-tuple-element.47.refs_8_), channel_id=1, source_target_pairs={{0,8},{8,0},{16,24},{24,16},{1,9},{9,1},{17,25},{25,17},{2,10},{10... | collective-permute-start | bytes 73736 | tf_op jit(solution)/shard_map/merge/ppermute | solution.py:376
  29.1 1.0 %collective-permute-done.10.refs_11_ = f32[8,768]{1,0:T(8,128)S(1)} collective-permute-done((f32[8,768]{1,0:T(8,128)S(1)}, f32[8,768]{1,0:T(8,128)S(1)}, u32[]{:S(2)}, u32[]{:S(2)}) %collective-permute-start.10) | collective-permute-done | bytes 24608 | tf_op jit(solution)/shard_map/merge/ppermute | solution.py:376
  30.2 1.9 %collective-permute-start.13 = (bf16[192,256]{1,0:T(8,128)(2,1)S(1)}, bf16[192,256]{1,0:T(8,128)(2,1)S(1)}, u32[]{:S(2)}, u32[]{:S(2)}) collective-permute-start(bf16[192,256]{1,0:T(8,128)(2,1)S(1)} %get-tuple-element.57), channel_id=1, source_target_pairs={{0,24},{8,16},{16,8},{24,0},{1,25},{9,17},{17,9},{25,1},{2,26},{10... | collective-permute-start | bytes 294920 | tf_op jit(solution)/shard_map/merge/ppermute | solution.py:376
  32.1 0.0 collective-permute-done.9.refs_10_
  32.1 0.0 collective-permute-done.8.refs_9_
  32.1 0.0 collective-permute-done.11.refs_2_
  32.1 0.0 collective-permute-done.12.refs_3_
  32.1 3.1 %gradients.2 = (f32[2,128,768]{2,1,0:T(8,128)S(1)}, f32[2,768]{1,0:T(2,128)S(1)}, f32[2,768]{1,0:T(2,128)S(1)}, f32[192,128]{1,0:T(8,128)S(1)}, bf16[2,2,192,256...) custom-call(bf16[2,192,256]{2,1,0:T(8,128)(2,1)S(1)} %get-tuple-element.40.refs_0_, ...), custom_call_target="tpu_custom_call" | custom-call | flops 12079595520 | bytes 3354624 | tf_op jit(solution)/shard_map/gradients/pallas_call | solution.py:339
  35.2 2.2 %collective-permute-start.17 = (bf16[2,2,192,256]{3,2,1,0:T(8,128)(2,1)S(1)}, bf16[2,2,192,256]{3,2,1,0:T(8,128)(2,1)S(1)}, u32[]{:S(2)}, u32[]{:S(2)}) collective-permute-start(bf16[2,2,192,256]{3,2,1,0:T(8,128)(2,1)S(1)} %get-tuple-element.72), channel_id=1, source_target_pairs={{0,1},{1,0},{2,3},{3,2},{4,5},{5,4},{6,7},{7,6},{8,9},{9,8},{10,11... | collective-permute-start | bytes 1179656 | tf_op jit(solution)/shard_map/gradients/ppermute | solution.py:441
  37.4 3.0 %collective-permute-start.18 = (bf16[2,2,192,256]{3,2,1,0:T(8,128)(2,1)S(1)}, bf16[2,2,192,256]{3,2,1,0:T(8,128)(2,1)S(1)}, u32[]{:S(2)}, u32[]{:S(2)}) collective-permute-start(bf16[2,2,192,256]{3,2,1,0:T(8,128)(2,1)S(1)} %get-tuple-element.73), channel_id=1, source_target_pairs={{0,0},{1,2},{2,1},{3,3},{4,4},{5,6},{6,5},{7,7},{8,8},{9,10},{10,9... | collective-permute-start | bytes 1179656 | tf_op jit(solution)/shard_map/gradients/ppermute | solution.py:441
  40.5 1.7 %gradients.3 = (bf16[192,256]{1,0:T(8,128)(2,1)S(1)}, bf16[192,256]{1,0:T(8,128)(2,1)S(1)}, bf16[192,256]{1,0:T(8,128)(2,1)S(1)}, bf16[192,256]{1,0:T(8,128)(2,1)S(1)}, bf16[2,2,192,256]{3,2,1,0:T(8,128)(2,1)S(1)}) custom-call(bf16[2,192,256]{2,1,0:T(8,128)(2,1)S(1)} %get-tuple-element.40.refs_0_, bf16[2,192,256]{2,1,0:T(8,128)(2,1)S(1)} %collective-permute-done.refs_1_, ...), custom_call_target="tpu_custom_call" | custom-call | flops 6039797760 | bytes 2764800 | tf_op jit(solution)/shard_map/gradients/pallas_call | solution.py:339
  42.2 0.0 collective-permute-done.13.refs_1_
  42.2 1.6 %collective-permute-start.14 = (bf16[192,256]{1,0:T(8,128)(2,1)S(1)}, bf16[192,256]{1,0:T(8,128)(2,1)S(1)}, u32[]{:S(2)}, u32[]{:S(2)}) collective-permute-start(bf16[192,256]{1,0:T(8,128)(2,1)S(1)} %get-tuple-element.64), channel_id=1, source_target_pairs={{0,24},{8,16},{16,8},{24,0},{1,25},{9,17},{17,9},{25,1},{2,26},{10... | collective-permute-start | bytes 294920 | tf_op jit(solution)/shard_map/return/ppermute | solution.py:376
  43.7 0.0 collective-permute-start.15
  43.7 2.1 %collective-permute-start.16 = (bf16[192,256]{1,0:T(8,128)(2,1)S(1)}, bf16[192,256]{1,0:T(8,128)(2,1)S(1)}, u32[]{:S(2)}, u32[]{:S(2)}) collective-permute-start(bf16[192,256]{1,0:T(8,128)(2,1)S(1)} %get-tuple-element.66), channel_id=1, source_target_pairs={{0,8},{8,0},{16,24},{24,16},{1,9},{9,1},{17,25},{25,17},{2,10},{10... | collective-permute-start | bytes 294920 | tf_op jit(solution)/shard_map/return/ppermute | solution.py:376
  45.8 0.0 collective-permute-done.17.refs_1_
  45.8 1.0 %collective-permute-done.18.refs_2_ = bf16[2,2,192,256]{3,2,1,0:T(8,128)(2,1)S(1)} collective-permute-done((bf16[2,2,192,256]{3,2,1,0:T(8,128)(2,1)S(1)}, bf16[2,2,192,256]{3,2,1,0:T(8,128)(2,1)S(1)}, u32[]{:S(2)}, u32[]{:S(2)}) %collective-permute-start.18) | collective-permute-done | bytes 393248 | tf_op jit(solution)/shard_map/gradients/ppermute | solution.py:441
  46.8 0.1 fusion
  46.9 0.3 collective-permute-start.19
  47.2 1.4 %collective-permute-done.14.refs_5_ = bf16[192,256]{1,0:T(8,128)(2,1)S(1)} collective-permute-done((bf16[192,256]{1,0:T(8,128)(2,1)S(1)}, bf16[192,256]{1,0:T(8,128)(2,1)S(1)}, u32[]{:S(2)}, u32[]{:S(2)}) %collective-permute-start.14) | collective-permute-done | bytes 98336 | tf_op jit(solution)/shard_map/return/ppermute | solution.py:376
  48.6 3.3 %collective-permute-done.15.refs_6_ = bf16[192,256]{1,0:T(8,128)(2,1)S(1)} collective-permute-done((bf16[192,256]{1,0:T(8,128)(2,1)S(1)}, bf16[192,256]{1,0:T(8,128)(2,1)S(1)}, u32[]{:S(2)}, u32[]{:S(2)}) %collective-permute-start.15) | collective-permute-done | bytes 98336 | tf_op jit(solution)/shard_map/return/ppermute | solution.py:376
  51.9 0.0 collective-permute-done.16.refs_7_
  51.9 1.0 %finish.2 = (bf16[192,256]{1,0:T(8,128)(2,1)}, bf16[192,256]{1,0:T(8,128)(2,1)}) custom-call(bf16[192,256]{1,0:T(8,128)(2,1)S(1)} %get-tuple-element.42.refs_0_, bf16[192,256]{1,0:T(8,128)(2,1)S(1)} %collective-permute-done.13.refs_1_, bf16[192,256]{1,0:T(8,128)(2,1)S(1)} %collective-permute-done.11.refs_2_, ...), custom_call_target="tpu_custom_call" | custom-call | flops 9059696640 | bytes 1376256 | tf_op jit(solution)/shard_map/finish/pallas_call | solution.py:339
  53.0 0.0 collective-permute-done.19.refs_3_
  53.0 0.9 %finish.3 = (bf16[192,256]{1,0:T(8,128)(2,1)}, bf16[192,256]{1,0:T(8,128)(2,1)}) custom-call(bf16[2,2,192,256]{3,2,1,0:T(8,128)(2,1)S(1)} %get-tuple-element.71.refs_0_, bf16[2,2,192,256]{3,2,1,0:T(8,128)(2,1)S(1)} %collective-permute-done.17.refs_1_, bf16[2,2,192,256]{3,2,1,0:T(8,128)(2,1)S(1)} %collective-permute-done.18.refs_2_, ...), custom_call_target="tpu_custom_call" | custom-call | bytes 1867776 | tf_op jit(solution)/shard_map/finish/pallas_call | solution.py:339
Async XLA Ops:
  1.9 10.3 %collective-permute-start.4 = (bf16[2,192,256]{2,1,0:T(8,128)(2,1)S(1)}, bf16[2,192,256]{2,1,0:T(8,128)(2,1)S(1)}, u32[]{:S(2)}, u32[]{:S(2)}) collective-permute-start(bf16[2,192,256]{2,1,0:T(8,128)(2,1)S(1)} %get-tuple-element.41.refs_3_.refs_1_.refs_4_), channel_id=1, source_target_pairs={{0,4},{4,0},{1,5},{5,1},{2,6},{6,2},{3,7},{7,3},{8,12},{12,8},{9,1... | collective-permute-start | bytes 589832 | tf_op jit(solution)/shard_map/halo/ppermute | solution.py:381
  4.0 10.9 %collective-permute-start.1 = (bf16[2,192,256]{2,1,0:T(8,128)(2,1)S(1)}, bf16[2,192,256]{2,1,0:T(8,128)(2,1)S(1)}, u32[]{:S(2)}, u32[]{:S(2)}) collective-permute-start(bf16[2,192,256]{2,1,0:T(8,128)(2,1)S(1)} %get-tuple-element.40.refs_0_), channel_id=1, source_target_pairs={{0,16},{8,24},{16,0},{24,8},{1,17},{9,25},{17,1},{25,9},{2,18},{10... | collective-permute-start | bytes 589832 | tf_op jit(solution)/shard_map/halo/ppermute | solution.py:376
  6.3 10.2 %collective-permute-start = (bf16[2,192,256]{2,1,0:T(8,128)(2,1)S(1)}, bf16[2,192,256]{2,1,0:T(8,128)(2,1)S(1)}, u32[]{:S(2)}, u32[]{:S(2)}) collective-permute-start(bf16[2,192,256]{2,1,0:T(8,128)(2,1)S(1)} %get-tuple-element.40.refs_0_), channel_id=1, source_target_pairs={{0,8},{8,0},{16,24},{24,16},{1,9},{9,1},{17,25},{25,17},{2,10},{10... | collective-permute-start | bytes 589832 | tf_op jit(solution)/shard_map/halo/ppermute | solution.py:376
  7.6 9.2 %collective-permute-start.3 = (bf16[2,192,256]{2,1,0:T(8,128)(2,1)S(1)}, bf16[2,192,256]{2,1,0:T(8,128)(2,1)S(1)}, u32[]{:S(2)}, u32[]{:S(2)}) collective-permute-start(bf16[2,192,256]{2,1,0:T(8,128)(2,1)S(1)} %get-tuple-element.41.refs_3_.refs_1_.refs_4_), channel_id=1, source_target_pairs={{0,0},{1,2},{2,1},{3,3},{4,4},{5,6},{6,5},{7,7},{8,8},{9,10},{10,9... | collective-permute-start | bytes 589832 | tf_op jit(solution)/shard_map/halo/ppermute | solution.py:386
  12.2 4.7 %collective-permute-start.2 = (bf16[2,192,256]{2,1,0:T(8,128)(2,1)S(1)}, bf16[2,192,256]{2,1,0:T(8,128)(2,1)S(1)}, u32[]{:S(2)}, u32[]{:S(2)}) collective-permute-start(bf16[2,192,256]{2,1,0:T(8,128)(2,1)S(1)} %get-tuple-element.41.refs_3_.refs_1_.refs_4_), channel_id=1, source_target_pairs={{0,1},{1,0},{2,3},{3,2},{4,5},{5,4},{6,7},{7,6},{8,9},{9,8},{10,11... | collective-permute-start | bytes 589832 | tf_op jit(solution)/shard_map/halo/ppermute | solution.py:386
  12.2 7.0 %collective-permute-start.6 = (bf16[2,192,256]{2,1,0:T(8,128)(2,1)S(1)}, bf16[2,192,256]{2,1,0:T(8,128)(2,1)S(1)}, u32[]{:S(2)}, u32[]{:S(2)}) collective-permute-start(bf16[2,192,256]{2,1,0:T(8,128)(2,1)S(1)} %collective-permute-done.4.refs_6_.refs_4_.refs_5_), channel_id=1, source_target_pairs={{0,0},{1,2},{2,1},{3,3},{4,4},{5,6},{6,5},{7,7},{8,8},{9,10},{10,9... | collective-permute-start | bytes 589832 | tf_op jit(solution)/shard_map/halo/ppermute | solution.py:386
  14.9 4.4 %collective-permute-start.5 = (bf16[2,192,256]{2,1,0:T(8,128)(2,1)S(1)}, bf16[2,192,256]{2,1,0:T(8,128)(2,1)S(1)}, u32[]{:S(2)}, u32[]{:S(2)}) collective-permute-start(bf16[2,192,256]{2,1,0:T(8,128)(2,1)S(1)} %collective-permute-done.4.refs_6_.refs_4_.refs_5_), channel_id=1, source_target_pairs={{0,1},{1,0},{2,3},{3,2},{4,5},{5,4},{6,7},{7,6},{8,9},{9,8},{10,11... | collective-permute-start | bytes 589832 | tf_op jit(solution)/shard_map/halo/ppermute | solution.py:386
  16.5 7.7 %collective-permute-start.7 = (bf16[2,192,256]{2,1,0:T(8,128)(2,1)S(1)}, bf16[2,192,256]{2,1,0:T(8,128)(2,1)S(1)}, u32[]{:S(2)}, u32[]{:S(2)}) collective-permute-start(bf16[2,192,256]{2,1,0:T(8,128)(2,1)S(1)} %collective-permute-done.1.refs_2_), channel_id=1, source_target_pairs={{0,8},{8,0},{16,24},{24,16},{1,9},{9,1},{17,25},{25,17},{2,10},{10... | collective-permute-start | bytes 589832 | tf_op jit(solution)/shard_map/halo/ppermute | solution.py:376
  22.4 9.6 %collective-permute-start.11 = (bf16[192,256]{1,0:T(8,128)(2,1)S(1)}, bf16[192,256]{1,0:T(8,128)(2,1)S(1)}, u32[]{:S(2)}, u32[]{:S(2)}) collective-permute-start(bf16[192,256]{1,0:T(8,128)(2,1)S(1)} %get-tuple-element.45), channel_id=1, source_target_pairs={{0,16},{8,24},{16,0},{24,8},{1,17},{9,25},{17,1},{25,9},{2,18},{10... | collective-permute-start | bytes 294920 | tf_op jit(solution)/shard_map/merge/ppermute | solution.py:376
  23.2 8.9 %collective-permute-start.12 = (bf16[192,256]{1,0:T(8,128)(2,1)S(1)}, bf16[192,256]{1,0:T(8,128)(2,1)S(1)}, u32[]{:S(2)}, u32[]{:S(2)}) collective-permute-start(bf16[192,256]{1,0:T(8,128)(2,1)S(1)} %get-tuple-element.46), channel_id=1, source_target_pairs={{0,8},{8,0},{16,24},{24,16},{1,9},{9,1},{17,25},{25,17},{2,10},{10... | collective-permute-start | bytes 294920 | tf_op jit(solution)/shard_map/merge/ppermute | solution.py:376
  25.6 4.6 %collective-permute-start.10 = (f32[8,768]{1,0:T(8,128)S(1)}, f32[8,768]{1,0:T(8,128)S(1)}, u32[]{:S(2)}, u32[]{:S(2)}) collective-permute-start(f32[8,768]{1,0:T(8,128)S(1)} %get-tuple-element.47.refs_8_), channel_id=1, source_target_pairs={{0,24},{8,16},{16,8},{24,0},{1,25},{9,17},{17,9},{25,1},{2,26},{10... | collective-permute-start | bytes 73736 | tf_op jit(solution)/shard_map/merge/ppermute | solution.py:376
  27.5 4.6 %collective-permute-start.9 = (f32[8,768]{1,0:T(8,128)S(1)}, f32[8,768]{1,0:T(8,128)S(1)}, u32[]{:S(2)}, u32[]{:S(2)}) collective-permute-start(f32[8,768]{1,0:T(8,128)S(1)} %get-tuple-element.47.refs_8_), channel_id=1, source_target_pairs={{0,16},{8,24},{16,0},{24,8},{1,17},{9,25},{17,1},{25,9},{2,18},{10... | collective-permute-start | bytes 73736 | tf_op jit(solution)/shard_map/merge/ppermute | solution.py:376
  27.5 4.6 %collective-permute-start.8 = (f32[8,768]{1,0:T(8,128)S(1)}, f32[8,768]{1,0:T(8,128)S(1)}, u32[]{:S(2)}, u32[]{:S(2)}) collective-permute-start(f32[8,768]{1,0:T(8,128)S(1)} %get-tuple-element.47.refs_8_), channel_id=1, source_target_pairs={{0,8},{8,0},{16,24},{24,16},{1,9},{9,1},{17,25},{25,17},{2,10},{10... | collective-permute-start | bytes 73736 | tf_op jit(solution)/shard_map/merge/ppermute | solution.py:376
  30.2 12.0 %collective-permute-start.13 = (bf16[192,256]{1,0:T(8,128)(2,1)S(1)}, bf16[192,256]{1,0:T(8,128)(2,1)S(1)}, u32[]{:S(2)}, u32[]{:S(2)}) collective-permute-start(bf16[192,256]{1,0:T(8,128)(2,1)S(1)} %get-tuple-element.57), channel_id=1, source_target_pairs={{0,24},{8,16},{16,8},{24,0},{1,25},{9,17},{17,9},{25,1},{2,26},{10... | collective-permute-start | bytes 294920 | tf_op jit(solution)/shard_map/merge/ppermute | solution.py:376
  35.2 10.6 %collective-permute-start.17 = (bf16[2,2,192,256]{3,2,1,0:T(8,128)(2,1)S(1)}, bf16[2,2,192,256]{3,2,1,0:T(8,128)(2,1)S(1)}, u32[]{:S(2)}, u32[]{:S(2)}) collective-permute-start(bf16[2,2,192,256]{3,2,1,0:T(8,128)(2,1)S(1)} %get-tuple-element.72), channel_id=1, source_target_pairs={{0,1},{1,0},{2,3},{3,2},{4,5},{5,4},{6,7},{7,6},{8,9},{9,8},{10,11... | collective-permute-start | bytes 1179656 | tf_op jit(solution)/shard_map/gradients/ppermute | solution.py:441
  37.4 9.4 %collective-permute-start.18 = (bf16[2,2,192,256]{3,2,1,0:T(8,128)(2,1)S(1)}, bf16[2,2,192,256]{3,2,1,0:T(8,128)(2,1)S(1)}, u32[]{:S(2)}, u32[]{:S(2)}) collective-permute-start(bf16[2,2,192,256]{3,2,1,0:T(8,128)(2,1)S(1)} %get-tuple-element.73), channel_id=1, source_target_pairs={{0,0},{1,2},{2,1},{3,3},{4,4},{5,6},{6,5},{7,7},{8,8},{9,10},{10,9... | collective-permute-start | bytes 1179656 | tf_op jit(solution)/shard_map/gradients/ppermute | solution.py:441
  42.2 6.4 %collective-permute-start.14 = (bf16[192,256]{1,0:T(8,128)(2,1)S(1)}, bf16[192,256]{1,0:T(8,128)(2,1)S(1)}, u32[]{:S(2)}, u32[]{:S(2)}) collective-permute-start(bf16[192,256]{1,0:T(8,128)(2,1)S(1)} %get-tuple-element.64), channel_id=1, source_target_pairs={{0,24},{8,16},{16,8},{24,0},{1,25},{9,17},{17,9},{25,1},{2,26},{10... | collective-permute-start | bytes 294920 | tf_op jit(solution)/shard_map/return/ppermute | solution.py:376
  43.7 8.2 %collective-permute-start.15 = (bf16[192,256]{1,0:T(8,128)(2,1)S(1)}, bf16[192,256]{1,0:T(8,128)(2,1)S(1)}, u32[]{:S(2)}, u32[]{:S(2)}) collective-permute-start(bf16[192,256]{1,0:T(8,128)(2,1)S(1)} %get-tuple-element.65), channel_id=1, source_target_pairs={{0,16},{8,24},{16,0},{24,8},{1,17},{9,25},{17,1},{25,9},{2,18},{10... | collective-permute-start | bytes 294920 | tf_op jit(solution)/shard_map/return/ppermute | solution.py:376
  43.7 8.2 %collective-permute-start.16 = (bf16[192,256]{1,0:T(8,128)(2,1)S(1)}, bf16[192,256]{1,0:T(8,128)(2,1)S(1)}, u32[]{:S(2)}, u32[]{:S(2)}) collective-permute-start(bf16[192,256]{1,0:T(8,128)(2,1)S(1)} %get-tuple-element.66), channel_id=1, source_target_pairs={{0,8},{8,0},{16,24},{24,16},{1,9},{9,1},{17,25},{25,17},{2,10},{10... | collective-permute-start | bytes 294920 | tf_op jit(solution)/shard_map/return/ppermute | solution.py:376
  46.9 6.1 %collective-permute-start.19 = (bf16[2,192,256]{2,1,0:T(8,128)(2,1)S(1)}, bf16[2,192,256]{2,1,0:T(8,128)(2,1)S(1)}, u32[]{:S(2)}, u32[]{:S(2)}) collective-permute-start(bf16[2,192,256]{2,1,0:T(8,128)(2,1)S(1)} %fusion), channel_id=1, source_target_pairs={{0,4},{4,0},{1,5},{5,1},{2,6},{6,2},{3,7},{7,3},{8,12},{12,8},{9,1... | collective-permute-start | bytes 589832 | tf_op jit(solution)/shard_map/return/ppermute | solution.py:450

commit v8 on v7

--- a/solution.py
+++ b/solution.py
@@ -163,40 +163,48 @@
             value_buf[at : at + cells] = kv_refs[member][1]
             at += cells
         spans.append((begin, at, group_bias(flags, sizes)))
-    lane = lax.broadcasted_iota(jnp.int32, (cells, DH), 1)
-    stats = []
-    for qg_ref, o_ref in zip(qg_refs, o_refs):
-        stat = jnp.zeros((cells, DH), F32)
-        for head in range(HEADS):
-            cut = head_slice(head)
-            scores = [dot_nt(qg_ref[0, :, cut], key_buf[lo:hi, cut]) for lo, hi, _ in spans]
-            best = None
-            for raw, (_, _, bias) in zip(scores, spans):
-                top = jnp.max(raw, axis=1, keepdims=True) * SCALE_LOG2
-                if bias is not None:
-                    top = top + bias
-                best = top if best is None else jnp.maximum(best, top)
-            total = None
-            out = None
-            for raw, (lo, hi, bias) in zip(scores, spans):
-                shift = best if bias is None else best - bias
-                weights = jnp.exp2(raw * SCALE_LOG2 - shift)
-                part = jnp.sum(weights, axis=1, keepdims=True)
-                piece = dot_nn(weights.astype(BF16), value_buf[lo:hi, cut])
-                total = part if total is None else total + part
-                out = piece if out is None else out + piece
-            out = out * (1.0 / total)
-            dotted = jnp.sum(out * qg_ref[1, :, cut].astype(F32), axis=1, keepdims=True)
-            o_ref[:, cut] = out.astype(BF16)
-            stat = jnp.where(lane == head, best + jnp.log2(total), stat)
-            stat = jnp.where(lane == HEADS + head, dotted, stat)
-        stats.append(stat)
+    lane = lax.broadcasted_iota(jnp.int32, (count * cells, DH), 1)
+    stat = jnp.zeros((count * cells, DH), F32)
+
+    def scores_of(head):
+        cut = head_slice(head)
+        query = jnp.concatenate([ref[0, :, cut] for ref in qg_refs], axis=0)
+        return [dot_nt(query, key_buf[lo:hi, cut]) for lo, hi, _ in spans]
+
+    ahead = scores_of(0)
+    for head in range(HEADS):
+        cut = head_slice(head)
+        scores = ahead
+        if head + 1 < HEADS:
+            ahead = scores_of(head + 1)
+        best = None
+        for raw, (_, _, bias) in zip(scores, spans):
+            top = jnp.max(raw, axis=1, keepdims=True) * SCALE_LOG2
+            if bias is not None:
+                top = top + bias
+            best = top if best is None else jnp.maximum(best, top)
+        total = None
+        out = None
+        for raw, (lo, hi, bias) in zip(scores, spans):
+            shift = best if bias is None else best - bias
+            weights = jnp.exp2(raw * SCALE_LOG2 - shift)
+            part = jnp.sum(weights, axis=1, keepdims=True)
+            piece = dot_nn(weights.astype(BF16), value_buf[lo:hi, cut])
+            total = part if total is None else total + part
+            out = piece if out is None else out + piece
+        out = out * (1.0 / total)
+        grad = jnp.concatenate([ref[1, :, cut] for ref in qg_refs], axis=0)
+        dotted = jnp.sum(out * grad.astype(F32), axis=1, keepdims=True)
+        out = out.astype(BF16)
+        for i, o_ref in enumerate(o_refs):
+            o_ref[:, cut] = out[i * cells : (i + 1) * cells]
+        stat = jnp.where(lane == head, best + jnp.log2(total), stat)
+        stat = jnp.where(lane == HEADS + head, dotted, stat)
     if last:
-        whole = jnp.concatenate([first_ref[...]] + stats, axis=0)
+        whole = jnp.concatenate([first_ref[...], stat], axis=0)
         stat_ref[...] = whole.T[: stat_ref.shape[0]]
     else:
-        for i, stat in enumerate(stats):
-            stat_ref[i * cells : (i + 1) * cells] = stat
+        stat_ref[...] = stat
 
 
 def seen_from(stat, distance, cells):
@@ -221,31 +229,6 @@
         [share[:HEADS] * part[HEADS : 2 * HEADS] for share, part in zip(shares, parts)],
     )
     return lse[:HEADS], delta, shares
-
-
-def gradient_blocks(cols, flags_of, sizes, key_buf, value_buf, queries, grads, lse, delta, span):
-    dq = None
-    results = []
-    for slot, col in enumerate(cols):
-        lo = slot * span
-        key = key_buf[lo : lo + span]
-        value = value_buf[lo : lo + span]
-        raw = dot_nt(key, queries)
-        prob_grad = dot_nt(value, grads)
-        cells = span // len(flags_of)
-        probs = []
-        for row, row_far in enumerate(flags_of):
-            bias = group_bias((row_far, col == 2), sizes)
-            shift = lse if bias is None else lse - bias
-            probs.append(jnp.exp2(raw[row * cells : (row + 1) * cells] * SCALE_LOG2 - shift))
-        probs = jnp.concatenate(probs, axis=0)
-        dscore = (probs * (prob_grad - delta)).astype(BF16)
-        dv = dot_nn(probs.astype(BF16), grads)
-        dk = dot_nn(dscore, queries) * SCALE
-        results.append((dk, dv))
-        part = dot_nn(key.T, dscore)
-        dq = part if dq is None else dq + part
-    return results, dq
 
 
 def backward_kernel(cols, grid_rows, sizes, cells, first, last, *refs):
@@ -278,22 +261,42 @@
     for i, ref in enumerate(kv_refs):
         key_buf[i * cells : (i + 1) * cells] = ref[0]
         value_buf[i * cells : (i + 1) * cells] = ref[1]
-    row_flags = [row == 2 for row in range(grid_rows)]
-    for head in range(HEADS):
-        cut = head_slice(head)
+    blocks = [(head, slot) for head in range(HEADS) for slot in range(len(cols))]
+
+    def products_of(head, slot):
+        cut = head_slice(head)
+        at = slice(slot * span, (slot + 1) * span)
         queries = jnp.concatenate([ref[0, :, cut] for ref in qg_refs], axis=0)
         grads = jnp.concatenate([ref[1, :, cut] for ref in qg_refs], axis=0)
-        results, dq = gradient_blocks(
-            cols, row_flags, sizes, key_buf.at[:, cut], value_buf.at[:, cut], queries, grads,
-            lse[head : head + 1], delta[head : head + 1], span,
-        )
-        for (dk, dv), ref in zip(results, col_refs):
-            for row in range(grid_rows):
-                at = slice(row * cells, (row + 1) * cells)
-                ref[row, 0, :, cut] = dk[at].astype(BF16)
-                ref[row, 1, :, cut] = dv[at].astype(BF16)
-        if not first:
-            dq = dq + dq_ref[head]
+        raw = dot_nt(key_buf[at, cut], queries)
+        return raw, dot_nt(value_buf[at, cut], grads), queries, grads
+
+    dqs = [None] * HEADS
+    ahead = products_of(*blocks[0])
+    for i, (head, slot) in enumerate(blocks):
+        raw, prob_grad, queries, grads = ahead
+        if i + 1 < len(blocks):
+            ahead = products_of(*blocks[i + 1])
+        cut = head_slice(head)
+        probs = []
+        for row in range(grid_rows):
+            bias = group_bias((row == 2, cols[slot] == 2), sizes)
+            shift = lse[head : head + 1]
+            shift = shift if bias is None else shift - bias
+            probs.append(jnp.exp2(raw[row * cells : (row + 1) * cells] * SCALE_LOG2 - shift))
+        probs = jnp.concatenate(probs, axis=0)
+        dscore = (probs * (prob_grad - delta[head : head + 1])).astype(BF16)
+        dv = dot_nn(probs.astype(BF16), grads).astype(BF16)
+        dk = (dot_nn(dscore, queries) * SCALE).astype(BF16)
+        for row in range(grid_rows):
+            at = slice(row * cells, (row + 1) * cells)
+            col_refs[slot][row, 0, :, cut] = dk[at]
+            col_refs[slot][row, 1, :, cut] = dv[at]
+        part = dot_nn(key_buf[slot * span : (slot + 1) * span, cut].T, dscore)
+        dqs[head] = part if dqs[head] is None else dqs[head] + part
+    for head in range(HEADS):
+        cut = head_slice(head)
+        dq = dqs[head] if first else dqs[head] + dq_ref[head]
         if last:
             dq = (dq * SCALE).T.astype(BF16)
             for i, ref in enumerate(dq_outs):

time: 54 us -> 53.7 us (level)
  starting transfers between devices: 30.7 us -> 31.8 us
  Pallas kernels: 12.5 us -> 11.4 us
    pallas_call x7, Pallas kernels: 12.5 us -> 11.4 us  [call(): pl.pallas_call(kernel, out_shape=out_shape, in_specs=[pl.BlockSpec(memory...]
    ppermute x2, starting transfers between devices: 5.23 us -> 5.88 us  [shards(): sides = [lax.ppermute(x, 'wa', pairs) for x, pairs in zip(sides, col_sides)]]
    ppermute x2, waiting for transfers between devices: 0.98 us -> 0.44 us  [shards(): sides = [lax.ppermute(x, 'wa', pairs) for x, pairs in zip(sides, col_sides)]]
  transfers between devices with their start and end apart: 20 -> 20, of which waited for: 6 -> 6; matrix products, arithmetic and copies ran while one was open for 0% -> 0% of each run, Pallas kernels for 19% -> 17%
where the time goes in v8:
time: 53.7 us; the launch traced here: 53.5 us
  starting transfers between devices  31.8 us (59%)
  Pallas kernels  11.4 us (21%)
  waiting for transfers between devices  9.57 us (18%)
  between operations  0.73 us (1%)
    ppermute x12, starting transfers between devices, other_frames(): lax.ppermute(x, 'ta', [(i, i ^ distance) for i in range(sizes['ta'])])  15.3 us
    pallas_call x7, Pallas kernels, call(): pl.pallas_call(kernel, out_shape=out_shape, in_specs=[pl.BlockSpec(memory...  11.4 us
    ppermute x4, starting transfers between devices, shards(): lax.ppermute(block, 'wa', pairs)  8.2 us
    ppermute x12, waiting for transfers between devices, other_frames(): lax.ppermute(x, 'ta', [(i, i ^ distance) for i in range(sizes['ta'])])  6.72 us
    ppermute x2, starting transfers between devices, shards(): sides = [lax.ppermute(x, 'wa', pairs) for x, pairs in zip(sides, col_sides)]  5.88 us
    ppermute x4, waiting for transfers between devices, shards(): lax.ppermute(block, 'wa', pairs)  2.4 us
    ppermute x1, starting transfers between devices, shards(): kv_rows = [kv] + [lax.ppermute(kv, 'ha', pairs) for pairs in row_sides]  2.11 us
  transfers between devices with their start and end apart: 20, of which 6 were waited for; matrix products, arithmetic and copies ran while one was open for 0% of the time, Pallas kernels for 17%

profile of v8, /device:TPU:1, one launch (start us, length us, event | category | flops | bytes accessed | tf_op | source)
XLA Modules:
  0.0 53.5 jit_solution(17421343914958660814)
XLA Ops:
  0.6 1.3 %rotate.1 = (bf16[2,192,256]{2,1,0:T(8,128)(2,1)S(1)}, bf16[2,192,256]{2,1,0:T(8,128)(2,1)S(1)}, f32[3,192,128]{2,1,0:T(8,128)S(1)}) custom-call(bf16[192,256]{1,0:T(8,128)(2,1)} %bitcast.10, bf16[192,256]{1,0:T(8,128)(2,1)} %bitcast.11, bf16[192,256]{1,0:T(8,128)(2,1)} %bitcast.12, bf16[192,256]{1,0:T(8,128)(2,1)} %bitcast.13, ...), custom_call_target="tpu_custom_call" | custom-call | bytes 1179648 | tf_op jit(solution)/shard_map/rotate/pallas_call | solution.py:342
  1.9 2.1 %collective-permute-start.4 = (bf16[2,192,256]{2,1,0:T(8,128)(2,1)S(1)}, bf16[2,192,256]{2,1,0:T(8,128)(2,1)S(1)}, u32[]{:S(2)}, u32[]{:S(2)}) collective-permute-start(bf16[2,192,256]{2,1,0:T(8,128)(2,1)S(1)} %get-tuple-element.41.refs_3_.refs_1_.refs_4_), channel_id=1, source_target_pairs={{0,4},{4,0},{1,5},{5,1},{2,6},{6,2},{3,7},{7,3},{8,12},{12,8},{9,1... | collective-permute-start | bytes 589832 | tf_op jit(solution)/shard_map/halo/ppermute | solution.py:384
  4.0 2.3 %collective-permute-start.1 = (bf16[2,192,256]{2,1,0:T(8,128)(2,1)S(1)}, bf16[2,192,256]{2,1,0:T(8,128)(2,1)S(1)}, u32[]{:S(2)}, u32[]{:S(2)}) collective-permute-start(bf16[2,192,256]{2,1,0:T(8,128)(2,1)S(1)} %get-tuple-element.40.refs_0_), channel_id=1, source_target_pairs={{0,16},{8,24},{16,0},{24,8},{1,17},{9,25},{17,1},{25,9},{2,18},{10... | collective-permute-start | bytes 589832 | tf_op jit(solution)/shard_map/halo/ppermute | solution.py:379
  6.3 1.3 %collective-permute-start = (bf16[2,192,256]{2,1,0:T(8,128)(2,1)S(1)}, bf16[2,192,256]{2,1,0:T(8,128)(2,1)S(1)}, u32[]{:S(2)}, u32[]{:S(2)}) collective-permute-start(bf16[2,192,256]{2,1,0:T(8,128)(2,1)S(1)} %get-tuple-element.40.refs_0_), channel_id=1, source_target_pairs={{0,8},{8,0},{16,24},{24,16},{1,9},{9,1},{17,25},{25,17},{2,10},{10... | collective-permute-start | bytes 589832 | tf_op jit(solution)/shard_map/halo/ppermute | solution.py:379
  7.6 4.5 %collective-permute-start.3 = (bf16[2,192,256]{2,1,0:T(8,128)(2,1)S(1)}, bf16[2,192,256]{2,1,0:T(8,128)(2,1)S(1)}, u32[]{:S(2)}, u32[]{:S(2)}) collective-permute-start(bf16[2,192,256]{2,1,0:T(8,128)(2,1)S(1)} %get-tuple-element.41.refs_3_.refs_1_.refs_4_), channel_id=1, source_target_pairs={{0,0},{1,2},{2,1},{3,3},{4,4},{5,6},{6,5},{7,7},{8,8},{9,10},{10,9... | collective-permute-start | bytes 589832 | tf_op jit(solution)/shard_map/halo/ppermute | solution.py:389
  12.2 0.1 collective-permute-start.2
  12.2 0.0 collective-permute-done.4.refs_6_.refs_4_.refs_5_
  12.2 1.9 %collective-permute-start.6 = (bf16[2,192,256]{2,1,0:T(8,128)(2,1)S(1)}, bf16[2,192,256]{2,1,0:T(8,128)(2,1)S(1)}, u32[]{:S(2)}, u32[]{:S(2)}) collective-permute-start(bf16[2,192,256]{2,1,0:T(8,128)(2,1)S(1)} %collective-permute-done.4.refs_6_.refs_4_.refs_5_), channel_id=1, source_target_pairs={{0,0},{1,2},{2,1},{3,3},{4,4},{5,6},{6,5},{7,7},{8,8},{9,10},{10,9... | collective-permute-start | bytes 589832 | tf_op jit(solution)/shard_map/halo/ppermute | solution.py:389
  14.2 0.7 %collective-permute-done.1.refs_2_ = bf16[2,192,256]{2,1,0:T(8,128)(2,1)S(1)} collective-permute-done((bf16[2,192,256]{2,1,0:T(8,128)(2,1)S(1)}, bf16[2,192,256]{2,1,0:T(8,128)(2,1)S(1)}, u32[]{:S(2)}, u32[]{:S(2)}) %collective-permute-start.1) | collective-permute-done | bytes 196640 | tf_op jit(solution)/shard_map/halo/ppermute | solution.py:379
  14.9 1.7 %collective-permute-start.5 = (bf16[2,192,256]{2,1,0:T(8,128)(2,1)S(1)}, bf16[2,192,256]{2,1,0:T(8,128)(2,1)S(1)}, u32[]{:S(2)}, u32[]{:S(2)}) collective-permute-start(bf16[2,192,256]{2,1,0:T(8,128)(2,1)S(1)} %collective-permute-done.4.refs_6_.refs_4_.refs_5_), channel_id=1, source_target_pairs={{0,1},{1,0},{2,3},{3,2},{4,5},{5,4},{6,7},{7,6},{8,9},{9,8},{10,11... | collective-permute-start | bytes 589832 | tf_op jit(solution)/shard_map/halo/ppermute | solution.py:389
  16.5 0.0 collective-permute-done.refs_1_
  16.5 0.3 collective-permute-start.7
  16.8 0.0 collective-permute-done.3.refs_5_.refs_3_.refs_6_
  16.8 0.0 collective-permute-done.2.refs_4_.refs_2_
  16.8 2.4 %collective-permute-done.6.refs_8_.refs_6_.refs_7_ = bf16[2,192,256]{2,1,0:T(8,128)(2,1)S(1)} collective-permute-done((bf16[2,192,256]{2,1,0:T(8,128)(2,1)S(1)}, bf16[2,192,256]{2,1,0:T(8,128)(2,1)S(1)}, u32[]{:S(2)}, u32[]{:S(2)}) %collective-permute-start.6) | collective-permute-done | bytes 196640 | tf_op jit(solution)/shard_map/halo/ppermute | solution.py:389
  19.2 0.0 collective-permute-done.5.refs_7_.refs_5_
  19.2 2.4 %attend.2 = (bf16[192,256]{1,0:T(8,128)(2,1)S(1)}, bf16[192,256]{1,0:T(8,128)(2,1)S(1)}, bf16[192,256]{1,0:T(8,128)(2,1)S(1)}, f32[576,128]{1,0:T(8,128)S(1)}) custom-call(bf16[2,192,256]{2,1,0:T(8,128)(2,1)S(1)} %get-tuple-element.40.refs_0_, bf16[2,192,256]{2,1,0:T(8,128)(2,1)S(1)} %collective-permute-done.refs_1_, ...), custom_call_target="tpu_custom_call" | custom-call | flops 5435817984 | bytes 2359296 | tf_op jit(solution)/shard_map/attend/pallas_call | solution.py:342
  21.7 0.8 %collective-permute-start.11 = (bf16[192,256]{1,0:T(8,128)(2,1)S(1)}, bf16[192,256]{1,0:T(8,128)(2,1)S(1)}, u32[]{:S(2)}, u32[]{:S(2)}) collective-permute-start(bf16[192,256]{1,0:T(8,128)(2,1)S(1)} %get-tuple-element.45), channel_id=1, source_target_pairs={{0,16},{8,24},{16,0},{24,8},{1,17},{9,25},{17,1},{25,9},{2,18},{10... | collective-permute-start | bytes 294920 | tf_op jit(solution)/shard_map/merge/ppermute | solution.py:379
  22.4 1.0 %collective-permute-start.12 = (bf16[192,256]{1,0:T(8,128)(2,1)S(1)}, bf16[192,256]{1,0:T(8,128)(2,1)S(1)}, u32[]{:S(2)}, u32[]{:S(2)}) collective-permute-start(bf16[192,256]{1,0:T(8,128)(2,1)S(1)} %get-tuple-element.46), channel_id=1, source_target_pairs={{0,8},{8,0},{16,24},{24,16},{1,9},{9,1},{17,25},{25,17},{2,10},{10... | collective-permute-start | bytes 294920 | tf_op jit(solution)/shard_map/merge/ppermute | solution.py:379
  23.5 0.0 collective-permute-done.7.refs_0_.refs_3_
  23.5 1.0 %attend.3 = (bf16[192,256]{1,0:T(8,128)(2,1)S(1)}, f32[8,768]{1,0:T(8,128)S(1)}) custom-call(bf16[2,192,256]{2,1,0:T(8,128)(2,1)S(1)} %collective-permute-done.7.refs_0_.refs_3_, bf16[2,192,256]{2,1,0:T(8,128)(2,1)S(1)} %get-tuple-element.41.refs_3_.refs_1_.refs_4_, bf16[2,192,256]{2,1,0:T(8,128)(2,1)S(1)} %collective-permute-done.2.refs_4_.refs_2_, ...), custom_call_target="tpu_custom_call" | custom-call | flops 1811939328 | bytes 1794048 | tf_op jit(solution)/shard_map/attend/pallas_call | solution.py:342
  24.5 2.7 %collective-permute-start.10 = (f32[8,768]{1,0:T(8,128)S(1)}, f32[8,768]{1,0:T(8,128)S(1)}, u32[]{:S(2)}, u32[]{:S(2)}) collective-permute-start(f32[8,768]{1,0:T(8,128)S(1)} %get-tuple-element.47.refs_8_), channel_id=1, source_target_pairs={{0,24},{8,16},{16,8},{24,0},{1,25},{9,17},{17,9},{25,1},{2,26},{10... | collective-permute-start | bytes 73736 | tf_op jit(solution)/shard_map/merge/ppermute | solution.py:379
  27.2 0.0 collective-permute-start.9
  27.2 0.9 %collective-permute-start.8 = (f32[8,768]{1,0:T(8,128)S(1)}, f32[8,768]{1,0:T(8,128)S(1)}, u32[]{:S(2)}, u32[]{:S(2)}) collective-permute-start(f32[8,768]{1,0:T(8,128)S(1)} %get-tuple-element.47.refs_8_), channel_id=1, source_target_pairs={{0,8},{8,0},{16,24},{24,16},{1,9},{9,1},{17,25},{25,17},{2,10},{10... | collective-permute-start | bytes 73736 | tf_op jit(solution)/shard_map/merge/ppermute | solution.py:379
  28.1 1.3 %collective-permute-done.10.refs_11_ = f32[8,768]{1,0:T(8,128)S(1)} collective-permute-done((f32[8,768]{1,0:T(8,128)S(1)}, f32[8,768]{1,0:T(8,128)S(1)}, u32[]{:S(2)}, u32[]{:S(2)}) %collective-permute-start.10) | collective-permute-done | bytes 24608 | tf_op jit(solution)/shard_map/merge/ppermute | solution.py:379
  29.4 2.4 %collective-permute-start.13 = (bf16[192,256]{1,0:T(8,128)(2,1)S(1)}, bf16[192,256]{1,0:T(8,128)(2,1)S(1)}, u32[]{:S(2)}, u32[]{:S(2)}) collective-permute-start(bf16[192,256]{1,0:T(8,128)(2,1)S(1)} %get-tuple-element.57), channel_id=1, source_target_pairs={{0,24},{8,16},{16,8},{24,0},{1,25},{9,17},{17,9},{25,1},{2,26},{10... | collective-permute-start | bytes 294920 | tf_op jit(solution)/shard_map/merge/ppermute | solution.py:379
  31.8 0.0 collective-permute-done.9.refs_10_
  31.8 0.0 collective-permute-done.8.refs_9_
  31.8 0.0 collective-permute-done.11.refs_2_
  31.8 0.0 collective-permute-done.12.refs_3_
  31.8 3.1 %gradients.2 = (f32[2,128,768]{2,1,0:T(8,128)S(1)}, f32[2,768]{1,0:T(2,128)S(1)}, f32[2,768]{1,0:T(2,128)S(1)}, f32[192,128]{1,0:T(8,128)S(1)}, bf16[2,2,192,256...) custom-call(bf16[2,192,256]{2,1,0:T(8,128)(2,1)S(1)} %get-tuple-element.40.refs_0_, ...), custom_call_target="tpu_custom_call" | custom-call | flops 12079595520 | bytes 3354624 | tf_op jit(solution)/shard_map/gradients/pallas_call | solution.py:342
  34.9 2.2 %collective-permute-start.17 = (bf16[2,2,192,256]{3,2,1,0:T(8,128)(2,1)S(1)}, bf16[2,2,192,256]{3,2,1,0:T(8,128)(2,1)S(1)}, u32[]{:S(2)}, u32[]{:S(2)}) collective-permute-start(bf16[2,2,192,256]{3,2,1,0:T(8,128)(2,1)S(1)} %get-tuple-element.72), channel_id=1, source_target_pairs={{0,1},{1,0},{2,3},{3,2},{4,5},{5,4},{6,7},{7,6},{8,9},{9,8},{10,11... | collective-permute-start | bytes 1179656 | tf_op jit(solution)/shard_map/gradients/ppermute | solution.py:444
  37.1 3.7 %collective-permute-start.18 = (bf16[2,2,192,256]{3,2,1,0:T(8,128)(2,1)S(1)}, bf16[2,2,192,256]{3,2,1,0:T(8,128)(2,1)S(1)}, u32[]{:S(2)}, u32[]{:S(2)}) collective-permute-start(bf16[2,2,192,256]{3,2,1,0:T(8,128)(2,1)S(1)} %get-tuple-element.73), channel_id=1, source_target_pairs={{0,0},{1,2},{2,1},{3,3},{4,4},{5,6},{6,5},{7,7},{8,8},{9,10},{10,9... | collective-permute-start | bytes 1179656 | tf_op jit(solution)/shard_map/gradients/ppermute | solution.py:444
  40.8 1.7 %gradients.3 = (bf16[192,256]{1,0:T(8,128)(2,1)S(1)}, bf16[192,256]{1,0:T(8,128)(2,1)S(1)}, bf16[192,256]{1,0:T(8,128)(2,1)S(1)}, bf16[192,256]{1,0:T(8,128)(2,1)S(1)}, bf16[2,2,192,256]{3,2,1,0:T(8,128)(2,1)S(1)}) custom-call(bf16[2,192,256]{2,1,0:T(8,128)(2,1)S(1)} %get-tuple-element.40.refs_0_, bf16[2,192,256]{2,1,0:T(8,128)(2,1)S(1)} %collective-permute-done.refs_1_, ...), custom_call_target="tpu_custom_call" | custom-call | flops 6039797760 | bytes 2764800 | tf_op jit(solution)/shard_map/gradients/pallas_call | solution.py:342
  42.5 0.0 collective-permute-done.13.refs_1_
  42.5 0.3 collective-permute-start.14
  42.8 0.8 %collective-permute-start.15 = (bf16[192,256]{1,0:T(8,128)(2,1)S(1)}, bf16[192,256]{1,0:T(8,128)(2,1)S(1)}, u32[]{:S(2)}, u32[]{:S(2)}) collective-permute-start(bf16[192,256]{1,0:T(8,128)(2,1)S(1)} %get-tuple-element.65), channel_id=1, source_target_pairs={{0,16},{8,24},{16,0},{24,8},{1,17},{9,25},{17,1},{25,9},{2,18},{10... | collective-permute-start | bytes 294920 | tf_op jit(solution)/shard_map/return/ppermute | solution.py:379
  43.7 2.4 %collective-permute-start.16 = (bf16[192,256]{1,0:T(8,128)(2,1)S(1)}, bf16[192,256]{1,0:T(8,128)(2,1)S(1)}, u32[]{:S(2)}, u32[]{:S(2)}) collective-permute-start(bf16[192,256]{1,0:T(8,128)(2,1)S(1)} %get-tuple-element.66), channel_id=1, source_target_pairs={{0,8},{8,0},{16,24},{24,16},{1,9},{9,1},{17,25},{25,17},{2,10},{10... | collective-permute-start | bytes 294920 | tf_op jit(solution)/shard_map/return/ppermute | solution.py:379
  46.1 0.0 collective-permute-done.17.refs_1_
  46.1 0.4 collective-permute-done.18.refs_2_
  46.6 0.1 fusion
  46.6 0.3 collective-permute-start.19
  47.0 1.6 %collective-permute-done.14.refs_5_ = bf16[192,256]{1,0:T(8,128)(2,1)S(1)} collective-permute-done((bf16[192,256]{1,0:T(8,128)(2,1)S(1)}, bf16[192,256]{1,0:T(8,128)(2,1)S(1)}, u32[]{:S(2)}, u32[]{:S(2)}) %collective-permute-start.14) | collective-permute-done | bytes 98336 | tf_op jit(solution)/shard_map/return/ppermute | solution.py:379
  48.6 3.1 %collective-permute-done.15.refs_6_ = bf16[192,256]{1,0:T(8,128)(2,1)S(1)} collective-permute-done((bf16[192,256]{1,0:T(8,128)(2,1)S(1)}, bf16[192,256]{1,0:T(8,128)(2,1)S(1)}, u32[]{:S(2)}, u32[]{:S(2)}) %collective-permute-start.15) | collective-permute-done | bytes 98336 | tf_op jit(solution)/shard_map/return/ppermute | solution.py:379
  51.6 0.0 collective-permute-done.16.refs_7_
  51.6 1.0 %finish.2 = (bf16[192,256]{1,0:T(8,128)(2,1)}, bf16[192,256]{1,0:T(8,128)(2,1)}) custom-call(bf16[192,256]{1,0:T(8,128)(2,1)S(1)} %get-tuple-element.42.refs_0_, bf16[192,256]{1,0:T(8,128)(2,1)S(1)} %collective-permute-done.13.refs_1_, bf16[192,256]{1,0:T(8,128)(2,1)S(1)} %collective-permute-done.11.refs_2_, ...), custom_call_target="tpu_custom_call" | custom-call | flops 9059696640 | bytes 1376256 | tf_op jit(solution)/shard_map/finish/pallas_call | solution.py:342
  52.7 0.0 collective-permute-done.19.refs_3_
  52.7 0.9 %finish.3 = (bf16[192,256]{1,0:T(8,128)(2,1)}, bf16[192,256]{1,0:T(8,128)(2,1)}) custom-call(bf16[2,2,192,256]{3,2,1,0:T(8,128)(2,1)S(1)} %get-tuple-element.71.refs_0_, bf16[2,2,192,256]{3,2,1,0:T(8,128)(2,1)S(1)} %collective-permute-done.17.refs_1_, bf16[2,2,192,256]{3,2,1,0:T(8,128)(2,1)S(1)} %collective-permute-done.18.refs_2_, ...), custom_call_target="tpu_custom_call" | custom-call | bytes 1867776 | tf_op jit(solution)/shard_map/finish/pallas_call | solution.py:342
Async XLA Ops:
  1.9 10.3 %collective-permute-start.4 = (bf16[2,192,256]{2,1,0:T(8,128)(2,1)S(1)}, bf16[2,192,256]{2,1,0:T(8,128)(2,1)S(1)}, u32[]{:S(2)}, u32[]{:S(2)}) collective-permute-start(bf16[2,192,256]{2,1,0:T(8,128)(2,1)S(1)} %get-tuple-element.41.refs_3_.refs_1_.refs_4_), channel_id=1, source_target_pairs={{0,4},{4,0},{1,5},{5,1},{2,6},{6,2},{3,7},{7,3},{8,12},{12,8},{9,1... | collective-permute-start | bytes 589832 | tf_op jit(solution)/shard_map/halo/ppermute | solution.py:384
  4.0 10.9 %collective-permute-start.1 = (bf16[2,192,256]{2,1,0:T(8,128)(2,1)S(1)}, bf16[2,192,256]{2,1,0:T(8,128)(2,1)S(1)}, u32[]{:S(2)}, u32[]{:S(2)}) collective-permute-start(bf16[2,192,256]{2,1,0:T(8,128)(2,1)S(1)} %get-tuple-element.40.refs_0_), channel_id=1, source_target_pairs={{0,16},{8,24},{16,0},{24,8},{1,17},{9,25},{17,1},{25,9},{2,18},{10... | collective-permute-start | bytes 589832 | tf_op jit(solution)/shard_map/halo/ppermute | solution.py:379
  6.3 10.2 %collective-permute-start = (bf16[2,192,256]{2,1,0:T(8,128)(2,1)S(1)}, bf16[2,192,256]{2,1,0:T(8,128)(2,1)S(1)}, u32[]{:S(2)}, u32[]{:S(2)}) collective-permute-start(bf16[2,192,256]{2,1,0:T(8,128)(2,1)S(1)} %get-tuple-element.40.refs_0_), channel_id=1, source_target_pairs={{0,8},{8,0},{16,24},{24,16},{1,9},{9,1},{17,25},{25,17},{2,10},{10... | collective-permute-start | bytes 589832 | tf_op jit(solution)/shard_map/halo/ppermute | solution.py:379
  7.6 9.2 %collective-permute-start.3 = (bf16[2,192,256]{2,1,0:T(8,128)(2,1)S(1)}, bf16[2,192,256]{2,1,0:T(8,128)(2,1)S(1)}, u32[]{:S(2)}, u32[]{:S(2)}) collective-permute-start(bf16[2,192,256]{2,1,0:T(8,128)(2,1)S(1)} %get-tuple-element.41.refs_3_.refs_1_.refs_4_), channel_id=1, source_target_pairs={{0,0},{1,2},{2,1},{3,3},{4,4},{5,6},{6,5},{7,7},{8,8},{9,10},{10,9... | collective-permute-start | bytes 589832 | tf_op jit(solution)/shard_map/halo/ppermute | solution.py:389
  12.2 4.7 %collective-permute-start.2 = (bf16[2,192,256]{2,1,0:T(8,128)(2,1)S(1)}, bf16[2,192,256]{2,1,0:T(8,128)(2,1)S(1)}, u32[]{:S(2)}, u32[]{:S(2)}) collective-permute-start(bf16[2,192,256]{2,1,0:T(8,128)(2,1)S(1)} %get-tuple-element.41.refs_3_.refs_1_.refs_4_), channel_id=1, source_target_pairs={{0,1},{1,0},{2,3},{3,2},{4,5},{5,4},{6,7},{7,6},{8,9},{9,8},{10,11... | collective-permute-start | bytes 589832 | tf_op jit(solution)/shard_map/halo/ppermute | solution.py:389
  12.2 7.0 %collective-permute-start.6 = (bf16[2,192,256]{2,1,0:T(8,128)(2,1)S(1)}, bf16[2,192,256]{2,1,0:T(8,128)(2,1)S(1)}, u32[]{:S(2)}, u32[]{:S(2)}) collective-permute-start(bf16[2,192,256]{2,1,0:T(8,128)(2,1)S(1)} %collective-permute-done.4.refs_6_.refs_4_.refs_5_), channel_id=1, source_target_pairs={{0,0},{1,2},{2,1},{3,3},{4,4},{5,6},{6,5},{7,7},{8,8},{9,10},{10,9... | collective-permute-start | bytes 589832 | tf_op jit(solution)/shard_map/halo/ppermute | solution.py:389
  14.9 4.4 %collective-permute-start.5 = (bf16[2,192,256]{2,1,0:T(8,128)(2,1)S(1)}, bf16[2,192,256]{2,1,0:T(8,128)(2,1)S(1)}, u32[]{:S(2)}, u32[]{:S(2)}) collective-permute-start(bf16[2,192,256]{2,1,0:T(8,128)(2,1)S(1)} %collective-permute-done.4.refs_6_.refs_4_.refs_5_), channel_id=1, source_target_pairs={{0,1},{1,0},{2,3},{3,2},{4,5},{5,4},{6,7},{7,6},{8,9},{9,8},{10,11... | collective-permute-start | bytes 589832 | tf_op jit(solution)/shard_map/halo/ppermute | solution.py:389
  16.5 7.0 %collective-permute-start.7 = (bf16[2,192,256]{2,1,0:T(8,128)(2,1)S(1)}, bf16[2,192,256]{2,1,0:T(8,128)(2,1)S(1)}, u32[]{:S(2)}, u32[]{:S(2)}) collective-permute-start(bf16[2,192,256]{2,1,0:T(8,128)(2,1)S(1)} %collective-permute-done.1.refs_2_), channel_id=1, source_target_pairs={{0,8},{8,0},{16,24},{24,16},{1,9},{9,1},{17,25},{25,17},{2,10},{10... | collective-permute-start | bytes 589832 | tf_op jit(solution)/shard_map/halo/ppermute | solution.py:379
  21.7 10.1 %collective-permute-start.11 = (bf16[192,256]{1,0:T(8,128)(2,1)S(1)}, bf16[192,256]{1,0:T(8,128)(2,1)S(1)}, u32[]{:S(2)}, u32[]{:S(2)}) collective-permute-start(bf16[192,256]{1,0:T(8,128)(2,1)S(1)} %get-tuple-element.45), channel_id=1, source_target_pairs={{0,16},{8,24},{16,0},{24,8},{1,17},{9,25},{17,1},{25,9},{2,18},{10... | collective-permute-start | bytes 294920 | tf_op jit(solution)/shard_map/merge/ppermute | solution.py:379
  22.4 9.4 %collective-permute-start.12 = (bf16[192,256]{1,0:T(8,128)(2,1)S(1)}, bf16[192,256]{1,0:T(8,128)(2,1)S(1)}, u32[]{:S(2)}, u32[]{:S(2)}) collective-permute-start(bf16[192,256]{1,0:T(8,128)(2,1)S(1)} %get-tuple-element.46), channel_id=1, source_target_pairs={{0,8},{8,0},{16,24},{24,16},{1,9},{9,1},{17,25},{25,17},{2,10},{10... | collective-permute-start | bytes 294920 | tf_op jit(solution)/shard_map/merge/ppermute | solution.py:379
  24.5 4.9 %collective-permute-start.10 = (f32[8,768]{1,0:T(8,128)S(1)}, f32[8,768]{1,0:T(8,128)S(1)}, u32[]{:S(2)}, u32[]{:S(2)}) collective-permute-start(f32[8,768]{1,0:T(8,128)S(1)} %get-tuple-element.47.refs_8_), channel_id=1, source_target_pairs={{0,24},{8,16},{16,8},{24,0},{1,25},{9,17},{17,9},{25,1},{2,26},{10... | collective-permute-start | bytes 73736 | tf_op jit(solution)/shard_map/merge/ppermute | solution.py:379
  27.2 4.6 %collective-permute-start.9 = (f32[8,768]{1,0:T(8,128)S(1)}, f32[8,768]{1,0:T(8,128)S(1)}, u32[]{:S(2)}, u32[]{:S(2)}) collective-permute-start(f32[8,768]{1,0:T(8,128)S(1)} %get-tuple-element.47.refs_8_), channel_id=1, source_target_pairs={{0,16},{8,24},{16,0},{24,8},{1,17},{9,25},{17,1},{25,9},{2,18},{10... | collective-permute-start | bytes 73736 | tf_op jit(solution)/shard_map/merge/ppermute | solution.py:379
  27.2 4.6 %collective-permute-start.8 = (f32[8,768]{1,0:T(8,128)S(1)}, f32[8,768]{1,0:T(8,128)S(1)}, u32[]{:S(2)}, u32[]{:S(2)}) collective-permute-start(f32[8,768]{1,0:T(8,128)S(1)} %get-tuple-element.47.refs_8_), channel_id=1, source_target_pairs={{0,8},{8,0},{16,24},{24,16},{1,9},{9,1},{17,25},{25,17},{2,10},{10... | collective-permute-start | bytes 73736 | tf_op jit(solution)/shard_map/merge/ppermute | solution.py:379
  29.4 13.1 %collective-permute-start.13 = (bf16[192,256]{1,0:T(8,128)(2,1)S(1)}, bf16[192,256]{1,0:T(8,128)(2,1)S(1)}, u32[]{:S(2)}, u32[]{:S(2)}) collective-permute-start(bf16[192,256]{1,0:T(8,128)(2,1)S(1)} %get-tuple-element.57), channel_id=1, source_target_pairs={{0,24},{8,16},{16,8},{24,0},{1,25},{9,17},{17,9},{25,1},{2,26},{10... | collective-permute-start | bytes 294920 | tf_op jit(solution)/shard_map/merge/ppermute | solution.py:379
  34.9 11.2 %collective-permute-start.17 = (bf16[2,2,192,256]{3,2,1,0:T(8,128)(2,1)S(1)}, bf16[2,2,192,256]{3,2,1,0:T(8,128)(2,1)S(1)}, u32[]{:S(2)}, u32[]{:S(2)}) collective-permute-start(bf16[2,2,192,256]{3,2,1,0:T(8,128)(2,1)S(1)} %get-tuple-element.72), channel_id=1, source_target_pairs={{0,1},{1,0},{2,3},{3,2},{4,5},{5,4},{6,7},{7,6},{8,9},{9,8},{10,11... | collective-permute-start | bytes 1179656 | tf_op jit(solution)/shard_map/gradients/ppermute | solution.py:444
  37.1 9.4 %collective-permute-start.18 = (bf16[2,2,192,256]{3,2,1,0:T(8,128)(2,1)S(1)}, bf16[2,2,192,256]{3,2,1,0:T(8,128)(2,1)S(1)}, u32[]{:S(2)}, u32[]{:S(2)}) collective-permute-start(bf16[2,2,192,256]{3,2,1,0:T(8,128)(2,1)S(1)} %get-tuple-element.73), channel_id=1, source_target_pairs={{0,0},{1,2},{2,1},{3,3},{4,4},{5,6},{6,5},{7,7},{8,8},{9,10},{10,9... | collective-permute-start | bytes 1179656 | tf_op jit(solution)/shard_map/gradients/ppermute | solution.py:444
  42.5 6.1 %collective-permute-start.14 = (bf16[192,256]{1,0:T(8,128)(2,1)S(1)}, bf16[192,256]{1,0:T(8,128)(2,1)S(1)}, u32[]{:S(2)}, u32[]{:S(2)}) collective-permute-start(bf16[192,256]{1,0:T(8,128)(2,1)S(1)} %get-tuple-element.64), channel_id=1, source_target_pairs={{0,24},{8,16},{16,8},{24,0},{1,25},{9,17},{17,9},{25,1},{2,26},{10... | collective-permute-start | bytes 294920 | tf_op jit(solution)/shard_map/return/ppermute | solution.py:379
  42.8 8.8 %collective-permute-start.15 = (bf16[192,256]{1,0:T(8,128)(2,1)S(1)}, bf16[192,256]{1,0:T(8,128)(2,1)S(1)}, u32[]{:S(2)}, u32[]{:S(2)}) collective-permute-start(bf16[192,256]{1,0:T(8,128)(2,1)S(1)} %get-tuple-element.65), channel_id=1, source_target_pairs={{0,16},{8,24},{16,0},{24,8},{1,17},{9,25},{17,1},{25,9},{2,18},{10... | collective-permute-start | bytes 294920 | tf_op jit(solution)/shard_map/return/ppermute | solution.py:379
  43.7 8.0 %collective-permute-start.16 = (bf16[192,256]{1,0:T(8,128)(2,1)S(1)}, bf16[192,256]{1,0:T(8,128)(2,1)S(1)}, u32[]{:S(2)}, u32[]{:S(2)}) collective-permute-start(bf16[192,256]{1,0:T(8,128)(2,1)S(1)} %get-tuple-element.66), channel_id=1, source_target_pairs={{0,8},{8,0},{16,24},{24,16},{1,9},{9,1},{17,25},{25,17},{2,10},{10... | collective-permute-start | bytes 294920 | tf_op jit(solution)/shard_map/return/ppermute | solution.py:379
  46.6 6.0 %collective-permute-start.19 = (bf16[2,192,256]{2,1,0:T(8,128)(2,1)S(1)}, bf16[2,192,256]{2,1,0:T(8,128)(2,1)S(1)}, u32[]{:S(2)}, u32[]{:S(2)}) collective-permute-start(bf16[2,192,256]{2,1,0:T(8,128)(2,1)S(1)} %fusion), channel_id=1, source_target_pairs={{0,4},{4,0},{1,5},{5,1},{2,6},{6,2},{3,7},{7,3},{8,12},{12,8},{9,1... | collective-permute-start | bytes 589832 | tf_op jit(solution)/shard_map/return/ppermute | solution.py:453

commit v9 on v8

--- a/solution.py
+++ b/solution.py
@@ -98,8 +98,8 @@
 
 
 def rotate_kernel(
-    dims, begins, q_hbm, k_hbm, v_hbm, g_hbm, table_hbm, kv_ref, qg_ref, rope_ref, q_ref, k_ref,
-    table_ref, sems,
+    dims, begins, q_hbm, k_hbm, v_hbm, g_hbm, table_hbm, kv_ref, qg_ref, turned_ref, rope_ref,
+    q_ref, k_ref, table_ref, sems,
 ):
     moves = [
         (table_hbm, table_ref),
@@ -119,7 +119,10 @@
         copy.wait()
         for head in range(HEADS):
             cut = head_slice(head)
-            target[0, :, cut] = turn(source[:, cut].astype(F32), *tables, 1.0).astype(BF16)
+            turned = turn(source[:, cut].astype(F32), *tables, 1.0).astype(BF16)
+            target[0, :, cut] = turned
+            if target is qg_ref:
+                turned_ref[:, cut] = turned
     copies[3].wait()
     copies[4].wait()
 
@@ -145,11 +148,24 @@
     return None if valid is None else jnp.where(valid, 0.0, NEGATIVE).astype(F32)
 
 
+def query_views(refs):
+    qg_ref, qg1_ref, q2_ref, g2_ref, q3_ref, g3_ref = refs
+    return (
+        [qg_ref.at[0], qg1_ref.at[0], q2_ref, q3_ref],
+        [qg_ref.at[1], qg1_ref.at[1], g2_ref, g3_ref],
+    )
+
+
 def forward_kernel(groups, sizes, cells, count, last, *refs):
     tile_count = sum(len(members) for _, members in groups)
-    qg_refs = refs[:count]
-    kv_refs = refs[count : count + tile_count]
-    rest = refs[count + tile_count :]
+    if last:
+        q_refs, g_refs, refs = refs[:1], refs[1:2], refs[2:]
+    else:
+        qg_ref, qg1_ref, q2_ref, g2_ref = refs[:4]
+        q_refs = [qg_ref.at[0], qg1_ref.at[0], q2_ref]
+        g_refs = [qg_ref.at[1], qg1_ref.at[1], g2_ref]
+        refs = refs[4:]
+    kv_refs, rest = refs[:tile_count], refs[tile_count:]
     if last:
         first_ref, rest = rest[0], rest[1:]
     o_refs = rest[:count]
@@ -168,7 +184,7 @@
 
     def scores_of(head):
         cut = head_slice(head)
-        query = jnp.concatenate([ref[0, :, cut] for ref in qg_refs], axis=0)
+        query = jnp.concatenate([ref[:, cut] for ref in q_refs], axis=0)
         return [dot_nt(query, key_buf[lo:hi, cut]) for lo, hi, _ in spans]
 
     ahead = scores_of(0)
@@ -193,7 +209,7 @@
             total = part if total is None else total + part
             out = piece if out is None else out + piece
         out = out * (1.0 / total)
-        grad = jnp.concatenate([ref[1, :, cut] for ref in qg_refs], axis=0)
+        grad = jnp.concatenate([ref[:, cut] for ref in g_refs], axis=0)
         dotted = jnp.sum(out * grad.astype(F32), axis=1, keepdims=True)
         out = out.astype(BF16)
         for i, o_ref in enumerate(o_refs):
@@ -233,9 +249,9 @@
 
 def backward_kernel(cols, grid_rows, sizes, cells, first, last, *refs):
     tile_count = grid_rows * len(cols)
-    qg_refs = refs[:4]
-    kv_refs = refs[4 : 4 + tile_count]
-    rest = refs[4 + tile_count :]
+    q_refs, g_refs = query_views(refs[:6])
+    kv_refs = refs[6 : 6 + tile_count]
+    rest = refs[6 + tile_count :]
     if first:
         stat_refs, rest = rest[:4], rest[4:]
     else:
@@ -266,8 +282,8 @@
     def products_of(head, slot):
         cut = head_slice(head)
         at = slice(slot * span, (slot + 1) * span)
-        queries = jnp.concatenate([ref[0, :, cut] for ref in qg_refs], axis=0)
-        grads = jnp.concatenate([ref[1, :, cut] for ref in qg_refs], axis=0)
+        queries = jnp.concatenate([ref[:, cut] for ref in q_refs], axis=0)
+        grads = jnp.concatenate([ref[:, cut] for ref in g_refs], axis=0)
         raw = dot_nt(key_buf[at, cut], queries)
         return raw, dot_nt(value_buf[at, cut], grads), queries, grads
 
@@ -366,9 +382,9 @@
         return jax.ShapeDtypeStruct(shape, F32)
 
     with jax.named_scope("rotate"):
-        kv, qg, rope = call(
+        kv, qg, turned, rope = call(
             functools.partial(rotate_kernel, dims, begins),
-            (pair, pair, real(3, cells, DH)),
+            (pair, pair, plain, real(3, cells, DH)),
             [pltpu.with_memory_space_constraint(x, pltpu.HBM) for x in (*flat, jnp.asarray(table))],
             scratch=[pltpu.VMEM((cells, chan), BF16)] * 2
             + [pltpu.VMEM(table.shape, F32), pltpu.SemaphoreType.DMA((5,))],
@@ -382,12 +398,14 @@
     col_sides = side_pairs(sizes["wa"])
     with jax.named_scope("halo"):
         kv_rows = [kv] + [lax.ppermute(kv, "ha", pairs) for pairs in row_sides]
-        qg2 = other_frames(qg, 2)
+        g2 = other_frames(flat[3], 2)
+        q2 = other_frames(turned, 2)
         qg1 = other_frames(qg, 1)
         tiles = []
         for block in kv_rows:
             tiles.append([block] + [lax.ppermute(block, "wa", pairs) for pairs in col_sides])
-        qg3 = other_frames(qg2, 1)
+        g3 = other_frames(g2, 1)
+        q3 = other_frames(q2, 1)
     grid_rows, grid_cols = 1 + len(row_sides), 1 + len(col_sides)
     flat_tiles = [tiles[row][col] for row in range(grid_rows) for col in range(grid_cols)]
     groups = {}
@@ -400,7 +418,7 @@
     product = 2 * cells * key_count * DH * HEADS
 
     def forward(blocks, first):
-        count = len(blocks)
+        count = 3 if first is None else 1
         stat = (count * cells, DH) if first is None else (8, 4 * cells)
         return call(
             functools.partial(forward_kernel, groups, sizes, cells, count, first is not None),
@@ -412,14 +430,13 @@
         )
 
     with jax.named_scope("attend"):
-        o0, o1, o2, first = forward((qg, qg1, qg2), None)
-        o3, stat = forward((qg3,), first)
+        o0, o1, o2, first = forward((qg, qg1, q2, g2), None)
+        o3, stat = forward((q3, g3), first)
     with jax.named_scope("merge"):
         stats = [stat] + [other_frames(stat, d) for d in (1, 2, 3)]
         outs = [other_frames(o, d) for d, o in ((3, o3), (2, o2), (1, o1))]
-        stats, outs[1:] = lax.optimization_barrier((stats, outs[1:]))
-
-    queries = (qg, qg1, qg2, qg3)
+
+    queries = (qg, qg1, q2, g2, q3, g3)
     col_shape = jax.ShapeDtypeStruct((grid_rows, 2, cells, chan), BF16)
 
     def gradients(which, carried):

time: 53.7 us -> 57.6 us (1.073); the launches traced: 53.5 us -> 56.8 us
  starting transfers between devices: 31.8 us -> 35.3 us
    ppermute x12 -> x14, starting transfers between devices: 15.3 us -> 17.7 us  [other_frames(): lax.ppermute(x, 'ta', [(i, i ^ distance) for i in range(sizes['ta'])])]
    ppermute x4, starting transfers between devices: 8.2 us -> 10.5 us  [shards(): lax.ppermute(block, 'wa', pairs)]
    ppermute x12 -> x14, waiting for transfers between devices: 6.72 us -> 4.63 us  [other_frames(): lax.ppermute(x, 'ta', [(i, i ^ distance) for i in range(sizes['ta'])])]
    ppermute x2, waiting for transfers between devices: 0.44 us -> 2.14 us  [shards(): sides = [lax.ppermute(x, 'wa', pairs) for x, pairs in zip(sides, col_sides)]]
    ppermute x2, starting transfers between devices: 5.88 us -> 4.63 us  [shards(): sides = [lax.ppermute(x, 'wa', pairs) for x, pairs in zip(sides, col_sides)]]
  transfers between devices with their start and end apart: 20 -> 22, of which waited for: 6 -> 5; matrix products, arithmetic and copies ran while one was open for 0% -> 0% of each run, Pallas kernels for 17% -> 15%
where the time goes in v9:
time: 57.6 us; the launch traced here: 56.8 us
  starting transfers between devices  35.3 us (61%)
  Pallas kernels  11.4 us (20%)
  waiting for transfers between devices  9.31 us (16%)
  between operations  0.76 us (1%)
    ppermute x14, starting transfers between devices, other_frames(): lax.ppermute(x, 'ta', [(i, i ^ distance) for i in range(sizes['ta'])])  17.7 us
    pallas_call x7, Pallas kernels, call(): pl.pallas_call(kernel, out_shape=out_shape, in_specs=[pl.BlockSpec(memory...  11.4 us
    ppermute x4, starting transfers between devices, shards(): lax.ppermute(block, 'wa', pairs)  10.5 us
    ppermute x2, starting transfers between devices, shards(): sides = [lax.ppermute(x, 'wa', pairs) for x, pairs in zip(sides, col_sides)]  4.63 us
    ppermute x14, waiting for transfers between devices, other_frames(): lax.ppermute(x, 'ta', [(i, i ^ distance) for i in range(sizes['ta'])])  4.63 us
    ppermute x4, waiting for transfers between devices, shards(): lax.ppermute(block, 'wa', pairs)  2.54 us
    ppermute x2, waiting for transfers between devices, shards(): sides = [lax.ppermute(x, 'wa', pairs) for x, pairs in zip(sides, col_sides)]  2.14 us
    ppermute x1, starting transfers between devices, shards(): kv_rows = [kv] + [lax.ppermute(kv, 'ha', pairs) for pairs in row_sides]  2.11 us
  transfers between devices with their start and end apart: 22, of which 5 were waited for; matrix products, arithmetic and copies ran while one was open for 0% of the time, Pallas kernels for 15%

profile of v9, /device:TPU:1, one launch (start us, length us, event | category | flops | bytes accessed | tf_op | source)
XLA Modules:
  0.0 56.8 jit_solution(16475756280049931187)
XLA Ops:
  0.6 0.0 copy-start
  0.6 1.3 %rotate.1 = (bf16[2,192,256]{2,1,0:T(8,128)(2,1)S(1)}, bf16[2,192,256]{2,1,0:T(8,128)(2,1)S(1)}, bf16[192,256]{1,0:T(8,128)(2,1)S(1)}, f32[3,192,128]{2,1,0:T(8,128)S(1)}) custom-call(bf16[192,256]{1,0:T(8,128)(2,1)} %bitcast.10, bf16[192,256]{1,0:T(8,128)(2,1)} %bitcast.11, bf16[192,256]{1,0:T(8,128)(2,1)} %bitcast.12, bf16[192,256]{1,0:T(8,128)(2,1)} %bitcast.13, ...), custom_call_target="tpu_custom_call" | custom-call | bytes 1277952 | tf_op jit(solution)/shard_map/rotate/pallas_call | solution.py:358
  1.9 2.1 %collective-permute-start.5 = (bf16[2,192,256]{2,1,0:T(8,128)(2,1)S(1)}, bf16[2,192,256]{2,1,0:T(8,128)(2,1)S(1)}, u32[]{:S(2)}, u32[]{:S(2)}) collective-permute-start(bf16[2,192,256]{2,1,0:T(8,128)(2,1)S(1)} %get-tuple-element.37.refs_4_.refs_2_.refs_6_), channel_id=1, source_target_pairs={{0,4},{4,0},{1,5},{5,1},{2,6},{6,2},{3,7},{7,3},{8,12},{12,8},{9,1... | collective-permute-start | bytes 589832 | tf_op jit(solution)/shard_map/halo/ppermute | solution.py:400
  4.0 0.0 copy-done
  4.0 2.3 %collective-permute-start.2 = (bf16[192,256]{1,0:T(8,128)(2,1)S(1)}, bf16[192,256]{1,0:T(8,128)(2,1)S(1)}, u32[]{:S(2)}, u32[]{:S(2)}) collective-permute-start(bf16[192,256]{1,0:T(8,128)(2,1)S(1)} %bitcast.14), channel_id=1, source_target_pairs={{0,16},{8,24},{16,0},{24,8},{1,17},{9,25},{17,1},{25,9},{2,18},{10... | collective-permute-start | bytes 294920 | tf_op jit(solution)/shard_map/halo/ppermute | solution.py:395
  6.4 0.1 collective-permute-start.1
  6.4 4.5 %collective-permute-start.4 = (bf16[2,192,256]{2,1,0:T(8,128)(2,1)S(1)}, bf16[2,192,256]{2,1,0:T(8,128)(2,1)S(1)}, u32[]{:S(2)}, u32[]{:S(2)}) collective-permute-start(bf16[2,192,256]{2,1,0:T(8,128)(2,1)S(1)} %get-tuple-element.37.refs_4_.refs_2_.refs_6_), channel_id=1, source_target_pairs={{0,0},{1,2},{2,1},{3,3},{4,4},{5,6},{6,5},{7,7},{8,8},{9,10},{10,9... | collective-permute-start | bytes 589832 | tf_op jit(solution)/shard_map/halo/ppermute | solution.py:406
  11.0 1.4 %collective-permute-start = (bf16[2,192,256]{2,1,0:T(8,128)(2,1)S(1)}, bf16[2,192,256]{2,1,0:T(8,128)(2,1)S(1)}, u32[]{:S(2)}, u32[]{:S(2)}) collective-permute-start(bf16[2,192,256]{2,1,0:T(8,128)(2,1)S(1)} %get-tuple-element.35.refs_0_), channel_id=1, source_target_pairs={{0,8},{8,0},{16,24},{24,16},{1,9},{9,1},{17,25},{25,17},{2,10},{10... | collective-permute-start | bytes 589832 | tf_op jit(solution)/shard_map/halo/ppermute | solution.py:395
  12.3 0.0 collective-permute-done.2.refs_3_
  12.3 3.0 %collective-permute-start.3 = (bf16[2,192,256]{2,1,0:T(8,128)(2,1)S(1)}, bf16[2,192,256]{2,1,0:T(8,128)(2,1)S(1)}, u32[]{:S(2)}, u32[]{:S(2)}) collective-permute-start(bf16[2,192,256]{2,1,0:T(8,128)(2,1)S(1)} %get-tuple-element.37.refs_4_.refs_2_.refs_6_), channel_id=1, source_target_pairs={{0,1},{1,0},{2,3},{3,2},{4,5},{5,4},{6,7},{7,6},{8,9},{9,8},{10,11... | collective-permute-start | bytes 589832 | tf_op jit(solution)/shard_map/halo/ppermute | solution.py:406
  15.3 0.0 collective-permute-done.5.refs_7_.refs_5_
  15.3 2.9 %collective-permute-start.7 = (bf16[2,192,256]{2,1,0:T(8,128)(2,1)S(1)}, bf16[2,192,256]{2,1,0:T(8,128)(2,1)S(1)}, u32[]{:S(2)}, u32[]{:S(2)}) collective-permute-start(bf16[2,192,256]{2,1,0:T(8,128)(2,1)S(1)} %collective-permute-done.5.refs_7_.refs_5_), channel_id=1, source_target_pairs={{0,0},{1,2},{2,1},{3,3},{4,4},{5,6},{6,5},{7,7},{8,8},{9,10},{10,9... | collective-permute-start | bytes 589832 | tf_op jit(solution)/shard_map/halo/ppermute | solution.py:406
  18.2 0.0 collective-permute-done.1.refs_2_
  18.2 0.1 collective-permute-start.6
  18.3 0.3 collective-permute-done.refs_1_
  18.6 0.0 collective-permute-start.9
  18.6 0.0 collective-permute-done.4.refs_6_.refs_4_.refs_8_
  18.6 1.5 %collective-permute-start.8 = (bf16[192,256]{1,0:T(8,128)(2,1)S(1)}, bf16[192,256]{1,0:T(8,128)(2,1)S(1)}, u32[]{:S(2)}, u32[]{:S(2)}) collective-permute-start(bf16[192,256]{1,0:T(8,128)(2,1)S(1)} %collective-permute-done.1.refs_2_), channel_id=1, source_target_pairs={{0,8},{8,0},{16,24},{24,16},{1,9},{9,1},{17,25},{25,17},{2,10},{10... | collective-permute-start | bytes 294920 | tf_op jit(solution)/shard_map/halo/ppermute | solution.py:395
  20.1 0.0 collective-permute-done.3.refs_5_.refs_3_.refs_6_
  20.1 2.5 %collective-permute-done.7.refs_9_.refs_7_ = bf16[2,192,256]{2,1,0:T(8,128)(2,1)S(1)} collective-permute-done((bf16[2,192,256]{2,1,0:T(8,128)(2,1)S(1)}, bf16[2,192,256]{2,1,0:T(8,128)(2,1)S(1)}, u32[]{:S(2)}, u32[]{:S(2)}) %collective-permute-start.7) | collective-permute-done | bytes 196640 | tf_op jit(solution)/shard_map/halo/ppermute | solution.py:406
  22.6 0.0 collective-permute-done.6.refs_8_.refs_6_.refs_7_
  22.6 2.4 %attend.2 = (bf16[192,256]{1,0:T(8,128)(2,1)S(1)}, bf16[192,256]{1,0:T(8,128)(2,1)S(1)}, bf16[192,256]{1,0:T(8,128)(2,1)S(1)}, f32[576,128]{1,0:T(8,128)S(1)}) custom-call(bf16[2,192,256]{2,1,0:T(8,128)(2,1)S(1)} %get-tuple-element.35.refs_0_, bf16[2,192,256]{2,1,0:T(8,128)(2,1)S(1)} %collective-permute-done.refs_1_, ...), custom_call_target="tpu_custom_call" | custom-call | flops 5435817984 | bytes 2359296 | tf_op jit(solution)/shard_map/attend/pallas_call | solution.py:358
  25.0 0.0 collective-permute-done.9.refs_1_.refs_5_
  25.0 0.0 collective-permute-done.8.refs_0_.refs_4_
  25.1 1.0 %attend.3 = (bf16[192,256]{1,0:T(8,128)(2,1)S(1)}, f32[8,768]{1,0:T(8,128)S(1)}) custom-call(bf16[192,256]{1,0:T(8,128)(2,1)S(1)} %collective-permute-done.8.refs_0_.refs_4_, bf16[192,256]{1,0:T(8,128)(2,1)S(1)} %collective-permute-done.9.refs_1_.refs_5_, bf16[2,192,256]{2,1,0:T(8,128)(2,1)S(1)} %get-tuple-element.37.refs_4_.refs_2_.refs_6_, ...), custom_call_target="tpu_custom_call" | custom-call | flops 1811939328 | bytes 1794048 | tf_op jit(solution)/shard_map/attend/pallas_call | solution.py:358
  26.1 4.4 %collective-permute-start.12 = (f32[8,768]{1,0:T(8,128)S(1)}, f32[8,768]{1,0:T(8,128)S(1)}, u32[]{:S(2)}, u32[]{:S(2)}) collective-permute-start(f32[8,768]{1,0:T(8,128)S(1)} %get-tuple-element.40.refs_10_), channel_id=1, source_target_pairs={{0,24},{8,16},{16,8},{24,0},{1,25},{9,17},{17,9},{25,1},{2,26},{10... | collective-permute-start | bytes 73736 | tf_op jit(solution)/shard_map/merge/ppermute | solution.py:395
  30.5 0.0 collective-permute-start.11
  30.5 0.4 collective-permute-start.10
  30.9 2.0 %collective-permute-start.14 = (bf16[192,256]{1,0:T(8,128)(2,1)S(1)}, bf16[192,256]{1,0:T(8,128)(2,1)S(1)}, u32[]{:S(2)}, u32[]{:S(2)}) collective-permute-start(bf16[192,256]{1,0:T(8,128)(2,1)S(1)} %get-tuple-element.48), channel_id=1, source_target_pairs={{0,16},{8,24},{16,0},{24,8},{1,17},{9,25},{17,1},{25,9},{2,18},{10... | collective-permute-start | bytes 294920 | tf_op jit(solution)/shard_map/merge/ppermute | solution.py:395
  32.9 1.5 %collective-permute-start.15 = (bf16[192,256]{1,0:T(8,128)(2,1)S(1)}, bf16[192,256]{1,0:T(8,128)(2,1)S(1)}, u32[]{:S(2)}, u32[]{:S(2)}) collective-permute-start(bf16[192,256]{1,0:T(8,128)(2,1)S(1)} %get-tuple-element.49), channel_id=1, source_target_pairs={{0,8},{8,0},{16,24},{24,16},{1,9},{9,1},{17,25},{25,17},{2,10},{10... | collective-permute-start | bytes 294920 | tf_op jit(solution)/shard_map/merge/ppermute | solution.py:395
  34.3 0.0 collective-permute-done.12.refs_13_
  34.3 0.6 %collective-permute-start.13 = (bf16[192,256]{1,0:T(8,128)(2,1)S(1)}, bf16[192,256]{1,0:T(8,128)(2,1)S(1)}, u32[]{:S(2)}, u32[]{:S(2)}) collective-permute-start(bf16[192,256]{1,0:T(8,128)(2,1)S(1)} %get-tuple-element.47), channel_id=1, source_target_pairs={{0,24},{8,16},{16,8},{24,0},{1,25},{9,17},{17,9},{25,1},{2,26},{10... | collective-permute-start | bytes 294920 | tf_op jit(solution)/shard_map/merge/ppermute | solution.py:395
  35.0 0.0 collective-permute-done.11.refs_12_
  35.0 0.0 collective-permute-done.10.refs_11_
  35.0 3.1 %gradients.2 = (f32[2,128,768]{2,1,0:T(8,128)S(1)}, f32[2,768]{1,0:T(2,128)S(1)}, f32[2,768]{1,0:T(2,128)S(1)}, f32[192,128]{1,0:T(8,128)S(1)}, bf16[2,2,192,256...) custom-call(bf16[2,192,256]{2,1,0:T(8,128)(2,1)S(1)} %get-tuple-element.35.refs_0_, ...), custom_call_target="tpu_custom_call" | custom-call | flops 12079595520 | bytes 3354624 | tf_op jit(solution)/shard_map/gradients/pallas_call | solution.py:358
  38.1 2.7 %collective-permute-start.19 = (bf16[2,2,192,256]{3,2,1,0:T(8,128)(2,1)S(1)}, bf16[2,2,192,256]{3,2,1,0:T(8,128)(2,1)S(1)}, u32[]{:S(2)}, u32[]{:S(2)}) collective-permute-start(bf16[2,2,192,256]{3,2,1,0:T(8,128)(2,1)S(1)} %get-tuple-element.62), channel_id=1, source_target_pairs={{0,1},{1,0},{2,3},{3,2},{4,5},{5,4},{6,7},{7,6},{8,9},{9,8},{10,11... | collective-permute-start | bytes 1179656 | tf_op jit(solution)/shard_map/gradients/ppermute | solution.py:461
  40.8 1.9 %collective-permute-start.20 = (bf16[2,2,192,256]{3,2,1,0:T(8,128)(2,1)S(1)}, bf16[2,2,192,256]{3,2,1,0:T(8,128)(2,1)S(1)}, u32[]{:S(2)}, u32[]{:S(2)}) collective-permute-start(bf16[2,2,192,256]{3,2,1,0:T(8,128)(2,1)S(1)} %get-tuple-element.63), channel_id=1, source_target_pairs={{0,0},{1,2},{2,1},{3,3},{4,4},{5,6},{6,5},{7,7},{8,8},{9,10},{10,9... | collective-permute-start | bytes 1179656 | tf_op jit(solution)/shard_map/gradients/ppermute | solution.py:461
  42.7 1.7 %gradients.3 = (bf16[192,256]{1,0:T(8,128)(2,1)S(1)}, bf16[192,256]{1,0:T(8,128)(2,1)S(1)}, bf16[192,256]{1,0:T(8,128)(2,1)S(1)}, bf16[192,256]{1,0:T(8,128)(2,1)S(1)}, bf16[2,2,192,256]{3,2,1,0:T(8,128)(2,1)S(1)}) custom-call(bf16[2,192,256]{2,1,0:T(8,128)(2,1)S(1)} %get-tuple-element.35.refs_0_, bf16[2,192,256]{2,1,0:T(8,128)(2,1)S(1)} %collective-permute-done.refs_1_, ...), custom_call_target="tpu_custom_call" | custom-call | flops 6039797760 | bytes 2764800 | tf_op jit(solution)/shard_map/gradients/pallas_call | solution.py:358
  44.4 0.0 collective-permute-done.14.refs_2_
  44.4 0.0 collective-permute-done.15.refs_3_
  44.4 0.0 collective-permute-done.13.refs_1_
  44.4 2.9 %collective-permute-start.16 = (bf16[192,256]{1,0:T(8,128)(2,1)S(1)}, bf16[192,256]{1,0:T(8,128)(2,1)S(1)}, u32[]{:S(2)}, u32[]{:S(2)}) collective-permute-start(bf16[192,256]{1,0:T(8,128)(2,1)S(1)} %get-tuple-element.54), channel_id=1, source_target_pairs={{0,24},{8,16},{16,8},{24,0},{1,25},{9,17},{17,9},{25,1},{2,26},{10... | collective-permute-start | bytes 294920 | tf_op jit(solution)/shard_map/return/ppermute | solution.py:395
  47.4 0.0 collective-permute-start.17
  47.4 0.7 %collective-permute-start.18 = (bf16[192,256]{1,0:T(8,128)(2,1)S(1)}, bf16[192,256]{1,0:T(8,128)(2,1)S(1)}, u32[]{:S(2)}, u32[]{:S(2)}) collective-permute-start(bf16[192,256]{1,0:T(8,128)(2,1)S(1)} %get-tuple-element.56), channel_id=1, source_target_pairs={{0,8},{8,0},{16,24},{24,16},{1,9},{9,1},{17,25},{25,17},{2,10},{10... | collective-permute-start | bytes 294920 | tf_op jit(solution)/shard_map/return/ppermute | solution.py:395
  48.1 0.0 collective-permute-done.19.refs_1_
  48.1 2.1 %collective-permute-done.20.refs_2_ = bf16[2,2,192,256]{3,2,1,0:T(8,128)(2,1)S(1)} collective-permute-done((bf16[2,2,192,256]{3,2,1,0:T(8,128)(2,1)S(1)}, bf16[2,2,192,256]{3,2,1,0:T(8,128)(2,1)S(1)}, u32[]{:S(2)}, u32[]{:S(2)}) %collective-permute-start.20) | collective-permute-done | bytes 393248 | tf_op jit(solution)/shard_map/gradients/ppermute | solution.py:461
  50.2 0.1 fusion
  50.3 0.3 collective-permute-start.21
  50.6 0.3 collective-permute-done.16.refs_5_
  50.9 4.1 %collective-permute-done.17.refs_6_ = bf16[192,256]{1,0:T(8,128)(2,1)S(1)} collective-permute-done((bf16[192,256]{1,0:T(8,128)(2,1)S(1)}, bf16[192,256]{1,0:T(8,128)(2,1)S(1)}, u32[]{:S(2)}, u32[]{:S(2)}) %collective-permute-start.17) | collective-permute-done | bytes 98336 | tf_op jit(solution)/shard_map/return/ppermute | solution.py:395
  54.9 0.0 collective-permute-done.18.refs_7_
  54.9 1.0 %finish.2 = (bf16[192,256]{1,0:T(8,128)(2,1)}, bf16[192,256]{1,0:T(8,128)(2,1)}) custom-call(bf16[192,256]{1,0:T(8,128)(2,1)S(1)} %get-tuple-element.38.refs_0_, bf16[192,256]{1,0:T(8,128)(2,1)S(1)} %collective-permute-done.13.refs_1_, bf16[192,256]{1,0:T(8,128)(2,1)S(1)} %collective-permute-done.14.refs_2_, ...), custom_call_target="tpu_custom_call" | custom-call | flops 9059696640 | bytes 1376256 | tf_op jit(solution)/shard_map/finish/pallas_call | solution.py:358
  56.0 0.0 collective-permute-done.21.refs_3_
  56.0 0.9 %finish.3 = (bf16[192,256]{1,0:T(8,128)(2,1)}, bf16[192,256]{1,0:T(8,128)(2,1)}) custom-call(bf16[2,2,192,256]{3,2,1,0:T(8,128)(2,1)S(1)} %get-tuple-element.61.refs_0_, bf16[2,2,192,256]{3,2,1,0:T(8,128)(2,1)S(1)} %collective-permute-done.19.refs_1_, bf16[2,2,192,256]{3,2,1,0:T(8,128)(2,1)S(1)} %collective-permute-done.20.refs_2_, ...), custom_call_target="tpu_custom_call" | custom-call | bytes 1867776 | tf_op jit(solution)/shard_map/finish/pallas_call | solution.py:358
Async XLA Ops:
  0.6 3.4 %copy-start = (bf16[3,8,8,256]{3,2,1,0:T(8,128)(2,1)S(1)}, bf16[3,8,8,256]{3,2,1,0:T(8,128)(2,1)}, u32[]{:S(2)}) copy-start(bf16[3,8,8,256]{3,2,1,0:T(8,128)(2,1)} %param.8) | copy-start | bytes 294916
  1.9 13.4 %collective-permute-start.5 = (bf16[2,192,256]{2,1,0:T(8,128)(2,1)S(1)}, bf16[2,192,256]{2,1,0:T(8,128)(2,1)S(1)}, u32[]{:S(2)}, u32[]{:S(2)}) collective-permute-start(bf16[2,192,256]{2,1,0:T(8,128)(2,1)S(1)} %get-tuple-element.37.refs_4_.refs_2_.refs_6_), channel_id=1, source_target_pairs={{0,4},{4,0},{1,5},{5,1},{2,6},{6,2},{3,7},{7,3},{8,12},{12,8},{9,1... | collective-permute-start | bytes 589832 | tf_op jit(solution)/shard_map/halo/ppermute | solution.py:400
  4.0 8.3 %collective-permute-start.2 = (bf16[192,256]{1,0:T(8,128)(2,1)S(1)}, bf16[192,256]{1,0:T(8,128)(2,1)S(1)}, u32[]{:S(2)}, u32[]{:S(2)}) collective-permute-start(bf16[192,256]{1,0:T(8,128)(2,1)S(1)} %bitcast.14), channel_id=1, source_target_pairs={{0,16},{8,24},{16,0},{24,8},{1,17},{9,25},{17,1},{25,9},{2,18},{10... | collective-permute-start | bytes 294920 | tf_op jit(solution)/shard_map/halo/ppermute | solution.py:395
  6.4 11.9 %collective-permute-start.1 = (bf16[192,256]{1,0:T(8,128)(2,1)S(1)}, bf16[192,256]{1,0:T(8,128)(2,1)S(1)}, u32[]{:S(2)}, u32[]{:S(2)}) collective-permute-start(bf16[192,256]{1,0:T(8,128)(2,1)S(1)} %get-tuple-element.36), channel_id=1, source_target_pairs={{0,16},{8,24},{16,0},{24,8},{1,17},{9,25},{17,1},{25,9},{2,18},{10... | collective-permute-start | bytes 294920 | tf_op jit(solution)/shard_map/halo/ppermute | solution.py:395
  6.4 12.2 %collective-permute-start.4 = (bf16[2,192,256]{2,1,0:T(8,128)(2,1)S(1)}, bf16[2,192,256]{2,1,0:T(8,128)(2,1)S(1)}, u32[]{:S(2)}, u32[]{:S(2)}) collective-permute-start(bf16[2,192,256]{2,1,0:T(8,128)(2,1)S(1)} %get-tuple-element.37.refs_4_.refs_2_.refs_6_), channel_id=1, source_target_pairs={{0,0},{1,2},{2,1},{3,3},{4,4},{5,6},{6,5},{7,7},{8,8},{9,10},{10,9... | collective-permute-start | bytes 589832 | tf_op jit(solution)/shard_map/halo/ppermute | solution.py:406
  11.0 7.6 %collective-permute-start = (bf16[2,192,256]{2,1,0:T(8,128)(2,1)S(1)}, bf16[2,192,256]{2,1,0:T(8,128)(2,1)S(1)}, u32[]{:S(2)}, u32[]{:S(2)}) collective-permute-start(bf16[2,192,256]{2,1,0:T(8,128)(2,1)S(1)} %get-tuple-element.35.refs_0_), channel_id=1, source_target_pairs={{0,8},{8,0},{16,24},{24,16},{1,9},{9,1},{17,25},{25,17},{2,10},{10... | collective-permute-start | bytes 589832 | tf_op jit(solution)/shard_map/halo/ppermute | solution.py:395
  12.3 7.7 %collective-permute-start.3 = (bf16[2,192,256]{2,1,0:T(8,128)(2,1)S(1)}, bf16[2,192,256]{2,1,0:T(8,128)(2,1)S(1)}, u32[]{:S(2)}, u32[]{:S(2)}) collective-permute-start(bf16[2,192,256]{2,1,0:T(8,128)(2,1)S(1)} %get-tuple-element.37.refs_4_.refs_2_.refs_6_), channel_id=1, source_target_pairs={{0,1},{1,0},{2,3},{3,2},{4,5},{5,4},{6,7},{7,6},{8,9},{9,8},{10,11... | collective-permute-start | bytes 589832 | tf_op jit(solution)/shard_map/halo/ppermute | solution.py:406
  15.3 7.3 %collective-permute-start.7 = (bf16[2,192,256]{2,1,0:T(8,128)(2,1)S(1)}, bf16[2,192,256]{2,1,0:T(8,128)(2,1)S(1)}, u32[]{:S(2)}, u32[]{:S(2)}) collective-permute-start(bf16[2,192,256]{2,1,0:T(8,128)(2,1)S(1)} %collective-permute-done.5.refs_7_.refs_5_), channel_id=1, source_target_pairs={{0,0},{1,2},{2,1},{3,3},{4,4},{5,6},{6,5},{7,7},{8,8},{9,10},{10,9... | collective-permute-start | bytes 589832 | tf_op jit(solution)/shard_map/halo/ppermute | solution.py:406
  18.2 4.4 %collective-permute-start.6 = (bf16[2,192,256]{2,1,0:T(8,128)(2,1)S(1)}, bf16[2,192,256]{2,1,0:T(8,128)(2,1)S(1)}, u32[]{:S(2)}, u32[]{:S(2)}) collective-permute-start(bf16[2,192,256]{2,1,0:T(8,128)(2,1)S(1)} %collective-permute-done.5.refs_7_.refs_5_), channel_id=1, source_target_pairs={{0,1},{1,0},{2,3},{3,2},{4,5},{5,4},{6,7},{7,6},{8,9},{9,8},{10,11... | collective-permute-start | bytes 589832 | tf_op jit(solution)/shard_map/halo/ppermute | solution.py:406
  18.6 6.5 %collective-permute-start.9 = (bf16[192,256]{1,0:T(8,128)(2,1)S(1)}, bf16[192,256]{1,0:T(8,128)(2,1)S(1)}, u32[]{:S(2)}, u32[]{:S(2)}) collective-permute-start(bf16[192,256]{1,0:T(8,128)(2,1)S(1)} %collective-permute-done.2.refs_3_), channel_id=1, source_target_pairs={{0,8},{8,0},{16,24},{24,16},{1,9},{9,1},{17,25},{25,17},{2,10},{10... | collective-permute-start | bytes 294920 | tf_op jit(solution)/shard_map/halo/ppermute | solution.py:395
  18.6 6.5 %collective-permute-start.8 = (bf16[192,256]{1,0:T(8,128)(2,1)S(1)}, bf16[192,256]{1,0:T(8,128)(2,1)S(1)}, u32[]{:S(2)}, u32[]{:S(2)}) collective-permute-start(bf16[192,256]{1,0:T(8,128)(2,1)S(1)} %collective-permute-done.1.refs_2_), channel_id=1, source_target_pairs={{0,8},{8,0},{16,24},{24,16},{1,9},{9,1},{17,25},{25,17},{2,10},{10... | collective-permute-start | bytes 294920 | tf_op jit(solution)/shard_map/halo/ppermute | solution.py:395
  26.1 8.3 %collective-permute-start.12 = (f32[8,768]{1,0:T(8,128)S(1)}, f32[8,768]{1,0:T(8,128)S(1)}, u32[]{:S(2)}, u32[]{:S(2)}) collective-permute-start(f32[8,768]{1,0:T(8,128)S(1)} %get-tuple-element.40.refs_10_), channel_id=1, source_target_pairs={{0,24},{8,16},{16,8},{24,0},{1,25},{9,17},{17,9},{25,1},{2,26},{10... | collective-permute-start | bytes 73736 | tf_op jit(solution)/shard_map/merge/ppermute | solution.py:395
  30.5 4.5 %collective-permute-start.11 = (f32[8,768]{1,0:T(8,128)S(1)}, f32[8,768]{1,0:T(8,128)S(1)}, u32[]{:S(2)}, u32[]{:S(2)}) collective-permute-start(f32[8,768]{1,0:T(8,128)S(1)} %get-tuple-element.40.refs_10_), channel_id=1, source_target_pairs={{0,16},{8,24},{16,0},{24,8},{1,17},{9,25},{17,1},{25,9},{2,18},{10... | collective-permute-start | bytes 73736 | tf_op jit(solution)/shard_map/merge/ppermute | solution.py:395
  30.5 4.5 %collective-permute-start.10 = (f32[8,768]{1,0:T(8,128)S(1)}, f32[8,768]{1,0:T(8,128)S(1)}, u32[]{:S(2)}, u32[]{:S(2)}) collective-permute-start(f32[8,768]{1,0:T(8,128)S(1)} %get-tuple-element.40.refs_10_), channel_id=1, source_target_pairs={{0,8},{8,0},{16,24},{24,16},{1,9},{9,1},{17,25},{25,17},{2,10},{10... | collective-permute-start | bytes 73736 | tf_op jit(solution)/shard_map/merge/ppermute | solution.py:395
  30.9 13.6 %collective-permute-start.14 = (bf16[192,256]{1,0:T(8,128)(2,1)S(1)}, bf16[192,256]{1,0:T(8,128)(2,1)S(1)}, u32[]{:S(2)}, u32[]{:S(2)}) collective-permute-start(bf16[192,256]{1,0:T(8,128)(2,1)S(1)} %get-tuple-element.48), channel_id=1, source_target_pairs={{0,16},{8,24},{16,0},{24,8},{1,17},{9,25},{17,1},{25,9},{2,18},{10... | collective-permute-start | bytes 294920 | tf_op jit(solution)/shard_map/merge/ppermute | solution.py:395
  32.9 11.6 %collective-permute-start.15 = (bf16[192,256]{1,0:T(8,128)(2,1)S(1)}, bf16[192,256]{1,0:T(8,128)(2,1)S(1)}, u32[]{:S(2)}, u32[]{:S(2)}) collective-permute-start(bf16[192,256]{1,0:T(8,128)(2,1)S(1)} %get-tuple-element.49), channel_id=1, source_target_pairs={{0,8},{8,0},{16,24},{24,16},{1,9},{9,1},{17,25},{25,17},{2,10},{10... | collective-permute-start | bytes 294920 | tf_op jit(solution)/shard_map/merge/ppermute | solution.py:395
  34.3 10.1 %collective-permute-start.13 = (bf16[192,256]{1,0:T(8,128)(2,1)S(1)}, bf16[192,256]{1,0:T(8,128)(2,1)S(1)}, u32[]{:S(2)}, u32[]{:S(2)}) collective-permute-start(bf16[192,256]{1,0:T(8,128)(2,1)S(1)} %get-tuple-element.47), channel_id=1, source_target_pairs={{0,24},{8,16},{16,8},{24,0},{1,25},{9,17},{17,9},{25,1},{2,26},{10... | collective-permute-start | bytes 294920 | tf_op jit(solution)/shard_map/merge/ppermute | solution.py:395
  38.1 10.0 %collective-permute-start.19 = (bf16[2,2,192,256]{3,2,1,0:T(8,128)(2,1)S(1)}, bf16[2,2,192,256]{3,2,1,0:T(8,128)(2,1)S(1)}, u32[]{:S(2)}, u32[]{:S(2)}) collective-permute-start(bf16[2,2,192,256]{3,2,1,0:T(8,128)(2,1)S(1)} %get-tuple-element.62), channel_id=1, source_target_pairs={{0,1},{1,0},{2,3},{3,2},{4,5},{5,4},{6,7},{7,6},{8,9},{9,8},{10,11... | collective-permute-start | bytes 1179656 | tf_op jit(solution)/shard_map/gradients/ppermute | solution.py:461
  40.8 9.4 %collective-permute-start.20 = (bf16[2,2,192,256]{3,2,1,0:T(8,128)(2,1)S(1)}, bf16[2,2,192,256]{3,2,1,0:T(8,128)(2,1)S(1)}, u32[]{:S(2)}, u32[]{:S(2)}) collective-permute-start(bf16[2,2,192,256]{3,2,1,0:T(8,128)(2,1)S(1)} %get-tuple-element.63), channel_id=1, source_target_pairs={{0,0},{1,2},{2,1},{3,3},{4,4},{5,6},{6,5},{7,7},{8,8},{9,10},{10,9... | collective-permute-start | bytes 1179656 | tf_op jit(solution)/shard_map/gradients/ppermute | solution.py:461
  44.4 6.4 %collective-permute-start.16 = (bf16[192,256]{1,0:T(8,128)(2,1)S(1)}, bf16[192,256]{1,0:T(8,128)(2,1)S(1)}, u32[]{:S(2)}, u32[]{:S(2)}) collective-permute-start(bf16[192,256]{1,0:T(8,128)(2,1)S(1)} %get-tuple-element.54), channel_id=1, source_target_pairs={{0,24},{8,16},{16,8},{24,0},{1,25},{9,17},{17,9},{25,1},{2,26},{10... | collective-permute-start | bytes 294920 | tf_op jit(solution)/shard_map/return/ppermute | solution.py:395
  47.4 7.6 %collective-permute-start.17 = (bf16[192,256]{1,0:T(8,128)(2,1)S(1)}, bf16[192,256]{1,0:T(8,128)(2,1)S(1)}, u32[]{:S(2)}, u32[]{:S(2)}) collective-permute-start(bf16[192,256]{1,0:T(8,128)(2,1)S(1)} %get-tuple-element.55), channel_id=1, source_target_pairs={{0,16},{8,24},{16,0},{24,8},{1,17},{9,25},{17,1},{25,9},{2,18},{10... | collective-permute-start | bytes 294920 | tf_op jit(solution)/shard_map/return/ppermute | solution.py:395
  47.4 7.6 %collective-permute-start.18 = (bf16[192,256]{1,0:T(8,128)(2,1)S(1)}, bf16[192,256]{1,0:T(8,128)(2,1)S(1)}, u32[]{:S(2)}, u32[]{:S(2)}) collective-permute-start(bf16[192,256]{1,0:T(8,128)(2,1)S(1)} %get-tuple-element.56), channel_id=1, source_target_pairs={{0,8},{8,0},{16,24},{24,16},{1,9},{9,1},{17,25},{25,17},{2,10},{10... | collective-permute-start | bytes 294920 | tf_op jit(solution)/shard_map/return/ppermute | solution.py:395
  50.3 5.7 %collective-permute-start.21 = (bf16[2,192,256]{2,1,0:T(8,128)(2,1)S(1)}, bf16[2,192,256]{2,1,0:T(8,128)(2,1)S(1)}, u32[]{:S(2)}, u32[]{:S(2)}) collective-permute-start(bf16[2,192,256]{2,1,0:T(8,128)(2,1)S(1)} %fusion), channel_id=1, source_target_pairs={{0,4},{4,0},{1,5},{5,1},{2,6},{6,2},{3,7},{7,3},{8,12},{12,8},{9,1... | collective-permute-start | bytes 589832 | tf_op jit(solution)/shard_map/return/ppermute | solution.py:470

commit v10 on v8

--- a/solution.py
+++ b/solution.py
@@ -20,6 +20,7 @@
 SCALE_LOG2 = SCALE * math.log2(math.e)
 F32 = jnp.float32
 BF16 = jnp.bfloat16
+STAT_ORDER = (1, 3, 2)
 VMEM_LIMIT = 48 * 1024 * 1024
 
 
@@ -218,7 +219,8 @@
 
 
 def merged_stats(stat_refs, cells):
-    parts = [seen_from(ref[...], distance, cells) for distance, ref in enumerate(stat_refs)]
+    refs = dict(zip((0, *STAT_ORDER), stat_refs))
+    parts = [seen_from(refs[distance][...], distance, cells) for distance in range(4)]
     top = functools.reduce(jnp.maximum, parts)
     shares = [jnp.exp2(part - top) for part in parts]
     total = functools.reduce(jnp.add, shares)
@@ -415,9 +417,8 @@
         o0, o1, o2, first = forward((qg, qg1, qg2), None)
         o3, stat = forward((qg3,), first)
     with jax.named_scope("merge"):
-        stats = [stat] + [other_frames(stat, d) for d in (1, 2, 3)]
+        stats = [stat] + [other_frames(stat, d) for d in STAT_ORDER]
         outs = [other_frames(o, d) for d, o in ((3, o3), (2, o2), (1, o1))]
-        stats, outs[1:] = lax.optimization_barrier((stats, outs[1:]))
 
     queries = (qg, qg1, qg2, qg3)
     col_shape = jax.ShapeDtypeStruct((grid_rows, 2, cells, chan), BF16)

time: 53.7 us -> 54.2 us (level)
  waiting for transfers between devices: 9.57 us -> 10.8 us
  starting transfers between devices: 31.8 us -> 30.7 us
    ppermute x12, waiting for transfers between devices: 6.72 us -> 7.39 us  [other_frames(): lax.ppermute(x, 'ta', [(i, i ^ distance) for i in range(sizes['ta'])])]
    ppermute x12, starting transfers between devices: 15.3 us -> 14.7 us  [other_frames(): lax.ppermute(x, 'ta', [(i, i ^ distance) for i in range(sizes['ta'])])]
    ppermute x2, waiting for transfers between devices: 0.44 us -> 0.99 us  [shards(): sides = [lax.ppermute(x, 'wa', pairs) for x, pairs in zip(sides, col_sides)]]
  transfers between devices with their start and end apart: 20 -> 20, of which waited for: 6 -> 6; matrix products, arithmetic and copies ran while one was open for 0% -> 0% of each run, Pallas kernels for 17% -> 15%
where the time goes in v10:
time: 54.2 us; the launch traced here: 53.7 us
  starting transfers between devices  30.7 us (57%)
  Pallas kernels  11.4 us (21%)
  waiting for transfers between devices  10.8 us (20%)
  between operations  0.74 us (1%)
    ppermute x12, starting transfers between devices, other_frames(): lax.ppermute(x, 'ta', [(i, i ^ distance) for i in range(sizes['ta'])])  14.7 us
    pallas_call x7, Pallas kernels, call(): pl.pallas_call(kernel, out_shape=out_shape, in_specs=[pl.BlockSpec(memory...  11.4 us
    ppermute x4, starting transfers between devices, shards(): lax.ppermute(block, 'wa', pairs)  8.2 us
    ppermute x12, waiting for transfers between devices, other_frames(): lax.ppermute(x, 'ta', [(i, i ^ distance) for i in range(sizes['ta'])])  7.39 us
    ppermute x2, starting transfers between devices, shards(): sides = [lax.ppermute(x, 'wa', pairs) for x, pairs in zip(sides, col_sides)]  5.38 us
    ppermute x4, waiting for transfers between devices, shards(): lax.ppermute(block, 'wa', pairs)  2.4 us
    ppermute x1, starting transfers between devices, shards(): kv_rows = [kv] + [lax.ppermute(kv, 'ha', pairs) for pairs in row_sides]  2.11 us
  transfers between devices with their start and end apart: 20, of which 6 were waited for; matrix products, arithmetic and copies ran while one was open for 0% of the time, Pallas kernels for 15%

profile of v10, /device:TPU:1, one launch (start us, length us, event | category | flops | bytes accessed | tf_op | source)
XLA Modules:
  0.0 53.7 jit_solution(6460960823435932846)
XLA Ops:
  0.6 1.3 %rotate.1 = (bf16[2,192,256]{2,1,0:T(8,128)(2,1)S(1)}, bf16[2,192,256]{2,1,0:T(8,128)(2,1)S(1)}, f32[3,192,128]{2,1,0:T(8,128)S(1)}) custom-call(bf16[192,256]{1,0:T(8,128)(2,1)} %bitcast.10, bf16[192,256]{1,0:T(8,128)(2,1)} %bitcast.11, bf16[192,256]{1,0:T(8,128)(2,1)} %bitcast.12, bf16[192,256]{1,0:T(8,128)(2,1)} %bitcast.13, ...), custom_call_target="tpu_custom_call" | custom-call | bytes 1179648 | tf_op jit(solution)/shard_map/rotate/pallas_call | solution.py:344
  1.9 2.1 %collective-permute-start.4 = (bf16[2,192,256]{2,1,0:T(8,128)(2,1)S(1)}, bf16[2,192,256]{2,1,0:T(8,128)(2,1)S(1)}, u32[]{:S(2)}, u32[]{:S(2)}) collective-permute-start(bf16[2,192,256]{2,1,0:T(8,128)(2,1)S(1)} %get-tuple-element.35.refs_3_.refs_1_.refs_4_), channel_id=1, source_target_pairs={{0,4},{4,0},{1,5},{5,1},{2,6},{6,2},{3,7},{7,3},{8,12},{12,8},{9,1... | collective-permute-start | bytes 589832 | tf_op jit(solution)/shard_map/halo/ppermute | solution.py:386
  4.0 2.3 %collective-permute-start.1 = (bf16[2,192,256]{2,1,0:T(8,128)(2,1)S(1)}, bf16[2,192,256]{2,1,0:T(8,128)(2,1)S(1)}, u32[]{:S(2)}, u32[]{:S(2)}) collective-permute-start(bf16[2,192,256]{2,1,0:T(8,128)(2,1)S(1)} %get-tuple-element.34.refs_0_), channel_id=1, source_target_pairs={{0,16},{8,24},{16,0},{24,8},{1,17},{9,25},{17,1},{25,9},{2,18},{10... | collective-permute-start | bytes 589832 | tf_op jit(solution)/shard_map/halo/ppermute | solution.py:381
  6.3 1.3 %collective-permute-start = (bf16[2,192,256]{2,1,0:T(8,128)(2,1)S(1)}, bf16[2,192,256]{2,1,0:T(8,128)(2,1)S(1)}, u32[]{:S(2)}, u32[]{:S(2)}) collective-permute-start(bf16[2,192,256]{2,1,0:T(8,128)(2,1)S(1)} %get-tuple-element.34.refs_0_), channel_id=1, source_target_pairs={{0,8},{8,0},{16,24},{24,16},{1,9},{9,1},{17,25},{25,17},{2,10},{10... | collective-permute-start | bytes 589832 | tf_op jit(solution)/shard_map/halo/ppermute | solution.py:381
  7.6 4.5 %collective-permute-start.3 = (bf16[2,192,256]{2,1,0:T(8,128)(2,1)S(1)}, bf16[2,192,256]{2,1,0:T(8,128)(2,1)S(1)}, u32[]{:S(2)}, u32[]{:S(2)}) collective-permute-start(bf16[2,192,256]{2,1,0:T(8,128)(2,1)S(1)} %get-tuple-element.35.refs_3_.refs_1_.refs_4_), channel_id=1, source_target_pairs={{0,0},{1,2},{2,1},{3,3},{4,4},{5,6},{6,5},{7,7},{8,8},{9,10},{10,9... | collective-permute-start | bytes 589832 | tf_op jit(solution)/shard_map/halo/ppermute | solution.py:391
  12.2 0.1 collective-permute-start.2
  12.2 0.0 collective-permute-done.4.refs_6_.refs_4_.refs_5_
  12.2 1.9 %collective-permute-start.6 = (bf16[2,192,256]{2,1,0:T(8,128)(2,1)S(1)}, bf16[2,192,256]{2,1,0:T(8,128)(2,1)S(1)}, u32[]{:S(2)}, u32[]{:S(2)}) collective-permute-start(bf16[2,192,256]{2,1,0:T(8,128)(2,1)S(1)} %collective-permute-done.4.refs_6_.refs_4_.refs_5_), channel_id=1, source_target_pairs={{0,0},{1,2},{2,1},{3,3},{4,4},{5,6},{6,5},{7,7},{8,8},{9,10},{10,9... | collective-permute-start | bytes 589832 | tf_op jit(solution)/shard_map/halo/ppermute | solution.py:391
  14.2 0.7 %collective-permute-done.1.refs_2_ = bf16[2,192,256]{2,1,0:T(8,128)(2,1)S(1)} collective-permute-done((bf16[2,192,256]{2,1,0:T(8,128)(2,1)S(1)}, bf16[2,192,256]{2,1,0:T(8,128)(2,1)S(1)}, u32[]{:S(2)}, u32[]{:S(2)}) %collective-permute-start.1) | collective-permute-done | bytes 196640 | tf_op jit(solution)/shard_map/halo/ppermute | solution.py:381
  14.9 1.7 %collective-permute-start.5 = (bf16[2,192,256]{2,1,0:T(8,128)(2,1)S(1)}, bf16[2,192,256]{2,1,0:T(8,128)(2,1)S(1)}, u32[]{:S(2)}, u32[]{:S(2)}) collective-permute-start(bf16[2,192,256]{2,1,0:T(8,128)(2,1)S(1)} %collective-permute-done.4.refs_6_.refs_4_.refs_5_), channel_id=1, source_target_pairs={{0,1},{1,0},{2,3},{3,2},{4,5},{5,4},{6,7},{7,6},{8,9},{9,8},{10,11... | collective-permute-start | bytes 589832 | tf_op jit(solution)/shard_map/halo/ppermute | solution.py:391
  16.5 0.0 collective-permute-done.refs_1_
  16.5 0.3 collective-permute-start.7
  16.8 0.0 collective-permute-done.3.refs_5_.refs_3_.refs_6_
  16.8 0.0 collective-permute-done.2.refs_4_.refs_2_
  16.8 2.4 %collective-permute-done.6.refs_8_.refs_6_.refs_7_ = bf16[2,192,256]{2,1,0:T(8,128)(2,1)S(1)} collective-permute-done((bf16[2,192,256]{2,1,0:T(8,128)(2,1)S(1)}, bf16[2,192,256]{2,1,0:T(8,128)(2,1)S(1)}, u32[]{:S(2)}, u32[]{:S(2)}) %collective-permute-start.6) | collective-permute-done | bytes 196640 | tf_op jit(solution)/shard_map/halo/ppermute | solution.py:391
  19.2 0.0 collective-permute-done.5.refs_7_.refs_5_
  19.2 2.4 %attend.2 = (bf16[192,256]{1,0:T(8,128)(2,1)S(1)}, bf16[192,256]{1,0:T(8,128)(2,1)S(1)}, bf16[192,256]{1,0:T(8,128)(2,1)S(1)}, f32[576,128]{1,0:T(8,128)S(1)}) custom-call(bf16[2,192,256]{2,1,0:T(8,128)(2,1)S(1)} %get-tuple-element.34.refs_0_, bf16[2,192,256]{2,1,0:T(8,128)(2,1)S(1)} %collective-permute-done.refs_1_, ...), custom_call_target="tpu_custom_call" | custom-call | flops 5435817984 | bytes 2359296 | tf_op jit(solution)/shard_map/attend/pallas_call | solution.py:344
  21.7 1.2 %collective-permute-done.7.refs_0_.refs_3_ = bf16[2,192,256]{2,1,0:T(8,128)(2,1)S(1)} collective-permute-done((bf16[2,192,256]{2,1,0:T(8,128)(2,1)S(1)}, bf16[2,192,256]{2,1,0:T(8,128)(2,1)S(1)}, u32[]{:S(2)}, u32[]{:S(2)}) %collective-permute-start.7) | collective-permute-done | bytes 196640 | tf_op jit(solution)/shard_map/halo/ppermute | solution.py:381
  22.9 1.0 %attend.3 = (bf16[192,256]{1,0:T(8,128)(2,1)S(1)}, f32[8,768]{1,0:T(8,128)S(1)}) custom-call(bf16[2,192,256]{2,1,0:T(8,128)(2,1)S(1)} %collective-permute-done.7.refs_0_.refs_3_, bf16[2,192,256]{2,1,0:T(8,128)(2,1)S(1)} %get-tuple-element.35.refs_3_.refs_1_.refs_4_, bf16[2,192,256]{2,1,0:T(8,128)(2,1)S(1)} %collective-permute-done.2.refs_4_.refs_2_, ...), custom_call_target="tpu_custom_call" | custom-call | flops 1811939328 | bytes 1794048 | tf_op jit(solution)/shard_map/attend/pallas_call | solution.py:344
  23.9 2.4 %collective-permute-start.10 = (f32[8,768]{1,0:T(8,128)S(1)}, f32[8,768]{1,0:T(8,128)S(1)}, u32[]{:S(2)}, u32[]{:S(2)}) collective-permute-start(f32[8,768]{1,0:T(8,128)S(1)} %get-tuple-element.38.refs_8_), channel_id=1, source_target_pairs={{0,16},{8,24},{16,0},{24,8},{1,17},{9,25},{17,1},{25,9},{2,18},{10... | collective-permute-start | bytes 73736 | tf_op jit(solution)/shard_map/merge/ppermute | solution.py:381
  26.2 1.1 %collective-permute-start.9 = (f32[8,768]{1,0:T(8,128)S(1)}, f32[8,768]{1,0:T(8,128)S(1)}, u32[]{:S(2)}, u32[]{:S(2)}) collective-permute-start(f32[8,768]{1,0:T(8,128)S(1)} %get-tuple-element.38.refs_8_), channel_id=1, source_target_pairs={{0,24},{8,16},{16,8},{24,0},{1,25},{9,17},{17,9},{25,1},{2,26},{10... | collective-permute-start | bytes 73736 | tf_op jit(solution)/shard_map/merge/ppermute | solution.py:381
  27.3 0.2 collective-permute-start.8
  27.5 2.3 %collective-permute-start.12 = (bf16[192,256]{1,0:T(8,128)(2,1)S(1)}, bf16[192,256]{1,0:T(8,128)(2,1)S(1)}, u32[]{:S(2)}, u32[]{:S(2)}) collective-permute-start(bf16[192,256]{1,0:T(8,128)(2,1)S(1)} %get-tuple-element.46), channel_id=1, source_target_pairs={{0,16},{8,24},{16,0},{24,8},{1,17},{9,25},{17,1},{25,9},{2,18},{10... | collective-permute-start | bytes 294920 | tf_op jit(solution)/shard_map/merge/ppermute | solution.py:381
  29.8 0.4 collective-permute-start.13
  30.2 0.0 collective-permute-done.10.refs_11_
  30.2 0.9 %collective-permute-start.11 = (bf16[192,256]{1,0:T(8,128)(2,1)S(1)}, bf16[192,256]{1,0:T(8,128)(2,1)S(1)}, u32[]{:S(2)}, u32[]{:S(2)}) collective-permute-start(bf16[192,256]{1,0:T(8,128)(2,1)S(1)} %get-tuple-element.45), channel_id=1, source_target_pairs={{0,24},{8,16},{16,8},{24,0},{1,25},{9,17},{17,9},{25,1},{2,26},{10... | collective-permute-start | bytes 294920 | tf_op jit(solution)/shard_map/merge/ppermute | solution.py:381
  31.1 0.0 collective-permute-done.9.refs_10_
  31.1 0.0 collective-permute-done.8.refs_9_
  31.1 3.1 %gradients.2 = (f32[2,128,768]{2,1,0:T(8,128)S(1)}, f32[2,768]{1,0:T(2,128)S(1)}, f32[2,768]{1,0:T(2,128)S(1)}, f32[192,128]{1,0:T(8,128)S(1)}, bf16[2,2,192,256...) custom-call(bf16[2,192,256]{2,1,0:T(8,128)(2,1)S(1)} %get-tuple-element.34.refs_0_, ...), custom_call_target="tpu_custom_call" | custom-call | flops 12079595520 | bytes 3354624 | tf_op jit(solution)/shard_map/gradients/pallas_call | solution.py:344
  34.2 2.3 %collective-permute-start.17 = (bf16[2,2,192,256]{3,2,1,0:T(8,128)(2,1)S(1)}, bf16[2,2,192,256]{3,2,1,0:T(8,128)(2,1)S(1)}, u32[]{:S(2)}, u32[]{:S(2)}) collective-permute-start(bf16[2,2,192,256]{3,2,1,0:T(8,128)(2,1)S(1)} %get-tuple-element.60), channel_id=1, source_target_pairs={{0,1},{1,0},{2,3},{3,2},{4,5},{5,4},{6,7},{7,6},{8,9},{9,8},{10,11... | collective-permute-start | bytes 1179656 | tf_op jit(solution)/shard_map/gradients/ppermute | solution.py:445
  36.5 3.1 %collective-permute-start.18 = (bf16[2,2,192,256]{3,2,1,0:T(8,128)(2,1)S(1)}, bf16[2,2,192,256]{3,2,1,0:T(8,128)(2,1)S(1)}, u32[]{:S(2)}, u32[]{:S(2)}) collective-permute-start(bf16[2,2,192,256]{3,2,1,0:T(8,128)(2,1)S(1)} %get-tuple-element.61), channel_id=1, source_target_pairs={{0,0},{1,2},{2,1},{3,3},{4,4},{5,6},{6,5},{7,7},{8,8},{9,10},{10,9... | collective-permute-start | bytes 1179656 | tf_op jit(solution)/shard_map/gradients/ppermute | solution.py:445
  39.6 1.7 %gradients.3 = (bf16[192,256]{1,0:T(8,128)(2,1)S(1)}, bf16[192,256]{1,0:T(8,128)(2,1)S(1)}, bf16[192,256]{1,0:T(8,128)(2,1)S(1)}, bf16[192,256]{1,0:T(8,128)(2,1)S(1)}, bf16[2,2,192,256]{3,2,1,0:T(8,128)(2,1)S(1)}) custom-call(bf16[2,192,256]{2,1,0:T(8,128)(2,1)S(1)} %get-tuple-element.34.refs_0_, bf16[2,192,256]{2,1,0:T(8,128)(2,1)S(1)} %collective-permute-done.refs_1_, ...), custom_call_target="tpu_custom_call" | custom-call | flops 6039797760 | bytes 2764800 | tf_op jit(solution)/shard_map/gradients/pallas_call | solution.py:344
  41.2 0.0 collective-permute-done.12.refs_2_
  41.3 0.0 collective-permute-done.13.refs_3_
  41.3 0.0 collective-permute-done.11.refs_1_
  41.3 2.6 %collective-permute-start.14 = (bf16[192,256]{1,0:T(8,128)(2,1)S(1)}, bf16[192,256]{1,0:T(8,128)(2,1)S(1)}, u32[]{:S(2)}, u32[]{:S(2)}) collective-permute-start(bf16[192,256]{1,0:T(8,128)(2,1)S(1)} %get-tuple-element.52), channel_id=1, source_target_pairs={{0,24},{8,16},{16,8},{24,0},{1,25},{9,17},{17,9},{25,1},{2,26},{10... | collective-permute-start | bytes 294920 | tf_op jit(solution)/shard_map/return/ppermute | solution.py:381
  43.9 0.0 collective-permute-start.15
  43.9 1.0 %collective-permute-start.16 = (bf16[192,256]{1,0:T(8,128)(2,1)S(1)}, bf16[192,256]{1,0:T(8,128)(2,1)S(1)}, u32[]{:S(2)}, u32[]{:S(2)}) collective-permute-start(bf16[192,256]{1,0:T(8,128)(2,1)S(1)} %get-tuple-element.54), channel_id=1, source_target_pairs={{0,8},{8,0},{16,24},{24,16},{1,9},{9,1},{17,25},{25,17},{2,10},{10... | collective-permute-start | bytes 294920 | tf_op jit(solution)/shard_map/return/ppermute | solution.py:381
  44.9 0.0 collective-permute-done.17.refs_1_
  44.9 1.0 %collective-permute-done.18.refs_2_ = bf16[2,2,192,256]{3,2,1,0:T(8,128)(2,1)S(1)} collective-permute-done((bf16[2,2,192,256]{3,2,1,0:T(8,128)(2,1)S(1)}, bf16[2,2,192,256]{3,2,1,0:T(8,128)(2,1)S(1)}, u32[]{:S(2)}, u32[]{:S(2)}) %collective-permute-start.18) | collective-permute-done | bytes 393248 | tf_op jit(solution)/shard_map/gradients/ppermute | solution.py:445
  45.9 0.1 fusion
  46.0 0.3 collective-permute-start.19
  46.3 1.4 %collective-permute-done.14.refs_5_ = bf16[192,256]{1,0:T(8,128)(2,1)S(1)} collective-permute-done((bf16[192,256]{1,0:T(8,128)(2,1)S(1)}, bf16[192,256]{1,0:T(8,128)(2,1)S(1)}, u32[]{:S(2)}, u32[]{:S(2)}) %collective-permute-start.14) | collective-permute-done | bytes 98336 | tf_op jit(solution)/shard_map/return/ppermute | solution.py:381
  47.7 4.0 %collective-permute-done.15.refs_6_ = bf16[192,256]{1,0:T(8,128)(2,1)S(1)} collective-permute-done((bf16[192,256]{1,0:T(8,128)(2,1)S(1)}, bf16[192,256]{1,0:T(8,128)(2,1)S(1)}, u32[]{:S(2)}, u32[]{:S(2)}) %collective-permute-start.15) | collective-permute-done | bytes 98336 | tf_op jit(solution)/shard_map/return/ppermute | solution.py:381
  51.8 0.0 collective-permute-done.16.refs_7_
  51.8 1.0 %finish.2 = (bf16[192,256]{1,0:T(8,128)(2,1)}, bf16[192,256]{1,0:T(8,128)(2,1)}) custom-call(bf16[192,256]{1,0:T(8,128)(2,1)S(1)} %get-tuple-element.36.refs_0_, bf16[192,256]{1,0:T(8,128)(2,1)S(1)} %collective-permute-done.11.refs_1_, bf16[192,256]{1,0:T(8,128)(2,1)S(1)} %collective-permute-done.12.refs_2_, ...), custom_call_target="tpu_custom_call" | custom-call | flops 9059696640 | bytes 1376256 | tf_op jit(solution)/shard_map/finish/pallas_call | solution.py:344
  52.8 0.0 collective-permute-done.19.refs_3_
  52.8 0.9 %finish.3 = (bf16[192,256]{1,0:T(8,128)(2,1)}, bf16[192,256]{1,0:T(8,128)(2,1)}) custom-call(bf16[2,2,192,256]{3,2,1,0:T(8,128)(2,1)S(1)} %get-tuple-element.59.refs_0_, bf16[2,2,192,256]{3,2,1,0:T(8,128)(2,1)S(1)} %collective-permute-done.17.refs_1_, bf16[2,2,192,256]{3,2,1,0:T(8,128)(2,1)S(1)} %collective-permute-done.18.refs_2_, ...), custom_call_target="tpu_custom_call" | custom-call | bytes 1867776 | tf_op jit(solution)/shard_map/finish/pallas_call | solution.py:344
Async XLA Ops:
  1.9 10.3 %collective-permute-start.4 = (bf16[2,192,256]{2,1,0:T(8,128)(2,1)S(1)}, bf16[2,192,256]{2,1,0:T(8,128)(2,1)S(1)}, u32[]{:S(2)}, u32[]{:S(2)}) collective-permute-start(bf16[2,192,256]{2,1,0:T(8,128)(2,1)S(1)} %get-tuple-element.35.refs_3_.refs_1_.refs_4_), channel_id=1, source_target_pairs={{0,4},{4,0},{1,5},{5,1},{2,6},{6,2},{3,7},{7,3},{8,12},{12,8},{9,1... | collective-permute-start | bytes 589832 | tf_op jit(solution)/shard_map/halo/ppermute | solution.py:386
  4.0 10.9 %collective-permute-start.1 = (bf16[2,192,256]{2,1,0:T(8,128)(2,1)S(1)}, bf16[2,192,256]{2,1,0:T(8,128)(2,1)S(1)}, u32[]{:S(2)}, u32[]{:S(2)}) collective-permute-start(bf16[2,192,256]{2,1,0:T(8,128)(2,1)S(1)} %get-tuple-element.34.refs_0_), channel_id=1, source_target_pairs={{0,16},{8,24},{16,0},{24,8},{1,17},{9,25},{17,1},{25,9},{2,18},{10... | collective-permute-start | bytes 589832 | tf_op jit(solution)/shard_map/halo/ppermute | solution.py:381
  6.3 10.2 %collective-permute-start = (bf16[2,192,256]{2,1,0:T(8,128)(2,1)S(1)}, bf16[2,192,256]{2,1,0:T(8,128)(2,1)S(1)}, u32[]{:S(2)}, u32[]{:S(2)}) collective-permute-start(bf16[2,192,256]{2,1,0:T(8,128)(2,1)S(1)} %get-tuple-element.34.refs_0_), channel_id=1, source_target_pairs={{0,8},{8,0},{16,24},{24,16},{1,9},{9,1},{17,25},{25,17},{2,10},{10... | collective-permute-start | bytes 589832 | tf_op jit(solution)/shard_map/halo/ppermute | solution.py:381
  7.6 9.2 %collective-permute-start.3 = (bf16[2,192,256]{2,1,0:T(8,128)(2,1)S(1)}, bf16[2,192,256]{2,1,0:T(8,128)(2,1)S(1)}, u32[]{:S(2)}, u32[]{:S(2)}) collective-permute-start(bf16[2,192,256]{2,1,0:T(8,128)(2,1)S(1)} %get-tuple-element.35.refs_3_.refs_1_.refs_4_), channel_id=1, source_target_pairs={{0,0},{1,2},{2,1},{3,3},{4,4},{5,6},{6,5},{7,7},{8,8},{9,10},{10,9... | collective-permute-start | bytes 589832 | tf_op jit(solution)/shard_map/halo/ppermute | solution.py:391
  12.2 4.7 %collective-permute-start.2 = (bf16[2,192,256]{2,1,0:T(8,128)(2,1)S(1)}, bf16[2,192,256]{2,1,0:T(8,128)(2,1)S(1)}, u32[]{:S(2)}, u32[]{:S(2)}) collective-permute-start(bf16[2,192,256]{2,1,0:T(8,128)(2,1)S(1)} %get-tuple-element.35.refs_3_.refs_1_.refs_4_), channel_id=1, source_target_pairs={{0,1},{1,0},{2,3},{3,2},{4,5},{5,4},{6,7},{7,6},{8,9},{9,8},{10,11... | collective-permute-start | bytes 589832 | tf_op jit(solution)/shard_map/halo/ppermute | solution.py:391
  12.2 7.0 %collective-permute-start.6 = (bf16[2,192,256]{2,1,0:T(8,128)(2,1)S(1)}, bf16[2,192,256]{2,1,0:T(8,128)(2,1)S(1)}, u32[]{:S(2)}, u32[]{:S(2)}) collective-permute-start(bf16[2,192,256]{2,1,0:T(8,128)(2,1)S(1)} %collective-permute-done.4.refs_6_.refs_4_.refs_5_), channel_id=1, source_target_pairs={{0,0},{1,2},{2,1},{3,3},{4,4},{5,6},{6,5},{7,7},{8,8},{9,10},{10,9... | collective-permute-start | bytes 589832 | tf_op jit(solution)/shard_map/halo/ppermute | solution.py:391
  14.9 4.4 %collective-permute-start.5 = (bf16[2,192,256]{2,1,0:T(8,128)(2,1)S(1)}, bf16[2,192,256]{2,1,0:T(8,128)(2,1)S(1)}, u32[]{:S(2)}, u32[]{:S(2)}) collective-permute-start(bf16[2,192,256]{2,1,0:T(8,128)(2,1)S(1)} %collective-permute-done.4.refs_6_.refs_4_.refs_5_), channel_id=1, source_target_pairs={{0,1},{1,0},{2,3},{3,2},{4,5},{5,4},{6,7},{7,6},{8,9},{9,8},{10,11... | collective-permute-start | bytes 589832 | tf_op jit(solution)/shard_map/halo/ppermute | solution.py:391
  16.5 6.3 %collective-permute-start.7 = (bf16[2,192,256]{2,1,0:T(8,128)(2,1)S(1)}, bf16[2,192,256]{2,1,0:T(8,128)(2,1)S(1)}, u32[]{:S(2)}, u32[]{:S(2)}) collective-permute-start(bf16[2,192,256]{2,1,0:T(8,128)(2,1)S(1)} %collective-permute-done.1.refs_2_), channel_id=1, source_target_pairs={{0,8},{8,0},{16,24},{24,16},{1,9},{9,1},{17,25},{25,17},{2,10},{10... | collective-permute-start | bytes 589832 | tf_op jit(solution)/shard_map/halo/ppermute | solution.py:381
  23.9 6.3 %collective-permute-start.10 = (f32[8,768]{1,0:T(8,128)S(1)}, f32[8,768]{1,0:T(8,128)S(1)}, u32[]{:S(2)}, u32[]{:S(2)}) collective-permute-start(f32[8,768]{1,0:T(8,128)S(1)} %get-tuple-element.38.refs_8_), channel_id=1, source_target_pairs={{0,16},{8,24},{16,0},{24,8},{1,17},{9,25},{17,1},{25,9},{2,18},{10... | collective-permute-start | bytes 73736 | tf_op jit(solution)/shard_map/merge/ppermute | solution.py:381
  26.2 4.8 %collective-permute-start.9 = (f32[8,768]{1,0:T(8,128)S(1)}, f32[8,768]{1,0:T(8,128)S(1)}, u32[]{:S(2)}, u32[]{:S(2)}) collective-permute-start(f32[8,768]{1,0:T(8,128)S(1)} %get-tuple-element.38.refs_8_), channel_id=1, source_target_pairs={{0,24},{8,16},{16,8},{24,0},{1,25},{9,17},{17,9},{25,1},{2,26},{10... | collective-permute-start | bytes 73736 | tf_op jit(solution)/shard_map/merge/ppermute | solution.py:381
  27.3 3.8 %collective-permute-start.8 = (f32[8,768]{1,0:T(8,128)S(1)}, f32[8,768]{1,0:T(8,128)S(1)}, u32[]{:S(2)}, u32[]{:S(2)}) collective-permute-start(f32[8,768]{1,0:T(8,128)S(1)} %get-tuple-element.38.refs_8_), channel_id=1, source_target_pairs={{0,8},{8,0},{16,24},{24,16},{1,9},{9,1},{17,25},{25,17},{2,10},{10... | collective-permute-start | bytes 73736 | tf_op jit(solution)/shard_map/merge/ppermute | solution.py:381
  27.5 13.7 %collective-permute-start.12 = (bf16[192,256]{1,0:T(8,128)(2,1)S(1)}, bf16[192,256]{1,0:T(8,128)(2,1)S(1)}, u32[]{:S(2)}, u32[]{:S(2)}) collective-permute-start(bf16[192,256]{1,0:T(8,128)(2,1)S(1)} %get-tuple-element.46), channel_id=1, source_target_pairs={{0,16},{8,24},{16,0},{24,8},{1,17},{9,25},{17,1},{25,9},{2,18},{10... | collective-permute-start | bytes 294920 | tf_op jit(solution)/shard_map/merge/ppermute | solution.py:381
  29.8 11.5 %collective-permute-start.13 = (bf16[192,256]{1,0:T(8,128)(2,1)S(1)}, bf16[192,256]{1,0:T(8,128)(2,1)S(1)}, u32[]{:S(2)}, u32[]{:S(2)}) collective-permute-start(bf16[192,256]{1,0:T(8,128)(2,1)S(1)} %get-tuple-element.47), channel_id=1, source_target_pairs={{0,8},{8,0},{16,24},{24,16},{1,9},{9,1},{17,25},{25,17},{2,10},{10... | collective-permute-start | bytes 294920 | tf_op jit(solution)/shard_map/merge/ppermute | solution.py:381
  30.2 11.1 %collective-permute-start.11 = (bf16[192,256]{1,0:T(8,128)(2,1)S(1)}, bf16[192,256]{1,0:T(8,128)(2,1)S(1)}, u32[]{:S(2)}, u32[]{:S(2)}) collective-permute-start(bf16[192,256]{1,0:T(8,128)(2,1)S(1)} %get-tuple-element.45), channel_id=1, source_target_pairs={{0,24},{8,16},{16,8},{24,0},{1,25},{9,17},{17,9},{25,1},{2,26},{10... | collective-permute-start | bytes 294920 | tf_op jit(solution)/shard_map/merge/ppermute | solution.py:381
  34.2 10.7 %collective-permute-start.17 = (bf16[2,2,192,256]{3,2,1,0:T(8,128)(2,1)S(1)}, bf16[2,2,192,256]{3,2,1,0:T(8,128)(2,1)S(1)}, u32[]{:S(2)}, u32[]{:S(2)}) collective-permute-start(bf16[2,2,192,256]{3,2,1,0:T(8,128)(2,1)S(1)} %get-tuple-element.60), channel_id=1, source_target_pairs={{0,1},{1,0},{2,3},{3,2},{4,5},{5,4},{6,7},{7,6},{8,9},{9,8},{10,11... | collective-permute-start | bytes 1179656 | tf_op jit(solution)/shard_map/gradients/ppermute | solution.py:445
  36.5 9.4 %collective-permute-start.18 = (bf16[2,2,192,256]{3,2,1,0:T(8,128)(2,1)S(1)}, bf16[2,2,192,256]{3,2,1,0:T(8,128)(2,1)S(1)}, u32[]{:S(2)}, u32[]{:S(2)}) collective-permute-start(bf16[2,2,192,256]{3,2,1,0:T(8,128)(2,1)S(1)} %get-tuple-element.61), channel_id=1, source_target_pairs={{0,0},{1,2},{2,1},{3,3},{4,4},{5,6},{6,5},{7,7},{8,8},{9,10},{10,9... | collective-permute-start | bytes 1179656 | tf_op jit(solution)/shard_map/gradients/ppermute | solution.py:445
  41.3 6.4 %collective-permute-start.14 = (bf16[192,256]{1,0:T(8,128)(2,1)S(1)}, bf16[192,256]{1,0:T(8,128)(2,1)S(1)}, u32[]{:S(2)}, u32[]{:S(2)}) collective-permute-start(bf16[192,256]{1,0:T(8,128)(2,1)S(1)} %get-tuple-element.52), channel_id=1, source_target_pairs={{0,24},{8,16},{16,8},{24,0},{1,25},{9,17},{17,9},{25,1},{2,26},{10... | collective-permute-start | bytes 294920 | tf_op jit(solution)/shard_map/return/ppermute | solution.py:381
  43.9 7.9 %collective-permute-start.15 = (bf16[192,256]{1,0:T(8,128)(2,1)S(1)}, bf16[192,256]{1,0:T(8,128)(2,1)S(1)}, u32[]{:S(2)}, u32[]{:S(2)}) collective-permute-start(bf16[192,256]{1,0:T(8,128)(2,1)S(1)} %get-tuple-element.53), channel_id=1, source_target_pairs={{0,16},{8,24},{16,0},{24,8},{1,17},{9,25},{17,1},{25,9},{2,18},{10... | collective-permute-start | bytes 294920 | tf_op jit(solution)/shard_map/return/ppermute | solution.py:381
  43.9 7.9 %collective-permute-start.16 = (bf16[192,256]{1,0:T(8,128)(2,1)S(1)}, bf16[192,256]{1,0:T(8,128)(2,1)S(1)}, u32[]{:S(2)}, u32[]{:S(2)}) collective-permute-start(bf16[192,256]{1,0:T(8,128)(2,1)S(1)} %get-tuple-element.54), channel_id=1, source_target_pairs={{0,8},{8,0},{16,24},{24,16},{1,9},{9,1},{17,25},{25,17},{2,10},{10... | collective-permute-start | bytes 294920 | tf_op jit(solution)/shard_map/return/ppermute | solution.py:381
  46.0 6.8 %collective-permute-start.19 = (bf16[2,192,256]{2,1,0:T(8,128)(2,1)S(1)}, bf16[2,192,256]{2,1,0:T(8,128)(2,1)S(1)}, u32[]{:S(2)}, u32[]{:S(2)}) collective-permute-start(bf16[2,192,256]{2,1,0:T(8,128)(2,1)S(1)} %fusion), channel_id=1, source_target_pairs={{0,4},{4,0},{1,5},{5,1},{2,6},{6,2},{3,7},{7,3},{8,12},{12,8},{9,1... | collective-permute-start | bytes 589832 | tf_op jit(solution)/shard_map/return/ppermute | solution.py:454

commit v11 on v8

--- a/solution.py
+++ b/solution.py
@@ -202,7 +202,9 @@
         stat = jnp.where(lane == HEADS + head, dotted, stat)
     if last:
         whole = jnp.concatenate([first_ref[...], stat], axis=0)
-        stat_ref[...] = whole.T[: stat_ref.shape[0]]
+        rows = whole.T[: stat_ref.shape[1]]
+        for i in range(stat_ref.shape[0]):
+            stat_ref[i] = rows
     else:
         stat_ref[...] = stat
 
@@ -217,8 +219,9 @@
     return stat
 
 
-def merged_stats(stat_refs, cells):
-    parts = [seen_from(ref[...], distance, cells) for distance, ref in enumerate(stat_refs)]
+def merged_stats(stat_ref, cells):
+    here = lax.axis_index("ta")
+    parts = [seen_from(stat_ref[here ^ distance], distance, cells) for distance in range(4)]
     top = functools.reduce(jnp.maximum, parts)
     shares = [jnp.exp2(part - top) for part in parts]
     total = functools.reduce(jnp.add, shares)
@@ -237,7 +240,7 @@
     kv_refs = refs[4 : 4 + tile_count]
     rest = refs[4 + tile_count :]
     if first:
-        stat_refs, rest = rest[:4], rest[4:]
+        stat_ref, rest = rest[0], rest[1:]
     else:
         (lse_ref, delta_ref, dq_ref), rest = rest[:3], rest[3:]
     if last:
@@ -246,7 +249,7 @@
         dq_out, rest = rest[0], rest[1:]
     if first:
         (lse_ref, delta_ref, share_ref), rest = rest[:3], rest[3:]
-        lse, delta, shares = merged_stats(stat_refs, cells)
+        lse, delta, shares = merged_stats(stat_ref, cells)
         lse_ref[...] = lse
         delta_ref[...] = delta
         rows = [shares[d][head : head + 1, : 2 * cells] for head in range(HEADS) for d in range(4)]
@@ -401,7 +404,7 @@
 
     def forward(blocks, first):
         count = len(blocks)
-        stat = (count * cells, DH) if first is None else (8, 4 * cells)
+        stat = (count * cells, DH) if first is None else (4, 8, 4 * cells)
         return call(
             functools.partial(forward_kernel, groups, sizes, cells, count, first is not None),
             (*[plain] * count, real(*stat)),
@@ -415,9 +418,8 @@
         o0, o1, o2, first = forward((qg, qg1, qg2), None)
         o3, stat = forward((qg3,), first)
     with jax.named_scope("merge"):
-        stats = [stat] + [other_frames(stat, d) for d in (1, 2, 3)]
+        stats = [lax.all_to_all(stat, "ta", 0, 0)]
         outs = [other_frames(o, d) for d, o in ((3, o3), (2, o2), (1, o1))]
-        stats, outs[1:] = lax.optimization_barrier((stats, outs[1:]))
 
     queries = (qg, qg1, qg2, qg3)
     col_shape = jax.ShapeDtypeStruct((grid_rows, 2, cells, chan), BF16)

time: 53.7 us -> 57.4 us (1.069)
  starting transfers between devices: 31.8 us -> 33.4 us
  waiting for transfers between devices: 9.57 us -> 10.8 us
  Pallas kernels: 11.4 us -> 12 us
    all_to_all x0 -> x1, starting transfers between devices: none -> 4.58 us  [shards(): stats = [lax.all_to_all(stat, 'ta', 0, 0)]]
    ppermute x12 -> x9, starting transfers between devices: 15.3 us -> 11.1 us  [other_frames(): lax.ppermute(x, 'ta', [(i, i ^ distance) for i in range(sizes['ta'])])]
    ppermute x2, starting transfers between devices: 5.88 us -> 7.16 us  [shards(): sides = [lax.ppermute(x, 'wa', pairs) for x, pairs in zip(sides, col_sides)]]
    all_to_all x0 -> x1, waiting for transfers between devices: none -> 1.27 us  [shards(): stats = [lax.all_to_all(stat, 'ta', 0, 0)]]
    pallas_call x7, Pallas kernels: 11.4 us -> 12 us  [call(): pl.pallas_call(kernel, out_shape=out_shape, in_specs=[pl.BlockSpec(memory...]
    ppermute x12 -> x9, waiting for transfers between devices: 6.72 us -> 6.14 us  [other_frames(): lax.ppermute(x, 'ta', [(i, i ^ distance) for i in range(sizes['ta'])])]
  transfers between devices with their start and end apart: 20 -> 18, of which waited for: 6 -> 7; matrix products, arithmetic and copies ran while one was open for 0% -> 0% of each run, Pallas kernels for 17% -> 14%
where the time goes in v11:
time: 57.4 us; the launch traced here: 57.1 us
  starting transfers between devices  33.4 us (58%)
  Pallas kernels  12 us (21%)
  waiting for transfers between devices  10.8 us (19%)
  between operations  0.74 us (1%)
    pallas_call x7, Pallas kernels, call(): pl.pallas_call(kernel, out_shape=out_shape, in_specs=[pl.BlockSpec(memory...  12 us
    ppermute x9, starting transfers between devices, other_frames(): lax.ppermute(x, 'ta', [(i, i ^ distance) for i in range(sizes['ta'])])  11.1 us
    ppermute x4, starting transfers between devices, shards(): lax.ppermute(block, 'wa', pairs)  8.2 us
    ppermute x2, starting transfers between devices, shards(): sides = [lax.ppermute(x, 'wa', pairs) for x, pairs in zip(sides, col_sides)]  7.16 us
    ppermute x9, waiting for transfers between devices, other_frames(): lax.ppermute(x, 'ta', [(i, i ^ distance) for i in range(sizes['ta'])])  6.14 us
    all_to_all x1, starting transfers between devices, shards(): stats = [lax.all_to_all(stat, 'ta', 0, 0)]  4.58 us
    ppermute x4, waiting for transfers between devices, shards(): lax.ppermute(block, 'wa', pairs)  2.4 us
    ppermute x1, starting transfers between devices, shards(): kv_rows = [kv] + [lax.ppermute(kv, 'ha', pairs) for pairs in row_sides]  2.11 us
  transfers between devices with their start and end apart: 18, of which 7 were waited for; matrix products, arithmetic and copies ran while one was open for 0% of the time, Pallas kernels for 14%

profile of v11, /device:TPU:1, one launch (start us, length us, event | category | flops | bytes accessed | tf_op | source)
XLA Modules:
  0.0 57.1 jit_solution(13804562714477911739)
XLA Ops:
  0.6 1.3 %rotate.1 = (bf16[2,192,256]{2,1,0:T(8,128)(2,1)S(1)}, bf16[2,192,256]{2,1,0:T(8,128)(2,1)S(1)}, f32[3,192,128]{2,1,0:T(8,128)S(1)}) custom-call(bf16[192,256]{1,0:T(8,128)(2,1)} %bitcast.10, bf16[192,256]{1,0:T(8,128)(2,1)} %bitcast.11, bf16[192,256]{1,0:T(8,128)(2,1)} %bitcast.12, bf16[192,256]{1,0:T(8,128)(2,1)} %bitcast.13, ...), custom_call_target="tpu_custom_call" | custom-call | bytes 1179648 | tf_op jit(solution)/shard_map/rotate/pallas_call | solution.py:345
  1.9 2.1 %collective-permute-start.4 = (bf16[2,192,256]{2,1,0:T(8,128)(2,1)S(1)}, bf16[2,192,256]{2,1,0:T(8,128)(2,1)S(1)}, u32[]{:S(2)}, u32[]{:S(2)}) collective-permute-start(bf16[2,192,256]{2,1,0:T(8,128)(2,1)S(1)} %get-tuple-element.35.refs_3_.refs_1_.refs_4_), channel_id=1, source_target_pairs={{0,4},{4,0},{1,5},{5,1},{2,6},{6,2},{3,7},{7,3},{8,12},{12,8},{9,1... | collective-permute-start | bytes 589832 | tf_op jit(solution)/shard_map/halo/ppermute | solution.py:387
  4.0 2.3 %collective-permute-start.1 = (bf16[2,192,256]{2,1,0:T(8,128)(2,1)S(1)}, bf16[2,192,256]{2,1,0:T(8,128)(2,1)S(1)}, u32[]{:S(2)}, u32[]{:S(2)}) collective-permute-start(bf16[2,192,256]{2,1,0:T(8,128)(2,1)S(1)} %get-tuple-element.34.refs_0_), channel_id=1, source_target_pairs={{0,16},{8,24},{16,0},{24,8},{1,17},{9,25},{17,1},{25,9},{2,18},{10... | collective-permute-start | bytes 589832 | tf_op jit(solution)/shard_map/halo/ppermute | solution.py:382
  6.3 1.3 %collective-permute-start = (bf16[2,192,256]{2,1,0:T(8,128)(2,1)S(1)}, bf16[2,192,256]{2,1,0:T(8,128)(2,1)S(1)}, u32[]{:S(2)}, u32[]{:S(2)}) collective-permute-start(bf16[2,192,256]{2,1,0:T(8,128)(2,1)S(1)} %get-tuple-element.34.refs_0_), channel_id=1, source_target_pairs={{0,8},{8,0},{16,24},{24,16},{1,9},{9,1},{17,25},{25,17},{2,10},{10... | collective-permute-start | bytes 589832 | tf_op jit(solution)/shard_map/halo/ppermute | solution.py:382
  7.6 4.5 %collective-permute-start.3 = (bf16[2,192,256]{2,1,0:T(8,128)(2,1)S(1)}, bf16[2,192,256]{2,1,0:T(8,128)(2,1)S(1)}, u32[]{:S(2)}, u32[]{:S(2)}) collective-permute-start(bf16[2,192,256]{2,1,0:T(8,128)(2,1)S(1)} %get-tuple-element.35.refs_3_.refs_1_.refs_4_), channel_id=1, source_target_pairs={{0,0},{1,2},{2,1},{3,3},{4,4},{5,6},{6,5},{7,7},{8,8},{9,10},{10,9... | collective-permute-start | bytes 589832 | tf_op jit(solution)/shard_map/halo/ppermute | solution.py:392
  12.2 0.1 collective-permute-start.2
  12.2 0.0 collective-permute-done.4.refs_6_.refs_4_.refs_5_
  12.2 1.9 %collective-permute-start.6 = (bf16[2,192,256]{2,1,0:T(8,128)(2,1)S(1)}, bf16[2,192,256]{2,1,0:T(8,128)(2,1)S(1)}, u32[]{:S(2)}, u32[]{:S(2)}) collective-permute-start(bf16[2,192,256]{2,1,0:T(8,128)(2,1)S(1)} %collective-permute-done.4.refs_6_.refs_4_.refs_5_), channel_id=1, source_target_pairs={{0,0},{1,2},{2,1},{3,3},{4,4},{5,6},{6,5},{7,7},{8,8},{9,10},{10,9... | collective-permute-start | bytes 589832 | tf_op jit(solution)/shard_map/halo/ppermute | solution.py:392
  14.2 0.7 %collective-permute-done.1.refs_2_ = bf16[2,192,256]{2,1,0:T(8,128)(2,1)S(1)} collective-permute-done((bf16[2,192,256]{2,1,0:T(8,128)(2,1)S(1)}, bf16[2,192,256]{2,1,0:T(8,128)(2,1)S(1)}, u32[]{:S(2)}, u32[]{:S(2)}) %collective-permute-start.1) | collective-permute-done | bytes 196640 | tf_op jit(solution)/shard_map/halo/ppermute | solution.py:382
  14.9 1.7 %collective-permute-start.5 = (bf16[2,192,256]{2,1,0:T(8,128)(2,1)S(1)}, bf16[2,192,256]{2,1,0:T(8,128)(2,1)S(1)}, u32[]{:S(2)}, u32[]{:S(2)}) collective-permute-start(bf16[2,192,256]{2,1,0:T(8,128)(2,1)S(1)} %collective-permute-done.4.refs_6_.refs_4_.refs_5_), channel_id=1, source_target_pairs={{0,1},{1,0},{2,3},{3,2},{4,5},{5,4},{6,7},{7,6},{8,9},{9,8},{10,11... | collective-permute-start | bytes 589832 | tf_op jit(solution)/shard_map/halo/ppermute | solution.py:392
  16.5 0.0 collective-permute-done.refs_1_
  16.5 0.3 collective-permute-start.7
  16.8 0.0 collective-permute-done.3.refs_5_.refs_3_.refs_6_
  16.8 0.0 collective-permute-done.2.refs_4_.refs_2_
  16.8 2.4 %collective-permute-done.6.refs_8_.refs_6_.refs_7_ = bf16[2,192,256]{2,1,0:T(8,128)(2,1)S(1)} collective-permute-done((bf16[2,192,256]{2,1,0:T(8,128)(2,1)S(1)}, bf16[2,192,256]{2,1,0:T(8,128)(2,1)S(1)}, u32[]{:S(2)}, u32[]{:S(2)}) %collective-permute-start.6) | collective-permute-done | bytes 196640 | tf_op jit(solution)/shard_map/halo/ppermute | solution.py:392
  19.2 0.0 collective-permute-done.5.refs_7_.refs_5_
  19.2 2.4 %attend.2 = (bf16[192,256]{1,0:T(8,128)(2,1)S(1)}, bf16[192,256]{1,0:T(8,128)(2,1)S(1)}, bf16[192,256]{1,0:T(8,128)(2,1)S(1)}, f32[576,128]{1,0:T(8,128)S(1)}) custom-call(bf16[2,192,256]{2,1,0:T(8,128)(2,1)S(1)} %get-tuple-element.34.refs_0_, bf16[2,192,256]{2,1,0:T(8,128)(2,1)S(1)} %collective-permute-done.refs_1_, ...), custom_call_target="tpu_custom_call" | custom-call | flops 5435817984 | bytes 2359296 | tf_op jit(solution)/shard_map/attend/pallas_call | solution.py:345
  21.7 1.2 %collective-permute-done.7.refs_0_.refs_3_ = bf16[2,192,256]{2,1,0:T(8,128)(2,1)S(1)} collective-permute-done((bf16[2,192,256]{2,1,0:T(8,128)(2,1)S(1)}, bf16[2,192,256]{2,1,0:T(8,128)(2,1)S(1)}, u32[]{:S(2)}, u32[]{:S(2)}) %collective-permute-start.7) | collective-permute-done | bytes 196640 | tf_op jit(solution)/shard_map/halo/ppermute | solution.py:382
  22.9 1.7 %attend.3 = (bf16[192,256]{1,0:T(8,128)(2,1)S(1)}, f32[4,8,768]{2,1,0:T(8,128)}) custom-call(bf16[2,192,256]{2,1,0:T(8,128)(2,1)S(1)} %collective-permute-done.7.refs_0_.refs_3_, bf16[2,192,256]{2,1,0:T(8,128)(2,1)S(1)} %get-tuple-element.35.refs_3_.refs_1_.refs_4_, bf16[2,192,256]{2,1,0:T(8,128)(2,1)S(1)} %collective-permute-done.2.refs_4_.refs_2_, ...), custom_call_target="tpu_custom_call" | custom-call | flops 1811939328 | bytes 1867776 | tf_op jit(solution)/shard_map/attend/pallas_call | solution.py:345
  24.5 4.6 %all-to-all-start = ((f32[4,8,768]{2,1,0:T(8,128)}), f32[4,8,768]{2,1,0:T(8,128)S(1)}, u32[]{:S(2)}, u32[]{:S(2)}) async-start(f32[4,8,768]{2,1,0:T(8,128)} %get-tuple-element.38), calls=%async_computation | async-start | bytes 196608 | tf_op jit(solution)/shard_map/merge/all_to_all | solution.py:421
  29.1 2.4 %collective-permute-start.9 = (bf16[192,256]{1,0:T(8,128)(2,1)S(1)}, bf16[192,256]{1,0:T(8,128)(2,1)S(1)}, u32[]{:S(2)}, u32[]{:S(2)}) collective-permute-start(bf16[192,256]{1,0:T(8,128)(2,1)S(1)} %get-tuple-element.46), channel_id=1, source_target_pairs={{0,16},{8,24},{16,0},{24,8},{1,17},{9,25},{17,1},{25,9},{2,18},{10... | collective-permute-start | bytes 294920 | tf_op jit(solution)/shard_map/merge/ppermute | solution.py:382
  31.5 1.2 %collective-permute-start.10 = (bf16[192,256]{1,0:T(8,128)(2,1)S(1)}, bf16[192,256]{1,0:T(8,128)(2,1)S(1)}, u32[]{:S(2)}, u32[]{:S(2)}) collective-permute-start(bf16[192,256]{1,0:T(8,128)(2,1)S(1)} %get-tuple-element.47), channel_id=1, source_target_pairs={{0,8},{8,0},{16,24},{24,16},{1,9},{9,1},{17,25},{25,17},{2,10},{10... | collective-permute-start | bytes 294920 | tf_op jit(solution)/shard_map/merge/ppermute | solution.py:382
  32.6 0.0 collective-permute-start.8
  32.7 1.3 %all-to-all-done.refs_8_ = f32[4,8,768]{2,1,0:T(8,128)S(1)} async-done(((f32[4,8,768]{2,1,0:T(8,128)}), f32[4,8,768]{2,1,0:T(8,128)S(1)}, u32[]{:S(2)}, u32[]{:S(2)}) %all-to-all-start) | async-done | bytes 98336 | tf_op jit(solution)/shard_map/merge/all_to_all | solution.py:421
  33.9 3.1 %gradients.2 = (f32[2,128,768]{2,1,0:T(8,128)S(1)}, f32[2,768]{1,0:T(2,128)S(1)}, f32[2,768]{1,0:T(2,128)S(1)}, f32[192,128]{1,0:T(8,128)S(1)}, bf16[2,2,192,256...) custom-call(bf16[2,192,256]{2,1,0:T(8,128)(2,1)S(1)} %get-tuple-element.34.refs_0_, ...), custom_call_target="tpu_custom_call" | custom-call | flops 12079595520 | bytes 3354624 | tf_op jit(solution)/shard_map/gradients/pallas_call | solution.py:345
  37.0 4.1 %collective-permute-start.14 = (bf16[2,2,192,256]{3,2,1,0:T(8,128)(2,1)S(1)}, bf16[2,2,192,256]{3,2,1,0:T(8,128)(2,1)S(1)}, u32[]{:S(2)}, u32[]{:S(2)}) collective-permute-start(bf16[2,2,192,256]{3,2,1,0:T(8,128)(2,1)S(1)} %get-tuple-element.60), channel_id=1, source_target_pairs={{0,1},{1,0},{2,3},{3,2},{4,5},{5,4},{6,7},{7,6},{8,9},{9,8},{10,11... | collective-permute-start | bytes 1179656 | tf_op jit(solution)/shard_map/gradients/ppermute | solution.py:446
  41.2 3.0 %collective-permute-start.15 = (bf16[2,2,192,256]{3,2,1,0:T(8,128)(2,1)S(1)}, bf16[2,2,192,256]{3,2,1,0:T(8,128)(2,1)S(1)}, u32[]{:S(2)}, u32[]{:S(2)}) collective-permute-start(bf16[2,2,192,256]{3,2,1,0:T(8,128)(2,1)S(1)} %get-tuple-element.61), channel_id=1, source_target_pairs={{0,0},{1,2},{2,1},{3,3},{4,4},{5,6},{6,5},{7,7},{8,8},{9,10},{10,9... | collective-permute-start | bytes 1179656 | tf_op jit(solution)/shard_map/gradients/ppermute | solution.py:446
  44.2 1.7 %gradients.3 = (bf16[192,256]{1,0:T(8,128)(2,1)S(1)}, bf16[192,256]{1,0:T(8,128)(2,1)S(1)}, bf16[192,256]{1,0:T(8,128)(2,1)S(1)}, bf16[192,256]{1,0:T(8,128)(2,1)S(1)}, bf16[2,2,192,256]{3,2,1,0:T(8,128)(2,1)S(1)}) custom-call(bf16[2,192,256]{2,1,0:T(8,128)(2,1)S(1)} %get-tuple-element.34.refs_0_, bf16[2,192,256]{2,1,0:T(8,128)(2,1)S(1)} %collective-permute-done.refs_1_, ...), custom_call_target="tpu_custom_call" | custom-call | flops 6039797760 | bytes 2764800 | tf_op jit(solution)/shard_map/gradients/pallas_call | solution.py:345
  45.9 0.0 collective-permute-done.9.refs_2_
  45.9 0.0 collective-permute-done.10.refs_3_
  45.9 0.0 collective-permute-done.8.refs_1_
  45.9 0.4 collective-permute-start.11
  46.3 0.6 collective-permute-start.12
  46.8 2.7 %collective-permute-start.13 = (bf16[192,256]{1,0:T(8,128)(2,1)S(1)}, bf16[192,256]{1,0:T(8,128)(2,1)S(1)}, u32[]{:S(2)}, u32[]{:S(2)}) collective-permute-start(bf16[192,256]{1,0:T(8,128)(2,1)S(1)} %get-tuple-element.54), channel_id=1, source_target_pairs={{0,8},{8,0},{16,24},{24,16},{1,9},{9,1},{17,25},{25,17},{2,10},{10... | collective-permute-start | bytes 294920 | tf_op jit(solution)/shard_map/return/ppermute | solution.py:382
  49.5 0.0 collective-permute-done.14.refs_1_
  49.5 1.0 %collective-permute-done.15.refs_2_ = bf16[2,2,192,256]{3,2,1,0:T(8,128)(2,1)S(1)} collective-permute-done((bf16[2,2,192,256]{3,2,1,0:T(8,128)(2,1)S(1)}, bf16[2,2,192,256]{3,2,1,0:T(8,128)(2,1)S(1)}, u32[]{:S(2)}, u32[]{:S(2)}) %collective-permute-start.15) | collective-permute-done | bytes 393248 | tf_op jit(solution)/shard_map/gradients/ppermute | solution.py:446
  50.5 0.1 fusion
  50.6 0.3 collective-permute-start.16
  50.9 1.4 %collective-permute-done.11.refs_5_ = bf16[192,256]{1,0:T(8,128)(2,1)S(1)} collective-permute-done((bf16[192,256]{1,0:T(8,128)(2,1)S(1)}, bf16[192,256]{1,0:T(8,128)(2,1)S(1)}, u32[]{:S(2)}, u32[]{:S(2)}) %collective-permute-start.11) | collective-permute-done | bytes 98336 | tf_op jit(solution)/shard_map/return/ppermute | solution.py:382
  52.4 2.8 %collective-permute-done.12.refs_6_ = bf16[192,256]{1,0:T(8,128)(2,1)S(1)} collective-permute-done((bf16[192,256]{1,0:T(8,128)(2,1)S(1)}, bf16[192,256]{1,0:T(8,128)(2,1)S(1)}, u32[]{:S(2)}, u32[]{:S(2)}) %collective-permute-start.12) | collective-permute-done | bytes 98336 | tf_op jit(solution)/shard_map/return/ppermute | solution.py:382
  55.2 0.0 collective-permute-done.13.refs_7_
  55.2 1.0 %finish.2 = (bf16[192,256]{1,0:T(8,128)(2,1)}, bf16[192,256]{1,0:T(8,128)(2,1)}) custom-call(bf16[192,256]{1,0:T(8,128)(2,1)S(1)} %get-tuple-element.36.refs_0_, bf16[192,256]{1,0:T(8,128)(2,1)S(1)} %collective-permute-done.8.refs_1_, bf16[192,256]{1,0:T(8,128)(2,1)S(1)} %collective-permute-done.9.refs_2_, ...), custom_call_target="tpu_custom_call" | custom-call | flops 9059696640 | bytes 1376256 | tf_op jit(solution)/shard_map/finish/pallas_call | solution.py:345
  56.2 0.0 collective-permute-done.16.refs_3_
  56.2 0.9 %finish.3 = (bf16[192,256]{1,0:T(8,128)(2,1)}, bf16[192,256]{1,0:T(8,128)(2,1)}) custom-call(bf16[2,2,192,256]{3,2,1,0:T(8,128)(2,1)S(1)} %get-tuple-element.59.refs_0_, bf16[2,2,192,256]{3,2,1,0:T(8,128)(2,1)S(1)} %collective-permute-done.14.refs_1_, bf16[2,2,192,256]{3,2,1,0:T(8,128)(2,1)S(1)} %collective-permute-done.15.refs_2_, ...), custom_call_target="tpu_custom_call" | custom-call | bytes 1867776 | tf_op jit(solution)/shard_map/finish/pallas_call | solution.py:345
Async XLA Ops:
  1.9 10.3 %collective-permute-start.4 = (bf16[2,192,256]{2,1,0:T(8,128)(2,1)S(1)}, bf16[2,192,256]{2,1,0:T(8,128)(2,1)S(1)}, u32[]{:S(2)}, u32[]{:S(2)}) collective-permute-start(bf16[2,192,256]{2,1,0:T(8,128)(2,1)S(1)} %get-tuple-element.35.refs_3_.refs_1_.refs_4_), channel_id=1, source_target_pairs={{0,4},{4,0},{1,5},{5,1},{2,6},{6,2},{3,7},{7,3},{8,12},{12,8},{9,1... | collective-permute-start | bytes 589832 | tf_op jit(solution)/shard_map/halo/ppermute | solution.py:387
  4.0 10.9 %collective-permute-start.1 = (bf16[2,192,256]{2,1,0:T(8,128)(2,1)S(1)}, bf16[2,192,256]{2,1,0:T(8,128)(2,1)S(1)}, u32[]{:S(2)}, u32[]{:S(2)}) collective-permute-start(bf16[2,192,256]{2,1,0:T(8,128)(2,1)S(1)} %get-tuple-element.34.refs_0_), channel_id=1, source_target_pairs={{0,16},{8,24},{16,0},{24,8},{1,17},{9,25},{17,1},{25,9},{2,18},{10... | collective-permute-start | bytes 589832 | tf_op jit(solution)/shard_map/halo/ppermute | solution.py:382
  6.3 10.2 %collective-permute-start = (bf16[2,192,256]{2,1,0:T(8,128)(2,1)S(1)}, bf16[2,192,256]{2,1,0:T(8,128)(2,1)S(1)}, u32[]{:S(2)}, u32[]{:S(2)}) collective-permute-start(bf16[2,192,256]{2,1,0:T(8,128)(2,1)S(1)} %get-tuple-element.34.refs_0_), channel_id=1, source_target_pairs={{0,8},{8,0},{16,24},{24,16},{1,9},{9,1},{17,25},{25,17},{2,10},{10... | collective-permute-start | bytes 589832 | tf_op jit(solution)/shard_map/halo/ppermute | solution.py:382
  7.6 9.2 %collective-permute-start.3 = (bf16[2,192,256]{2,1,0:T(8,128)(2,1)S(1)}, bf16[2,192,256]{2,1,0:T(8,128)(2,1)S(1)}, u32[]{:S(2)}, u32[]{:S(2)}) collective-permute-start(bf16[2,192,256]{2,1,0:T(8,128)(2,1)S(1)} %get-tuple-element.35.refs_3_.refs_1_.refs_4_), channel_id=1, source_target_pairs={{0,0},{1,2},{2,1},{3,3},{4,4},{5,6},{6,5},{7,7},{8,8},{9,10},{10,9... | collective-permute-start | bytes 589832 | tf_op jit(solution)/shard_map/halo/ppermute | solution.py:392
  12.2 4.7 %collective-permute-start.2 = (bf16[2,192,256]{2,1,0:T(8,128)(2,1)S(1)}, bf16[2,192,256]{2,1,0:T(8,128)(2,1)S(1)}, u32[]{:S(2)}, u32[]{:S(2)}) collective-permute-start(bf16[2,192,256]{2,1,0:T(8,128)(2,1)S(1)} %get-tuple-element.35.refs_3_.refs_1_.refs_4_), channel_id=1, source_target_pairs={{0,1},{1,0},{2,3},{3,2},{4,5},{5,4},{6,7},{7,6},{8,9},{9,8},{10,11... | collective-permute-start | bytes 589832 | tf_op jit(solution)/shard_map/halo/ppermute | solution.py:392
  12.2 7.0 %collective-permute-start.6 = (bf16[2,192,256]{2,1,0:T(8,128)(2,1)S(1)}, bf16[2,192,256]{2,1,0:T(8,128)(2,1)S(1)}, u32[]{:S(2)}, u32[]{:S(2)}) collective-permute-start(bf16[2,192,256]{2,1,0:T(8,128)(2,1)S(1)} %collective-permute-done.4.refs_6_.refs_4_.refs_5_), channel_id=1, source_target_pairs={{0,0},{1,2},{2,1},{3,3},{4,4},{5,6},{6,5},{7,7},{8,8},{9,10},{10,9... | collective-permute-start | bytes 589832 | tf_op jit(solution)/shard_map/halo/ppermute | solution.py:392
  14.9 4.4 %collective-permute-start.5 = (bf16[2,192,256]{2,1,0:T(8,128)(2,1)S(1)}, bf16[2,192,256]{2,1,0:T(8,128)(2,1)S(1)}, u32[]{:S(2)}, u32[]{:S(2)}) collective-permute-start(bf16[2,192,256]{2,1,0:T(8,128)(2,1)S(1)} %collective-permute-done.4.refs_6_.refs_4_.refs_5_), channel_id=1, source_target_pairs={{0,1},{1,0},{2,3},{3,2},{4,5},{5,4},{6,7},{7,6},{8,9},{9,8},{10,11... | collective-permute-start | bytes 589832 | tf_op jit(solution)/shard_map/halo/ppermute | solution.py:392
  16.5 6.3 %collective-permute-start.7 = (bf16[2,192,256]{2,1,0:T(8,128)(2,1)S(1)}, bf16[2,192,256]{2,1,0:T(8,128)(2,1)S(1)}, u32[]{:S(2)}, u32[]{:S(2)}) collective-permute-start(bf16[2,192,256]{2,1,0:T(8,128)(2,1)S(1)} %collective-permute-done.1.refs_2_), channel_id=1, source_target_pairs={{0,8},{8,0},{16,24},{24,16},{1,9},{9,1},{17,25},{25,17},{2,10},{10... | collective-permute-start | bytes 589832 | tf_op jit(solution)/shard_map/halo/ppermute | solution.py:382
  24.5 9.4 %all-to-all-start = ((f32[4,8,768]{2,1,0:T(8,128)}), f32[4,8,768]{2,1,0:T(8,128)S(1)}, u32[]{:S(2)}, u32[]{:S(2)}) async-start(f32[4,8,768]{2,1,0:T(8,128)} %get-tuple-element.38), calls=%async_computation | async-start | bytes 196608 | tf_op jit(solution)/shard_map/merge/all_to_all | solution.py:421
  29.1 16.8 %collective-permute-start.9 = (bf16[192,256]{1,0:T(8,128)(2,1)S(1)}, bf16[192,256]{1,0:T(8,128)(2,1)S(1)}, u32[]{:S(2)}, u32[]{:S(2)}) collective-permute-start(bf16[192,256]{1,0:T(8,128)(2,1)S(1)} %get-tuple-element.46), channel_id=1, source_target_pairs={{0,16},{8,24},{16,0},{24,8},{1,17},{9,25},{17,1},{25,9},{2,18},{10... | collective-permute-start | bytes 294920 | tf_op jit(solution)/shard_map/merge/ppermute | solution.py:382
  31.5 14.4 %collective-permute-start.10 = (bf16[192,256]{1,0:T(8,128)(2,1)S(1)}, bf16[192,256]{1,0:T(8,128)(2,1)S(1)}, u32[]{:S(2)}, u32[]{:S(2)}) collective-permute-start(bf16[192,256]{1,0:T(8,128)(2,1)S(1)} %get-tuple-element.47), channel_id=1, source_target_pairs={{0,8},{8,0},{16,24},{24,16},{1,9},{9,1},{17,25},{25,17},{2,10},{10... | collective-permute-start | bytes 294920 | tf_op jit(solution)/shard_map/merge/ppermute | solution.py:382
  32.6 13.3 %collective-permute-start.8 = (bf16[192,256]{1,0:T(8,128)(2,1)S(1)}, bf16[192,256]{1,0:T(8,128)(2,1)S(1)}, u32[]{:S(2)}, u32[]{:S(2)}) collective-permute-start(bf16[192,256]{1,0:T(8,128)(2,1)S(1)} %get-tuple-element.45), channel_id=1, source_target_pairs={{0,24},{8,16},{16,8},{24,0},{1,25},{9,17},{17,9},{25,1},{2,26},{10... | collective-permute-start | bytes 294920 | tf_op jit(solution)/shard_map/merge/ppermute | solution.py:382
  37.0 12.5 %collective-permute-start.14 = (bf16[2,2,192,256]{3,2,1,0:T(8,128)(2,1)S(1)}, bf16[2,2,192,256]{3,2,1,0:T(8,128)(2,1)S(1)}, u32[]{:S(2)}, u32[]{:S(2)}) collective-permute-start(bf16[2,2,192,256]{3,2,1,0:T(8,128)(2,1)S(1)} %get-tuple-element.60), channel_id=1, source_target_pairs={{0,1},{1,0},{2,3},{3,2},{4,5},{5,4},{6,7},{7,6},{8,9},{9,8},{10,11... | collective-permute-start | bytes 1179656 | tf_op jit(solution)/shard_map/gradients/ppermute | solution.py:446
  41.2 9.4 %collective-permute-start.15 = (bf16[2,2,192,256]{3,2,1,0:T(8,128)(2,1)S(1)}, bf16[2,2,192,256]{3,2,1,0:T(8,128)(2,1)S(1)}, u32[]{:S(2)}, u32[]{:S(2)}) collective-permute-start(bf16[2,2,192,256]{3,2,1,0:T(8,128)(2,1)S(1)} %get-tuple-element.61), channel_id=1, source_target_pairs={{0,0},{1,2},{2,1},{3,3},{4,4},{5,6},{6,5},{7,7},{8,8},{9,10},{10,9... | collective-permute-start | bytes 1179656 | tf_op jit(solution)/shard_map/gradients/ppermute | solution.py:446
  45.9 6.4 %collective-permute-start.11 = (bf16[192,256]{1,0:T(8,128)(2,1)S(1)}, bf16[192,256]{1,0:T(8,128)(2,1)S(1)}, u32[]{:S(2)}, u32[]{:S(2)}) collective-permute-start(bf16[192,256]{1,0:T(8,128)(2,1)S(1)} %get-tuple-element.52), channel_id=1, source_target_pairs={{0,24},{8,16},{16,8},{24,0},{1,25},{9,17},{17,9},{25,1},{2,26},{10... | collective-permute-start | bytes 294920 | tf_op jit(solution)/shard_map/return/ppermute | solution.py:382
  46.3 8.9 %collective-permute-start.12 = (bf16[192,256]{1,0:T(8,128)(2,1)S(1)}, bf16[192,256]{1,0:T(8,128)(2,1)S(1)}, u32[]{:S(2)}, u32[]{:S(2)}) collective-permute-start(bf16[192,256]{1,0:T(8,128)(2,1)S(1)} %get-tuple-element.53), channel_id=1, source_target_pairs={{0,16},{8,24},{16,0},{24,8},{1,17},{9,25},{17,1},{25,9},{2,18},{10... | collective-permute-start | bytes 294920 | tf_op jit(solution)/shard_map/return/ppermute | solution.py:382
  46.8 8.3 %collective-permute-start.13 = (bf16[192,256]{1,0:T(8,128)(2,1)S(1)}, bf16[192,256]{1,0:T(8,128)(2,1)S(1)}, u32[]{:S(2)}, u32[]{:S(2)}) collective-permute-start(bf16[192,256]{1,0:T(8,128)(2,1)S(1)} %get-tuple-element.54), channel_id=1, source_target_pairs={{0,8},{8,0},{16,24},{24,16},{1,9},{9,1},{17,25},{25,17},{2,10},{10... | collective-permute-start | bytes 294920 | tf_op jit(solution)/shard_map/return/ppermute | solution.py:382
  50.6 5.6 %collective-permute-start.16 = (bf16[2,192,256]{2,1,0:T(8,128)(2,1)S(1)}, bf16[2,192,256]{2,1,0:T(8,128)(2,1)S(1)}, u32[]{:S(2)}, u32[]{:S(2)}) collective-permute-start(bf16[2,192,256]{2,1,0:T(8,128)(2,1)S(1)} %fusion), channel_id=1, source_target_pairs={{0,4},{4,0},{1,5},{5,1},{2,6},{6,2},{3,7},{7,3},{8,12},{12,8},{9,1... | collective-permute-start | bytes 589832 | tf_op jit(solution)/shard_map/return/ppermute | solution.py:455

commit v12 on v8

--- a/solution.py
+++ b/solution.py
@@ -20,6 +20,7 @@
 SCALE_LOG2 = SCALE * math.log2(math.e)
 F32 = jnp.float32
 BF16 = jnp.bfloat16
+NEAR = 1
 VMEM_LIMIT = 48 * 1024 * 1024
 
 
@@ -233,19 +234,18 @@
 
 def backward_kernel(cols, grid_rows, sizes, cells, first, last, *refs):
     tile_count = grid_rows * len(cols)
-    qg_refs = refs[:4]
-    kv_refs = refs[4 : 4 + tile_count]
-    rest = refs[4 + tile_count :]
+    qg_refs, refs = refs[:4], refs[4:]
+    kv_refs, refs = refs[:tile_count], refs[tile_count:]
     if first:
-        stat_refs, rest = rest[:4], rest[4:]
+        stat_refs, refs = refs[:4], refs[4:]
     else:
-        (lse_ref, delta_ref, dq_ref), rest = rest[:3], rest[3:]
+        (lse_ref, delta_ref, dq_ref), refs = refs[:3], refs[3:]
     if last:
-        dq_outs, rest = rest[:4], rest[4:]
+        dq_outs, refs = refs[:4], refs[4:]
     else:
-        dq_out, rest = rest[0], rest[1:]
+        dq_out, refs = refs[0], refs[1:]
     if first:
-        (lse_ref, delta_ref, share_ref), rest = rest[:3], rest[3:]
+        (lse_ref, delta_ref, share_ref), refs = refs[:3], refs[3:]
         lse, delta, shares = merged_stats(stat_refs, cells)
         lse_ref[...] = lse
         delta_ref[...] = delta
@@ -254,30 +254,38 @@
         share_ref[...] = wide.T[:cells]
     else:
         lse, delta = lse_ref[...], delta_ref[...]
-    col_refs = rest[: len(cols)]
-    key_buf, value_buf = rest[len(cols) :]
-
-    span = grid_rows * cells
+    own_refs, rest_refs = [], []
+    for col in cols:
+        own_refs.append(refs[0].at[0] if col == NEAR else refs[0])
+        rest_refs.append(refs[0].at[pl.ds(1, grid_rows - 1)] if col == NEAR else refs[1])
+        refs = refs[1:] if col == NEAR else refs[2:]
+    key_buf, value_buf = refs
     for i, ref in enumerate(kv_refs):
         key_buf[i * cells : (i + 1) * cells] = ref[0]
         value_buf[i * cells : (i + 1) * cells] = ref[1]
+    span = grid_rows * cells
     blocks = [(head, slot) for head in range(HEADS) for slot in range(len(cols))]
+    heads = []
+    for head in range(HEADS):
+        cut = head_slice(head)
+        heads.append(
+            [jnp.concatenate([ref[i, :, cut] for ref in qg_refs], axis=0) for i in range(2)]
+        )
 
     def products_of(head, slot):
         cut = head_slice(head)
         at = slice(slot * span, (slot + 1) * span)
-        queries = jnp.concatenate([ref[0, :, cut] for ref in qg_refs], axis=0)
-        grads = jnp.concatenate([ref[1, :, cut] for ref in qg_refs], axis=0)
-        raw = dot_nt(key_buf[at, cut], queries)
-        return raw, dot_nt(value_buf[at, cut], grads), queries, grads
-
+        queries, grads = heads[head]
+        return dot_nt(key_buf[at, cut], queries), dot_nt(value_buf[at, cut], grads)
+
+    ahead = products_of(*blocks[0])
     dqs = [None] * HEADS
-    ahead = products_of(*blocks[0])
     for i, (head, slot) in enumerate(blocks):
-        raw, prob_grad, queries, grads = ahead
+        raw, prob_grad = ahead
         if i + 1 < len(blocks):
             ahead = products_of(*blocks[i + 1])
         cut = head_slice(head)
+        queries, grads = heads[head]
         probs = []
         for row in range(grid_rows):
             bias = group_bias((row == 2, cols[slot] == 2), sizes)
@@ -288,10 +296,10 @@
         dscore = (probs * (prob_grad - delta[head : head + 1])).astype(BF16)
         dv = dot_nn(probs.astype(BF16), grads).astype(BF16)
         dk = (dot_nn(dscore, queries) * SCALE).astype(BF16)
-        for row in range(grid_rows):
-            at = slice(row * cells, (row + 1) * cells)
-            col_refs[slot][row, 0, :, cut] = dk[at]
-            col_refs[slot][row, 1, :, cut] = dv[at]
+        for which, part in enumerate((dk, dv)):
+            own_refs[slot][which, :, cut] = part[:cells]
+            for row in range(1, grid_rows):
+                rest_refs[slot][row - 1, which, :, cut] = part[row * cells : (row + 1) * cells]
         part = dot_nn(key_buf[slot * span : (slot + 1) * span, cut].T, dscore)
         dqs[head] = part if dqs[head] is None else dqs[head] + part
     for head in range(HEADS):
@@ -319,15 +327,14 @@
         dq_out[:, cut] = turn(dq, rope_ref[0], rope_ref[1], rope_ref[2], -1.0).astype(BF16)
 
 
-def finish_key_kernel(cols, rows, *refs):
-    col_refs, row_refs = refs[:cols], refs[cols : cols + rows]
-    rope_ref, dk_out, dv_out = refs[cols + rows :]
+def finish_key_kernel(count, *refs):
+    near_ref, own_ref, rope_ref, dk_out, dv_out = refs[count:]
+    part_refs = [*refs[:count], near_ref.at[0], own_ref]
     for head in range(HEADS):
         cut = head_slice(head)
         sums = []
         for which in range(2):
-            terms = [ref[0, which, :, cut].astype(F32) for ref in col_refs]
-            terms += [ref[which, :, cut].astype(F32) for ref in row_refs]
+            terms = [ref[which, :, cut].astype(F32) for ref in part_refs]
             sums.append(functools.reduce(jnp.add, terms))
         dk_out[:, cut] = turn(
             sums[0], rope_ref[0], rope_ref[1], rope_ref[2], -1.0
@@ -420,7 +427,8 @@
         stats, outs[1:] = lax.optimization_barrier((stats, outs[1:]))
 
     queries = (qg, qg1, qg2, qg3)
-    col_shape = jax.ShapeDtypeStruct((grid_rows, 2, cells, chan), BF16)
+    whole = jax.ShapeDtypeStruct((grid_rows, 2, cells, chan), BF16)
+    rest_shape = jax.ShapeDtypeStruct((grid_rows - 1, 2, cells, chan), BF16)
 
     def gradients(which, carried):
         count = len(which)
@@ -431,7 +439,7 @@
             (
                 *([plain] * 4 if last else [real(HEADS, DH, 4 * cells)]),
                 *(stat_outs if first else []),
-                *[col_shape] * count,
+                *[x for col in which for x in ([whole] if col == NEAR else [pair, rest_shape])],
             ),
             (*queries, *[tiles[row][col] for col in which for row in range(grid_rows)], *carried),
             20 * product * count // grid_cols,
@@ -440,26 +448,30 @@
         )
 
     with jax.named_scope("gradients"):
-        dq, lse, delta, shares, *sides = gradients(tuple(range(1, grid_cols)), stats)
-        sides = [lax.ppermute(x, "wa", pairs) for x, pairs in zip(sides, col_sides)]
-        d0, d1, d2, d3, own = gradients((0,), (lse, delta, dq))
+        dq, lse, delta, shares, near, *far = gradients(tuple(range(1, grid_cols)), stats)
+        near = lax.ppermute(near, "wa", col_sides[0])
+        rests = [near[1:]]
+        if far:
+            rests.append(lax.ppermute(far[1], "wa", col_sides[1]))
+        d0, d1, d2, d3, own, rest = gradients((0,), (lse, delta, dq))
     with jax.named_scope("return"):
         (d1, d2, d3), outs = lax.optimization_barrier(((d1, d2, d3), outs))
-        col_parts = [own, *sides]
-        dqs = [d0] + [other_frames(x, d) for d, x in ((3, d3), (2, d2), (1, d1))]
+        dqs = [d0] + [other_frames(x, d) for d, x in ((2, d2), (3, d3), (1, d1))]
         row_parts = []
-        for row, pairs in enumerate(row_sides, start=1):
-            partial_sum = sum(x[row].astype(F32) for x in col_parts).astype(BF16)
+        for row, pairs in enumerate(row_sides):
+            partial_sum = sum(x[row].astype(F32) for x in (rest, *rests)).astype(BF16)
+            far, partial_sum = lax.optimization_barrier((far, partial_sum))
             row_parts.append(lax.ppermute(partial_sum, "ha", pairs))
+        far_parts = [lax.ppermute(far[0], "wa", col_sides[1])] if far else []
 
     with jax.named_scope("finish"):
         attended, grad_query = call(
             finish_query_kernel, (plain, plain), (o0, *outs, *dqs, shares, rope), 10 * product
         )
         grad_key, grad_value = call(
-            functools.partial(finish_key_kernel, grid_cols, len(row_parts)),
+            functools.partial(finish_key_kernel, len(row_parts) + len(far_parts)),
             (plain, plain),
-            (*col_parts, *row_parts, rope),
+            (*row_parts, *far_parts, near, own, rope),
         )
     return tuple(x.reshape(query_in.shape) for x in (attended, grad_query, grad_key, grad_value))
 

time: 53.7 us -> 55.2 us (1.028); the launches traced: 53.5 us -> 54.1 us
  starting transfers between devices: 31.8 us -> 33.9 us
  waiting for transfers between devices: 9.57 us -> 8.01 us
    ppermute x2 -> x3, starting transfers between devices: 5.88 us -> 8.9 us  [the longest x1 5.8 us: shards(): rests.append(lax.ppermute(far[1], 'wa', col_sides[1]))]
    ppermute x12, waiting for transfers between devices: 6.72 us -> 5.59 us  [other_frames(): lax.ppermute(x, 'ta', [(i, i ^ distance) for i in range(sizes['ta'])])]
    ppermute x12, starting transfers between devices: 15.3 us -> 14.4 us  [other_frames(): lax.ppermute(x, 'ta', [(i, i ^ distance) for i in range(sizes['ta'])])]
  transfers between devices with their start and end apart: 20 -> 21, of which waited for: 6 -> 5; matrix products, arithmetic and copies ran while one was open for 0% -> 0% of each run, Pallas kernels for 17% -> 17%
where the time goes in v12:
time: 55.2 us; the launch traced here: 54.1 us
  starting transfers between devices  33.9 us (61%)
  Pallas kernels  11.4 us (21%)
  waiting for transfers between devices  8.01 us (15%)
  between operations  0.75 us (1%)
    ppermute x12, starting transfers between devices, other_frames(): lax.ppermute(x, 'ta', [(i, i ^ distance) for i in range(sizes['ta'])])  14.4 us
    pallas_call x7, Pallas kernels, call(): pl.pallas_call(kernel, out_shape=out_shape, in_specs=[pl.BlockSpec(memory...  11.4 us
    ppermute x4, starting transfers between devices, shards(): lax.ppermute(block, 'wa', pairs)  8.2 us
    ppermute x1, starting transfers between devices, shards(): rests.append(lax.ppermute(far[1], 'wa', col_sides[1]))  5.8 us
    ppermute x12, waiting for transfers between devices, other_frames(): lax.ppermute(x, 'ta', [(i, i ^ distance) for i in range(sizes['ta'])])  5.59 us
    ppermute x1, starting transfers between devices, shards(): far_parts = [lax.ppermute(far[0], 'wa', col_sides[1])] if far else []  3.03 us
    ppermute x4, waiting for transfers between devices, shards(): lax.ppermute(block, 'wa', pairs)  2.4 us
    ppermute x1, starting transfers between devices, shards(): kv_rows = [kv] + [lax.ppermute(kv, 'ha', pairs) for pairs in row_sides]  2.11 us
  transfers between devices with their start and end apart: 21, of which 5 were waited for; matrix products, arithmetic and copies ran while one was open for 0% of the time, Pallas kernels for 17%

profile of v12, /device:TPU:1, one launch (start us, length us, event | category | flops | bytes accessed | tf_op | source)
XLA Modules:
  0.0 54.1 jit_solution(5411296904812376345)
XLA Ops:
  0.6 1.3 %rotate.1 = (bf16[2,192,256]{2,1,0:T(8,128)(2,1)S(1)}, bf16[2,192,256]{2,1,0:T(8,128)(2,1)S(1)}, f32[3,192,128]{2,1,0:T(8,128)S(1)}) custom-call(bf16[192,256]{1,0:T(8,128)(2,1)} %bitcast.10, bf16[192,256]{1,0:T(8,128)(2,1)} %bitcast.11, bf16[192,256]{1,0:T(8,128)(2,1)} %bitcast.12, bf16[192,256]{1,0:T(8,128)(2,1)} %bitcast.13, ...), custom_call_target="tpu_custom_call" | custom-call | bytes 1179648 | tf_op jit(solution)/shard_map/rotate/pallas_call | solution.py:349
  1.9 2.1 %collective-permute-start.4 = (bf16[2,192,256]{2,1,0:T(8,128)(2,1)S(1)}, bf16[2,192,256]{2,1,0:T(8,128)(2,1)S(1)}, u32[]{:S(2)}, u32[]{:S(2)}) collective-permute-start(bf16[2,192,256]{2,1,0:T(8,128)(2,1)S(1)} %get-tuple-element.45.refs_3_.refs_1_.refs_4_), channel_id=1, source_target_pairs={{0,4},{4,0},{1,5},{5,1},{2,6},{6,2},{3,7},{7,3},{8,12},{12,8},{9,1... | collective-permute-start | bytes 589832 | tf_op jit(solution)/shard_map/halo/ppermute | solution.py:391
  4.0 2.3 %collective-permute-start.1 = (bf16[2,192,256]{2,1,0:T(8,128)(2,1)S(1)}, bf16[2,192,256]{2,1,0:T(8,128)(2,1)S(1)}, u32[]{:S(2)}, u32[]{:S(2)}) collective-permute-start(bf16[2,192,256]{2,1,0:T(8,128)(2,1)S(1)} %get-tuple-element.44.refs_0_), channel_id=1, source_target_pairs={{0,16},{8,24},{16,0},{24,8},{1,17},{9,25},{17,1},{25,9},{2,18},{10... | collective-permute-start | bytes 589832 | tf_op jit(solution)/shard_map/halo/ppermute | solution.py:386
  6.3 1.3 %collective-permute-start = (bf16[2,192,256]{2,1,0:T(8,128)(2,1)S(1)}, bf16[2,192,256]{2,1,0:T(8,128)(2,1)S(1)}, u32[]{:S(2)}, u32[]{:S(2)}) collective-permute-start(bf16[2,192,256]{2,1,0:T(8,128)(2,1)S(1)} %get-tuple-element.44.refs_0_), channel_id=1, source_target_pairs={{0,8},{8,0},{16,24},{24,16},{1,9},{9,1},{17,25},{25,17},{2,10},{10... | collective-permute-start | bytes 589832 | tf_op jit(solution)/shard_map/halo/ppermute | solution.py:386
  7.6 4.5 %collective-permute-start.3 = (bf16[2,192,256]{2,1,0:T(8,128)(2,1)S(1)}, bf16[2,192,256]{2,1,0:T(8,128)(2,1)S(1)}, u32[]{:S(2)}, u32[]{:S(2)}) collective-permute-start(bf16[2,192,256]{2,1,0:T(8,128)(2,1)S(1)} %get-tuple-element.45.refs_3_.refs_1_.refs_4_), channel_id=1, source_target_pairs={{0,0},{1,2},{2,1},{3,3},{4,4},{5,6},{6,5},{7,7},{8,8},{9,10},{10,9... | collective-permute-start | bytes 589832 | tf_op jit(solution)/shard_map/halo/ppermute | solution.py:396
  12.2 0.1 collective-permute-start.2
  12.2 0.0 collective-permute-done.4.refs_6_.refs_4_.refs_5_
  12.2 1.9 %collective-permute-start.6 = (bf16[2,192,256]{2,1,0:T(8,128)(2,1)S(1)}, bf16[2,192,256]{2,1,0:T(8,128)(2,1)S(1)}, u32[]{:S(2)}, u32[]{:S(2)}) collective-permute-start(bf16[2,192,256]{2,1,0:T(8,128)(2,1)S(1)} %collective-permute-done.4.refs_6_.refs_4_.refs_5_), channel_id=1, source_target_pairs={{0,0},{1,2},{2,1},{3,3},{4,4},{5,6},{6,5},{7,7},{8,8},{9,10},{10,9... | collective-permute-start | bytes 589832 | tf_op jit(solution)/shard_map/halo/ppermute | solution.py:396
  14.2 0.7 %collective-permute-done.1.refs_2_ = bf16[2,192,256]{2,1,0:T(8,128)(2,1)S(1)} collective-permute-done((bf16[2,192,256]{2,1,0:T(8,128)(2,1)S(1)}, bf16[2,192,256]{2,1,0:T(8,128)(2,1)S(1)}, u32[]{:S(2)}, u32[]{:S(2)}) %collective-permute-start.1) | collective-permute-done | bytes 196640 | tf_op jit(solution)/shard_map/halo/ppermute | solution.py:386
  14.9 1.7 %collective-permute-start.5 = (bf16[2,192,256]{2,1,0:T(8,128)(2,1)S(1)}, bf16[2,192,256]{2,1,0:T(8,128)(2,1)S(1)}, u32[]{:S(2)}, u32[]{:S(2)}) collective-permute-start(bf16[2,192,256]{2,1,0:T(8,128)(2,1)S(1)} %collective-permute-done.4.refs_6_.refs_4_.refs_5_), channel_id=1, source_target_pairs={{0,1},{1,0},{2,3},{3,2},{4,5},{5,4},{6,7},{7,6},{8,9},{9,8},{10,11... | collective-permute-start | bytes 589832 | tf_op jit(solution)/shard_map/halo/ppermute | solution.py:396
  16.5 0.0 collective-permute-done.refs_1_
  16.5 0.3 collective-permute-start.7
  16.8 0.0 collective-permute-done.3.refs_5_.refs_3_.refs_6_
  16.8 0.0 collective-permute-done.2.refs_4_.refs_2_
  16.8 2.4 %collective-permute-done.6.refs_8_.refs_6_.refs_7_ = bf16[2,192,256]{2,1,0:T(8,128)(2,1)S(1)} collective-permute-done((bf16[2,192,256]{2,1,0:T(8,128)(2,1)S(1)}, bf16[2,192,256]{2,1,0:T(8,128)(2,1)S(1)}, u32[]{:S(2)}, u32[]{:S(2)}) %collective-permute-start.6) | collective-permute-done | bytes 196640 | tf_op jit(solution)/shard_map/halo/ppermute | solution.py:396
  19.2 0.0 collective-permute-done.5.refs_7_.refs_5_
  19.2 2.4 %attend.2 = (bf16[192,256]{1,0:T(8,128)(2,1)S(1)}, bf16[192,256]{1,0:T(8,128)(2,1)S(1)}, bf16[192,256]{1,0:T(8,128)(2,1)S(1)}, f32[576,128]{1,0:T(8,128)S(1)}) custom-call(bf16[2,192,256]{2,1,0:T(8,128)(2,1)S(1)} %get-tuple-element.44.refs_0_, bf16[2,192,256]{2,1,0:T(8,128)(2,1)S(1)} %collective-permute-done.refs_1_, ...), custom_call_target="tpu_custom_call" | custom-call | flops 5435817984 | bytes 2359296 | tf_op jit(solution)/shard_map/attend/pallas_call | solution.py:349
  21.7 0.8 %collective-permute-start.11 = (bf16[192,256]{1,0:T(8,128)(2,1)S(1)}, bf16[192,256]{1,0:T(8,128)(2,1)S(1)}, u32[]{:S(2)}, u32[]{:S(2)}) collective-permute-start(bf16[192,256]{1,0:T(8,128)(2,1)S(1)} %get-tuple-element.49), channel_id=1, source_target_pairs={{0,16},{8,24},{16,0},{24,8},{1,17},{9,25},{17,1},{25,9},{2,18},{10... | collective-permute-start | bytes 294920 | tf_op jit(solution)/shard_map/merge/ppermute | solution.py:386
  22.4 1.0 %collective-permute-start.12 = (bf16[192,256]{1,0:T(8,128)(2,1)S(1)}, bf16[192,256]{1,0:T(8,128)(2,1)S(1)}, u32[]{:S(2)}, u32[]{:S(2)}) collective-permute-start(bf16[192,256]{1,0:T(8,128)(2,1)S(1)} %get-tuple-element.50), channel_id=1, source_target_pairs={{0,8},{8,0},{16,24},{24,16},{1,9},{9,1},{17,25},{25,17},{2,10},{10... | collective-permute-start | bytes 294920 | tf_op jit(solution)/shard_map/merge/ppermute | solution.py:386
  23.5 0.0 collective-permute-done.7.refs_0_.refs_3_
  23.5 1.0 %attend.3 = (bf16[192,256]{1,0:T(8,128)(2,1)S(1)}, f32[8,768]{1,0:T(8,128)S(1)}) custom-call(bf16[2,192,256]{2,1,0:T(8,128)(2,1)S(1)} %collective-permute-done.7.refs_0_.refs_3_, bf16[2,192,256]{2,1,0:T(8,128)(2,1)S(1)} %get-tuple-element.45.refs_3_.refs_1_.refs_4_, bf16[2,192,256]{2,1,0:T(8,128)(2,1)S(1)} %collective-permute-done.2.refs_4_.refs_2_, ...), custom_call_target="tpu_custom_call" | custom-call | flops 1811939328 | bytes 1794048 | tf_op jit(solution)/shard_map/attend/pallas_call | solution.py:349
  24.5 2.7 %collective-permute-start.10 = (f32[8,768]{1,0:T(8,128)S(1)}, f32[8,768]{1,0:T(8,128)S(1)}, u32[]{:S(2)}, u32[]{:S(2)}) collective-permute-start(f32[8,768]{1,0:T(8,128)S(1)} %get-tuple-element.51.refs_8_), channel_id=1, source_target_pairs={{0,24},{8,16},{16,8},{24,0},{1,25},{9,17},{17,9},{25,1},{2,26},{10... | collective-permute-start | bytes 73736 | tf_op jit(solution)/shard_map/merge/ppermute | solution.py:386
  27.2 0.0 collective-permute-start.9
  27.2 0.9 %collective-permute-start.8 = (f32[8,768]{1,0:T(8,128)S(1)}, f32[8,768]{1,0:T(8,128)S(1)}, u32[]{:S(2)}, u32[]{:S(2)}) collective-permute-start(f32[8,768]{1,0:T(8,128)S(1)} %get-tuple-element.51.refs_8_), channel_id=1, source_target_pairs={{0,8},{8,0},{16,24},{24,16},{1,9},{9,1},{17,25},{25,17},{2,10},{10... | collective-permute-start | bytes 73736 | tf_op jit(solution)/shard_map/merge/ppermute | solution.py:386
  28.1 1.3 %collective-permute-done.10.refs_11_ = f32[8,768]{1,0:T(8,128)S(1)} collective-permute-done((f32[8,768]{1,0:T(8,128)S(1)}, f32[8,768]{1,0:T(8,128)S(1)}, u32[]{:S(2)}, u32[]{:S(2)}) %collective-permute-start.10) | collective-permute-done | bytes 24608 | tf_op jit(solution)/shard_map/merge/ppermute | solution.py:386
  29.4 2.4 %collective-permute-start.13 = (bf16[192,256]{1,0:T(8,128)(2,1)S(1)}, bf16[192,256]{1,0:T(8,128)(2,1)S(1)}, u32[]{:S(2)}, u32[]{:S(2)}) collective-permute-start(bf16[192,256]{1,0:T(8,128)(2,1)S(1)} %get-tuple-element.61), channel_id=1, source_target_pairs={{0,24},{8,16},{16,8},{24,0},{1,25},{9,17},{17,9},{25,1},{2,26},{10... | collective-permute-start | bytes 294920 | tf_op jit(solution)/shard_map/merge/ppermute | solution.py:386
  31.8 0.0 collective-permute-done.9.refs_10_
  31.8 0.0 collective-permute-done.8.refs_9_
  31.8 0.0 collective-permute-done.11.refs_2_
  31.8 0.0 collective-permute-done.12.refs_3_
  31.8 3.1 %gradients.2 = (f32[2,128,768]{2,1,0:T(8,128)S(1)}, f32[2,768]{1,0:T(2,128)S(1)}, f32[2,768]{1,0:T(2,128)S(1)}, f32[192,128]{1,0:T(8,128)S(1)}, bf16[2,2,192,256...) custom-call(bf16[2,192,256]{2,1,0:T(8,128)(2,1)S(1)} %get-tuple-element.44.refs_0_, ...), custom_call_target="tpu_custom_call" | custom-call | flops 12079595520 | bytes 3354624 | tf_op jit(solution)/shard_map/gradients/pallas_call | solution.py:349
  34.9 5.8 %collective-permute-start.18 = (bf16[1,2,192,256]{3,2,1,0:T(8,128)(2,1)S(1)}, bf16[1,2,192,256]{3,2,1,0:T(8,128)(2,1)S(1)}, u32[]{:S(2)}, u32[]{:S(2)}) collective-permute-start(bf16[1,2,192,256]{3,2,1,0:T(8,128)(2,1)S(1)} %get-tuple-element.76), channel_id=1, source_target_pairs={{0,0},{1,2},{2,1},{3,3},{4,4},{5,6},{6,5},{7,7},{8,8},{9,10},{10,9... | collective-permute-start | bytes 589832 | tf_op jit(solution)/shard_map/gradients/ppermute | solution.py:455
  40.7 0.1 collective-permute-start.17
  40.8 1.7 %gradients.3 = (bf16[192,256]{1,0:T(8,128)(2,1)S(1)}, bf16[192,256]{1,0:T(8,128)(2,1)S(1)}, bf16[192,256]{1,0:T(8,128)(2,1)S(1)}, bf16[192,256]{1,0:T(8,128)(2,1...) custom-call(bf16[2,192,256]{2,1,0:T(8,128)(2,1)S(1)} %get-tuple-element.44.refs_0_, ...), custom_call_target="tpu_custom_call" | custom-call | flops 6039797760 | bytes 2764800 | tf_op jit(solution)/shard_map/gradients/pallas_call | solution.py:349
  42.5 0.0 collective-permute-done.13.refs_1_
  42.5 1.1 %collective-permute-start.14 = (bf16[192,256]{1,0:T(8,128)(2,1)S(1)}, bf16[192,256]{1,0:T(8,128)(2,1)S(1)}, u32[]{:S(2)}, u32[]{:S(2)}) collective-permute-start(bf16[192,256]{1,0:T(8,128)(2,1)S(1)} %get-tuple-element.68), channel_id=1, source_target_pairs={{0,16},{8,24},{16,0},{24,8},{1,17},{9,25},{17,1},{25,9},{2,18},{10... | collective-permute-start | bytes 294920 | tf_op jit(solution)/shard_map/return/ppermute | solution.py:386
  43.6 0.0 collective-permute-start.15
  43.6 1.6 %collective-permute-start.16 = (bf16[192,256]{1,0:T(8,128)(2,1)S(1)}, bf16[192,256]{1,0:T(8,128)(2,1)S(1)}, u32[]{:S(2)}, u32[]{:S(2)}) collective-permute-start(bf16[192,256]{1,0:T(8,128)(2,1)S(1)} %get-tuple-element.70), channel_id=1, source_target_pairs={{0,8},{8,0},{16,24},{24,16},{1,9},{9,1},{17,25},{25,17},{2,10},{10... | collective-permute-start | bytes 294920 | tf_op jit(solution)/shard_map/return/ppermute | solution.py:386
  45.2 0.0 collective-permute-done.18
  45.2 0.0 collective-permute-done.17.refs_2_
  45.2 0.1 fusion
  45.3 0.3 collective-permute-start.19
  45.6 3.0 %collective-permute-start.20 = (bf16[2,192,256]{2,1,0:T(8,128)(2,1)S(1)}, bf16[2,192,256]{2,1,0:T(8,128)(2,1)S(1)}, u32[]{:S(2)}, u32[]{:S(2)}) collective-permute-start(bf16[2,192,256]{2,1,0:T(8,128)(2,1)S(1)} %get-tuple-element.80), channel_id=1, source_target_pairs={{0,0},{1,2},{2,1},{3,3},{4,4},{5,6},{6,5},{7,7},{8,8},{9,10},{10,9... | collective-permute-start | bytes 589832 | tf_op jit(solution)/shard_map/return/ppermute | solution.py:465
  48.7 1.5 %collective-permute-done.14.refs_5_ = bf16[192,256]{1,0:T(8,128)(2,1)S(1)} collective-permute-done((bf16[192,256]{1,0:T(8,128)(2,1)S(1)}, bf16[192,256]{1,0:T(8,128)(2,1)S(1)}, u32[]{:S(2)}, u32[]{:S(2)}) %collective-permute-start.14) | collective-permute-done | bytes 98336 | tf_op jit(solution)/shard_map/return/ppermute | solution.py:386
  50.1 0.0 collective-permute-done.15.refs_6_
  50.1 2.1 %collective-permute-done.16.refs_7_ = bf16[192,256]{1,0:T(8,128)(2,1)S(1)} collective-permute-done((bf16[192,256]{1,0:T(8,128)(2,1)S(1)}, bf16[192,256]{1,0:T(8,128)(2,1)S(1)}, u32[]{:S(2)}, u32[]{:S(2)}) %collective-permute-start.16) | collective-permute-done | bytes 98336 | tf_op jit(solution)/shard_map/return/ppermute | solution.py:386
  52.2 1.0 %finish.2 = (bf16[192,256]{1,0:T(8,128)(2,1)}, bf16[192,256]{1,0:T(8,128)(2,1)}) custom-call(bf16[192,256]{1,0:T(8,128)(2,1)S(1)} %get-tuple-element.46.refs_0_, bf16[192,256]{1,0:T(8,128)(2,1)S(1)} %collective-permute-done.13.refs_1_, bf16[192,256]{1,0:T(8,128)(2,1)S(1)} %collective-permute-done.11.refs_2_, ...), custom_call_target="tpu_custom_call" | custom-call | flops 9059696640 | bytes 1376256 | tf_op jit(solution)/shard_map/finish/pallas_call | solution.py:349
  53.2 0.0 collective-permute-done.19.refs_0_
  53.3 0.0 collective-permute-done.20.refs_1_
  53.3 0.9 %finish.3 = (bf16[192,256]{1,0:T(8,128)(2,1)}, bf16[192,256]{1,0:T(8,128)(2,1)}) custom-call(bf16[2,192,256]{2,1,0:T(8,128)(2,1)S(1)} %collective-permute-done.19.refs_0_, bf16[2,192,256]{2,1,0:T(8,128)(2,1)S(1)} %collective-permute-done.20.refs_1_, bf16[2,2,192,256]{3,2,1,0:T(8,128)(2,1)S(1)} %collective-permute-done.17.refs_2_, ...), custom_call_target="tpu_custom_call" | custom-call | bytes 1474560 | tf_op jit(solution)/shard_map/finish/pallas_call | solution.py:349
Async XLA Ops:
  1.9 10.3 %collective-permute-start.4 = (bf16[2,192,256]{2,1,0:T(8,128)(2,1)S(1)}, bf16[2,192,256]{2,1,0:T(8,128)(2,1)S(1)}, u32[]{:S(2)}, u32[]{:S(2)}) collective-permute-start(bf16[2,192,256]{2,1,0:T(8,128)(2,1)S(1)} %get-tuple-element.45.refs_3_.refs_1_.refs_4_), channel_id=1, source_target_pairs={{0,4},{4,0},{1,5},{5,1},{2,6},{6,2},{3,7},{7,3},{8,12},{12,8},{9,1... | collective-permute-start | bytes 589832 | tf_op jit(solution)/shard_map/halo/ppermute | solution.py:391
  4.0 10.9 %collective-permute-start.1 = (bf16[2,192,256]{2,1,0:T(8,128)(2,1)S(1)}, bf16[2,192,256]{2,1,0:T(8,128)(2,1)S(1)}, u32[]{:S(2)}, u32[]{:S(2)}) collective-permute-start(bf16[2,192,256]{2,1,0:T(8,128)(2,1)S(1)} %get-tuple-element.44.refs_0_), channel_id=1, source_target_pairs={{0,16},{8,24},{16,0},{24,8},{1,17},{9,25},{17,1},{25,9},{2,18},{10... | collective-permute-start | bytes 589832 | tf_op jit(solution)/shard_map/halo/ppermute | solution.py:386
  6.3 10.2 %collective-permute-start = (bf16[2,192,256]{2,1,0:T(8,128)(2,1)S(1)}, bf16[2,192,256]{2,1,0:T(8,128)(2,1)S(1)}, u32[]{:S(2)}, u32[]{:S(2)}) collective-permute-start(bf16[2,192,256]{2,1,0:T(8,128)(2,1)S(1)} %get-tuple-element.44.refs_0_), channel_id=1, source_target_pairs={{0,8},{8,0},{16,24},{24,16},{1,9},{9,1},{17,25},{25,17},{2,10},{10... | collective-permute-start | bytes 589832 | tf_op jit(solution)/shard_map/halo/ppermute | solution.py:386
  7.6 9.2 %collective-permute-start.3 = (bf16[2,192,256]{2,1,0:T(8,128)(2,1)S(1)}, bf16[2,192,256]{2,1,0:T(8,128)(2,1)S(1)}, u32[]{:S(2)}, u32[]{:S(2)}) collective-permute-start(bf16[2,192,256]{2,1,0:T(8,128)(2,1)S(1)} %get-tuple-element.45.refs_3_.refs_1_.refs_4_), channel_id=1, source_target_pairs={{0,0},{1,2},{2,1},{3,3},{4,4},{5,6},{6,5},{7,7},{8,8},{9,10},{10,9... | collective-permute-start | bytes 589832 | tf_op jit(solution)/shard_map/halo/ppermute | solution.py:396
  12.2 4.7 %collective-permute-start.2 = (bf16[2,192,256]{2,1,0:T(8,128)(2,1)S(1)}, bf16[2,192,256]{2,1,0:T(8,128)(2,1)S(1)}, u32[]{:S(2)}, u32[]{:S(2)}) collective-permute-start(bf16[2,192,256]{2,1,0:T(8,128)(2,1)S(1)} %get-tuple-element.45.refs_3_.refs_1_.refs_4_), channel_id=1, source_target_pairs={{0,1},{1,0},{2,3},{3,2},{4,5},{5,4},{6,7},{7,6},{8,9},{9,8},{10,11... | collective-permute-start | bytes 589832 | tf_op jit(solution)/shard_map/halo/ppermute | solution.py:396
  12.2 7.0 %collective-permute-start.6 = (bf16[2,192,256]{2,1,0:T(8,128)(2,1)S(1)}, bf16[2,192,256]{2,1,0:T(8,128)(2,1)S(1)}, u32[]{:S(2)}, u32[]{:S(2)}) collective-permute-start(bf16[2,192,256]{2,1,0:T(8,128)(2,1)S(1)} %collective-permute-done.4.refs_6_.refs_4_.refs_5_), channel_id=1, source_target_pairs={{0,0},{1,2},{2,1},{3,3},{4,4},{5,6},{6,5},{7,7},{8,8},{9,10},{10,9... | collective-permute-start | bytes 589832 | tf_op jit(solution)/shard_map/halo/ppermute | solution.py:396
  14.9 4.4 %collective-permute-start.5 = (bf16[2,192,256]{2,1,0:T(8,128)(2,1)S(1)}, bf16[2,192,256]{2,1,0:T(8,128)(2,1)S(1)}, u32[]{:S(2)}, u32[]{:S(2)}) collective-permute-start(bf16[2,192,256]{2,1,0:T(8,128)(2,1)S(1)} %collective-permute-done.4.refs_6_.refs_4_.refs_5_), channel_id=1, source_target_pairs={{0,1},{1,0},{2,3},{3,2},{4,5},{5,4},{6,7},{7,6},{8,9},{9,8},{10,11... | collective-permute-start | bytes 589832 | tf_op jit(solution)/shard_map/halo/ppermute | solution.py:396
  16.5 7.0 %collective-permute-start.7 = (bf16[2,192,256]{2,1,0:T(8,128)(2,1)S(1)}, bf16[2,192,256]{2,1,0:T(8,128)(2,1)S(1)}, u32[]{:S(2)}, u32[]{:S(2)}) collective-permute-start(bf16[2,192,256]{2,1,0:T(8,128)(2,1)S(1)} %collective-permute-done.1.refs_2_), channel_id=1, source_target_pairs={{0,8},{8,0},{16,24},{24,16},{1,9},{9,1},{17,25},{25,17},{2,10},{10... | collective-permute-start | bytes 589832 | tf_op jit(solution)/shard_map/halo/ppermute | solution.py:386
  21.7 10.1 %collective-permute-start.11 = (bf16[192,256]{1,0:T(8,128)(2,1)S(1)}, bf16[192,256]{1,0:T(8,128)(2,1)S(1)}, u32[]{:S(2)}, u32[]{:S(2)}) collective-permute-start(bf16[192,256]{1,0:T(8,128)(2,1)S(1)} %get-tuple-element.49), channel_id=1, source_target_pairs={{0,16},{8,24},{16,0},{24,8},{1,17},{9,25},{17,1},{25,9},{2,18},{10... | collective-permute-start | bytes 294920 | tf_op jit(solution)/shard_map/merge/ppermute | solution.py:386
  22.4 9.4 %collective-permute-start.12 = (bf16[192,256]{1,0:T(8,128)(2,1)S(1)}, bf16[192,256]{1,0:T(8,128)(2,1)S(1)}, u32[]{:S(2)}, u32[]{:S(2)}) collective-permute-start(bf16[192,256]{1,0:T(8,128)(2,1)S(1)} %get-tuple-element.50), channel_id=1, source_target_pairs={{0,8},{8,0},{16,24},{24,16},{1,9},{9,1},{17,25},{25,17},{2,10},{10... | collective-permute-start | bytes 294920 | tf_op jit(solution)/shard_map/merge/ppermute | solution.py:386
  24.5 4.9 %collective-permute-start.10 = (f32[8,768]{1,0:T(8,128)S(1)}, f32[8,768]{1,0:T(8,128)S(1)}, u32[]{:S(2)}, u32[]{:S(2)}) collective-permute-start(f32[8,768]{1,0:T(8,128)S(1)} %get-tuple-element.51.refs_8_), channel_id=1, source_target_pairs={{0,24},{8,16},{16,8},{24,0},{1,25},{9,17},{17,9},{25,1},{2,26},{10... | collective-permute-start | bytes 73736 | tf_op jit(solution)/shard_map/merge/ppermute | solution.py:386
  27.2 4.6 %collective-permute-start.9 = (f32[8,768]{1,0:T(8,128)S(1)}, f32[8,768]{1,0:T(8,128)S(1)}, u32[]{:S(2)}, u32[]{:S(2)}) collective-permute-start(f32[8,768]{1,0:T(8,128)S(1)} %get-tuple-element.51.refs_8_), channel_id=1, source_target_pairs={{0,16},{8,24},{16,0},{24,8},{1,17},{9,25},{17,1},{25,9},{2,18},{10... | collective-permute-start | bytes 73736 | tf_op jit(solution)/shard_map/merge/ppermute | solution.py:386
  27.2 4.6 %collective-permute-start.8 = (f32[8,768]{1,0:T(8,128)S(1)}, f32[8,768]{1,0:T(8,128)S(1)}, u32[]{:S(2)}, u32[]{:S(2)}) collective-permute-start(f32[8,768]{1,0:T(8,128)S(1)} %get-tuple-element.51.refs_8_), channel_id=1, source_target_pairs={{0,8},{8,0},{16,24},{24,16},{1,9},{9,1},{17,25},{25,17},{2,10},{10... | collective-permute-start | bytes 73736 | tf_op jit(solution)/shard_map/merge/ppermute | solution.py:386
  29.4 13.1 %collective-permute-start.13 = (bf16[192,256]{1,0:T(8,128)(2,1)S(1)}, bf16[192,256]{1,0:T(8,128)(2,1)S(1)}, u32[]{:S(2)}, u32[]{:S(2)}) collective-permute-start(bf16[192,256]{1,0:T(8,128)(2,1)S(1)} %get-tuple-element.61), channel_id=1, source_target_pairs={{0,24},{8,16},{16,8},{24,0},{1,25},{9,17},{17,9},{25,1},{2,26},{10... | collective-permute-start | bytes 294920 | tf_op jit(solution)/shard_map/merge/ppermute | solution.py:386
  34.9 10.3 %collective-permute-start.18 = (bf16[1,2,192,256]{3,2,1,0:T(8,128)(2,1)S(1)}, bf16[1,2,192,256]{3,2,1,0:T(8,128)(2,1)S(1)}, u32[]{:S(2)}, u32[]{:S(2)}) collective-permute-start(bf16[1,2,192,256]{3,2,1,0:T(8,128)(2,1)S(1)} %get-tuple-element.76), channel_id=1, source_target_pairs={{0,0},{1,2},{2,1},{3,3},{4,4},{5,6},{6,5},{7,7},{8,8},{9,10},{10,9... | collective-permute-start | bytes 589832 | tf_op jit(solution)/shard_map/gradients/ppermute | solution.py:455
  40.7 4.5 %collective-permute-start.17 = (bf16[2,2,192,256]{3,2,1,0:T(8,128)(2,1)S(1)}, bf16[2,2,192,256]{3,2,1,0:T(8,128)(2,1)S(1)}, u32[]{:S(2)}, u32[]{:S(2)}) collective-permute-start(bf16[2,2,192,256]{3,2,1,0:T(8,128)(2,1)S(1)} %get-tuple-element.78), channel_id=1, source_target_pairs={{0,1},{1,0},{2,3},{3,2},{4,5},{5,4},{6,7},{7,6},{8,9},{9,8},{10,11... | collective-permute-start | bytes 1179656 | tf_op jit(solution)/shard_map/gradients/ppermute | solution.py:452
  42.5 7.6 %collective-permute-start.14 = (bf16[192,256]{1,0:T(8,128)(2,1)S(1)}, bf16[192,256]{1,0:T(8,128)(2,1)S(1)}, u32[]{:S(2)}, u32[]{:S(2)}) collective-permute-start(bf16[192,256]{1,0:T(8,128)(2,1)S(1)} %get-tuple-element.68), channel_id=1, source_target_pairs={{0,16},{8,24},{16,0},{24,8},{1,17},{9,25},{17,1},{25,9},{2,18},{10... | collective-permute-start | bytes 294920 | tf_op jit(solution)/shard_map/return/ppermute | solution.py:386
  43.6 6.5 %collective-permute-start.15 = (bf16[192,256]{1,0:T(8,128)(2,1)S(1)}, bf16[192,256]{1,0:T(8,128)(2,1)S(1)}, u32[]{:S(2)}, u32[]{:S(2)}) collective-permute-start(bf16[192,256]{1,0:T(8,128)(2,1)S(1)} %get-tuple-element.69), channel_id=1, source_target_pairs={{0,24},{8,16},{16,8},{24,0},{1,25},{9,17},{17,9},{25,1},{2,26},{10... | collective-permute-start | bytes 294920 | tf_op jit(solution)/shard_map/return/ppermute | solution.py:386
  43.6 8.6 %collective-permute-start.16 = (bf16[192,256]{1,0:T(8,128)(2,1)S(1)}, bf16[192,256]{1,0:T(8,128)(2,1)S(1)}, u32[]{:S(2)}, u32[]{:S(2)}) collective-permute-start(bf16[192,256]{1,0:T(8,128)(2,1)S(1)} %get-tuple-element.70), channel_id=1, source_target_pairs={{0,8},{8,0},{16,24},{24,16},{1,9},{9,1},{17,25},{25,17},{2,10},{10... | collective-permute-start | bytes 294920 | tf_op jit(solution)/shard_map/return/ppermute | solution.py:386
  45.3 8.0 %collective-permute-start.19 = (bf16[2,192,256]{2,1,0:T(8,128)(2,1)S(1)}, bf16[2,192,256]{2,1,0:T(8,128)(2,1)S(1)}, u32[]{:S(2)}, u32[]{:S(2)}) collective-permute-start(bf16[2,192,256]{2,1,0:T(8,128)(2,1)S(1)} %fusion), channel_id=1, source_target_pairs={{0,4},{4,0},{1,5},{5,1},{2,6},{6,2},{3,7},{7,3},{8,12},{12,8},{9,1... | collective-permute-start | bytes 589832 | tf_op jit(solution)/shard_map/return/ppermute | solution.py:464
  45.6 7.6 %collective-permute-start.20 = (bf16[2,192,256]{2,1,0:T(8,128)(2,1)S(1)}, bf16[2,192,256]{2,1,0:T(8,128)(2,1)S(1)}, u32[]{:S(2)}, u32[]{:S(2)}) collective-permute-start(bf16[2,192,256]{2,1,0:T(8,128)(2,1)S(1)} %get-tuple-element.80), channel_id=1, source_target_pairs={{0,0},{1,2},{2,1},{3,3},{4,4},{5,6},{6,5},{7,7},{8,8},{9,10},{10,9... | collective-permute-start | bytes 589832 | tf_op jit(solution)/shard_map/return/ppermute | solution.py:465

commit v13 on v8

--- a/solution.py
+++ b/solution.py
@@ -415,9 +415,9 @@
         o0, o1, o2, first = forward((qg, qg1, qg2), None)
         o3, stat = forward((qg3,), first)
     with jax.named_scope("merge"):
-        stats = [stat] + [other_frames(stat, d) for d in (1, 2, 3)]
         outs = [other_frames(o, d) for d, o in ((3, o3), (2, o2), (1, o1))]
-        stats, outs[1:] = lax.optimization_barrier((stats, outs[1:]))
+        stat_near, outs[1:] = lax.optimization_barrier((stat, outs[1:]))
+        stats = [stat, other_frames(stat_near, 1), other_frames(stat, 2), other_frames(stat, 3)]
 
     queries = (qg, qg1, qg2, qg3)
     col_shape = jax.ShapeDtypeStruct((grid_rows, 2, cells, chan), BF16)

time: 53.7 us -> 52.9 us (0.985)
  starting transfers between devices: 31.8 us -> 31.1 us
    ppermute x12, starting transfers between devices: 15.3 us -> 14 us  [other_frames(): lax.ppermute(x, 'ta', [(i, i ^ distance) for i in range(sizes['ta'])])]
    ppermute x2, starting transfers between devices: 5.88 us -> 6.54 us  [shards(): sides = [lax.ppermute(x, 'wa', pairs) for x, pairs in zip(sides, col_sides)]]
  transfers between devices with their start and end apart: 20 -> 20, of which waited for: 6 -> 7; matrix products, arithmetic and copies ran while one was open for 0% -> 0% of each run, Pallas kernels for 17% -> 18%
where the time goes in v13:
time: 52.9 us; the launch traced here: 52.7 us
  starting transfers between devices  31.1 us (59%)
  Pallas kernels  11.4 us (22%)
  waiting for transfers between devices  9.36 us (18%)
  between operations  0.72 us (1%)
    ppermute x12, starting transfers between devices, other_frames(): lax.ppermute(x, 'ta', [(i, i ^ distance) for i in range(sizes['ta'])])  14 us
    pallas_call x7, Pallas kernels, call(): pl.pallas_call(kernel, out_shape=out_shape, in_specs=[pl.BlockSpec(memory...  11.4 us
    ppermute x4, starting transfers between devices, shards(): lax.ppermute(block, 'wa', pairs)  8.2 us
    ppermute x2, starting transfers between devices, shards(): sides = [lax.ppermute(x, 'wa', pairs) for x, pairs in zip(sides, col_sides)]  6.54 us
    ppermute x12, waiting for transfers between devices, other_frames(): lax.ppermute(x, 'ta', [(i, i ^ distance) for i in range(sizes['ta'])])  6.52 us
    ppermute x4, waiting for transfers between devices, shards(): lax.ppermute(block, 'wa', pairs)  2.4 us
    ppermute x1, starting transfers between devices, shards(): kv_rows = [kv] + [lax.ppermute(kv, 'ha', pairs) for pairs in row_sides]  2.11 us
  transfers between devices with their start and end apart: 20, of which 7 were waited for; matrix products, arithmetic and copies ran while one was open for 0% of the time, Pallas kernels for 18%

profile of v13, /device:TPU:1, one launch (start us, length us, event | category | flops | bytes accessed | tf_op | source)
XLA Modules:
  0.0 52.7 jit_solution(14757612554989193642)
XLA Ops:
  0.6 1.3 %rotate.1 = (bf16[2,192,256]{2,1,0:T(8,128)(2,1)S(1)}, bf16[2,192,256]{2,1,0:T(8,128)(2,1)S(1)}, f32[3,192,128]{2,1,0:T(8,128)S(1)}) custom-call(bf16[192,256]{1,0:T(8,128)(2,1)} %bitcast.10, bf16[192,256]{1,0:T(8,128)(2,1)} %bitcast.11, bf16[192,256]{1,0:T(8,128)(2,1)} %bitcast.12, bf16[192,256]{1,0:T(8,128)(2,1)} %bitcast.13, ...), custom_call_target="tpu_custom_call" | custom-call | bytes 1179648 | tf_op jit(solution)/shard_map/rotate/pallas_call | solution.py:342
  1.9 2.1 %collective-permute-start.4 = (bf16[2,192,256]{2,1,0:T(8,128)(2,1)S(1)}, bf16[2,192,256]{2,1,0:T(8,128)(2,1)S(1)}, u32[]{:S(2)}, u32[]{:S(2)}) collective-permute-start(bf16[2,192,256]{2,1,0:T(8,128)(2,1)S(1)} %get-tuple-element.38.refs_3_.refs_1_.refs_4_), channel_id=1, source_target_pairs={{0,4},{4,0},{1,5},{5,1},{2,6},{6,2},{3,7},{7,3},{8,12},{12,8},{9,1... | collective-permute-start | bytes 589832 | tf_op jit(solution)/shard_map/halo/ppermute | solution.py:384
  4.0 2.3 %collective-permute-start.1 = (bf16[2,192,256]{2,1,0:T(8,128)(2,1)S(1)}, bf16[2,192,256]{2,1,0:T(8,128)(2,1)S(1)}, u32[]{:S(2)}, u32[]{:S(2)}) collective-permute-start(bf16[2,192,256]{2,1,0:T(8,128)(2,1)S(1)} %get-tuple-element.37.refs_0_), channel_id=1, source_target_pairs={{0,16},{8,24},{16,0},{24,8},{1,17},{9,25},{17,1},{25,9},{2,18},{10... | collective-permute-start | bytes 589832 | tf_op jit(solution)/shard_map/halo/ppermute | solution.py:379
  6.3 1.3 %collective-permute-start = (bf16[2,192,256]{2,1,0:T(8,128)(2,1)S(1)}, bf16[2,192,256]{2,1,0:T(8,128)(2,1)S(1)}, u32[]{:S(2)}, u32[]{:S(2)}) collective-permute-start(bf16[2,192,256]{2,1,0:T(8,128)(2,1)S(1)} %get-tuple-element.37.refs_0_), channel_id=1, source_target_pairs={{0,8},{8,0},{16,24},{24,16},{1,9},{9,1},{17,25},{25,17},{2,10},{10... | collective-permute-start | bytes 589832 | tf_op jit(solution)/shard_map/halo/ppermute | solution.py:379
  7.6 4.5 %collective-permute-start.3 = (bf16[2,192,256]{2,1,0:T(8,128)(2,1)S(1)}, bf16[2,192,256]{2,1,0:T(8,128)(2,1)S(1)}, u32[]{:S(2)}, u32[]{:S(2)}) collective-permute-start(bf16[2,192,256]{2,1,0:T(8,128)(2,1)S(1)} %get-tuple-element.38.refs_3_.refs_1_.refs_4_), channel_id=1, source_target_pairs={{0,0},{1,2},{2,1},{3,3},{4,4},{5,6},{6,5},{7,7},{8,8},{9,10},{10,9... | collective-permute-start | bytes 589832 | tf_op jit(solution)/shard_map/halo/ppermute | solution.py:389
  12.2 0.1 collective-permute-start.2
  12.2 0.0 collective-permute-done.4.refs_6_.refs_4_.refs_5_
  12.2 1.9 %collective-permute-start.6 = (bf16[2,192,256]{2,1,0:T(8,128)(2,1)S(1)}, bf16[2,192,256]{2,1,0:T(8,128)(2,1)S(1)}, u32[]{:S(2)}, u32[]{:S(2)}) collective-permute-start(bf16[2,192,256]{2,1,0:T(8,128)(2,1)S(1)} %collective-permute-done.4.refs_6_.refs_4_.refs_5_), channel_id=1, source_target_pairs={{0,0},{1,2},{2,1},{3,3},{4,4},{5,6},{6,5},{7,7},{8,8},{9,10},{10,9... | collective-permute-start | bytes 589832 | tf_op jit(solution)/shard_map/halo/ppermute | solution.py:389
  14.2 0.7 %collective-permute-done.1.refs_2_ = bf16[2,192,256]{2,1,0:T(8,128)(2,1)S(1)} collective-permute-done((bf16[2,192,256]{2,1,0:T(8,128)(2,1)S(1)}, bf16[2,192,256]{2,1,0:T(8,128)(2,1)S(1)}, u32[]{:S(2)}, u32[]{:S(2)}) %collective-permute-start.1) | collective-permute-done | bytes 196640 | tf_op jit(solution)/shard_map/halo/ppermute | solution.py:379
  14.9 1.7 %collective-permute-start.5 = (bf16[2,192,256]{2,1,0:T(8,128)(2,1)S(1)}, bf16[2,192,256]{2,1,0:T(8,128)(2,1)S(1)}, u32[]{:S(2)}, u32[]{:S(2)}) collective-permute-start(bf16[2,192,256]{2,1,0:T(8,128)(2,1)S(1)} %collective-permute-done.4.refs_6_.refs_4_.refs_5_), channel_id=1, source_target_pairs={{0,1},{1,0},{2,3},{3,2},{4,5},{5,4},{6,7},{7,6},{8,9},{9,8},{10,11... | collective-permute-start | bytes 589832 | tf_op jit(solution)/shard_map/halo/ppermute | solution.py:389
  16.5 0.0 collective-permute-done.refs_1_
  16.5 0.3 collective-permute-start.7
  16.8 0.0 collective-permute-done.3.refs_5_.refs_3_.refs_6_
  16.8 0.0 collective-permute-done.2.refs_4_.refs_2_
  16.8 2.4 %collective-permute-done.6.refs_8_.refs_6_.refs_7_ = bf16[2,192,256]{2,1,0:T(8,128)(2,1)S(1)} collective-permute-done((bf16[2,192,256]{2,1,0:T(8,128)(2,1)S(1)}, bf16[2,192,256]{2,1,0:T(8,128)(2,1)S(1)}, u32[]{:S(2)}, u32[]{:S(2)}) %collective-permute-start.6) | collective-permute-done | bytes 196640 | tf_op jit(solution)/shard_map/halo/ppermute | solution.py:389
  19.2 0.0 collective-permute-done.5.refs_7_.refs_5_
  19.2 2.4 %attend.2 = (bf16[192,256]{1,0:T(8,128)(2,1)S(1)}, bf16[192,256]{1,0:T(8,128)(2,1)S(1)}, bf16[192,256]{1,0:T(8,128)(2,1)S(1)}, f32[576,128]{1,0:T(8,128)S(1)}) custom-call(bf16[2,192,256]{2,1,0:T(8,128)(2,1)S(1)} %get-tuple-element.37.refs_0_, bf16[2,192,256]{2,1,0:T(8,128)(2,1)S(1)} %collective-permute-done.refs_1_, ...), custom_call_target="tpu_custom_call" | custom-call | flops 5435817984 | bytes 2359296 | tf_op jit(solution)/shard_map/attend/pallas_call | solution.py:342
  21.7 0.8 %collective-permute-start.8 = (bf16[192,256]{1,0:T(8,128)(2,1)S(1)}, bf16[192,256]{1,0:T(8,128)(2,1)S(1)}, u32[]{:S(2)}, u32[]{:S(2)}) collective-permute-start(bf16[192,256]{1,0:T(8,128)(2,1)S(1)} %get-tuple-element.42), channel_id=1, source_target_pairs={{0,16},{8,24},{16,0},{24,8},{1,17},{9,25},{17,1},{25,9},{2,18},{10... | collective-permute-start | bytes 294920 | tf_op jit(solution)/shard_map/merge/ppermute | solution.py:379
  22.4 1.0 %collective-permute-start.9 = (bf16[192,256]{1,0:T(8,128)(2,1)S(1)}, bf16[192,256]{1,0:T(8,128)(2,1)S(1)}, u32[]{:S(2)}, u32[]{:S(2)}) collective-permute-start(bf16[192,256]{1,0:T(8,128)(2,1)S(1)} %get-tuple-element.43), channel_id=1, source_target_pairs={{0,8},{8,0},{16,24},{24,16},{1,9},{9,1},{17,25},{25,17},{2,10},{10... | collective-permute-start | bytes 294920 | tf_op jit(solution)/shard_map/merge/ppermute | solution.py:379
  23.5 0.0 collective-permute-done.7.refs_0_.refs_3_
  23.5 1.0 %attend.3 = (bf16[192,256]{1,0:T(8,128)(2,1)S(1)}, f32[8,768]{1,0:T(8,128)S(1)}) custom-call(bf16[2,192,256]{2,1,0:T(8,128)(2,1)S(1)} %collective-permute-done.7.refs_0_.refs_3_, bf16[2,192,256]{2,1,0:T(8,128)(2,1)S(1)} %get-tuple-element.38.refs_3_.refs_1_.refs_4_, bf16[2,192,256]{2,1,0:T(8,128)(2,1)S(1)} %collective-permute-done.2.refs_4_.refs_2_, ...), custom_call_target="tpu_custom_call" | custom-call | flops 1811939328 | bytes 1794048 | tf_op jit(solution)/shard_map/attend/pallas_call | solution.py:342
  24.5 2.7 %collective-permute-start.12 = (f32[8,768]{1,0:T(8,128)S(1)}, f32[8,768]{1,0:T(8,128)S(1)}, u32[]{:S(2)}, u32[]{:S(2)}) collective-permute-start(f32[8,768]{1,0:T(8,128)S(1)} %get-tuple-element.44.refs_8_), channel_id=1, source_target_pairs={{0,24},{8,16},{16,8},{24,0},{1,25},{9,17},{17,9},{25,1},{2,26},{10... | collective-permute-start | bytes 73736 | tf_op jit(solution)/shard_map/merge/ppermute | solution.py:379
  27.2 0.0 collective-permute-start.11
  27.2 1.6 %collective-permute-done.8.refs_2_ = bf16[192,256]{1,0:T(8,128)(2,1)S(1)} collective-permute-done((bf16[192,256]{1,0:T(8,128)(2,1)S(1)}, bf16[192,256]{1,0:T(8,128)(2,1)S(1)}, u32[]{:S(2)}, u32[]{:S(2)}) %collective-permute-start.8) | collective-permute-done | bytes 98336 | tf_op jit(solution)/shard_map/merge/ppermute | solution.py:379
  28.8 0.0 collective-permute-done.9.refs_3_
  28.8 0.0 collective-permute-start.10
  28.8 1.9 %collective-permute-start.13 = (bf16[192,256]{1,0:T(8,128)(2,1)S(1)}, bf16[192,256]{1,0:T(8,128)(2,1)S(1)}, u32[]{:S(2)}, u32[]{:S(2)}) collective-permute-start(bf16[192,256]{1,0:T(8,128)(2,1)S(1)} %get-tuple-element.51), channel_id=1, source_target_pairs={{0,24},{8,16},{16,8},{24,0},{1,25},{9,17},{17,9},{25,1},{2,26},{10... | collective-permute-start | bytes 294920 | tf_op jit(solution)/shard_map/merge/ppermute | solution.py:379
  30.8 0.0 collective-permute-done.12.refs_11_
  30.8 0.0 collective-permute-done.11.refs_10_
  30.8 0.7 %collective-permute-done.10.refs_9_ = f32[8,768]{1,0:T(8,128)S(1)} collective-permute-done((f32[8,768]{1,0:T(8,128)S(1)}, f32[8,768]{1,0:T(8,128)S(1)}, u32[]{:S(2)}, u32[]{:S(2)}) %collective-permute-start.10) | collective-permute-done | bytes 24608 | tf_op jit(solution)/shard_map/merge/ppermute | solution.py:379
  31.5 3.1 %gradients.2 = (f32[2,128,768]{2,1,0:T(8,128)S(1)}, f32[2,768]{1,0:T(2,128)S(1)}, f32[2,768]{1,0:T(2,128)S(1)}, f32[192,128]{1,0:T(8,128)S(1)}, bf16[2,2,192,256...) custom-call(bf16[2,192,256]{2,1,0:T(8,128)(2,1)S(1)} %get-tuple-element.37.refs_0_, ...), custom_call_target="tpu_custom_call" | custom-call | flops 12079595520 | bytes 3354624 | tf_op jit(solution)/shard_map/gradients/pallas_call | solution.py:342
  34.6 1.6 %collective-permute-start.17 = (bf16[2,2,192,256]{3,2,1,0:T(8,128)(2,1)S(1)}, bf16[2,2,192,256]{3,2,1,0:T(8,128)(2,1)S(1)}, u32[]{:S(2)}, u32[]{:S(2)}) collective-permute-start(bf16[2,2,192,256]{3,2,1,0:T(8,128)(2,1)S(1)} %get-tuple-element.66), channel_id=1, source_target_pairs={{0,1},{1,0},{2,3},{3,2},{4,5},{5,4},{6,7},{7,6},{8,9},{9,8},{10,11... | collective-permute-start | bytes 1179656 | tf_op jit(solution)/shard_map/gradients/ppermute | solution.py:444
  36.3 4.9 %collective-permute-start.18 = (bf16[2,2,192,256]{3,2,1,0:T(8,128)(2,1)S(1)}, bf16[2,2,192,256]{3,2,1,0:T(8,128)(2,1)S(1)}, u32[]{:S(2)}, u32[]{:S(2)}) collective-permute-start(bf16[2,2,192,256]{3,2,1,0:T(8,128)(2,1)S(1)} %get-tuple-element.67), channel_id=1, source_target_pairs={{0,0},{1,2},{2,1},{3,3},{4,4},{5,6},{6,5},{7,7},{8,8},{9,10},{10,9... | collective-permute-start | bytes 1179656 | tf_op jit(solution)/shard_map/gradients/ppermute | solution.py:444
  41.2 1.7 %gradients.3 = (bf16[192,256]{1,0:T(8,128)(2,1)S(1)}, bf16[192,256]{1,0:T(8,128)(2,1)S(1)}, bf16[192,256]{1,0:T(8,128)(2,1)S(1)}, bf16[192,256]{1,0:T(8,128)(2,1)S(1)}, bf16[2,2,192,256]{3,2,1,0:T(8,128)(2,1)S(1)}) custom-call(bf16[2,192,256]{2,1,0:T(8,128)(2,1)S(1)} %get-tuple-element.37.refs_0_, bf16[2,192,256]{2,1,0:T(8,128)(2,1)S(1)} %collective-permute-done.refs_1_, ...), custom_call_target="tpu_custom_call" | custom-call | flops 6039797760 | bytes 2764800 | tf_op jit(solution)/shard_map/gradients/pallas_call | solution.py:342
  42.9 0.0 collective-permute-done.13.refs_1_
  42.9 0.6 %collective-permute-start.14 = (bf16[192,256]{1,0:T(8,128)(2,1)S(1)}, bf16[192,256]{1,0:T(8,128)(2,1)S(1)}, u32[]{:S(2)}, u32[]{:S(2)}) collective-permute-start(bf16[192,256]{1,0:T(8,128)(2,1)S(1)} %get-tuple-element.58), channel_id=1, source_target_pairs={{0,24},{8,16},{16,8},{24,0},{1,25},{9,17},{17,9},{25,1},{2,26},{10... | collective-permute-start | bytes 294920 | tf_op jit(solution)/shard_map/return/ppermute | solution.py:379
  43.5 0.0 collective-permute-start.15
  43.5 3.0 %collective-permute-start.16 = (bf16[192,256]{1,0:T(8,128)(2,1)S(1)}, bf16[192,256]{1,0:T(8,128)(2,1)S(1)}, u32[]{:S(2)}, u32[]{:S(2)}) collective-permute-start(bf16[192,256]{1,0:T(8,128)(2,1)S(1)} %get-tuple-element.60), channel_id=1, source_target_pairs={{0,8},{8,0},{16,24},{24,16},{1,9},{9,1},{17,25},{25,17},{2,10},{10... | collective-permute-start | bytes 294920 | tf_op jit(solution)/shard_map/return/ppermute | solution.py:379
  46.5 0.0 collective-permute-done.17.refs_1_
  46.5 0.4 collective-permute-done.18.refs_2_
  46.9 0.1 fusion
  47.0 0.3 collective-permute-start.19
  47.3 1.5 %collective-permute-done.14.refs_5_ = bf16[192,256]{1,0:T(8,128)(2,1)S(1)} collective-permute-done((bf16[192,256]{1,0:T(8,128)(2,1)S(1)}, bf16[192,256]{1,0:T(8,128)(2,1)S(1)}, u32[]{:S(2)}, u32[]{:S(2)}) %collective-permute-start.14) | collective-permute-done | bytes 98336 | tf_op jit(solution)/shard_map/return/ppermute | solution.py:379
  48.8 2.0 %collective-permute-done.15.refs_6_ = bf16[192,256]{1,0:T(8,128)(2,1)S(1)} collective-permute-done((bf16[192,256]{1,0:T(8,128)(2,1)S(1)}, bf16[192,256]{1,0:T(8,128)(2,1)S(1)}, u32[]{:S(2)}, u32[]{:S(2)}) %collective-permute-start.15) | collective-permute-done | bytes 98336 | tf_op jit(solution)/shard_map/return/ppermute | solution.py:379
  50.8 0.0 collective-permute-done.16.refs_7_
  50.8 1.0 %finish.2 = (bf16[192,256]{1,0:T(8,128)(2,1)}, bf16[192,256]{1,0:T(8,128)(2,1)}) custom-call(bf16[192,256]{1,0:T(8,128)(2,1)S(1)} %get-tuple-element.39.refs_0_, bf16[192,256]{1,0:T(8,128)(2,1)S(1)} %collective-permute-done.13.refs_1_, bf16[192,256]{1,0:T(8,128)(2,1)S(1)} %collective-permute-done.8.refs_2_, ...), custom_call_target="tpu_custom_call" | custom-call | flops 9059696640 | bytes 1376256 | tf_op jit(solution)/shard_map/finish/pallas_call | solution.py:342
  51.8 0.0 collective-permute-done.19.refs_3_
  51.8 0.9 %finish.3 = (bf16[192,256]{1,0:T(8,128)(2,1)}, bf16[192,256]{1,0:T(8,128)(2,1)}) custom-call(bf16[2,2,192,256]{3,2,1,0:T(8,128)(2,1)S(1)} %get-tuple-element.65.refs_0_, bf16[2,2,192,256]{3,2,1,0:T(8,128)(2,1)S(1)} %collective-permute-done.17.refs_1_, bf16[2,2,192,256]{3,2,1,0:T(8,128)(2,1)S(1)} %collective-permute-done.18.refs_2_, ...), custom_call_target="tpu_custom_call" | custom-call | bytes 1867776 | tf_op jit(solution)/shard_map/finish/pallas_call | solution.py:342
Async XLA Ops:
  1.9 10.3 %collective-permute-start.4 = (bf16[2,192,256]{2,1,0:T(8,128)(2,1)S(1)}, bf16[2,192,256]{2,1,0:T(8,128)(2,1)S(1)}, u32[]{:S(2)}, u32[]{:S(2)}) collective-permute-start(bf16[2,192,256]{2,1,0:T(8,128)(2,1)S(1)} %get-tuple-element.38.refs_3_.refs_1_.refs_4_), channel_id=1, source_target_pairs={{0,4},{4,0},{1,5},{5,1},{2,6},{6,2},{3,7},{7,3},{8,12},{12,8},{9,1... | collective-permute-start | bytes 589832 | tf_op jit(solution)/shard_map/halo/ppermute | solution.py:384
  4.0 10.9 %collective-permute-start.1 = (bf16[2,192,256]{2,1,0:T(8,128)(2,1)S(1)}, bf16[2,192,256]{2,1,0:T(8,128)(2,1)S(1)}, u32[]{:S(2)}, u32[]{:S(2)}) collective-permute-start(bf16[2,192,256]{2,1,0:T(8,128)(2,1)S(1)} %get-tuple-element.37.refs_0_), channel_id=1, source_target_pairs={{0,16},{8,24},{16,0},{24,8},{1,17},{9,25},{17,1},{25,9},{2,18},{10... | collective-permute-start | bytes 589832 | tf_op jit(solution)/shard_map/halo/ppermute | solution.py:379
  6.3 10.2 %collective-permute-start = (bf16[2,192,256]{2,1,0:T(8,128)(2,1)S(1)}, bf16[2,192,256]{2,1,0:T(8,128)(2,1)S(1)}, u32[]{:S(2)}, u32[]{:S(2)}) collective-permute-start(bf16[2,192,256]{2,1,0:T(8,128)(2,1)S(1)} %get-tuple-element.37.refs_0_), channel_id=1, source_target_pairs={{0,8},{8,0},{16,24},{24,16},{1,9},{9,1},{17,25},{25,17},{2,10},{10... | collective-permute-start | bytes 589832 | tf_op jit(solution)/shard_map/halo/ppermute | solution.py:379
  7.6 9.2 %collective-permute-start.3 = (bf16[2,192,256]{2,1,0:T(8,128)(2,1)S(1)}, bf16[2,192,256]{2,1,0:T(8,128)(2,1)S(1)}, u32[]{:S(2)}, u32[]{:S(2)}) collective-permute-start(bf16[2,192,256]{2,1,0:T(8,128)(2,1)S(1)} %get-tuple-element.38.refs_3_.refs_1_.refs_4_), channel_id=1, source_target_pairs={{0,0},{1,2},{2,1},{3,3},{4,4},{5,6},{6,5},{7,7},{8,8},{9,10},{10,9... | collective-permute-start | bytes 589832 | tf_op jit(solution)/shard_map/halo/ppermute | solution.py:389
  12.2 4.7 %collective-permute-start.2 = (bf16[2,192,256]{2,1,0:T(8,128)(2,1)S(1)}, bf16[2,192,256]{2,1,0:T(8,128)(2,1)S(1)}, u32[]{:S(2)}, u32[]{:S(2)}) collective-permute-start(bf16[2,192,256]{2,1,0:T(8,128)(2,1)S(1)} %get-tuple-element.38.refs_3_.refs_1_.refs_4_), channel_id=1, source_target_pairs={{0,1},{1,0},{2,3},{3,2},{4,5},{5,4},{6,7},{7,6},{8,9},{9,8},{10,11... | collective-permute-start | bytes 589832 | tf_op jit(solution)/shard_map/halo/ppermute | solution.py:389
  12.2 7.0 %collective-permute-start.6 = (bf16[2,192,256]{2,1,0:T(8,128)(2,1)S(1)}, bf16[2,192,256]{2,1,0:T(8,128)(2,1)S(1)}, u32[]{:S(2)}, u32[]{:S(2)}) collective-permute-start(bf16[2,192,256]{2,1,0:T(8,128)(2,1)S(1)} %collective-permute-done.4.refs_6_.refs_4_.refs_5_), channel_id=1, source_target_pairs={{0,0},{1,2},{2,1},{3,3},{4,4},{5,6},{6,5},{7,7},{8,8},{9,10},{10,9... | collective-permute-start | bytes 589832 | tf_op jit(solution)/shard_map/halo/ppermute | solution.py:389
  14.9 4.4 %collective-permute-start.5 = (bf16[2,192,256]{2,1,0:T(8,128)(2,1)S(1)}, bf16[2,192,256]{2,1,0:T(8,128)(2,1)S(1)}, u32[]{:S(2)}, u32[]{:S(2)}) collective-permute-start(bf16[2,192,256]{2,1,0:T(8,128)(2,1)S(1)} %collective-permute-done.4.refs_6_.refs_4_.refs_5_), channel_id=1, source_target_pairs={{0,1},{1,0},{2,3},{3,2},{4,5},{5,4},{6,7},{7,6},{8,9},{9,8},{10,11... | collective-permute-start | bytes 589832 | tf_op jit(solution)/shard_map/halo/ppermute | solution.py:389
  16.5 7.0 %collective-permute-start.7 = (bf16[2,192,256]{2,1,0:T(8,128)(2,1)S(1)}, bf16[2,192,256]{2,1,0:T(8,128)(2,1)S(1)}, u32[]{:S(2)}, u32[]{:S(2)}) collective-permute-start(bf16[2,192,256]{2,1,0:T(8,128)(2,1)S(1)} %collective-permute-done.1.refs_2_), channel_id=1, source_target_pairs={{0,8},{8,0},{16,24},{24,16},{1,9},{9,1},{17,25},{25,17},{2,10},{10... | collective-permute-start | bytes 589832 | tf_op jit(solution)/shard_map/halo/ppermute | solution.py:379
  21.7 7.2 %collective-permute-start.8 = (bf16[192,256]{1,0:T(8,128)(2,1)S(1)}, bf16[192,256]{1,0:T(8,128)(2,1)S(1)}, u32[]{:S(2)}, u32[]{:S(2)}) collective-permute-start(bf16[192,256]{1,0:T(8,128)(2,1)S(1)} %get-tuple-element.42), channel_id=1, source_target_pairs={{0,16},{8,24},{16,0},{24,8},{1,17},{9,25},{17,1},{25,9},{2,18},{10... | collective-permute-start | bytes 294920 | tf_op jit(solution)/shard_map/merge/ppermute | solution.py:379
  22.4 6.4 %collective-permute-start.9 = (bf16[192,256]{1,0:T(8,128)(2,1)S(1)}, bf16[192,256]{1,0:T(8,128)(2,1)S(1)}, u32[]{:S(2)}, u32[]{:S(2)}) collective-permute-start(bf16[192,256]{1,0:T(8,128)(2,1)S(1)} %get-tuple-element.43), channel_id=1, source_target_pairs={{0,8},{8,0},{16,24},{24,16},{1,9},{9,1},{17,25},{25,17},{2,10},{10... | collective-permute-start | bytes 294920 | tf_op jit(solution)/shard_map/merge/ppermute | solution.py:379
  24.5 6.3 %collective-permute-start.12 = (f32[8,768]{1,0:T(8,128)S(1)}, f32[8,768]{1,0:T(8,128)S(1)}, u32[]{:S(2)}, u32[]{:S(2)}) collective-permute-start(f32[8,768]{1,0:T(8,128)S(1)} %get-tuple-element.44.refs_8_), channel_id=1, source_target_pairs={{0,24},{8,16},{16,8},{24,0},{1,25},{9,17},{17,9},{25,1},{2,26},{10... | collective-permute-start | bytes 73736 | tf_op jit(solution)/shard_map/merge/ppermute | solution.py:379
  27.2 3.6 %collective-permute-start.11 = (f32[8,768]{1,0:T(8,128)S(1)}, f32[8,768]{1,0:T(8,128)S(1)}, u32[]{:S(2)}, u32[]{:S(2)}) collective-permute-start(f32[8,768]{1,0:T(8,128)S(1)} %get-tuple-element.44.refs_8_), channel_id=1, source_target_pairs={{0,16},{8,24},{16,0},{24,8},{1,17},{9,25},{17,1},{25,9},{2,18},{10... | collective-permute-start | bytes 73736 | tf_op jit(solution)/shard_map/merge/ppermute | solution.py:379
  28.8 2.7 %collective-permute-start.10 = (f32[8,768]{1,0:T(8,128)S(1)}, f32[8,768]{1,0:T(8,128)S(1)}, u32[]{:S(2)}, u32[]{:S(2)}) collective-permute-start(f32[8,768]{1,0:T(8,128)S(1)} %get-tuple-element.44.refs_8_), channel_id=1, source_target_pairs={{0,8},{8,0},{16,24},{24,16},{1,9},{9,1},{17,25},{25,17},{2,10},{10... | collective-permute-start | bytes 73736 | tf_op jit(solution)/shard_map/merge/ppermute | solution.py:379
  28.8 14.0 %collective-permute-start.13 = (bf16[192,256]{1,0:T(8,128)(2,1)S(1)}, bf16[192,256]{1,0:T(8,128)(2,1)S(1)}, u32[]{:S(2)}, u32[]{:S(2)}) collective-permute-start(bf16[192,256]{1,0:T(8,128)(2,1)S(1)} %get-tuple-element.51), channel_id=1, source_target_pairs={{0,24},{8,16},{16,8},{24,0},{1,25},{9,17},{17,9},{25,1},{2,26},{10... | collective-permute-start | bytes 294920 | tf_op jit(solution)/shard_map/merge/ppermute | solution.py:379
  34.6 11.9 %collective-permute-start.17 = (bf16[2,2,192,256]{3,2,1,0:T(8,128)(2,1)S(1)}, bf16[2,2,192,256]{3,2,1,0:T(8,128)(2,1)S(1)}, u32[]{:S(2)}, u32[]{:S(2)}) collective-permute-start(bf16[2,2,192,256]{3,2,1,0:T(8,128)(2,1)S(1)} %get-tuple-element.66), channel_id=1, source_target_pairs={{0,1},{1,0},{2,3},{3,2},{4,5},{5,4},{6,7},{7,6},{8,9},{9,8},{10,11... | collective-permute-start | bytes 1179656 | tf_op jit(solution)/shard_map/gradients/ppermute | solution.py:444
  36.3 10.6 %collective-permute-start.18 = (bf16[2,2,192,256]{3,2,1,0:T(8,128)(2,1)S(1)}, bf16[2,2,192,256]{3,2,1,0:T(8,128)(2,1)S(1)}, u32[]{:S(2)}, u32[]{:S(2)}) collective-permute-start(bf16[2,2,192,256]{3,2,1,0:T(8,128)(2,1)S(1)} %get-tuple-element.67), channel_id=1, source_target_pairs={{0,0},{1,2},{2,1},{3,3},{4,4},{5,6},{6,5},{7,7},{8,8},{9,10},{10,9... | collective-permute-start | bytes 1179656 | tf_op jit(solution)/shard_map/gradients/ppermute | solution.py:444
  42.9 5.9 %collective-permute-start.14 = (bf16[192,256]{1,0:T(8,128)(2,1)S(1)}, bf16[192,256]{1,0:T(8,128)(2,1)S(1)}, u32[]{:S(2)}, u32[]{:S(2)}) collective-permute-start(bf16[192,256]{1,0:T(8,128)(2,1)S(1)} %get-tuple-element.58), channel_id=1, source_target_pairs={{0,24},{8,16},{16,8},{24,0},{1,25},{9,17},{17,9},{25,1},{2,26},{10... | collective-permute-start | bytes 294920 | tf_op jit(solution)/shard_map/return/ppermute | solution.py:379
  43.5 7.3 %collective-permute-start.15 = (bf16[192,256]{1,0:T(8,128)(2,1)S(1)}, bf16[192,256]{1,0:T(8,128)(2,1)S(1)}, u32[]{:S(2)}, u32[]{:S(2)}) collective-permute-start(bf16[192,256]{1,0:T(8,128)(2,1)S(1)} %get-tuple-element.59), channel_id=1, source_target_pairs={{0,16},{8,24},{16,0},{24,8},{1,17},{9,25},{17,1},{25,9},{2,18},{10... | collective-permute-start | bytes 294920 | tf_op jit(solution)/shard_map/return/ppermute | solution.py:379
  43.5 7.3 %collective-permute-start.16 = (bf16[192,256]{1,0:T(8,128)(2,1)S(1)}, bf16[192,256]{1,0:T(8,128)(2,1)S(1)}, u32[]{:S(2)}, u32[]{:S(2)}) collective-permute-start(bf16[192,256]{1,0:T(8,128)(2,1)S(1)} %get-tuple-element.60), channel_id=1, source_target_pairs={{0,8},{8,0},{16,24},{24,16},{1,9},{9,1},{17,25},{25,17},{2,10},{10... | collective-permute-start | bytes 294920 | tf_op jit(solution)/shard_map/return/ppermute | solution.py:379
  47.0 4.8 %collective-permute-start.19 = (bf16[2,192,256]{2,1,0:T(8,128)(2,1)S(1)}, bf16[2,192,256]{2,1,0:T(8,128)(2,1)S(1)}, u32[]{:S(2)}, u32[]{:S(2)}) collective-permute-start(bf16[2,192,256]{2,1,0:T(8,128)(2,1)S(1)} %fusion), channel_id=1, source_target_pairs={{0,4},{4,0},{1,5},{5,1},{2,6},{6,2},{3,7},{7,3},{8,12},{12,8},{9,1... | collective-permute-start | bytes 589832 | tf_op jit(solution)/shard_map/return/ppermute | solution.py:453

commit v14 on v13

--- a/solution.py
+++ b/solution.py
@@ -20,6 +20,7 @@
 SCALE_LOG2 = SCALE * math.log2(math.e)
 F32 = jnp.float32
 BF16 = jnp.bfloat16
+STAT_ORDER = (0, 1, 3, 2)
 VMEM_LIMIT = 48 * 1024 * 1024
 
 
@@ -218,7 +219,8 @@
 
 
 def merged_stats(stat_refs, cells):
-    parts = [seen_from(ref[...], distance, cells) for distance, ref in enumerate(stat_refs)]
+    refs = dict(zip(STAT_ORDER, stat_refs))
+    parts = [seen_from(refs[distance][...], distance, cells) for distance in range(4)]
     top = functools.reduce(jnp.maximum, parts)
     shares = [jnp.exp2(part - top) for part in parts]
     total = functools.reduce(jnp.add, shares)
@@ -417,7 +419,7 @@
     with jax.named_scope("merge"):
         outs = [other_frames(o, d) for d, o in ((3, o3), (2, o2), (1, o1))]
         stat_near, outs[1:] = lax.optimization_barrier((stat, outs[1:]))
-        stats = [stat, other_frames(stat_near, 1), other_frames(stat, 2), other_frames(stat, 3)]
+        stats = [stat, other_frames(stat_near, 1), other_frames(stat, 3), other_frames(stat, 2)]
 
     queries = (qg, qg1, qg2, qg3)
     col_shape = jax.ShapeDtypeStruct((grid_rows, 2, cells, chan), BF16)

time: 52.9 us -> 52.8 us (level)
  waiting for transfers between devices: 9.36 us -> 10.8 us
  starting transfers between devices: 31.1 us -> 29.7 us
    ppermute x2, starting transfers between devices: 6.54 us -> 4.87 us  [shards(): sides = [lax.ppermute(x, 'wa', pairs) for x, pairs in zip(sides, col_sides)]]
    ppermute x12, waiting for transfers between devices: 6.52 us -> 7.42 us  [other_frames(): lax.ppermute(x, 'ta', [(i, i ^ distance) for i in range(sizes['ta'])])]
where the time goes in v14:
time: 52.8 us; the launch traced here: 52.6 us
  starting transfers between devices  29.7 us (56%)
  Pallas kernels  11.4 us (22%)
  waiting for transfers between devices  10.8 us (20%)
  between operations  0.72 us (1%)
    ppermute x12, starting transfers between devices, other_frames(): lax.ppermute(x, 'ta', [(i, i ^ distance) for i in range(sizes['ta'])])  14.2 us
    pallas_call x7, Pallas kernels, call(): pl.pallas_call(kernel, out_shape=out_shape, in_specs=[pl.BlockSpec(memory...  11.4 us
    ppermute x4, starting transfers between devices, shards(): lax.ppermute(block, 'wa', pairs)  8.2 us
    ppermute x12, waiting for transfers between devices, other_frames(): lax.ppermute(x, 'ta', [(i, i ^ distance) for i in range(sizes['ta'])])  7.42 us
    ppermute x2, starting transfers between devices, shards(): sides = [lax.ppermute(x, 'wa', pairs) for x, pairs in zip(sides, col_sides)]  4.87 us
    ppermute x4, waiting for transfers between devices, shards(): lax.ppermute(block, 'wa', pairs)  2.4 us
    ppermute x1, starting transfers between devices, shards(): kv_rows = [kv] + [lax.ppermute(kv, 'ha', pairs) for pairs in row_sides]  2.11 us
  transfers between devices with their start and end apart: 20, of which 7 were waited for; matrix products, arithmetic and copies ran while one was open for 0% of the time, Pallas kernels for 18%

profile of v14, /device:TPU:1, one launch (start us, length us, event | category | flops | bytes accessed | tf_op | source)
XLA Modules:
  0.0 52.6 jit_solution(13088924873909118265)
XLA Ops:
  0.6 1.3 %rotate.1 = (bf16[2,192,256]{2,1,0:T(8,128)(2,1)S(1)}, bf16[2,192,256]{2,1,0:T(8,128)(2,1)S(1)}, f32[3,192,128]{2,1,0:T(8,128)S(1)}) custom-call(bf16[192,256]{1,0:T(8,128)(2,1)} %bitcast.10, bf16[192,256]{1,0:T(8,128)(2,1)} %bitcast.11, bf16[192,256]{1,0:T(8,128)(2,1)} %bitcast.12, bf16[192,256]{1,0:T(8,128)(2,1)} %bitcast.13, ...), custom_call_target="tpu_custom_call" | custom-call | bytes 1179648 | tf_op jit(solution)/shard_map/rotate/pallas_call | solution.py:344
  1.9 2.1 %collective-permute-start.4 = (bf16[2,192,256]{2,1,0:T(8,128)(2,1)S(1)}, bf16[2,192,256]{2,1,0:T(8,128)(2,1)S(1)}, u32[]{:S(2)}, u32[]{:S(2)}) collective-permute-start(bf16[2,192,256]{2,1,0:T(8,128)(2,1)S(1)} %get-tuple-element.38.refs_3_.refs_1_.refs_4_), channel_id=1, source_target_pairs={{0,4},{4,0},{1,5},{5,1},{2,6},{6,2},{3,7},{7,3},{8,12},{12,8},{9,1... | collective-permute-start | bytes 589832 | tf_op jit(solution)/shard_map/halo/ppermute | solution.py:386
  4.0 2.3 %collective-permute-start.1 = (bf16[2,192,256]{2,1,0:T(8,128)(2,1)S(1)}, bf16[2,192,256]{2,1,0:T(8,128)(2,1)S(1)}, u32[]{:S(2)}, u32[]{:S(2)}) collective-permute-start(bf16[2,192,256]{2,1,0:T(8,128)(2,1)S(1)} %get-tuple-element.37.refs_0_), channel_id=1, source_target_pairs={{0,16},{8,24},{16,0},{24,8},{1,17},{9,25},{17,1},{25,9},{2,18},{10... | collective-permute-start | bytes 589832 | tf_op jit(solution)/shard_map/halo/ppermute | solution.py:381
  6.3 1.3 %collective-permute-start = (bf16[2,192,256]{2,1,0:T(8,128)(2,1)S(1)}, bf16[2,192,256]{2,1,0:T(8,128)(2,1)S(1)}, u32[]{:S(2)}, u32[]{:S(2)}) collective-permute-start(bf16[2,192,256]{2,1,0:T(8,128)(2,1)S(1)} %get-tuple-element.37.refs_0_), channel_id=1, source_target_pairs={{0,8},{8,0},{16,24},{24,16},{1,9},{9,1},{17,25},{25,17},{2,10},{10... | collective-permute-start | bytes 589832 | tf_op jit(solution)/shard_map/halo/ppermute | solution.py:381
  7.6 4.5 %collective-permute-start.3 = (bf16[2,192,256]{2,1,0:T(8,128)(2,1)S(1)}, bf16[2,192,256]{2,1,0:T(8,128)(2,1)S(1)}, u32[]{:S(2)}, u32[]{:S(2)}) collective-permute-start(bf16[2,192,256]{2,1,0:T(8,128)(2,1)S(1)} %get-tuple-element.38.refs_3_.refs_1_.refs_4_), channel_id=1, source_target_pairs={{0,0},{1,2},{2,1},{3,3},{4,4},{5,6},{6,5},{7,7},{8,8},{9,10},{10,9... | collective-permute-start | bytes 589832 | tf_op jit(solution)/shard_map/halo/ppermute | solution.py:391
  12.2 0.1 collective-permute-start.2
  12.2 0.0 collective-permute-done.4.refs_6_.refs_4_.refs_5_
  12.2 1.9 %collective-permute-start.6 = (bf16[2,192,256]{2,1,0:T(8,128)(2,1)S(1)}, bf16[2,192,256]{2,1,0:T(8,128)(2,1)S(1)}, u32[]{:S(2)}, u32[]{:S(2)}) collective-permute-start(bf16[2,192,256]{2,1,0:T(8,128)(2,1)S(1)} %collective-permute-done.4.refs_6_.refs_4_.refs_5_), channel_id=1, source_target_pairs={{0,0},{1,2},{2,1},{3,3},{4,4},{5,6},{6,5},{7,7},{8,8},{9,10},{10,9... | collective-permute-start | bytes 589832 | tf_op jit(solution)/shard_map/halo/ppermute | solution.py:391
  14.2 0.7 %collective-permute-done.1.refs_2_ = bf16[2,192,256]{2,1,0:T(8,128)(2,1)S(1)} collective-permute-done((bf16[2,192,256]{2,1,0:T(8,128)(2,1)S(1)}, bf16[2,192,256]{2,1,0:T(8,128)(2,1)S(1)}, u32[]{:S(2)}, u32[]{:S(2)}) %collective-permute-start.1) | collective-permute-done | bytes 196640 | tf_op jit(solution)/shard_map/halo/ppermute | solution.py:381
  14.9 1.7 %collective-permute-start.5 = (bf16[2,192,256]{2,1,0:T(8,128)(2,1)S(1)}, bf16[2,192,256]{2,1,0:T(8,128)(2,1)S(1)}, u32[]{:S(2)}, u32[]{:S(2)}) collective-permute-start(bf16[2,192,256]{2,1,0:T(8,128)(2,1)S(1)} %collective-permute-done.4.refs_6_.refs_4_.refs_5_), channel_id=1, source_target_pairs={{0,1},{1,0},{2,3},{3,2},{4,5},{5,4},{6,7},{7,6},{8,9},{9,8},{10,11... | collective-permute-start | bytes 589832 | tf_op jit(solution)/shard_map/halo/ppermute | solution.py:391
  16.5 0.0 collective-permute-done.refs_1_
  16.5 0.3 collective-permute-start.7
  16.8 0.0 collective-permute-done.3.refs_5_.refs_3_.refs_6_
  16.8 0.0 collective-permute-done.2.refs_4_.refs_2_
  16.8 2.4 %collective-permute-done.6.refs_8_.refs_6_.refs_7_ = bf16[2,192,256]{2,1,0:T(8,128)(2,1)S(1)} collective-permute-done((bf16[2,192,256]{2,1,0:T(8,128)(2,1)S(1)}, bf16[2,192,256]{2,1,0:T(8,128)(2,1)S(1)}, u32[]{:S(2)}, u32[]{:S(2)}) %collective-permute-start.6) | collective-permute-done | bytes 196640 | tf_op jit(solution)/shard_map/halo/ppermute | solution.py:391
  19.2 0.0 collective-permute-done.5.refs_7_.refs_5_
  19.2 2.4 %attend.2 = (bf16[192,256]{1,0:T(8,128)(2,1)S(1)}, bf16[192,256]{1,0:T(8,128)(2,1)S(1)}, bf16[192,256]{1,0:T(8,128)(2,1)S(1)}, f32[576,128]{1,0:T(8,128)S(1)}) custom-call(bf16[2,192,256]{2,1,0:T(8,128)(2,1)S(1)} %get-tuple-element.37.refs_0_, bf16[2,192,256]{2,1,0:T(8,128)(2,1)S(1)} %collective-permute-done.refs_1_, ...), custom_call_target="tpu_custom_call" | custom-call | flops 5435817984 | bytes 2359296 | tf_op jit(solution)/shard_map/attend/pallas_call | solution.py:344
  21.7 0.8 %collective-permute-start.8 = (bf16[192,256]{1,0:T(8,128)(2,1)S(1)}, bf16[192,256]{1,0:T(8,128)(2,1)S(1)}, u32[]{:S(2)}, u32[]{:S(2)}) collective-permute-start(bf16[192,256]{1,0:T(8,128)(2,1)S(1)} %get-tuple-element.42), channel_id=1, source_target_pairs={{0,16},{8,24},{16,0},{24,8},{1,17},{9,25},{17,1},{25,9},{2,18},{10... | collective-permute-start | bytes 294920 | tf_op jit(solution)/shard_map/merge/ppermute | solution.py:381
  22.4 1.0 %collective-permute-start.9 = (bf16[192,256]{1,0:T(8,128)(2,1)S(1)}, bf16[192,256]{1,0:T(8,128)(2,1)S(1)}, u32[]{:S(2)}, u32[]{:S(2)}) collective-permute-start(bf16[192,256]{1,0:T(8,128)(2,1)S(1)} %get-tuple-element.43), channel_id=1, source_target_pairs={{0,8},{8,0},{16,24},{24,16},{1,9},{9,1},{17,25},{25,17},{2,10},{10... | collective-permute-start | bytes 294920 | tf_op jit(solution)/shard_map/merge/ppermute | solution.py:381
  23.5 0.0 collective-permute-done.7.refs_0_.refs_3_
  23.5 1.0 %attend.3 = (bf16[192,256]{1,0:T(8,128)(2,1)S(1)}, f32[8,768]{1,0:T(8,128)S(1)}) custom-call(bf16[2,192,256]{2,1,0:T(8,128)(2,1)S(1)} %collective-permute-done.7.refs_0_.refs_3_, bf16[2,192,256]{2,1,0:T(8,128)(2,1)S(1)} %get-tuple-element.38.refs_3_.refs_1_.refs_4_, bf16[2,192,256]{2,1,0:T(8,128)(2,1)S(1)} %collective-permute-done.2.refs_4_.refs_2_, ...), custom_call_target="tpu_custom_call" | custom-call | flops 1811939328 | bytes 1794048 | tf_op jit(solution)/shard_map/attend/pallas_call | solution.py:344
  24.5 1.7 %collective-permute-start.12 = (f32[8,768]{1,0:T(8,128)S(1)}, f32[8,768]{1,0:T(8,128)S(1)}, u32[]{:S(2)}, u32[]{:S(2)}) collective-permute-start(f32[8,768]{1,0:T(8,128)S(1)} %get-tuple-element.44.refs_8_), channel_id=1, source_target_pairs={{0,16},{8,24},{16,0},{24,8},{1,17},{9,25},{17,1},{25,9},{2,18},{10... | collective-permute-start | bytes 73736 | tf_op jit(solution)/shard_map/merge/ppermute | solution.py:381
  26.3 1.1 %collective-permute-start.11 = (f32[8,768]{1,0:T(8,128)S(1)}, f32[8,768]{1,0:T(8,128)S(1)}, u32[]{:S(2)}, u32[]{:S(2)}) collective-permute-start(f32[8,768]{1,0:T(8,128)S(1)} %get-tuple-element.44.refs_8_), channel_id=1, source_target_pairs={{0,24},{8,16},{16,8},{24,0},{1,25},{9,17},{17,9},{25,1},{2,26},{10... | collective-permute-start | bytes 73736 | tf_op jit(solution)/shard_map/merge/ppermute | solution.py:381
  27.3 1.4 %collective-permute-done.8.refs_2_ = bf16[192,256]{1,0:T(8,128)(2,1)S(1)} collective-permute-done((bf16[192,256]{1,0:T(8,128)(2,1)S(1)}, bf16[192,256]{1,0:T(8,128)(2,1)S(1)}, u32[]{:S(2)}, u32[]{:S(2)}) %collective-permute-start.8) | collective-permute-done | bytes 98336 | tf_op jit(solution)/shard_map/merge/ppermute | solution.py:381
  28.7 0.0 collective-permute-done.9.refs_3_
  28.7 0.0 collective-permute-start.10
  28.7 2.1 %collective-permute-start.13 = (bf16[192,256]{1,0:T(8,128)(2,1)S(1)}, bf16[192,256]{1,0:T(8,128)(2,1)S(1)}, u32[]{:S(2)}, u32[]{:S(2)}) collective-permute-start(bf16[192,256]{1,0:T(8,128)(2,1)S(1)} %get-tuple-element.51), channel_id=1, source_target_pairs={{0,24},{8,16},{16,8},{24,0},{1,25},{9,17},{17,9},{25,1},{2,26},{10... | collective-permute-start | bytes 294920 | tf_op jit(solution)/shard_map/merge/ppermute | solution.py:381
  30.8 0.0 collective-permute-done.12.refs_11_
  30.8 0.0 collective-permute-done.11.refs_10_
  30.8 0.6 %collective-permute-done.10.refs_9_ = f32[8,768]{1,0:T(8,128)S(1)} collective-permute-done((f32[8,768]{1,0:T(8,128)S(1)}, f32[8,768]{1,0:T(8,128)S(1)}, u32[]{:S(2)}, u32[]{:S(2)}) %collective-permute-start.10) | collective-permute-done | bytes 24608 | tf_op jit(solution)/shard_map/merge/ppermute | solution.py:381
  31.4 3.1 %gradients.2 = (f32[2,128,768]{2,1,0:T(8,128)S(1)}, f32[2,768]{1,0:T(2,128)S(1)}, f32[2,768]{1,0:T(2,128)S(1)}, f32[192,128]{1,0:T(8,128)S(1)}, bf16[2,2,192,256...) custom-call(bf16[2,192,256]{2,1,0:T(8,128)(2,1)S(1)} %get-tuple-element.37.refs_0_, ...), custom_call_target="tpu_custom_call" | custom-call | flops 12079595520 | bytes 3354624 | tf_op jit(solution)/shard_map/gradients/pallas_call | solution.py:344
  34.5 1.8 %collective-permute-start.17 = (bf16[2,2,192,256]{3,2,1,0:T(8,128)(2,1)S(1)}, bf16[2,2,192,256]{3,2,1,0:T(8,128)(2,1)S(1)}, u32[]{:S(2)}, u32[]{:S(2)}) collective-permute-start(bf16[2,2,192,256]{3,2,1,0:T(8,128)(2,1)S(1)} %get-tuple-element.66), channel_id=1, source_target_pairs={{0,1},{1,0},{2,3},{3,2},{4,5},{5,4},{6,7},{7,6},{8,9},{9,8},{10,11... | collective-permute-start | bytes 1179656 | tf_op jit(solution)/shard_map/gradients/ppermute | solution.py:446
  36.2 3.1 %collective-permute-start.18 = (bf16[2,2,192,256]{3,2,1,0:T(8,128)(2,1)S(1)}, bf16[2,2,192,256]{3,2,1,0:T(8,128)(2,1)S(1)}, u32[]{:S(2)}, u32[]{:S(2)}) collective-permute-start(bf16[2,2,192,256]{3,2,1,0:T(8,128)(2,1)S(1)} %get-tuple-element.67), channel_id=1, source_target_pairs={{0,0},{1,2},{2,1},{3,3},{4,4},{5,6},{6,5},{7,7},{8,8},{9,10},{10,9... | collective-permute-start | bytes 1179656 | tf_op jit(solution)/shard_map/gradients/ppermute | solution.py:446
  39.4 1.7 %gradients.3 = (bf16[192,256]{1,0:T(8,128)(2,1)S(1)}, bf16[192,256]{1,0:T(8,128)(2,1)S(1)}, bf16[192,256]{1,0:T(8,128)(2,1)S(1)}, bf16[192,256]{1,0:T(8,128)(2,1)S(1)}, bf16[2,2,192,256]{3,2,1,0:T(8,128)(2,1)S(1)}) custom-call(bf16[2,192,256]{2,1,0:T(8,128)(2,1)S(1)} %get-tuple-element.37.refs_0_, bf16[2,192,256]{2,1,0:T(8,128)(2,1)S(1)} %collective-permute-done.refs_1_, ...), custom_call_target="tpu_custom_call" | custom-call | flops 6039797760 | bytes 2764800 | tf_op jit(solution)/shard_map/gradients/pallas_call | solution.py:344
  41.0 0.0 collective-permute-done.13.refs_1_
  41.0 2.6 %collective-permute-start.14 = (bf16[192,256]{1,0:T(8,128)(2,1)S(1)}, bf16[192,256]{1,0:T(8,128)(2,1)S(1)}, u32[]{:S(2)}, u32[]{:S(2)}) collective-permute-start(bf16[192,256]{1,0:T(8,128)(2,1)S(1)} %get-tuple-element.58), channel_id=1, source_target_pairs={{0,24},{8,16},{16,8},{24,0},{1,25},{9,17},{17,9},{25,1},{2,26},{10... | collective-permute-start | bytes 294920 | tf_op jit(solution)/shard_map/return/ppermute | solution.py:381
  43.6 0.0 collective-permute-start.15
  43.6 1.0 %collective-permute-start.16 = (bf16[192,256]{1,0:T(8,128)(2,1)S(1)}, bf16[192,256]{1,0:T(8,128)(2,1)S(1)}, u32[]{:S(2)}, u32[]{:S(2)}) collective-permute-start(bf16[192,256]{1,0:T(8,128)(2,1)S(1)} %get-tuple-element.60), channel_id=1, source_target_pairs={{0,8},{8,0},{16,24},{24,16},{1,9},{9,1},{17,25},{25,17},{2,10},{10... | collective-permute-start | bytes 294920 | tf_op jit(solution)/shard_map/return/ppermute | solution.py:381
  44.7 0.0 collective-permute-done.17.refs_1_
  44.7 0.9 %collective-permute-done.18.refs_2_ = bf16[2,2,192,256]{3,2,1,0:T(8,128)(2,1)S(1)} collective-permute-done((bf16[2,2,192,256]{3,2,1,0:T(8,128)(2,1)S(1)}, bf16[2,2,192,256]{3,2,1,0:T(8,128)(2,1)S(1)}, u32[]{:S(2)}, u32[]{:S(2)}) %collective-permute-start.18) | collective-permute-done | bytes 393248 | tf_op jit(solution)/shard_map/gradients/ppermute | solution.py:446
  45.6 0.1 fusion
  45.7 0.3 collective-permute-start.19
  46.0 0.7 %collective-permute-done.14.refs_5_ = bf16[192,256]{1,0:T(8,128)(2,1)S(1)} collective-permute-done((bf16[192,256]{1,0:T(8,128)(2,1)S(1)}, bf16[192,256]{1,0:T(8,128)(2,1)S(1)}, u32[]{:S(2)}, u32[]{:S(2)}) %collective-permute-start.14) | collective-permute-done | bytes 98336 | tf_op jit(solution)/shard_map/return/ppermute | solution.py:381
  46.7 4.1 %collective-permute-done.15.refs_6_ = bf16[192,256]{1,0:T(8,128)(2,1)S(1)} collective-permute-done((bf16[192,256]{1,0:T(8,128)(2,1)S(1)}, bf16[192,256]{1,0:T(8,128)(2,1)S(1)}, u32[]{:S(2)}, u32[]{:S(2)}) %collective-permute-start.15) | collective-permute-done | bytes 98336 | tf_op jit(solution)/shard_map/return/ppermute | solution.py:381
  50.7 0.0 collective-permute-done.16.refs_7_
  50.7 1.0 %finish.2 = (bf16[192,256]{1,0:T(8,128)(2,1)}, bf16[192,256]{1,0:T(8,128)(2,1)}) custom-call(bf16[192,256]{1,0:T(8,128)(2,1)S(1)} %get-tuple-element.39.refs_0_, bf16[192,256]{1,0:T(8,128)(2,1)S(1)} %collective-permute-done.13.refs_1_, bf16[192,256]{1,0:T(8,128)(2,1)S(1)} %collective-permute-done.8.refs_2_, ...), custom_call_target="tpu_custom_call" | custom-call | flops 9059696640 | bytes 1376256 | tf_op jit(solution)/shard_map/finish/pallas_call | solution.py:344
  51.8 0.0 collective-permute-done.19.refs_3_
  51.8 0.9 %finish.3 = (bf16[192,256]{1,0:T(8,128)(2,1)}, bf16[192,256]{1,0:T(8,128)(2,1)}) custom-call(bf16[2,2,192,256]{3,2,1,0:T(8,128)(2,1)S(1)} %get-tuple-element.65.refs_0_, bf16[2,2,192,256]{3,2,1,0:T(8,128)(2,1)S(1)} %collective-permute-done.17.refs_1_, bf16[2,2,192,256]{3,2,1,0:T(8,128)(2,1)S(1)} %collective-permute-done.18.refs_2_, ...), custom_call_target="tpu_custom_call" | custom-call | bytes 1867776 | tf_op jit(solution)/shard_map/finish/pallas_call | solution.py:344
Async XLA Ops:
  1.9 10.3 %collective-permute-start.4 = (bf16[2,192,256]{2,1,0:T(8,128)(2,1)S(1)}, bf16[2,192,256]{2,1,0:T(8,128)(2,1)S(1)}, u32[]{:S(2)}, u32[]{:S(2)}) collective-permute-start(bf16[2,192,256]{2,1,0:T(8,128)(2,1)S(1)} %get-tuple-element.38.refs_3_.refs_1_.refs_4_), channel_id=1, source_target_pairs={{0,4},{4,0},{1,5},{5,1},{2,6},{6,2},{3,7},{7,3},{8,12},{12,8},{9,1... | collective-permute-start | bytes 589832 | tf_op jit(solution)/shard_map/halo/ppermute | solution.py:386
  4.0 10.9 %collective-permute-start.1 = (bf16[2,192,256]{2,1,0:T(8,128)(2,1)S(1)}, bf16[2,192,256]{2,1,0:T(8,128)(2,1)S(1)}, u32[]{:S(2)}, u32[]{:S(2)}) collective-permute-start(bf16[2,192,256]{2,1,0:T(8,128)(2,1)S(1)} %get-tuple-element.37.refs_0_), channel_id=1, source_target_pairs={{0,16},{8,24},{16,0},{24,8},{1,17},{9,25},{17,1},{25,9},{2,18},{10... | collective-permute-start | bytes 589832 | tf_op jit(solution)/shard_map/halo/ppermute | solution.py:381
  6.3 10.2 %collective-permute-start = (bf16[2,192,256]{2,1,0:T(8,128)(2,1)S(1)}, bf16[2,192,256]{2,1,0:T(8,128)(2,1)S(1)}, u32[]{:S(2)}, u32[]{:S(2)}) collective-permute-start(bf16[2,192,256]{2,1,0:T(8,128)(2,1)S(1)} %get-tuple-element.37.refs_0_), channel_id=1, source_target_pairs={{0,8},{8,0},{16,24},{24,16},{1,9},{9,1},{17,25},{25,17},{2,10},{10... | collective-permute-start | bytes 589832 | tf_op jit(solution)/shard_map/halo/ppermute | solution.py:381
  7.6 9.2 %collective-permute-start.3 = (bf16[2,192,256]{2,1,0:T(8,128)(2,1)S(1)}, bf16[2,192,256]{2,1,0:T(8,128)(2,1)S(1)}, u32[]{:S(2)}, u32[]{:S(2)}) collective-permute-start(bf16[2,192,256]{2,1,0:T(8,128)(2,1)S(1)} %get-tuple-element.38.refs_3_.refs_1_.refs_4_), channel_id=1, source_target_pairs={{0,0},{1,2},{2,1},{3,3},{4,4},{5,6},{6,5},{7,7},{8,8},{9,10},{10,9... | collective-permute-start | bytes 589832 | tf_op jit(solution)/shard_map/halo/ppermute | solution.py:391
  12.2 4.7 %collective-permute-start.2 = (bf16[2,192,256]{2,1,0:T(8,128)(2,1)S(1)}, bf16[2,192,256]{2,1,0:T(8,128)(2,1)S(1)}, u32[]{:S(2)}, u32[]{:S(2)}) collective-permute-start(bf16[2,192,256]{2,1,0:T(8,128)(2,1)S(1)} %get-tuple-element.38.refs_3_.refs_1_.refs_4_), channel_id=1, source_target_pairs={{0,1},{1,0},{2,3},{3,2},{4,5},{5,4},{6,7},{7,6},{8,9},{9,8},{10,11... | collective-permute-start | bytes 589832 | tf_op jit(solution)/shard_map/halo/ppermute | solution.py:391
  12.2 7.0 %collective-permute-start.6 = (bf16[2,192,256]{2,1,0:T(8,128)(2,1)S(1)}, bf16[2,192,256]{2,1,0:T(8,128)(2,1)S(1)}, u32[]{:S(2)}, u32[]{:S(2)}) collective-permute-start(bf16[2,192,256]{2,1,0:T(8,128)(2,1)S(1)} %collective-permute-done.4.refs_6_.refs_4_.refs_5_), channel_id=1, source_target_pairs={{0,0},{1,2},{2,1},{3,3},{4,4},{5,6},{6,5},{7,7},{8,8},{9,10},{10,9... | collective-permute-start | bytes 589832 | tf_op jit(solution)/shard_map/halo/ppermute | solution.py:391
  14.9 4.4 %collective-permute-start.5 = (bf16[2,192,256]{2,1,0:T(8,128)(2,1)S(1)}, bf16[2,192,256]{2,1,0:T(8,128)(2,1)S(1)}, u32[]{:S(2)}, u32[]{:S(2)}) collective-permute-start(bf16[2,192,256]{2,1,0:T(8,128)(2,1)S(1)} %collective-permute-done.4.refs_6_.refs_4_.refs_5_), channel_id=1, source_target_pairs={{0,1},{1,0},{2,3},{3,2},{4,5},{5,4},{6,7},{7,6},{8,9},{9,8},{10,11... | collective-permute-start | bytes 589832 | tf_op jit(solution)/shard_map/halo/ppermute | solution.py:391
  16.5 7.0 %collective-permute-start.7 = (bf16[2,192,256]{2,1,0:T(8,128)(2,1)S(1)}, bf16[2,192,256]{2,1,0:T(8,128)(2,1)S(1)}, u32[]{:S(2)}, u32[]{:S(2)}) collective-permute-start(bf16[2,192,256]{2,1,0:T(8,128)(2,1)S(1)} %collective-permute-done.1.refs_2_), channel_id=1, source_target_pairs={{0,8},{8,0},{16,24},{24,16},{1,9},{9,1},{17,25},{25,17},{2,10},{10... | collective-permute-start | bytes 589832 | tf_op jit(solution)/shard_map/halo/ppermute | solution.py:381
  21.7 7.0 %collective-permute-start.8 = (bf16[192,256]{1,0:T(8,128)(2,1)S(1)}, bf16[192,256]{1,0:T(8,128)(2,1)S(1)}, u32[]{:S(2)}, u32[]{:S(2)}) collective-permute-start(bf16[192,256]{1,0:T(8,128)(2,1)S(1)} %get-tuple-element.42), channel_id=1, source_target_pairs={{0,16},{8,24},{16,0},{24,8},{1,17},{9,25},{17,1},{25,9},{2,18},{10... | collective-permute-start | bytes 294920 | tf_op jit(solution)/shard_map/merge/ppermute | solution.py:381
  22.4 6.2 %collective-permute-start.9 = (bf16[192,256]{1,0:T(8,128)(2,1)S(1)}, bf16[192,256]{1,0:T(8,128)(2,1)S(1)}, u32[]{:S(2)}, u32[]{:S(2)}) collective-permute-start(bf16[192,256]{1,0:T(8,128)(2,1)S(1)} %get-tuple-element.43), channel_id=1, source_target_pairs={{0,8},{8,0},{16,24},{24,16},{1,9},{9,1},{17,25},{25,17},{2,10},{10... | collective-permute-start | bytes 294920 | tf_op jit(solution)/shard_map/merge/ppermute | solution.py:381
  24.5 6.3 %collective-permute-start.12 = (f32[8,768]{1,0:T(8,128)S(1)}, f32[8,768]{1,0:T(8,128)S(1)}, u32[]{:S(2)}, u32[]{:S(2)}) collective-permute-start(f32[8,768]{1,0:T(8,128)S(1)} %get-tuple-element.44.refs_8_), channel_id=1, source_target_pairs={{0,16},{8,24},{16,0},{24,8},{1,17},{9,25},{17,1},{25,9},{2,18},{10... | collective-permute-start | bytes 73736 | tf_op jit(solution)/shard_map/merge/ppermute | solution.py:381
  26.3 4.5 %collective-permute-start.11 = (f32[8,768]{1,0:T(8,128)S(1)}, f32[8,768]{1,0:T(8,128)S(1)}, u32[]{:S(2)}, u32[]{:S(2)}) collective-permute-start(f32[8,768]{1,0:T(8,128)S(1)} %get-tuple-element.44.refs_8_), channel_id=1, source_target_pairs={{0,24},{8,16},{16,8},{24,0},{1,25},{9,17},{17,9},{25,1},{2,26},{10... | collective-permute-start | bytes 73736 | tf_op jit(solution)/shard_map/merge/ppermute | solution.py:381
  28.7 2.7 %collective-permute-start.10 = (f32[8,768]{1,0:T(8,128)S(1)}, f32[8,768]{1,0:T(8,128)S(1)}, u32[]{:S(2)}, u32[]{:S(2)}) collective-permute-start(f32[8,768]{1,0:T(8,128)S(1)} %get-tuple-element.44.refs_8_), channel_id=1, source_target_pairs={{0,8},{8,0},{16,24},{24,16},{1,9},{9,1},{17,25},{25,17},{2,10},{10... | collective-permute-start | bytes 73736 | tf_op jit(solution)/shard_map/merge/ppermute | solution.py:381
  28.7 12.3 %collective-permute-start.13 = (bf16[192,256]{1,0:T(8,128)(2,1)S(1)}, bf16[192,256]{1,0:T(8,128)(2,1)S(1)}, u32[]{:S(2)}, u32[]{:S(2)}) collective-permute-start(bf16[192,256]{1,0:T(8,128)(2,1)S(1)} %get-tuple-element.51), channel_id=1, source_target_pairs={{0,24},{8,16},{16,8},{24,0},{1,25},{9,17},{17,9},{25,1},{2,26},{10... | collective-permute-start | bytes 294920 | tf_op jit(solution)/shard_map/merge/ppermute | solution.py:381
  34.5 10.2 %collective-permute-start.17 = (bf16[2,2,192,256]{3,2,1,0:T(8,128)(2,1)S(1)}, bf16[2,2,192,256]{3,2,1,0:T(8,128)(2,1)S(1)}, u32[]{:S(2)}, u32[]{:S(2)}) collective-permute-start(bf16[2,2,192,256]{3,2,1,0:T(8,128)(2,1)S(1)} %get-tuple-element.66), channel_id=1, source_target_pairs={{0,1},{1,0},{2,3},{3,2},{4,5},{5,4},{6,7},{7,6},{8,9},{9,8},{10,11... | collective-permute-start | bytes 1179656 | tf_op jit(solution)/shard_map/gradients/ppermute | solution.py:446
  36.2 9.4 %collective-permute-start.18 = (bf16[2,2,192,256]{3,2,1,0:T(8,128)(2,1)S(1)}, bf16[2,2,192,256]{3,2,1,0:T(8,128)(2,1)S(1)}, u32[]{:S(2)}, u32[]{:S(2)}) collective-permute-start(bf16[2,2,192,256]{3,2,1,0:T(8,128)(2,1)S(1)} %get-tuple-element.67), channel_id=1, source_target_pairs={{0,0},{1,2},{2,1},{3,3},{4,4},{5,6},{6,5},{7,7},{8,8},{9,10},{10,9... | collective-permute-start | bytes 1179656 | tf_op jit(solution)/shard_map/gradients/ppermute | solution.py:446
  41.0 5.6 %collective-permute-start.14 = (bf16[192,256]{1,0:T(8,128)(2,1)S(1)}, bf16[192,256]{1,0:T(8,128)(2,1)S(1)}, u32[]{:S(2)}, u32[]{:S(2)}) collective-permute-start(bf16[192,256]{1,0:T(8,128)(2,1)S(1)} %get-tuple-element.58), channel_id=1, source_target_pairs={{0,24},{8,16},{16,8},{24,0},{1,25},{9,17},{17,9},{25,1},{2,26},{10... | collective-permute-start | bytes 294920 | tf_op jit(solution)/shard_map/return/ppermute | solution.py:381
  43.6 7.1 %collective-permute-start.15 = (bf16[192,256]{1,0:T(8,128)(2,1)S(1)}, bf16[192,256]{1,0:T(8,128)(2,1)S(1)}, u32[]{:S(2)}, u32[]{:S(2)}) collective-permute-start(bf16[192,256]{1,0:T(8,128)(2,1)S(1)} %get-tuple-element.59), channel_id=1, source_target_pairs={{0,16},{8,24},{16,0},{24,8},{1,17},{9,25},{17,1},{25,9},{2,18},{10... | collective-permute-start | bytes 294920 | tf_op jit(solution)/shard_map/return/ppermute | solution.py:381
  43.6 7.1 %collective-permute-start.16 = (bf16[192,256]{1,0:T(8,128)(2,1)S(1)}, bf16[192,256]{1,0:T(8,128)(2,1)S(1)}, u32[]{:S(2)}, u32[]{:S(2)}) collective-permute-start(bf16[192,256]{1,0:T(8,128)(2,1)S(1)} %get-tuple-element.60), channel_id=1, source_target_pairs={{0,8},{8,0},{16,24},{24,16},{1,9},{9,1},{17,25},{25,17},{2,10},{10... | collective-permute-start | bytes 294920 | tf_op jit(solution)/shard_map/return/ppermute | solution.py:381
  45.7 6.1 %collective-permute-start.19 = (bf16[2,192,256]{2,1,0:T(8,128)(2,1)S(1)}, bf16[2,192,256]{2,1,0:T(8,128)(2,1)S(1)}, u32[]{:S(2)}, u32[]{:S(2)}) collective-permute-start(bf16[2,192,256]{2,1,0:T(8,128)(2,1)S(1)} %fusion), channel_id=1, source_target_pairs={{0,4},{4,0},{1,5},{5,1},{2,6},{6,2},{3,7},{7,3},{8,12},{12,8},{9,1... | collective-permute-start | bytes 589832 | tf_op jit(solution)/shard_map/return/ppermute | solution.py:455

commit v15 on v14

--- a/solution.py
+++ b/solution.py
@@ -418,7 +418,7 @@
         o3, stat = forward((qg3,), first)
     with jax.named_scope("merge"):
         outs = [other_frames(o, d) for d, o in ((3, o3), (2, o2), (1, o1))]
-        stat_near, outs[1:] = lax.optimization_barrier((stat, outs[1:]))
+        stat_near, outs[1] = lax.optimization_barrier((stat, outs[1]))
         stats = [stat, other_frames(stat_near, 1), other_frames(stat, 3), other_frames(stat, 2)]
 
     queries = (qg, qg1, qg2, qg3)

time: 52.8 us -> 53.4 us (1.011)
  transfers between devices with their start and end apart: 20 -> 20, of which waited for: 7 -> 8; matrix products, arithmetic and copies ran while one was open for 0% -> 0% of each run, Pallas kernels for 18% -> 18%
where the time goes in v15:
time: 53.4 us; the launch traced here: 52.9 us
  starting transfers between devices  29.7 us (56%)
  Pallas kernels  11.4 us (21%)
  waiting for transfers between devices  11 us (21%)
  between operations  0.73 us (1%)
    ppermute x12, starting transfers between devices, other_frames(): lax.ppermute(x, 'ta', [(i, i ^ distance) for i in range(sizes['ta'])])  14.6 us
    pallas_call x7, Pallas kernels, call(): pl.pallas_call(kernel, out_shape=out_shape, in_specs=[pl.BlockSpec(memory...  11.4 us
    ppermute x4, starting transfers between devices, shards(): lax.ppermute(block, 'wa', pairs)  8.2 us
    ppermute x12, waiting for transfers between devices, other_frames(): lax.ppermute(x, 'ta', [(i, i ^ distance) for i in range(sizes['ta'])])  7.59 us
    ppermute x2, starting transfers between devices, shards(): sides = [lax.ppermute(x, 'wa', pairs) for x, pairs in zip(sides, col_sides)]  4.37 us
    ppermute x4, waiting for transfers between devices, shards(): lax.ppermute(block, 'wa', pairs)  2.4 us
    ppermute x1, starting transfers between devices, shards(): kv_rows = [kv] + [lax.ppermute(kv, 'ha', pairs) for pairs in row_sides]  2.11 us
  transfers between devices with their start and end apart: 20, of which 8 were waited for; matrix products, arithmetic and copies ran while one was open for 0% of the time, Pallas kernels for 18%

profile of v15, /device:TPU:1, one launch (start us, length us, event | category | flops | bytes accessed | tf_op | source)
XLA Modules:
  0.0 52.9 jit_solution(8757601954200165649)
XLA Ops:
  0.6 1.3 %rotate.1 = (bf16[2,192,256]{2,1,0:T(8,128)(2,1)S(1)}, bf16[2,192,256]{2,1,0:T(8,128)(2,1)S(1)}, f32[3,192,128]{2,1,0:T(8,128)S(1)}) custom-call(bf16[192,256]{1,0:T(8,128)(2,1)} %bitcast.10, bf16[192,256]{1,0:T(8,128)(2,1)} %bitcast.11, bf16[192,256]{1,0:T(8,128)(2,1)} %bitcast.12, bf16[192,256]{1,0:T(8,128)(2,1)} %bitcast.13, ...), custom_call_target="tpu_custom_call" | custom-call | bytes 1179648 | tf_op jit(solution)/shard_map/rotate/pallas_call | solution.py:344
  1.9 2.1 %collective-permute-start.4 = (bf16[2,192,256]{2,1,0:T(8,128)(2,1)S(1)}, bf16[2,192,256]{2,1,0:T(8,128)(2,1)S(1)}, u32[]{:S(2)}, u32[]{:S(2)}) collective-permute-start(bf16[2,192,256]{2,1,0:T(8,128)(2,1)S(1)} %get-tuple-element.37.refs_3_.refs_1_.refs_4_), channel_id=1, source_target_pairs={{0,4},{4,0},{1,5},{5,1},{2,6},{6,2},{3,7},{7,3},{8,12},{12,8},{9,1... | collective-permute-start | bytes 589832 | tf_op jit(solution)/shard_map/halo/ppermute | solution.py:386
  4.0 2.3 %collective-permute-start.1 = (bf16[2,192,256]{2,1,0:T(8,128)(2,1)S(1)}, bf16[2,192,256]{2,1,0:T(8,128)(2,1)S(1)}, u32[]{:S(2)}, u32[]{:S(2)}) collective-permute-start(bf16[2,192,256]{2,1,0:T(8,128)(2,1)S(1)} %get-tuple-element.36.refs_0_), channel_id=1, source_target_pairs={{0,16},{8,24},{16,0},{24,8},{1,17},{9,25},{17,1},{25,9},{2,18},{10... | collective-permute-start | bytes 589832 | tf_op jit(solution)/shard_map/halo/ppermute | solution.py:381
  6.3 1.3 %collective-permute-start = (bf16[2,192,256]{2,1,0:T(8,128)(2,1)S(1)}, bf16[2,192,256]{2,1,0:T(8,128)(2,1)S(1)}, u32[]{:S(2)}, u32[]{:S(2)}) collective-permute-start(bf16[2,192,256]{2,1,0:T(8,128)(2,1)S(1)} %get-tuple-element.36.refs_0_), channel_id=1, source_target_pairs={{0,8},{8,0},{16,24},{24,16},{1,9},{9,1},{17,25},{25,17},{2,10},{10... | collective-permute-start | bytes 589832 | tf_op jit(solution)/shard_map/halo/ppermute | solution.py:381
  7.6 4.5 %collective-permute-start.3 = (bf16[2,192,256]{2,1,0:T(8,128)(2,1)S(1)}, bf16[2,192,256]{2,1,0:T(8,128)(2,1)S(1)}, u32[]{:S(2)}, u32[]{:S(2)}) collective-permute-start(bf16[2,192,256]{2,1,0:T(8,128)(2,1)S(1)} %get-tuple-element.37.refs_3_.refs_1_.refs_4_), channel_id=1, source_target_pairs={{0,0},{1,2},{2,1},{3,3},{4,4},{5,6},{6,5},{7,7},{8,8},{9,10},{10,9... | collective-permute-start | bytes 589832 | tf_op jit(solution)/shard_map/halo/ppermute | solution.py:391
  12.2 0.1 collective-permute-start.2
  12.2 0.0 collective-permute-done.4.refs_6_.refs_4_.refs_5_
  12.2 1.9 %collective-permute-start.6 = (bf16[2,192,256]{2,1,0:T(8,128)(2,1)S(1)}, bf16[2,192,256]{2,1,0:T(8,128)(2,1)S(1)}, u32[]{:S(2)}, u32[]{:S(2)}) collective-permute-start(bf16[2,192,256]{2,1,0:T(8,128)(2,1)S(1)} %collective-permute-done.4.refs_6_.refs_4_.refs_5_), channel_id=1, source_target_pairs={{0,0},{1,2},{2,1},{3,3},{4,4},{5,6},{6,5},{7,7},{8,8},{9,10},{10,9... | collective-permute-start | bytes 589832 | tf_op jit(solution)/shard_map/halo/ppermute | solution.py:391
  14.2 0.7 %collective-permute-done.1.refs_2_ = bf16[2,192,256]{2,1,0:T(8,128)(2,1)S(1)} collective-permute-done((bf16[2,192,256]{2,1,0:T(8,128)(2,1)S(1)}, bf16[2,192,256]{2,1,0:T(8,128)(2,1)S(1)}, u32[]{:S(2)}, u32[]{:S(2)}) %collective-permute-start.1) | collective-permute-done | bytes 196640 | tf_op jit(solution)/shard_map/halo/ppermute | solution.py:381
  14.9 1.7 %collective-permute-start.5 = (bf16[2,192,256]{2,1,0:T(8,128)(2,1)S(1)}, bf16[2,192,256]{2,1,0:T(8,128)(2,1)S(1)}, u32[]{:S(2)}, u32[]{:S(2)}) collective-permute-start(bf16[2,192,256]{2,1,0:T(8,128)(2,1)S(1)} %collective-permute-done.4.refs_6_.refs_4_.refs_5_), channel_id=1, source_target_pairs={{0,1},{1,0},{2,3},{3,2},{4,5},{5,4},{6,7},{7,6},{8,9},{9,8},{10,11... | collective-permute-start | bytes 589832 | tf_op jit(solution)/shard_map/halo/ppermute | solution.py:391
  16.5 0.0 collective-permute-done.refs_1_
  16.5 0.3 collective-permute-start.7
  16.8 0.0 collective-permute-done.3.refs_5_.refs_3_.refs_6_
  16.8 0.0 collective-permute-done.2.refs_4_.refs_2_
  16.8 2.4 %collective-permute-done.6.refs_8_.refs_6_.refs_7_ = bf16[2,192,256]{2,1,0:T(8,128)(2,1)S(1)} collective-permute-done((bf16[2,192,256]{2,1,0:T(8,128)(2,1)S(1)}, bf16[2,192,256]{2,1,0:T(8,128)(2,1)S(1)}, u32[]{:S(2)}, u32[]{:S(2)}) %collective-permute-start.6) | collective-permute-done | bytes 196640 | tf_op jit(solution)/shard_map/halo/ppermute | solution.py:391
  19.2 0.0 collective-permute-done.5.refs_7_.refs_5_
  19.2 2.4 %attend.2 = (bf16[192,256]{1,0:T(8,128)(2,1)S(1)}, bf16[192,256]{1,0:T(8,128)(2,1)S(1)}, bf16[192,256]{1,0:T(8,128)(2,1)S(1)}, f32[576,128]{1,0:T(8,128)S(1)}) custom-call(bf16[2,192,256]{2,1,0:T(8,128)(2,1)S(1)} %get-tuple-element.36.refs_0_, bf16[2,192,256]{2,1,0:T(8,128)(2,1)S(1)} %collective-permute-done.refs_1_, ...), custom_call_target="tpu_custom_call" | custom-call | flops 5435817984 | bytes 2359296 | tf_op jit(solution)/shard_map/attend/pallas_call | solution.py:344
  21.7 0.8 %collective-permute-start.8 = (bf16[192,256]{1,0:T(8,128)(2,1)S(1)}, bf16[192,256]{1,0:T(8,128)(2,1)S(1)}, u32[]{:S(2)}, u32[]{:S(2)}) collective-permute-start(bf16[192,256]{1,0:T(8,128)(2,1)S(1)} %get-tuple-element.41), channel_id=1, source_target_pairs={{0,16},{8,24},{16,0},{24,8},{1,17},{9,25},{17,1},{25,9},{2,18},{10... | collective-permute-start | bytes 294920 | tf_op jit(solution)/shard_map/merge/ppermute | solution.py:381
  22.4 0.4 collective-permute-done.7.refs_0_.refs_3_
  22.9 1.0 %attend.3 = (bf16[192,256]{1,0:T(8,128)(2,1)S(1)}, f32[8,768]{1,0:T(8,128)S(1)}) custom-call(bf16[2,192,256]{2,1,0:T(8,128)(2,1)S(1)} %collective-permute-done.7.refs_0_.refs_3_, bf16[2,192,256]{2,1,0:T(8,128)(2,1)S(1)} %get-tuple-element.37.refs_3_.refs_1_.refs_4_, bf16[2,192,256]{2,1,0:T(8,128)(2,1)S(1)} %collective-permute-done.2.refs_4_.refs_2_, ...), custom_call_target="tpu_custom_call" | custom-call | flops 1811939328 | bytes 1794048 | tf_op jit(solution)/shard_map/attend/pallas_call | solution.py:344
  23.9 2.4 %collective-permute-start.11 = (f32[8,768]{1,0:T(8,128)S(1)}, f32[8,768]{1,0:T(8,128)S(1)}, u32[]{:S(2)}, u32[]{:S(2)}) collective-permute-start(f32[8,768]{1,0:T(8,128)S(1)} %get-tuple-element.42.refs_8_), channel_id=1, source_target_pairs={{0,16},{8,24},{16,0},{24,8},{1,17},{9,25},{17,1},{25,9},{2,18},{10... | collective-permute-start | bytes 73736 | tf_op jit(solution)/shard_map/merge/ppermute | solution.py:381
  26.3 1.1 %collective-permute-start.10 = (f32[8,768]{1,0:T(8,128)S(1)}, f32[8,768]{1,0:T(8,128)S(1)}, u32[]{:S(2)}, u32[]{:S(2)}) collective-permute-start(f32[8,768]{1,0:T(8,128)S(1)} %get-tuple-element.42.refs_8_), channel_id=1, source_target_pairs={{0,24},{8,16},{16,8},{24,0},{1,25},{9,17},{17,9},{25,1},{2,26},{10... | collective-permute-start | bytes 73736 | tf_op jit(solution)/shard_map/merge/ppermute | solution.py:381
  27.3 2.1 %collective-permute-done.8.refs_2_ = bf16[192,256]{1,0:T(8,128)(2,1)S(1)} collective-permute-done((bf16[192,256]{1,0:T(8,128)(2,1)S(1)}, bf16[192,256]{1,0:T(8,128)(2,1)S(1)}, u32[]{:S(2)}, u32[]{:S(2)}) %collective-permute-start.8) | collective-permute-done | bytes 98336 | tf_op jit(solution)/shard_map/merge/ppermute | solution.py:381
  29.4 0.0 collective-permute-start.9
  29.4 1.5 %collective-permute-start.13 = (bf16[192,256]{1,0:T(8,128)(2,1)S(1)}, bf16[192,256]{1,0:T(8,128)(2,1)S(1)}, u32[]{:S(2)}, u32[]{:S(2)}) collective-permute-start(bf16[192,256]{1,0:T(8,128)(2,1)S(1)} %get-tuple-element.51), channel_id=1, source_target_pairs={{0,8},{8,0},{16,24},{24,16},{1,9},{9,1},{17,25},{25,17},{2,10},{10... | collective-permute-start | bytes 294920 | tf_op jit(solution)/shard_map/merge/ppermute | solution.py:381
  30.9 1.4 %collective-permute-start.12 = (bf16[192,256]{1,0:T(8,128)(2,1)S(1)}, bf16[192,256]{1,0:T(8,128)(2,1)S(1)}, u32[]{:S(2)}, u32[]{:S(2)}) collective-permute-start(bf16[192,256]{1,0:T(8,128)(2,1)S(1)} %get-tuple-element.49), channel_id=1, source_target_pairs={{0,24},{8,16},{16,8},{24,0},{1,25},{9,17},{17,9},{25,1},{2,26},{10... | collective-permute-start | bytes 294920 | tf_op jit(solution)/shard_map/merge/ppermute | solution.py:381
  32.3 0.0 collective-permute-done.11.refs_11_
  32.3 0.0 collective-permute-done.10.refs_10_
  32.3 0.6 %collective-permute-done.9.refs_9_ = f32[8,768]{1,0:T(8,128)S(1)} collective-permute-done((f32[8,768]{1,0:T(8,128)S(1)}, f32[8,768]{1,0:T(8,128)S(1)}, u32[]{:S(2)}, u32[]{:S(2)}) %collective-permute-start.9) | collective-permute-done | bytes 24608 | tf_op jit(solution)/shard_map/merge/ppermute | solution.py:381
  32.9 3.1 %gradients.2 = (f32[2,128,768]{2,1,0:T(8,128)S(1)}, f32[2,768]{1,0:T(2,128)S(1)}, f32[2,768]{1,0:T(2,128)S(1)}, f32[192,128]{1,0:T(8,128)S(1)}, bf16[2,2,192,256...) custom-call(bf16[2,192,256]{2,1,0:T(8,128)(2,1)S(1)} %get-tuple-element.36.refs_0_, ...), custom_call_target="tpu_custom_call" | custom-call | flops 12079595520 | bytes 3354624 | tf_op jit(solution)/shard_map/gradients/pallas_call | solution.py:344
  36.0 1.3 %collective-permute-start.17 = (bf16[2,2,192,256]{3,2,1,0:T(8,128)(2,1)S(1)}, bf16[2,2,192,256]{3,2,1,0:T(8,128)(2,1)S(1)}, u32[]{:S(2)}, u32[]{:S(2)}) collective-permute-start(bf16[2,2,192,256]{3,2,1,0:T(8,128)(2,1)S(1)} %get-tuple-element.64), channel_id=1, source_target_pairs={{0,1},{1,0},{2,3},{3,2},{4,5},{5,4},{6,7},{7,6},{8,9},{9,8},{10,11... | collective-permute-start | bytes 1179656 | tf_op jit(solution)/shard_map/gradients/ppermute | solution.py:446
  37.3 3.0 %collective-permute-start.18 = (bf16[2,2,192,256]{3,2,1,0:T(8,128)(2,1)S(1)}, bf16[2,2,192,256]{3,2,1,0:T(8,128)(2,1)S(1)}, u32[]{:S(2)}, u32[]{:S(2)}) collective-permute-start(bf16[2,2,192,256]{3,2,1,0:T(8,128)(2,1)S(1)} %get-tuple-element.65), channel_id=1, source_target_pairs={{0,0},{1,2},{2,1},{3,3},{4,4},{5,6},{6,5},{7,7},{8,8},{9,10},{10,9... | collective-permute-start | bytes 1179656 | tf_op jit(solution)/shard_map/gradients/ppermute | solution.py:446
  40.4 1.7 %gradients.3 = (bf16[192,256]{1,0:T(8,128)(2,1)S(1)}, bf16[192,256]{1,0:T(8,128)(2,1)S(1)}, bf16[192,256]{1,0:T(8,128)(2,1)S(1)}, bf16[192,256]{1,0:T(8,128)(2,1)S(1)}, bf16[2,2,192,256]{3,2,1,0:T(8,128)(2,1)S(1)}) custom-call(bf16[2,192,256]{2,1,0:T(8,128)(2,1)S(1)} %get-tuple-element.36.refs_0_, bf16[2,192,256]{2,1,0:T(8,128)(2,1)S(1)} %collective-permute-done.refs_1_, ...), custom_call_target="tpu_custom_call" | custom-call | flops 6039797760 | bytes 2764800 | tf_op jit(solution)/shard_map/gradients/pallas_call | solution.py:344
  42.0 0.0 collective-permute-done.13.refs_3_
  42.1 0.0 collective-permute-done.12.refs_1_
  42.1 1.6 %collective-permute-start.14 = (bf16[192,256]{1,0:T(8,128)(2,1)S(1)}, bf16[192,256]{1,0:T(8,128)(2,1)S(1)}, u32[]{:S(2)}, u32[]{:S(2)}) collective-permute-start(bf16[192,256]{1,0:T(8,128)(2,1)S(1)} %get-tuple-element.56), channel_id=1, source_target_pairs={{0,24},{8,16},{16,8},{24,0},{1,25},{9,17},{17,9},{25,1},{2,26},{10... | collective-permute-start | bytes 294920 | tf_op jit(solution)/shard_map/return/ppermute | solution.py:381
  43.6 0.0 collective-permute-start.15
  43.6 2.0 %collective-permute-start.16 = (bf16[192,256]{1,0:T(8,128)(2,1)S(1)}, bf16[192,256]{1,0:T(8,128)(2,1)S(1)}, u32[]{:S(2)}, u32[]{:S(2)}) collective-permute-start(bf16[192,256]{1,0:T(8,128)(2,1)S(1)} %get-tuple-element.58), channel_id=1, source_target_pairs={{0,8},{8,0},{16,24},{24,16},{1,9},{9,1},{17,25},{25,17},{2,10},{10... | collective-permute-start | bytes 294920 | tf_op jit(solution)/shard_map/return/ppermute | solution.py:381
  45.7 0.0 collective-permute-done.17.refs_1_
  45.7 1.0 %collective-permute-done.18.refs_2_ = bf16[2,2,192,256]{3,2,1,0:T(8,128)(2,1)S(1)} collective-permute-done((bf16[2,2,192,256]{3,2,1,0:T(8,128)(2,1)S(1)}, bf16[2,2,192,256]{3,2,1,0:T(8,128)(2,1)S(1)}, u32[]{:S(2)}, u32[]{:S(2)}) %collective-permute-start.18) | collective-permute-done | bytes 393248 | tf_op jit(solution)/shard_map/gradients/ppermute | solution.py:446
  46.7 0.1 fusion
  46.8 0.4 collective-permute-start.19
  47.2 1.3 %collective-permute-done.14.refs_5_ = bf16[192,256]{1,0:T(8,128)(2,1)S(1)} collective-permute-done((bf16[192,256]{1,0:T(8,128)(2,1)S(1)}, bf16[192,256]{1,0:T(8,128)(2,1)S(1)}, u32[]{:S(2)}, u32[]{:S(2)}) %collective-permute-start.14) | collective-permute-done | bytes 98336 | tf_op jit(solution)/shard_map/return/ppermute | solution.py:381
  48.5 2.5 %collective-permute-done.15.refs_6_ = bf16[192,256]{1,0:T(8,128)(2,1)S(1)} collective-permute-done((bf16[192,256]{1,0:T(8,128)(2,1)S(1)}, bf16[192,256]{1,0:T(8,128)(2,1)S(1)}, u32[]{:S(2)}, u32[]{:S(2)}) %collective-permute-start.15) | collective-permute-done | bytes 98336 | tf_op jit(solution)/shard_map/return/ppermute | solution.py:381
  51.0 0.0 collective-permute-done.16.refs_7_
  51.0 1.0 %finish.2 = (bf16[192,256]{1,0:T(8,128)(2,1)}, bf16[192,256]{1,0:T(8,128)(2,1)}) custom-call(bf16[192,256]{1,0:T(8,128)(2,1)S(1)} %get-tuple-element.38.refs_0_, bf16[192,256]{1,0:T(8,128)(2,1)S(1)} %collective-permute-done.12.refs_1_, bf16[192,256]{1,0:T(8,128)(2,1)S(1)} %collective-permute-done.8.refs_2_, ...), custom_call_target="tpu_custom_call" | custom-call | flops 9059696640 | bytes 1376256 | tf_op jit(solution)/shard_map/finish/pallas_call | solution.py:344
  52.0 0.0 collective-permute-done.19.refs_3_
  52.0 0.9 %finish.3 = (bf16[192,256]{1,0:T(8,128)(2,1)}, bf16[192,256]{1,0:T(8,128)(2,1)}) custom-call(bf16[2,2,192,256]{3,2,1,0:T(8,128)(2,1)S(1)} %get-tuple-element.63.refs_0_, bf16[2,2,192,256]{3,2,1,0:T(8,128)(2,1)S(1)} %collective-permute-done.17.refs_1_, bf16[2,2,192,256]{3,2,1,0:T(8,128)(2,1)S(1)} %collective-permute-done.18.refs_2_, ...), custom_call_target="tpu_custom_call" | custom-call | bytes 1867776 | tf_op jit(solution)/shard_map/finish/pallas_call | solution.py:344
Async XLA Ops:
  1.9 10.3 %collective-permute-start.4 = (bf16[2,192,256]{2,1,0:T(8,128)(2,1)S(1)}, bf16[2,192,256]{2,1,0:T(8,128)(2,1)S(1)}, u32[]{:S(2)}, u32[]{:S(2)}) collective-permute-start(bf16[2,192,256]{2,1,0:T(8,128)(2,1)S(1)} %get-tuple-element.37.refs_3_.refs_1_.refs_4_), channel_id=1, source_target_pairs={{0,4},{4,0},{1,5},{5,1},{2,6},{6,2},{3,7},{7,3},{8,12},{12,8},{9,1... | collective-permute-start | bytes 589832 | tf_op jit(solution)/shard_map/halo/ppermute | solution.py:386
  4.0 10.9 %collective-permute-start.1 = (bf16[2,192,256]{2,1,0:T(8,128)(2,1)S(1)}, bf16[2,192,256]{2,1,0:T(8,128)(2,1)S(1)}, u32[]{:S(2)}, u32[]{:S(2)}) collective-permute-start(bf16[2,192,256]{2,1,0:T(8,128)(2,1)S(1)} %get-tuple-element.36.refs_0_), channel_id=1, source_target_pairs={{0,16},{8,24},{16,0},{24,8},{1,17},{9,25},{17,1},{25,9},{2,18},{10... | collective-permute-start | bytes 589832 | tf_op jit(solution)/shard_map/halo/ppermute | solution.py:381
  6.3 10.2 %collective-permute-start = (bf16[2,192,256]{2,1,0:T(8,128)(2,1)S(1)}, bf16[2,192,256]{2,1,0:T(8,128)(2,1)S(1)}, u32[]{:S(2)}, u32[]{:S(2)}) collective-permute-start(bf16[2,192,256]{2,1,0:T(8,128)(2,1)S(1)} %get-tuple-element.36.refs_0_), channel_id=1, source_target_pairs={{0,8},{8,0},{16,24},{24,16},{1,9},{9,1},{17,25},{25,17},{2,10},{10... | collective-permute-start | bytes 589832 | tf_op jit(solution)/shard_map/halo/ppermute | solution.py:381
  7.6 9.2 %collective-permute-start.3 = (bf16[2,192,256]{2,1,0:T(8,128)(2,1)S(1)}, bf16[2,192,256]{2,1,0:T(8,128)(2,1)S(1)}, u32[]{:S(2)}, u32[]{:S(2)}) collective-permute-start(bf16[2,192,256]{2,1,0:T(8,128)(2,1)S(1)} %get-tuple-element.37.refs_3_.refs_1_.refs_4_), channel_id=1, source_target_pairs={{0,0},{1,2},{2,1},{3,3},{4,4},{5,6},{6,5},{7,7},{8,8},{9,10},{10,9... | collective-permute-start | bytes 589832 | tf_op jit(solution)/shard_map/halo/ppermute | solution.py:391
  12.2 4.7 %collective-permute-start.2 = (bf16[2,192,256]{2,1,0:T(8,128)(2,1)S(1)}, bf16[2,192,256]{2,1,0:T(8,128)(2,1)S(1)}, u32[]{:S(2)}, u32[]{:S(2)}) collective-permute-start(bf16[2,192,256]{2,1,0:T(8,128)(2,1)S(1)} %get-tuple-element.37.refs_3_.refs_1_.refs_4_), channel_id=1, source_target_pairs={{0,1},{1,0},{2,3},{3,2},{4,5},{5,4},{6,7},{7,6},{8,9},{9,8},{10,11... | collective-permute-start | bytes 589832 | tf_op jit(solution)/shard_map/halo/ppermute | solution.py:391
  12.2 7.0 %collective-permute-start.6 = (bf16[2,192,256]{2,1,0:T(8,128)(2,1)S(1)}, bf16[2,192,256]{2,1,0:T(8,128)(2,1)S(1)}, u32[]{:S(2)}, u32[]{:S(2)}) collective-permute-start(bf16[2,192,256]{2,1,0:T(8,128)(2,1)S(1)} %collective-permute-done.4.refs_6_.refs_4_.refs_5_), channel_id=1, source_target_pairs={{0,0},{1,2},{2,1},{3,3},{4,4},{5,6},{6,5},{7,7},{8,8},{9,10},{10,9... | collective-permute-start | bytes 589832 | tf_op jit(solution)/shard_map/halo/ppermute | solution.py:391
  14.9 4.4 %collective-permute-start.5 = (bf16[2,192,256]{2,1,0:T(8,128)(2,1)S(1)}, bf16[2,192,256]{2,1,0:T(8,128)(2,1)S(1)}, u32[]{:S(2)}, u32[]{:S(2)}) collective-permute-start(bf16[2,192,256]{2,1,0:T(8,128)(2,1)S(1)} %collective-permute-done.4.refs_6_.refs_4_.refs_5_), channel_id=1, source_target_pairs={{0,1},{1,0},{2,3},{3,2},{4,5},{5,4},{6,7},{7,6},{8,9},{9,8},{10,11... | collective-permute-start | bytes 589832 | tf_op jit(solution)/shard_map/halo/ppermute | solution.py:391
  16.5 6.3 %collective-permute-start.7 = (bf16[2,192,256]{2,1,0:T(8,128)(2,1)S(1)}, bf16[2,192,256]{2,1,0:T(8,128)(2,1)S(1)}, u32[]{:S(2)}, u32[]{:S(2)}) collective-permute-start(bf16[2,192,256]{2,1,0:T(8,128)(2,1)S(1)} %collective-permute-done.1.refs_2_), channel_id=1, source_target_pairs={{0,8},{8,0},{16,24},{24,16},{1,9},{9,1},{17,25},{25,17},{2,10},{10... | collective-permute-start | bytes 589832 | tf_op jit(solution)/shard_map/halo/ppermute | solution.py:381
  21.7 7.7 %collective-permute-start.8 = (bf16[192,256]{1,0:T(8,128)(2,1)S(1)}, bf16[192,256]{1,0:T(8,128)(2,1)S(1)}, u32[]{:S(2)}, u32[]{:S(2)}) collective-permute-start(bf16[192,256]{1,0:T(8,128)(2,1)S(1)} %get-tuple-element.41), channel_id=1, source_target_pairs={{0,16},{8,24},{16,0},{24,8},{1,17},{9,25},{17,1},{25,9},{2,18},{10... | collective-permute-start | bytes 294920 | tf_op jit(solution)/shard_map/merge/ppermute | solution.py:381
  23.9 8.4 %collective-permute-start.11 = (f32[8,768]{1,0:T(8,128)S(1)}, f32[8,768]{1,0:T(8,128)S(1)}, u32[]{:S(2)}, u32[]{:S(2)}) collective-permute-start(f32[8,768]{1,0:T(8,128)S(1)} %get-tuple-element.42.refs_8_), channel_id=1, source_target_pairs={{0,16},{8,24},{16,0},{24,8},{1,17},{9,25},{17,1},{25,9},{2,18},{10... | collective-permute-start | bytes 73736 | tf_op jit(solution)/shard_map/merge/ppermute | solution.py:381
  26.3 6.0 %collective-permute-start.10 = (f32[8,768]{1,0:T(8,128)S(1)}, f32[8,768]{1,0:T(8,128)S(1)}, u32[]{:S(2)}, u32[]{:S(2)}) collective-permute-start(f32[8,768]{1,0:T(8,128)S(1)} %get-tuple-element.42.refs_8_), channel_id=1, source_target_pairs={{0,24},{8,16},{16,8},{24,0},{1,25},{9,17},{17,9},{25,1},{2,26},{10... | collective-permute-start | bytes 73736 | tf_op jit(solution)/shard_map/merge/ppermute | solution.py:381
  29.4 3.5 %collective-permute-start.9 = (f32[8,768]{1,0:T(8,128)S(1)}, f32[8,768]{1,0:T(8,128)S(1)}, u32[]{:S(2)}, u32[]{:S(2)}) collective-permute-start(f32[8,768]{1,0:T(8,128)S(1)} %get-tuple-element.42.refs_8_), channel_id=1, source_target_pairs={{0,8},{8,0},{16,24},{24,16},{1,9},{9,1},{17,25},{25,17},{2,10},{10... | collective-permute-start | bytes 73736 | tf_op jit(solution)/shard_map/merge/ppermute | solution.py:381
  29.4 12.6 %collective-permute-start.13 = (bf16[192,256]{1,0:T(8,128)(2,1)S(1)}, bf16[192,256]{1,0:T(8,128)(2,1)S(1)}, u32[]{:S(2)}, u32[]{:S(2)}) collective-permute-start(bf16[192,256]{1,0:T(8,128)(2,1)S(1)} %get-tuple-element.51), channel_id=1, source_target_pairs={{0,8},{8,0},{16,24},{24,16},{1,9},{9,1},{17,25},{25,17},{2,10},{10... | collective-permute-start | bytes 294920 | tf_op jit(solution)/shard_map/merge/ppermute | solution.py:381
  30.9 11.2 %collective-permute-start.12 = (bf16[192,256]{1,0:T(8,128)(2,1)S(1)}, bf16[192,256]{1,0:T(8,128)(2,1)S(1)}, u32[]{:S(2)}, u32[]{:S(2)}) collective-permute-start(bf16[192,256]{1,0:T(8,128)(2,1)S(1)} %get-tuple-element.49), channel_id=1, source_target_pairs={{0,24},{8,16},{16,8},{24,0},{1,25},{9,17},{17,9},{25,1},{2,26},{10... | collective-permute-start | bytes 294920 | tf_op jit(solution)/shard_map/merge/ppermute | solution.py:381
  36.0 9.7 %collective-permute-start.17 = (bf16[2,2,192,256]{3,2,1,0:T(8,128)(2,1)S(1)}, bf16[2,2,192,256]{3,2,1,0:T(8,128)(2,1)S(1)}, u32[]{:S(2)}, u32[]{:S(2)}) collective-permute-start(bf16[2,2,192,256]{3,2,1,0:T(8,128)(2,1)S(1)} %get-tuple-element.64), channel_id=1, source_target_pairs={{0,1},{1,0},{2,3},{3,2},{4,5},{5,4},{6,7},{7,6},{8,9},{9,8},{10,11... | collective-permute-start | bytes 1179656 | tf_op jit(solution)/shard_map/gradients/ppermute | solution.py:446
  37.3 9.4 %collective-permute-start.18 = (bf16[2,2,192,256]{3,2,1,0:T(8,128)(2,1)S(1)}, bf16[2,2,192,256]{3,2,1,0:T(8,128)(2,1)S(1)}, u32[]{:S(2)}, u32[]{:S(2)}) collective-permute-start(bf16[2,2,192,256]{3,2,1,0:T(8,128)(2,1)S(1)} %get-tuple-element.65), channel_id=1, source_target_pairs={{0,0},{1,2},{2,1},{3,3},{4,4},{5,6},{6,5},{7,7},{8,8},{9,10},{10,9... | collective-permute-start | bytes 1179656 | tf_op jit(solution)/shard_map/gradients/ppermute | solution.py:446
  42.1 6.4 %collective-permute-start.14 = (bf16[192,256]{1,0:T(8,128)(2,1)S(1)}, bf16[192,256]{1,0:T(8,128)(2,1)S(1)}, u32[]{:S(2)}, u32[]{:S(2)}) collective-permute-start(bf16[192,256]{1,0:T(8,128)(2,1)S(1)} %get-tuple-element.56), channel_id=1, source_target_pairs={{0,24},{8,16},{16,8},{24,0},{1,25},{9,17},{17,9},{25,1},{2,26},{10... | collective-permute-start | bytes 294920 | tf_op jit(solution)/shard_map/return/ppermute | solution.py:381
  43.6 7.3 %collective-permute-start.15 = (bf16[192,256]{1,0:T(8,128)(2,1)S(1)}, bf16[192,256]{1,0:T(8,128)(2,1)S(1)}, u32[]{:S(2)}, u32[]{:S(2)}) collective-permute-start(bf16[192,256]{1,0:T(8,128)(2,1)S(1)} %get-tuple-element.57), channel_id=1, source_target_pairs={{0,16},{8,24},{16,0},{24,8},{1,17},{9,25},{17,1},{25,9},{2,18},{10... | collective-permute-start | bytes 294920 | tf_op jit(solution)/shard_map/return/ppermute | solution.py:381
  43.6 7.3 %collective-permute-start.16 = (bf16[192,256]{1,0:T(8,128)(2,1)S(1)}, bf16[192,256]{1,0:T(8,128)(2,1)S(1)}, u32[]{:S(2)}, u32[]{:S(2)}) collective-permute-start(bf16[192,256]{1,0:T(8,128)(2,1)S(1)} %get-tuple-element.58), channel_id=1, source_target_pairs={{0,8},{8,0},{16,24},{24,16},{1,9},{9,1},{17,25},{25,17},{2,10},{10... | collective-permute-start | bytes 294920 | tf_op jit(solution)/shard_map/return/ppermute | solution.py:381
  46.8 5.2 %collective-permute-start.19 = (bf16[2,192,256]{2,1,0:T(8,128)(2,1)S(1)}, bf16[2,192,256]{2,1,0:T(8,128)(2,1)S(1)}, u32[]{:S(2)}, u32[]{:S(2)}) collective-permute-start(bf16[2,192,256]{2,1,0:T(8,128)(2,1)S(1)} %fusion), channel_id=1, source_target_pairs={{0,4},{4,0},{1,5},{5,1},{2,6},{6,2},{3,7},{7,3},{8,12},{12,8},{9,1... | collective-permute-start | bytes 589832 | tf_op jit(solution)/shard_map/return/ppermute | solution.py:455

commit v16 on v14

--- a/solution.py
+++ b/solution.py
@@ -448,7 +448,7 @@
     with jax.named_scope("return"):
         (d1, d2, d3), outs = lax.optimization_barrier(((d1, d2, d3), outs))
         col_parts = [own, *sides]
-        dqs = [d0] + [other_frames(x, d) for d, x in ((3, d3), (2, d2), (1, d1))]
+        dqs = [d0] + [other_frames(x, d) for d, x in ((2, d2), (3, d3), (1, d1))]
         row_parts = []
         for row, pairs in enumerate(row_sides, start=1):
             partial_sum = sum(x[row].astype(F32) for x in col_parts).astype(BF16)

time: 52.8 us -> 52.2 us (0.989)
  starting transfers between devices: 29.7 us -> 29 us
    ppermute x12, starting transfers between devices: 14.2 us -> 13.5 us  [other_frames(): lax.ppermute(x, 'ta', [(i, i ^ distance) for i in range(sizes['ta'])])]
    ppermute x2, waiting for transfers between devices: 0.95 us -> 1.64 us  [shards(): sides = [lax.ppermute(x, 'wa', pairs) for x, pairs in zip(sides, col_sides)]]
    ppermute x12, waiting for transfers between devices: 7.42 us -> 6.74 us  [other_frames(): lax.ppermute(x, 'ta', [(i, i ^ distance) for i in range(sizes['ta'])])]
where the time goes in v16:
time: 52.2 us; the launch traced here: 52 us
  starting transfers between devices  29 us (56%)
  Pallas kernels  11.4 us (22%)
  waiting for transfers between devices  10.8 us (21%)
  between operations  0.72 us (1%)
    ppermute x12, starting transfers between devices, other_frames(): lax.ppermute(x, 'ta', [(i, i ^ distance) for i in range(sizes['ta'])])  13.5 us
    pallas_call x7, Pallas kernels, call(): pl.pallas_call(kernel, out_shape=out_shape, in_specs=[pl.BlockSpec(memory...  11.4 us
    ppermute x4, starting transfers between devices, shards(): lax.ppermute(block, 'wa', pairs)  8.2 us
    ppermute x12, waiting for transfers between devices, other_frames(): lax.ppermute(x, 'ta', [(i, i ^ distance) for i in range(sizes['ta'])])  6.74 us
    ppermute x2, starting transfers between devices, shards(): sides = [lax.ppermute(x, 'wa', pairs) for x, pairs in zip(sides, col_sides)]  4.87 us
    ppermute x4, waiting for transfers between devices, shards(): lax.ppermute(block, 'wa', pairs)  2.4 us
    ppermute x1, starting transfers between devices, shards(): kv_rows = [kv] + [lax.ppermute(kv, 'ha', pairs) for pairs in row_sides]  2.11 us
    ppermute x2, waiting for transfers between devices, shards(): sides = [lax.ppermute(x, 'wa', pairs) for x, pairs in zip(sides, col_sides)]  1.64 us
  transfers between devices with their start and end apart: 20, of which 7 were waited for; matrix products, arithmetic and copies ran while one was open for 0% of the time, Pallas kernels for 18%

profile of v16, /device:TPU:1, one launch (start us, length us, event | category | flops | bytes accessed | tf_op | source)
XLA Modules:
  0.0 52.0 jit_solution(12937181092599468538)
XLA Ops:
  0.6 1.3 %rotate.1 = (bf16[2,192,256]{2,1,0:T(8,128)(2,1)S(1)}, bf16[2,192,256]{2,1,0:T(8,128)(2,1)S(1)}, f32[3,192,128]{2,1,0:T(8,128)S(1)}) custom-call(bf16[192,256]{1,0:T(8,128)(2,1)} %bitcast.10, bf16[192,256]{1,0:T(8,128)(2,1)} %bitcast.11, bf16[192,256]{1,0:T(8,128)(2,1)} %bitcast.12, bf16[192,256]{1,0:T(8,128)(2,1)} %bitcast.13, ...), custom_call_target="tpu_custom_call" | custom-call | bytes 1179648 | tf_op jit(solution)/shard_map/rotate/pallas_call | solution.py:344
  1.9 2.1 %collective-permute-start.4 = (bf16[2,192,256]{2,1,0:T(8,128)(2,1)S(1)}, bf16[2,192,256]{2,1,0:T(8,128)(2,1)S(1)}, u32[]{:S(2)}, u32[]{:S(2)}) collective-permute-start(bf16[2,192,256]{2,1,0:T(8,128)(2,1)S(1)} %get-tuple-element.38.refs_3_.refs_1_.refs_4_), channel_id=1, source_target_pairs={{0,4},{4,0},{1,5},{5,1},{2,6},{6,2},{3,7},{7,3},{8,12},{12,8},{9,1... | collective-permute-start | bytes 589832 | tf_op jit(solution)/shard_map/halo/ppermute | solution.py:386
  4.0 2.3 %collective-permute-start.1 = (bf16[2,192,256]{2,1,0:T(8,128)(2,1)S(1)}, bf16[2,192,256]{2,1,0:T(8,128)(2,1)S(1)}, u32[]{:S(2)}, u32[]{:S(2)}) collective-permute-start(bf16[2,192,256]{2,1,0:T(8,128)(2,1)S(1)} %get-tuple-element.37.refs_0_), channel_id=1, source_target_pairs={{0,16},{8,24},{16,0},{24,8},{1,17},{9,25},{17,1},{25,9},{2,18},{10... | collective-permute-start | bytes 589832 | tf_op jit(solution)/shard_map/halo/ppermute | solution.py:381
  6.3 1.3 %collective-permute-start = (bf16[2,192,256]{2,1,0:T(8,128)(2,1)S(1)}, bf16[2,192,256]{2,1,0:T(8,128)(2,1)S(1)}, u32[]{:S(2)}, u32[]{:S(2)}) collective-permute-start(bf16[2,192,256]{2,1,0:T(8,128)(2,1)S(1)} %get-tuple-element.37.refs_0_), channel_id=1, source_target_pairs={{0,8},{8,0},{16,24},{24,16},{1,9},{9,1},{17,25},{25,17},{2,10},{10... | collective-permute-start | bytes 589832 | tf_op jit(solution)/shard_map/halo/ppermute | solution.py:381
  7.6 4.5 %collective-permute-start.3 = (bf16[2,192,256]{2,1,0:T(8,128)(2,1)S(1)}, bf16[2,192,256]{2,1,0:T(8,128)(2,1)S(1)}, u32[]{:S(2)}, u32[]{:S(2)}) collective-permute-start(bf16[2,192,256]{2,1,0:T(8,128)(2,1)S(1)} %get-tuple-element.38.refs_3_.refs_1_.refs_4_), channel_id=1, source_target_pairs={{0,0},{1,2},{2,1},{3,3},{4,4},{5,6},{6,5},{7,7},{8,8},{9,10},{10,9... | collective-permute-start | bytes 589832 | tf_op jit(solution)/shard_map/halo/ppermute | solution.py:391
  12.2 0.1 collective-permute-start.2
  12.2 0.0 collective-permute-done.4.refs_6_.refs_4_.refs_5_
  12.2 1.9 %collective-permute-start.6 = (bf16[2,192,256]{2,1,0:T(8,128)(2,1)S(1)}, bf16[2,192,256]{2,1,0:T(8,128)(2,1)S(1)}, u32[]{:S(2)}, u32[]{:S(2)}) collective-permute-start(bf16[2,192,256]{2,1,0:T(8,128)(2,1)S(1)} %collective-permute-done.4.refs_6_.refs_4_.refs_5_), channel_id=1, source_target_pairs={{0,0},{1,2},{2,1},{3,3},{4,4},{5,6},{6,5},{7,7},{8,8},{9,10},{10,9... | collective-permute-start | bytes 589832 | tf_op jit(solution)/shard_map/halo/ppermute | solution.py:391
  14.2 0.7 %collective-permute-done.1.refs_2_ = bf16[2,192,256]{2,1,0:T(8,128)(2,1)S(1)} collective-permute-done((bf16[2,192,256]{2,1,0:T(8,128)(2,1)S(1)}, bf16[2,192,256]{2,1,0:T(8,128)(2,1)S(1)}, u32[]{:S(2)}, u32[]{:S(2)}) %collective-permute-start.1) | collective-permute-done | bytes 196640 | tf_op jit(solution)/shard_map/halo/ppermute | solution.py:381
  14.9 1.7 %collective-permute-start.5 = (bf16[2,192,256]{2,1,0:T(8,128)(2,1)S(1)}, bf16[2,192,256]{2,1,0:T(8,128)(2,1)S(1)}, u32[]{:S(2)}, u32[]{:S(2)}) collective-permute-start(bf16[2,192,256]{2,1,0:T(8,128)(2,1)S(1)} %collective-permute-done.4.refs_6_.refs_4_.refs_5_), channel_id=1, source_target_pairs={{0,1},{1,0},{2,3},{3,2},{4,5},{5,4},{6,7},{7,6},{8,9},{9,8},{10,11... | collective-permute-start | bytes 589832 | tf_op jit(solution)/shard_map/halo/ppermute | solution.py:391
  16.5 0.0 collective-permute-done.refs_1_
  16.5 0.3 collective-permute-start.7
  16.8 0.0 collective-permute-done.3.refs_5_.refs_3_.refs_6_
  16.8 0.0 collective-permute-done.2.refs_4_.refs_2_
  16.8 2.4 %collective-permute-done.6.refs_8_.refs_6_.refs_7_ = bf16[2,192,256]{2,1,0:T(8,128)(2,1)S(1)} collective-permute-done((bf16[2,192,256]{2,1,0:T(8,128)(2,1)S(1)}, bf16[2,192,256]{2,1,0:T(8,128)(2,1)S(1)}, u32[]{:S(2)}, u32[]{:S(2)}) %collective-permute-start.6) | collective-permute-done | bytes 196640 | tf_op jit(solution)/shard_map/halo/ppermute | solution.py:391
  19.2 0.0 collective-permute-done.5.refs_7_.refs_5_
  19.2 2.4 %attend.2 = (bf16[192,256]{1,0:T(8,128)(2,1)S(1)}, bf16[192,256]{1,0:T(8,128)(2,1)S(1)}, bf16[192,256]{1,0:T(8,128)(2,1)S(1)}, f32[576,128]{1,0:T(8,128)S(1)}) custom-call(bf16[2,192,256]{2,1,0:T(8,128)(2,1)S(1)} %get-tuple-element.37.refs_0_, bf16[2,192,256]{2,1,0:T(8,128)(2,1)S(1)} %collective-permute-done.refs_1_, ...), custom_call_target="tpu_custom_call" | custom-call | flops 5435817984 | bytes 2359296 | tf_op jit(solution)/shard_map/attend/pallas_call | solution.py:344
  21.7 0.8 %collective-permute-start.8 = (bf16[192,256]{1,0:T(8,128)(2,1)S(1)}, bf16[192,256]{1,0:T(8,128)(2,1)S(1)}, u32[]{:S(2)}, u32[]{:S(2)}) collective-permute-start(bf16[192,256]{1,0:T(8,128)(2,1)S(1)} %get-tuple-element.42), channel_id=1, source_target_pairs={{0,16},{8,24},{16,0},{24,8},{1,17},{9,25},{17,1},{25,9},{2,18},{10... | collective-permute-start | bytes 294920 | tf_op jit(solution)/shard_map/merge/ppermute | solution.py:381
  22.4 1.0 %collective-permute-start.9 = (bf16[192,256]{1,0:T(8,128)(2,1)S(1)}, bf16[192,256]{1,0:T(8,128)(2,1)S(1)}, u32[]{:S(2)}, u32[]{:S(2)}) collective-permute-start(bf16[192,256]{1,0:T(8,128)(2,1)S(1)} %get-tuple-element.43), channel_id=1, source_target_pairs={{0,8},{8,0},{16,24},{24,16},{1,9},{9,1},{17,25},{25,17},{2,10},{10... | collective-permute-start | bytes 294920 | tf_op jit(solution)/shard_map/merge/ppermute | solution.py:381
  23.5 0.0 collective-permute-done.7.refs_0_.refs_3_
  23.5 1.0 %attend.3 = (bf16[192,256]{1,0:T(8,128)(2,1)S(1)}, f32[8,768]{1,0:T(8,128)S(1)}) custom-call(bf16[2,192,256]{2,1,0:T(8,128)(2,1)S(1)} %collective-permute-done.7.refs_0_.refs_3_, bf16[2,192,256]{2,1,0:T(8,128)(2,1)S(1)} %get-tuple-element.38.refs_3_.refs_1_.refs_4_, bf16[2,192,256]{2,1,0:T(8,128)(2,1)S(1)} %collective-permute-done.2.refs_4_.refs_2_, ...), custom_call_target="tpu_custom_call" | custom-call | flops 1811939328 | bytes 1794048 | tf_op jit(solution)/shard_map/attend/pallas_call | solution.py:344
  24.5 1.7 %collective-permute-start.12 = (f32[8,768]{1,0:T(8,128)S(1)}, f32[8,768]{1,0:T(8,128)S(1)}, u32[]{:S(2)}, u32[]{:S(2)}) collective-permute-start(f32[8,768]{1,0:T(8,128)S(1)} %get-tuple-element.44.refs_8_), channel_id=1, source_target_pairs={{0,16},{8,24},{16,0},{24,8},{1,17},{9,25},{17,1},{25,9},{2,18},{10... | collective-permute-start | bytes 73736 | tf_op jit(solution)/shard_map/merge/ppermute | solution.py:381
  26.3 1.1 %collective-permute-start.11 = (f32[8,768]{1,0:T(8,128)S(1)}, f32[8,768]{1,0:T(8,128)S(1)}, u32[]{:S(2)}, u32[]{:S(2)}) collective-permute-start(f32[8,768]{1,0:T(8,128)S(1)} %get-tuple-element.44.refs_8_), channel_id=1, source_target_pairs={{0,24},{8,16},{16,8},{24,0},{1,25},{9,17},{17,9},{25,1},{2,26},{10... | collective-permute-start | bytes 73736 | tf_op jit(solution)/shard_map/merge/ppermute | solution.py:381
  27.3 1.4 %collective-permute-done.8.refs_2_ = bf16[192,256]{1,0:T(8,128)(2,1)S(1)} collective-permute-done((bf16[192,256]{1,0:T(8,128)(2,1)S(1)}, bf16[192,256]{1,0:T(8,128)(2,1)S(1)}, u32[]{:S(2)}, u32[]{:S(2)}) %collective-permute-start.8) | collective-permute-done | bytes 98336 | tf_op jit(solution)/shard_map/merge/ppermute | solution.py:381
  28.7 0.0 collective-permute-done.9.refs_3_
  28.7 0.0 collective-permute-start.10
  28.7 2.1 %collective-permute-start.13 = (bf16[192,256]{1,0:T(8,128)(2,1)S(1)}, bf16[192,256]{1,0:T(8,128)(2,1)S(1)}, u32[]{:S(2)}, u32[]{:S(2)}) collective-permute-start(bf16[192,256]{1,0:T(8,128)(2,1)S(1)} %get-tuple-element.51), channel_id=1, source_target_pairs={{0,24},{8,16},{16,8},{24,0},{1,25},{9,17},{17,9},{25,1},{2,26},{10... | collective-permute-start | bytes 294920 | tf_op jit(solution)/shard_map/merge/ppermute | solution.py:381
  30.8 0.0 collective-permute-done.12.refs_11_
  30.8 0.0 collective-permute-done.11.refs_10_
  30.8 0.6 %collective-permute-done.10.refs_9_ = f32[8,768]{1,0:T(8,128)S(1)} collective-permute-done((f32[8,768]{1,0:T(8,128)S(1)}, f32[8,768]{1,0:T(8,128)S(1)}, u32[]{:S(2)}, u32[]{:S(2)}) %collective-permute-start.10) | collective-permute-done | bytes 24608 | tf_op jit(solution)/shard_map/merge/ppermute | solution.py:381
  31.4 3.1 %gradients.2 = (f32[2,128,768]{2,1,0:T(8,128)S(1)}, f32[2,768]{1,0:T(2,128)S(1)}, f32[2,768]{1,0:T(2,128)S(1)}, f32[192,128]{1,0:T(8,128)S(1)}, bf16[2,2,192,256...) custom-call(bf16[2,192,256]{2,1,0:T(8,128)(2,1)S(1)} %get-tuple-element.37.refs_0_, ...), custom_call_target="tpu_custom_call" | custom-call | flops 12079595520 | bytes 3354624 | tf_op jit(solution)/shard_map/gradients/pallas_call | solution.py:344
  34.5 1.8 %collective-permute-start.17 = (bf16[2,2,192,256]{3,2,1,0:T(8,128)(2,1)S(1)}, bf16[2,2,192,256]{3,2,1,0:T(8,128)(2,1)S(1)}, u32[]{:S(2)}, u32[]{:S(2)}) collective-permute-start(bf16[2,2,192,256]{3,2,1,0:T(8,128)(2,1)S(1)} %get-tuple-element.66), channel_id=1, source_target_pairs={{0,1},{1,0},{2,3},{3,2},{4,5},{5,4},{6,7},{7,6},{8,9},{9,8},{10,11... | collective-permute-start | bytes 1179656 | tf_op jit(solution)/shard_map/gradients/ppermute | solution.py:446
  36.2 3.1 %collective-permute-start.18 = (bf16[2,2,192,256]{3,2,1,0:T(8,128)(2,1)S(1)}, bf16[2,2,192,256]{3,2,1,0:T(8,128)(2,1)S(1)}, u32[]{:S(2)}, u32[]{:S(2)}) collective-permute-start(bf16[2,2,192,256]{3,2,1,0:T(8,128)(2,1)S(1)} %get-tuple-element.67), channel_id=1, source_target_pairs={{0,0},{1,2},{2,1},{3,3},{4,4},{5,6},{6,5},{7,7},{8,8},{9,10},{10,9... | collective-permute-start | bytes 1179656 | tf_op jit(solution)/shard_map/gradients/ppermute | solution.py:446
  39.4 1.7 %gradients.3 = (bf16[192,256]{1,0:T(8,128)(2,1)S(1)}, bf16[192,256]{1,0:T(8,128)(2,1)S(1)}, bf16[192,256]{1,0:T(8,128)(2,1)S(1)}, bf16[192,256]{1,0:T(8,128)(2,1)S(1)}, bf16[2,2,192,256]{3,2,1,0:T(8,128)(2,1)S(1)}) custom-call(bf16[2,192,256]{2,1,0:T(8,128)(2,1)S(1)} %get-tuple-element.37.refs_0_, bf16[2,192,256]{2,1,0:T(8,128)(2,1)S(1)} %collective-permute-done.refs_1_, ...), custom_call_target="tpu_custom_call" | custom-call | flops 6039797760 | bytes 2764800 | tf_op jit(solution)/shard_map/gradients/pallas_call | solution.py:344
  41.0 0.0 collective-permute-done.13.refs_1_
  41.0 1.6 %collective-permute-start.14 = (bf16[192,256]{1,0:T(8,128)(2,1)S(1)}, bf16[192,256]{1,0:T(8,128)(2,1)S(1)}, u32[]{:S(2)}, u32[]{:S(2)}) collective-permute-start(bf16[192,256]{1,0:T(8,128)(2,1)S(1)} %get-tuple-element.58), channel_id=1, source_target_pairs={{0,16},{8,24},{16,0},{24,8},{1,17},{9,25},{17,1},{25,9},{2,18},{10... | collective-permute-start | bytes 294920 | tf_op jit(solution)/shard_map/return/ppermute | solution.py:381
  42.7 1.3 %collective-permute-start.15 = (bf16[192,256]{1,0:T(8,128)(2,1)S(1)}, bf16[192,256]{1,0:T(8,128)(2,1)S(1)}, u32[]{:S(2)}, u32[]{:S(2)}) collective-permute-start(bf16[192,256]{1,0:T(8,128)(2,1)S(1)} %get-tuple-element.59), channel_id=1, source_target_pairs={{0,24},{8,16},{16,8},{24,0},{1,25},{9,17},{17,9},{25,1},{2,26},{10... | collective-permute-start | bytes 294920 | tf_op jit(solution)/shard_map/return/ppermute | solution.py:381
  44.0 0.0 collective-permute-start.16
  44.0 0.0 collective-permute-done.17.refs_1_
  44.0 1.6 %collective-permute-done.18.refs_2_ = bf16[2,2,192,256]{3,2,1,0:T(8,128)(2,1)S(1)} collective-permute-done((bf16[2,2,192,256]{3,2,1,0:T(8,128)(2,1)S(1)}, bf16[2,2,192,256]{3,2,1,0:T(8,128)(2,1)S(1)}, u32[]{:S(2)}, u32[]{:S(2)}) %collective-permute-start.18) | collective-permute-done | bytes 393248 | tf_op jit(solution)/shard_map/gradients/ppermute | solution.py:446
  45.6 0.1 fusion
  45.7 0.3 collective-permute-start.19
  46.0 3.8 %collective-permute-done.14.refs_5_ = bf16[192,256]{1,0:T(8,128)(2,1)S(1)} collective-permute-done((bf16[192,256]{1,0:T(8,128)(2,1)S(1)}, bf16[192,256]{1,0:T(8,128)(2,1)S(1)}, u32[]{:S(2)}, u32[]{:S(2)}) %collective-permute-start.14) | collective-permute-done | bytes 98336 | tf_op jit(solution)/shard_map/return/ppermute | solution.py:381
  49.8 0.0 collective-permute-done.15.refs_6_
  49.8 0.3 collective-permute-done.16.refs_7_
  50.1 1.0 %finish.2 = (bf16[192,256]{1,0:T(8,128)(2,1)}, bf16[192,256]{1,0:T(8,128)(2,1)}) custom-call(bf16[192,256]{1,0:T(8,128)(2,1)S(1)} %get-tuple-element.39.refs_0_, bf16[192,256]{1,0:T(8,128)(2,1)S(1)} %collective-permute-done.13.refs_1_, bf16[192,256]{1,0:T(8,128)(2,1)S(1)} %collective-permute-done.8.refs_2_, ...), custom_call_target="tpu_custom_call" | custom-call | flops 9059696640 | bytes 1376256 | tf_op jit(solution)/shard_map/finish/pallas_call | solution.py:344
  51.1 0.0 collective-permute-done.19.refs_3_
  51.1 0.9 %finish.3 = (bf16[192,256]{1,0:T(8,128)(2,1)}, bf16[192,256]{1,0:T(8,128)(2,1)}) custom-call(bf16[2,2,192,256]{3,2,1,0:T(8,128)(2,1)S(1)} %get-tuple-element.65.refs_0_, bf16[2,2,192,256]{3,2,1,0:T(8,128)(2,1)S(1)} %collective-permute-done.17.refs_1_, bf16[2,2,192,256]{3,2,1,0:T(8,128)(2,1)S(1)} %collective-permute-done.18.refs_2_, ...), custom_call_target="tpu_custom_call" | custom-call | bytes 1867776 | tf_op jit(solution)/shard_map/finish/pallas_call | solution.py:344
Async XLA Ops:
  1.9 10.3 %collective-permute-start.4 = (bf16[2,192,256]{2,1,0:T(8,128)(2,1)S(1)}, bf16[2,192,256]{2,1,0:T(8,128)(2,1)S(1)}, u32[]{:S(2)}, u32[]{:S(2)}) collective-permute-start(bf16[2,192,256]{2,1,0:T(8,128)(2,1)S(1)} %get-tuple-element.38.refs_3_.refs_1_.refs_4_), channel_id=1, source_target_pairs={{0,4},{4,0},{1,5},{5,1},{2,6},{6,2},{3,7},{7,3},{8,12},{12,8},{9,1... | collective-permute-start | bytes 589832 | tf_op jit(solution)/shard_map/halo/ppermute | solution.py:386
  4.0 10.9 %collective-permute-start.1 = (bf16[2,192,256]{2,1,0:T(8,128)(2,1)S(1)}, bf16[2,192,256]{2,1,0:T(8,128)(2,1)S(1)}, u32[]{:S(2)}, u32[]{:S(2)}) collective-permute-start(bf16[2,192,256]{2,1,0:T(8,128)(2,1)S(1)} %get-tuple-element.37.refs_0_), channel_id=1, source_target_pairs={{0,16},{8,24},{16,0},{24,8},{1,17},{9,25},{17,1},{25,9},{2,18},{10... | collective-permute-start | bytes 589832 | tf_op jit(solution)/shard_map/halo/ppermute | solution.py:381
  6.3 10.2 %collective-permute-start = (bf16[2,192,256]{2,1,0:T(8,128)(2,1)S(1)}, bf16[2,192,256]{2,1,0:T(8,128)(2,1)S(1)}, u32[]{:S(2)}, u32[]{:S(2)}) collective-permute-start(bf16[2,192,256]{2,1,0:T(8,128)(2,1)S(1)} %get-tuple-element.37.refs_0_), channel_id=1, source_target_pairs={{0,8},{8,0},{16,24},{24,16},{1,9},{9,1},{17,25},{25,17},{2,10},{10... | collective-permute-start | bytes 589832 | tf_op jit(solution)/shard_map/halo/ppermute | solution.py:381
  7.6 9.2 %collective-permute-start.3 = (bf16[2,192,256]{2,1,0:T(8,128)(2,1)S(1)}, bf16[2,192,256]{2,1,0:T(8,128)(2,1)S(1)}, u32[]{:S(2)}, u32[]{:S(2)}) collective-permute-start(bf16[2,192,256]{2,1,0:T(8,128)(2,1)S(1)} %get-tuple-element.38.refs_3_.refs_1_.refs_4_), channel_id=1, source_target_pairs={{0,0},{1,2},{2,1},{3,3},{4,4},{5,6},{6,5},{7,7},{8,8},{9,10},{10,9... | collective-permute-start | bytes 589832 | tf_op jit(solution)/shard_map/halo/ppermute | solution.py:391
  12.2 4.7 %collective-permute-start.2 = (bf16[2,192,256]{2,1,0:T(8,128)(2,1)S(1)}, bf16[2,192,256]{2,1,0:T(8,128)(2,1)S(1)}, u32[]{:S(2)}, u32[]{:S(2)}) collective-permute-start(bf16[2,192,256]{2,1,0:T(8,128)(2,1)S(1)} %get-tuple-element.38.refs_3_.refs_1_.refs_4_), channel_id=1, source_target_pairs={{0,1},{1,0},{2,3},{3,2},{4,5},{5,4},{6,7},{7,6},{8,9},{9,8},{10,11... | collective-permute-start | bytes 589832 | tf_op jit(solution)/shard_map/halo/ppermute | solution.py:391
  12.2 7.0 %collective-permute-start.6 = (bf16[2,192,256]{2,1,0:T(8,128)(2,1)S(1)}, bf16[2,192,256]{2,1,0:T(8,128)(2,1)S(1)}, u32[]{:S(2)}, u32[]{:S(2)}) collective-permute-start(bf16[2,192,256]{2,1,0:T(8,128)(2,1)S(1)} %collective-permute-done.4.refs_6_.refs_4_.refs_5_), channel_id=1, source_target_pairs={{0,0},{1,2},{2,1},{3,3},{4,4},{5,6},{6,5},{7,7},{8,8},{9,10},{10,9... | collective-permute-start | bytes 589832 | tf_op jit(solution)/shard_map/halo/ppermute | solution.py:391
  14.9 4.4 %collective-permute-start.5 = (bf16[2,192,256]{2,1,0:T(8,128)(2,1)S(1)}, bf16[2,192,256]{2,1,0:T(8,128)(2,1)S(1)}, u32[]{:S(2)}, u32[]{:S(2)}) collective-permute-start(bf16[2,192,256]{2,1,0:T(8,128)(2,1)S(1)} %collective-permute-done.4.refs_6_.refs_4_.refs_5_), channel_id=1, source_target_pairs={{0,1},{1,0},{2,3},{3,2},{4,5},{5,4},{6,7},{7,6},{8,9},{9,8},{10,11... | collective-permute-start | bytes 589832 | tf_op jit(solution)/shard_map/halo/ppermute | solution.py:391
  16.5 7.0 %collective-permute-start.7 = (bf16[2,192,256]{2,1,0:T(8,128)(2,1)S(1)}, bf16[2,192,256]{2,1,0:T(8,128)(2,1)S(1)}, u32[]{:S(2)}, u32[]{:S(2)}) collective-permute-start(bf16[2,192,256]{2,1,0:T(8,128)(2,1)S(1)} %collective-permute-done.1.refs_2_), channel_id=1, source_target_pairs={{0,8},{8,0},{16,24},{24,16},{1,9},{9,1},{17,25},{25,17},{2,10},{10... | collective-permute-start | bytes 589832 | tf_op jit(solution)/shard_map/halo/ppermute | solution.py:381
  21.7 7.0 %collective-permute-start.8 = (bf16[192,256]{1,0:T(8,128)(2,1)S(1)}, bf16[192,256]{1,0:T(8,128)(2,1)S(1)}, u32[]{:S(2)}, u32[]{:S(2)}) collective-permute-start(bf16[192,256]{1,0:T(8,128)(2,1)S(1)} %get-tuple-element.42), channel_id=1, source_target_pairs={{0,16},{8,24},{16,0},{24,8},{1,17},{9,25},{17,1},{25,9},{2,18},{10... | collective-permute-start | bytes 294920 | tf_op jit(solution)/shard_map/merge/ppermute | solution.py:381
  22.4 6.2 %collective-permute-start.9 = (bf16[192,256]{1,0:T(8,128)(2,1)S(1)}, bf16[192,256]{1,0:T(8,128)(2,1)S(1)}, u32[]{:S(2)}, u32[]{:S(2)}) collective-permute-start(bf16[192,256]{1,0:T(8,128)(2,1)S(1)} %get-tuple-element.43), channel_id=1, source_target_pairs={{0,8},{8,0},{16,24},{24,16},{1,9},{9,1},{17,25},{25,17},{2,10},{10... | collective-permute-start | bytes 294920 | tf_op jit(solution)/shard_map/merge/ppermute | solution.py:381
  24.5 6.3 %collective-permute-start.12 = (f32[8,768]{1,0:T(8,128)S(1)}, f32[8,768]{1,0:T(8,128)S(1)}, u32[]{:S(2)}, u32[]{:S(2)}) collective-permute-start(f32[8,768]{1,0:T(8,128)S(1)} %get-tuple-element.44.refs_8_), channel_id=1, source_target_pairs={{0,16},{8,24},{16,0},{24,8},{1,17},{9,25},{17,1},{25,9},{2,18},{10... | collective-permute-start | bytes 73736 | tf_op jit(solution)/shard_map/merge/ppermute | solution.py:381
  26.3 4.5 %collective-permute-start.11 = (f32[8,768]{1,0:T(8,128)S(1)}, f32[8,768]{1,0:T(8,128)S(1)}, u32[]{:S(2)}, u32[]{:S(2)}) collective-permute-start(f32[8,768]{1,0:T(8,128)S(1)} %get-tuple-element.44.refs_8_), channel_id=1, source_target_pairs={{0,24},{8,16},{16,8},{24,0},{1,25},{9,17},{17,9},{25,1},{2,26},{10... | collective-permute-start | bytes 73736 | tf_op jit(solution)/shard_map/merge/ppermute | solution.py:381
  28.7 2.7 %collective-permute-start.10 = (f32[8,768]{1,0:T(8,128)S(1)}, f32[8,768]{1,0:T(8,128)S(1)}, u32[]{:S(2)}, u32[]{:S(2)}) collective-permute-start(f32[8,768]{1,0:T(8,128)S(1)} %get-tuple-element.44.refs_8_), channel_id=1, source_target_pairs={{0,8},{8,0},{16,24},{24,16},{1,9},{9,1},{17,25},{25,17},{2,10},{10... | collective-permute-start | bytes 73736 | tf_op jit(solution)/shard_map/merge/ppermute | solution.py:381
  28.7 12.3 %collective-permute-start.13 = (bf16[192,256]{1,0:T(8,128)(2,1)S(1)}, bf16[192,256]{1,0:T(8,128)(2,1)S(1)}, u32[]{:S(2)}, u32[]{:S(2)}) collective-permute-start(bf16[192,256]{1,0:T(8,128)(2,1)S(1)} %get-tuple-element.51), channel_id=1, source_target_pairs={{0,24},{8,16},{16,8},{24,0},{1,25},{9,17},{17,9},{25,1},{2,26},{10... | collective-permute-start | bytes 294920 | tf_op jit(solution)/shard_map/merge/ppermute | solution.py:381
  34.5 9.5 %collective-permute-start.17 = (bf16[2,2,192,256]{3,2,1,0:T(8,128)(2,1)S(1)}, bf16[2,2,192,256]{3,2,1,0:T(8,128)(2,1)S(1)}, u32[]{:S(2)}, u32[]{:S(2)}) collective-permute-start(bf16[2,2,192,256]{3,2,1,0:T(8,128)(2,1)S(1)} %get-tuple-element.66), channel_id=1, source_target_pairs={{0,1},{1,0},{2,3},{3,2},{4,5},{5,4},{6,7},{7,6},{8,9},{9,8},{10,11... | collective-permute-start | bytes 1179656 | tf_op jit(solution)/shard_map/gradients/ppermute | solution.py:446
  36.2 9.4 %collective-permute-start.18 = (bf16[2,2,192,256]{3,2,1,0:T(8,128)(2,1)S(1)}, bf16[2,2,192,256]{3,2,1,0:T(8,128)(2,1)S(1)}, u32[]{:S(2)}, u32[]{:S(2)}) collective-permute-start(bf16[2,2,192,256]{3,2,1,0:T(8,128)(2,1)S(1)} %get-tuple-element.67), channel_id=1, source_target_pairs={{0,0},{1,2},{2,1},{3,3},{4,4},{5,6},{6,5},{7,7},{8,8},{9,10},{10,9... | collective-permute-start | bytes 1179656 | tf_op jit(solution)/shard_map/gradients/ppermute | solution.py:446
  41.0 8.7 %collective-permute-start.14 = (bf16[192,256]{1,0:T(8,128)(2,1)S(1)}, bf16[192,256]{1,0:T(8,128)(2,1)S(1)}, u32[]{:S(2)}, u32[]{:S(2)}) collective-permute-start(bf16[192,256]{1,0:T(8,128)(2,1)S(1)} %get-tuple-element.58), channel_id=1, source_target_pairs={{0,16},{8,24},{16,0},{24,8},{1,17},{9,25},{17,1},{25,9},{2,18},{10... | collective-permute-start | bytes 294920 | tf_op jit(solution)/shard_map/return/ppermute | solution.py:381
  42.7 7.1 %collective-permute-start.15 = (bf16[192,256]{1,0:T(8,128)(2,1)S(1)}, bf16[192,256]{1,0:T(8,128)(2,1)S(1)}, u32[]{:S(2)}, u32[]{:S(2)}) collective-permute-start(bf16[192,256]{1,0:T(8,128)(2,1)S(1)} %get-tuple-element.59), channel_id=1, source_target_pairs={{0,24},{8,16},{16,8},{24,0},{1,25},{9,17},{17,9},{25,1},{2,26},{10... | collective-permute-start | bytes 294920 | tf_op jit(solution)/shard_map/return/ppermute | solution.py:381
  44.0 6.1 %collective-permute-start.16 = (bf16[192,256]{1,0:T(8,128)(2,1)S(1)}, bf16[192,256]{1,0:T(8,128)(2,1)S(1)}, u32[]{:S(2)}, u32[]{:S(2)}) collective-permute-start(bf16[192,256]{1,0:T(8,128)(2,1)S(1)} %get-tuple-element.60), channel_id=1, source_target_pairs={{0,8},{8,0},{16,24},{24,16},{1,9},{9,1},{17,25},{25,17},{2,10},{10... | collective-permute-start | bytes 294920 | tf_op jit(solution)/shard_map/return/ppermute | solution.py:381
  45.7 5.4 %collective-permute-start.19 = (bf16[2,192,256]{2,1,0:T(8,128)(2,1)S(1)}, bf16[2,192,256]{2,1,0:T(8,128)(2,1)S(1)}, u32[]{:S(2)}, u32[]{:S(2)}) collective-permute-start(bf16[2,192,256]{2,1,0:T(8,128)(2,1)S(1)} %fusion), channel_id=1, source_target_pairs={{0,4},{4,0},{1,5},{5,1},{2,6},{6,2},{3,7},{7,3},{8,12},{12,8},{9,1... | collective-permute-start | bytes 589832 | tf_op jit(solution)/shard_map/return/ppermute | solution.py:455

commit v17 on v16

--- a/solution.py
+++ b/solution.py
@@ -307,9 +307,11 @@
             dq_out[head] = dq
 
 
-def finish_query_kernel(*refs):
-    o_refs, dq_refs = refs[:4], refs[4:8]
-    share_ref, rope_ref, out_ref, dq_out = refs[8:]
+def finish_kernel(cols, rows, *refs):
+    o_refs, dq_refs, refs = refs[:4], refs[4:8], refs[8:]
+    col_refs, row_refs = refs[:cols], refs[cols : cols + 2 * rows]
+    share_ref, rope_ref, out_ref, dq_out, dk_out, dv_out = refs[cols + 2 * rows :]
+    tables = [rope_ref[plane] for plane in range(3)]
     for head in range(HEADS):
         cut = head_slice(head)
         outs = []
@@ -318,22 +320,13 @@
             outs.append(o_ref[:, cut].astype(F32) * weight)
         out_ref[:, cut] = functools.reduce(jnp.add, outs).astype(BF16)
         dq = functools.reduce(jnp.add, [ref[:, cut].astype(F32) for ref in dq_refs])
-        dq_out[:, cut] = turn(dq, rope_ref[0], rope_ref[1], rope_ref[2], -1.0).astype(BF16)
-
-
-def finish_key_kernel(cols, rows, *refs):
-    col_refs, row_refs = refs[:cols], refs[cols : cols + rows]
-    rope_ref, dk_out, dv_out = refs[cols + rows :]
-    for head in range(HEADS):
-        cut = head_slice(head)
+        dq_out[:, cut] = turn(dq, *tables, -1.0).astype(BF16)
         sums = []
         for which in range(2):
             terms = [ref[0, which, :, cut].astype(F32) for ref in col_refs]
-            terms += [ref[which, :, cut].astype(F32) for ref in row_refs]
+            terms += [ref[:, cut].astype(F32) for ref in row_refs[which::2]]
             sums.append(functools.reduce(jnp.add, terms))
-        dk_out[:, cut] = turn(
-            sums[0], rope_ref[0], rope_ref[1], rope_ref[2], -1.0
-        ).astype(BF16)
+        dk_out[:, cut] = turn(sums[0], *tables, -1.0).astype(BF16)
         dv_out[:, cut] = sums[1].astype(BF16)
 
 
@@ -451,19 +444,17 @@
         dqs = [d0] + [other_frames(x, d) for d, x in ((2, d2), (3, d3), (1, d1))]
         row_parts = []
         for row, pairs in enumerate(row_sides, start=1):
-            partial_sum = sum(x[row].astype(F32) for x in col_parts).astype(BF16)
-            row_parts.append(lax.ppermute(partial_sum, "ha", pairs))
+            for which in range(2):
+                partial_sum = sum(x[row, which].astype(F32) for x in col_parts).astype(BF16)
+                row_parts.append(lax.ppermute(partial_sum, "ha", pairs))
 
     with jax.named_scope("finish"):
-        attended, grad_query = call(
-            finish_query_kernel, (plain, plain), (o0, *outs, *dqs, shares, rope), 10 * product
+        results = call(
+            functools.partial(finish_kernel, grid_cols, len(row_parts) // 2),
+            [plain] * 4,
+            (o0, *outs, *dqs, *col_parts, *row_parts, shares, rope),
         )
-        grad_key, grad_value = call(
-            functools.partial(finish_key_kernel, grid_cols, len(row_parts)),
-            (plain, plain),
-            (*col_parts, *row_parts, rope),
-        )
-    return tuple(x.reshape(query_in.shape) for x in (attended, grad_query, grad_key, grad_value))
+    return tuple(x.reshape(query_in.shape) for x in results)
 
 
 def solution(mesh):

time: 52.2 us -> 51.7 us (level)
  starting transfers between devices: 29 us -> 30.2 us
  waiting for transfers between devices: 10.8 us -> 9.75 us
  Pallas kernels: 11.4 us -> 10.7 us
    ppermute x12, waiting for transfers between devices: 6.74 us -> 5.49 us  [other_frames(): lax.ppermute(x, 'ta', [(i, i ^ distance) for i in range(sizes['ta'])])]
    ppermute x1 -> x2, starting transfers between devices: 0.28 us -> 1.53 us  [shards(): row_parts.append(lax.ppermute(partial_sum, 'ha', pairs))]
    pallas_call x7 -> x6, Pallas kernels: 11.4 us -> 10.7 us  [call(): pl.pallas_call(kernel, out_shape=out_shape, in_specs=[pl.BlockSpec(memory...]
  transfers between devices with their start and end apart: 20 -> 21, of which waited for: 7 -> 8; matrix products, arithmetic and copies ran while one was open for 0% -> 0% of each run, Pallas kernels for 18% -> 16%
where the time goes in v17:
time: 51.7 us; the launch traced here: 51.5 us
  starting transfers between devices  30.2 us (58%)
  Pallas kernels  10.7 us (21%)
  waiting for transfers between devices  9.75 us (19%)
  between operations  0.72 us (1%)
    ppermute x12, starting transfers between devices, other_frames(): lax.ppermute(x, 'ta', [(i, i ^ distance) for i in range(sizes['ta'])])  13.5 us
    pallas_call x6, Pallas kernels, call(): pl.pallas_call(kernel, out_shape=out_shape, in_specs=[pl.BlockSpec(memory...  10.7 us
    ppermute x4, starting transfers between devices, shards(): lax.ppermute(block, 'wa', pairs)  8.2 us
    ppermute x12, waiting for transfers between devices, other_frames(): lax.ppermute(x, 'ta', [(i, i ^ distance) for i in range(sizes['ta'])])  5.49 us
    ppermute x2, starting transfers between devices, shards(): sides = [lax.ppermute(x, 'wa', pairs) for x, pairs in zip(sides, col_sides)]  4.87 us
    ppermute x4, waiting for transfers between devices, shards(): lax.ppermute(block, 'wa', pairs)  2.4 us
    ppermute x1, starting transfers between devices, shards(): kv_rows = [kv] + [lax.ppermute(kv, 'ha', pairs) for pairs in row_sides]  2.11 us
    ppermute x2, waiting for transfers between devices, shards(): sides = [lax.ppermute(x, 'wa', pairs) for x, pairs in zip(sides, col_sides)]  1.64 us
  transfers between devices with their start and end apart: 21, of which 8 were waited for; matrix products, arithmetic and copies ran while one was open for 0% of the time, Pallas kernels for 16%

profile of v17, /device:TPU:1, one launch (start us, length us, event | category | flops | bytes accessed | tf_op | source)
XLA Modules:
  0.0 51.5 jit_solution(5073965822972304939)
XLA Ops:
  0.6 1.3 %rotate.1 = (bf16[2,192,256]{2,1,0:T(8,128)(2,1)S(1)}, bf16[2,192,256]{2,1,0:T(8,128)(2,1)S(1)}, f32[3,192,128]{2,1,0:T(8,128)S(1)}) custom-call(bf16[192,256]{1,0:T(8,128)(2,1)} %bitcast.12, bf16[192,256]{1,0:T(8,128)(2,1)} %bitcast.13, bf16[192,256]{1,0:T(8,128)(2,1)} %bitcast.14, bf16[192,256]{1,0:T(8,128)(2,1)} %bitcast.15, ...), custom_call_target="tpu_custom_call" | custom-call | bytes 1179648 | tf_op jit(solution)/shard_map/rotate/pallas_call | solution.py:337
  1.9 2.1 %collective-permute-start.4 = (bf16[2,192,256]{2,1,0:T(8,128)(2,1)S(1)}, bf16[2,192,256]{2,1,0:T(8,128)(2,1)S(1)}, u32[]{:S(2)}, u32[]{:S(2)}) collective-permute-start(bf16[2,192,256]{2,1,0:T(8,128)(2,1)S(1)} %get-tuple-element.38.refs_3_.refs_1_.refs_4_), channel_id=1, source_target_pairs={{0,4},{4,0},{1,5},{5,1},{2,6},{6,2},{3,7},{7,3},{8,12},{12,8},{9,1... | collective-permute-start | bytes 589832 | tf_op jit(solution)/shard_map/halo/ppermute | solution.py:379
  4.0 2.3 %collective-permute-start.1 = (bf16[2,192,256]{2,1,0:T(8,128)(2,1)S(1)}, bf16[2,192,256]{2,1,0:T(8,128)(2,1)S(1)}, u32[]{:S(2)}, u32[]{:S(2)}) collective-permute-start(bf16[2,192,256]{2,1,0:T(8,128)(2,1)S(1)} %get-tuple-element.37.refs_0_), channel_id=1, source_target_pairs={{0,16},{8,24},{16,0},{24,8},{1,17},{9,25},{17,1},{25,9},{2,18},{10... | collective-permute-start | bytes 589832 | tf_op jit(solution)/shard_map/halo/ppermute | solution.py:374
  6.3 1.3 %collective-permute-start = (bf16[2,192,256]{2,1,0:T(8,128)(2,1)S(1)}, bf16[2,192,256]{2,1,0:T(8,128)(2,1)S(1)}, u32[]{:S(2)}, u32[]{:S(2)}) collective-permute-start(bf16[2,192,256]{2,1,0:T(8,128)(2,1)S(1)} %get-tuple-element.37.refs_0_), channel_id=1, source_target_pairs={{0,8},{8,0},{16,24},{24,16},{1,9},{9,1},{17,25},{25,17},{2,10},{10... | collective-permute-start | bytes 589832 | tf_op jit(solution)/shard_map/halo/ppermute | solution.py:374
  7.6 4.5 %collective-permute-start.3 = (bf16[2,192,256]{2,1,0:T(8,128)(2,1)S(1)}, bf16[2,192,256]{2,1,0:T(8,128)(2,1)S(1)}, u32[]{:S(2)}, u32[]{:S(2)}) collective-permute-start(bf16[2,192,256]{2,1,0:T(8,128)(2,1)S(1)} %get-tuple-element.38.refs_3_.refs_1_.refs_4_), channel_id=1, source_target_pairs={{0,0},{1,2},{2,1},{3,3},{4,4},{5,6},{6,5},{7,7},{8,8},{9,10},{10,9... | collective-permute-start | bytes 589832 | tf_op jit(solution)/shard_map/halo/ppermute | solution.py:384
  12.2 0.1 collective-permute-start.2
  12.2 0.0 collective-permute-done.4.refs_6_.refs_4_.refs_5_
  12.2 1.9 %collective-permute-start.6 = (bf16[2,192,256]{2,1,0:T(8,128)(2,1)S(1)}, bf16[2,192,256]{2,1,0:T(8,128)(2,1)S(1)}, u32[]{:S(2)}, u32[]{:S(2)}) collective-permute-start(bf16[2,192,256]{2,1,0:T(8,128)(2,1)S(1)} %collective-permute-done.4.refs_6_.refs_4_.refs_5_), channel_id=1, source_target_pairs={{0,0},{1,2},{2,1},{3,3},{4,4},{5,6},{6,5},{7,7},{8,8},{9,10},{10,9... | collective-permute-start | bytes 589832 | tf_op jit(solution)/shard_map/halo/ppermute | solution.py:384
  14.2 0.7 %collective-permute-done.1.refs_2_ = bf16[2,192,256]{2,1,0:T(8,128)(2,1)S(1)} collective-permute-done((bf16[2,192,256]{2,1,0:T(8,128)(2,1)S(1)}, bf16[2,192,256]{2,1,0:T(8,128)(2,1)S(1)}, u32[]{:S(2)}, u32[]{:S(2)}) %collective-permute-start.1) | collective-permute-done | bytes 196640 | tf_op jit(solution)/shard_map/halo/ppermute | solution.py:374
  14.9 1.7 %collective-permute-start.5 = (bf16[2,192,256]{2,1,0:T(8,128)(2,1)S(1)}, bf16[2,192,256]{2,1,0:T(8,128)(2,1)S(1)}, u32[]{:S(2)}, u32[]{:S(2)}) collective-permute-start(bf16[2,192,256]{2,1,0:T(8,128)(2,1)S(1)} %collective-permute-done.4.refs_6_.refs_4_.refs_5_), channel_id=1, source_target_pairs={{0,1},{1,0},{2,3},{3,2},{4,5},{5,4},{6,7},{7,6},{8,9},{9,8},{10,11... | collective-permute-start | bytes 589832 | tf_op jit(solution)/shard_map/halo/ppermute | solution.py:384
  16.5 0.0 collective-permute-done.refs_1_
  16.5 0.3 collective-permute-start.7
  16.8 0.0 collective-permute-done.3.refs_5_.refs_3_.refs_6_
  16.8 0.0 collective-permute-done.2.refs_4_.refs_2_
  16.8 2.4 %collective-permute-done.6.refs_8_.refs_6_.refs_7_ = bf16[2,192,256]{2,1,0:T(8,128)(2,1)S(1)} collective-permute-done((bf16[2,192,256]{2,1,0:T(8,128)(2,1)S(1)}, bf16[2,192,256]{2,1,0:T(8,128)(2,1)S(1)}, u32[]{:S(2)}, u32[]{:S(2)}) %collective-permute-start.6) | collective-permute-done | bytes 196640 | tf_op jit(solution)/shard_map/halo/ppermute | solution.py:384
  19.2 0.0 collective-permute-done.5.refs_7_.refs_5_
  19.2 2.4 %attend.2 = (bf16[192,256]{1,0:T(8,128)(2,1)S(1)}, bf16[192,256]{1,0:T(8,128)(2,1)S(1)}, bf16[192,256]{1,0:T(8,128)(2,1)S(1)}, f32[576,128]{1,0:T(8,128)S(1)}) custom-call(bf16[2,192,256]{2,1,0:T(8,128)(2,1)S(1)} %get-tuple-element.37.refs_0_, bf16[2,192,256]{2,1,0:T(8,128)(2,1)S(1)} %collective-permute-done.refs_1_, ...), custom_call_target="tpu_custom_call" | custom-call | flops 5435817984 | bytes 2359296 | tf_op jit(solution)/shard_map/attend/pallas_call | solution.py:337
  21.7 0.8 %collective-permute-start.8 = (bf16[192,256]{1,0:T(8,128)(2,1)S(1)}, bf16[192,256]{1,0:T(8,128)(2,1)S(1)}, u32[]{:S(2)}, u32[]{:S(2)}) collective-permute-start(bf16[192,256]{1,0:T(8,128)(2,1)S(1)} %get-tuple-element.42), channel_id=1, source_target_pairs={{0,16},{8,24},{16,0},{24,8},{1,17},{9,25},{17,1},{25,9},{2,18},{10... | collective-permute-start | bytes 294920 | tf_op jit(solution)/shard_map/merge/ppermute | solution.py:374
  22.4 1.0 %collective-permute-start.9 = (bf16[192,256]{1,0:T(8,128)(2,1)S(1)}, bf16[192,256]{1,0:T(8,128)(2,1)S(1)}, u32[]{:S(2)}, u32[]{:S(2)}) collective-permute-start(bf16[192,256]{1,0:T(8,128)(2,1)S(1)} %get-tuple-element.43), channel_id=1, source_target_pairs={{0,8},{8,0},{16,24},{24,16},{1,9},{9,1},{17,25},{25,17},{2,10},{10... | collective-permute-start | bytes 294920 | tf_op jit(solution)/shard_map/merge/ppermute | solution.py:374
  23.5 0.0 collective-permute-done.7.refs_0_.refs_3_
  23.5 1.0 %attend.3 = (bf16[192,256]{1,0:T(8,128)(2,1)S(1)}, f32[8,768]{1,0:T(8,128)S(1)}) custom-call(bf16[2,192,256]{2,1,0:T(8,128)(2,1)S(1)} %collective-permute-done.7.refs_0_.refs_3_, bf16[2,192,256]{2,1,0:T(8,128)(2,1)S(1)} %get-tuple-element.38.refs_3_.refs_1_.refs_4_, bf16[2,192,256]{2,1,0:T(8,128)(2,1)S(1)} %collective-permute-done.2.refs_4_.refs_2_, ...), custom_call_target="tpu_custom_call" | custom-call | flops 1811939328 | bytes 1794048 | tf_op jit(solution)/shard_map/attend/pallas_call | solution.py:337
  24.5 1.7 %collective-permute-start.12 = (f32[8,768]{1,0:T(8,128)S(1)}, f32[8,768]{1,0:T(8,128)S(1)}, u32[]{:S(2)}, u32[]{:S(2)}) collective-permute-start(f32[8,768]{1,0:T(8,128)S(1)} %get-tuple-element.44.refs_8_), channel_id=1, source_target_pairs={{0,16},{8,24},{16,0},{24,8},{1,17},{9,25},{17,1},{25,9},{2,18},{10... | collective-permute-start | bytes 73736 | tf_op jit(solution)/shard_map/merge/ppermute | solution.py:374
  26.3 1.1 %collective-permute-start.11 = (f32[8,768]{1,0:T(8,128)S(1)}, f32[8,768]{1,0:T(8,128)S(1)}, u32[]{:S(2)}, u32[]{:S(2)}) collective-permute-start(f32[8,768]{1,0:T(8,128)S(1)} %get-tuple-element.44.refs_8_), channel_id=1, source_target_pairs={{0,24},{8,16},{16,8},{24,0},{1,25},{9,17},{17,9},{25,1},{2,26},{10... | collective-permute-start | bytes 73736 | tf_op jit(solution)/shard_map/merge/ppermute | solution.py:374
  27.3 1.4 %collective-permute-done.8.refs_2_ = bf16[192,256]{1,0:T(8,128)(2,1)S(1)} collective-permute-done((bf16[192,256]{1,0:T(8,128)(2,1)S(1)}, bf16[192,256]{1,0:T(8,128)(2,1)S(1)}, u32[]{:S(2)}, u32[]{:S(2)}) %collective-permute-start.8) | collective-permute-done | bytes 98336 | tf_op jit(solution)/shard_map/merge/ppermute | solution.py:374
  28.7 0.0 collective-permute-done.9.refs_3_
  28.7 0.0 collective-permute-start.10
  28.7 2.1 %collective-permute-start.13 = (bf16[192,256]{1,0:T(8,128)(2,1)S(1)}, bf16[192,256]{1,0:T(8,128)(2,1)S(1)}, u32[]{:S(2)}, u32[]{:S(2)}) collective-permute-start(bf16[192,256]{1,0:T(8,128)(2,1)S(1)} %get-tuple-element.51), channel_id=1, source_target_pairs={{0,24},{8,16},{16,8},{24,0},{1,25},{9,17},{17,9},{25,1},{2,26},{10... | collective-permute-start | bytes 294920 | tf_op jit(solution)/shard_map/merge/ppermute | solution.py:374
  30.8 0.0 collective-permute-done.12.refs_11_
  30.8 0.0 collective-permute-done.11.refs_10_
  30.8 0.6 %collective-permute-done.10.refs_9_ = f32[8,768]{1,0:T(8,128)S(1)} collective-permute-done((f32[8,768]{1,0:T(8,128)S(1)}, f32[8,768]{1,0:T(8,128)S(1)}, u32[]{:S(2)}, u32[]{:S(2)}) %collective-permute-start.10) | collective-permute-done | bytes 24608 | tf_op jit(solution)/shard_map/merge/ppermute | solution.py:374
  31.4 3.1 %gradients.2 = (f32[2,128,768]{2,1,0:T(8,128)S(1)}, f32[2,768]{1,0:T(2,128)S(1)}, f32[2,768]{1,0:T(2,128)S(1)}, f32[192,128]{1,0:T(8,128)S(1)}, bf16[2,2,192,256...) custom-call(bf16[2,192,256]{2,1,0:T(8,128)(2,1)S(1)} %get-tuple-element.37.refs_0_, ...), custom_call_target="tpu_custom_call" | custom-call | flops 12079595520 | bytes 3354624 | tf_op jit(solution)/shard_map/gradients/pallas_call | solution.py:337
  34.5 1.8 %collective-permute-start.17 = (bf16[2,2,192,256]{3,2,1,0:T(8,128)(2,1)S(1)}, bf16[2,2,192,256]{3,2,1,0:T(8,128)(2,1)S(1)}, u32[]{:S(2)}, u32[]{:S(2)}) collective-permute-start(bf16[2,2,192,256]{3,2,1,0:T(8,128)(2,1)S(1)} %get-tuple-element.62), channel_id=1, source_target_pairs={{0,1},{1,0},{2,3},{3,2},{4,5},{5,4},{6,7},{7,6},{8,9},{9,8},{10,11... | collective-permute-start | bytes 1179656 | tf_op jit(solution)/shard_map/gradients/ppermute | solution.py:439
  36.2 3.1 %collective-permute-start.18 = (bf16[2,2,192,256]{3,2,1,0:T(8,128)(2,1)S(1)}, bf16[2,2,192,256]{3,2,1,0:T(8,128)(2,1)S(1)}, u32[]{:S(2)}, u32[]{:S(2)}) collective-permute-start(bf16[2,2,192,256]{3,2,1,0:T(8,128)(2,1)S(1)} %get-tuple-element.63), channel_id=1, source_target_pairs={{0,0},{1,2},{2,1},{3,3},{4,4},{5,6},{6,5},{7,7},{8,8},{9,10},{10,9... | collective-permute-start | bytes 1179656 | tf_op jit(solution)/shard_map/gradients/ppermute | solution.py:439
  39.4 1.7 %gradients.3 = (bf16[192,256]{1,0:T(8,128)(2,1)S(1)}, bf16[192,256]{1,0:T(8,128)(2,1)S(1)}, bf16[192,256]{1,0:T(8,128)(2,1)S(1)}, bf16[192,256]{1,0:T(8,128)(2,1)S(1)}, bf16[2,2,192,256]{3,2,1,0:T(8,128)(2,1)S(1)}) custom-call(bf16[2,192,256]{2,1,0:T(8,128)(2,1)S(1)} %get-tuple-element.37.refs_0_, bf16[2,192,256]{2,1,0:T(8,128)(2,1)S(1)} %collective-permute-done.refs_1_, ...), custom_call_target="tpu_custom_call" | custom-call | flops 6039797760 | bytes 2764800 | tf_op jit(solution)/shard_map/gradients/pallas_call | solution.py:337
  41.0 0.0 collective-permute-done.13.refs_1_
  41.0 1.6 %collective-permute-start.14 = (bf16[192,256]{1,0:T(8,128)(2,1)S(1)}, bf16[192,256]{1,0:T(8,128)(2,1)S(1)}, u32[]{:S(2)}, u32[]{:S(2)}) collective-permute-start(bf16[192,256]{1,0:T(8,128)(2,1)S(1)} %get-tuple-element.58), channel_id=1, source_target_pairs={{0,16},{8,24},{16,0},{24,8},{1,17},{9,25},{17,1},{25,9},{2,18},{10... | collective-permute-start | bytes 294920 | tf_op jit(solution)/shard_map/return/ppermute | solution.py:374
  42.7 1.3 %collective-permute-start.15 = (bf16[192,256]{1,0:T(8,128)(2,1)S(1)}, bf16[192,256]{1,0:T(8,128)(2,1)S(1)}, u32[]{:S(2)}, u32[]{:S(2)}) collective-permute-start(bf16[192,256]{1,0:T(8,128)(2,1)S(1)} %get-tuple-element.59), channel_id=1, source_target_pairs={{0,24},{8,16},{16,8},{24,0},{1,25},{9,17},{17,9},{25,1},{2,26},{10... | collective-permute-start | bytes 294920 | tf_op jit(solution)/shard_map/return/ppermute | solution.py:374
  44.0 0.0 collective-permute-start.16
  44.0 0.0 collective-permute-done.17.refs_9_
  44.0 1.6 %collective-permute-done.18.refs_10_ = bf16[2,2,192,256]{3,2,1,0:T(8,128)(2,1)S(1)} collective-permute-done((bf16[2,2,192,256]{3,2,1,0:T(8,128)(2,1)S(1)}, bf16[2,2,192,256]{3,2,1,0:T(8,128)(2,1)S(1)}, u32[]{:S(2)}, u32[]{:S(2)}) %collective-permute-start.18) | collective-permute-done | bytes 393248 | tf_op jit(solution)/shard_map/gradients/ppermute | solution.py:439
  45.6 0.1 fusion.1
  45.7 0.3 collective-permute-start.20
  46.0 1.2 %collective-permute-start.19 = (bf16[192,256]{1,0:T(8,128)(2,1)S(1)}, bf16[192,256]{1,0:T(8,128)(2,1)S(1)}, u32[]{:S(2)}, u32[]{:S(2)}) collective-permute-start(bf16[192,256]{1,0:T(8,128)(2,1)S(1)} %get-tuple-element.71), channel_id=1, source_target_pairs={{0,4},{4,0},{1,5},{5,1},{2,6},{6,2},{3,7},{7,3},{8,12},{12,8},{9,1... | collective-permute-start | bytes 294920 | tf_op jit(solution)/shard_map/return/ppermute | solution.py:449
  47.2 2.5 %collective-permute-done.14.refs_5_ = bf16[192,256]{1,0:T(8,128)(2,1)S(1)} collective-permute-done((bf16[192,256]{1,0:T(8,128)(2,1)S(1)}, bf16[192,256]{1,0:T(8,128)(2,1)S(1)}, u32[]{:S(2)}, u32[]{:S(2)}) %collective-permute-start.14) | collective-permute-done | bytes 98336 | tf_op jit(solution)/shard_map/return/ppermute | solution.py:374
  49.8 0.0 collective-permute-done.15.refs_6_
  49.8 0.3 collective-permute-done.16.refs_7_
  50.1 0.0 collective-permute-done.20.refs_12_
  50.1 0.2 collective-permute-done.19.refs_11_
  50.3 1.2 %finish.1 = (bf16[192,256]{1,0:T(8,128)(2,1)}, bf16[192,256]{1,0:T(8,128)(2,1)}, bf16[192,256]{1,0:T(8,128)(2,1)}, bf16[192,256]{1,0:T(8,128)(2,1)}) custom-call(bf16[192,256]{1,0:T(8,128)(2,1)S(1)} %get-tuple-element.39.refs_0_, bf16[192,256]{1,0:T(8,128)(2,1)S(1)} %collective-permute-done.13.refs_1_, bf16[192,256]{1,0:T(8,128)(2,1)S(1)} %collective-permute-done.8.refs_2_, ...), custom_call_target="tpu_custom_call" | custom-call | bytes 2949120 | tf_op jit(solution)/shard_map/finish/pallas_call | solution.py:337
Async XLA Ops:
  1.9 10.3 %collective-permute-start.4 = (bf16[2,192,256]{2,1,0:T(8,128)(2,1)S(1)}, bf16[2,192,256]{2,1,0:T(8,128)(2,1)S(1)}, u32[]{:S(2)}, u32[]{:S(2)}) collective-permute-start(bf16[2,192,256]{2,1,0:T(8,128)(2,1)S(1)} %get-tuple-element.38.refs_3_.refs_1_.refs_4_), channel_id=1, source_target_pairs={{0,4},{4,0},{1,5},{5,1},{2,6},{6,2},{3,7},{7,3},{8,12},{12,8},{9,1... | collective-permute-start | bytes 589832 | tf_op jit(solution)/shard_map/halo/ppermute | solution.py:379
  4.0 10.9 %collective-permute-start.1 = (bf16[2,192,256]{2,1,0:T(8,128)(2,1)S(1)}, bf16[2,192,256]{2,1,0:T(8,128)(2,1)S(1)}, u32[]{:S(2)}, u32[]{:S(2)}) collective-permute-start(bf16[2,192,256]{2,1,0:T(8,128)(2,1)S(1)} %get-tuple-element.37.refs_0_), channel_id=1, source_target_pairs={{0,16},{8,24},{16,0},{24,8},{1,17},{9,25},{17,1},{25,9},{2,18},{10... | collective-permute-start | bytes 589832 | tf_op jit(solution)/shard_map/halo/ppermute | solution.py:374
  6.3 10.2 %collective-permute-start = (bf16[2,192,256]{2,1,0:T(8,128)(2,1)S(1)}, bf16[2,192,256]{2,1,0:T(8,128)(2,1)S(1)}, u32[]{:S(2)}, u32[]{:S(2)}) collective-permute-start(bf16[2,192,256]{2,1,0:T(8,128)(2,1)S(1)} %get-tuple-element.37.refs_0_), channel_id=1, source_target_pairs={{0,8},{8,0},{16,24},{24,16},{1,9},{9,1},{17,25},{25,17},{2,10},{10... | collective-permute-start | bytes 589832 | tf_op jit(solution)/shard_map/halo/ppermute | solution.py:374
  7.6 9.2 %collective-permute-start.3 = (bf16[2,192,256]{2,1,0:T(8,128)(2,1)S(1)}, bf16[2,192,256]{2,1,0:T(8,128)(2,1)S(1)}, u32[]{:S(2)}, u32[]{:S(2)}) collective-permute-start(bf16[2,192,256]{2,1,0:T(8,128)(2,1)S(1)} %get-tuple-element.38.refs_3_.refs_1_.refs_4_), channel_id=1, source_target_pairs={{0,0},{1,2},{2,1},{3,3},{4,4},{5,6},{6,5},{7,7},{8,8},{9,10},{10,9... | collective-permute-start | bytes 589832 | tf_op jit(solution)/shard_map/halo/ppermute | solution.py:384
  12.2 4.7 %collective-permute-start.2 = (bf16[2,192,256]{2,1,0:T(8,128)(2,1)S(1)}, bf16[2,192,256]{2,1,0:T(8,128)(2,1)S(1)}, u32[]{:S(2)}, u32[]{:S(2)}) collective-permute-start(bf16[2,192,256]{2,1,0:T(8,128)(2,1)S(1)} %get-tuple-element.38.refs_3_.refs_1_.refs_4_), channel_id=1, source_target_pairs={{0,1},{1,0},{2,3},{3,2},{4,5},{5,4},{6,7},{7,6},{8,9},{9,8},{10,11... | collective-permute-start | bytes 589832 | tf_op jit(solution)/shard_map/halo/ppermute | solution.py:384
  12.2 7.0 %collective-permute-start.6 = (bf16[2,192,256]{2,1,0:T(8,128)(2,1)S(1)}, bf16[2,192,256]{2,1,0:T(8,128)(2,1)S(1)}, u32[]{:S(2)}, u32[]{:S(2)}) collective-permute-start(bf16[2,192,256]{2,1,0:T(8,128)(2,1)S(1)} %collective-permute-done.4.refs_6_.refs_4_.refs_5_), channel_id=1, source_target_pairs={{0,0},{1,2},{2,1},{3,3},{4,4},{5,6},{6,5},{7,7},{8,8},{9,10},{10,9... | collective-permute-start | bytes 589832 | tf_op jit(solution)/shard_map/halo/ppermute | solution.py:384
  14.9 4.4 %collective-permute-start.5 = (bf16[2,192,256]{2,1,0:T(8,128)(2,1)S(1)}, bf16[2,192,256]{2,1,0:T(8,128)(2,1)S(1)}, u32[]{:S(2)}, u32[]{:S(2)}) collective-permute-start(bf16[2,192,256]{2,1,0:T(8,128)(2,1)S(1)} %collective-permute-done.4.refs_6_.refs_4_.refs_5_), channel_id=1, source_target_pairs={{0,1},{1,0},{2,3},{3,2},{4,5},{5,4},{6,7},{7,6},{8,9},{9,8},{10,11... | collective-permute-start | bytes 589832 | tf_op jit(solution)/shard_map/halo/ppermute | solution.py:384
  16.5 7.0 %collective-permute-start.7 = (bf16[2,192,256]{2,1,0:T(8,128)(2,1)S(1)}, bf16[2,192,256]{2,1,0:T(8,128)(2,1)S(1)}, u32[]{:S(2)}, u32[]{:S(2)}) collective-permute-start(bf16[2,192,256]{2,1,0:T(8,128)(2,1)S(1)} %collective-permute-done.1.refs_2_), channel_id=1, source_target_pairs={{0,8},{8,0},{16,24},{24,16},{1,9},{9,1},{17,25},{25,17},{2,10},{10... | collective-permute-start | bytes 589832 | tf_op jit(solution)/shard_map/halo/ppermute | solution.py:374
  21.7 7.0 %collective-permute-start.8 = (bf16[192,256]{1,0:T(8,128)(2,1)S(1)}, bf16[192,256]{1,0:T(8,128)(2,1)S(1)}, u32[]{:S(2)}, u32[]{:S(2)}) collective-permute-start(bf16[192,256]{1,0:T(8,128)(2,1)S(1)} %get-tuple-element.42), channel_id=1, source_target_pairs={{0,16},{8,24},{16,0},{24,8},{1,17},{9,25},{17,1},{25,9},{2,18},{10... | collective-permute-start | bytes 294920 | tf_op jit(solution)/shard_map/merge/ppermute | solution.py:374
  22.4 6.2 %collective-permute-start.9 = (bf16[192,256]{1,0:T(8,128)(2,1)S(1)}, bf16[192,256]{1,0:T(8,128)(2,1)S(1)}, u32[]{:S(2)}, u32[]{:S(2)}) collective-permute-start(bf16[192,256]{1,0:T(8,128)(2,1)S(1)} %get-tuple-element.43), channel_id=1, source_target_pairs={{0,8},{8,0},{16,24},{24,16},{1,9},{9,1},{17,25},{25,17},{2,10},{10... | collective-permute-start | bytes 294920 | tf_op jit(solution)/shard_map/merge/ppermute | solution.py:374
  24.5 6.3 %collective-permute-start.12 = (f32[8,768]{1,0:T(8,128)S(1)}, f32[8,768]{1,0:T(8,128)S(1)}, u32[]{:S(2)}, u32[]{:S(2)}) collective-permute-start(f32[8,768]{1,0:T(8,128)S(1)} %get-tuple-element.44.refs_8_), channel_id=1, source_target_pairs={{0,16},{8,24},{16,0},{24,8},{1,17},{9,25},{17,1},{25,9},{2,18},{10... | collective-permute-start | bytes 73736 | tf_op jit(solution)/shard_map/merge/ppermute | solution.py:374
  26.3 4.5 %collective-permute-start.11 = (f32[8,768]{1,0:T(8,128)S(1)}, f32[8,768]{1,0:T(8,128)S(1)}, u32[]{:S(2)}, u32[]{:S(2)}) collective-permute-start(f32[8,768]{1,0:T(8,128)S(1)} %get-tuple-element.44.refs_8_), channel_id=1, source_target_pairs={{0,24},{8,16},{16,8},{24,0},{1,25},{9,17},{17,9},{25,1},{2,26},{10... | collective-permute-start | bytes 73736 | tf_op jit(solution)/shard_map/merge/ppermute | solution.py:374
  28.7 2.7 %collective-permute-start.10 = (f32[8,768]{1,0:T(8,128)S(1)}, f32[8,768]{1,0:T(8,128)S(1)}, u32[]{:S(2)}, u32[]{:S(2)}) collective-permute-start(f32[8,768]{1,0:T(8,128)S(1)} %get-tuple-element.44.refs_8_), channel_id=1, source_target_pairs={{0,8},{8,0},{16,24},{24,16},{1,9},{9,1},{17,25},{25,17},{2,10},{10... | collective-permute-start | bytes 73736 | tf_op jit(solution)/shard_map/merge/ppermute | solution.py:374
  28.7 12.3 %collective-permute-start.13 = (bf16[192,256]{1,0:T(8,128)(2,1)S(1)}, bf16[192,256]{1,0:T(8,128)(2,1)S(1)}, u32[]{:S(2)}, u32[]{:S(2)}) collective-permute-start(bf16[192,256]{1,0:T(8,128)(2,1)S(1)} %get-tuple-element.51), channel_id=1, source_target_pairs={{0,24},{8,16},{16,8},{24,0},{1,25},{9,17},{17,9},{25,1},{2,26},{10... | collective-permute-start | bytes 294920 | tf_op jit(solution)/shard_map/merge/ppermute | solution.py:374
  34.5 9.5 %collective-permute-start.17 = (bf16[2,2,192,256]{3,2,1,0:T(8,128)(2,1)S(1)}, bf16[2,2,192,256]{3,2,1,0:T(8,128)(2,1)S(1)}, u32[]{:S(2)}, u32[]{:S(2)}) collective-permute-start(bf16[2,2,192,256]{3,2,1,0:T(8,128)(2,1)S(1)} %get-tuple-element.62), channel_id=1, source_target_pairs={{0,1},{1,0},{2,3},{3,2},{4,5},{5,4},{6,7},{7,6},{8,9},{9,8},{10,11... | collective-permute-start | bytes 1179656 | tf_op jit(solution)/shard_map/gradients/ppermute | solution.py:439
  36.2 9.4 %collective-permute-start.18 = (bf16[2,2,192,256]{3,2,1,0:T(8,128)(2,1)S(1)}, bf16[2,2,192,256]{3,2,1,0:T(8,128)(2,1)S(1)}, u32[]{:S(2)}, u32[]{:S(2)}) collective-permute-start(bf16[2,2,192,256]{3,2,1,0:T(8,128)(2,1)S(1)} %get-tuple-element.63), channel_id=1, source_target_pairs={{0,0},{1,2},{2,1},{3,3},{4,4},{5,6},{6,5},{7,7},{8,8},{9,10},{10,9... | collective-permute-start | bytes 1179656 | tf_op jit(solution)/shard_map/gradients/ppermute | solution.py:439
  41.0 8.7 %collective-permute-start.14 = (bf16[192,256]{1,0:T(8,128)(2,1)S(1)}, bf16[192,256]{1,0:T(8,128)(2,1)S(1)}, u32[]{:S(2)}, u32[]{:S(2)}) collective-permute-start(bf16[192,256]{1,0:T(8,128)(2,1)S(1)} %get-tuple-element.58), channel_id=1, source_target_pairs={{0,16},{8,24},{16,0},{24,8},{1,17},{9,25},{17,1},{25,9},{2,18},{10... | collective-permute-start | bytes 294920 | tf_op jit(solution)/shard_map/return/ppermute | solution.py:374
  42.7 7.1 %collective-permute-start.15 = (bf16[192,256]{1,0:T(8,128)(2,1)S(1)}, bf16[192,256]{1,0:T(8,128)(2,1)S(1)}, u32[]{:S(2)}, u32[]{:S(2)}) collective-permute-start(bf16[192,256]{1,0:T(8,128)(2,1)S(1)} %get-tuple-element.59), channel_id=1, source_target_pairs={{0,24},{8,16},{16,8},{24,0},{1,25},{9,17},{17,9},{25,1},{2,26},{10... | collective-permute-start | bytes 294920 | tf_op jit(solution)/shard_map/return/ppermute | solution.py:374
  44.0 6.1 %collective-permute-start.16 = (bf16[192,256]{1,0:T(8,128)(2,1)S(1)}, bf16[192,256]{1,0:T(8,128)(2,1)S(1)}, u32[]{:S(2)}, u32[]{:S(2)}) collective-permute-start(bf16[192,256]{1,0:T(8,128)(2,1)S(1)} %get-tuple-element.60), channel_id=1, source_target_pairs={{0,8},{8,0},{16,24},{24,16},{1,9},{9,1},{17,25},{25,17},{2,10},{10... | collective-permute-start | bytes 294920 | tf_op jit(solution)/shard_map/return/ppermute | solution.py:374
  45.7 4.4 %collective-permute-start.20 = (bf16[192,256]{1,0:T(8,128)(2,1)S(1)}, bf16[192,256]{1,0:T(8,128)(2,1)S(1)}, u32[]{:S(2)}, u32[]{:S(2)}) collective-permute-start(bf16[192,256]{1,0:T(8,128)(2,1)S(1)} %get-tuple-element.70), channel_id=1, source_target_pairs={{0,4},{4,0},{1,5},{5,1},{2,6},{6,2},{3,7},{7,3},{8,12},{12,8},{9,1... | collective-permute-start | bytes 294920 | tf_op jit(solution)/shard_map/return/ppermute | solution.py:449
  46.0 4.3 %collective-permute-start.19 = (bf16[192,256]{1,0:T(8,128)(2,1)S(1)}, bf16[192,256]{1,0:T(8,128)(2,1)S(1)}, u32[]{:S(2)}, u32[]{:S(2)}) collective-permute-start(bf16[192,256]{1,0:T(8,128)(2,1)S(1)} %get-tuple-element.71), channel_id=1, source_target_pairs={{0,4},{4,0},{1,5},{5,1},{2,6},{6,2},{3,7},{7,3},{8,12},{12,8},{9,1... | collective-permute-start | bytes 294920 | tf_op jit(solution)/shard_map/return/ppermute | solution.py:449

commit v18 on v17

--- a/solution.py
+++ b/solution.py
@@ -273,7 +273,7 @@
         raw = dot_nt(key_buf[at, cut], queries)
         return raw, dot_nt(value_buf[at, cut], grads), queries, grads
 
-    dqs = [None] * HEADS
+    dscores = [[] for _ in range(HEADS)]
     ahead = products_of(*blocks[0])
     for i, (head, slot) in enumerate(blocks):
         raw, prob_grad, queries, grads = ahead
@@ -294,11 +294,11 @@
             at = slice(row * cells, (row + 1) * cells)
             col_refs[slot][row, 0, :, cut] = dk[at]
             col_refs[slot][row, 1, :, cut] = dv[at]
-        part = dot_nn(key_buf[slot * span : (slot + 1) * span, cut].T, dscore)
-        dqs[head] = part if dqs[head] is None else dqs[head] + part
+        dscores[head].append(dscore)
     for head in range(HEADS):
         cut = head_slice(head)
-        dq = dqs[head] if first else dqs[head] + dq_ref[head]
+        dq = dot_nn(key_buf[:, cut].T, jnp.concatenate(dscores[head], axis=0))
+        dq = dq if first else dq + dq_ref[head]
         if last:
             dq = (dq * SCALE).T.astype(BF16)
             for i, ref in enumerate(dq_outs):
@@ -310,27 +310,43 @@
 def finish_kernel(cols, rows, *refs):
     o_refs, dq_refs, refs = refs[:4], refs[4:8], refs[8:]
     col_refs, row_refs = refs[:cols], refs[cols : cols + 2 * rows]
-    share_ref, rope_ref, out_ref, dq_out, dk_out, dv_out = refs[cols + 2 * rows :]
+    share_ref, rope_ref, *outs, made_ref, sems = refs[cols + 2 * rows :]
+    copies = [
+        pltpu.make_async_copy(made_ref.at[i], out, sems.at[i]) for i, out in enumerate(outs)
+    ]
     tables = [rope_ref[plane] for plane in range(3)]
-    for head in range(HEADS):
-        cut = head_slice(head)
-        outs = []
+    cuts = [head_slice(head) for head in range(HEADS)]
+
+    def summed(parts):
+        return functools.reduce(jnp.add, [part.astype(F32) for part in parts])
+
+    def returned(which, cut):
+        return summed(
+            [ref[0, which, :, cut] for ref in col_refs] + [ref[:, cut] for ref in row_refs[which::2]]
+        )
+
+    for head, cut in enumerate(cuts):
+        weighted = []
         for d, o_ref in zip((0, 3, 2, 1), o_refs):
             weight = share_ref[:, 4 * head + d : 4 * head + d + 1]
-            outs.append(o_ref[:, cut].astype(F32) * weight)
-        out_ref[:, cut] = functools.reduce(jnp.add, outs).astype(BF16)
-        dq = functools.reduce(jnp.add, [ref[:, cut].astype(F32) for ref in dq_refs])
-        dq_out[:, cut] = turn(dq, *tables, -1.0).astype(BF16)
-        sums = []
-        for which in range(2):
-            terms = [ref[0, which, :, cut].astype(F32) for ref in col_refs]
-            terms += [ref[:, cut].astype(F32) for ref in row_refs[which::2]]
-            sums.append(functools.reduce(jnp.add, terms))
-        dk_out[:, cut] = turn(sums[0], *tables, -1.0).astype(BF16)
-        dv_out[:, cut] = sums[1].astype(BF16)
-
-
-def call(kernel, out_shape, args, flops=0, exps=0, scratch=(), space=pltpu.VMEM, limit=VMEM_LIMIT):
+            weighted.append(o_ref[:, cut].astype(F32) * weight)
+        made_ref[0, :, cut] = functools.reduce(jnp.add, weighted).astype(BF16)
+    copies[0].start()
+    for cut in cuts:
+        made_ref[3, :, cut] = returned(1, cut).astype(BF16)
+    copies[3].start()
+    for cut in cuts:
+        dq = summed([ref[:, cut] for ref in dq_refs])
+        made_ref[1, :, cut] = turn(dq, *tables, -1.0).astype(BF16)
+    copies[1].start()
+    for cut in cuts:
+        made_ref[2, :, cut] = turn(returned(0, cut), *tables, -1.0).astype(BF16)
+    copies[2].start()
+    for copy in copies:
+        copy.wait()
+
+
+def call(kernel, out_shape, args, flops=0, exps=0, scratch=(), space=pltpu.VMEM, out_space=pltpu.VMEM):
     shapes = jax.tree.leaves(out_shape)
     flops *= 8
     moved = sum(math.prod(x.shape) * x.dtype.itemsize for x in list(args) + shapes)
@@ -338,8 +354,9 @@
         kernel,
         out_shape=out_shape,
         in_specs=[pl.BlockSpec(memory_space=space)] * len(args),
+        out_specs=jax.tree.map(lambda _: pl.BlockSpec(memory_space=out_space), out_shape),
         scratch_shapes=list(scratch),
-        compiler_params=pltpu.CompilerParams(vmem_limit_bytes=limit),
+        compiler_params=pltpu.CompilerParams(vmem_limit_bytes=VMEM_LIMIT),
         cost_estimate=pl.CostEstimate(flops=flops, bytes_accessed=moved, transcendentals=exps),
     )(*args)
 
@@ -453,6 +470,8 @@
             functools.partial(finish_kernel, grid_cols, len(row_parts) // 2),
             [plain] * 4,
             (o0, *outs, *dqs, *col_parts, *row_parts, shares, rope),
+            scratch=[pltpu.VMEM((4, cells, chan), BF16), pltpu.SemaphoreType.DMA((4,))],
+            out_space=pltpu.HBM,
         )
     return tuple(x.reshape(query_in.shape) for x in results)
 

time: 51.7 us -> 51.5 us (level)
  no operation moved by 1% of the time
where the time goes in v18:
time: 51.5 us; the launch traced here: 51.3 us
  starting transfers between devices  30.2 us (59%)
  Pallas kernels  10.6 us (21%)
  waiting for transfers between devices  9.74 us (19%)
  between operations  0.72 us (1%)
    ppermute x12, starting transfers between devices, other_frames(): lax.ppermute(x, 'ta', [(i, i ^ distance) for i in range(sizes['ta'])])  13.5 us
    pallas_call x6, Pallas kernels, call(): pl.pallas_call(kernel, out_shape=out_shape, in_specs=[pl.BlockSpec(memory...  10.6 us
    ppermute x4, starting transfers between devices, shards(): lax.ppermute(block, 'wa', pairs)  8.2 us
    ppermute x12, waiting for transfers between devices, other_frames(): lax.ppermute(x, 'ta', [(i, i ^ distance) for i in range(sizes['ta'])])  5.48 us
    ppermute x2, starting transfers between devices, shards(): sides = [lax.ppermute(x, 'wa', pairs) for x, pairs in zip(sides, col_sides)]  4.86 us
    ppermute x4, waiting for transfers between devices, shards(): lax.ppermute(block, 'wa', pairs)  2.4 us
    ppermute x1, starting transfers between devices, shards(): kv_rows = [kv] + [lax.ppermute(kv, 'ha', pairs) for pairs in row_sides]  2.11 us
    ppermute x2, waiting for transfers between devices, shards(): sides = [lax.ppermute(x, 'wa', pairs) for x, pairs in zip(sides, col_sides)]  1.63 us
  transfers between devices with their start and end apart: 21, of which 8 were waited for; matrix products, arithmetic and copies ran while one was open for 0% of the time, Pallas kernels for 16%

profile of v18, /device:TPU:1, one launch (start us, length us, event | category | flops | bytes accessed | tf_op | source)
XLA Modules:
  0.0 51.3 jit_solution(17186401144087570252)
XLA Ops:
  0.6 1.3 %rotate.1 = (bf16[2,192,256]{2,1,0:T(8,128)(2,1)S(1)}, bf16[2,192,256]{2,1,0:T(8,128)(2,1)S(1)}, f32[3,192,128]{2,1,0:T(8,128)S(1)}) custom-call(bf16[192,256]{1,0:T(8,128)(2,1)} %bitcast.12, bf16[192,256]{1,0:T(8,128)(2,1)} %bitcast.13, bf16[192,256]{1,0:T(8,128)(2,1)} %bitcast.14, bf16[192,256]{1,0:T(8,128)(2,1)} %bitcast.15, ...), custom_call_target="tpu_custom_call" | custom-call | bytes 1179648 | tf_op jit(solution)/shard_map/rotate/pallas_call | solution.py:353
  1.9 2.1 %collective-permute-start.4 = (bf16[2,192,256]{2,1,0:T(8,128)(2,1)S(1)}, bf16[2,192,256]{2,1,0:T(8,128)(2,1)S(1)}, u32[]{:S(2)}, u32[]{:S(2)}) collective-permute-start(bf16[2,192,256]{2,1,0:T(8,128)(2,1)S(1)} %get-tuple-element.38.refs_3_.refs_1_.refs_4_), channel_id=1, source_target_pairs={{0,4},{4,0},{1,5},{5,1},{2,6},{6,2},{3,7},{7,3},{8,12},{12,8},{9,1... | collective-permute-start | bytes 589832 | tf_op jit(solution)/shard_map/halo/ppermute | solution.py:396
  4.0 2.3 %collective-permute-start.1 = (bf16[2,192,256]{2,1,0:T(8,128)(2,1)S(1)}, bf16[2,192,256]{2,1,0:T(8,128)(2,1)S(1)}, u32[]{:S(2)}, u32[]{:S(2)}) collective-permute-start(bf16[2,192,256]{2,1,0:T(8,128)(2,1)S(1)} %get-tuple-element.37.refs_0_), channel_id=1, source_target_pairs={{0,16},{8,24},{16,0},{24,8},{1,17},{9,25},{17,1},{25,9},{2,18},{10... | collective-permute-start | bytes 589832 | tf_op jit(solution)/shard_map/halo/ppermute | solution.py:391
  6.3 1.3 %collective-permute-start = (bf16[2,192,256]{2,1,0:T(8,128)(2,1)S(1)}, bf16[2,192,256]{2,1,0:T(8,128)(2,1)S(1)}, u32[]{:S(2)}, u32[]{:S(2)}) collective-permute-start(bf16[2,192,256]{2,1,0:T(8,128)(2,1)S(1)} %get-tuple-element.37.refs_0_), channel_id=1, source_target_pairs={{0,8},{8,0},{16,24},{24,16},{1,9},{9,1},{17,25},{25,17},{2,10},{10... | collective-permute-start | bytes 589832 | tf_op jit(solution)/shard_map/halo/ppermute | solution.py:391
  7.6 4.5 %collective-permute-start.3 = (bf16[2,192,256]{2,1,0:T(8,128)(2,1)S(1)}, bf16[2,192,256]{2,1,0:T(8,128)(2,1)S(1)}, u32[]{:S(2)}, u32[]{:S(2)}) collective-permute-start(bf16[2,192,256]{2,1,0:T(8,128)(2,1)S(1)} %get-tuple-element.38.refs_3_.refs_1_.refs_4_), channel_id=1, source_target_pairs={{0,0},{1,2},{2,1},{3,3},{4,4},{5,6},{6,5},{7,7},{8,8},{9,10},{10,9... | collective-permute-start | bytes 589832 | tf_op jit(solution)/shard_map/halo/ppermute | solution.py:401
  12.2 0.1 collective-permute-start.2
  12.2 0.0 collective-permute-done.4.refs_6_.refs_4_.refs_5_
  12.2 1.9 %collective-permute-start.6 = (bf16[2,192,256]{2,1,0:T(8,128)(2,1)S(1)}, bf16[2,192,256]{2,1,0:T(8,128)(2,1)S(1)}, u32[]{:S(2)}, u32[]{:S(2)}) collective-permute-start(bf16[2,192,256]{2,1,0:T(8,128)(2,1)S(1)} %collective-permute-done.4.refs_6_.refs_4_.refs_5_), channel_id=1, source_target_pairs={{0,0},{1,2},{2,1},{3,3},{4,4},{5,6},{6,5},{7,7},{8,8},{9,10},{10,9... | collective-permute-start | bytes 589832 | tf_op jit(solution)/shard_map/halo/ppermute | solution.py:401
  14.2 0.7 %collective-permute-done.1.refs_2_ = bf16[2,192,256]{2,1,0:T(8,128)(2,1)S(1)} collective-permute-done((bf16[2,192,256]{2,1,0:T(8,128)(2,1)S(1)}, bf16[2,192,256]{2,1,0:T(8,128)(2,1)S(1)}, u32[]{:S(2)}, u32[]{:S(2)}) %collective-permute-start.1) | collective-permute-done | bytes 196640 | tf_op jit(solution)/shard_map/halo/ppermute | solution.py:391
  14.9 1.7 %collective-permute-start.5 = (bf16[2,192,256]{2,1,0:T(8,128)(2,1)S(1)}, bf16[2,192,256]{2,1,0:T(8,128)(2,1)S(1)}, u32[]{:S(2)}, u32[]{:S(2)}) collective-permute-start(bf16[2,192,256]{2,1,0:T(8,128)(2,1)S(1)} %collective-permute-done.4.refs_6_.refs_4_.refs_5_), channel_id=1, source_target_pairs={{0,1},{1,0},{2,3},{3,2},{4,5},{5,4},{6,7},{7,6},{8,9},{9,8},{10,11... | collective-permute-start | bytes 589832 | tf_op jit(solution)/shard_map/halo/ppermute | solution.py:401
  16.5 0.0 collective-permute-done.refs_1_
  16.5 0.3 collective-permute-start.7
  16.8 0.0 collective-permute-done.3.refs_5_.refs_3_.refs_6_
  16.8 0.0 collective-permute-done.2.refs_4_.refs_2_
  16.8 2.4 %collective-permute-done.6.refs_8_.refs_6_.refs_7_ = bf16[2,192,256]{2,1,0:T(8,128)(2,1)S(1)} collective-permute-done((bf16[2,192,256]{2,1,0:T(8,128)(2,1)S(1)}, bf16[2,192,256]{2,1,0:T(8,128)(2,1)S(1)}, u32[]{:S(2)}, u32[]{:S(2)}) %collective-permute-start.6) | collective-permute-done | bytes 196640 | tf_op jit(solution)/shard_map/halo/ppermute | solution.py:401
  19.2 0.0 collective-permute-done.5.refs_7_.refs_5_
  19.2 2.4 %attend.2 = (bf16[192,256]{1,0:T(8,128)(2,1)S(1)}, bf16[192,256]{1,0:T(8,128)(2,1)S(1)}, bf16[192,256]{1,0:T(8,128)(2,1)S(1)}, f32[576,128]{1,0:T(8,128)S(1)}) custom-call(bf16[2,192,256]{2,1,0:T(8,128)(2,1)S(1)} %get-tuple-element.37.refs_0_, bf16[2,192,256]{2,1,0:T(8,128)(2,1)S(1)} %collective-permute-done.refs_1_, ...), custom_call_target="tpu_custom_call" | custom-call | flops 5435817984 | bytes 2359296 | tf_op jit(solution)/shard_map/attend/pallas_call | solution.py:353
  21.7 0.8 %collective-permute-start.8 = (bf16[192,256]{1,0:T(8,128)(2,1)S(1)}, bf16[192,256]{1,0:T(8,128)(2,1)S(1)}, u32[]{:S(2)}, u32[]{:S(2)}) collective-permute-start(bf16[192,256]{1,0:T(8,128)(2,1)S(1)} %get-tuple-element.42), channel_id=1, source_target_pairs={{0,16},{8,24},{16,0},{24,8},{1,17},{9,25},{17,1},{25,9},{2,18},{10... | collective-permute-start | bytes 294920 | tf_op jit(solution)/shard_map/merge/ppermute | solution.py:391
  22.4 1.0 %collective-permute-start.9 = (bf16[192,256]{1,0:T(8,128)(2,1)S(1)}, bf16[192,256]{1,0:T(8,128)(2,1)S(1)}, u32[]{:S(2)}, u32[]{:S(2)}) collective-permute-start(bf16[192,256]{1,0:T(8,128)(2,1)S(1)} %get-tuple-element.43), channel_id=1, source_target_pairs={{0,8},{8,0},{16,24},{24,16},{1,9},{9,1},{17,25},{25,17},{2,10},{10... | collective-permute-start | bytes 294920 | tf_op jit(solution)/shard_map/merge/ppermute | solution.py:391
  23.5 0.0 collective-permute-done.7.refs_0_.refs_3_
  23.5 1.0 %attend.3 = (bf16[192,256]{1,0:T(8,128)(2,1)S(1)}, f32[8,768]{1,0:T(8,128)S(1)}) custom-call(bf16[2,192,256]{2,1,0:T(8,128)(2,1)S(1)} %collective-permute-done.7.refs_0_.refs_3_, bf16[2,192,256]{2,1,0:T(8,128)(2,1)S(1)} %get-tuple-element.38.refs_3_.refs_1_.refs_4_, bf16[2,192,256]{2,1,0:T(8,128)(2,1)S(1)} %collective-permute-done.2.refs_4_.refs_2_, ...), custom_call_target="tpu_custom_call" | custom-call | flops 1811939328 | bytes 1794048 | tf_op jit(solution)/shard_map/attend/pallas_call | solution.py:353
  24.5 1.7 %collective-permute-start.12 = (f32[8,768]{1,0:T(8,128)S(1)}, f32[8,768]{1,0:T(8,128)S(1)}, u32[]{:S(2)}, u32[]{:S(2)}) collective-permute-start(f32[8,768]{1,0:T(8,128)S(1)} %get-tuple-element.44.refs_8_), channel_id=1, source_target_pairs={{0,16},{8,24},{16,0},{24,8},{1,17},{9,25},{17,1},{25,9},{2,18},{10... | collective-permute-start | bytes 73736 | tf_op jit(solution)/shard_map/merge/ppermute | solution.py:391
  26.3 1.1 %collective-permute-start.11 = (f32[8,768]{1,0:T(8,128)S(1)}, f32[8,768]{1,0:T(8,128)S(1)}, u32[]{:S(2)}, u32[]{:S(2)}) collective-permute-start(f32[8,768]{1,0:T(8,128)S(1)} %get-tuple-element.44.refs_8_), channel_id=1, source_target_pairs={{0,24},{8,16},{16,8},{24,0},{1,25},{9,17},{17,9},{25,1},{2,26},{10... | collective-permute-start | bytes 73736 | tf_op jit(solution)/shard_map/merge/ppermute | solution.py:391
  27.3 1.4 %collective-permute-done.8.refs_2_ = bf16[192,256]{1,0:T(8,128)(2,1)S(1)} collective-permute-done((bf16[192,256]{1,0:T(8,128)(2,1)S(1)}, bf16[192,256]{1,0:T(8,128)(2,1)S(1)}, u32[]{:S(2)}, u32[]{:S(2)}) %collective-permute-start.8) | collective-permute-done | bytes 98336 | tf_op jit(solution)/shard_map/merge/ppermute | solution.py:391
  28.7 0.0 collective-permute-done.9.refs_3_
  28.7 0.0 collective-permute-start.10
  28.7 2.1 %collective-permute-start.13 = (bf16[192,256]{1,0:T(8,128)(2,1)S(1)}, bf16[192,256]{1,0:T(8,128)(2,1)S(1)}, u32[]{:S(2)}, u32[]{:S(2)}) collective-permute-start(bf16[192,256]{1,0:T(8,128)(2,1)S(1)} %get-tuple-element.51), channel_id=1, source_target_pairs={{0,24},{8,16},{16,8},{24,0},{1,25},{9,17},{17,9},{25,1},{2,26},{10... | collective-permute-start | bytes 294920 | tf_op jit(solution)/shard_map/merge/ppermute | solution.py:391
  30.8 0.0 collective-permute-done.12.refs_11_
  30.8 0.0 collective-permute-done.11.refs_10_
  30.8 0.6 %collective-permute-done.10.refs_9_ = f32[8,768]{1,0:T(8,128)S(1)} collective-permute-done((f32[8,768]{1,0:T(8,128)S(1)}, f32[8,768]{1,0:T(8,128)S(1)}, u32[]{:S(2)}, u32[]{:S(2)}) %collective-permute-start.10) | collective-permute-done | bytes 24608 | tf_op jit(solution)/shard_map/merge/ppermute | solution.py:391
  31.4 2.9 %gradients.2 = (f32[2,128,768]{2,1,0:T(8,128)S(1)}, f32[2,768]{1,0:T(2,128)S(1)}, f32[2,768]{1,0:T(2,128)S(1)}, f32[192,128]{1,0:T(8,128)S(1)}, bf16[2,2,192,256...) custom-call(bf16[2,192,256]{2,1,0:T(8,128)(2,1)S(1)} %get-tuple-element.37.refs_0_, ...), custom_call_target="tpu_custom_call" | custom-call | flops 12079595520 | bytes 3354624 | tf_op jit(solution)/shard_map/gradients/pallas_call | solution.py:353
  34.3 1.7 %collective-permute-start.17 = (bf16[2,2,192,256]{3,2,1,0:T(8,128)(2,1)S(1)}, bf16[2,2,192,256]{3,2,1,0:T(8,128)(2,1)S(1)}, u32[]{:S(2)}, u32[]{:S(2)}) collective-permute-start(bf16[2,2,192,256]{3,2,1,0:T(8,128)(2,1)S(1)} %get-tuple-element.62), channel_id=1, source_target_pairs={{0,1},{1,0},{2,3},{3,2},{4,5},{5,4},{6,7},{7,6},{8,9},{9,8},{10,11... | collective-permute-start | bytes 1179656 | tf_op jit(solution)/shard_map/gradients/ppermute | solution.py:456
  36.1 3.1 %collective-permute-start.18 = (bf16[2,2,192,256]{3,2,1,0:T(8,128)(2,1)S(1)}, bf16[2,2,192,256]{3,2,1,0:T(8,128)(2,1)S(1)}, u32[]{:S(2)}, u32[]{:S(2)}) collective-permute-start(bf16[2,2,192,256]{3,2,1,0:T(8,128)(2,1)S(1)} %get-tuple-element.63), channel_id=1, source_target_pairs={{0,0},{1,2},{2,1},{3,3},{4,4},{5,6},{6,5},{7,7},{8,8},{9,10},{10,9... | collective-permute-start | bytes 1179656 | tf_op jit(solution)/shard_map/gradients/ppermute | solution.py:456
  39.2 1.7 %gradients.3 = (bf16[192,256]{1,0:T(8,128)(2,1)S(1)}, bf16[192,256]{1,0:T(8,128)(2,1)S(1)}, bf16[192,256]{1,0:T(8,128)(2,1)S(1)}, bf16[192,256]{1,0:T(8,128)(2,1)S(1)}, bf16[2,2,192,256]{3,2,1,0:T(8,128)(2,1)S(1)}) custom-call(bf16[2,192,256]{2,1,0:T(8,128)(2,1)S(1)} %get-tuple-element.37.refs_0_, bf16[2,192,256]{2,1,0:T(8,128)(2,1)S(1)} %collective-permute-done.refs_1_, ...), custom_call_target="tpu_custom_call" | custom-call | flops 6039797760 | bytes 2764800 | tf_op jit(solution)/shard_map/gradients/pallas_call | solution.py:353
  40.9 0.0 collective-permute-done.13.refs_1_
  40.9 1.6 %collective-permute-start.14 = (bf16[192,256]{1,0:T(8,128)(2,1)S(1)}, bf16[192,256]{1,0:T(8,128)(2,1)S(1)}, u32[]{:S(2)}, u32[]{:S(2)}) collective-permute-start(bf16[192,256]{1,0:T(8,128)(2,1)S(1)} %get-tuple-element.58), channel_id=1, source_target_pairs={{0,16},{8,24},{16,0},{24,8},{1,17},{9,25},{17,1},{25,9},{2,18},{10... | collective-permute-start | bytes 294920 | tf_op jit(solution)/shard_map/return/ppermute | solution.py:391
  42.5 1.3 %collective-permute-start.15 = (bf16[192,256]{1,0:T(8,128)(2,1)S(1)}, bf16[192,256]{1,0:T(8,128)(2,1)S(1)}, u32[]{:S(2)}, u32[]{:S(2)}) collective-permute-start(bf16[192,256]{1,0:T(8,128)(2,1)S(1)} %get-tuple-element.59), channel_id=1, source_target_pairs={{0,24},{8,16},{16,8},{24,0},{1,25},{9,17},{17,9},{25,1},{2,26},{10... | collective-permute-start | bytes 294920 | tf_op jit(solution)/shard_map/return/ppermute | solution.py:391
  43.8 0.0 collective-permute-start.16
  43.8 0.0 collective-permute-done.17.refs_9_
  43.8 1.6 %collective-permute-done.18.refs_10_ = bf16[2,2,192,256]{3,2,1,0:T(8,128)(2,1)S(1)} collective-permute-done((bf16[2,2,192,256]{3,2,1,0:T(8,128)(2,1)S(1)}, bf16[2,2,192,256]{3,2,1,0:T(8,128)(2,1)S(1)}, u32[]{:S(2)}, u32[]{:S(2)}) %collective-permute-start.18) | collective-permute-done | bytes 393248 | tf_op jit(solution)/shard_map/gradients/ppermute | solution.py:456
  45.4 0.1 fusion.1
  45.5 0.3 collective-permute-start.20
  45.8 1.2 %collective-permute-start.19 = (bf16[192,256]{1,0:T(8,128)(2,1)S(1)}, bf16[192,256]{1,0:T(8,128)(2,1)S(1)}, u32[]{:S(2)}, u32[]{:S(2)}) collective-permute-start(bf16[192,256]{1,0:T(8,128)(2,1)S(1)} %get-tuple-element.71), channel_id=1, source_target_pairs={{0,4},{4,0},{1,5},{5,1},{2,6},{6,2},{3,7},{7,3},{8,12},{12,8},{9,1... | collective-permute-start | bytes 294920 | tf_op jit(solution)/shard_map/return/ppermute | solution.py:466
  47.0 2.5 %collective-permute-done.14.refs_5_ = bf16[192,256]{1,0:T(8,128)(2,1)S(1)} collective-permute-done((bf16[192,256]{1,0:T(8,128)(2,1)S(1)}, bf16[192,256]{1,0:T(8,128)(2,1)S(1)}, u32[]{:S(2)}, u32[]{:S(2)}) %collective-permute-start.14) | collective-permute-done | bytes 98336 | tf_op jit(solution)/shard_map/return/ppermute | solution.py:391
  49.6 0.0 collective-permute-done.15.refs_6_
  49.6 0.3 collective-permute-done.16.refs_7_
  49.9 0.0 collective-permute-done.20.refs_12_
  49.9 0.2 collective-permute-done.19.refs_11_
  50.1 1.2 %finish.1 = (bf16[192,256]{1,0:T(8,128)(2,1)}, bf16[192,256]{1,0:T(8,128)(2,1)}, bf16[192,256]{1,0:T(8,128)(2,1)}, bf16[192,256]{1,0:T(8,128)(2,1)}) custom-call(bf16[192,256]{1,0:T(8,128)(2,1)S(1)} %get-tuple-element.39.refs_0_, bf16[192,256]{1,0:T(8,128)(2,1)S(1)} %collective-permute-done.13.refs_1_, bf16[192,256]{1,0:T(8,128)(2,1)S(1)} %collective-permute-done.8.refs_2_, ...), custom_call_target="tpu_custom_call" | custom-call | bytes 2949120 | tf_op jit(solution)/shard_map/finish/pallas_call | solution.py:353
Async XLA Ops:
  1.9 10.3 %collective-permute-start.4 = (bf16[2,192,256]{2,1,0:T(8,128)(2,1)S(1)}, bf16[2,192,256]{2,1,0:T(8,128)(2,1)S(1)}, u32[]{:S(2)}, u32[]{:S(2)}) collective-permute-start(bf16[2,192,256]{2,1,0:T(8,128)(2,1)S(1)} %get-tuple-element.38.refs_3_.refs_1_.refs_4_), channel_id=1, source_target_pairs={{0,4},{4,0},{1,5},{5,1},{2,6},{6,2},{3,7},{7,3},{8,12},{12,8},{9,1... | collective-permute-start | bytes 589832 | tf_op jit(solution)/shard_map/halo/ppermute | solution.py:396
  4.0 10.9 %collective-permute-start.1 = (bf16[2,192,256]{2,1,0:T(8,128)(2,1)S(1)}, bf16[2,192,256]{2,1,0:T(8,128)(2,1)S(1)}, u32[]{:S(2)}, u32[]{:S(2)}) collective-permute-start(bf16[2,192,256]{2,1,0:T(8,128)(2,1)S(1)} %get-tuple-element.37.refs_0_), channel_id=1, source_target_pairs={{0,16},{8,24},{16,0},{24,8},{1,17},{9,25},{17,1},{25,9},{2,18},{10... | collective-permute-start | bytes 589832 | tf_op jit(solution)/shard_map/halo/ppermute | solution.py:391
  6.3 10.2 %collective-permute-start = (bf16[2,192,256]{2,1,0:T(8,128)(2,1)S(1)}, bf16[2,192,256]{2,1,0:T(8,128)(2,1)S(1)}, u32[]{:S(2)}, u32[]{:S(2)}) collective-permute-start(bf16[2,192,256]{2,1,0:T(8,128)(2,1)S(1)} %get-tuple-element.37.refs_0_), channel_id=1, source_target_pairs={{0,8},{8,0},{16,24},{24,16},{1,9},{9,1},{17,25},{25,17},{2,10},{10... | collective-permute-start | bytes 589832 | tf_op jit(solution)/shard_map/halo/ppermute | solution.py:391
  7.6 9.2 %collective-permute-start.3 = (bf16[2,192,256]{2,1,0:T(8,128)(2,1)S(1)}, bf16[2,192,256]{2,1,0:T(8,128)(2,1)S(1)}, u32[]{:S(2)}, u32[]{:S(2)}) collective-permute-start(bf16[2,192,256]{2,1,0:T(8,128)(2,1)S(1)} %get-tuple-element.38.refs_3_.refs_1_.refs_4_), channel_id=1, source_target_pairs={{0,0},{1,2},{2,1},{3,3},{4,4},{5,6},{6,5},{7,7},{8,8},{9,10},{10,9... | collective-permute-start | bytes 589832 | tf_op jit(solution)/shard_map/halo/ppermute | solution.py:401
  12.2 4.7 %collective-permute-start.2 = (bf16[2,192,256]{2,1,0:T(8,128)(2,1)S(1)}, bf16[2,192,256]{2,1,0:T(8,128)(2,1)S(1)}, u32[]{:S(2)}, u32[]{:S(2)}) collective-permute-start(bf16[2,192,256]{2,1,0:T(8,128)(2,1)S(1)} %get-tuple-element.38.refs_3_.refs_1_.refs_4_), channel_id=1, source_target_pairs={{0,1},{1,0},{2,3},{3,2},{4,5},{5,4},{6,7},{7,6},{8,9},{9,8},{10,11... | collective-permute-start | bytes 589832 | tf_op jit(solution)/shard_map/halo/ppermute | solution.py:401
  12.2 7.0 %collective-permute-start.6 = (bf16[2,192,256]{2,1,0:T(8,128)(2,1)S(1)}, bf16[2,192,256]{2,1,0:T(8,128)(2,1)S(1)}, u32[]{:S(2)}, u32[]{:S(2)}) collective-permute-start(bf16[2,192,256]{2,1,0:T(8,128)(2,1)S(1)} %collective-permute-done.4.refs_6_.refs_4_.refs_5_), channel_id=1, source_target_pairs={{0,0},{1,2},{2,1},{3,3},{4,4},{5,6},{6,5},{7,7},{8,8},{9,10},{10,9... | collective-permute-start | bytes 589832 | tf_op jit(solution)/shard_map/halo/ppermute | solution.py:401
  14.9 4.4 %collective-permute-start.5 = (bf16[2,192,256]{2,1,0:T(8,128)(2,1)S(1)}, bf16[2,192,256]{2,1,0:T(8,128)(2,1)S(1)}, u32[]{:S(2)}, u32[]{:S(2)}) collective-permute-start(bf16[2,192,256]{2,1,0:T(8,128)(2,1)S(1)} %collective-permute-done.4.refs_6_.refs_4_.refs_5_), channel_id=1, source_target_pairs={{0,1},{1,0},{2,3},{3,2},{4,5},{5,4},{6,7},{7,6},{8,9},{9,8},{10,11... | collective-permute-start | bytes 589832 | tf_op jit(solution)/shard_map/halo/ppermute | solution.py:401
  16.5 7.0 %collective-permute-start.7 = (bf16[2,192,256]{2,1,0:T(8,128)(2,1)S(1)}, bf16[2,192,256]{2,1,0:T(8,128)(2,1)S(1)}, u32[]{:S(2)}, u32[]{:S(2)}) collective-permute-start(bf16[2,192,256]{2,1,0:T(8,128)(2,1)S(1)} %collective-permute-done.1.refs_2_), channel_id=1, source_target_pairs={{0,8},{8,0},{16,24},{24,16},{1,9},{9,1},{17,25},{25,17},{2,10},{10... | collective-permute-start | bytes 589832 | tf_op jit(solution)/shard_map/halo/ppermute | solution.py:391
  21.7 7.0 %collective-permute-start.8 = (bf16[192,256]{1,0:T(8,128)(2,1)S(1)}, bf16[192,256]{1,0:T(8,128)(2,1)S(1)}, u32[]{:S(2)}, u32[]{:S(2)}) collective-permute-start(bf16[192,256]{1,0:T(8,128)(2,1)S(1)} %get-tuple-element.42), channel_id=1, source_target_pairs={{0,16},{8,24},{16,0},{24,8},{1,17},{9,25},{17,1},{25,9},{2,18},{10... | collective-permute-start | bytes 294920 | tf_op jit(solution)/shard_map/merge/ppermute | solution.py:391
  22.4 6.2 %collective-permute-start.9 = (bf16[192,256]{1,0:T(8,128)(2,1)S(1)}, bf16[192,256]{1,0:T(8,128)(2,1)S(1)}, u32[]{:S(2)}, u32[]{:S(2)}) collective-permute-start(bf16[192,256]{1,0:T(8,128)(2,1)S(1)} %get-tuple-element.43), channel_id=1, source_target_pairs={{0,8},{8,0},{16,24},{24,16},{1,9},{9,1},{17,25},{25,17},{2,10},{10... | collective-permute-start | bytes 294920 | tf_op jit(solution)/shard_map/merge/ppermute | solution.py:391
  24.5 6.3 %collective-permute-start.12 = (f32[8,768]{1,0:T(8,128)S(1)}, f32[8,768]{1,0:T(8,128)S(1)}, u32[]{:S(2)}, u32[]{:S(2)}) collective-permute-start(f32[8,768]{1,0:T(8,128)S(1)} %get-tuple-element.44.refs_8_), channel_id=1, source_target_pairs={{0,16},{8,24},{16,0},{24,8},{1,17},{9,25},{17,1},{25,9},{2,18},{10... | collective-permute-start | bytes 73736 | tf_op jit(solution)/shard_map/merge/ppermute | solution.py:391
  26.3 4.5 %collective-permute-start.11 = (f32[8,768]{1,0:T(8,128)S(1)}, f32[8,768]{1,0:T(8,128)S(1)}, u32[]{:S(2)}, u32[]{:S(2)}) collective-permute-start(f32[8,768]{1,0:T(8,128)S(1)} %get-tuple-element.44.refs_8_), channel_id=1, source_target_pairs={{0,24},{8,16},{16,8},{24,0},{1,25},{9,17},{17,9},{25,1},{2,26},{10... | collective-permute-start | bytes 73736 | tf_op jit(solution)/shard_map/merge/ppermute | solution.py:391
  28.7 2.7 %collective-permute-start.10 = (f32[8,768]{1,0:T(8,128)S(1)}, f32[8,768]{1,0:T(8,128)S(1)}, u32[]{:S(2)}, u32[]{:S(2)}) collective-permute-start(f32[8,768]{1,0:T(8,128)S(1)} %get-tuple-element.44.refs_8_), channel_id=1, source_target_pairs={{0,8},{8,0},{16,24},{24,16},{1,9},{9,1},{17,25},{25,17},{2,10},{10... | collective-permute-start | bytes 73736 | tf_op jit(solution)/shard_map/merge/ppermute | solution.py:391
  28.7 12.2 %collective-permute-start.13 = (bf16[192,256]{1,0:T(8,128)(2,1)S(1)}, bf16[192,256]{1,0:T(8,128)(2,1)S(1)}, u32[]{:S(2)}, u32[]{:S(2)}) collective-permute-start(bf16[192,256]{1,0:T(8,128)(2,1)S(1)} %get-tuple-element.51), channel_id=1, source_target_pairs={{0,24},{8,16},{16,8},{24,0},{1,25},{9,17},{17,9},{25,1},{2,26},{10... | collective-permute-start | bytes 294920 | tf_op jit(solution)/shard_map/merge/ppermute | solution.py:391
  34.3 9.5 %collective-permute-start.17 = (bf16[2,2,192,256]{3,2,1,0:T(8,128)(2,1)S(1)}, bf16[2,2,192,256]{3,2,1,0:T(8,128)(2,1)S(1)}, u32[]{:S(2)}, u32[]{:S(2)}) collective-permute-start(bf16[2,2,192,256]{3,2,1,0:T(8,128)(2,1)S(1)} %get-tuple-element.62), channel_id=1, source_target_pairs={{0,1},{1,0},{2,3},{3,2},{4,5},{5,4},{6,7},{7,6},{8,9},{9,8},{10,11... | collective-permute-start | bytes 1179656 | tf_op jit(solution)/shard_map/gradients/ppermute | solution.py:456
  36.1 9.4 %collective-permute-start.18 = (bf16[2,2,192,256]{3,2,1,0:T(8,128)(2,1)S(1)}, bf16[2,2,192,256]{3,2,1,0:T(8,128)(2,1)S(1)}, u32[]{:S(2)}, u32[]{:S(2)}) collective-permute-start(bf16[2,2,192,256]{3,2,1,0:T(8,128)(2,1)S(1)} %get-tuple-element.63), channel_id=1, source_target_pairs={{0,0},{1,2},{2,1},{3,3},{4,4},{5,6},{6,5},{7,7},{8,8},{9,10},{10,9... | collective-permute-start | bytes 1179656 | tf_op jit(solution)/shard_map/gradients/ppermute | solution.py:456
  40.9 8.7 %collective-permute-start.14 = (bf16[192,256]{1,0:T(8,128)(2,1)S(1)}, bf16[192,256]{1,0:T(8,128)(2,1)S(1)}, u32[]{:S(2)}, u32[]{:S(2)}) collective-permute-start(bf16[192,256]{1,0:T(8,128)(2,1)S(1)} %get-tuple-element.58), channel_id=1, source_target_pairs={{0,16},{8,24},{16,0},{24,8},{1,17},{9,25},{17,1},{25,9},{2,18},{10... | collective-permute-start | bytes 294920 | tf_op jit(solution)/shard_map/return/ppermute | solution.py:391
  42.5 7.1 %collective-permute-start.15 = (bf16[192,256]{1,0:T(8,128)(2,1)S(1)}, bf16[192,256]{1,0:T(8,128)(2,1)S(1)}, u32[]{:S(2)}, u32[]{:S(2)}) collective-permute-start(bf16[192,256]{1,0:T(8,128)(2,1)S(1)} %get-tuple-element.59), channel_id=1, source_target_pairs={{0,24},{8,16},{16,8},{24,0},{1,25},{9,17},{17,9},{25,1},{2,26},{10... | collective-permute-start | bytes 294920 | tf_op jit(solution)/shard_map/return/ppermute | solution.py:391
  43.8 6.1 %collective-permute-start.16 = (bf16[192,256]{1,0:T(8,128)(2,1)S(1)}, bf16[192,256]{1,0:T(8,128)(2,1)S(1)}, u32[]{:S(2)}, u32[]{:S(2)}) collective-permute-start(bf16[192,256]{1,0:T(8,128)(2,1)S(1)} %get-tuple-element.60), channel_id=1, source_target_pairs={{0,8},{8,0},{16,24},{24,16},{1,9},{9,1},{17,25},{25,17},{2,10},{10... | collective-permute-start | bytes 294920 | tf_op jit(solution)/shard_map/return/ppermute | solution.py:391
  45.5 4.4 %collective-permute-start.20 = (bf16[192,256]{1,0:T(8,128)(2,1)S(1)}, bf16[192,256]{1,0:T(8,128)(2,1)S(1)}, u32[]{:S(2)}, u32[]{:S(2)}) collective-permute-start(bf16[192,256]{1,0:T(8,128)(2,1)S(1)} %get-tuple-element.70), channel_id=1, source_target_pairs={{0,4},{4,0},{1,5},{5,1},{2,6},{6,2},{3,7},{7,3},{8,12},{12,8},{9,1... | collective-permute-start | bytes 294920 | tf_op jit(solution)/shard_map/return/ppermute | solution.py:466
  45.8 4.3 %collective-permute-start.19 = (bf16[192,256]{1,0:T(8,128)(2,1)S(1)}, bf16[192,256]{1,0:T(8,128)(2,1)S(1)}, u32[]{:S(2)}, u32[]{:S(2)}) collective-permute-start(bf16[192,256]{1,0:T(8,128)(2,1)S(1)} %get-tuple-element.71), channel_id=1, source_target_pairs={{0,4},{4,0},{1,5},{5,1},{2,6},{6,2},{3,7},{7,3},{8,12},{12,8},{9,1... | collective-permute-start | bytes 294920 | tf_op jit(solution)/shard_map/return/ppermute | solution.py:466

commit v19 on v18

--- a/solution.py
+++ b/solution.py
@@ -153,24 +153,19 @@
     rest = refs[count + tile_count :]
     if last:
         first_ref, rest = rest[0], rest[1:]
-    o_refs = rest[:count]
-    stat_ref, key_buf, value_buf = rest[count:]
-    at = 0
-    spans = []
-    for flags, members in groups:
-        begin = at
-        for member in members:
-            key_buf[at : at + cells] = kv_refs[member][0]
-            value_buf[at : at + cells] = kv_refs[member][1]
-            at += cells
-        spans.append((begin, at, group_bias(flags, sizes)))
+    o_refs, stat_ref = rest[:count], rest[count]
+    spans = [(members, group_bias(flags, sizes)) for flags, members in groups]
+
+    def joined(members, which, cut):
+        return jnp.concatenate([kv_refs[i][which, :, cut] for i in members], axis=0)
+
     lane = lax.broadcasted_iota(jnp.int32, (count * cells, DH), 1)
     stat = jnp.zeros((count * cells, DH), F32)
 
     def scores_of(head):
         cut = head_slice(head)
         query = jnp.concatenate([ref[0, :, cut] for ref in qg_refs], axis=0)
-        return [dot_nt(query, key_buf[lo:hi, cut]) for lo, hi, _ in spans]
+        return [dot_nt(query, joined(members, 0, cut)) for members, _ in spans]
 
     ahead = scores_of(0)
     for head in range(HEADS):
@@ -179,18 +174,18 @@
         if head + 1 < HEADS:
             ahead = scores_of(head + 1)
         best = None
-        for raw, (_, _, bias) in zip(scores, spans):
+        for raw, (_, bias) in zip(scores, spans):
             top = jnp.max(raw, axis=1, keepdims=True) * SCALE_LOG2
             if bias is not None:
                 top = top + bias
             best = top if best is None else jnp.maximum(best, top)
         total = None
         out = None
-        for raw, (lo, hi, bias) in zip(scores, spans):
+        for raw, (members, bias) in zip(scores, spans):
             shift = best if bias is None else best - bias
             weights = jnp.exp2(raw * SCALE_LOG2 - shift)
             part = jnp.sum(weights, axis=1, keepdims=True)
-            piece = dot_nn(weights.astype(BF16), value_buf[lo:hi, cut])
+            piece = dot_nn(weights.astype(BF16), joined(members, 1, cut))
             total = part if total is None else total + part
             out = piece if out is None else out + piece
         out = out * (1.0 / total)
@@ -256,22 +251,19 @@
         share_ref[...] = wide.T[:cells]
     else:
         lse, delta = lse_ref[...], delta_ref[...]
-    col_refs = rest[: len(cols)]
-    key_buf, value_buf = rest[len(cols) :]
-
-    span = grid_rows * cells
-    for i, ref in enumerate(kv_refs):
-        key_buf[i * cells : (i + 1) * cells] = ref[0]
-        value_buf[i * cells : (i + 1) * cells] = ref[1]
+    col_refs = rest
     blocks = [(head, slot) for head in range(HEADS) for slot in range(len(cols))]
+
+    def joined(slots, which, cut):
+        picked = [kv_refs[slot * grid_rows + row] for slot in slots for row in range(grid_rows)]
+        return jnp.concatenate([ref[which, :, cut] for ref in picked], axis=0)
 
     def products_of(head, slot):
         cut = head_slice(head)
-        at = slice(slot * span, (slot + 1) * span)
         queries = jnp.concatenate([ref[0, :, cut] for ref in qg_refs], axis=0)
         grads = jnp.concatenate([ref[1, :, cut] for ref in qg_refs], axis=0)
-        raw = dot_nt(key_buf[at, cut], queries)
-        return raw, dot_nt(value_buf[at, cut], grads), queries, grads
+        raw = dot_nt(joined([slot], 0, cut), queries)
+        return raw, dot_nt(joined([slot], 1, cut), grads), queries, grads
 
     dscores = [[] for _ in range(HEADS)]
     ahead = products_of(*blocks[0])
@@ -297,7 +289,7 @@
         dscores[head].append(dscore)
     for head in range(HEADS):
         cut = head_slice(head)
-        dq = dot_nn(key_buf[:, cut].T, jnp.concatenate(dscores[head], axis=0))
+        dq = dot_nn(joined(range(len(cols)), 0, cut).T, jnp.concatenate(dscores[head], axis=0))
         dq = dq if first else dq + dq_ref[head]
         if last:
             dq = (dq * SCALE).T.astype(BF16)
@@ -420,7 +412,6 @@
             (*blocks, *flat_tiles) + (() if first is None else (first,)),
             2 * product * count,
             cells * key_count * HEADS * count,
-            [pltpu.VMEM((key_count, chan), BF16)] * 2,
         )
 
     with jax.named_scope("attend"):
@@ -448,7 +439,6 @@
             (*queries, *[tiles[row][col] for col in which for row in range(grid_rows)], *carried),
             20 * product * count // grid_cols,
             4 * cells * key_count * HEADS * count // grid_cols,
-            [pltpu.VMEM((count * grid_rows * cells, chan), BF16)] * 2,
         )
 
     with jax.named_scope("gradients"):

time: 51.5 us -> 51.4 us (level)
  no operation moved by 1% of the time
where the time goes in v19:
time: 51.4 us; the launch traced here: 51.2 us
  starting transfers between devices  30.3 us (59%)
  Pallas kernels  10.4 us (20%)
  waiting for transfers between devices  9.64 us (19%)
  between operations  0.72 us (1%)
    ppermute x12, starting transfers between devices, other_frames(): lax.ppermute(x, 'ta', [(i, i ^ distance) for i in range(sizes['ta'])])  13.6 us
    pallas_call x6, Pallas kernels, call(): pl.pallas_call(kernel, out_shape=out_shape, in_specs=[pl.BlockSpec(memory...  10.4 us
    ppermute x4, starting transfers between devices, shards(): lax.ppermute(block, 'wa', pairs)  8.2 us
    ppermute x12, waiting for transfers between devices, other_frames(): lax.ppermute(x, 'ta', [(i, i ^ distance) for i in range(sizes['ta'])])  5.5 us
    ppermute x2, starting transfers between devices, shards(): sides = [lax.ppermute(x, 'wa', pairs) for x, pairs in zip(sides, col_sides)]  4.91 us
    ppermute x4, waiting for transfers between devices, shards(): lax.ppermute(block, 'wa', pairs)  2.4 us
    ppermute x1, starting transfers between devices, shards(): kv_rows = [kv] + [lax.ppermute(kv, 'ha', pairs) for pairs in row_sides]  2.11 us
    ppermute x2, waiting for transfers between devices, shards(): sides = [lax.ppermute(x, 'wa', pairs) for x, pairs in zip(sides, col_sides)]  1.59 us
  transfers between devices with their start and end apart: 21, of which 8 were waited for; matrix products, arithmetic and copies ran while one was open for 0% of the time, Pallas kernels for 16%

profile of v19, /device:TPU:1, one launch (start us, length us, event | category | flops | bytes accessed | tf_op | source)
XLA Modules:
  0.0 51.2 jit_solution(11633825048875736785)
XLA Ops:
  0.6 1.3 %rotate.1 = (bf16[2,192,256]{2,1,0:T(8,128)(2,1)S(1)}, bf16[2,192,256]{2,1,0:T(8,128)(2,1)S(1)}, f32[3,192,128]{2,1,0:T(8,128)S(1)}) custom-call(bf16[192,256]{1,0:T(8,128)(2,1)} %bitcast.12, bf16[192,256]{1,0:T(8,128)(2,1)} %bitcast.13, bf16[192,256]{1,0:T(8,128)(2,1)} %bitcast.14, bf16[192,256]{1,0:T(8,128)(2,1)} %bitcast.15, ...), custom_call_target="tpu_custom_call" | custom-call | bytes 1179648 | tf_op jit(solution)/shard_map/rotate/pallas_call | solution.py:345
  1.9 2.1 %collective-permute-start.4 = (bf16[2,192,256]{2,1,0:T(8,128)(2,1)S(1)}, bf16[2,192,256]{2,1,0:T(8,128)(2,1)S(1)}, u32[]{:S(2)}, u32[]{:S(2)}) collective-permute-start(bf16[2,192,256]{2,1,0:T(8,128)(2,1)S(1)} %get-tuple-element.38.refs_3_.refs_1_.refs_4_), channel_id=1, source_target_pairs={{0,4},{4,0},{1,5},{5,1},{2,6},{6,2},{3,7},{7,3},{8,12},{12,8},{9,1... | collective-permute-start | bytes 589832 | tf_op jit(solution)/shard_map/halo/ppermute | solution.py:388
  4.0 2.3 %collective-permute-start.1 = (bf16[2,192,256]{2,1,0:T(8,128)(2,1)S(1)}, bf16[2,192,256]{2,1,0:T(8,128)(2,1)S(1)}, u32[]{:S(2)}, u32[]{:S(2)}) collective-permute-start(bf16[2,192,256]{2,1,0:T(8,128)(2,1)S(1)} %get-tuple-element.37.refs_0_), channel_id=1, source_target_pairs={{0,16},{8,24},{16,0},{24,8},{1,17},{9,25},{17,1},{25,9},{2,18},{10... | collective-permute-start | bytes 589832 | tf_op jit(solution)/shard_map/halo/ppermute | solution.py:383
  6.3 1.3 %collective-permute-start = (bf16[2,192,256]{2,1,0:T(8,128)(2,1)S(1)}, bf16[2,192,256]{2,1,0:T(8,128)(2,1)S(1)}, u32[]{:S(2)}, u32[]{:S(2)}) collective-permute-start(bf16[2,192,256]{2,1,0:T(8,128)(2,1)S(1)} %get-tuple-element.37.refs_0_), channel_id=1, source_target_pairs={{0,8},{8,0},{16,24},{24,16},{1,9},{9,1},{17,25},{25,17},{2,10},{10... | collective-permute-start | bytes 589832 | tf_op jit(solution)/shard_map/halo/ppermute | solution.py:383
  7.6 4.5 %collective-permute-start.3 = (bf16[2,192,256]{2,1,0:T(8,128)(2,1)S(1)}, bf16[2,192,256]{2,1,0:T(8,128)(2,1)S(1)}, u32[]{:S(2)}, u32[]{:S(2)}) collective-permute-start(bf16[2,192,256]{2,1,0:T(8,128)(2,1)S(1)} %get-tuple-element.38.refs_3_.refs_1_.refs_4_), channel_id=1, source_target_pairs={{0,0},{1,2},{2,1},{3,3},{4,4},{5,6},{6,5},{7,7},{8,8},{9,10},{10,9... | collective-permute-start | bytes 589832 | tf_op jit(solution)/shard_map/halo/ppermute | solution.py:393
  12.2 0.1 collective-permute-start.2
  12.2 0.0 collective-permute-done.4.refs_6_.refs_4_.refs_5_
  12.2 1.9 %collective-permute-start.6 = (bf16[2,192,256]{2,1,0:T(8,128)(2,1)S(1)}, bf16[2,192,256]{2,1,0:T(8,128)(2,1)S(1)}, u32[]{:S(2)}, u32[]{:S(2)}) collective-permute-start(bf16[2,192,256]{2,1,0:T(8,128)(2,1)S(1)} %collective-permute-done.4.refs_6_.refs_4_.refs_5_), channel_id=1, source_target_pairs={{0,0},{1,2},{2,1},{3,3},{4,4},{5,6},{6,5},{7,7},{8,8},{9,10},{10,9... | collective-permute-start | bytes 589832 | tf_op jit(solution)/shard_map/halo/ppermute | solution.py:393
  14.2 0.7 %collective-permute-done.1.refs_2_ = bf16[2,192,256]{2,1,0:T(8,128)(2,1)S(1)} collective-permute-done((bf16[2,192,256]{2,1,0:T(8,128)(2,1)S(1)}, bf16[2,192,256]{2,1,0:T(8,128)(2,1)S(1)}, u32[]{:S(2)}, u32[]{:S(2)}) %collective-permute-start.1) | collective-permute-done | bytes 196640 | tf_op jit(solution)/shard_map/halo/ppermute | solution.py:383
  14.9 1.7 %collective-permute-start.5 = (bf16[2,192,256]{2,1,0:T(8,128)(2,1)S(1)}, bf16[2,192,256]{2,1,0:T(8,128)(2,1)S(1)}, u32[]{:S(2)}, u32[]{:S(2)}) collective-permute-start(bf16[2,192,256]{2,1,0:T(8,128)(2,1)S(1)} %collective-permute-done.4.refs_6_.refs_4_.refs_5_), channel_id=1, source_target_pairs={{0,1},{1,0},{2,3},{3,2},{4,5},{5,4},{6,7},{7,6},{8,9},{9,8},{10,11... | collective-permute-start | bytes 589832 | tf_op jit(solution)/shard_map/halo/ppermute | solution.py:393
  16.5 0.0 collective-permute-done.refs_1_
  16.5 0.3 collective-permute-start.7
  16.8 0.0 collective-permute-done.3.refs_5_.refs_3_.refs_6_
  16.8 0.0 collective-permute-done.2.refs_4_.refs_2_
  16.8 2.4 %collective-permute-done.6.refs_8_.refs_6_.refs_7_ = bf16[2,192,256]{2,1,0:T(8,128)(2,1)S(1)} collective-permute-done((bf16[2,192,256]{2,1,0:T(8,128)(2,1)S(1)}, bf16[2,192,256]{2,1,0:T(8,128)(2,1)S(1)}, u32[]{:S(2)}, u32[]{:S(2)}) %collective-permute-start.6) | collective-permute-done | bytes 196640 | tf_op jit(solution)/shard_map/halo/ppermute | solution.py:393
  19.2 0.0 collective-permute-done.5.refs_7_.refs_5_
  19.2 2.4 %attend.2 = (bf16[192,256]{1,0:T(8,128)(2,1)S(1)}, bf16[192,256]{1,0:T(8,128)(2,1)S(1)}, bf16[192,256]{1,0:T(8,128)(2,1)S(1)}, f32[576,128]{1,0:T(8,128)S(1)}) custom-call(bf16[2,192,256]{2,1,0:T(8,128)(2,1)S(1)} %get-tuple-element.37.refs_0_, bf16[2,192,256]{2,1,0:T(8,128)(2,1)S(1)} %collective-permute-done.refs_1_, ...), custom_call_target="tpu_custom_call" | custom-call | flops 5435817984 | bytes 2359296 | tf_op jit(solution)/shard_map/attend/pallas_call | solution.py:345
  21.6 0.8 %collective-permute-start.8 = (bf16[192,256]{1,0:T(8,128)(2,1)S(1)}, bf16[192,256]{1,0:T(8,128)(2,1)S(1)}, u32[]{:S(2)}, u32[]{:S(2)}) collective-permute-start(bf16[192,256]{1,0:T(8,128)(2,1)S(1)} %get-tuple-element.42), channel_id=1, source_target_pairs={{0,16},{8,24},{16,0},{24,8},{1,17},{9,25},{17,1},{25,9},{2,18},{10... | collective-permute-start | bytes 294920 | tf_op jit(solution)/shard_map/merge/ppermute | solution.py:383
  22.4 1.0 %collective-permute-start.9 = (bf16[192,256]{1,0:T(8,128)(2,1)S(1)}, bf16[192,256]{1,0:T(8,128)(2,1)S(1)}, u32[]{:S(2)}, u32[]{:S(2)}) collective-permute-start(bf16[192,256]{1,0:T(8,128)(2,1)S(1)} %get-tuple-element.43), channel_id=1, source_target_pairs={{0,8},{8,0},{16,24},{24,16},{1,9},{9,1},{17,25},{25,17},{2,10},{10... | collective-permute-start | bytes 294920 | tf_op jit(solution)/shard_map/merge/ppermute | solution.py:383
  23.4 0.0 collective-permute-done.7.refs_0_.refs_3_
  23.4 1.0 %attend.3 = (bf16[192,256]{1,0:T(8,128)(2,1)S(1)}, f32[8,768]{1,0:T(8,128)S(1)}) custom-call(bf16[2,192,256]{2,1,0:T(8,128)(2,1)S(1)} %collective-permute-done.7.refs_0_.refs_3_, bf16[2,192,256]{2,1,0:T(8,128)(2,1)S(1)} %get-tuple-element.38.refs_3_.refs_1_.refs_4_, bf16[2,192,256]{2,1,0:T(8,128)(2,1)S(1)} %collective-permute-done.2.refs_4_.refs_2_, ...), custom_call_target="tpu_custom_call" | custom-call | flops 1811939328 | bytes 1794048 | tf_op jit(solution)/shard_map/attend/pallas_call | solution.py:345
  24.4 1.8 %collective-permute-start.12 = (f32[8,768]{1,0:T(8,128)S(1)}, f32[8,768]{1,0:T(8,128)S(1)}, u32[]{:S(2)}, u32[]{:S(2)}) collective-permute-start(f32[8,768]{1,0:T(8,128)S(1)} %get-tuple-element.44.refs_8_), channel_id=1, source_target_pairs={{0,16},{8,24},{16,0},{24,8},{1,17},{9,25},{17,1},{25,9},{2,18},{10... | collective-permute-start | bytes 73736 | tf_op jit(solution)/shard_map/merge/ppermute | solution.py:383
  26.2 1.1 %collective-permute-start.11 = (f32[8,768]{1,0:T(8,128)S(1)}, f32[8,768]{1,0:T(8,128)S(1)}, u32[]{:S(2)}, u32[]{:S(2)}) collective-permute-start(f32[8,768]{1,0:T(8,128)S(1)} %get-tuple-element.44.refs_8_), channel_id=1, source_target_pairs={{0,24},{8,16},{16,8},{24,0},{1,25},{9,17},{17,9},{25,1},{2,26},{10... | collective-permute-start | bytes 73736 | tf_op jit(solution)/shard_map/merge/ppermute | solution.py:383
  27.3 1.3 %collective-permute-done.8.refs_2_ = bf16[192,256]{1,0:T(8,128)(2,1)S(1)} collective-permute-done((bf16[192,256]{1,0:T(8,128)(2,1)S(1)}, bf16[192,256]{1,0:T(8,128)(2,1)S(1)}, u32[]{:S(2)}, u32[]{:S(2)}) %collective-permute-start.8) | collective-permute-done | bytes 98336 | tf_op jit(solution)/shard_map/merge/ppermute | solution.py:383
  28.6 0.0 collective-permute-done.9.refs_3_
  28.6 0.0 collective-permute-start.10
  28.6 2.1 %collective-permute-start.13 = (bf16[192,256]{1,0:T(8,128)(2,1)S(1)}, bf16[192,256]{1,0:T(8,128)(2,1)S(1)}, u32[]{:S(2)}, u32[]{:S(2)}) collective-permute-start(bf16[192,256]{1,0:T(8,128)(2,1)S(1)} %get-tuple-element.51), channel_id=1, source_target_pairs={{0,24},{8,16},{16,8},{24,0},{1,25},{9,17},{17,9},{25,1},{2,26},{10... | collective-permute-start | bytes 294920 | tf_op jit(solution)/shard_map/merge/ppermute | solution.py:383
  30.7 0.0 collective-permute-done.12.refs_11_
  30.7 0.0 collective-permute-done.11.refs_10_
  30.7 0.6 %collective-permute-done.10.refs_9_ = f32[8,768]{1,0:T(8,128)S(1)} collective-permute-done((f32[8,768]{1,0:T(8,128)S(1)}, f32[8,768]{1,0:T(8,128)S(1)}, u32[]{:S(2)}, u32[]{:S(2)}) %collective-permute-start.10) | collective-permute-done | bytes 24608 | tf_op jit(solution)/shard_map/merge/ppermute | solution.py:383
  31.3 2.9 %gradients.2 = (f32[2,128,768]{2,1,0:T(8,128)S(1)}, f32[2,768]{1,0:T(2,128)S(1)}, f32[2,768]{1,0:T(2,128)S(1)}, f32[192,128]{1,0:T(8,128)S(1)}, bf16[2,2,192,256...) custom-call(bf16[2,192,256]{2,1,0:T(8,128)(2,1)S(1)} %get-tuple-element.37.refs_0_, ...), custom_call_target="tpu_custom_call" | custom-call | flops 12079595520 | bytes 3354624 | tf_op jit(solution)/shard_map/gradients/pallas_call | solution.py:345
  34.2 1.7 %collective-permute-start.17 = (bf16[2,2,192,256]{3,2,1,0:T(8,128)(2,1)S(1)}, bf16[2,2,192,256]{3,2,1,0:T(8,128)(2,1)S(1)}, u32[]{:S(2)}, u32[]{:S(2)}) collective-permute-start(bf16[2,2,192,256]{3,2,1,0:T(8,128)(2,1)S(1)} %get-tuple-element.62), channel_id=1, source_target_pairs={{0,1},{1,0},{2,3},{3,2},{4,5},{5,4},{6,7},{7,6},{8,9},{9,8},{10,11... | collective-permute-start | bytes 1179656 | tf_op jit(solution)/shard_map/gradients/ppermute | solution.py:446
  35.9 3.2 %collective-permute-start.18 = (bf16[2,2,192,256]{3,2,1,0:T(8,128)(2,1)S(1)}, bf16[2,2,192,256]{3,2,1,0:T(8,128)(2,1)S(1)}, u32[]{:S(2)}, u32[]{:S(2)}) collective-permute-start(bf16[2,2,192,256]{3,2,1,0:T(8,128)(2,1)S(1)} %get-tuple-element.63), channel_id=1, source_target_pairs={{0,0},{1,2},{2,1},{3,3},{4,4},{5,6},{6,5},{7,7},{8,8},{9,10},{10,9... | collective-permute-start | bytes 1179656 | tf_op jit(solution)/shard_map/gradients/ppermute | solution.py:446
  39.1 1.7 %gradients.3 = (bf16[192,256]{1,0:T(8,128)(2,1)S(1)}, bf16[192,256]{1,0:T(8,128)(2,1)S(1)}, bf16[192,256]{1,0:T(8,128)(2,1)S(1)}, bf16[192,256]{1,0:T(8,128)(2,1)S(1)}, bf16[2,2,192,256]{3,2,1,0:T(8,128)(2,1)S(1)}) custom-call(bf16[2,192,256]{2,1,0:T(8,128)(2,1)S(1)} %get-tuple-element.37.refs_0_, bf16[2,192,256]{2,1,0:T(8,128)(2,1)S(1)} %collective-permute-done.refs_1_, ...), custom_call_target="tpu_custom_call" | custom-call | flops 6039797760 | bytes 2764800 | tf_op jit(solution)/shard_map/gradients/pallas_call | solution.py:345
  40.8 0.0 collective-permute-done.13.refs_1_
  40.8 1.7 %collective-permute-start.14 = (bf16[192,256]{1,0:T(8,128)(2,1)S(1)}, bf16[192,256]{1,0:T(8,128)(2,1)S(1)}, u32[]{:S(2)}, u32[]{:S(2)}) collective-permute-start(bf16[192,256]{1,0:T(8,128)(2,1)S(1)} %get-tuple-element.58), channel_id=1, source_target_pairs={{0,16},{8,24},{16,0},{24,8},{1,17},{9,25},{17,1},{25,9},{2,18},{10... | collective-permute-start | bytes 294920 | tf_op jit(solution)/shard_map/return/ppermute | solution.py:383
  42.5 1.2 %collective-permute-start.15 = (bf16[192,256]{1,0:T(8,128)(2,1)S(1)}, bf16[192,256]{1,0:T(8,128)(2,1)S(1)}, u32[]{:S(2)}, u32[]{:S(2)}) collective-permute-start(bf16[192,256]{1,0:T(8,128)(2,1)S(1)} %get-tuple-element.59), channel_id=1, source_target_pairs={{0,24},{8,16},{16,8},{24,0},{1,25},{9,17},{17,9},{25,1},{2,26},{10... | collective-permute-start | bytes 294920 | tf_op jit(solution)/shard_map/return/ppermute | solution.py:383
  43.7 0.0 collective-permute-start.16
  43.7 0.0 collective-permute-done.17.refs_9_
  43.7 1.6 %collective-permute-done.18.refs_10_ = bf16[2,2,192,256]{3,2,1,0:T(8,128)(2,1)S(1)} collective-permute-done((bf16[2,2,192,256]{3,2,1,0:T(8,128)(2,1)S(1)}, bf16[2,2,192,256]{3,2,1,0:T(8,128)(2,1)S(1)}, u32[]{:S(2)}, u32[]{:S(2)}) %collective-permute-start.18) | collective-permute-done | bytes 393248 | tf_op jit(solution)/shard_map/gradients/ppermute | solution.py:446
  45.3 0.1 fusion.1
  45.4 0.4 collective-permute-start.20
  45.8 1.2 %collective-permute-start.19 = (bf16[192,256]{1,0:T(8,128)(2,1)S(1)}, bf16[192,256]{1,0:T(8,128)(2,1)S(1)}, u32[]{:S(2)}, u32[]{:S(2)}) collective-permute-start(bf16[192,256]{1,0:T(8,128)(2,1)S(1)} %get-tuple-element.71), channel_id=1, source_target_pairs={{0,4},{4,0},{1,5},{5,1},{2,6},{6,2},{3,7},{7,3},{8,12},{12,8},{9,1... | collective-permute-start | bytes 294920 | tf_op jit(solution)/shard_map/return/ppermute | solution.py:456
  46.9 2.6 %collective-permute-done.14.refs_5_ = bf16[192,256]{1,0:T(8,128)(2,1)S(1)} collective-permute-done((bf16[192,256]{1,0:T(8,128)(2,1)S(1)}, bf16[192,256]{1,0:T(8,128)(2,1)S(1)}, u32[]{:S(2)}, u32[]{:S(2)}) %collective-permute-start.14) | collective-permute-done | bytes 98336 | tf_op jit(solution)/shard_map/return/ppermute | solution.py:383
  49.5 0.0 collective-permute-done.15.refs_6_
  49.5 0.3 collective-permute-done.16.refs_7_
  49.8 0.0 collective-permute-done.20.refs_12_
  49.8 0.1 collective-permute-done.19.refs_11_
  50.0 1.2 %finish.1 = (bf16[192,256]{1,0:T(8,128)(2,1)}, bf16[192,256]{1,0:T(8,128)(2,1)}, bf16[192,256]{1,0:T(8,128)(2,1)}, bf16[192,256]{1,0:T(8,128)(2,1)}) custom-call(bf16[192,256]{1,0:T(8,128)(2,1)S(1)} %get-tuple-element.39.refs_0_, bf16[192,256]{1,0:T(8,128)(2,1)S(1)} %collective-permute-done.13.refs_1_, bf16[192,256]{1,0:T(8,128)(2,1)S(1)} %collective-permute-done.8.refs_2_, ...), custom_call_target="tpu_custom_call" | custom-call | bytes 2949120 | tf_op jit(solution)/shard_map/finish/pallas_call | solution.py:345
Async XLA Ops:
  1.9 10.3 %collective-permute-start.4 = (bf16[2,192,256]{2,1,0:T(8,128)(2,1)S(1)}, bf16[2,192,256]{2,1,0:T(8,128)(2,1)S(1)}, u32[]{:S(2)}, u32[]{:S(2)}) collective-permute-start(bf16[2,192,256]{2,1,0:T(8,128)(2,1)S(1)} %get-tuple-element.38.refs_3_.refs_1_.refs_4_), channel_id=1, source_target_pairs={{0,4},{4,0},{1,5},{5,1},{2,6},{6,2},{3,7},{7,3},{8,12},{12,8},{9,1... | collective-permute-start | bytes 589832 | tf_op jit(solution)/shard_map/halo/ppermute | solution.py:388
  4.0 10.9 %collective-permute-start.1 = (bf16[2,192,256]{2,1,0:T(8,128)(2,1)S(1)}, bf16[2,192,256]{2,1,0:T(8,128)(2,1)S(1)}, u32[]{:S(2)}, u32[]{:S(2)}) collective-permute-start(bf16[2,192,256]{2,1,0:T(8,128)(2,1)S(1)} %get-tuple-element.37.refs_0_), channel_id=1, source_target_pairs={{0,16},{8,24},{16,0},{24,8},{1,17},{9,25},{17,1},{25,9},{2,18},{10... | collective-permute-start | bytes 589832 | tf_op jit(solution)/shard_map/halo/ppermute | solution.py:383
  6.3 10.2 %collective-permute-start = (bf16[2,192,256]{2,1,0:T(8,128)(2,1)S(1)}, bf16[2,192,256]{2,1,0:T(8,128)(2,1)S(1)}, u32[]{:S(2)}, u32[]{:S(2)}) collective-permute-start(bf16[2,192,256]{2,1,0:T(8,128)(2,1)S(1)} %get-tuple-element.37.refs_0_), channel_id=1, source_target_pairs={{0,8},{8,0},{16,24},{24,16},{1,9},{9,1},{17,25},{25,17},{2,10},{10... | collective-permute-start | bytes 589832 | tf_op jit(solution)/shard_map/halo/ppermute | solution.py:383
  7.6 9.2 %collective-permute-start.3 = (bf16[2,192,256]{2,1,0:T(8,128)(2,1)S(1)}, bf16[2,192,256]{2,1,0:T(8,128)(2,1)S(1)}, u32[]{:S(2)}, u32[]{:S(2)}) collective-permute-start(bf16[2,192,256]{2,1,0:T(8,128)(2,1)S(1)} %get-tuple-element.38.refs_3_.refs_1_.refs_4_), channel_id=1, source_target_pairs={{0,0},{1,2},{2,1},{3,3},{4,4},{5,6},{6,5},{7,7},{8,8},{9,10},{10,9... | collective-permute-start | bytes 589832 | tf_op jit(solution)/shard_map/halo/ppermute | solution.py:393
  12.2 4.7 %collective-permute-start.2 = (bf16[2,192,256]{2,1,0:T(8,128)(2,1)S(1)}, bf16[2,192,256]{2,1,0:T(8,128)(2,1)S(1)}, u32[]{:S(2)}, u32[]{:S(2)}) collective-permute-start(bf16[2,192,256]{2,1,0:T(8,128)(2,1)S(1)} %get-tuple-element.38.refs_3_.refs_1_.refs_4_), channel_id=1, source_target_pairs={{0,1},{1,0},{2,3},{3,2},{4,5},{5,4},{6,7},{7,6},{8,9},{9,8},{10,11... | collective-permute-start | bytes 589832 | tf_op jit(solution)/shard_map/halo/ppermute | solution.py:393
  12.2 7.0 %collective-permute-start.6 = (bf16[2,192,256]{2,1,0:T(8,128)(2,1)S(1)}, bf16[2,192,256]{2,1,0:T(8,128)(2,1)S(1)}, u32[]{:S(2)}, u32[]{:S(2)}) collective-permute-start(bf16[2,192,256]{2,1,0:T(8,128)(2,1)S(1)} %collective-permute-done.4.refs_6_.refs_4_.refs_5_), channel_id=1, source_target_pairs={{0,0},{1,2},{2,1},{3,3},{4,4},{5,6},{6,5},{7,7},{8,8},{9,10},{10,9... | collective-permute-start | bytes 589832 | tf_op jit(solution)/shard_map/halo/ppermute | solution.py:393
  14.9 4.4 %collective-permute-start.5 = (bf16[2,192,256]{2,1,0:T(8,128)(2,1)S(1)}, bf16[2,192,256]{2,1,0:T(8,128)(2,1)S(1)}, u32[]{:S(2)}, u32[]{:S(2)}) collective-permute-start(bf16[2,192,256]{2,1,0:T(8,128)(2,1)S(1)} %collective-permute-done.4.refs_6_.refs_4_.refs_5_), channel_id=1, source_target_pairs={{0,1},{1,0},{2,3},{3,2},{4,5},{5,4},{6,7},{7,6},{8,9},{9,8},{10,11... | collective-permute-start | bytes 589832 | tf_op jit(solution)/shard_map/halo/ppermute | solution.py:393
  16.5 6.9 %collective-permute-start.7 = (bf16[2,192,256]{2,1,0:T(8,128)(2,1)S(1)}, bf16[2,192,256]{2,1,0:T(8,128)(2,1)S(1)}, u32[]{:S(2)}, u32[]{:S(2)}) collective-permute-start(bf16[2,192,256]{2,1,0:T(8,128)(2,1)S(1)} %collective-permute-done.1.refs_2_), channel_id=1, source_target_pairs={{0,8},{8,0},{16,24},{24,16},{1,9},{9,1},{17,25},{25,17},{2,10},{10... | collective-permute-start | bytes 589832 | tf_op jit(solution)/shard_map/halo/ppermute | solution.py:383
  21.6 7.0 %collective-permute-start.8 = (bf16[192,256]{1,0:T(8,128)(2,1)S(1)}, bf16[192,256]{1,0:T(8,128)(2,1)S(1)}, u32[]{:S(2)}, u32[]{:S(2)}) collective-permute-start(bf16[192,256]{1,0:T(8,128)(2,1)S(1)} %get-tuple-element.42), channel_id=1, source_target_pairs={{0,16},{8,24},{16,0},{24,8},{1,17},{9,25},{17,1},{25,9},{2,18},{10... | collective-permute-start | bytes 294920 | tf_op jit(solution)/shard_map/merge/ppermute | solution.py:383
  22.4 6.2 %collective-permute-start.9 = (bf16[192,256]{1,0:T(8,128)(2,1)S(1)}, bf16[192,256]{1,0:T(8,128)(2,1)S(1)}, u32[]{:S(2)}, u32[]{:S(2)}) collective-permute-start(bf16[192,256]{1,0:T(8,128)(2,1)S(1)} %get-tuple-element.43), channel_id=1, source_target_pairs={{0,8},{8,0},{16,24},{24,16},{1,9},{9,1},{17,25},{25,17},{2,10},{10... | collective-permute-start | bytes 294920 | tf_op jit(solution)/shard_map/merge/ppermute | solution.py:383
  24.4 6.3 %collective-permute-start.12 = (f32[8,768]{1,0:T(8,128)S(1)}, f32[8,768]{1,0:T(8,128)S(1)}, u32[]{:S(2)}, u32[]{:S(2)}) collective-permute-start(f32[8,768]{1,0:T(8,128)S(1)} %get-tuple-element.44.refs_8_), channel_id=1, source_target_pairs={{0,16},{8,24},{16,0},{24,8},{1,17},{9,25},{17,1},{25,9},{2,18},{10... | collective-permute-start | bytes 73736 | tf_op jit(solution)/shard_map/merge/ppermute | solution.py:383
  26.2 4.5 %collective-permute-start.11 = (f32[8,768]{1,0:T(8,128)S(1)}, f32[8,768]{1,0:T(8,128)S(1)}, u32[]{:S(2)}, u32[]{:S(2)}) collective-permute-start(f32[8,768]{1,0:T(8,128)S(1)} %get-tuple-element.44.refs_8_), channel_id=1, source_target_pairs={{0,24},{8,16},{16,8},{24,0},{1,25},{9,17},{17,9},{25,1},{2,26},{10... | collective-permute-start | bytes 73736 | tf_op jit(solution)/shard_map/merge/ppermute | solution.py:383
  28.6 2.7 %collective-permute-start.10 = (f32[8,768]{1,0:T(8,128)S(1)}, f32[8,768]{1,0:T(8,128)S(1)}, u32[]{:S(2)}, u32[]{:S(2)}) collective-permute-start(f32[8,768]{1,0:T(8,128)S(1)} %get-tuple-element.44.refs_8_), channel_id=1, source_target_pairs={{0,8},{8,0},{16,24},{24,16},{1,9},{9,1},{17,25},{25,17},{2,10},{10... | collective-permute-start | bytes 73736 | tf_op jit(solution)/shard_map/merge/ppermute | solution.py:383
  28.6 12.2 %collective-permute-start.13 = (bf16[192,256]{1,0:T(8,128)(2,1)S(1)}, bf16[192,256]{1,0:T(8,128)(2,1)S(1)}, u32[]{:S(2)}, u32[]{:S(2)}) collective-permute-start(bf16[192,256]{1,0:T(8,128)(2,1)S(1)} %get-tuple-element.51), channel_id=1, source_target_pairs={{0,24},{8,16},{16,8},{24,0},{1,25},{9,17},{17,9},{25,1},{2,26},{10... | collective-permute-start | bytes 294920 | tf_op jit(solution)/shard_map/merge/ppermute | solution.py:383
  34.2 9.5 %collective-permute-start.17 = (bf16[2,2,192,256]{3,2,1,0:T(8,128)(2,1)S(1)}, bf16[2,2,192,256]{3,2,1,0:T(8,128)(2,1)S(1)}, u32[]{:S(2)}, u32[]{:S(2)}) collective-permute-start(bf16[2,2,192,256]{3,2,1,0:T(8,128)(2,1)S(1)} %get-tuple-element.62), channel_id=1, source_target_pairs={{0,1},{1,0},{2,3},{3,2},{4,5},{5,4},{6,7},{7,6},{8,9},{9,8},{10,11... | collective-permute-start | bytes 1179656 | tf_op jit(solution)/shard_map/gradients/ppermute | solution.py:446
  35.9 9.4 %collective-permute-start.18 = (bf16[2,2,192,256]{3,2,1,0:T(8,128)(2,1)S(1)}, bf16[2,2,192,256]{3,2,1,0:T(8,128)(2,1)S(1)}, u32[]{:S(2)}, u32[]{:S(2)}) collective-permute-start(bf16[2,2,192,256]{3,2,1,0:T(8,128)(2,1)S(1)} %get-tuple-element.63), channel_id=1, source_target_pairs={{0,0},{1,2},{2,1},{3,3},{4,4},{5,6},{6,5},{7,7},{8,8},{9,10},{10,9... | collective-permute-start | bytes 1179656 | tf_op jit(solution)/shard_map/gradients/ppermute | solution.py:446
  40.8 8.7 %collective-permute-start.14 = (bf16[192,256]{1,0:T(8,128)(2,1)S(1)}, bf16[192,256]{1,0:T(8,128)(2,1)S(1)}, u32[]{:S(2)}, u32[]{:S(2)}) collective-permute-start(bf16[192,256]{1,0:T(8,128)(2,1)S(1)} %get-tuple-element.58), channel_id=1, source_target_pairs={{0,16},{8,24},{16,0},{24,8},{1,17},{9,25},{17,1},{25,9},{2,18},{10... | collective-permute-start | bytes 294920 | tf_op jit(solution)/shard_map/return/ppermute | solution.py:383
  42.5 7.0 %collective-permute-start.15 = (bf16[192,256]{1,0:T(8,128)(2,1)S(1)}, bf16[192,256]{1,0:T(8,128)(2,1)S(1)}, u32[]{:S(2)}, u32[]{:S(2)}) collective-permute-start(bf16[192,256]{1,0:T(8,128)(2,1)S(1)} %get-tuple-element.59), channel_id=1, source_target_pairs={{0,24},{8,16},{16,8},{24,0},{1,25},{9,17},{17,9},{25,1},{2,26},{10... | collective-permute-start | bytes 294920 | tf_op jit(solution)/shard_map/return/ppermute | solution.py:383
  43.7 6.1 %collective-permute-start.16 = (bf16[192,256]{1,0:T(8,128)(2,1)S(1)}, bf16[192,256]{1,0:T(8,128)(2,1)S(1)}, u32[]{:S(2)}, u32[]{:S(2)}) collective-permute-start(bf16[192,256]{1,0:T(8,128)(2,1)S(1)} %get-tuple-element.60), channel_id=1, source_target_pairs={{0,8},{8,0},{16,24},{24,16},{1,9},{9,1},{17,25},{25,17},{2,10},{10... | collective-permute-start | bytes 294920 | tf_op jit(solution)/shard_map/return/ppermute | solution.py:383
  45.4 4.4 %collective-permute-start.20 = (bf16[192,256]{1,0:T(8,128)(2,1)S(1)}, bf16[192,256]{1,0:T(8,128)(2,1)S(1)}, u32[]{:S(2)}, u32[]{:S(2)}) collective-permute-start(bf16[192,256]{1,0:T(8,128)(2,1)S(1)} %get-tuple-element.70), channel_id=1, source_target_pairs={{0,4},{4,0},{1,5},{5,1},{2,6},{6,2},{3,7},{7,3},{8,12},{12,8},{9,1... | collective-permute-start | bytes 294920 | tf_op jit(solution)/shard_map/return/ppermute | solution.py:456
  45.8 4.2 %collective-permute-start.19 = (bf16[192,256]{1,0:T(8,128)(2,1)S(1)}, bf16[192,256]{1,0:T(8,128)(2,1)S(1)}, u32[]{:S(2)}, u32[]{:S(2)}) collective-permute-start(bf16[192,256]{1,0:T(8,128)(2,1)S(1)} %get-tuple-element.71), channel_id=1, source_target_pairs={{0,4},{4,0},{1,5},{5,1},{2,6},{6,2},{3,7},{7,3},{8,12},{12,8},{9,1... | collective-permute-start | bytes 294920 | tf_op jit(solution)/shard_map/return/ppermute | solution.py:456

commit v20 on v19

--- a/solution.py
+++ b/solution.py
@@ -299,46 +299,41 @@
             dq_out[head] = dq
 
 
-def finish_kernel(cols, rows, *refs):
-    o_refs, dq_refs, refs = refs[:4], refs[4:8], refs[8:]
-    col_refs, row_refs = refs[:cols], refs[cols : cols + 2 * rows]
-    share_ref, rope_ref, *outs, made_ref, sems = refs[cols + 2 * rows :]
-    copies = [
-        pltpu.make_async_copy(made_ref.at[i], out, sems.at[i]) for i, out in enumerate(outs)
-    ]
-    tables = [rope_ref[plane] for plane in range(3)]
-    cuts = [head_slice(head) for head in range(HEADS)]
-
-    def summed(parts):
-        return functools.reduce(jnp.add, [part.astype(F32) for part in parts])
-
-    def returned(which, cut):
-        return summed(
-            [ref[0, which, :, cut] for ref in col_refs] + [ref[:, cut] for ref in row_refs[which::2]]
-        )
-
-    for head, cut in enumerate(cuts):
+def summed(parts):
+    return functools.reduce(jnp.add, [part.astype(F32) for part in parts])
+
+
+def gather_kernel(cols, *refs):
+    o_refs, col_refs = refs[:4], refs[4 : 4 + cols]
+    share_ref, out_ref, sum_ref = refs[4 + cols :]
+    for head in range(HEADS):
+        cut = head_slice(head)
         weighted = []
         for d, o_ref in zip((0, 3, 2, 1), o_refs):
             weight = share_ref[:, 4 * head + d : 4 * head + d + 1]
             weighted.append(o_ref[:, cut].astype(F32) * weight)
-        made_ref[0, :, cut] = functools.reduce(jnp.add, weighted).astype(BF16)
-    copies[0].start()
-    for cut in cuts:
-        made_ref[3, :, cut] = returned(1, cut).astype(BF16)
-    copies[3].start()
-    for cut in cuts:
+        out_ref[:, cut] = functools.reduce(jnp.add, weighted).astype(BF16)
+        for which in range(2):
+            sum_ref[which, :, cut] = summed([ref[0, which, :, cut] for ref in col_refs])
+
+
+def finish_kernel(rows, *refs):
+    dq_refs, row_refs = refs[:4], refs[4 : 4 + 2 * rows]
+    sum_ref, rope_ref, dq_out, dk_out, dv_out = refs[4 + 2 * rows :]
+    tables = [rope_ref[plane] for plane in range(3)]
+    for head in range(HEADS):
+        cut = head_slice(head)
         dq = summed([ref[:, cut] for ref in dq_refs])
-        made_ref[1, :, cut] = turn(dq, *tables, -1.0).astype(BF16)
-    copies[1].start()
-    for cut in cuts:
-        made_ref[2, :, cut] = turn(returned(0, cut), *tables, -1.0).astype(BF16)
-    copies[2].start()
-    for copy in copies:
-        copy.wait()
-
-
-def call(kernel, out_shape, args, flops=0, exps=0, scratch=(), space=pltpu.VMEM, out_space=pltpu.VMEM):
+        dq_out[:, cut] = turn(dq, *tables, -1.0).astype(BF16)
+        dk, dv = [
+            summed([sum_ref[which, :, cut]] + [ref[:, cut] for ref in row_refs[which::2]])
+            for which in range(2)
+        ]
+        dk_out[:, cut] = turn(dk, *tables, -1.0).astype(BF16)
+        dv_out[:, cut] = dv.astype(BF16)
+
+
+def call(kernel, out_shape, args, flops=0, exps=0, scratch=(), space=pltpu.VMEM):
     shapes = jax.tree.leaves(out_shape)
     flops *= 8
     moved = sum(math.prod(x.shape) * x.dtype.itemsize for x in list(args) + shapes)
@@ -346,7 +341,6 @@
         kernel,
         out_shape=out_shape,
         in_specs=[pl.BlockSpec(memory_space=space)] * len(args),
-        out_specs=jax.tree.map(lambda _: pl.BlockSpec(memory_space=out_space), out_shape),
         scratch_shapes=list(scratch),
         compiler_params=pltpu.CompilerParams(vmem_limit_bytes=VMEM_LIMIT),
         cost_estimate=pl.CostEstimate(flops=flops, bytes_accessed=moved, transcendentals=exps),
@@ -456,14 +450,17 @@
                 row_parts.append(lax.ppermute(partial_sum, "ha", pairs))
 
     with jax.named_scope("finish"):
+        attended, sums = call(
+            functools.partial(gather_kernel, grid_cols),
+            (plain, real(2, cells, chan)),
+            (o0, *outs, *col_parts, shares),
+        )
         results = call(
-            functools.partial(finish_kernel, grid_cols, len(row_parts) // 2),
-            [plain] * 4,
-            (o0, *outs, *dqs, *col_parts, *row_parts, shares, rope),
-            scratch=[pltpu.VMEM((4, cells, chan), BF16), pltpu.SemaphoreType.DMA((4,))],
-            out_space=pltpu.HBM,
+            functools.partial(finish_kernel, len(row_parts) // 2),
+            [plain] * 3,
+            (*dqs, *row_parts, sums, rope),
         )
-    return tuple(x.reshape(query_in.shape) for x in results)
+    return tuple(x.reshape(query_in.shape) for x in (attended, *results))
 
 
 def solution(mesh):

time: 51.4 us -> 51.1 us (level)
  waiting for transfers between devices: 9.64 us -> 8.69 us
  Pallas kernels: 10.4 us -> 11.1 us
    ppermute x12, waiting for transfers between devices: 5.5 us -> 4.55 us  [other_frames(): lax.ppermute(x, 'ta', [(i, i ^ distance) for i in range(sizes['ta'])])]
    pallas_call x6 -> x7, Pallas kernels: 10.4 us -> 11.1 us  [call(): pl.pallas_call(kernel, out_shape=out_shape, in_specs=[pl.BlockSpec(memory...]
  transfers between devices with their start and end apart: 21 -> 21, of which waited for: 8 -> 8; matrix products, arithmetic and copies ran while one was open for 0% -> 0% of each run, Pallas kernels for 16% -> 18%
where the time goes in v20:
time: 51.1 us; the launch traced here: 50.9 us
  starting transfers between devices  30.3 us (59%)
  Pallas kernels  11.1 us (22%)
  waiting for transfers between devices  8.69 us (17%)
  between operations  0.72 us (1%)
    ppermute x12, starting transfers between devices, other_frames(): lax.ppermute(x, 'ta', [(i, i ^ distance) for i in range(sizes['ta'])])  13.6 us
    pallas_call x7, Pallas kernels, call(): pl.pallas_call(kernel, out_shape=out_shape, in_specs=[pl.BlockSpec(memory...  11.1 us
    ppermute x4, starting transfers between devices, shards(): lax.ppermute(block, 'wa', pairs)  8.2 us
    ppermute x2, starting transfers between devices, shards(): sides = [lax.ppermute(x, 'wa', pairs) for x, pairs in zip(sides, col_sides)]  4.91 us
    ppermute x12, waiting for transfers between devices, other_frames(): lax.ppermute(x, 'ta', [(i, i ^ distance) for i in range(sizes['ta'])])  4.55 us
    ppermute x4, waiting for transfers between devices, shards(): lax.ppermute(block, 'wa', pairs)  2.4 us
    ppermute x1, starting transfers between devices, shards(): kv_rows = [kv] + [lax.ppermute(kv, 'ha', pairs) for pairs in row_sides]  2.11 us
    ppermute x2, waiting for transfers between devices, shards(): sides = [lax.ppermute(x, 'wa', pairs) for x, pairs in zip(sides, col_sides)]  1.59 us
  transfers between devices with their start and end apart: 21, of which 8 were waited for; matrix products, arithmetic and copies ran while one was open for 0% of the time, Pallas kernels for 18%

profile of v20, /device:TPU:1, one launch (start us, length us, event | category | flops | bytes accessed | tf_op | source)
XLA Modules:
  0.0 50.9 jit_solution(16710712895996111610)
XLA Ops:
  0.6 1.3 %rotate.1 = (bf16[2,192,256]{2,1,0:T(8,128)(2,1)S(1)}, bf16[2,192,256]{2,1,0:T(8,128)(2,1)S(1)}, f32[3,192,128]{2,1,0:T(8,128)S(1)}) custom-call(bf16[192,256]{1,0:T(8,128)(2,1)} %bitcast.12, bf16[192,256]{1,0:T(8,128)(2,1)} %bitcast.13, bf16[192,256]{1,0:T(8,128)(2,1)} %bitcast.14, bf16[192,256]{1,0:T(8,128)(2,1)} %bitcast.15, ...), custom_call_target="tpu_custom_call" | custom-call | bytes 1179648 | tf_op jit(solution)/shard_map/rotate/pallas_call | solution.py:340
  1.9 2.1 %collective-permute-start.4 = (bf16[2,192,256]{2,1,0:T(8,128)(2,1)S(1)}, bf16[2,192,256]{2,1,0:T(8,128)(2,1)S(1)}, u32[]{:S(2)}, u32[]{:S(2)}) collective-permute-start(bf16[2,192,256]{2,1,0:T(8,128)(2,1)S(1)} %get-tuple-element.39.refs_3_.refs_1_.refs_4_), channel_id=1, source_target_pairs={{0,4},{4,0},{1,5},{5,1},{2,6},{6,2},{3,7},{7,3},{8,12},{12,8},{9,1... | collective-permute-start | bytes 589832 | tf_op jit(solution)/shard_map/halo/ppermute | solution.py:382
  4.0 2.3 %collective-permute-start.1 = (bf16[2,192,256]{2,1,0:T(8,128)(2,1)S(1)}, bf16[2,192,256]{2,1,0:T(8,128)(2,1)S(1)}, u32[]{:S(2)}, u32[]{:S(2)}) collective-permute-start(bf16[2,192,256]{2,1,0:T(8,128)(2,1)S(1)} %get-tuple-element.38.refs_0_), channel_id=1, source_target_pairs={{0,16},{8,24},{16,0},{24,8},{1,17},{9,25},{17,1},{25,9},{2,18},{10... | collective-permute-start | bytes 589832 | tf_op jit(solution)/shard_map/halo/ppermute | solution.py:377
  6.3 1.3 %collective-permute-start = (bf16[2,192,256]{2,1,0:T(8,128)(2,1)S(1)}, bf16[2,192,256]{2,1,0:T(8,128)(2,1)S(1)}, u32[]{:S(2)}, u32[]{:S(2)}) collective-permute-start(bf16[2,192,256]{2,1,0:T(8,128)(2,1)S(1)} %get-tuple-element.38.refs_0_), channel_id=1, source_target_pairs={{0,8},{8,0},{16,24},{24,16},{1,9},{9,1},{17,25},{25,17},{2,10},{10... | collective-permute-start | bytes 589832 | tf_op jit(solution)/shard_map/halo/ppermute | solution.py:377
  7.6 4.5 %collective-permute-start.3 = (bf16[2,192,256]{2,1,0:T(8,128)(2,1)S(1)}, bf16[2,192,256]{2,1,0:T(8,128)(2,1)S(1)}, u32[]{:S(2)}, u32[]{:S(2)}) collective-permute-start(bf16[2,192,256]{2,1,0:T(8,128)(2,1)S(1)} %get-tuple-element.39.refs_3_.refs_1_.refs_4_), channel_id=1, source_target_pairs={{0,0},{1,2},{2,1},{3,3},{4,4},{5,6},{6,5},{7,7},{8,8},{9,10},{10,9... | collective-permute-start | bytes 589832 | tf_op jit(solution)/shard_map/halo/ppermute | solution.py:387
  12.2 0.1 collective-permute-start.2
  12.2 0.0 collective-permute-done.4.refs_6_.refs_4_.refs_5_
  12.2 1.9 %collective-permute-start.6 = (bf16[2,192,256]{2,1,0:T(8,128)(2,1)S(1)}, bf16[2,192,256]{2,1,0:T(8,128)(2,1)S(1)}, u32[]{:S(2)}, u32[]{:S(2)}) collective-permute-start(bf16[2,192,256]{2,1,0:T(8,128)(2,1)S(1)} %collective-permute-done.4.refs_6_.refs_4_.refs_5_), channel_id=1, source_target_pairs={{0,0},{1,2},{2,1},{3,3},{4,4},{5,6},{6,5},{7,7},{8,8},{9,10},{10,9... | collective-permute-start | bytes 589832 | tf_op jit(solution)/shard_map/halo/ppermute | solution.py:387
  14.2 0.7 %collective-permute-done.1.refs_2_ = bf16[2,192,256]{2,1,0:T(8,128)(2,1)S(1)} collective-permute-done((bf16[2,192,256]{2,1,0:T(8,128)(2,1)S(1)}, bf16[2,192,256]{2,1,0:T(8,128)(2,1)S(1)}, u32[]{:S(2)}, u32[]{:S(2)}) %collective-permute-start.1) | collective-permute-done | bytes 196640 | tf_op jit(solution)/shard_map/halo/ppermute | solution.py:377
  14.9 1.7 %collective-permute-start.5 = (bf16[2,192,256]{2,1,0:T(8,128)(2,1)S(1)}, bf16[2,192,256]{2,1,0:T(8,128)(2,1)S(1)}, u32[]{:S(2)}, u32[]{:S(2)}) collective-permute-start(bf16[2,192,256]{2,1,0:T(8,128)(2,1)S(1)} %collective-permute-done.4.refs_6_.refs_4_.refs_5_), channel_id=1, source_target_pairs={{0,1},{1,0},{2,3},{3,2},{4,5},{5,4},{6,7},{7,6},{8,9},{9,8},{10,11... | collective-permute-start | bytes 589832 | tf_op jit(solution)/shard_map/halo/ppermute | solution.py:387
  16.5 0.0 collective-permute-done.refs_1_
  16.5 0.3 collective-permute-start.7
  16.8 0.0 collective-permute-done.3.refs_5_.refs_3_.refs_6_
  16.8 0.0 collective-permute-done.2.refs_4_.refs_2_
  16.8 2.4 %collective-permute-done.6.refs_8_.refs_6_.refs_7_ = bf16[2,192,256]{2,1,0:T(8,128)(2,1)S(1)} collective-permute-done((bf16[2,192,256]{2,1,0:T(8,128)(2,1)S(1)}, bf16[2,192,256]{2,1,0:T(8,128)(2,1)S(1)}, u32[]{:S(2)}, u32[]{:S(2)}) %collective-permute-start.6) | collective-permute-done | bytes 196640 | tf_op jit(solution)/shard_map/halo/ppermute | solution.py:387
  19.2 0.0 collective-permute-done.5.refs_7_.refs_5_
  19.2 2.4 %attend.2 = (bf16[192,256]{1,0:T(8,128)(2,1)S(1)}, bf16[192,256]{1,0:T(8,128)(2,1)S(1)}, bf16[192,256]{1,0:T(8,128)(2,1)S(1)}, f32[576,128]{1,0:T(8,128)S(1)}) custom-call(bf16[2,192,256]{2,1,0:T(8,128)(2,1)S(1)} %get-tuple-element.38.refs_0_, bf16[2,192,256]{2,1,0:T(8,128)(2,1)S(1)} %collective-permute-done.refs_1_, ...), custom_call_target="tpu_custom_call" | custom-call | flops 5435817984 | bytes 2359296 | tf_op jit(solution)/shard_map/attend/pallas_call | solution.py:340
  21.6 0.8 %collective-permute-start.8 = (bf16[192,256]{1,0:T(8,128)(2,1)S(1)}, bf16[192,256]{1,0:T(8,128)(2,1)S(1)}, u32[]{:S(2)}, u32[]{:S(2)}) collective-permute-start(bf16[192,256]{1,0:T(8,128)(2,1)S(1)} %get-tuple-element.43), channel_id=1, source_target_pairs={{0,16},{8,24},{16,0},{24,8},{1,17},{9,25},{17,1},{25,9},{2,18},{10... | collective-permute-start | bytes 294920 | tf_op jit(solution)/shard_map/merge/ppermute | solution.py:377
  22.4 1.0 %collective-permute-start.9 = (bf16[192,256]{1,0:T(8,128)(2,1)S(1)}, bf16[192,256]{1,0:T(8,128)(2,1)S(1)}, u32[]{:S(2)}, u32[]{:S(2)}) collective-permute-start(bf16[192,256]{1,0:T(8,128)(2,1)S(1)} %get-tuple-element.44), channel_id=1, source_target_pairs={{0,8},{8,0},{16,24},{24,16},{1,9},{9,1},{17,25},{25,17},{2,10},{10... | collective-permute-start | bytes 294920 | tf_op jit(solution)/shard_map/merge/ppermute | solution.py:377
  23.4 0.0 collective-permute-done.7.refs_0_.refs_3_
  23.4 1.0 %attend.3 = (bf16[192,256]{1,0:T(8,128)(2,1)S(1)}, f32[8,768]{1,0:T(8,128)S(1)}) custom-call(bf16[2,192,256]{2,1,0:T(8,128)(2,1)S(1)} %collective-permute-done.7.refs_0_.refs_3_, bf16[2,192,256]{2,1,0:T(8,128)(2,1)S(1)} %get-tuple-element.39.refs_3_.refs_1_.refs_4_, bf16[2,192,256]{2,1,0:T(8,128)(2,1)S(1)} %collective-permute-done.2.refs_4_.refs_2_, ...), custom_call_target="tpu_custom_call" | custom-call | flops 1811939328 | bytes 1794048 | tf_op jit(solution)/shard_map/attend/pallas_call | solution.py:340
  24.4 1.8 %collective-permute-start.12 = (f32[8,768]{1,0:T(8,128)S(1)}, f32[8,768]{1,0:T(8,128)S(1)}, u32[]{:S(2)}, u32[]{:S(2)}) collective-permute-start(f32[8,768]{1,0:T(8,128)S(1)} %get-tuple-element.45.refs_8_), channel_id=1, source_target_pairs={{0,16},{8,24},{16,0},{24,8},{1,17},{9,25},{17,1},{25,9},{2,18},{10... | collective-permute-start | bytes 73736 | tf_op jit(solution)/shard_map/merge/ppermute | solution.py:377
  26.2 1.1 %collective-permute-start.11 = (f32[8,768]{1,0:T(8,128)S(1)}, f32[8,768]{1,0:T(8,128)S(1)}, u32[]{:S(2)}, u32[]{:S(2)}) collective-permute-start(f32[8,768]{1,0:T(8,128)S(1)} %get-tuple-element.45.refs_8_), channel_id=1, source_target_pairs={{0,24},{8,16},{16,8},{24,0},{1,25},{9,17},{17,9},{25,1},{2,26},{10... | collective-permute-start | bytes 73736 | tf_op jit(solution)/shard_map/merge/ppermute | solution.py:377
  27.3 1.3 %collective-permute-done.8.refs_2_ = bf16[192,256]{1,0:T(8,128)(2,1)S(1)} collective-permute-done((bf16[192,256]{1,0:T(8,128)(2,1)S(1)}, bf16[192,256]{1,0:T(8,128)(2,1)S(1)}, u32[]{:S(2)}, u32[]{:S(2)}) %collective-permute-start.8) | collective-permute-done | bytes 98336 | tf_op jit(solution)/shard_map/merge/ppermute | solution.py:377
  28.6 0.0 collective-permute-done.9.refs_3_
  28.6 0.0 collective-permute-start.10
  28.6 2.1 %collective-permute-start.13 = (bf16[192,256]{1,0:T(8,128)(2,1)S(1)}, bf16[192,256]{1,0:T(8,128)(2,1)S(1)}, u32[]{:S(2)}, u32[]{:S(2)}) collective-permute-start(bf16[192,256]{1,0:T(8,128)(2,1)S(1)} %get-tuple-element.52), channel_id=1, source_target_pairs={{0,24},{8,16},{16,8},{24,0},{1,25},{9,17},{17,9},{25,1},{2,26},{10... | collective-permute-start | bytes 294920 | tf_op jit(solution)/shard_map/merge/ppermute | solution.py:377
  30.7 0.0 collective-permute-done.12.refs_11_
  30.7 0.0 collective-permute-done.11.refs_10_
  30.7 0.6 %collective-permute-done.10.refs_9_ = f32[8,768]{1,0:T(8,128)S(1)} collective-permute-done((f32[8,768]{1,0:T(8,128)S(1)}, f32[8,768]{1,0:T(8,128)S(1)}, u32[]{:S(2)}, u32[]{:S(2)}) %collective-permute-start.10) | collective-permute-done | bytes 24608 | tf_op jit(solution)/shard_map/merge/ppermute | solution.py:377
  31.3 2.9 %gradients.2 = (f32[2,128,768]{2,1,0:T(8,128)S(1)}, f32[2,768]{1,0:T(2,128)S(1)}, f32[2,768]{1,0:T(2,128)S(1)}, f32[192,128]{1,0:T(8,128)S(1)}, bf16[2,2,192,256...) custom-call(bf16[2,192,256]{2,1,0:T(8,128)(2,1)S(1)} %get-tuple-element.38.refs_0_, ...), custom_call_target="tpu_custom_call" | custom-call | flops 12079595520 | bytes 3354624 | tf_op jit(solution)/shard_map/gradients/pallas_call | solution.py:340
  34.2 1.7 %collective-permute-start.14 = (bf16[2,2,192,256]{3,2,1,0:T(8,128)(2,1)S(1)}, bf16[2,2,192,256]{3,2,1,0:T(8,128)(2,1)S(1)}, u32[]{:S(2)}, u32[]{:S(2)}) collective-permute-start(bf16[2,2,192,256]{3,2,1,0:T(8,128)(2,1)S(1)} %get-tuple-element.59), channel_id=1, source_target_pairs={{0,1},{1,0},{2,3},{3,2},{4,5},{5,4},{6,7},{7,6},{8,9},{9,8},{10,11... | collective-permute-start | bytes 1179656 | tf_op jit(solution)/shard_map/gradients/ppermute | solution.py:440
  35.9 3.2 %collective-permute-start.15 = (bf16[2,2,192,256]{3,2,1,0:T(8,128)(2,1)S(1)}, bf16[2,2,192,256]{3,2,1,0:T(8,128)(2,1)S(1)}, u32[]{:S(2)}, u32[]{:S(2)}) collective-permute-start(bf16[2,2,192,256]{3,2,1,0:T(8,128)(2,1)S(1)} %get-tuple-element.60), channel_id=1, source_target_pairs={{0,0},{1,2},{2,1},{3,3},{4,4},{5,6},{6,5},{7,7},{8,8},{9,10},{10,9... | collective-permute-start | bytes 1179656 | tf_op jit(solution)/shard_map/gradients/ppermute | solution.py:440
  39.1 1.7 %gradients.3 = (bf16[192,256]{1,0:T(8,128)(2,1)S(1)}, bf16[192,256]{1,0:T(8,128)(2,1)S(1)}, bf16[192,256]{1,0:T(8,128)(2,1)S(1)}, bf16[192,256]{1,0:T(8,128)(2,1)S(1)}, bf16[2,2,192,256]{3,2,1,0:T(8,128)(2,1)S(1)}) custom-call(bf16[2,192,256]{2,1,0:T(8,128)(2,1)S(1)} %get-tuple-element.38.refs_0_, bf16[2,192,256]{2,1,0:T(8,128)(2,1)S(1)} %collective-permute-done.refs_1_, ...), custom_call_target="tpu_custom_call" | custom-call | flops 6039797760 | bytes 2764800 | tf_op jit(solution)/shard_map/gradients/pallas_call | solution.py:340
  40.8 0.0 collective-permute-done.13.refs_1_
  40.8 1.7 %collective-permute-start.16 = (bf16[192,256]{1,0:T(8,128)(2,1)S(1)}, bf16[192,256]{1,0:T(8,128)(2,1)S(1)}, u32[]{:S(2)}, u32[]{:S(2)}) collective-permute-start(bf16[192,256]{1,0:T(8,128)(2,1)S(1)} %get-tuple-element.64), channel_id=1, source_target_pairs={{0,16},{8,24},{16,0},{24,8},{1,17},{9,25},{17,1},{25,9},{2,18},{10... | collective-permute-start | bytes 294920 | tf_op jit(solution)/shard_map/return/ppermute | solution.py:377
  42.5 1.2 %collective-permute-start.17 = (bf16[192,256]{1,0:T(8,128)(2,1)S(1)}, bf16[192,256]{1,0:T(8,128)(2,1)S(1)}, u32[]{:S(2)}, u32[]{:S(2)}) collective-permute-start(bf16[192,256]{1,0:T(8,128)(2,1)S(1)} %get-tuple-element.65), channel_id=1, source_target_pairs={{0,24},{8,16},{16,8},{24,0},{1,25},{9,17},{17,9},{25,1},{2,26},{10... | collective-permute-start | bytes 294920 | tf_op jit(solution)/shard_map/return/ppermute | solution.py:377
  43.7 0.0 collective-permute-start.18
  43.7 0.0 collective-permute-done.14.refs_5_
  43.7 1.6 %collective-permute-done.15.refs_6_ = bf16[2,2,192,256]{3,2,1,0:T(8,128)(2,1)S(1)} collective-permute-done((bf16[2,2,192,256]{3,2,1,0:T(8,128)(2,1)S(1)}, bf16[2,2,192,256]{3,2,1,0:T(8,128)(2,1)S(1)}, u32[]{:S(2)}, u32[]{:S(2)}) %collective-permute-start.15) | collective-permute-done | bytes 393248 | tf_op jit(solution)/shard_map/gradients/ppermute | solution.py:440
  45.3 0.1 fusion.1
  45.4 0.4 collective-permute-start.20
  45.8 1.2 %collective-permute-start.19 = (bf16[192,256]{1,0:T(8,128)(2,1)S(1)}, bf16[192,256]{1,0:T(8,128)(2,1)S(1)}, u32[]{:S(2)}, u32[]{:S(2)}) collective-permute-start(bf16[192,256]{1,0:T(8,128)(2,1)S(1)} %get-tuple-element.73), channel_id=1, source_target_pairs={{0,4},{4,0},{1,5},{5,1},{2,6},{6,2},{3,7},{7,3},{8,12},{12,8},{9,1... | collective-permute-start | bytes 294920 | tf_op jit(solution)/shard_map/return/ppermute | solution.py:450
  46.9 1.0 %finish.2 = (bf16[192,256]{1,0:T(8,128)(2,1)}, f32[2,192,256]{2,1,0:T(8,128)S(1)}) custom-call(bf16[192,256]{1,0:T(8,128)(2,1)S(1)} %get-tuple-element.40.refs_0_, bf16[192,256]{1,0:T(8,128)(2,1)S(1)} %collective-permute-done.13.refs_1_, bf16[192,256]{1,0:T(8,128)(2,1)S(1)} %collective-permute-done.8.refs_2_, ...), custom_call_target="tpu_custom_call" | custom-call | bytes 2162688 | tf_op jit(solution)/shard_map/finish/pallas_call | solution.py:340
  47.9 1.7 %collective-permute-done.16.refs_1_ = bf16[192,256]{1,0:T(8,128)(2,1)S(1)} collective-permute-done((bf16[192,256]{1,0:T(8,128)(2,1)S(1)}, bf16[192,256]{1,0:T(8,128)(2,1)S(1)}, u32[]{:S(2)}, u32[]{:S(2)}) %collective-permute-start.16) | collective-permute-done | bytes 98336 | tf_op jit(solution)/shard_map/return/ppermute | solution.py:377
  49.5 0.0 collective-permute-done.17.refs_2_
  49.5 0.3 collective-permute-done.18.refs_3_
  49.8 0.0 collective-permute-done.20.refs_5_
  49.8 0.1 collective-permute-done.19.refs_4_
  50.0 1.0 %finish.3 = (bf16[192,256]{1,0:T(8,128)(2,1)}, bf16[192,256]{1,0:T(8,128)(2,1)}, bf16[192,256]{1,0:T(8,128)(2,1)}) custom-call(bf16[192,256]{1,0:T(8,128)(2,1)S(1)} %get-tuple-element.63.refs_0_, bf16[192,256]{1,0:T(8,128)(2,1)S(1)} %collective-permute-done.16.refs_1_, bf16[192,256]{1,0:T(8,128)(2,1)S(1)} %collective-permute-done.17.refs_2_, ...), custom_call_target="tpu_custom_call" | custom-call | bytes 1572864 | tf_op jit(solution)/shard_map/finish/pallas_call | solution.py:340
Async XLA Ops:
  1.9 10.3 %collective-permute-start.4 = (bf16[2,192,256]{2,1,0:T(8,128)(2,1)S(1)}, bf16[2,192,256]{2,1,0:T(8,128)(2,1)S(1)}, u32[]{:S(2)}, u32[]{:S(2)}) collective-permute-start(bf16[2,192,256]{2,1,0:T(8,128)(2,1)S(1)} %get-tuple-element.39.refs_3_.refs_1_.refs_4_), channel_id=1, source_target_pairs={{0,4},{4,0},{1,5},{5,1},{2,6},{6,2},{3,7},{7,3},{8,12},{12,8},{9,1... | collective-permute-start | bytes 589832 | tf_op jit(solution)/shard_map/halo/ppermute | solution.py:382
  4.0 10.9 %collective-permute-start.1 = (bf16[2,192,256]{2,1,0:T(8,128)(2,1)S(1)}, bf16[2,192,256]{2,1,0:T(8,128)(2,1)S(1)}, u32[]{:S(2)}, u32[]{:S(2)}) collective-permute-start(bf16[2,192,256]{2,1,0:T(8,128)(2,1)S(1)} %get-tuple-element.38.refs_0_), channel_id=1, source_target_pairs={{0,16},{8,24},{16,0},{24,8},{1,17},{9,25},{17,1},{25,9},{2,18},{10... | collective-permute-start | bytes 589832 | tf_op jit(solution)/shard_map/halo/ppermute | solution.py:377
  6.3 10.2 %collective-permute-start = (bf16[2,192,256]{2,1,0:T(8,128)(2,1)S(1)}, bf16[2,192,256]{2,1,0:T(8,128)(2,1)S(1)}, u32[]{:S(2)}, u32[]{:S(2)}) collective-permute-start(bf16[2,192,256]{2,1,0:T(8,128)(2,1)S(1)} %get-tuple-element.38.refs_0_), channel_id=1, source_target_pairs={{0,8},{8,0},{16,24},{24,16},{1,9},{9,1},{17,25},{25,17},{2,10},{10... | collective-permute-start | bytes 589832 | tf_op jit(solution)/shard_map/halo/ppermute | solution.py:377
  7.6 9.2 %collective-permute-start.3 = (bf16[2,192,256]{2,1,0:T(8,128)(2,1)S(1)}, bf16[2,192,256]{2,1,0:T(8,128)(2,1)S(1)}, u32[]{:S(2)}, u32[]{:S(2)}) collective-permute-start(bf16[2,192,256]{2,1,0:T(8,128)(2,1)S(1)} %get-tuple-element.39.refs_3_.refs_1_.refs_4_), channel_id=1, source_target_pairs={{0,0},{1,2},{2,1},{3,3},{4,4},{5,6},{6,5},{7,7},{8,8},{9,10},{10,9... | collective-permute-start | bytes 589832 | tf_op jit(solution)/shard_map/halo/ppermute | solution.py:387
  12.2 4.7 %collective-permute-start.2 = (bf16[2,192,256]{2,1,0:T(8,128)(2,1)S(1)}, bf16[2,192,256]{2,1,0:T(8,128)(2,1)S(1)}, u32[]{:S(2)}, u32[]{:S(2)}) collective-permute-start(bf16[2,192,256]{2,1,0:T(8,128)(2,1)S(1)} %get-tuple-element.39.refs_3_.refs_1_.refs_4_), channel_id=1, source_target_pairs={{0,1},{1,0},{2,3},{3,2},{4,5},{5,4},{6,7},{7,6},{8,9},{9,8},{10,11... | collective-permute-start | bytes 589832 | tf_op jit(solution)/shard_map/halo/ppermute | solution.py:387
  12.2 7.0 %collective-permute-start.6 = (bf16[2,192,256]{2,1,0:T(8,128)(2,1)S(1)}, bf16[2,192,256]{2,1,0:T(8,128)(2,1)S(1)}, u32[]{:S(2)}, u32[]{:S(2)}) collective-permute-start(bf16[2,192,256]{2,1,0:T(8,128)(2,1)S(1)} %collective-permute-done.4.refs_6_.refs_4_.refs_5_), channel_id=1, source_target_pairs={{0,0},{1,2},{2,1},{3,3},{4,4},{5,6},{6,5},{7,7},{8,8},{9,10},{10,9... | collective-permute-start | bytes 589832 | tf_op jit(solution)/shard_map/halo/ppermute | solution.py:387
  14.9 4.4 %collective-permute-start.5 = (bf16[2,192,256]{2,1,0:T(8,128)(2,1)S(1)}, bf16[2,192,256]{2,1,0:T(8,128)(2,1)S(1)}, u32[]{:S(2)}, u32[]{:S(2)}) collective-permute-start(bf16[2,192,256]{2,1,0:T(8,128)(2,1)S(1)} %collective-permute-done.4.refs_6_.refs_4_.refs_5_), channel_id=1, source_target_pairs={{0,1},{1,0},{2,3},{3,2},{4,5},{5,4},{6,7},{7,6},{8,9},{9,8},{10,11... | collective-permute-start | bytes 589832 | tf_op jit(solution)/shard_map/halo/ppermute | solution.py:387
  16.5 6.9 %collective-permute-start.7 = (bf16[2,192,256]{2,1,0:T(8,128)(2,1)S(1)}, bf16[2,192,256]{2,1,0:T(8,128)(2,1)S(1)}, u32[]{:S(2)}, u32[]{:S(2)}) collective-permute-start(bf16[2,192,256]{2,1,0:T(8,128)(2,1)S(1)} %collective-permute-done.1.refs_2_), channel_id=1, source_target_pairs={{0,8},{8,0},{16,24},{24,16},{1,9},{9,1},{17,25},{25,17},{2,10},{10... | collective-permute-start | bytes 589832 | tf_op jit(solution)/shard_map/halo/ppermute | solution.py:377
  21.6 7.0 %collective-permute-start.8 = (bf16[192,256]{1,0:T(8,128)(2,1)S(1)}, bf16[192,256]{1,0:T(8,128)(2,1)S(1)}, u32[]{:S(2)}, u32[]{:S(2)}) collective-permute-start(bf16[192,256]{1,0:T(8,128)(2,1)S(1)} %get-tuple-element.43), channel_id=1, source_target_pairs={{0,16},{8,24},{16,0},{24,8},{1,17},{9,25},{17,1},{25,9},{2,18},{10... | collective-permute-start | bytes 294920 | tf_op jit(solution)/shard_map/merge/ppermute | solution.py:377
  22.4 6.2 %collective-permute-start.9 = (bf16[192,256]{1,0:T(8,128)(2,1)S(1)}, bf16[192,256]{1,0:T(8,128)(2,1)S(1)}, u32[]{:S(2)}, u32[]{:S(2)}) collective-permute-start(bf16[192,256]{1,0:T(8,128)(2,1)S(1)} %get-tuple-element.44), channel_id=1, source_target_pairs={{0,8},{8,0},{16,24},{24,16},{1,9},{9,1},{17,25},{25,17},{2,10},{10... | collective-permute-start | bytes 294920 | tf_op jit(solution)/shard_map/merge/ppermute | solution.py:377
  24.4 6.3 %collective-permute-start.12 = (f32[8,768]{1,0:T(8,128)S(1)}, f32[8,768]{1,0:T(8,128)S(1)}, u32[]{:S(2)}, u32[]{:S(2)}) collective-permute-start(f32[8,768]{1,0:T(8,128)S(1)} %get-tuple-element.45.refs_8_), channel_id=1, source_target_pairs={{0,16},{8,24},{16,0},{24,8},{1,17},{9,25},{17,1},{25,9},{2,18},{10... | collective-permute-start | bytes 73736 | tf_op jit(solution)/shard_map/merge/ppermute | solution.py:377
  26.2 4.5 %collective-permute-start.11 = (f32[8,768]{1,0:T(8,128)S(1)}, f32[8,768]{1,0:T(8,128)S(1)}, u32[]{:S(2)}, u32[]{:S(2)}) collective-permute-start(f32[8,768]{1,0:T(8,128)S(1)} %get-tuple-element.45.refs_8_), channel_id=1, source_target_pairs={{0,24},{8,16},{16,8},{24,0},{1,25},{9,17},{17,9},{25,1},{2,26},{10... | collective-permute-start | bytes 73736 | tf_op jit(solution)/shard_map/merge/ppermute | solution.py:377
  28.6 2.7 %collective-permute-start.10 = (f32[8,768]{1,0:T(8,128)S(1)}, f32[8,768]{1,0:T(8,128)S(1)}, u32[]{:S(2)}, u32[]{:S(2)}) collective-permute-start(f32[8,768]{1,0:T(8,128)S(1)} %get-tuple-element.45.refs_8_), channel_id=1, source_target_pairs={{0,8},{8,0},{16,24},{24,16},{1,9},{9,1},{17,25},{25,17},{2,10},{10... | collective-permute-start | bytes 73736 | tf_op jit(solution)/shard_map/merge/ppermute | solution.py:377
  28.6 12.2 %collective-permute-start.13 = (bf16[192,256]{1,0:T(8,128)(2,1)S(1)}, bf16[192,256]{1,0:T(8,128)(2,1)S(1)}, u32[]{:S(2)}, u32[]{:S(2)}) collective-permute-start(bf16[192,256]{1,0:T(8,128)(2,1)S(1)} %get-tuple-element.52), channel_id=1, source_target_pairs={{0,24},{8,16},{16,8},{24,0},{1,25},{9,17},{17,9},{25,1},{2,26},{10... | collective-permute-start | bytes 294920 | tf_op jit(solution)/shard_map/merge/ppermute | solution.py:377
  34.2 9.5 %collective-permute-start.14 = (bf16[2,2,192,256]{3,2,1,0:T(8,128)(2,1)S(1)}, bf16[2,2,192,256]{3,2,1,0:T(8,128)(2,1)S(1)}, u32[]{:S(2)}, u32[]{:S(2)}) collective-permute-start(bf16[2,2,192,256]{3,2,1,0:T(8,128)(2,1)S(1)} %get-tuple-element.59), channel_id=1, source_target_pairs={{0,1},{1,0},{2,3},{3,2},{4,5},{5,4},{6,7},{7,6},{8,9},{9,8},{10,11... | collective-permute-start | bytes 1179656 | tf_op jit(solution)/shard_map/gradients/ppermute | solution.py:440
  35.9 9.4 %collective-permute-start.15 = (bf16[2,2,192,256]{3,2,1,0:T(8,128)(2,1)S(1)}, bf16[2,2,192,256]{3,2,1,0:T(8,128)(2,1)S(1)}, u32[]{:S(2)}, u32[]{:S(2)}) collective-permute-start(bf16[2,2,192,256]{3,2,1,0:T(8,128)(2,1)S(1)} %get-tuple-element.60), channel_id=1, source_target_pairs={{0,0},{1,2},{2,1},{3,3},{4,4},{5,6},{6,5},{7,7},{8,8},{9,10},{10,9... | collective-permute-start | bytes 1179656 | tf_op jit(solution)/shard_map/gradients/ppermute | solution.py:440
  40.8 8.7 %collective-permute-start.16 = (bf16[192,256]{1,0:T(8,128)(2,1)S(1)}, bf16[192,256]{1,0:T(8,128)(2,1)S(1)}, u32[]{:S(2)}, u32[]{:S(2)}) collective-permute-start(bf16[192,256]{1,0:T(8,128)(2,1)S(1)} %get-tuple-element.64), channel_id=1, source_target_pairs={{0,16},{8,24},{16,0},{24,8},{1,17},{9,25},{17,1},{25,9},{2,18},{10... | collective-permute-start | bytes 294920 | tf_op jit(solution)/shard_map/return/ppermute | solution.py:377
  42.5 7.0 %collective-permute-start.17 = (bf16[192,256]{1,0:T(8,128)(2,1)S(1)}, bf16[192,256]{1,0:T(8,128)(2,1)S(1)}, u32[]{:S(2)}, u32[]{:S(2)}) collective-permute-start(bf16[192,256]{1,0:T(8,128)(2,1)S(1)} %get-tuple-element.65), channel_id=1, source_target_pairs={{0,24},{8,16},{16,8},{24,0},{1,25},{9,17},{17,9},{25,1},{2,26},{10... | collective-permute-start | bytes 294920 | tf_op jit(solution)/shard_map/return/ppermute | solution.py:377
  43.7 6.1 %collective-permute-start.18 = (bf16[192,256]{1,0:T(8,128)(2,1)S(1)}, bf16[192,256]{1,0:T(8,128)(2,1)S(1)}, u32[]{:S(2)}, u32[]{:S(2)}) collective-permute-start(bf16[192,256]{1,0:T(8,128)(2,1)S(1)} %get-tuple-element.66), channel_id=1, source_target_pairs={{0,8},{8,0},{16,24},{24,16},{1,9},{9,1},{17,25},{25,17},{2,10},{10... | collective-permute-start | bytes 294920 | tf_op jit(solution)/shard_map/return/ppermute | solution.py:377
  45.4 4.4 %collective-permute-start.20 = (bf16[192,256]{1,0:T(8,128)(2,1)S(1)}, bf16[192,256]{1,0:T(8,128)(2,1)S(1)}, u32[]{:S(2)}, u32[]{:S(2)}) collective-permute-start(bf16[192,256]{1,0:T(8,128)(2,1)S(1)} %get-tuple-element.72), channel_id=1, source_target_pairs={{0,4},{4,0},{1,5},{5,1},{2,6},{6,2},{3,7},{7,3},{8,12},{12,8},{9,1... | collective-permute-start | bytes 294920 | tf_op jit(solution)/shard_map/return/ppermute | solution.py:450
  45.8 4.2 %collective-permute-start.19 = (bf16[192,256]{1,0:T(8,128)(2,1)S(1)}, bf16[192,256]{1,0:T(8,128)(2,1)S(1)}, u32[]{:S(2)}, u32[]{:S(2)}) collective-permute-start(bf16[192,256]{1,0:T(8,128)(2,1)S(1)} %get-tuple-element.73), channel_id=1, source_target_pairs={{0,4},{4,0},{1,5},{5,1},{2,6},{6,2},{3,7},{7,3},{8,12},{12,8},{9,1... | collective-permute-start | bytes 294920 | tf_op jit(solution)/shard_map/return/ppermute | solution.py:450

commit v21 on v20

--- a/solution.py
+++ b/solution.py
@@ -413,8 +413,9 @@
         o3, stat = forward((qg3,), first)
     with jax.named_scope("merge"):
         outs = [other_frames(o, d) for d, o in ((3, o3), (2, o2), (1, o1))]
-        stat_near, outs[1:] = lax.optimization_barrier((stat, outs[1:]))
+        stat_near, outs[2] = lax.optimization_barrier((stat, outs[2]))
         stats = [stat, other_frames(stat_near, 1), other_frames(stat, 3), other_frames(stat, 2)]
+        stats, outs[1] = lax.optimization_barrier((stats, outs[1]))
 
     queries = (qg, qg1, qg2, qg3)
     col_shape = jax.ShapeDtypeStruct((grid_rows, 2, cells, chan), BF16)

time: 51.1 us -> 52.1 us (1.020)
  starting transfers between devices: 30.3 us -> 31.5 us
    ppermute x2, starting transfers between devices: 4.91 us -> 6.04 us  [shards(): sides = [lax.ppermute(x, 'wa', pairs) for x, pairs in zip(sides, col_sides)]]
    ppermute x12, waiting for transfers between devices: 4.55 us -> 3.83 us  [other_frames(): lax.ppermute(x, 'ta', [(i, i ^ distance) for i in range(sizes['ta'])])]
  transfers between devices with their start and end apart: 21 -> 21, of which waited for: 8 -> 10; matrix products, arithmetic and copies ran while one was open for 0% -> 0% of each run, Pallas kernels for 18% -> 17%
where the time goes in v21:
time: 52.1 us; the launch traced here: 51.9 us
  starting transfers between devices  31.5 us (60%)
  Pallas kernels  11.1 us (21%)
  waiting for transfers between devices  8.49 us (16%)
  between operations  0.72 us (1%)
    ppermute x12, starting transfers between devices, other_frames(): lax.ppermute(x, 'ta', [(i, i ^ distance) for i in range(sizes['ta'])])  13.6 us
    pallas_call x7, Pallas kernels, call(): pl.pallas_call(kernel, out_shape=out_shape, in_specs=[pl.BlockSpec(memory...  11.1 us
    ppermute x4, starting transfers between devices, shards(): lax.ppermute(block, 'wa', pairs)  8.2 us
    ppermute x2, starting transfers between devices, shards(): sides = [lax.ppermute(x, 'wa', pairs) for x, pairs in zip(sides, col_sides)]  6.04 us
    ppermute x12, waiting for transfers between devices, other_frames(): lax.ppermute(x, 'ta', [(i, i ^ distance) for i in range(sizes['ta'])])  3.83 us
    ppermute x4, waiting for transfers between devices, shards(): lax.ppermute(block, 'wa', pairs)  2.4 us
    ppermute x1, starting transfers between devices, shards(): kv_rows = [kv] + [lax.ppermute(kv, 'ha', pairs) for pairs in row_sides]  2.11 us
    ppermute x2, waiting for transfers between devices, shards(): sides = [lax.ppermute(x, 'wa', pairs) for x, pairs in zip(sides, col_sides)]  1.9 us
  transfers between devices with their start and end apart: 21, of which 10 were waited for; matrix products, arithmetic and copies ran while one was open for 0% of the time, Pallas kernels for 17%

profile of v21, /device:TPU:1, one launch (start us, length us, event | category | flops | bytes accessed | tf_op | source)
XLA Modules:
  0.0 51.9 jit_solution(5526061201770608690)
XLA Ops:
  0.6 1.3 %rotate.1 = (bf16[2,192,256]{2,1,0:T(8,128)(2,1)S(1)}, bf16[2,192,256]{2,1,0:T(8,128)(2,1)S(1)}, f32[3,192,128]{2,1,0:T(8,128)S(1)}) custom-call(bf16[192,256]{1,0:T(8,128)(2,1)} %bitcast.12, bf16[192,256]{1,0:T(8,128)(2,1)} %bitcast.13, bf16[192,256]{1,0:T(8,128)(2,1)} %bitcast.14, bf16[192,256]{1,0:T(8,128)(2,1)} %bitcast.15, ...), custom_call_target="tpu_custom_call" | custom-call | bytes 1179648 | tf_op jit(solution)/shard_map/rotate/pallas_call | solution.py:340
  1.9 2.1 %collective-permute-start.4 = (bf16[2,192,256]{2,1,0:T(8,128)(2,1)S(1)}, bf16[2,192,256]{2,1,0:T(8,128)(2,1)S(1)}, u32[]{:S(2)}, u32[]{:S(2)}) collective-permute-start(bf16[2,192,256]{2,1,0:T(8,128)(2,1)S(1)} %get-tuple-element.43.refs_3_.refs_1_.refs_4_), channel_id=1, source_target_pairs={{0,4},{4,0},{1,5},{5,1},{2,6},{6,2},{3,7},{7,3},{8,12},{12,8},{9,1... | collective-permute-start | bytes 589832 | tf_op jit(solution)/shard_map/halo/ppermute | solution.py:382
  4.0 2.3 %collective-permute-start.1 = (bf16[2,192,256]{2,1,0:T(8,128)(2,1)S(1)}, bf16[2,192,256]{2,1,0:T(8,128)(2,1)S(1)}, u32[]{:S(2)}, u32[]{:S(2)}) collective-permute-start(bf16[2,192,256]{2,1,0:T(8,128)(2,1)S(1)} %get-tuple-element.42.refs_0_), channel_id=1, source_target_pairs={{0,16},{8,24},{16,0},{24,8},{1,17},{9,25},{17,1},{25,9},{2,18},{10... | collective-permute-start | bytes 589832 | tf_op jit(solution)/shard_map/halo/ppermute | solution.py:377
  6.3 1.3 %collective-permute-start = (bf16[2,192,256]{2,1,0:T(8,128)(2,1)S(1)}, bf16[2,192,256]{2,1,0:T(8,128)(2,1)S(1)}, u32[]{:S(2)}, u32[]{:S(2)}) collective-permute-start(bf16[2,192,256]{2,1,0:T(8,128)(2,1)S(1)} %get-tuple-element.42.refs_0_), channel_id=1, source_target_pairs={{0,8},{8,0},{16,24},{24,16},{1,9},{9,1},{17,25},{25,17},{2,10},{10... | collective-permute-start | bytes 589832 | tf_op jit(solution)/shard_map/halo/ppermute | solution.py:377
  7.6 4.5 %collective-permute-start.3 = (bf16[2,192,256]{2,1,0:T(8,128)(2,1)S(1)}, bf16[2,192,256]{2,1,0:T(8,128)(2,1)S(1)}, u32[]{:S(2)}, u32[]{:S(2)}) collective-permute-start(bf16[2,192,256]{2,1,0:T(8,128)(2,1)S(1)} %get-tuple-element.43.refs_3_.refs_1_.refs_4_), channel_id=1, source_target_pairs={{0,0},{1,2},{2,1},{3,3},{4,4},{5,6},{6,5},{7,7},{8,8},{9,10},{10,9... | collective-permute-start | bytes 589832 | tf_op jit(solution)/shard_map/halo/ppermute | solution.py:387
  12.2 0.1 collective-permute-start.2
  12.2 0.0 collective-permute-done.4.refs_6_.refs_4_.refs_5_
  12.2 1.9 %collective-permute-start.6 = (bf16[2,192,256]{2,1,0:T(8,128)(2,1)S(1)}, bf16[2,192,256]{2,1,0:T(8,128)(2,1)S(1)}, u32[]{:S(2)}, u32[]{:S(2)}) collective-permute-start(bf16[2,192,256]{2,1,0:T(8,128)(2,1)S(1)} %collective-permute-done.4.refs_6_.refs_4_.refs_5_), channel_id=1, source_target_pairs={{0,0},{1,2},{2,1},{3,3},{4,4},{5,6},{6,5},{7,7},{8,8},{9,10},{10,9... | collective-permute-start | bytes 589832 | tf_op jit(solution)/shard_map/halo/ppermute | solution.py:387
  14.2 0.7 %collective-permute-done.1.refs_2_ = bf16[2,192,256]{2,1,0:T(8,128)(2,1)S(1)} collective-permute-done((bf16[2,192,256]{2,1,0:T(8,128)(2,1)S(1)}, bf16[2,192,256]{2,1,0:T(8,128)(2,1)S(1)}, u32[]{:S(2)}, u32[]{:S(2)}) %collective-permute-start.1) | collective-permute-done | bytes 196640 | tf_op jit(solution)/shard_map/halo/ppermute | solution.py:377
  14.9 1.7 %collective-permute-start.5 = (bf16[2,192,256]{2,1,0:T(8,128)(2,1)S(1)}, bf16[2,192,256]{2,1,0:T(8,128)(2,1)S(1)}, u32[]{:S(2)}, u32[]{:S(2)}) collective-permute-start(bf16[2,192,256]{2,1,0:T(8,128)(2,1)S(1)} %collective-permute-done.4.refs_6_.refs_4_.refs_5_), channel_id=1, source_target_pairs={{0,1},{1,0},{2,3},{3,2},{4,5},{5,4},{6,7},{7,6},{8,9},{9,8},{10,11... | collective-permute-start | bytes 589832 | tf_op jit(solution)/shard_map/halo/ppermute | solution.py:387
  16.5 0.0 collective-permute-done.refs_1_
  16.5 0.3 collective-permute-start.7
  16.8 0.0 collective-permute-done.3.refs_5_.refs_3_.refs_6_
  16.8 0.0 collective-permute-done.2.refs_4_.refs_2_
  16.8 2.4 %collective-permute-done.6.refs_8_.refs_6_.refs_7_ = bf16[2,192,256]{2,1,0:T(8,128)(2,1)S(1)} collective-permute-done((bf16[2,192,256]{2,1,0:T(8,128)(2,1)S(1)}, bf16[2,192,256]{2,1,0:T(8,128)(2,1)S(1)}, u32[]{:S(2)}, u32[]{:S(2)}) %collective-permute-start.6) | collective-permute-done | bytes 196640 | tf_op jit(solution)/shard_map/halo/ppermute | solution.py:387
  19.2 0.0 collective-permute-done.5.refs_7_.refs_5_
  19.2 2.4 %attend.2 = (bf16[192,256]{1,0:T(8,128)(2,1)S(1)}, bf16[192,256]{1,0:T(8,128)(2,1)S(1)}, bf16[192,256]{1,0:T(8,128)(2,1)S(1)}, f32[576,128]{1,0:T(8,128)S(1)}) custom-call(bf16[2,192,256]{2,1,0:T(8,128)(2,1)S(1)} %get-tuple-element.42.refs_0_, bf16[2,192,256]{2,1,0:T(8,128)(2,1)S(1)} %collective-permute-done.refs_1_, ...), custom_call_target="tpu_custom_call" | custom-call | flops 5435817984 | bytes 2359296 | tf_op jit(solution)/shard_map/attend/pallas_call | solution.py:340
  21.6 0.2 collective-permute-start.8
  21.8 1.6 %collective-permute-start.12 = (bf16[192,256]{1,0:T(8,128)(2,1)S(1)}, bf16[192,256]{1,0:T(8,128)(2,1)S(1)}, u32[]{:S(2)}, u32[]{:S(2)}) collective-permute-start(bf16[192,256]{1,0:T(8,128)(2,1)S(1)} %get-tuple-element.49), channel_id=1, source_target_pairs={{0,16},{8,24},{16,0},{24,8},{1,17},{9,25},{17,1},{25,9},{2,18},{10... | collective-permute-start | bytes 294920 | tf_op jit(solution)/shard_map/merge/ppermute | solution.py:377
  23.4 0.0 collective-permute-done.7.refs_0_.refs_3_
  23.4 1.0 %attend.3 = (bf16[192,256]{1,0:T(8,128)(2,1)S(1)}, f32[8,768]{1,0:T(8,128)S(1)}) custom-call(bf16[2,192,256]{2,1,0:T(8,128)(2,1)S(1)} %collective-permute-done.7.refs_0_.refs_3_, bf16[2,192,256]{2,1,0:T(8,128)(2,1)S(1)} %get-tuple-element.43.refs_3_.refs_1_.refs_4_, bf16[2,192,256]{2,1,0:T(8,128)(2,1)S(1)} %collective-permute-done.2.refs_4_.refs_2_, ...), custom_call_target="tpu_custom_call" | custom-call | flops 1811939328 | bytes 1794048 | tf_op jit(solution)/shard_map/attend/pallas_call | solution.py:340
  24.4 1.8 %collective-permute-start.11 = (f32[8,768]{1,0:T(8,128)S(1)}, f32[8,768]{1,0:T(8,128)S(1)}, u32[]{:S(2)}, u32[]{:S(2)}) collective-permute-start(f32[8,768]{1,0:T(8,128)S(1)} %get-tuple-element.50.refs_8_), channel_id=1, source_target_pairs={{0,16},{8,24},{16,0},{24,8},{1,17},{9,25},{17,1},{25,9},{2,18},{10... | collective-permute-start | bytes 73736 | tf_op jit(solution)/shard_map/merge/ppermute | solution.py:377
  26.2 1.1 %collective-permute-start.10 = (f32[8,768]{1,0:T(8,128)S(1)}, f32[8,768]{1,0:T(8,128)S(1)}, u32[]{:S(2)}, u32[]{:S(2)}) collective-permute-start(f32[8,768]{1,0:T(8,128)S(1)} %get-tuple-element.50.refs_8_), channel_id=1, source_target_pairs={{0,24},{8,16},{16,8},{24,0},{1,25},{9,17},{17,9},{25,1},{2,26},{10... | collective-permute-start | bytes 73736 | tf_op jit(solution)/shard_map/merge/ppermute | solution.py:377
  27.3 0.2 collective-permute-done.8.refs_3_
  27.5 0.0 collective-permute-start.9
  27.5 2.3 %collective-permute-start.13 = (bf16[192,256]{1,0:T(8,128)(2,1)S(1)}, bf16[192,256]{1,0:T(8,128)(2,1)S(1)}, u32[]{:S(2)}, u32[]{:S(2)}) collective-permute-start(bf16[192,256]{1,0:T(8,128)(2,1)S(1)} %get-tuple-element.60), channel_id=1, source_target_pairs={{0,24},{8,16},{16,8},{24,0},{1,25},{9,17},{17,9},{25,1},{2,26},{10... | collective-permute-start | bytes 294920 | tf_op jit(solution)/shard_map/merge/ppermute | solution.py:377
  29.8 0.8 %collective-permute-done.11.refs_11_ = f32[8,768]{1,0:T(8,128)S(1)} collective-permute-done((f32[8,768]{1,0:T(8,128)S(1)}, f32[8,768]{1,0:T(8,128)S(1)}, u32[]{:S(2)}, u32[]{:S(2)}) %collective-permute-start.11) | collective-permute-done | bytes 24608 | tf_op jit(solution)/shard_map/merge/ppermute | solution.py:377
  30.7 0.1 collective-permute-done.10.refs_10_
  30.8 0.0 collective-permute-done.12.refs_2_
  30.8 0.2 collective-permute-done.9.refs_9_
  31.0 2.9 %gradients.2 = (f32[2,128,768]{2,1,0:T(8,128)S(1)}, f32[2,768]{1,0:T(2,128)S(1)}, f32[2,768]{1,0:T(2,128)S(1)}, f32[192,128]{1,0:T(8,128)S(1)}, bf16[2,2,192,256...) custom-call(bf16[2,192,256]{2,1,0:T(8,128)(2,1)S(1)} %get-tuple-element.42.refs_0_, ...), custom_call_target="tpu_custom_call" | custom-call | flops 12079595520 | bytes 3354624 | tf_op jit(solution)/shard_map/gradients/pallas_call | solution.py:340
  33.9 3.0 %collective-permute-start.14 = (bf16[2,2,192,256]{3,2,1,0:T(8,128)(2,1)S(1)}, bf16[2,2,192,256]{3,2,1,0:T(8,128)(2,1)S(1)}, u32[]{:S(2)}, u32[]{:S(2)}) collective-permute-start(bf16[2,2,192,256]{3,2,1,0:T(8,128)(2,1)S(1)} %get-tuple-element.67), channel_id=1, source_target_pairs={{0,1},{1,0},{2,3},{3,2},{4,5},{5,4},{6,7},{7,6},{8,9},{9,8},{10,11... | collective-permute-start | bytes 1179656 | tf_op jit(solution)/shard_map/gradients/ppermute | solution.py:441
  36.9 3.1 %collective-permute-start.15 = (bf16[2,2,192,256]{3,2,1,0:T(8,128)(2,1)S(1)}, bf16[2,2,192,256]{3,2,1,0:T(8,128)(2,1)S(1)}, u32[]{:S(2)}, u32[]{:S(2)}) collective-permute-start(bf16[2,2,192,256]{3,2,1,0:T(8,128)(2,1)S(1)} %get-tuple-element.68), channel_id=1, source_target_pairs={{0,0},{1,2},{2,1},{3,3},{4,4},{5,6},{6,5},{7,7},{8,8},{9,10},{10,9... | collective-permute-start | bytes 1179656 | tf_op jit(solution)/shard_map/gradients/ppermute | solution.py:441
  40.0 1.7 %gradients.3 = (bf16[192,256]{1,0:T(8,128)(2,1)S(1)}, bf16[192,256]{1,0:T(8,128)(2,1)S(1)}, bf16[192,256]{1,0:T(8,128)(2,1)S(1)}, bf16[192,256]{1,0:T(8,128)(2,1)S(1)}, bf16[2,2,192,256]{3,2,1,0:T(8,128)(2,1)S(1)}) custom-call(bf16[2,192,256]{2,1,0:T(8,128)(2,1)S(1)} %get-tuple-element.42.refs_0_, bf16[2,192,256]{2,1,0:T(8,128)(2,1)S(1)} %collective-permute-done.refs_1_, ...), custom_call_target="tpu_custom_call" | custom-call | flops 6039797760 | bytes 2764800 | tf_op jit(solution)/shard_map/gradients/pallas_call | solution.py:340
  41.6 0.0 collective-permute-done.13.refs_1_
  41.7 0.5 collective-permute-start.16
  42.1 2.1 %collective-permute-start.17 = (bf16[192,256]{1,0:T(8,128)(2,1)S(1)}, bf16[192,256]{1,0:T(8,128)(2,1)S(1)}, u32[]{:S(2)}, u32[]{:S(2)}) collective-permute-start(bf16[192,256]{1,0:T(8,128)(2,1)S(1)} %get-tuple-element.73), channel_id=1, source_target_pairs={{0,24},{8,16},{16,8},{24,0},{1,25},{9,17},{17,9},{25,1},{2,26},{10... | collective-permute-start | bytes 294920 | tf_op jit(solution)/shard_map/return/ppermute | solution.py:377
  44.2 0.2 collective-permute-start.18
  44.4 0.0 collective-permute-done.14.refs_5_
  44.4 1.9 %collective-permute-done.15.refs_6_ = bf16[2,2,192,256]{3,2,1,0:T(8,128)(2,1)S(1)} collective-permute-done((bf16[2,2,192,256]{3,2,1,0:T(8,128)(2,1)S(1)}, bf16[2,2,192,256]{3,2,1,0:T(8,128)(2,1)S(1)}, u32[]{:S(2)}, u32[]{:S(2)}) %collective-permute-start.15) | collective-permute-done | bytes 393248 | tf_op jit(solution)/shard_map/gradients/ppermute | solution.py:441
  46.3 0.1 fusion.1
  46.4 0.3 collective-permute-start.20
  46.7 1.2 %collective-permute-start.19 = (bf16[192,256]{1,0:T(8,128)(2,1)S(1)}, bf16[192,256]{1,0:T(8,128)(2,1)S(1)}, u32[]{:S(2)}, u32[]{:S(2)}) collective-permute-start(bf16[192,256]{1,0:T(8,128)(2,1)S(1)} %get-tuple-element.81), channel_id=1, source_target_pairs={{0,4},{4,0},{1,5},{5,1},{2,6},{6,2},{3,7},{7,3},{8,12},{12,8},{9,1... | collective-permute-start | bytes 294920 | tf_op jit(solution)/shard_map/return/ppermute | solution.py:451
  47.9 1.0 %finish.2 = (bf16[192,256]{1,0:T(8,128)(2,1)}, f32[2,192,256]{2,1,0:T(8,128)S(1)}) custom-call(bf16[192,256]{1,0:T(8,128)(2,1)S(1)} %get-tuple-element.44.refs_0_, bf16[192,256]{1,0:T(8,128)(2,1)S(1)} %collective-permute-done.13.refs_1_, bf16[192,256]{1,0:T(8,128)(2,1)S(1)} %collective-permute-done.12.refs_2_, ...), custom_call_target="tpu_custom_call" | custom-call | bytes 2162688 | tf_op jit(solution)/shard_map/finish/pallas_call | solution.py:340
  48.8 1.3 %collective-permute-done.16.refs_1_ = bf16[192,256]{1,0:T(8,128)(2,1)S(1)} collective-permute-done((bf16[192,256]{1,0:T(8,128)(2,1)S(1)}, bf16[192,256]{1,0:T(8,128)(2,1)S(1)}, u32[]{:S(2)}, u32[]{:S(2)}) %collective-permute-start.16) | collective-permute-done | bytes 98336 | tf_op jit(solution)/shard_map/return/ppermute | solution.py:377
  50.1 0.0 collective-permute-done.17.refs_2_
  50.1 0.5 collective-permute-done.18.refs_3_
  50.6 0.0 collective-permute-done.20.refs_5_
  50.6 0.4 collective-permute-done.19.refs_4_
  50.9 1.0 %finish.3 = (bf16[192,256]{1,0:T(8,128)(2,1)}, bf16[192,256]{1,0:T(8,128)(2,1)}, bf16[192,256]{1,0:T(8,128)(2,1)}) custom-call(bf16[192,256]{1,0:T(8,128)(2,1)S(1)} %get-tuple-element.71.refs_0_, bf16[192,256]{1,0:T(8,128)(2,1)S(1)} %collective-permute-done.16.refs_1_, bf16[192,256]{1,0:T(8,128)(2,1)S(1)} %collective-permute-done.17.refs_2_, ...), custom_call_target="tpu_custom_call" | custom-call | bytes 1572864 | tf_op jit(solution)/shard_map/finish/pallas_call | solution.py:340
Async XLA Ops:
  1.9 10.3 %collective-permute-start.4 = (bf16[2,192,256]{2,1,0:T(8,128)(2,1)S(1)}, bf16[2,192,256]{2,1,0:T(8,128)(2,1)S(1)}, u32[]{:S(2)}, u32[]{:S(2)}) collective-permute-start(bf16[2,192,256]{2,1,0:T(8,128)(2,1)S(1)} %get-tuple-element.43.refs_3_.refs_1_.refs_4_), channel_id=1, source_target_pairs={{0,4},{4,0},{1,5},{5,1},{2,6},{6,2},{3,7},{7,3},{8,12},{12,8},{9,1... | collective-permute-start | bytes 589832 | tf_op jit(solution)/shard_map/halo/ppermute | solution.py:382
  4.0 10.9 %collective-permute-start.1 = (bf16[2,192,256]{2,1,0:T(8,128)(2,1)S(1)}, bf16[2,192,256]{2,1,0:T(8,128)(2,1)S(1)}, u32[]{:S(2)}, u32[]{:S(2)}) collective-permute-start(bf16[2,192,256]{2,1,0:T(8,128)(2,1)S(1)} %get-tuple-element.42.refs_0_), channel_id=1, source_target_pairs={{0,16},{8,24},{16,0},{24,8},{1,17},{9,25},{17,1},{25,9},{2,18},{10... | collective-permute-start | bytes 589832 | tf_op jit(solution)/shard_map/halo/ppermute | solution.py:377
  6.3 10.2 %collective-permute-start = (bf16[2,192,256]{2,1,0:T(8,128)(2,1)S(1)}, bf16[2,192,256]{2,1,0:T(8,128)(2,1)S(1)}, u32[]{:S(2)}, u32[]{:S(2)}) collective-permute-start(bf16[2,192,256]{2,1,0:T(8,128)(2,1)S(1)} %get-tuple-element.42.refs_0_), channel_id=1, source_target_pairs={{0,8},{8,0},{16,24},{24,16},{1,9},{9,1},{17,25},{25,17},{2,10},{10... | collective-permute-start | bytes 589832 | tf_op jit(solution)/shard_map/halo/ppermute | solution.py:377
  7.6 9.2 %collective-permute-start.3 = (bf16[2,192,256]{2,1,0:T(8,128)(2,1)S(1)}, bf16[2,192,256]{2,1,0:T(8,128)(2,1)S(1)}, u32[]{:S(2)}, u32[]{:S(2)}) collective-permute-start(bf16[2,192,256]{2,1,0:T(8,128)(2,1)S(1)} %get-tuple-element.43.refs_3_.refs_1_.refs_4_), channel_id=1, source_target_pairs={{0,0},{1,2},{2,1},{3,3},{4,4},{5,6},{6,5},{7,7},{8,8},{9,10},{10,9... | collective-permute-start | bytes 589832 | tf_op jit(solution)/shard_map/halo/ppermute | solution.py:387
  12.2 4.7 %collective-permute-start.2 = (bf16[2,192,256]{2,1,0:T(8,128)(2,1)S(1)}, bf16[2,192,256]{2,1,0:T(8,128)(2,1)S(1)}, u32[]{:S(2)}, u32[]{:S(2)}) collective-permute-start(bf16[2,192,256]{2,1,0:T(8,128)(2,1)S(1)} %get-tuple-element.43.refs_3_.refs_1_.refs_4_), channel_id=1, source_target_pairs={{0,1},{1,0},{2,3},{3,2},{4,5},{5,4},{6,7},{7,6},{8,9},{9,8},{10,11... | collective-permute-start | bytes 589832 | tf_op jit(solution)/shard_map/halo/ppermute | solution.py:387
  12.2 7.0 %collective-permute-start.6 = (bf16[2,192,256]{2,1,0:T(8,128)(2,1)S(1)}, bf16[2,192,256]{2,1,0:T(8,128)(2,1)S(1)}, u32[]{:S(2)}, u32[]{:S(2)}) collective-permute-start(bf16[2,192,256]{2,1,0:T(8,128)(2,1)S(1)} %collective-permute-done.4.refs_6_.refs_4_.refs_5_), channel_id=1, source_target_pairs={{0,0},{1,2},{2,1},{3,3},{4,4},{5,6},{6,5},{7,7},{8,8},{9,10},{10,9... | collective-permute-start | bytes 589832 | tf_op jit(solution)/shard_map/halo/ppermute | solution.py:387
  14.9 4.4 %collective-permute-start.5 = (bf16[2,192,256]{2,1,0:T(8,128)(2,1)S(1)}, bf16[2,192,256]{2,1,0:T(8,128)(2,1)S(1)}, u32[]{:S(2)}, u32[]{:S(2)}) collective-permute-start(bf16[2,192,256]{2,1,0:T(8,128)(2,1)S(1)} %collective-permute-done.4.refs_6_.refs_4_.refs_5_), channel_id=1, source_target_pairs={{0,1},{1,0},{2,3},{3,2},{4,5},{5,4},{6,7},{7,6},{8,9},{9,8},{10,11... | collective-permute-start | bytes 589832 | tf_op jit(solution)/shard_map/halo/ppermute | solution.py:387
  16.5 6.9 %collective-permute-start.7 = (bf16[2,192,256]{2,1,0:T(8,128)(2,1)S(1)}, bf16[2,192,256]{2,1,0:T(8,128)(2,1)S(1)}, u32[]{:S(2)}, u32[]{:S(2)}) collective-permute-start(bf16[2,192,256]{2,1,0:T(8,128)(2,1)S(1)} %collective-permute-done.1.refs_2_), channel_id=1, source_target_pairs={{0,8},{8,0},{16,24},{24,16},{1,9},{9,1},{17,25},{25,17},{2,10},{10... | collective-permute-start | bytes 589832 | tf_op jit(solution)/shard_map/halo/ppermute | solution.py:377
  21.6 5.9 %collective-permute-start.8 = (bf16[192,256]{1,0:T(8,128)(2,1)S(1)}, bf16[192,256]{1,0:T(8,128)(2,1)S(1)}, u32[]{:S(2)}, u32[]{:S(2)}) collective-permute-start(bf16[192,256]{1,0:T(8,128)(2,1)S(1)} %get-tuple-element.47), channel_id=1, source_target_pairs={{0,8},{8,0},{16,24},{24,16},{1,9},{9,1},{17,25},{25,17},{2,10},{10... | collective-permute-start | bytes 294920 | tf_op jit(solution)/shard_map/merge/ppermute | solution.py:377
  21.8 9.0 %collective-permute-start.12 = (bf16[192,256]{1,0:T(8,128)(2,1)S(1)}, bf16[192,256]{1,0:T(8,128)(2,1)S(1)}, u32[]{:S(2)}, u32[]{:S(2)}) collective-permute-start(bf16[192,256]{1,0:T(8,128)(2,1)S(1)} %get-tuple-element.49), channel_id=1, source_target_pairs={{0,16},{8,24},{16,0},{24,8},{1,17},{9,25},{17,1},{25,9},{2,18},{10... | collective-permute-start | bytes 294920 | tf_op jit(solution)/shard_map/merge/ppermute | solution.py:377
  24.4 6.3 %collective-permute-start.11 = (f32[8,768]{1,0:T(8,128)S(1)}, f32[8,768]{1,0:T(8,128)S(1)}, u32[]{:S(2)}, u32[]{:S(2)}) collective-permute-start(f32[8,768]{1,0:T(8,128)S(1)} %get-tuple-element.50.refs_8_), channel_id=1, source_target_pairs={{0,16},{8,24},{16,0},{24,8},{1,17},{9,25},{17,1},{25,9},{2,18},{10... | collective-permute-start | bytes 73736 | tf_op jit(solution)/shard_map/merge/ppermute | solution.py:377
  26.2 4.6 %collective-permute-start.10 = (f32[8,768]{1,0:T(8,128)S(1)}, f32[8,768]{1,0:T(8,128)S(1)}, u32[]{:S(2)}, u32[]{:S(2)}) collective-permute-start(f32[8,768]{1,0:T(8,128)S(1)} %get-tuple-element.50.refs_8_), channel_id=1, source_target_pairs={{0,24},{8,16},{16,8},{24,0},{1,25},{9,17},{17,9},{25,1},{2,26},{10... | collective-permute-start | bytes 73736 | tf_op jit(solution)/shard_map/merge/ppermute | solution.py:377
  27.5 3.5 %collective-permute-start.9 = (f32[8,768]{1,0:T(8,128)S(1)}, f32[8,768]{1,0:T(8,128)S(1)}, u32[]{:S(2)}, u32[]{:S(2)}) collective-permute-start(f32[8,768]{1,0:T(8,128)S(1)} %get-tuple-element.50.refs_8_), channel_id=1, source_target_pairs={{0,8},{8,0},{16,24},{24,16},{1,9},{9,1},{17,25},{25,17},{2,10},{10... | collective-permute-start | bytes 73736 | tf_op jit(solution)/shard_map/merge/ppermute | solution.py:377
  27.5 14.1 %collective-permute-start.13 = (bf16[192,256]{1,0:T(8,128)(2,1)S(1)}, bf16[192,256]{1,0:T(8,128)(2,1)S(1)}, u32[]{:S(2)}, u32[]{:S(2)}) collective-permute-start(bf16[192,256]{1,0:T(8,128)(2,1)S(1)} %get-tuple-element.60), channel_id=1, source_target_pairs={{0,24},{8,16},{16,8},{24,0},{1,25},{9,17},{17,9},{25,1},{2,26},{10... | collective-permute-start | bytes 294920 | tf_op jit(solution)/shard_map/merge/ppermute | solution.py:377
  33.9 10.5 %collective-permute-start.14 = (bf16[2,2,192,256]{3,2,1,0:T(8,128)(2,1)S(1)}, bf16[2,2,192,256]{3,2,1,0:T(8,128)(2,1)S(1)}, u32[]{:S(2)}, u32[]{:S(2)}) collective-permute-start(bf16[2,2,192,256]{3,2,1,0:T(8,128)(2,1)S(1)} %get-tuple-element.67), channel_id=1, source_target_pairs={{0,1},{1,0},{2,3},{3,2},{4,5},{5,4},{6,7},{7,6},{8,9},{9,8},{10,11... | collective-permute-start | bytes 1179656 | tf_op jit(solution)/shard_map/gradients/ppermute | solution.py:441
  36.9 9.4 %collective-permute-start.15 = (bf16[2,2,192,256]{3,2,1,0:T(8,128)(2,1)S(1)}, bf16[2,2,192,256]{3,2,1,0:T(8,128)(2,1)S(1)}, u32[]{:S(2)}, u32[]{:S(2)}) collective-permute-start(bf16[2,2,192,256]{3,2,1,0:T(8,128)(2,1)S(1)} %get-tuple-element.68), channel_id=1, source_target_pairs={{0,0},{1,2},{2,1},{3,3},{4,4},{5,6},{6,5},{7,7},{8,8},{9,10},{10,9... | collective-permute-start | bytes 1179656 | tf_op jit(solution)/shard_map/gradients/ppermute | solution.py:441
  41.7 8.5 %collective-permute-start.16 = (bf16[192,256]{1,0:T(8,128)(2,1)S(1)}, bf16[192,256]{1,0:T(8,128)(2,1)S(1)}, u32[]{:S(2)}, u32[]{:S(2)}) collective-permute-start(bf16[192,256]{1,0:T(8,128)(2,1)S(1)} %get-tuple-element.72), channel_id=1, source_target_pairs={{0,16},{8,24},{16,0},{24,8},{1,17},{9,25},{17,1},{25,9},{2,18},{10... | collective-permute-start | bytes 294920 | tf_op jit(solution)/shard_map/return/ppermute | solution.py:377
  42.1 8.0 %collective-permute-start.17 = (bf16[192,256]{1,0:T(8,128)(2,1)S(1)}, bf16[192,256]{1,0:T(8,128)(2,1)S(1)}, u32[]{:S(2)}, u32[]{:S(2)}) collective-permute-start(bf16[192,256]{1,0:T(8,128)(2,1)S(1)} %get-tuple-element.73), channel_id=1, source_target_pairs={{0,24},{8,16},{16,8},{24,0},{1,25},{9,17},{17,9},{25,1},{2,26},{10... | collective-permute-start | bytes 294920 | tf_op jit(solution)/shard_map/return/ppermute | solution.py:377
  44.2 6.4 %collective-permute-start.18 = (bf16[192,256]{1,0:T(8,128)(2,1)S(1)}, bf16[192,256]{1,0:T(8,128)(2,1)S(1)}, u32[]{:S(2)}, u32[]{:S(2)}) collective-permute-start(bf16[192,256]{1,0:T(8,128)(2,1)S(1)} %get-tuple-element.74), channel_id=1, source_target_pairs={{0,8},{8,0},{16,24},{24,16},{1,9},{9,1},{17,25},{25,17},{2,10},{10... | collective-permute-start | bytes 294920 | tf_op jit(solution)/shard_map/return/ppermute | solution.py:377
  46.4 4.2 %collective-permute-start.20 = (bf16[192,256]{1,0:T(8,128)(2,1)S(1)}, bf16[192,256]{1,0:T(8,128)(2,1)S(1)}, u32[]{:S(2)}, u32[]{:S(2)}) collective-permute-start(bf16[192,256]{1,0:T(8,128)(2,1)S(1)} %get-tuple-element.80), channel_id=1, source_target_pairs={{0,4},{4,0},{1,5},{5,1},{2,6},{6,2},{3,7},{7,3},{8,12},{12,8},{9,1... | collective-permute-start | bytes 294920 | tf_op jit(solution)/shard_map/return/ppermute | solution.py:451
  46.7 4.3 %collective-permute-start.19 = (bf16[192,256]{1,0:T(8,128)(2,1)S(1)}, bf16[192,256]{1,0:T(8,128)(2,1)S(1)}, u32[]{:S(2)}, u32[]{:S(2)}) collective-permute-start(bf16[192,256]{1,0:T(8,128)(2,1)S(1)} %get-tuple-element.81), channel_id=1, source_target_pairs={{0,4},{4,0},{1,5},{5,1},{2,6},{6,2},{3,7},{7,3},{8,12},{12,8},{9,1... | collective-permute-start | bytes 294920 | tf_op jit(solution)/shard_map/return/ppermute | solution.py:451

commit v22 on v20

--- a/solution.py
+++ b/solution.py
@@ -442,7 +442,7 @@
     with jax.named_scope("return"):
         (d1, d2, d3), outs = lax.optimization_barrier(((d1, d2, d3), outs))
         col_parts = [own, *sides]
-        dqs = [d0] + [other_frames(x, d) for d, x in ((2, d2), (3, d3), (1, d1))]
+        dqs = [d0] + [other_frames(x, d) for d, x in ((2, d2), (1, d1), (3, d3))]
         row_parts = []
         for row, pairs in enumerate(row_sides, start=1):
             for which in range(2):

time: 51.1 us -> 51.2 us (level)
  starting transfers between devices: 30.3 us -> 31 us
  waiting for transfers between devices: 8.69 us -> 8.02 us
    ppermute x2, waiting for transfers between devices: 1.59 us -> 0.58 us  [shards(): sides = [lax.ppermute(x, 'wa', pairs) for x, pairs in zip(sides, col_sides)]]
    ppermute x12, starting transfers between devices: 13.6 us -> 14.3 us  [other_frames(): lax.ppermute(x, 'ta', [(i, i ^ distance) for i in range(sizes['ta'])])]
  transfers between devices with their start and end apart: 21 -> 21, of which waited for: 8 -> 7; matrix products, arithmetic and copies ran while one was open for 0% -> 0% of each run, Pallas kernels for 18% -> 17%
where the time goes in v22:
time: 51.2 us; the launch traced here: 51 us
  starting transfers between devices  31 us (61%)
  Pallas kernels  11.1 us (22%)
  waiting for transfers between devices  8.02 us (16%)
  between operations  0.73 us (1%)
    ppermute x12, starting transfers between devices, other_frames(): lax.ppermute(x, 'ta', [(i, i ^ distance) for i in range(sizes['ta'])])  14.3 us
    pallas_call x7, Pallas kernels, call(): pl.pallas_call(kernel, out_shape=out_shape, in_specs=[pl.BlockSpec(memory...  11.1 us
    ppermute x4, starting transfers between devices, shards(): lax.ppermute(block, 'wa', pairs)  8.2 us
    ppermute x2, starting transfers between devices, shards(): sides = [lax.ppermute(x, 'wa', pairs) for x, pairs in zip(sides, col_sides)]  4.91 us
    ppermute x12, waiting for transfers between devices, other_frames(): lax.ppermute(x, 'ta', [(i, i ^ distance) for i in range(sizes['ta'])])  4.47 us
    ppermute x4, waiting for transfers between devices, shards(): lax.ppermute(block, 'wa', pairs)  2.4 us
    ppermute x1, starting transfers between devices, shards(): kv_rows = [kv] + [lax.ppermute(kv, 'ha', pairs) for pairs in row_sides]  2.11 us
    ppermute x2, starting transfers between devices, shards(): row_parts.append(lax.ppermute(partial_sum, 'ha', pairs))  1.53 us
  transfers between devices with their start and end apart: 21, of which 7 were waited for; matrix products, arithmetic and copies ran while one was open for 0% of the time, Pallas kernels for 17%

profile of v22, /device:TPU:1, one launch (start us, length us, event | category | flops | bytes accessed | tf_op | source)
XLA Modules:
  0.0 51.0 jit_solution(11054234555849652625)
XLA Ops:
  0.6 1.3 %rotate.1 = (bf16[2,192,256]{2,1,0:T(8,128)(2,1)S(1)}, bf16[2,192,256]{2,1,0:T(8,128)(2,1)S(1)}, f32[3,192,128]{2,1,0:T(8,128)S(1)}) custom-call(bf16[192,256]{1,0:T(8,128)(2,1)} %bitcast.12, bf16[192,256]{1,0:T(8,128)(2,1)} %bitcast.13, bf16[192,256]{1,0:T(8,128)(2,1)} %bitcast.14, bf16[192,256]{1,0:T(8,128)(2,1)} %bitcast.15, ...), custom_call_target="tpu_custom_call" | custom-call | bytes 1179648 | tf_op jit(solution)/shard_map/rotate/pallas_call | solution.py:340
  1.9 2.1 %collective-permute-start.4 = (bf16[2,192,256]{2,1,0:T(8,128)(2,1)S(1)}, bf16[2,192,256]{2,1,0:T(8,128)(2,1)S(1)}, u32[]{:S(2)}, u32[]{:S(2)}) collective-permute-start(bf16[2,192,256]{2,1,0:T(8,128)(2,1)S(1)} %get-tuple-element.39.refs_3_.refs_1_.refs_4_), channel_id=1, source_target_pairs={{0,4},{4,0},{1,5},{5,1},{2,6},{6,2},{3,7},{7,3},{8,12},{12,8},{9,1... | collective-permute-start | bytes 589832 | tf_op jit(solution)/shard_map/halo/ppermute | solution.py:382
  4.0 2.3 %collective-permute-start.1 = (bf16[2,192,256]{2,1,0:T(8,128)(2,1)S(1)}, bf16[2,192,256]{2,1,0:T(8,128)(2,1)S(1)}, u32[]{:S(2)}, u32[]{:S(2)}) collective-permute-start(bf16[2,192,256]{2,1,0:T(8,128)(2,1)S(1)} %get-tuple-element.38.refs_0_), channel_id=1, source_target_pairs={{0,16},{8,24},{16,0},{24,8},{1,17},{9,25},{17,1},{25,9},{2,18},{10... | collective-permute-start | bytes 589832 | tf_op jit(solution)/shard_map/halo/ppermute | solution.py:377
  6.3 1.3 %collective-permute-start = (bf16[2,192,256]{2,1,0:T(8,128)(2,1)S(1)}, bf16[2,192,256]{2,1,0:T(8,128)(2,1)S(1)}, u32[]{:S(2)}, u32[]{:S(2)}) collective-permute-start(bf16[2,192,256]{2,1,0:T(8,128)(2,1)S(1)} %get-tuple-element.38.refs_0_), channel_id=1, source_target_pairs={{0,8},{8,0},{16,24},{24,16},{1,9},{9,1},{17,25},{25,17},{2,10},{10... | collective-permute-start | bytes 589832 | tf_op jit(solution)/shard_map/halo/ppermute | solution.py:377
  7.6 4.5 %collective-permute-start.3 = (bf16[2,192,256]{2,1,0:T(8,128)(2,1)S(1)}, bf16[2,192,256]{2,1,0:T(8,128)(2,1)S(1)}, u32[]{:S(2)}, u32[]{:S(2)}) collective-permute-start(bf16[2,192,256]{2,1,0:T(8,128)(2,1)S(1)} %get-tuple-element.39.refs_3_.refs_1_.refs_4_), channel_id=1, source_target_pairs={{0,0},{1,2},{2,1},{3,3},{4,4},{5,6},{6,5},{7,7},{8,8},{9,10},{10,9... | collective-permute-start | bytes 589832 | tf_op jit(solution)/shard_map/halo/ppermute | solution.py:387
  12.2 0.1 collective-permute-start.2
  12.2 0.0 collective-permute-done.4.refs_6_.refs_4_.refs_5_
  12.2 1.9 %collective-permute-start.6 = (bf16[2,192,256]{2,1,0:T(8,128)(2,1)S(1)}, bf16[2,192,256]{2,1,0:T(8,128)(2,1)S(1)}, u32[]{:S(2)}, u32[]{:S(2)}) collective-permute-start(bf16[2,192,256]{2,1,0:T(8,128)(2,1)S(1)} %collective-permute-done.4.refs_6_.refs_4_.refs_5_), channel_id=1, source_target_pairs={{0,0},{1,2},{2,1},{3,3},{4,4},{5,6},{6,5},{7,7},{8,8},{9,10},{10,9... | collective-permute-start | bytes 589832 | tf_op jit(solution)/shard_map/halo/ppermute | solution.py:387
  14.2 0.7 %collective-permute-done.1.refs_2_ = bf16[2,192,256]{2,1,0:T(8,128)(2,1)S(1)} collective-permute-done((bf16[2,192,256]{2,1,0:T(8,128)(2,1)S(1)}, bf16[2,192,256]{2,1,0:T(8,128)(2,1)S(1)}, u32[]{:S(2)}, u32[]{:S(2)}) %collective-permute-start.1) | collective-permute-done | bytes 196640 | tf_op jit(solution)/shard_map/halo/ppermute | solution.py:377
  14.9 1.7 %collective-permute-start.5 = (bf16[2,192,256]{2,1,0:T(8,128)(2,1)S(1)}, bf16[2,192,256]{2,1,0:T(8,128)(2,1)S(1)}, u32[]{:S(2)}, u32[]{:S(2)}) collective-permute-start(bf16[2,192,256]{2,1,0:T(8,128)(2,1)S(1)} %collective-permute-done.4.refs_6_.refs_4_.refs_5_), channel_id=1, source_target_pairs={{0,1},{1,0},{2,3},{3,2},{4,5},{5,4},{6,7},{7,6},{8,9},{9,8},{10,11... | collective-permute-start | bytes 589832 | tf_op jit(solution)/shard_map/halo/ppermute | solution.py:387
  16.5 0.0 collective-permute-done.refs_1_
  16.5 0.3 collective-permute-start.7
  16.8 0.0 collective-permute-done.3.refs_5_.refs_3_.refs_6_
  16.8 0.0 collective-permute-done.2.refs_4_.refs_2_
  16.8 2.4 %collective-permute-done.6.refs_8_.refs_6_.refs_7_ = bf16[2,192,256]{2,1,0:T(8,128)(2,1)S(1)} collective-permute-done((bf16[2,192,256]{2,1,0:T(8,128)(2,1)S(1)}, bf16[2,192,256]{2,1,0:T(8,128)(2,1)S(1)}, u32[]{:S(2)}, u32[]{:S(2)}) %collective-permute-start.6) | collective-permute-done | bytes 196640 | tf_op jit(solution)/shard_map/halo/ppermute | solution.py:387
  19.2 0.0 collective-permute-done.5.refs_7_.refs_5_
  19.2 2.4 %attend.2 = (bf16[192,256]{1,0:T(8,128)(2,1)S(1)}, bf16[192,256]{1,0:T(8,128)(2,1)S(1)}, bf16[192,256]{1,0:T(8,128)(2,1)S(1)}, f32[576,128]{1,0:T(8,128)S(1)}) custom-call(bf16[2,192,256]{2,1,0:T(8,128)(2,1)S(1)} %get-tuple-element.38.refs_0_, bf16[2,192,256]{2,1,0:T(8,128)(2,1)S(1)} %collective-permute-done.refs_1_, ...), custom_call_target="tpu_custom_call" | custom-call | flops 5435817984 | bytes 2359296 | tf_op jit(solution)/shard_map/attend/pallas_call | solution.py:340
  21.6 0.8 %collective-permute-start.8 = (bf16[192,256]{1,0:T(8,128)(2,1)S(1)}, bf16[192,256]{1,0:T(8,128)(2,1)S(1)}, u32[]{:S(2)}, u32[]{:S(2)}) collective-permute-start(bf16[192,256]{1,0:T(8,128)(2,1)S(1)} %get-tuple-element.43), channel_id=1, source_target_pairs={{0,16},{8,24},{16,0},{24,8},{1,17},{9,25},{17,1},{25,9},{2,18},{10... | collective-permute-start | bytes 294920 | tf_op jit(solution)/shard_map/merge/ppermute | solution.py:377
  22.4 1.0 %collective-permute-start.9 = (bf16[192,256]{1,0:T(8,128)(2,1)S(1)}, bf16[192,256]{1,0:T(8,128)(2,1)S(1)}, u32[]{:S(2)}, u32[]{:S(2)}) collective-permute-start(bf16[192,256]{1,0:T(8,128)(2,1)S(1)} %get-tuple-element.44), channel_id=1, source_target_pairs={{0,8},{8,0},{16,24},{24,16},{1,9},{9,1},{17,25},{25,17},{2,10},{10... | collective-permute-start | bytes 294920 | tf_op jit(solution)/shard_map/merge/ppermute | solution.py:377
  23.4 0.0 collective-permute-done.7.refs_0_.refs_3_
  23.4 1.0 %attend.3 = (bf16[192,256]{1,0:T(8,128)(2,1)S(1)}, f32[8,768]{1,0:T(8,128)S(1)}) custom-call(bf16[2,192,256]{2,1,0:T(8,128)(2,1)S(1)} %collective-permute-done.7.refs_0_.refs_3_, bf16[2,192,256]{2,1,0:T(8,128)(2,1)S(1)} %get-tuple-element.39.refs_3_.refs_1_.refs_4_, bf16[2,192,256]{2,1,0:T(8,128)(2,1)S(1)} %collective-permute-done.2.refs_4_.refs_2_, ...), custom_call_target="tpu_custom_call" | custom-call | flops 1811939328 | bytes 1794048 | tf_op jit(solution)/shard_map/attend/pallas_call | solution.py:340
  24.4 1.8 %collective-permute-start.12 = (f32[8,768]{1,0:T(8,128)S(1)}, f32[8,768]{1,0:T(8,128)S(1)}, u32[]{:S(2)}, u32[]{:S(2)}) collective-permute-start(f32[8,768]{1,0:T(8,128)S(1)} %get-tuple-element.45.refs_8_), channel_id=1, source_target_pairs={{0,16},{8,24},{16,0},{24,8},{1,17},{9,25},{17,1},{25,9},{2,18},{10... | collective-permute-start | bytes 73736 | tf_op jit(solution)/shard_map/merge/ppermute | solution.py:377
  26.2 1.1 %collective-permute-start.11 = (f32[8,768]{1,0:T(8,128)S(1)}, f32[8,768]{1,0:T(8,128)S(1)}, u32[]{:S(2)}, u32[]{:S(2)}) collective-permute-start(f32[8,768]{1,0:T(8,128)S(1)} %get-tuple-element.45.refs_8_), channel_id=1, source_target_pairs={{0,24},{8,16},{16,8},{24,0},{1,25},{9,17},{17,9},{25,1},{2,26},{10... | collective-permute-start | bytes 73736 | tf_op jit(solution)/shard_map/merge/ppermute | solution.py:377
  27.3 1.3 %collective-permute-done.8.refs_2_ = bf16[192,256]{1,0:T(8,128)(2,1)S(1)} collective-permute-done((bf16[192,256]{1,0:T(8,128)(2,1)S(1)}, bf16[192,256]{1,0:T(8,128)(2,1)S(1)}, u32[]{:S(2)}, u32[]{:S(2)}) %collective-permute-start.8) | collective-permute-done | bytes 98336 | tf_op jit(solution)/shard_map/merge/ppermute | solution.py:377
  28.6 0.0 collective-permute-done.9.refs_3_
  28.6 0.0 collective-permute-start.10
  28.6 2.1 %collective-permute-start.13 = (bf16[192,256]{1,0:T(8,128)(2,1)S(1)}, bf16[192,256]{1,0:T(8,128)(2,1)S(1)}, u32[]{:S(2)}, u32[]{:S(2)}) collective-permute-start(bf16[192,256]{1,0:T(8,128)(2,1)S(1)} %get-tuple-element.52), channel_id=1, source_target_pairs={{0,24},{8,16},{16,8},{24,0},{1,25},{9,17},{17,9},{25,1},{2,26},{10... | collective-permute-start | bytes 294920 | tf_op jit(solution)/shard_map/merge/ppermute | solution.py:377
  30.7 0.0 collective-permute-done.12.refs_11_
  30.7 0.0 collective-permute-done.11.refs_10_
  30.7 0.6 %collective-permute-done.10.refs_9_ = f32[8,768]{1,0:T(8,128)S(1)} collective-permute-done((f32[8,768]{1,0:T(8,128)S(1)}, f32[8,768]{1,0:T(8,128)S(1)}, u32[]{:S(2)}, u32[]{:S(2)}) %collective-permute-start.10) | collective-permute-done | bytes 24608 | tf_op jit(solution)/shard_map/merge/ppermute | solution.py:377
  31.3 2.9 %gradients.2 = (f32[2,128,768]{2,1,0:T(8,128)S(1)}, f32[2,768]{1,0:T(2,128)S(1)}, f32[2,768]{1,0:T(2,128)S(1)}, f32[192,128]{1,0:T(8,128)S(1)}, bf16[2,2,192,256...) custom-call(bf16[2,192,256]{2,1,0:T(8,128)(2,1)S(1)} %get-tuple-element.38.refs_0_, ...), custom_call_target="tpu_custom_call" | custom-call | flops 12079595520 | bytes 3354624 | tf_op jit(solution)/shard_map/gradients/pallas_call | solution.py:340
  34.2 1.7 %collective-permute-start.14 = (bf16[2,2,192,256]{3,2,1,0:T(8,128)(2,1)S(1)}, bf16[2,2,192,256]{3,2,1,0:T(8,128)(2,1)S(1)}, u32[]{:S(2)}, u32[]{:S(2)}) collective-permute-start(bf16[2,2,192,256]{3,2,1,0:T(8,128)(2,1)S(1)} %get-tuple-element.59), channel_id=1, source_target_pairs={{0,1},{1,0},{2,3},{3,2},{4,5},{5,4},{6,7},{7,6},{8,9},{9,8},{10,11... | collective-permute-start | bytes 1179656 | tf_op jit(solution)/shard_map/gradients/ppermute | solution.py:440
  35.9 3.2 %collective-permute-start.15 = (bf16[2,2,192,256]{3,2,1,0:T(8,128)(2,1)S(1)}, bf16[2,2,192,256]{3,2,1,0:T(8,128)(2,1)S(1)}, u32[]{:S(2)}, u32[]{:S(2)}) collective-permute-start(bf16[2,2,192,256]{3,2,1,0:T(8,128)(2,1)S(1)} %get-tuple-element.60), channel_id=1, source_target_pairs={{0,0},{1,2},{2,1},{3,3},{4,4},{5,6},{6,5},{7,7},{8,8},{9,10},{10,9... | collective-permute-start | bytes 1179656 | tf_op jit(solution)/shard_map/gradients/ppermute | solution.py:440
  39.1 1.7 %gradients.3 = (bf16[192,256]{1,0:T(8,128)(2,1)S(1)}, bf16[192,256]{1,0:T(8,128)(2,1)S(1)}, bf16[192,256]{1,0:T(8,128)(2,1)S(1)}, bf16[192,256]{1,0:T(8,128)(2,1)S(1)}, bf16[2,2,192,256]{3,2,1,0:T(8,128)(2,1)S(1)}) custom-call(bf16[2,192,256]{2,1,0:T(8,128)(2,1)S(1)} %get-tuple-element.38.refs_0_, bf16[2,192,256]{2,1,0:T(8,128)(2,1)S(1)} %collective-permute-done.refs_1_, ...), custom_call_target="tpu_custom_call" | custom-call | flops 6039797760 | bytes 2764800 | tf_op jit(solution)/shard_map/gradients/pallas_call | solution.py:340
  40.8 0.0 collective-permute-done.13.refs_1_
  40.8 1.7 %collective-permute-start.16 = (bf16[192,256]{1,0:T(8,128)(2,1)S(1)}, bf16[192,256]{1,0:T(8,128)(2,1)S(1)}, u32[]{:S(2)}, u32[]{:S(2)}) collective-permute-start(bf16[192,256]{1,0:T(8,128)(2,1)S(1)} %get-tuple-element.64), channel_id=1, source_target_pairs={{0,16},{8,24},{16,0},{24,8},{1,17},{9,25},{17,1},{25,9},{2,18},{10... | collective-permute-start | bytes 294920 | tf_op jit(solution)/shard_map/return/ppermute | solution.py:377
  42.5 1.1 %collective-permute-start.17 = (bf16[192,256]{1,0:T(8,128)(2,1)S(1)}, bf16[192,256]{1,0:T(8,128)(2,1)S(1)}, u32[]{:S(2)}, u32[]{:S(2)}) collective-permute-start(bf16[192,256]{1,0:T(8,128)(2,1)S(1)} %get-tuple-element.65), channel_id=1, source_target_pairs={{0,8},{8,0},{16,24},{24,16},{1,9},{9,1},{17,25},{25,17},{2,10},{10... | collective-permute-start | bytes 294920 | tf_op jit(solution)/shard_map/return/ppermute | solution.py:377
  43.6 0.8 %collective-permute-start.18 = (bf16[192,256]{1,0:T(8,128)(2,1)S(1)}, bf16[192,256]{1,0:T(8,128)(2,1)S(1)}, u32[]{:S(2)}, u32[]{:S(2)}) collective-permute-start(bf16[192,256]{1,0:T(8,128)(2,1)S(1)} %get-tuple-element.66), channel_id=1, source_target_pairs={{0,24},{8,16},{16,8},{24,0},{1,25},{9,17},{17,9},{25,1},{2,26},{10... | collective-permute-start | bytes 294920 | tf_op jit(solution)/shard_map/return/ppermute | solution.py:377
  44.4 0.0 collective-permute-done.14.refs_5_
  44.5 0.6 %collective-permute-done.15.refs_6_ = bf16[2,2,192,256]{3,2,1,0:T(8,128)(2,1)S(1)} collective-permute-done((bf16[2,2,192,256]{3,2,1,0:T(8,128)(2,1)S(1)}, bf16[2,2,192,256]{3,2,1,0:T(8,128)(2,1)S(1)}, u32[]{:S(2)}, u32[]{:S(2)}) %collective-permute-start.15) | collective-permute-done | bytes 393248 | tf_op jit(solution)/shard_map/gradients/ppermute | solution.py:440
  45.0 0.1 fusion.1
  45.1 0.5 collective-permute-start.20
  45.6 1.0 %collective-permute-start.19 = (bf16[192,256]{1,0:T(8,128)(2,1)S(1)}, bf16[192,256]{1,0:T(8,128)(2,1)S(1)}, u32[]{:S(2)}, u32[]{:S(2)}) collective-permute-start(bf16[192,256]{1,0:T(8,128)(2,1)S(1)} %get-tuple-element.73), channel_id=1, source_target_pairs={{0,4},{4,0},{1,5},{5,1},{2,6},{6,2},{3,7},{7,3},{8,12},{12,8},{9,1... | collective-permute-start | bytes 294920 | tf_op jit(solution)/shard_map/return/ppermute | solution.py:450
  46.6 1.0 %finish.2 = (bf16[192,256]{1,0:T(8,128)(2,1)}, f32[2,192,256]{2,1,0:T(8,128)S(1)}) custom-call(bf16[192,256]{1,0:T(8,128)(2,1)S(1)} %get-tuple-element.40.refs_0_, bf16[192,256]{1,0:T(8,128)(2,1)S(1)} %collective-permute-done.13.refs_1_, bf16[192,256]{1,0:T(8,128)(2,1)S(1)} %collective-permute-done.8.refs_2_, ...), custom_call_target="tpu_custom_call" | custom-call | bytes 2162688 | tf_op jit(solution)/shard_map/finish/pallas_call | solution.py:340
  47.6 1.9 %collective-permute-done.16.refs_1_ = bf16[192,256]{1,0:T(8,128)(2,1)S(1)} collective-permute-done((bf16[192,256]{1,0:T(8,128)(2,1)S(1)}, bf16[192,256]{1,0:T(8,128)(2,1)S(1)}, u32[]{:S(2)}, u32[]{:S(2)}) %collective-permute-start.16) | collective-permute-done | bytes 98336 | tf_op jit(solution)/shard_map/return/ppermute | solution.py:377
  49.5 0.0 collective-permute-done.17.refs_2_
  49.5 0.0 collective-permute-done.18.refs_3_
  49.5 0.0 collective-permute-done.20.refs_5_
  49.5 0.6 %collective-permute-done.19.refs_4_ = bf16[192,256]{1,0:T(8,128)(2,1)S(1)} collective-permute-done((bf16[192,256]{1,0:T(8,128)(2,1)S(1)}, bf16[192,256]{1,0:T(8,128)(2,1)S(1)}, u32[]{:S(2)}, u32[]{:S(2)}) %collective-permute-start.19) | collective-permute-done | bytes 98336 | tf_op jit(solution)/shard_map/return/ppermute | solution.py:450
  50.0 1.0 %finish.3 = (bf16[192,256]{1,0:T(8,128)(2,1)}, bf16[192,256]{1,0:T(8,128)(2,1)}, bf16[192,256]{1,0:T(8,128)(2,1)}) custom-call(bf16[192,256]{1,0:T(8,128)(2,1)S(1)} %get-tuple-element.63.refs_0_, bf16[192,256]{1,0:T(8,128)(2,1)S(1)} %collective-permute-done.16.refs_1_, bf16[192,256]{1,0:T(8,128)(2,1)S(1)} %collective-permute-done.17.refs_2_, ...), custom_call_target="tpu_custom_call" | custom-call | bytes 1572864 | tf_op jit(solution)/shard_map/finish/pallas_call | solution.py:340
Async XLA Ops:
  1.9 10.3 %collective-permute-start.4 = (bf16[2,192,256]{2,1,0:T(8,128)(2,1)S(1)}, bf16[2,192,256]{2,1,0:T(8,128)(2,1)S(1)}, u32[]{:S(2)}, u32[]{:S(2)}) collective-permute-start(bf16[2,192,256]{2,1,0:T(8,128)(2,1)S(1)} %get-tuple-element.39.refs_3_.refs_1_.refs_4_), channel_id=1, source_target_pairs={{0,4},{4,0},{1,5},{5,1},{2,6},{6,2},{3,7},{7,3},{8,12},{12,8},{9,1... | collective-permute-start | bytes 589832 | tf_op jit(solution)/shard_map/halo/ppermute | solution.py:382
  4.0 10.9 %collective-permute-start.1 = (bf16[2,192,256]{2,1,0:T(8,128)(2,1)S(1)}, bf16[2,192,256]{2,1,0:T(8,128)(2,1)S(1)}, u32[]{:S(2)}, u32[]{:S(2)}) collective-permute-start(bf16[2,192,256]{2,1,0:T(8,128)(2,1)S(1)} %get-tuple-element.38.refs_0_), channel_id=1, source_target_pairs={{0,16},{8,24},{16,0},{24,8},{1,17},{9,25},{17,1},{25,9},{2,18},{10... | collective-permute-start | bytes 589832 | tf_op jit(solution)/shard_map/halo/ppermute | solution.py:377
  6.3 10.2 %collective-permute-start = (bf16[2,192,256]{2,1,0:T(8,128)(2,1)S(1)}, bf16[2,192,256]{2,1,0:T(8,128)(2,1)S(1)}, u32[]{:S(2)}, u32[]{:S(2)}) collective-permute-start(bf16[2,192,256]{2,1,0:T(8,128)(2,1)S(1)} %get-tuple-element.38.refs_0_), channel_id=1, source_target_pairs={{0,8},{8,0},{16,24},{24,16},{1,9},{9,1},{17,25},{25,17},{2,10},{10... | collective-permute-start | bytes 589832 | tf_op jit(solution)/shard_map/halo/ppermute | solution.py:377
  7.6 9.2 %collective-permute-start.3 = (bf16[2,192,256]{2,1,0:T(8,128)(2,1)S(1)}, bf16[2,192,256]{2,1,0:T(8,128)(2,1)S(1)}, u32[]{:S(2)}, u32[]{:S(2)}) collective-permute-start(bf16[2,192,256]{2,1,0:T(8,128)(2,1)S(1)} %get-tuple-element.39.refs_3_.refs_1_.refs_4_), channel_id=1, source_target_pairs={{0,0},{1,2},{2,1},{3,3},{4,4},{5,6},{6,5},{7,7},{8,8},{9,10},{10,9... | collective-permute-start | bytes 589832 | tf_op jit(solution)/shard_map/halo/ppermute | solution.py:387
  12.2 4.7 %collective-permute-start.2 = (bf16[2,192,256]{2,1,0:T(8,128)(2,1)S(1)}, bf16[2,192,256]{2,1,0:T(8,128)(2,1)S(1)}, u32[]{:S(2)}, u32[]{:S(2)}) collective-permute-start(bf16[2,192,256]{2,1,0:T(8,128)(2,1)S(1)} %get-tuple-element.39.refs_3_.refs_1_.refs_4_), channel_id=1, source_target_pairs={{0,1},{1,0},{2,3},{3,2},{4,5},{5,4},{6,7},{7,6},{8,9},{9,8},{10,11... | collective-permute-start | bytes 589832 | tf_op jit(solution)/shard_map/halo/ppermute | solution.py:387
  12.2 7.0 %collective-permute-start.6 = (bf16[2,192,256]{2,1,0:T(8,128)(2,1)S(1)}, bf16[2,192,256]{2,1,0:T(8,128)(2,1)S(1)}, u32[]{:S(2)}, u32[]{:S(2)}) collective-permute-start(bf16[2,192,256]{2,1,0:T(8,128)(2,1)S(1)} %collective-permute-done.4.refs_6_.refs_4_.refs_5_), channel_id=1, source_target_pairs={{0,0},{1,2},{2,1},{3,3},{4,4},{5,6},{6,5},{7,7},{8,8},{9,10},{10,9... | collective-permute-start | bytes 589832 | tf_op jit(solution)/shard_map/halo/ppermute | solution.py:387
  14.9 4.4 %collective-permute-start.5 = (bf16[2,192,256]{2,1,0:T(8,128)(2,1)S(1)}, bf16[2,192,256]{2,1,0:T(8,128)(2,1)S(1)}, u32[]{:S(2)}, u32[]{:S(2)}) collective-permute-start(bf16[2,192,256]{2,1,0:T(8,128)(2,1)S(1)} %collective-permute-done.4.refs_6_.refs_4_.refs_5_), channel_id=1, source_target_pairs={{0,1},{1,0},{2,3},{3,2},{4,5},{5,4},{6,7},{7,6},{8,9},{9,8},{10,11... | collective-permute-start | bytes 589832 | tf_op jit(solution)/shard_map/halo/ppermute | solution.py:387
  16.5 6.9 %collective-permute-start.7 = (bf16[2,192,256]{2,1,0:T(8,128)(2,1)S(1)}, bf16[2,192,256]{2,1,0:T(8,128)(2,1)S(1)}, u32[]{:S(2)}, u32[]{:S(2)}) collective-permute-start(bf16[2,192,256]{2,1,0:T(8,128)(2,1)S(1)} %collective-permute-done.1.refs_2_), channel_id=1, source_target_pairs={{0,8},{8,0},{16,24},{24,16},{1,9},{9,1},{17,25},{25,17},{2,10},{10... | collective-permute-start | bytes 589832 | tf_op jit(solution)/shard_map/halo/ppermute | solution.py:377
  21.6 7.0 %collective-permute-start.8 = (bf16[192,256]{1,0:T(8,128)(2,1)S(1)}, bf16[192,256]{1,0:T(8,128)(2,1)S(1)}, u32[]{:S(2)}, u32[]{:S(2)}) collective-permute-start(bf16[192,256]{1,0:T(8,128)(2,1)S(1)} %get-tuple-element.43), channel_id=1, source_target_pairs={{0,16},{8,24},{16,0},{24,8},{1,17},{9,25},{17,1},{25,9},{2,18},{10... | collective-permute-start | bytes 294920 | tf_op jit(solution)/shard_map/merge/ppermute | solution.py:377
  22.4 6.2 %collective-permute-start.9 = (bf16[192,256]{1,0:T(8,128)(2,1)S(1)}, bf16[192,256]{1,0:T(8,128)(2,1)S(1)}, u32[]{:S(2)}, u32[]{:S(2)}) collective-permute-start(bf16[192,256]{1,0:T(8,128)(2,1)S(1)} %get-tuple-element.44), channel_id=1, source_target_pairs={{0,8},{8,0},{16,24},{24,16},{1,9},{9,1},{17,25},{25,17},{2,10},{10... | collective-permute-start | bytes 294920 | tf_op jit(solution)/shard_map/merge/ppermute | solution.py:377
  24.4 6.3 %collective-permute-start.12 = (f32[8,768]{1,0:T(8,128)S(1)}, f32[8,768]{1,0:T(8,128)S(1)}, u32[]{:S(2)}, u32[]{:S(2)}) collective-permute-start(f32[8,768]{1,0:T(8,128)S(1)} %get-tuple-element.45.refs_8_), channel_id=1, source_target_pairs={{0,16},{8,24},{16,0},{24,8},{1,17},{9,25},{17,1},{25,9},{2,18},{10... | collective-permute-start | bytes 73736 | tf_op jit(solution)/shard_map/merge/ppermute | solution.py:377
  26.2 4.5 %collective-permute-start.11 = (f32[8,768]{1,0:T(8,128)S(1)}, f32[8,768]{1,0:T(8,128)S(1)}, u32[]{:S(2)}, u32[]{:S(2)}) collective-permute-start(f32[8,768]{1,0:T(8,128)S(1)} %get-tuple-element.45.refs_8_), channel_id=1, source_target_pairs={{0,24},{8,16},{16,8},{24,0},{1,25},{9,17},{17,9},{25,1},{2,26},{10... | collective-permute-start | bytes 73736 | tf_op jit(solution)/shard_map/merge/ppermute | solution.py:377
  28.6 2.7 %collective-permute-start.10 = (f32[8,768]{1,0:T(8,128)S(1)}, f32[8,768]{1,0:T(8,128)S(1)}, u32[]{:S(2)}, u32[]{:S(2)}) collective-permute-start(f32[8,768]{1,0:T(8,128)S(1)} %get-tuple-element.45.refs_8_), channel_id=1, source_target_pairs={{0,8},{8,0},{16,24},{24,16},{1,9},{9,1},{17,25},{25,17},{2,10},{10... | collective-permute-start | bytes 73736 | tf_op jit(solution)/shard_map/merge/ppermute | solution.py:377
  28.6 12.2 %collective-permute-start.13 = (bf16[192,256]{1,0:T(8,128)(2,1)S(1)}, bf16[192,256]{1,0:T(8,128)(2,1)S(1)}, u32[]{:S(2)}, u32[]{:S(2)}) collective-permute-start(bf16[192,256]{1,0:T(8,128)(2,1)S(1)} %get-tuple-element.52), channel_id=1, source_target_pairs={{0,24},{8,16},{16,8},{24,0},{1,25},{9,17},{17,9},{25,1},{2,26},{10... | collective-permute-start | bytes 294920 | tf_op jit(solution)/shard_map/merge/ppermute | solution.py:377
  34.2 10.2 %collective-permute-start.14 = (bf16[2,2,192,256]{3,2,1,0:T(8,128)(2,1)S(1)}, bf16[2,2,192,256]{3,2,1,0:T(8,128)(2,1)S(1)}, u32[]{:S(2)}, u32[]{:S(2)}) collective-permute-start(bf16[2,2,192,256]{3,2,1,0:T(8,128)(2,1)S(1)} %get-tuple-element.59), channel_id=1, source_target_pairs={{0,1},{1,0},{2,3},{3,2},{4,5},{5,4},{6,7},{7,6},{8,9},{9,8},{10,11... | collective-permute-start | bytes 1179656 | tf_op jit(solution)/shard_map/gradients/ppermute | solution.py:440
  35.9 9.1 %collective-permute-start.15 = (bf16[2,2,192,256]{3,2,1,0:T(8,128)(2,1)S(1)}, bf16[2,2,192,256]{3,2,1,0:T(8,128)(2,1)S(1)}, u32[]{:S(2)}, u32[]{:S(2)}) collective-permute-start(bf16[2,2,192,256]{3,2,1,0:T(8,128)(2,1)S(1)} %get-tuple-element.60), channel_id=1, source_target_pairs={{0,0},{1,2},{2,1},{3,3},{4,4},{5,6},{6,5},{7,7},{8,8},{9,10},{10,9... | collective-permute-start | bytes 1179656 | tf_op jit(solution)/shard_map/gradients/ppermute | solution.py:440
  40.8 8.6 %collective-permute-start.16 = (bf16[192,256]{1,0:T(8,128)(2,1)S(1)}, bf16[192,256]{1,0:T(8,128)(2,1)S(1)}, u32[]{:S(2)}, u32[]{:S(2)}) collective-permute-start(bf16[192,256]{1,0:T(8,128)(2,1)S(1)} %get-tuple-element.64), channel_id=1, source_target_pairs={{0,16},{8,24},{16,0},{24,8},{1,17},{9,25},{17,1},{25,9},{2,18},{10... | collective-permute-start | bytes 294920 | tf_op jit(solution)/shard_map/return/ppermute | solution.py:377
  42.5 7.0 %collective-permute-start.17 = (bf16[192,256]{1,0:T(8,128)(2,1)S(1)}, bf16[192,256]{1,0:T(8,128)(2,1)S(1)}, u32[]{:S(2)}, u32[]{:S(2)}) collective-permute-start(bf16[192,256]{1,0:T(8,128)(2,1)S(1)} %get-tuple-element.65), channel_id=1, source_target_pairs={{0,8},{8,0},{16,24},{24,16},{1,9},{9,1},{17,25},{25,17},{2,10},{10... | collective-permute-start | bytes 294920 | tf_op jit(solution)/shard_map/return/ppermute | solution.py:377
  43.6 5.8 %collective-permute-start.18 = (bf16[192,256]{1,0:T(8,128)(2,1)S(1)}, bf16[192,256]{1,0:T(8,128)(2,1)S(1)}, u32[]{:S(2)}, u32[]{:S(2)}) collective-permute-start(bf16[192,256]{1,0:T(8,128)(2,1)S(1)} %get-tuple-element.66), channel_id=1, source_target_pairs={{0,24},{8,16},{16,8},{24,0},{1,25},{9,17},{17,9},{25,1},{2,26},{10... | collective-permute-start | bytes 294920 | tf_op jit(solution)/shard_map/return/ppermute | solution.py:377
  45.1 4.4 %collective-permute-start.20 = (bf16[192,256]{1,0:T(8,128)(2,1)S(1)}, bf16[192,256]{1,0:T(8,128)(2,1)S(1)}, u32[]{:S(2)}, u32[]{:S(2)}) collective-permute-start(bf16[192,256]{1,0:T(8,128)(2,1)S(1)} %get-tuple-element.72), channel_id=1, source_target_pairs={{0,4},{4,0},{1,5},{5,1},{2,6},{6,2},{3,7},{7,3},{8,12},{12,8},{9,1... | collective-permute-start | bytes 294920 | tf_op jit(solution)/shard_map/return/ppermute | solution.py:450
  45.6 4.4 %collective-permute-start.19 = (bf16[192,256]{1,0:T(8,128)(2,1)S(1)}, bf16[192,256]{1,0:T(8,128)(2,1)S(1)}, u32[]{:S(2)}, u32[]{:S(2)}) collective-permute-start(bf16[192,256]{1,0:T(8,128)(2,1)S(1)} %get-tuple-element.73), channel_id=1, source_target_pairs={{0,4},{4,0},{1,5},{5,1},{2,6},{6,2},{3,7},{7,3},{8,12},{12,8},{9,1... | collective-permute-start | bytes 294920 | tf_op jit(solution)/shard_map/return/ppermute | solution.py:450

commit v23 on v20

--- a/solution.py
+++ b/solution.py
@@ -184,8 +184,10 @@
         for raw, (members, bias) in zip(scores, spans):
             shift = best if bias is None else best - bias
             weights = jnp.exp2(raw * SCALE_LOG2 - shift)
-            part = jnp.sum(weights, axis=1, keepdims=True)
-            piece = dot_nn(weights.astype(BF16), joined(members, 1, cut))
+            values = joined(members, 1, cut)
+            wide = jnp.concatenate([values, jnp.ones_like(values)], axis=1)
+            both = dot_nn(weights.astype(BF16), wide)
+            piece, part = both[:, :DH], both[:, DH : DH + 1]
             total = part if total is None else total + part
             out = piece if out is None else out + piece
         out = out * (1.0 / total)

time: 51.1 us -> 52.2 us (1.022)
  Pallas kernels: 11.1 us -> 12.5 us
    pallas_call x7, Pallas kernels: 11.1 us -> 12.5 us  [call(): pl.pallas_call(kernel, out_shape=out_shape, in_specs=[pl.BlockSpec(memory...]
  transfers between devices with their start and end apart: 21 -> 21, of which waited for: 8 -> 8; matrix products, arithmetic and copies ran while one was open for 0% -> 0% of each run, Pallas kernels for 18% -> 20%
where the time goes in v23:
time: 52.2 us; the launch traced here: 52 us
  starting transfers between devices  30.1 us (58%)
  Pallas kernels  12.5 us (24%)
  waiting for transfers between devices  8.62 us (17%)
  between operations  0.72 us (1%)
    ppermute x12, starting transfers between devices, other_frames(): lax.ppermute(x, 'ta', [(i, i ^ distance) for i in range(sizes['ta'])])  13.7 us
    pallas_call x7, Pallas kernels, call(): pl.pallas_call(kernel, out_shape=out_shape, in_specs=[pl.BlockSpec(memory...  12.5 us
    ppermute x4, starting transfers between devices, shards(): lax.ppermute(block, 'wa', pairs)  8.2 us
    ppermute x2, starting transfers between devices, shards(): sides = [lax.ppermute(x, 'wa', pairs) for x, pairs in zip(sides, col_sides)]  4.58 us
    ppermute x12, waiting for transfers between devices, other_frames(): lax.ppermute(x, 'ta', [(i, i ^ distance) for i in range(sizes['ta'])])  4.58 us
    ppermute x4, waiting for transfers between devices, shards(): lax.ppermute(block, 'wa', pairs)  2.4 us
    ppermute x1, starting transfers between devices, shards(): kv_rows = [kv] + [lax.ppermute(kv, 'ha', pairs) for pairs in row_sides]  2.11 us
    ppermute x2, starting transfers between devices, shards(): row_parts.append(lax.ppermute(partial_sum, 'ha', pairs))  1.53 us
  transfers between devices with their start and end apart: 21, of which 8 were waited for; matrix products, arithmetic and copies ran while one was open for 0% of the time, Pallas kernels for 20%

profile of v23, /device:TPU:1, one launch (start us, length us, event | category | flops | bytes accessed | tf_op | source)
XLA Modules:
  0.0 52.0 jit_solution(15743584440913152959)
XLA Ops:
  0.6 1.3 %rotate.1 = (bf16[2,192,256]{2,1,0:T(8,128)(2,1)S(1)}, bf16[2,192,256]{2,1,0:T(8,128)(2,1)S(1)}, f32[3,192,128]{2,1,0:T(8,128)S(1)}) custom-call(bf16[192,256]{1,0:T(8,128)(2,1)} %bitcast.12, bf16[192,256]{1,0:T(8,128)(2,1)} %bitcast.13, bf16[192,256]{1,0:T(8,128)(2,1)} %bitcast.14, bf16[192,256]{1,0:T(8,128)(2,1)} %bitcast.15, ...), custom_call_target="tpu_custom_call" | custom-call | bytes 1179648 | tf_op jit(solution)/shard_map/rotate/pallas_call | solution.py:342
  1.9 2.1 %collective-permute-start.4 = (bf16[2,192,256]{2,1,0:T(8,128)(2,1)S(1)}, bf16[2,192,256]{2,1,0:T(8,128)(2,1)S(1)}, u32[]{:S(2)}, u32[]{:S(2)}) collective-permute-start(bf16[2,192,256]{2,1,0:T(8,128)(2,1)S(1)} %get-tuple-element.39.refs_3_.refs_1_.refs_4_), channel_id=1, source_target_pairs={{0,4},{4,0},{1,5},{5,1},{2,6},{6,2},{3,7},{7,3},{8,12},{12,8},{9,1... | collective-permute-start | bytes 589832 | tf_op jit(solution)/shard_map/halo/ppermute | solution.py:384
  4.0 2.3 %collective-permute-start.1 = (bf16[2,192,256]{2,1,0:T(8,128)(2,1)S(1)}, bf16[2,192,256]{2,1,0:T(8,128)(2,1)S(1)}, u32[]{:S(2)}, u32[]{:S(2)}) collective-permute-start(bf16[2,192,256]{2,1,0:T(8,128)(2,1)S(1)} %get-tuple-element.38.refs_0_), channel_id=1, source_target_pairs={{0,16},{8,24},{16,0},{24,8},{1,17},{9,25},{17,1},{25,9},{2,18},{10... | collective-permute-start | bytes 589832 | tf_op jit(solution)/shard_map/halo/ppermute | solution.py:379
  6.3 1.3 %collective-permute-start = (bf16[2,192,256]{2,1,0:T(8,128)(2,1)S(1)}, bf16[2,192,256]{2,1,0:T(8,128)(2,1)S(1)}, u32[]{:S(2)}, u32[]{:S(2)}) collective-permute-start(bf16[2,192,256]{2,1,0:T(8,128)(2,1)S(1)} %get-tuple-element.38.refs_0_), channel_id=1, source_target_pairs={{0,8},{8,0},{16,24},{24,16},{1,9},{9,1},{17,25},{25,17},{2,10},{10... | collective-permute-start | bytes 589832 | tf_op jit(solution)/shard_map/halo/ppermute | solution.py:379
  7.6 4.5 %collective-permute-start.3 = (bf16[2,192,256]{2,1,0:T(8,128)(2,1)S(1)}, bf16[2,192,256]{2,1,0:T(8,128)(2,1)S(1)}, u32[]{:S(2)}, u32[]{:S(2)}) collective-permute-start(bf16[2,192,256]{2,1,0:T(8,128)(2,1)S(1)} %get-tuple-element.39.refs_3_.refs_1_.refs_4_), channel_id=1, source_target_pairs={{0,0},{1,2},{2,1},{3,3},{4,4},{5,6},{6,5},{7,7},{8,8},{9,10},{10,9... | collective-permute-start | bytes 589832 | tf_op jit(solution)/shard_map/halo/ppermute | solution.py:389
  12.2 0.1 collective-permute-start.2
  12.2 0.0 collective-permute-done.4.refs_6_.refs_4_.refs_5_
  12.2 1.9 %collective-permute-start.6 = (bf16[2,192,256]{2,1,0:T(8,128)(2,1)S(1)}, bf16[2,192,256]{2,1,0:T(8,128)(2,1)S(1)}, u32[]{:S(2)}, u32[]{:S(2)}) collective-permute-start(bf16[2,192,256]{2,1,0:T(8,128)(2,1)S(1)} %collective-permute-done.4.refs_6_.refs_4_.refs_5_), channel_id=1, source_target_pairs={{0,0},{1,2},{2,1},{3,3},{4,4},{5,6},{6,5},{7,7},{8,8},{9,10},{10,9... | collective-permute-start | bytes 589832 | tf_op jit(solution)/shard_map/halo/ppermute | solution.py:389
  14.2 0.7 %collective-permute-done.1.refs_2_ = bf16[2,192,256]{2,1,0:T(8,128)(2,1)S(1)} collective-permute-done((bf16[2,192,256]{2,1,0:T(8,128)(2,1)S(1)}, bf16[2,192,256]{2,1,0:T(8,128)(2,1)S(1)}, u32[]{:S(2)}, u32[]{:S(2)}) %collective-permute-start.1) | collective-permute-done | bytes 196640 | tf_op jit(solution)/shard_map/halo/ppermute | solution.py:379
  14.9 1.7 %collective-permute-start.5 = (bf16[2,192,256]{2,1,0:T(8,128)(2,1)S(1)}, bf16[2,192,256]{2,1,0:T(8,128)(2,1)S(1)}, u32[]{:S(2)}, u32[]{:S(2)}) collective-permute-start(bf16[2,192,256]{2,1,0:T(8,128)(2,1)S(1)} %collective-permute-done.4.refs_6_.refs_4_.refs_5_), channel_id=1, source_target_pairs={{0,1},{1,0},{2,3},{3,2},{4,5},{5,4},{6,7},{7,6},{8,9},{9,8},{10,11... | collective-permute-start | bytes 589832 | tf_op jit(solution)/shard_map/halo/ppermute | solution.py:389
  16.5 0.0 collective-permute-done.refs_1_
  16.5 0.3 collective-permute-start.7
  16.8 0.0 collective-permute-done.3.refs_5_.refs_3_.refs_6_
  16.8 0.0 collective-permute-done.2.refs_4_.refs_2_
  16.8 2.4 %collective-permute-done.6.refs_8_.refs_6_.refs_7_ = bf16[2,192,256]{2,1,0:T(8,128)(2,1)S(1)} collective-permute-done((bf16[2,192,256]{2,1,0:T(8,128)(2,1)S(1)}, bf16[2,192,256]{2,1,0:T(8,128)(2,1)S(1)}, u32[]{:S(2)}, u32[]{:S(2)}) %collective-permute-start.6) | collective-permute-done | bytes 196640 | tf_op jit(solution)/shard_map/halo/ppermute | solution.py:389
  19.2 0.0 collective-permute-done.5.refs_7_.refs_5_
  19.2 3.5 %attend.2 = (bf16[192,256]{1,0:T(8,128)(2,1)S(1)}, bf16[192,256]{1,0:T(8,128)(2,1)S(1)}, bf16[192,256]{1,0:T(8,128)(2,1)S(1)}, f32[576,128]{1,0:T(8,128)S(1)}) custom-call(bf16[2,192,256]{2,1,0:T(8,128)(2,1)S(1)} %get-tuple-element.38.refs_0_, bf16[2,192,256]{2,1,0:T(8,128)(2,1)S(1)} %collective-permute-done.refs_1_, ...), custom_call_target="tpu_custom_call" | custom-call | flops 5435817984 | bytes 2359296 | tf_op jit(solution)/shard_map/attend/pallas_call | solution.py:342
  22.7 0.8 %collective-permute-start.8 = (bf16[192,256]{1,0:T(8,128)(2,1)S(1)}, bf16[192,256]{1,0:T(8,128)(2,1)S(1)}, u32[]{:S(2)}, u32[]{:S(2)}) collective-permute-start(bf16[192,256]{1,0:T(8,128)(2,1)S(1)} %get-tuple-element.43), channel_id=1, source_target_pairs={{0,16},{8,24},{16,0},{24,8},{1,17},{9,25},{17,1},{25,9},{2,18},{10... | collective-permute-start | bytes 294920 | tf_op jit(solution)/shard_map/merge/ppermute | solution.py:379
  23.5 1.0 %collective-permute-start.9 = (bf16[192,256]{1,0:T(8,128)(2,1)S(1)}, bf16[192,256]{1,0:T(8,128)(2,1)S(1)}, u32[]{:S(2)}, u32[]{:S(2)}) collective-permute-start(bf16[192,256]{1,0:T(8,128)(2,1)S(1)} %get-tuple-element.44), channel_id=1, source_target_pairs={{0,8},{8,0},{16,24},{24,16},{1,9},{9,1},{17,25},{25,17},{2,10},{10... | collective-permute-start | bytes 294920 | tf_op jit(solution)/shard_map/merge/ppermute | solution.py:379
  24.5 0.0 collective-permute-done.7.refs_0_.refs_3_
  24.5 1.2 %attend.3 = (bf16[192,256]{1,0:T(8,128)(2,1)S(1)}, f32[8,768]{1,0:T(8,128)S(1)}) custom-call(bf16[2,192,256]{2,1,0:T(8,128)(2,1)S(1)} %collective-permute-done.7.refs_0_.refs_3_, bf16[2,192,256]{2,1,0:T(8,128)(2,1)S(1)} %get-tuple-element.39.refs_3_.refs_1_.refs_4_, bf16[2,192,256]{2,1,0:T(8,128)(2,1)S(1)} %collective-permute-done.2.refs_4_.refs_2_, ...), custom_call_target="tpu_custom_call" | custom-call | flops 1811939328 | bytes 1794048 | tf_op jit(solution)/shard_map/attend/pallas_call | solution.py:342
  25.8 0.8 %collective-permute-start.12 = (f32[8,768]{1,0:T(8,128)S(1)}, f32[8,768]{1,0:T(8,128)S(1)}, u32[]{:S(2)}, u32[]{:S(2)}) collective-permute-start(f32[8,768]{1,0:T(8,128)S(1)} %get-tuple-element.45.refs_8_), channel_id=1, source_target_pairs={{0,16},{8,24},{16,0},{24,8},{1,17},{9,25},{17,1},{25,9},{2,18},{10... | collective-permute-start | bytes 73736 | tf_op jit(solution)/shard_map/merge/ppermute | solution.py:379
  26.6 1.7 %collective-permute-start.11 = (f32[8,768]{1,0:T(8,128)S(1)}, f32[8,768]{1,0:T(8,128)S(1)}, u32[]{:S(2)}, u32[]{:S(2)}) collective-permute-start(f32[8,768]{1,0:T(8,128)S(1)} %get-tuple-element.45.refs_8_), channel_id=1, source_target_pairs={{0,24},{8,16},{16,8},{24,0},{1,25},{9,17},{17,9},{25,1},{2,26},{10... | collective-permute-start | bytes 73736 | tf_op jit(solution)/shard_map/merge/ppermute | solution.py:379
  28.3 1.4 %collective-permute-done.8.refs_2_ = bf16[192,256]{1,0:T(8,128)(2,1)S(1)} collective-permute-done((bf16[192,256]{1,0:T(8,128)(2,1)S(1)}, bf16[192,256]{1,0:T(8,128)(2,1)S(1)}, u32[]{:S(2)}, u32[]{:S(2)}) %collective-permute-start.8) | collective-permute-done | bytes 98336 | tf_op jit(solution)/shard_map/merge/ppermute | solution.py:379
  29.7 0.0 collective-permute-done.9.refs_3_
  29.7 0.0 collective-permute-start.10
  29.8 2.3 %collective-permute-start.13 = (bf16[192,256]{1,0:T(8,128)(2,1)S(1)}, bf16[192,256]{1,0:T(8,128)(2,1)S(1)}, u32[]{:S(2)}, u32[]{:S(2)}) collective-permute-start(bf16[192,256]{1,0:T(8,128)(2,1)S(1)} %get-tuple-element.52), channel_id=1, source_target_pairs={{0,24},{8,16},{16,8},{24,0},{1,25},{9,17},{17,9},{25,1},{2,26},{10... | collective-permute-start | bytes 294920 | tf_op jit(solution)/shard_map/merge/ppermute | solution.py:379
  32.1 0.0 collective-permute-done.12.refs_11_
  32.1 0.0 collective-permute-done.11.refs_10_
  32.1 0.5 collective-permute-done.10.refs_9_
  32.6 2.9 %gradients.2 = (f32[2,128,768]{2,1,0:T(8,128)S(1)}, f32[2,768]{1,0:T(2,128)S(1)}, f32[2,768]{1,0:T(2,128)S(1)}, f32[192,128]{1,0:T(8,128)S(1)}, bf16[2,2,192,256...) custom-call(bf16[2,192,256]{2,1,0:T(8,128)(2,1)S(1)} %get-tuple-element.38.refs_0_, ...), custom_call_target="tpu_custom_call" | custom-call | flops 12079595520 | bytes 3354624 | tf_op jit(solution)/shard_map/gradients/pallas_call | solution.py:342
  35.5 1.5 %collective-permute-start.14 = (bf16[2,2,192,256]{3,2,1,0:T(8,128)(2,1)S(1)}, bf16[2,2,192,256]{3,2,1,0:T(8,128)(2,1)S(1)}, u32[]{:S(2)}, u32[]{:S(2)}) collective-permute-start(bf16[2,2,192,256]{3,2,1,0:T(8,128)(2,1)S(1)} %get-tuple-element.59), channel_id=1, source_target_pairs={{0,1},{1,0},{2,3},{3,2},{4,5},{5,4},{6,7},{7,6},{8,9},{9,8},{10,11... | collective-permute-start | bytes 1179656 | tf_op jit(solution)/shard_map/gradients/ppermute | solution.py:442
  37.0 3.1 %collective-permute-start.15 = (bf16[2,2,192,256]{3,2,1,0:T(8,128)(2,1)S(1)}, bf16[2,2,192,256]{3,2,1,0:T(8,128)(2,1)S(1)}, u32[]{:S(2)}, u32[]{:S(2)}) collective-permute-start(bf16[2,2,192,256]{3,2,1,0:T(8,128)(2,1)S(1)} %get-tuple-element.60), channel_id=1, source_target_pairs={{0,0},{1,2},{2,1},{3,3},{4,4},{5,6},{6,5},{7,7},{8,8},{9,10},{10,9... | collective-permute-start | bytes 1179656 | tf_op jit(solution)/shard_map/gradients/ppermute | solution.py:442
  40.1 1.7 %gradients.3 = (bf16[192,256]{1,0:T(8,128)(2,1)S(1)}, bf16[192,256]{1,0:T(8,128)(2,1)S(1)}, bf16[192,256]{1,0:T(8,128)(2,1)S(1)}, bf16[192,256]{1,0:T(8,128)(2,1)S(1)}, bf16[2,2,192,256]{3,2,1,0:T(8,128)(2,1)S(1)}) custom-call(bf16[2,192,256]{2,1,0:T(8,128)(2,1)S(1)} %get-tuple-element.38.refs_0_, bf16[2,192,256]{2,1,0:T(8,128)(2,1)S(1)} %collective-permute-done.refs_1_, ...), custom_call_target="tpu_custom_call" | custom-call | flops 6039797760 | bytes 2764800 | tf_op jit(solution)/shard_map/gradients/pallas_call | solution.py:342
  41.8 0.0 collective-permute-done.13.refs_1_
  41.8 1.6 %collective-permute-start.16 = (bf16[192,256]{1,0:T(8,128)(2,1)S(1)}, bf16[192,256]{1,0:T(8,128)(2,1)S(1)}, u32[]{:S(2)}, u32[]{:S(2)}) collective-permute-start(bf16[192,256]{1,0:T(8,128)(2,1)S(1)} %get-tuple-element.64), channel_id=1, source_target_pairs={{0,16},{8,24},{16,0},{24,8},{1,17},{9,25},{17,1},{25,9},{2,18},{10... | collective-permute-start | bytes 294920 | tf_op jit(solution)/shard_map/return/ppermute | solution.py:379
  43.4 1.4 %collective-permute-start.17 = (bf16[192,256]{1,0:T(8,128)(2,1)S(1)}, bf16[192,256]{1,0:T(8,128)(2,1)S(1)}, u32[]{:S(2)}, u32[]{:S(2)}) collective-permute-start(bf16[192,256]{1,0:T(8,128)(2,1)S(1)} %get-tuple-element.65), channel_id=1, source_target_pairs={{0,24},{8,16},{16,8},{24,0},{1,25},{9,17},{17,9},{25,1},{2,26},{10... | collective-permute-start | bytes 294920 | tf_op jit(solution)/shard_map/return/ppermute | solution.py:379
  44.8 0.1 collective-permute-start.18
  44.9 0.0 collective-permute-done.14.refs_5_
  44.9 1.5 %collective-permute-done.15.refs_6_ = bf16[2,2,192,256]{3,2,1,0:T(8,128)(2,1)S(1)} collective-permute-done((bf16[2,2,192,256]{3,2,1,0:T(8,128)(2,1)S(1)}, bf16[2,2,192,256]{3,2,1,0:T(8,128)(2,1)S(1)}, u32[]{:S(2)}, u32[]{:S(2)}) %collective-permute-start.15) | collective-permute-done | bytes 393248 | tf_op jit(solution)/shard_map/gradients/ppermute | solution.py:442
  46.4 0.1 fusion.1
  46.4 0.3 collective-permute-start.20
  46.8 1.2 %collective-permute-start.19 = (bf16[192,256]{1,0:T(8,128)(2,1)S(1)}, bf16[192,256]{1,0:T(8,128)(2,1)S(1)}, u32[]{:S(2)}, u32[]{:S(2)}) collective-permute-start(bf16[192,256]{1,0:T(8,128)(2,1)S(1)} %get-tuple-element.73), channel_id=1, source_target_pairs={{0,4},{4,0},{1,5},{5,1},{2,6},{6,2},{3,7},{7,3},{8,12},{12,8},{9,1... | collective-permute-start | bytes 294920 | tf_op jit(solution)/shard_map/return/ppermute | solution.py:452
  48.0 1.0 %finish.2 = (bf16[192,256]{1,0:T(8,128)(2,1)}, f32[2,192,256]{2,1,0:T(8,128)S(1)}) custom-call(bf16[192,256]{1,0:T(8,128)(2,1)S(1)} %get-tuple-element.40.refs_0_, bf16[192,256]{1,0:T(8,128)(2,1)S(1)} %collective-permute-done.13.refs_1_, bf16[192,256]{1,0:T(8,128)(2,1)S(1)} %collective-permute-done.8.refs_2_, ...), custom_call_target="tpu_custom_call" | custom-call | bytes 2162688 | tf_op jit(solution)/shard_map/finish/pallas_call | solution.py:342
  48.9 1.6 %collective-permute-done.16.refs_1_ = bf16[192,256]{1,0:T(8,128)(2,1)S(1)} collective-permute-done((bf16[192,256]{1,0:T(8,128)(2,1)S(1)}, bf16[192,256]{1,0:T(8,128)(2,1)S(1)}, u32[]{:S(2)}, u32[]{:S(2)}) %collective-permute-start.16) | collective-permute-done | bytes 98336 | tf_op jit(solution)/shard_map/return/ppermute | solution.py:379
  50.5 0.0 collective-permute-done.17.refs_2_
  50.5 0.4 collective-permute-done.18.refs_3_
  50.9 0.0 collective-permute-done.20.refs_5_
  50.9 0.2 collective-permute-done.19.refs_4_
  51.0 1.0 %finish.3 = (bf16[192,256]{1,0:T(8,128)(2,1)}, bf16[192,256]{1,0:T(8,128)(2,1)}, bf16[192,256]{1,0:T(8,128)(2,1)}) custom-call(bf16[192,256]{1,0:T(8,128)(2,1)S(1)} %get-tuple-element.63.refs_0_, bf16[192,256]{1,0:T(8,128)(2,1)S(1)} %collective-permute-done.16.refs_1_, bf16[192,256]{1,0:T(8,128)(2,1)S(1)} %collective-permute-done.17.refs_2_, ...), custom_call_target="tpu_custom_call" | custom-call | bytes 1572864 | tf_op jit(solution)/shard_map/finish/pallas_call | solution.py:342
Async XLA Ops:
  1.9 10.3 %collective-permute-start.4 = (bf16[2,192,256]{2,1,0:T(8,128)(2,1)S(1)}, bf16[2,192,256]{2,1,0:T(8,128)(2,1)S(1)}, u32[]{:S(2)}, u32[]{:S(2)}) collective-permute-start(bf16[2,192,256]{2,1,0:T(8,128)(2,1)S(1)} %get-tuple-element.39.refs_3_.refs_1_.refs_4_), channel_id=1, source_target_pairs={{0,4},{4,0},{1,5},{5,1},{2,6},{6,2},{3,7},{7,3},{8,12},{12,8},{9,1... | collective-permute-start | bytes 589832 | tf_op jit(solution)/shard_map/halo/ppermute | solution.py:384
  4.0 10.9 %collective-permute-start.1 = (bf16[2,192,256]{2,1,0:T(8,128)(2,1)S(1)}, bf16[2,192,256]{2,1,0:T(8,128)(2,1)S(1)}, u32[]{:S(2)}, u32[]{:S(2)}) collective-permute-start(bf16[2,192,256]{2,1,0:T(8,128)(2,1)S(1)} %get-tuple-element.38.refs_0_), channel_id=1, source_target_pairs={{0,16},{8,24},{16,0},{24,8},{1,17},{9,25},{17,1},{25,9},{2,18},{10... | collective-permute-start | bytes 589832 | tf_op jit(solution)/shard_map/halo/ppermute | solution.py:379
  6.3 10.2 %collective-permute-start = (bf16[2,192,256]{2,1,0:T(8,128)(2,1)S(1)}, bf16[2,192,256]{2,1,0:T(8,128)(2,1)S(1)}, u32[]{:S(2)}, u32[]{:S(2)}) collective-permute-start(bf16[2,192,256]{2,1,0:T(8,128)(2,1)S(1)} %get-tuple-element.38.refs_0_), channel_id=1, source_target_pairs={{0,8},{8,0},{16,24},{24,16},{1,9},{9,1},{17,25},{25,17},{2,10},{10... | collective-permute-start | bytes 589832 | tf_op jit(solution)/shard_map/halo/ppermute | solution.py:379
  7.6 9.2 %collective-permute-start.3 = (bf16[2,192,256]{2,1,0:T(8,128)(2,1)S(1)}, bf16[2,192,256]{2,1,0:T(8,128)(2,1)S(1)}, u32[]{:S(2)}, u32[]{:S(2)}) collective-permute-start(bf16[2,192,256]{2,1,0:T(8,128)(2,1)S(1)} %get-tuple-element.39.refs_3_.refs_1_.refs_4_), channel_id=1, source_target_pairs={{0,0},{1,2},{2,1},{3,3},{4,4},{5,6},{6,5},{7,7},{8,8},{9,10},{10,9... | collective-permute-start | bytes 589832 | tf_op jit(solution)/shard_map/halo/ppermute | solution.py:389
  12.2 4.7 %collective-permute-start.2 = (bf16[2,192,256]{2,1,0:T(8,128)(2,1)S(1)}, bf16[2,192,256]{2,1,0:T(8,128)(2,1)S(1)}, u32[]{:S(2)}, u32[]{:S(2)}) collective-permute-start(bf16[2,192,256]{2,1,0:T(8,128)(2,1)S(1)} %get-tuple-element.39.refs_3_.refs_1_.refs_4_), channel_id=1, source_target_pairs={{0,1},{1,0},{2,3},{3,2},{4,5},{5,4},{6,7},{7,6},{8,9},{9,8},{10,11... | collective-permute-start | bytes 589832 | tf_op jit(solution)/shard_map/halo/ppermute | solution.py:389
  12.2 7.0 %collective-permute-start.6 = (bf16[2,192,256]{2,1,0:T(8,128)(2,1)S(1)}, bf16[2,192,256]{2,1,0:T(8,128)(2,1)S(1)}, u32[]{:S(2)}, u32[]{:S(2)}) collective-permute-start(bf16[2,192,256]{2,1,0:T(8,128)(2,1)S(1)} %collective-permute-done.4.refs_6_.refs_4_.refs_5_), channel_id=1, source_target_pairs={{0,0},{1,2},{2,1},{3,3},{4,4},{5,6},{6,5},{7,7},{8,8},{9,10},{10,9... | collective-permute-start | bytes 589832 | tf_op jit(solution)/shard_map/halo/ppermute | solution.py:389
  14.9 4.4 %collective-permute-start.5 = (bf16[2,192,256]{2,1,0:T(8,128)(2,1)S(1)}, bf16[2,192,256]{2,1,0:T(8,128)(2,1)S(1)}, u32[]{:S(2)}, u32[]{:S(2)}) collective-permute-start(bf16[2,192,256]{2,1,0:T(8,128)(2,1)S(1)} %collective-permute-done.4.refs_6_.refs_4_.refs_5_), channel_id=1, source_target_pairs={{0,1},{1,0},{2,3},{3,2},{4,5},{5,4},{6,7},{7,6},{8,9},{9,8},{10,11... | collective-permute-start | bytes 589832 | tf_op jit(solution)/shard_map/halo/ppermute | solution.py:389
  16.5 8.0 %collective-permute-start.7 = (bf16[2,192,256]{2,1,0:T(8,128)(2,1)S(1)}, bf16[2,192,256]{2,1,0:T(8,128)(2,1)S(1)}, u32[]{:S(2)}, u32[]{:S(2)}) collective-permute-start(bf16[2,192,256]{2,1,0:T(8,128)(2,1)S(1)} %collective-permute-done.1.refs_2_), channel_id=1, source_target_pairs={{0,8},{8,0},{16,24},{24,16},{1,9},{9,1},{17,25},{25,17},{2,10},{10... | collective-permute-start | bytes 589832 | tf_op jit(solution)/shard_map/halo/ppermute | solution.py:379
  22.7 7.0 %collective-permute-start.8 = (bf16[192,256]{1,0:T(8,128)(2,1)S(1)}, bf16[192,256]{1,0:T(8,128)(2,1)S(1)}, u32[]{:S(2)}, u32[]{:S(2)}) collective-permute-start(bf16[192,256]{1,0:T(8,128)(2,1)S(1)} %get-tuple-element.43), channel_id=1, source_target_pairs={{0,16},{8,24},{16,0},{24,8},{1,17},{9,25},{17,1},{25,9},{2,18},{10... | collective-permute-start | bytes 294920 | tf_op jit(solution)/shard_map/merge/ppermute | solution.py:379
  23.5 6.3 %collective-permute-start.9 = (bf16[192,256]{1,0:T(8,128)(2,1)S(1)}, bf16[192,256]{1,0:T(8,128)(2,1)S(1)}, u32[]{:S(2)}, u32[]{:S(2)}) collective-permute-start(bf16[192,256]{1,0:T(8,128)(2,1)S(1)} %get-tuple-element.44), channel_id=1, source_target_pairs={{0,8},{8,0},{16,24},{24,16},{1,9},{9,1},{17,25},{25,17},{2,10},{10... | collective-permute-start | bytes 294920 | tf_op jit(solution)/shard_map/merge/ppermute | solution.py:379
  25.8 6.3 %collective-permute-start.12 = (f32[8,768]{1,0:T(8,128)S(1)}, f32[8,768]{1,0:T(8,128)S(1)}, u32[]{:S(2)}, u32[]{:S(2)}) collective-permute-start(f32[8,768]{1,0:T(8,128)S(1)} %get-tuple-element.45.refs_8_), channel_id=1, source_target_pairs={{0,16},{8,24},{16,0},{24,8},{1,17},{9,25},{17,1},{25,9},{2,18},{10... | collective-permute-start | bytes 73736 | tf_op jit(solution)/shard_map/merge/ppermute | solution.py:379
  26.6 5.5 %collective-permute-start.11 = (f32[8,768]{1,0:T(8,128)S(1)}, f32[8,768]{1,0:T(8,128)S(1)}, u32[]{:S(2)}, u32[]{:S(2)}) collective-permute-start(f32[8,768]{1,0:T(8,128)S(1)} %get-tuple-element.45.refs_8_), channel_id=1, source_target_pairs={{0,24},{8,16},{16,8},{24,0},{1,25},{9,17},{17,9},{25,1},{2,26},{10... | collective-permute-start | bytes 73736 | tf_op jit(solution)/shard_map/merge/ppermute | solution.py:379
  29.7 2.8 %collective-permute-start.10 = (f32[8,768]{1,0:T(8,128)S(1)}, f32[8,768]{1,0:T(8,128)S(1)}, u32[]{:S(2)}, u32[]{:S(2)}) collective-permute-start(f32[8,768]{1,0:T(8,128)S(1)} %get-tuple-element.45.refs_8_), channel_id=1, source_target_pairs={{0,8},{8,0},{16,24},{24,16},{1,9},{9,1},{17,25},{25,17},{2,10},{10... | collective-permute-start | bytes 73736 | tf_op jit(solution)/shard_map/merge/ppermute | solution.py:379
  29.8 12.0 %collective-permute-start.13 = (bf16[192,256]{1,0:T(8,128)(2,1)S(1)}, bf16[192,256]{1,0:T(8,128)(2,1)S(1)}, u32[]{:S(2)}, u32[]{:S(2)}) collective-permute-start(bf16[192,256]{1,0:T(8,128)(2,1)S(1)} %get-tuple-element.52), channel_id=1, source_target_pairs={{0,24},{8,16},{16,8},{24,0},{1,25},{9,17},{17,9},{25,1},{2,26},{10... | collective-permute-start | bytes 294920 | tf_op jit(solution)/shard_map/merge/ppermute | solution.py:379
  35.5 9.4 %collective-permute-start.14 = (bf16[2,2,192,256]{3,2,1,0:T(8,128)(2,1)S(1)}, bf16[2,2,192,256]{3,2,1,0:T(8,128)(2,1)S(1)}, u32[]{:S(2)}, u32[]{:S(2)}) collective-permute-start(bf16[2,2,192,256]{3,2,1,0:T(8,128)(2,1)S(1)} %get-tuple-element.59), channel_id=1, source_target_pairs={{0,1},{1,0},{2,3},{3,2},{4,5},{5,4},{6,7},{7,6},{8,9},{9,8},{10,11... | collective-permute-start | bytes 1179656 | tf_op jit(solution)/shard_map/gradients/ppermute | solution.py:442
  37.0 9.4 %collective-permute-start.15 = (bf16[2,2,192,256]{3,2,1,0:T(8,128)(2,1)S(1)}, bf16[2,2,192,256]{3,2,1,0:T(8,128)(2,1)S(1)}, u32[]{:S(2)}, u32[]{:S(2)}) collective-permute-start(bf16[2,2,192,256]{3,2,1,0:T(8,128)(2,1)S(1)} %get-tuple-element.60), channel_id=1, source_target_pairs={{0,0},{1,2},{2,1},{3,3},{4,4},{5,6},{6,5},{7,7},{8,8},{9,10},{10,9... | collective-permute-start | bytes 1179656 | tf_op jit(solution)/shard_map/gradients/ppermute | solution.py:442
  41.8 8.7 %collective-permute-start.16 = (bf16[192,256]{1,0:T(8,128)(2,1)S(1)}, bf16[192,256]{1,0:T(8,128)(2,1)S(1)}, u32[]{:S(2)}, u32[]{:S(2)}) collective-permute-start(bf16[192,256]{1,0:T(8,128)(2,1)S(1)} %get-tuple-element.64), channel_id=1, source_target_pairs={{0,16},{8,24},{16,0},{24,8},{1,17},{9,25},{17,1},{25,9},{2,18},{10... | collective-permute-start | bytes 294920 | tf_op jit(solution)/shard_map/return/ppermute | solution.py:379
  43.4 7.1 %collective-permute-start.17 = (bf16[192,256]{1,0:T(8,128)(2,1)S(1)}, bf16[192,256]{1,0:T(8,128)(2,1)S(1)}, u32[]{:S(2)}, u32[]{:S(2)}) collective-permute-start(bf16[192,256]{1,0:T(8,128)(2,1)S(1)} %get-tuple-element.65), channel_id=1, source_target_pairs={{0,24},{8,16},{16,8},{24,0},{1,25},{9,17},{17,9},{25,1},{2,26},{10... | collective-permute-start | bytes 294920 | tf_op jit(solution)/shard_map/return/ppermute | solution.py:379
  44.8 6.0 %collective-permute-start.18 = (bf16[192,256]{1,0:T(8,128)(2,1)S(1)}, bf16[192,256]{1,0:T(8,128)(2,1)S(1)}, u32[]{:S(2)}, u32[]{:S(2)}) collective-permute-start(bf16[192,256]{1,0:T(8,128)(2,1)S(1)} %get-tuple-element.66), channel_id=1, source_target_pairs={{0,8},{8,0},{16,24},{24,16},{1,9},{9,1},{17,25},{25,17},{2,10},{10... | collective-permute-start | bytes 294920 | tf_op jit(solution)/shard_map/return/ppermute | solution.py:379
  46.4 4.4 %collective-permute-start.20 = (bf16[192,256]{1,0:T(8,128)(2,1)S(1)}, bf16[192,256]{1,0:T(8,128)(2,1)S(1)}, u32[]{:S(2)}, u32[]{:S(2)}) collective-permute-start(bf16[192,256]{1,0:T(8,128)(2,1)S(1)} %get-tuple-element.72), channel_id=1, source_target_pairs={{0,4},{4,0},{1,5},{5,1},{2,6},{6,2},{3,7},{7,3},{8,12},{12,8},{9,1... | collective-permute-start | bytes 294920 | tf_op jit(solution)/shard_map/return/ppermute | solution.py:452
  46.8 4.3 %collective-permute-start.19 = (bf16[192,256]{1,0:T(8,128)(2,1)S(1)}, bf16[192,256]{1,0:T(8,128)(2,1)S(1)}, u32[]{:S(2)}, u32[]{:S(2)}) collective-permute-start(bf16[192,256]{1,0:T(8,128)(2,1)S(1)} %get-tuple-element.73), channel_id=1, source_target_pairs={{0,4},{4,0},{1,5},{5,1},{2,6},{6,2},{3,7},{7,3},{8,12},{12,8},{9,1... | collective-permute-start | bytes 294920 | tf_op jit(solution)/shard_map/return/ppermute | solution.py:452
